TPU v7x, 32 devices: a whole 2x2x4 slice. The times are simulated.
32 devices in a mesh: row: 2 (over x), col: 8 (over z, y), img: 2 (over core).
Axes of the slice: x: 2, y: 2, z: 4, core: 2. Of those that a mesh axis runs over, the one named last changes fastest.
Arguments:
- x_in: bfloat16 [2, 64, 64, 1536], P('img', 'row', 'col'), may hold values from -6 to 6
- gate_in: bfloat16 [2, 64, 64, 1536], P('img', 'row', 'col'), may hold values from -6 to 6
- proj_bc: bfloat16 [2, 64, 64, 64], P('img', 'row', 'col'), may hold values from -3 to 3
- dt_raw: bfloat16 [2, 64, 64, 48], P('img', 'row', 'col'), may hold values from -3 to 3
- step_index: int32 [2], P('img'), may hold values from 0 to 999
- step_table: float32 [1000, 48], replicated, may hold values from -1.5 to 0.5
- rates: float32 [2, 24], replicated, may hold values from 0.0015625 to 0.1875, as said below
- skip: float32 [24], replicated, may hold values from 0.5 to 2
- norm_gain: float32 [1536], replicated, may hold values from 0.5 to 1.5
Outputs:
- mixed: bfloat16 [2, 64, 64, 1536], P('img', 'row', 'col')
Inputs may be any that keep to these rules, and one draw needn't show every extreme that they name: rates of the row heads are given per column step and those of the column heads per row step.
All inputs are finite; a program needn't handle non-finite values.
Results may differ from a plain program's by a relative error of at most 0.0065.
Values may be sent and summed in bfloat16 or wider, within the bound.
No kernel may reach another device: no remote copies, remote signals or barrier semaphores. Data moves between devices by JAX's collectives and lax.ppermute only.
A program may use at most 128 MiB of HBM per device.

v0:
```python
import jax
import jax.numpy as jnp
from jax import lax
from jax.sharding import PartitionSpec as P

SPAN = 64


def prefix(part, axis, combine, identity):
    place = lax.axis_index(axis)
    gathered = jax.tree.map(lambda a: lax.all_gather(a, axis), part)
    state = jax.tree.map(lambda a, e: jnp.zeros_like(a) + jnp.asarray(e, a.dtype), part, identity)

    def one(turn, state):
        return combine(
            state, jax.tree.map(lambda a: lax.dynamic_index_in_dim(a, turn, 0, False), gathered)
        )

    return lax.fori_loop(0, place, one, state)


def segment_scan(inputs, decay_log, in_map, out_map):
    line_count, length, heads, width = inputs.shape
    block = min(SPAN, length)
    blocks = length // block
    values = inputs.astype(jnp.float32).reshape(line_count, blocks, block, heads, width)
    running = jnp.cumsum(decay_log.reshape(line_count, blocks, block, heads), axis=2)
    b_block = in_map.reshape(line_count, blocks, block, -1)
    c_block = out_map.reshape(line_count, blocks, block, -1)
    scores = jnp.einsum("lkin,lkjn->lkij", c_block, b_block, preferred_element_type=jnp.float32)
    spacing = running[:, :, :, None, :] - running[:, :, None, :, :]
    positions = jnp.arange(block)
    lower = (positions[:, None] >= positions[None, :])[None, None, :, :, None]
    weights = jnp.where(lower, jnp.exp(jnp.where(lower, spacing, 0.0)), 0.0) * scores[..., None]
    within = jnp.einsum("lkijh,lkjhp->lkihp", weights, values, precision=lax.Precision.HIGHEST)
    to_end = jnp.exp(running[:, :, -1:, :] - running)
    b_float = b_block.astype(jnp.float32)
    c_float = c_block.astype(jnp.float32)
    block_states = jnp.einsum(
        "lkjh,lkjhp,lkjn->lkhpn", to_end, values, b_float, precision=lax.Precision.HIGHEST
    )
    block_ends = running[:, :, -1, :]

    def advance(carry, items):
        state_now, total_now = carry
        block_state, block_end = items
        state_next = jnp.exp(block_end)[..., None, None] * state_now + block_state
        return ((state_next, total_now + block_end), (state_now, total_now))

    start = (
        jnp.zeros((line_count, heads, width, b_block.shape[-1]), jnp.float32),
        jnp.zeros((line_count, heads), jnp.float32),
    )
    (final, total), (before, offsets) = lax.scan(
        advance, start, (jnp.moveaxis(block_states, 1, 0), jnp.moveaxis(block_ends, 1, 0))
    )
    before = jnp.moveaxis(before, 0, 1)
    offsets = jnp.moveaxis(offsets, 0, 1)
    carried = jnp.exp(running)[..., None] * jnp.einsum(
        "lkin,lkhpn->lkihp", c_float, before, precision=lax.Precision.HIGHEST
    )
    outputs = (within + carried).reshape(line_count, length, heads, width)
    whole_running = (running + offsets[:, :, None, :]).reshape(line_count, length, heads)
    return (outputs, final, total, whole_running)


def prepare(tokens, raw_steps, line_bias, rate):
    line_count, length, channels = tokens.shape
    heads = raw_steps.shape[-1]
    step_size = jax.nn.softplus(raw_steps.astype(jnp.float32) + line_bias[:, None, :])
    decay_log = -rate * step_size
    scaled = (
        step_size[..., None]
        * tokens.astype(jnp.float32).reshape(line_count, length, heads, channels // heads)
    ).astype(jnp.bfloat16)
    return (scaled, decay_log)


def run_lines(tokens, raw_steps, maps, line_bias, rate):
    line_count, length, channels = tokens.shape
    state = maps.shape[-1] // 2
    scaled, decay_log = prepare(tokens, raw_steps, line_bias, rate)
    outputs, final, total, whole_running = segment_scan(
        scaled, decay_log, maps[..., :state], maps[..., state:]
    )
    return outputs.astype(jnp.bfloat16).reshape(line_count, length, channels)


def join_states(earlier, later):
    total_early, state_early = earlier
    total_late, state_late = later
    return (
        total_early + total_late,
        jnp.exp(total_late)[..., None, None] * state_early + state_late,
    )


def body(x_in, gate_in, proj_bc, dt_raw, step_index, step_table, rates, skip, norm_gain):
    images, tile_rows, tile_cols, channels = x_in.shape
    heads = skip.shape[0]
    width = channels // heads
    state = proj_bc.shape[-1] // 4
    onehot = (jnp.arange(step_table.shape[0])[None, :] == step_index[:, None]).astype(jnp.float32)
    image_bias = jnp.dot(
        onehot, step_table, precision=lax.Precision.HIGHEST, preferred_element_type=jnp.float32
    )
    row_lines = images * tile_rows
    sent_rows = (
        x_in.reshape(row_lines, tile_cols, channels),
        dt_raw[..., :heads].reshape(row_lines, tile_cols, heads),
        proj_bc[..., : 2 * state].reshape(row_lines, tile_cols, 2 * state),
    )
    got_tokens, got_steps, got_maps = (
        lax.all_to_all(sent_rows[0], "col", split_axis=0, concat_axis=1, tiled=True),
        lax.all_to_all(sent_rows[1], "col", split_axis=0, concat_axis=1, tiled=True),
        lax.all_to_all(sent_rows[2], "col", split_axis=0, concat_axis=1, tiled=True),
    )
    per_device = got_tokens.shape[0]
    row_bias = lax.dynamic_slice_in_dim(
        jnp.repeat(image_bias[:, :heads], tile_rows, axis=0),
        lax.axis_index("col") * per_device,
        per_device,
        0,
    )
    row_result = run_lines(got_tokens, got_steps, got_maps, row_bias, rates[0])
    y_row = lax.all_to_all(row_result, "col", split_axis=1, concat_axis=0, tiled=True).reshape(
        images, tile_rows, tile_cols, heads, width
    )
    col_lines = images * tile_cols
    col_tokens = jnp.swapaxes(x_in, 1, 2).reshape(col_lines, tile_rows, channels)
    col_steps = jnp.swapaxes(dt_raw[..., heads:], 1, 2).reshape(col_lines, tile_rows, heads)
    col_maps = jnp.swapaxes(proj_bc[..., 2 * state :], 1, 2).reshape(
        col_lines, tile_rows, 2 * state
    )
    col_bias_all = jnp.repeat(image_bias[:, heads:], tile_cols, axis=0)
    scaled, decay_log = prepare(col_tokens, col_steps, col_bias_all, rates[1])
    outputs, final, total, whole_running = segment_scan(
        scaled, decay_log, col_maps[..., :state], col_maps[..., state:]
    )
    total_in, state_in = prefix(
        (total, final), "row", join_states, (jnp.zeros_like(total), jnp.zeros_like(final))
    )
    entering = jnp.einsum(
        "lsn,lhpn->lshp",
        col_maps[..., state:].astype(jnp.float32),
        state_in,
        precision=lax.Precision.HIGHEST,
    )
    outputs = outputs + jnp.exp(whole_running)[..., None] * entering
    y_col_lines = outputs.astype(jnp.bfloat16).reshape(col_lines, tile_rows, channels)
    y_col = jnp.swapaxes(y_col_lines.reshape(images, tile_cols, tile_rows, heads, width), 1, 2)
    x_heads = x_in.astype(jnp.float32).reshape(images, tile_rows, tile_cols, heads, width)
    gate = jax.nn.silu(
        gate_in.astype(jnp.float32).reshape(images, tile_rows, tile_cols, heads, width)
    )
    mixed = (y_row.astype(jnp.float32) + y_col.astype(jnp.float32) + skip[:, None] * x_heads) * gate
    power = jnp.mean(mixed * mixed, axis=(-2, -1), keepdims=True)
    normed = mixed * lax.rsqrt(power + 1e-05) * norm_gain.reshape(heads, width)
    return normed.astype(jnp.bfloat16).reshape(images, tile_rows, tile_cols, channels)


def solution(mesh):
    return jax.shard_map(
        body,
        mesh=mesh,
        in_specs=(
            P("img", "row", "col", None),
            P("img", "row", "col", None),
            P("img", "row", "col", None),
            P("img", "row", "col", None),
            P("img"),
            P(),
            P(),
            P(),
            P(),
        ),
        out_specs=P("img", "row", "col", None),
        check_vma=False,
    )
```

profile of v0, /device:TPU:0, one launch (start us, length us, event | category | flops | bytes accessed | tf_op | source)
XLA Modules:
  0.0 146.1 jit_solution(13849060148230732743)
XLA Ops:
  6.5 0.0 all-gather.4.cloned.1.call-start
  7.3 1.6 %fusion.76 = (bf16[1,32,8,24]{3,2,1,0:T(8,128)(2,1)S(1)}, bf16[32,8,24]{2,1,0:T(8,128)(2,1)}) fusion(bf16[1,32,8,48]{3,2,1,0:T(8,128)(2,1)} %param.14), kind=kLoop, calls=%fused_computation.112 | loop fusion | bytes 49152 | tf_op jit(solution)/shard_map/slice | solution.py:131
  8.8 0.1 copy.102
  8.9 0.1 fusion.78
  9.1 1.4 negate_bitcast_fusion
  10.5 0.1 fusion.58
  10.6 0.1 copy.87
  10.7 1.9 %fusion.77 = f32[8,1,32,24]{3,0,1,2:T(8,128)S(1)} fusion(f32[8,1,32,24]{3,0,1,2:T(8,128)S(1)} %copy.87), kind=kOutput, calls=%fused_computation.113 | output fusion | flops 190464 | bytes 49152 | tf_op jit(solution)/shard_map/jit(cumsum)/reduce_window_sum | solution.py:27
  12.6 0.8 compare_select_fusion.2
  13.4 0.7 bitcast_exponential_fusion
  14.1 0.8 copy.92
  14.9 1.6 %fusion.75 = (bf16[1,32,8,32]{3,2,1,0:T(8,128)(2,1)S(1)}, bf16[32,8,32]{2,1,0:T(8,128)(2,1)}) fusion(bf16[1,32,8,64]{3,2,1,0:T(8,128)(2,1)} %param.13), kind=kLoop, calls=%fused_computation.111 | loop fusion | bytes 65536 | tf_op jit(solution)/shard_map/slice | solution.py:132
  16.4 0.1 copy.103
  16.5 0.6 slice_convert_fusion
  17.2 2.5 %convert_bitcast_fusion.2 = f32[1,8,32,1536]{3,1,2,0:T(8,128)} fusion(bf16[1,32,8,1536]{3,2,1,0:T(8,128)(2,1)} %param.11), kind=kLoop, calls=%fused_computation.54 | loop fusion | flops 393216 | bytes 2359296 | tf_op jit(solution)/shard_map/convert_element_type | solution.py:74
  19.7 2.4 %reshape.447 = f32[8,32,24,64]{3,2,0,1:T(8,128)S(1)} reshape(f32[1,8,32,1536]{3,1,2,0:T(8,128)} %convert_bitcast_fusion.2) | data formatting | bytes 3145728 | tf_op jit(solution)/shard_map/convert_element_type | solution.py:74
  22.1 6.1 %fusion.34 = f32[8,24,64,16]{2,3,1,0:T(8,128)} fusion(f32[8,32,16]{1,2,0:T(8,128)} %slice_convert_fusion, f32[8,32,24]{1,2,0:T(8,128)} %copy.92, f32[8,24]{1,0:T(8,128)S(1)} %exponential_multiply_fusion, f32[8,32,24,64]{3,2,0,1:T(8,128)S(1)} %reshape.447, f32[8,32,24]{1,2,0:T(8,128)} %compare_select_fusion.2), kind=kOutput, calls=%fused_computation.49 | convolution fusion | flops 76578816 | bytes 2425600 | tf_op jit(solution)/shard_map/lkjh,lkjhp,lkjn->lkhpn/dot_general | solution.py:39
  28.3 0.0 all-gather.4.cloned.1.call-update
  28.3 1.6 %reshape.463 = bf16[8,2,384]{2,1,0:T(2,128)(2,1)} reshape(bf16[32,8,24]{2,1,0:T(8,128)(2,1)} %get-tuple-element.105) | data formatting | bytes 24576
  29.9 7.3 %all-to-all-start = ((bf16[8,2,384]{2,1,0:T(2,128)(2,1)}), bf16[8,2,384]{2,1,0:T(2,128)(2,1)S(1)}, u32[]{:S(2)}, u32[]{:S(2)}) async-start(bf16[8,2,384]{2,1,0:T(2,128)(2,1)} %reshape.463), calls=%async_computation | async-start | bytes 24576 | tf_op jit(solution)/shard_map/all_to_all | solution.py:115
  37.1 0.6 iota_compare_fusion
  37.7 1.6 %reshape.465 = bf16[8,2,512]{2,1,0:T(2,128)(2,1)} reshape(bf16[32,8,32]{2,1,0:T(8,128)(2,1)} %get-tuple-element.103) | data formatting | bytes 32768
  39.3 4.4 %all-to-all-done = bf16[8,2,384]{2,1,0:T(2,128)(2,1)S(1)} async-done(((bf16[8,2,384]{2,1,0:T(2,128)(2,1)}), bf16[8,2,384]{2,1,0:T(2,128)(2,1)S(1)}, u32[]{:S(2)}, u32[]{:S(2)}) %all-to-all-start) | async-done | bytes 12320 | tf_op jit(solution)/shard_map/all_to_all | solution.py:115
  43.7 4.0 %all-to-all-start.2 = ((bf16[8,2,512]{2,1,0:T(2,128)(2,1)}), bf16[8,2,512]{2,1,0:T(2,128)(2,1)}, u32[]{:S(2)}, u32[]{:S(2)}) async-start(bf16[8,2,512]{2,1,0:T(2,128)(2,1)} %reshape.465), calls=%async_computation.2 | async-start | bytes 32768 | tf_op jit(solution)/shard_map/all_to_all | solution.py:116
  47.7 0.6 iota_compare_fusion.1
  48.3 3.3 %reshape.450 = f32[1,32,8,24,64]{4,3,2,1,0:T(8,128)} reshape(bf16[1,32,8,1536]{3,2,1,0:T(8,128)(2,1)} %param.11) | data formatting | bytes 2359296 | tf_op jit(solution)/shard_map/reshape | solution.py:152
  51.5 1.7 %copy.91 = f32[8,32,24]{1,2,0:T(8,128)} copy(f32[8,32,24]{2,0,1:T(8,128)} %get-tuple-element.98) | data formatting | bytes 49152 | tf_op jit(solution)/shard_map/exp | solution.py:59
  53.2 0.8 copy.88
  53.9 3.3 %reshape.452 = f32[1,32,8,24,64]{4,3,2,1,0:T(8,128)} reshape(bf16[1,32,8,1536]{3,2,1,0:T(8,128)(2,1)} %param.12) | data formatting | bytes 2359296 | tf_op jit(solution)/shard_map/reshape | solution.py:154
  57.2 0.7 mul.216
  57.9 4.4 %all-gather = f32[16,1,1,24]{3,0,1,2:T(8,128)S(1)} all-gather(f32[8,1,1,24]{3,0,1,2:T(8,128)S(1)} %get-tuple-element.101), channel_id=2, replica_groups=mesh['row'=2,'col'=8,'img'=2] {'row'}, dimensions={0}, use_global_device_ids=true | all-gather | bytes 2304 | tf_op jit(solution)/shard_map/all_gather | solution.py:11
  62.3 0.0 all-to-all-done.2
  62.3 5.9 %all-to-all-start.1 = ((bf16[32,8,1536]{2,1,0:T(8,128)(2,1)}), bf16[32,8,1536]{2,1,0:T(8,128)(2,1)}, u32[]{:S(2)}, u32[]{:S(2)}) async-start(bf16[32,8,1536]{2,1,0:T(8,128)(2,1)} %bitcast.210), calls=%async_computation.1 | async-start | bytes 1572864 | tf_op jit(solution)/shard_map/all_to_all | solution.py:114
  68.2 0.2 fusion.66
  68.4 2.5 %fusion.39 = f32[8,24,64,32]{2,3,1,0:T(8,128)} fusion(bf16[8,32,32]{1,2,0:T(8,128)(2,1)S(1)} %bitcast.217), kind=kOutput, calls=%fused_computation.52 | convolution fusion | flops 75497472 | bytes 1605632 | tf_op jit(solution)/shard_map/lkin,lkhpn->lkihp/dot_general | solution.py:59
  70.9 0.0 copy-done.1
  70.9 6.2 %fusion.8 = f32[8,24,64,32]{2,3,1,0:T(8,128)} fusion(f32[8,32,32]{2,1,0:T(8,128)S(1)} %fusion.66, f32[8,32,24]{1,2,0:T(8,128)S(1)} %copy-done.5, pred[32,32]{1,0:T(8,128)(4,1)S(1)} %copy-done.12, f32[8,32,24,64]{3,2,0,1:T(8,128)S(1)} %reshape.447, f32[8,32,24]{1,2,0:T(8,128)S(1)} %copy-done.1), kind=kOutput, calls=%fused_computation.20 | convolution fusion | flops 152567808 | bytes 3228672 | tf_op jit(solution)/shard_map/lkijh,lkjhp->lkihp/dot_general | solution.py:35
  77.1 0.1 reshape.464
  77.2 0.7 broadcast_multiply_fusion
  78.0 0.1 reduce_window_sum.22
  78.1 0.7 copy.75
  78.9 0.7 copy.81
  79.6 0.8 reshape.466
  80.4 0.9 fusion.59
  81.3 4.7 %all-to-all-done.1 = bf16[32,8,1536]{2,1,0:T(8,128)(2,1)} async-done(((bf16[32,8,1536]{2,1,0:T(8,128)(2,1)}), bf16[32,8,1536]{2,1,0:T(8,128)(2,1)}, u32[]{:S(2)}, u32[]{:S(2)}) %all-to-all-start.1) | async-done | bytes 786464 | tf_op jit(solution)/shard_map/all_to_all | solution.py:114
  86.0 2.5 %copy_bitcast_fusion = f32[4,8,8,1536]{3,2,1,0:T(8,128)} fusion(bf16[8,4,8,1536]{3,2,1,0:T(8,128)(2,1)} %bitcast.53), kind=kLoop, calls=%fused_computation.37 | loop fusion | flops 393216 | bytes 2359296 | tf_op jit(solution)/shard_map/convert_element_type | solution.py:74
  88.5 2.4 %reshape.444 = f32[4,64,24,64]{3,2,1,0:T(8,128)S(1)} reshape(f32[4,8,8,1536]{3,2,1,0:T(8,128)} %copy_bitcast_fusion) | data formatting | bytes 3145728 | tf_op jit(solution)/shard_map/convert_element_type | solution.py:74
  91.0 1.9 %multiply_convert_fusion.1 = bf16[4,64,24,64]{3,2,1,0:T(8,128)(2,1)S(1)} fusion(f32[4,64,24,64]{3,2,1,0:T(8,128)S(1)} %reshape.444, f32[4,64,24]{2,1,0:T(8,128)} %get-tuple-element.97), kind=kLoop, calls=%fused_computation.32 | loop fusion | flops 786432 | bytes 2383872 | tf_op jit(solution)/shard_map/convert_element_type | solution.py:75
  92.9 3.7 %fusion.14 = f32[4,24,64,64]{3,2,1,0:T(8,128)S(1)} fusion(bf16[4,64,24,64]{3,2,1,0:T(8,128)(2,1)S(1)} %multiply_convert_fusion.1, f32[4,64,64]{2,1,0:T(8,128)S(1)} %copy-done.3, f32[4,64,24]{1,2,0:T(8,128)S(1)} %copy-done.9, pred[64,64]{1,0:T(8,128)(4,1)S(1)} %copy-done.11), kind=kOutput, calls=%fused_computation.26 | convolution fusion | flops 303562752 | bytes 2453504 | tf_op jit(solution)/shard_map/lkijh,lkjhp->lkihp/dot_general | solution.py:35
  96.6 1.6 %fusion.6 = bf16[4,1,64,24,64]{2,4,3,0,1:T(8,128)(2,1)S(1)} fusion(f32[4,24,64,64]{3,2,1,0:T(8,128)S(1)} %fusion.14, f32[4,64,24]{1,2,0:T(8,128)S(1)} %copy-done.2, bf16[4,64,32]{2,1,0:T(8,128)(2,1)S(1)} %bitcast.214), kind=kOutput, calls=%fused_computation.11 | convolution fusion | flops 76677120 | bytes 2400256 | tf_op jit(solution)/shard_map/lkin,lkhpn->lkihp/dot_general | solution.py:59
  98.2 1.5 %copy.82 = bf16[4,64,1536]{2,0,1:T(4,128)(2,1)} copy(bf16[4,64,1536]{1,2,0:T(8,128)(2,1)S(1)} %bitcast.211) | data formatting | bytes 1572864 | tf_op jit(solution)/shard_map/convert_element_type | solution.py:86
  99.7 3.5 %all-to-all-start.3 = ((bf16[4,64,1536]{2,0,1:T(4,128)(2,1)}), bf16[4,64,1536]{2,0,1:T(4,128)(2,1)S(1)}, u32[]{:S(2)}, u32[]{:S(2)}) async-start(bf16[4,64,1536]{2,0,1:T(4,128)(2,1)} %copy.82), calls=%async_computation.3 | async-start | bytes 1572864 | tf_op jit(solution)/shard_map/all_to_all | solution.py:126
  103.2 0.0 all-gather.4.cloned.1.call-done
  103.3 0.1 transpose.85
  103.4 0.2 while.3
  103.6 18.8 %all-to-all-done.3 = bf16[4,64,1536]{2,0,1:T(4,128)(2,1)S(1)} async-done(((bf16[4,64,1536]{2,0,1:T(4,128)(2,1)}), bf16[4,64,1536]{2,0,1:T(4,128)(2,1)S(1)}, u32[]{:S(2)}, u32[]{:S(2)}) %all-to-all-start.3) | async-done | bytes 786464 | tf_op jit(solution)/shard_map/all_to_all | solution.py:126
  122.4 0.2 convert_bitcast_fusion.1
  122.6 0.1 copy.84
  122.7 0.0 copy-start.15
  122.8 2.0 %reshape.445 = f32[1,32,8,24,64]{4,3,2,1,0:T(8,128)} reshape(f32[8,4,8,1536]{3,2,1,0:T(8,128)S(1)} %copy.84) | data formatting | bytes 3145728 | tf_op jit(solution)/shard_map/convert_element_type | solution.py:156
  124.8 11.7 %multiply_reduce_fusion = (f32[32,8]{0,1:T(8,128)S(1)}, f32[1,32,8,24,64]{4,1,3,2,0:T(8,128)S(1)}) fusion(f32[1,32,8,24,64]{4,3,2,1,0:T(8,128)} %reshape.452, f32[1,32,8,24,64]{4,3,2,1,0:T(8,128)} %reshape.450, f32[24]{0:T(128)S(1)} %copy-done.15, f32[8,24,64,16]{2,3,1,0:T(8,128)S(1)} %get-tuple-element.85, bf16[8,32,32]{1,2,0:T(8,128)(2,1)S(1)} %bitcast.218, ...), kind=kOutput, calls=%fused_computation.19 | convolution fusion | flops 81788672 | bytes 11142656 | tf_op jit(solution)/shard_map/lsn,lhpn->lshp/dot_general | solution.py:143
  136.5 0.5 multiply_convert_fusion
  137.0 0.6 copy.97
  137.6 1.7 %reshape.442 = bf16[1,32,8,1536]{3,2,1,0:T(8,128)(2,1)} reshape(bf16[1,32,8,24,64]{4,3,2,1,0:T(8,128)(2,1)S(1)} %copy.97) | data formatting | bytes 1572864 | tf_op jit(solution)/shard_map/reshape | solution.py:159
  (37 shorter events, 0.1 us)
Async XLA Ops:
  6.5 2.4 %copy-start = (f32[1000,48]{0,1:T(8,128)S(1)}, f32[1000,48]{0,1:T(8,128)}, u32[]{:S(2)}) copy-start(f32[1000,48]{0,1:T(8,128)} %param.16) | copy-start | bytes 576004
  6.5 96.7 %all-gather.4.cloned.1.call-start = ((), (), s32[]{:S(2)}) async-start(), calls=%async_computation.4 | async-start | bytes 4718592 | tf_op jit(solution)/shard_map/all_gather | solution.py:11
  29.9 13.8 %all-to-all-start = ((bf16[8,2,384]{2,1,0:T(2,128)(2,1)}), bf16[8,2,384]{2,1,0:T(2,128)(2,1)S(1)}, u32[]{:S(2)}, u32[]{:S(2)}) async-start(bf16[8,2,384]{2,1,0:T(2,128)(2,1)} %reshape.463), calls=%async_computation | async-start | bytes 24576 | tf_op jit(solution)/shard_map/all_to_all | solution.py:115
  43.7 13.5 %copy-start.7 = (bf16[8,2,384]{2,1,0:T(2,128)(2,1)}, bf16[8,2,384]{2,1,0:T(2,128)(2,1)S(1)}, u32[]{:S(2)}) copy-start(bf16[8,2,384]{2,1,0:T(2,128)(2,1)S(1)} %all-to-all-done) | copy-start | bytes 36868
  43.7 18.6 %all-to-all-start.2 = ((bf16[8,2,512]{2,1,0:T(2,128)(2,1)}), bf16[8,2,512]{2,1,0:T(2,128)(2,1)}, u32[]{:S(2)}, u32[]{:S(2)}) async-start(bf16[8,2,512]{2,1,0:T(2,128)(2,1)} %reshape.465), calls=%async_computation.2 | async-start | bytes 32768 | tf_op jit(solution)/shard_map/all_to_all | solution.py:116
  53.9 3.3 %copy-start.10 = (f32[1536]{0:T(1024)S(1)}, f32[1536]{0:T(1024)}, u32[]{:S(2)}) copy-start(f32[1536]{0:T(1024)} %param.19) | copy-start | bytes 18436
  57.2 13.7 %copy-start.1 = (f32[8,32,24]{1,2,0:T(8,128)S(1)}, f32[8,32,24]{1,2,0:T(8,128)}, u32[]{:S(2)}) copy-start(f32[8,32,24]{1,2,0:T(8,128)} %compare_select_fusion.2) | copy-start | bytes 73732
  57.2 13.7 %copy-start.12 = (pred[32,32]{1,0:T(8,128)(4,1)S(1)}, pred[32,32]{1,0:T(8,128)(4,1)}, u32[]{:S(2)}) copy-start(pred[32,32]{1,0:T(8,128)(4,1)} %iota_compare_fusion.1) | copy-start | bytes 3076
  62.3 23.7 %all-to-all-start.1 = ((bf16[32,8,1536]{2,1,0:T(8,128)(2,1)}), bf16[32,8,1536]{2,1,0:T(8,128)(2,1)}, u32[]{:S(2)}, u32[]{:S(2)}) async-start(bf16[32,8,1536]{2,1,0:T(8,128)(2,1)} %bitcast.210), calls=%async_computation.1 | async-start | bytes 1572864 | tf_op jit(solution)/shard_map/all_to_all | solution.py:114
  68.2 2.7 %copy-start.5 = (f32[8,32,24]{1,2,0:T(8,128)S(1)}, f32[8,32,24]{1,2,0:T(8,128)}, u32[]{:S(2)}) copy-start(f32[8,32,24]{1,2,0:T(8,128)} %copy.88) | copy-start | bytes 73732
  70.9 6.2 %copy-start.8 = (bf16[8,2,384]{2,1,0:T(2,128)(2,1)S(1)}, bf16[8,2,384]{2,1,0:T(2,128)(2,1)}, u32[]{:S(2)}) copy-start(bf16[8,2,384]{2,1,0:T(2,128)(2,1)} %copy-done.7) | copy-start | bytes 36868
  70.9 6.3 %copy-start.13 = (f32[24]{0:T(128)S(1)}, f32[24]{0:T(128)}, u32[]{:S(2)}) copy-start(f32[24]{0:T(128)} %get-tuple-element.107) | copy-start | bytes 292
  70.9 6.3 %copy-start.14 = (f32[24]{0:T(128)S(1)}, f32[24]{0:T(128)}, u32[]{:S(2)}) copy-start(f32[24]{0:T(128)} %get-tuple-element.112) | copy-start | bytes 292
  90.9 1.9 %copy-start.3 = (f32[4,64,64]{2,1,0:T(8,128)S(1)}, f32[4,64,64]{2,1,0:T(8,128)}, u32[]{:S(2)}) copy-start(f32[4,64,64]{2,1,0:T(8,128)} %fusion.59) | copy-start | bytes 196612
  90.9 1.9 %copy-start.9 = (f32[4,64,24]{1,2,0:T(8,128)S(1)}, f32[4,64,24]{1,2,0:T(8,128)}, u32[]{:S(2)}) copy-start(f32[4,64,24]{1,2,0:T(8,128)} %copy.75) | copy-start | bytes 73732
  91.0 1.9 %copy-start.11 = (pred[64,64]{1,0:T(8,128)(4,1)S(1)}, pred[64,64]{1,0:T(8,128)(4,1)}, u32[]{:S(2)}) copy-start(pred[64,64]{1,0:T(8,128)(4,1)} %iota_compare_fusion) | copy-start | bytes 12292
  92.9 3.7 %copy-start.2 = (f32[4,64,24]{1,2,0:T(8,128)S(1)}, f32[4,64,24]{1,2,0:T(8,128)}, u32[]{:S(2)}) copy-start(f32[4,64,24]{1,2,0:T(8,128)} %copy.81) | copy-start | bytes 73732
  99.7 22.7 %all-to-all-start.3 = ((bf16[4,64,1536]{2,0,1:T(4,128)(2,1)}), bf16[4,64,1536]{2,0,1:T(4,128)(2,1)S(1)}, u32[]{:S(2)}, u32[]{:S(2)}) async-start(bf16[4,64,1536]{2,0,1:T(4,128)(2,1)} %copy.82), calls=%async_computation.3 | async-start | bytes 1572864 | tf_op jit(solution)/shard_map/all_to_all | solution.py:126
  122.7 2.0 %copy-start.4 = (f32[8,32,24]{1,2,0:T(8,128)S(1)}, f32[8,32,24]{1,2,0:T(8,128)}, u32[]{:S(2)}) copy-start(f32[8,32,24]{1,2,0:T(8,128)} %copy.91) | copy-start | bytes 73732
  122.7 2.0 %copy-start.15 = (f32[24]{0:T(128)S(1)}, f32[24]{0:T(128)}, u32[]{:S(2)}) copy-start(f32[24]{0:T(128)} %param.18) | copy-start | bytes 292
  124.8 11.7 %copy-start.6 = (f32[24,64]{1,0:T(8,128)S(1)}, f32[24,64]{1,0:T(8,128)}, u32[]{:S(2)}) copy-start(f32[24,64]{1,0:T(8,128)} %mul.216) | copy-start | bytes 18436
Sparse Core Ops, SparseCore 0:
  28.4 47.7 all-gather.3
where the time goes:
time: 147 us; the launch traced here: 146 us
  matrix products  33 us (22%)
  local copies, waits for them, and re-layouts  30.4 us (21%)
  waiting for transfers between devices  27.9 us (19%)
  starting transfers between devices  20.7 us (14%)
  other arithmetic  15.1 us (10%)
  between operations  14.5 us (10%)
  blocking collectives  4.38 us (3%)
    all_to_all x1, waiting for transfers between devices, body(): lax.all_to_all(row_result, 'col', split_axis=1, concat_axis=0, tiled=True)  18.8 us
    dot_general x1, matrix products, body(): jnp.einsum('lsn,lhpn->lshp', col_maps[..., state:].astype(jnp.float32), s...  11.7 us
    dot_general x2, matrix products, segment_scan(): jnp.einsum('lkijh,lkjhp->lkihp', weights, values, precision=lax.Precision...  9.82 us
    all_to_all x1, starting transfers between devices, body(): lax.all_to_all(sent_rows[1], 'col', split_axis=0, concat_axis=1, tiled=True)  7.28 us
    dot_general x1, matrix products, segment_scan(): jnp.einsum('lkjh,lkjhp,lkjn->lkhpn', to_end, values, b_float, precision=l...  6.14 us
    all_to_all x1, starting transfers between devices, body(): lax.all_to_all(sent_rows[0], 'col', split_axis=0, concat_axis=1, tiled=True)  5.91 us
    convert_element_type x2, other arithmetic, prepare(): tokens.astype(jnp.float32)  4.99 us
    convert_element_type x2, local copies, waits for them, and re-layouts, prepare(): tokens.astype(jnp.float32)  4.9 us
  transfers between devices with their start and end apart: 5, of which 3 were waited for; matrix products, arithmetic and copies ran while one was open for 28% of the time, Pallas kernels for 0%

commit v1 on v0

v1 whole, which is shorter than its diff:
```python
import functools

import jax
import jax.numpy as jnp
from jax import lax
from jax.experimental import pallas as pl
from jax.experimental.pallas import tpu as pltpu
from jax.sharding import PartitionSpec as P

LANES = 128
CHUNK = 512
F32 = jnp.float32
BF16 = jnp.bfloat16


def dot(a, b):
    return jnp.dot(a, b, preferred_element_type=F32)


def iota(shape, dim):
    return lax.broadcasted_iota(jnp.int32, shape, dim)


def parts(values, count):
    terms = []
    for _ in range(count):
        term = values.astype(BF16)
        terms.append(term)
        values = values - term.astype(F32)
    return jnp.concatenate(terms, axis=1)


def spread(pair, first_channel, channels, width):
    heads = pair.shape[1] // 2
    head_of = (first_channel + iota((2 * heads, channels), 1)) // width
    pick = (iota((2 * heads, channels), 0) % heads == head_of).astype(BF16)
    return dot(pair, pick)


def summed(mask, values):
    heads = values.shape[1]
    sums = dot(mask, parts(values, 3))
    return sums[:, :heads] + sums[:, heads : 2 * heads] + sums[:, 2 * heads :]


def step_sizes(raw, bias):
    shifted = raw.astype(F32) + bias
    return jnp.maximum(shifted, 0.0) + jnp.log1p(jnp.exp(-jnp.abs(shifted)))


def bias_row(index_ref, table_ref):
    return table_ref[pl.ds(index_ref[0] % 8, 1), :]


def row_prepare(index_ref, aux_ref, table_ref, rates_ref, mix, grow, fade, cols, lines, state):
    tokens = mix.shape[0]
    heads = fade.shape[1] // 2
    aux = aux_ref[...]
    steps = step_sizes(aux[:, :heads], bias_row(index_ref, table_ref)[:, :heads])
    decay = -rates_ref[0:1, :] * steps
    out, into = iota((tokens, tokens), 0), iota((tokens, tokens), 1)
    same = (out // cols) % lines == (into // cols) % lines
    lower = jnp.logical_and(same, out >= into)
    running = summed(lower.astype(BF16), decay)
    fade[...] = parts(jnp.exp(running), 2)
    grow[...] = parts(steps * jnp.exp(-running), 2)
    b = aux[:, heads : heads + state]
    c = aux[:, heads + state : heads + 2 * state]
    scores = lax.dot_general(c, b, (((1,), (1,)), ((), ())), preferred_element_type=F32)
    mix[...] = jnp.where(lower, scores, 0.0).astype(BF16)


def row_kernel(index_ref, x_ref, aux_ref, table_ref, rates_ref, y_ref, mix, grow, fade, *, cols, lines, state, width):
    step = pl.program_id(0)
    channels = x_ref.shape[1]

    @pl.when(step == 0)
    def _():
        row_prepare(index_ref, aux_ref, table_ref, rates_ref, mix, grow, fade, cols, lines, state)

    first = step * channels
    values = (x_ref[...].astype(F32) * spread(grow[...], first, channels, width)).astype(BF16)
    y_ref[...] = (dot(mix[...], values) * spread(fade[...], first, channels, width)).astype(BF16)


def col_running(index_ref, raw_ref, table_ref, rates_ref, lower, heads):
    steps = step_sizes(raw_ref[:, heads:], bias_row(index_ref, table_ref)[:, heads:])
    decay = -rates_ref[1:2, :] * steps
    return steps, decay, summed(lower, decay)


def widen(maps, cols, state):
    tokens = maps.shape[0]
    places = cols * state
    copy = (iota((state, places), 1) % state == iota((state, places), 0)).astype(BF16)
    own = iota((tokens, places), 1) // state == iota((tokens, places), 0) % cols
    return jnp.where(own, dot(maps, copy), 0.0).astype(BF16)


def state_kernel(index_ref, x_ref, raw_ref, maps_ref, table_ref, rates_ref, s_ref, into, grow, end, *, cols, state, width):
    step = pl.program_id(0)
    channels = x_ref.shape[1]
    tokens = x_ref.shape[0]
    heads = grow.shape[1] // 2

    @pl.when(step == 0)
    def _():
        a, b = iota((tokens, tokens), 0), iota((tokens, tokens), 1)
        lower = jnp.logical_and(a % cols == b % cols, a >= b).astype(BF16)
        steps, decay, running = col_running(index_ref, raw_ref, table_ref, rates_ref, lower, heads)
        grow[...] = parts(steps * jnp.exp(-running), 2)
        places = (cols * state, tokens)
        whole = (iota(places, 0) // state == iota(places, 1) % cols).astype(BF16)
        end[...] = parts(jnp.exp(summed(whole, decay)), 2)
        into[...] = widen(maps_ref[:, 2 * state : 3 * state], cols, state).astype(F32).T.astype(BF16)

    first = step * channels
    values = (x_ref[...].astype(F32) * spread(grow[...], first, channels, width)).astype(BF16)
    s_ref[...] = (dot(into[...], values) * spread(end[...], first, channels, width)).astype(BF16)


def final_kernel(
    index_ref, x_ref, gate_ref, row_ref, s_ref, raw_ref, maps_ref, table_ref, rates_ref, skip_ref, gain_ref,
    out_ref, mix, grow, fade, kept, power, *, cols, state, width
):
    step = pl.program_id(0)
    channels = x_ref.shape[1]
    tokens = x_ref.shape[0]
    heads = grow.shape[1] // 2

    @pl.when(step == 0)
    def _():
        a, b = iota((tokens, tokens), 0), iota((tokens, tokens), 1)
        lower = jnp.logical_and(a % cols == b % cols, a >= b)
        steps, decay, running = col_running(
            index_ref, raw_ref, table_ref, rates_ref, lower.astype(BF16), heads
        )
        fade[...] = parts(jnp.exp(running), 2)
        grow[...] = parts(steps * jnp.exp(-running), 2)
        b_map = maps_ref[:, 2 * state : 3 * state]
        c_map = maps_ref[:, 3 * state :]
        scores = lax.dot_general(c_map, b_map, (((1,), (1,)), ((), ())), preferred_element_type=F32)
        mix[:, :tokens] = jnp.where(lower, scores, 0.0).astype(BF16)
        mix[:, tokens:] = widen(c_map, cols, state)
        power[...] = jnp.zeros_like(power)

    first = step * channels
    x = x_ref[...].astype(F32)
    values = (x * spread(grow[...], first, channels, width)).astype(BF16)
    y_col = dot(mix[...], jnp.concatenate([values, s_ref[...]], axis=0))
    y_col = y_col * spread(fade[...], first, channels, width)
    gate = gate_ref[...].astype(F32)
    v = (row_ref[...].astype(F32) + y_col + skip_ref[...] * x) * (gate / (1.0 + jnp.exp(-gate)))
    kept[step] = v
    power[...] += jnp.sum(v * v, axis=1, keepdims=True)

    @pl.when(step == pl.num_programs(0) - 1)
    def _():
        count = kept.shape[0]
        scale = lax.rsqrt(power[:, 0:1] / (count * channels) + 1e-5)
        for i in range(count):
            part = pl.ds(i * channels, channels)
            out_ref[:, part] = (kept[i] * scale * gain_ref[:, part]).astype(BF16)


def call(kernel, grid, in_specs, out_specs, out_shape, scratch, cost):
    return pl.pallas_call(
        kernel,
        grid_spec=pltpu.PrefetchScalarGridSpec(
            num_scalar_prefetch=1,
            grid=grid,
            in_specs=in_specs,
            out_specs=out_specs,
            scratch_shapes=scratch,
        ),
        out_shape=out_shape,
        compiler_params=pltpu.CompilerParams(vmem_limit_bytes=32 * 1024 * 1024),
        cost_estimate=pl.CostEstimate(flops=cost[0], bytes_accessed=cost[1], transcendentals=0),
    )


def entering_states(ends, state_decay, axis, count):
    onward = [(i, i + 1) for i in range(count - 1)]
    if count == 1:
        return jnp.zeros_like(ends)
    entering = lax.ppermute(ends, axis, onward)
    for _ in range(count - 2):
        passed = (ends.astype(F32) + state_decay() * entering.astype(F32)).astype(BF16)
        entering = lax.ppermute(passed, axis, onward)
    return entering


def body(x_in, gate_in, proj_bc, dt_raw, step_index, step_table, rates, skip, norm_gain, *, row_count, col_count):
    images, tile_rows, tile_cols, channels = x_in.shape
    heads = skip.shape[0]
    width = channels // heads
    state = proj_bc.shape[-1] // 4
    tokens = images * tile_rows * tile_cols
    lines = images * tile_rows // col_count
    chunk = CHUNK
    steps = channels // chunk
    places = tile_cols * state

    x = x_in.reshape(tokens, channels)
    gate = gate_in.reshape(tokens, channels)
    maps = proj_bc.reshape(tokens, 4 * state)
    raw = dt_raw.reshape(tokens, 2 * heads)

    table_spec = pl.BlockSpec((8, 2 * heads), lambda i, index: (index[0] // 8, 0))
    whole = lambda shape: pl.BlockSpec(shape, lambda i, index: (0,) * len(shape))
    part = lambda rows: pl.BlockSpec((rows, chunk), lambda i, index: (0, i))
    pair = pltpu.VMEM((tokens, 2 * heads), BF16)

    aux = jnp.concatenate(
        [raw[:, :heads], maps[:, : 2 * state], jnp.zeros((tokens, LANES - heads - 2 * state), BF16)], axis=1
    )
    sent = jnp.concatenate([x, aux], axis=1).reshape(col_count, tokens // col_count, channels + LANES)
    got = lax.all_to_all(sent, "col", split_axis=0, concat_axis=0, tiled=True)
    got = got.reshape(tokens, channels + LANES)

    ends = call(
        functools.partial(state_kernel, cols=tile_cols, state=state, width=width),
        (steps,),
        [part(tokens), whole((tokens, 2 * heads)), whole((tokens, 4 * state)), table_spec, whole((2, heads))],
        part(places),
        jax.ShapeDtypeStruct((places, channels), BF16),
        [pltpu.VMEM((places, tokens), BF16), pair, pltpu.VMEM((places, 2 * heads), BF16)],
        (2 * places * tokens * channels, 2 * tokens * channels),
    )(step_index, x, raw, maps, step_table, rates)

    def state_decay():
        bias = lax.dynamic_slice_in_dim(step_table, step_index[0], 1, 0)[:, heads:]
        total = -rates[1] * jnp.sum(
            jax.nn.softplus(raw[:, heads:].astype(F32) + bias).reshape(tile_rows, tile_cols, heads), axis=0
        )
        return jnp.repeat(jnp.repeat(jnp.exp(total), state, axis=0), width, axis=1)

    entering = entering_states(ends, state_decay, "row", row_count)

    y_row = call(
        functools.partial(row_kernel, cols=tile_cols, lines=lines, state=state, width=width),
        (steps,),
        [
            part(tokens),
            pl.BlockSpec((tokens, LANES), lambda i, index: (0, channels // LANES)),
            table_spec,
            whole((2, heads)),
        ],
        part(tokens),
        jax.ShapeDtypeStruct((tokens, channels), BF16),
        [pltpu.VMEM((tokens, tokens), BF16), pair, pair],
        (2 * tokens * tokens * channels, 4 * tokens * channels),
    )(step_index, got, got, step_table, rates)
    y_row = lax.all_to_all(
        y_row.reshape(col_count, tokens // col_count, channels), "col", split_axis=0, concat_axis=0, tiled=True
    ).reshape(tokens, channels)

    mixed = call(
        functools.partial(final_kernel, cols=tile_cols, state=state, width=width),
        (steps,),
        [
            part(tokens),
            part(tokens),
            part(tokens),
            part(places),
            whole((tokens, 2 * heads)),
            whole((tokens, 4 * state)),
            table_spec,
            whole((2, heads)),
            pl.BlockSpec((1, chunk), lambda i, index: (0, i)),
            whole((1, channels)),
        ],
        whole((tokens, channels)),
        jax.ShapeDtypeStruct((tokens, channels), BF16),
        [
            pltpu.VMEM((tokens, tokens + places), BF16),
            pair,
            pair,
            pltpu.VMEM((steps, tokens, chunk), F32),
            pltpu.VMEM((tokens, LANES), F32),
        ],
        (2 * tokens * tokens * channels, 8 * tokens * channels),
    )(
        step_index, x, gate, y_row, entering, raw, maps, step_table, rates,
        jnp.repeat(skip, width).reshape(1, channels), norm_gain.reshape(1, channels),
    )
    return mixed.reshape(x_in.shape)


def solution(mesh):
    tile = P("img", "row", "col", None)
    return jax.shard_map(
        functools.partial(body, row_count=mesh.shape["row"], col_count=mesh.shape["col"]),
        mesh=mesh,
        in_specs=(tile, tile, tile, tile, P("img"), P(), P(), P(), P()),
        out_specs=tile,
        check_vma=False,
    )
```

time: 147 us -> 63.7 us (0.43)
  matrix products: 33 us -> 0 us
  local copies, waits for them, and re-layouts: 30.4 us -> 3.86 us
  other arithmetic: 15.1 us -> 0 us
  between operations: 14.5 us -> 0.74 us
  Pallas kernels: 0 us -> 10.4 us
  starting transfers between devices: 20.7 us -> 14.5 us
  waiting for transfers between devices: 27.9 us -> 33.8 us
  blocking collectives: 4.38 us -> 0 us
    dot_general x9 -> x0, matrix products: 33 us -> none  [the longest x1 11.7 us: body(): jnp.einsum('lsn,lhpn->lshp', col_maps[..., state:].astype(jnp.float32), s...]
    pallas_call x0 -> x3, Pallas kernels: none -> 10.4 us  [the longest x1 4.35 us: body(): call(functools.partial(final_kernel, cols=tile_cols, state=state, width=w...]
    all_to_all x4 -> x2, starting transfers between devices: 20.7 us -> 11.1 us  [the longest x1 7.41 us: body(): got = lax.all_to_all(sent, 'col', split_axis=0, concat_axis=0, tiled=True)]
    convert_element_type x6 -> x0, local copies, waits for them, and re-layouts: 9.11 us -> none  [the longest x2 4.9 us: prepare(): tokens.astype(jnp.float32)]
    reshape x3 -> x1, local copies, waits for them, and re-layouts: 8.27 us -> 0.01 us  [body(): norm_gain.reshape(1, channels)]
    ppermute x0 -> x1, waiting for transfers between devices: none -> 7.72 us  [entering_states(): entering = lax.ppermute(ends, axis, onward)]
    convert_element_type x5 -> x0, other arithmetic: 7.54 us -> none  [the longest x2 4.99 us: prepare(): tokens.astype(jnp.float32)]
    all_gather x1 -> x0, blocking collectives: 4.38 us -> none  [prefix(): gathered = jax.tree.map(lambda a: lax.all_gather(a, axis), part)]
  transfers between devices with their start and end apart: 5 -> 3, of which waited for: 3 -> 3; matrix products, arithmetic and copies ran while one was open for 28% -> 1% of each run, Pallas kernels for 0% -> 5%
where the time goes in v1:
time: 63.7 us; the launch traced here: 63.3 us
  waiting for transfers between devices  33.8 us (53%)
  starting transfers between devices  14.5 us (23%)
  Pallas kernels  10.4 us (16%)
  local copies, waits for them, and re-layouts  3.86 us (6%)
  between operations  0.74 us (1%)
    all_to_all x1, waiting for transfers between devices, body(): got = lax.all_to_all(sent, 'col', split_axis=0, concat_axis=0, tiled=True)  20.8 us
    ppermute x1, waiting for transfers between devices, entering_states(): entering = lax.ppermute(ends, axis, onward)  7.72 us
    all_to_all x1, starting transfers between devices, body(): got = lax.all_to_all(sent, 'col', split_axis=0, concat_axis=0, tiled=True)  7.41 us
    all_to_all x1, waiting for transfers between devices, body(): lax.all_to_all(y_row.reshape(col_count, tokens // col_count, channels), '...  5.35 us
    pallas_call x1, Pallas kernels, body(): call(functools.partial(final_kernel, cols=tile_cols, state=state, width=w...  4.35 us
    all_to_all x1, starting transfers between devices, body(): lax.all_to_all(y_row.reshape(col_count, tokens // col_count, channels), '...  3.68 us
    ppermute x1, starting transfers between devices, entering_states(): entering = lax.ppermute(ends, axis, onward)  3.4 us
    pallas_call x1, Pallas kernels, body(): call(functools.partial(row_kernel, cols=tile_cols, lines=lines, state=sta...  3.05 us
  transfers between devices with their start and end apart: 3, of which 3 were waited for; matrix products, arithmetic and copies ran while one was open for 1% of the time, Pallas kernels for 5%

profile of v1, /device:TPU:0, one launch (start us, length us, event | category | flops | bytes accessed | tf_op | source)
XLA Modules:
  0.0 63.3 jit_solution(13078687070946521959)
XLA Ops:
  0.0 0.0 copy-start.2
  0.0 0.8 %copy-done.2 = bf16[1,32,8,48]{3,2,1,0:T(8,128)(2,1)S(1)} copy-done((bf16[1,32,8,48]{3,2,1,0:T(8,128)(2,1)S(1)}, bf16[1,32,8,48]{3,2,1,0:T(8,128)(2,1)}, u32[]{:S(2)}) %copy-start.2) | copy-done | bytes 24600
  0.8 2.0 %concatenate.13 = bf16[8,32,1664]{2,1,0:T(8,128)(2,1)} concatenate(bf16[8,32,1536]{2,1,0:T(8,128)(2,1)} %bitcast.15, bf16[8,32,24]{2,1,0:T(8,128)(2,1)S(1)} %bitcast.20, bf16[8,32,32]{2,1,0:T(8,128)(2,1)} %bitcast.23, bf16[8,32,72]{2,1,0:T(8,128)(2,1)S(1)} %broadcast_in_dim.6), dimensions={2} | concatenate | bytes 1703936 | tf_op jit(solution)/shard_map/concatenate | solution.py:217
  2.9 0.0 copy-start.5
  2.9 7.4 %all-to-all-start = ((bf16[8,32,1664]{2,1,0:T(8,128)(2,1)}), bf16[8,32,1664]{2,1,0:T(8,128)(2,1)S(1)}, u32[]{:S(2)}, u32[]{:S(2)}) async-start(bf16[8,32,1664]{2,1,0:T(8,128)(2,1)} %concatenate.13), calls=%async_computation | async-start | bytes 1703936 | tf_op jit(solution)/shard_map/all_to_all | solution.py:218
  10.9 0.0 copy-done.5
  10.9 0.2 copy.10.table_ref
  11.1 0.0 copy-start.4
  11.2 20.8 %all-to-all-done = bf16[8,32,1664]{2,1,0:T(8,128)(2,1)S(1)} async-done(((bf16[8,32,1664]{2,1,0:T(8,128)(2,1)}), bf16[8,32,1664]{2,1,0:T(8,128)(2,1)S(1)}, u32[]{:S(2)}, u32[]{:S(2)}) %all-to-all-start) | async-done | bytes 852000 | tf_op jit(solution)/shard_map/all_to_all | solution.py:218
  31.9 0.0 copy-done.4
  31.9 3.0 %shard_map.91 = bf16[256,1536]{1,0:T(8,128)(2,1)} custom-call(s32[1]{0:T(128)S(6)} %copy.13.index_ref, bf16[256,1664]{1,0:T(8,128)(2,1)S(1)} %bitcast.13, bf16[256,1664]{1,0:T(8,128)(2,1)S(1)} %bitcast.14, f32[1000,48]{1,0:T(8,128)S(1)} %copy.10.table_ref, f32[2,24]{1,0:T(2,128)S(1)} %copy-done.4), custom_call_target="tpu_custom_call" | custom-call | flops 201326592 | bytes 1572864 | tf_op jit(solution)/shard_map/pallas_call | solution.py:240
  35.0 0.0 copy-start
  35.0 0.0 copy-start.3
  35.0 3.7 %all-to-all-start.1 = ((bf16[8,32,1536]{2,1,0:T(8,128)(2,1)}), bf16[8,32,1536]{2,1,0:T(8,128)(2,1)S(1)}, u32[]{:S(2)}, u32[]{:S(2)}) async-start(bf16[8,32,1536]{2,1,0:T(8,128)(2,1)} %bitcast.8), calls=%async_computation.1 | async-start | bytes 1572864 | tf_op jit(solution)/shard_map/all_to_all | solution.py:254
  38.6 0.0 copy-done
  38.7 0.0 copy-done.3
  38.7 0.0 copy-start.7
  38.7 0.0 copy-start.1
  38.7 3.0 %shard_map.92 = bf16[128,1536]{1,0:T(8,128)(2,1)} custom-call(s32[1]{0:T(128)S(6)} %copy.13.index_ref, bf16[256,1536]{1,0:T(8,128)(2,1)S(1)} %bitcast.16, bf16[256,48]{1,0:T(8,128)(2,1)S(1)} %bitcast.21, bf16[256,64]{1,0:T(8,128)(2,1)S(1)} %bitcast.24, f32[1000,48]{1,0:T(8,128)S(1)} %copy.10.table_ref, f32[2,24]{1,0:T(2,128)S(1)} %copy-done.4), custom_call_target="tpu_custom_call" | custom-call | flops 100663296 | bytes 786432 | tf_op jit(solution)/shard_map/pallas_call | solution.py:221
  41.7 3.4 %collective-permute-start = (bf16[128,1536]{1,0:T(8,128)(2,1)}, bf16[128,1536]{1,0:T(8,128)(2,1)S(1)}, u32[]{:S(2)}, u32[]{:S(2)}) collective-permute-start(bf16[128,1536]{1,0:T(8,128)(2,1)} %shard_map.92), channel_id=1, source_target_pairs={{0,16},{1,17},{2,18},{3,19},{4,20},{5,21},{6,22},{7,23},{8,24},{9,... | collective-permute-start | bytes 1179656 | tf_op jit(solution)/shard_map/ppermute | solution.py:186
  45.1 0.0 copy-done.7
  45.1 0.1 broadcast_in_dim.7
  45.2 0.0 copy-start.6
  45.2 0.1 reshape_reshape.3.skip_ref
  45.3 0.6 copy-done.6
  45.9 7.7 %collective-permute-done.s_ref = bf16[128,1536]{1,0:T(8,128)(2,1)S(1)} collective-permute-done((bf16[128,1536]{1,0:T(8,128)(2,1)}, bf16[128,1536]{1,0:T(8,128)(2,1)S(1)}, u32[]{:S(2)}, u32[]{:S(2)}) %collective-permute-start) | collective-permute-done | bytes 393248 | tf_op jit(solution)/shard_map/ppermute | solution.py:186
  53.6 5.4 %all-to-all-done.1 = bf16[8,32,1536]{2,1,0:T(8,128)(2,1)S(1)} async-done(((bf16[8,32,1536]{2,1,0:T(8,128)(2,1)}), bf16[8,32,1536]{2,1,0:T(8,128)(2,1)S(1)}, u32[]{:S(2)}, u32[]{:S(2)}) %all-to-all-start.1) | async-done | bytes 786464 | tf_op jit(solution)/shard_map/all_to_all | solution.py:254
  59.0 0.0 copy-done.1
  59.0 4.4 %shard_map.93 = bf16[256,1536]{1,0:T(8,128)(2,1)} custom-call(s32[1]{0:T(128)S(6)} %copy.13.index_ref, bf16[256,1536]{1,0:T(8,128)(2,1)S(1)} %bitcast.17, bf16[256,1536]{1,0:T(8,128)(2,1)S(1)} %bitcast.19, bf16[256,1536]{1,0:T(8,128)(2,1)S(1)} %bitcast.18, bf16[128,1536]{1,0:T(8,128)(2,1)S(1)} %collective-permute-done.s_ref, bf16[256,48]{1,0:T(8,128)(2,1)S(1)} %bitcast.22, ...), custom_call_target="tpu_custom_call" | custom-call | flops 201326592 | bytes 3145728 | tf_op jit(solution)/shard_map/pallas_call | solution.py:258
  (2 shorter events, 0.0 us)
Async XLA Ops:
  0.0 0.8 %copy-start.2 = (bf16[1,32,8,48]{3,2,1,0:T(8,128)(2,1)S(1)}, bf16[1,32,8,48]{3,2,1,0:T(8,128)(2,1)}, u32[]{:S(2)}) copy-start(bf16[1,32,8,48]{3,2,1,0:T(8,128)(2,1)} %param.12) | copy-start | bytes 73732
  2.9 8.1 %copy-start.5 = (f32[1000,48]{0,1:T(8,128)S(1)}, f32[1000,48]{0,1:T(8,128)}, u32[]{:S(2)}) copy-start(f32[1000,48]{0,1:T(8,128)} %param.14) | copy-start | bytes 576004
  2.9 29.0 %all-to-all-start = ((bf16[8,32,1664]{2,1,0:T(8,128)(2,1)}), bf16[8,32,1664]{2,1,0:T(8,128)(2,1)S(1)}, u32[]{:S(2)}, u32[]{:S(2)}) async-start(bf16[8,32,1664]{2,1,0:T(8,128)(2,1)} %concatenate.13), calls=%async_computation | async-start | bytes 1703936 | tf_op jit(solution)/shard_map/all_to_all | solution.py:218
  11.1 20.8 %copy-start.4 = (f32[2,24]{1,0:T(2,128)S(1)}, f32[2,24]{1,0:T(2,128)}, u32[]{:S(2)}) copy-start(f32[2,24]{1,0:T(2,128)} %rates_ref.5) | copy-start | bytes 580
  35.0 3.7 %copy-start = (bf16[1,32,8,1536]{3,2,1,0:T(8,128)(2,1)S(1)}, bf16[1,32,8,1536]{3,2,1,0:T(8,128)(2,1)}, u32[]{:S(2)}) copy-start(bf16[1,32,8,1536]{3,2,1,0:T(8,128)(2,1)} %param.9) | copy-start | bytes 2359300
  35.0 3.7 %copy-start.3 = (bf16[1,32,8,64]{3,2,1,0:T(8,128)(2,1)S(1)}, bf16[1,32,8,64]{3,2,1,0:T(8,128)(2,1)}, u32[]{:S(2)}) copy-start(bf16[1,32,8,64]{3,2,1,0:T(8,128)(2,1)} %param.11) | copy-start | bytes 98308
  35.0 24.0 %all-to-all-start.1 = ((bf16[8,32,1536]{2,1,0:T(8,128)(2,1)}), bf16[8,32,1536]{2,1,0:T(8,128)(2,1)S(1)}, u32[]{:S(2)}, u32[]{:S(2)}) async-start(bf16[8,32,1536]{2,1,0:T(8,128)(2,1)} %bitcast.8), calls=%async_computation.1 | async-start | bytes 1572864 | tf_op jit(solution)/shard_map/all_to_all | solution.py:254
  38.7 6.5 %copy-start.7 = (f32[24]{0:T(128)S(1)}, f32[24]{0:T(128)}, u32[]{:S(2)}) copy-start(f32[24]{0:T(128)} %param.16) | copy-start | bytes 292
  38.7 20.3 %copy-start.1 = (bf16[1,32,8,1536]{3,2,1,0:T(8,128)(2,1)S(1)}, bf16[1,32,8,1536]{3,2,1,0:T(8,128)(2,1)}, u32[]{:S(2)}) copy-start(bf16[1,32,8,1536]{3,2,1,0:T(8,128)(2,1)} %param.10) | copy-start | bytes 2359300
  41.7 11.9 %collective-permute-start = (bf16[128,1536]{1,0:T(8,128)(2,1)}, bf16[128,1536]{1,0:T(8,128)(2,1)S(1)}, u32[]{:S(2)}, u32[]{:S(2)}) collective-permute-start(bf16[128,1536]{1,0:T(8,128)(2,1)} %shard_map.92), channel_id=1, source_target_pairs={{0,16},{1,17},{2,18},{3,19},{4,20},{5,21},{6,22},{7,23},{8,24},{9,... | collective-permute-start | bytes 1179656 | tf_op jit(solution)/shard_map/ppermute | solution.py:186
  45.2 0.7 %copy-start.6 = (f32[1536]{0:T(1024)S(1)}, f32[1536]{0:T(1024)}, u32[]{:S(2)}) copy-start(f32[1536]{0:T(1024)} %param.17) | copy-start | bytes 18436

commit v2 on v0

v2 whole, which is shorter than its diff:
```python
import functools

import jax
import jax.numpy as jnp
from jax import lax
from jax.experimental import pallas as pl
from jax.experimental.pallas import tpu as pltpu
from jax.sharding import PartitionSpec as P

LANES = 128
GROUP = 4
PIECES = 2
STRIP = 512
F32 = jnp.float32
BF16 = jnp.bfloat16


def dot(a, b):
    return jnp.dot(a, b, preferred_element_type=F32)


def iota(shape, dim):
    return lax.broadcasted_iota(jnp.int32, shape, dim)


def div(a, n):
    return lax.shift_right_logical(a, n.bit_length() - 1) if n & (n - 1) == 0 else a // n


def mod(a, n):
    return jnp.bitwise_and(a, n - 1) if n & (n - 1) == 0 else a % n


def parts(values, count):
    terms = []
    for _ in range(count):
        term = values.astype(BF16)
        terms.append(term)
        values = values - term.astype(F32)
    return jnp.concatenate(terms, axis=1)


def picks(heads, width, first, channels):
    row = iota((2 * heads, 1), 0)
    head = jnp.where(row >= heads, row - heads, row)
    return (head == div(first + iota((1, channels), 1), width)).astype(BF16)


def summed(mask, values):
    heads = values.shape[1]
    sums = dot(mask, parts(values, 3))
    return sums[:, :heads] + sums[:, heads : 2 * heads] + sums[:, 2 * heads :]


def step_sizes(raw, bias):
    shifted = raw.astype(F32) + bias
    return jnp.maximum(shifted, 0.0) + jnp.log1p(jnp.exp(-jnp.abs(shifted)))


def widen(maps, line, lines):
    state = maps.shape[1]
    places = lines * state
    copy = (mod(iota((1, places), 1), state) == iota((state, 1), 0)).astype(BF16)
    own = div(iota((1, places), 1), state) == line
    return jnp.where(own, dot(maps, copy), 0.0).astype(BF16)


class Scan:
    def __init__(self, order, lines, raw, bias, rates, b_map, c_map):
        tokens, self.heads = raw.shape
        self.lines, self.b_map, self.c_map = lines, b_map, c_map
        self.line, place = order(iota((tokens, 1), 0))
        self.line_in, place_in = order(iota((1, tokens), 1))
        self.lower = jnp.logical_and(self.line == self.line_in, place >= place_in)
        steps = step_sizes(raw, bias)
        self.decay = -rates * steps
        running = summed(self.lower.astype(BF16), self.decay)
        self.fade = parts(jnp.exp(running), 2)
        self.grow = parts(steps * jnp.exp(-running), 2)

    def ends(self):
        places = self.lines * self.b_map.shape[1]
        own = div(iota((places, 1), 0), self.b_map.shape[1]) == self.line_in
        return jnp.exp(summed(own.astype(BF16), self.decay))

    def into(self):
        return widen(self.b_map, self.line, self.lines).astype(F32).T.astype(BF16)

    def mix(self):
        scores = lax.dot_general(
            self.c_map, self.b_map, (((1,), (1,)), ((), ())), preferred_element_type=F32
        )
        within = jnp.where(self.lower, scores, 0.0).astype(BF16)
        return jnp.concatenate([within, widen(self.c_map, self.line, self.lines)], axis=1)


def column_order(cols):
    return lambda token: (mod(token, cols), div(token, cols))


def row_order(cols, lines, member):
    def order(token):
        source = jnp.bitwise_xor(div(token, cols * lines), member)
        return mod(div(token, cols), lines), source * cols + mod(token, cols)

    return order


def strips(channels):
    return [(first, min(STRIP, channels - first)) for first in range(0, channels, STRIP)]


def pack_kernel(index_ref, x_ref, raw_ref, maps_ref, table_ref, bias_ref, *sent, group, axis, heads, state):
    member = mod(lax.axis_index(axis), group)
    pieces = len(sent) // group
    share = x_ref.shape[0] // group
    rows = share // pieces
    channels = x_ref.shape[1]
    for s in range(group):
        for piece in range(pieces):
            first = pl.multiple_of(jnp.bitwise_xor(member, s) * share + piece * rows, rows)
            part = pl.ds(first, rows)
            out = sent[piece * group + s]
            out[:, :channels] = x_ref[part, :]
            used = heads + 2 * state
            out[:, channels : channels + heads] = raw_ref[part, :heads]
            out[:, channels + heads : channels + used] = maps_ref[part, : 2 * state]
            out[:, channels + used :] = jnp.zeros((rows, LANES - used), BF16)
    lanes = table_ref.shape[1]
    mine = iota(table_ref.shape, 1) == mod(index_ref[0], lanes)
    row = jnp.where(mine, table_ref[...], 0.0)
    ones = jnp.ones((8, lanes), BF16)
    total = jnp.zeros((8, row.shape[0]), F32)
    for _ in range(3):
        term = row.astype(BF16)
        row = row - term.astype(F32)
        total += lax.dot_general(ones, term, (((1,), (1,)), ((), ())), preferred_element_type=F32)
    bias_ref[...] = total


def row_scan(bias_ref, rates_ref, blocks, member, cols, heads, state):
    channels = blocks[0].shape[1] - LANES
    tokens = blocks[0].shape[0] * len(blocks)
    lines = tokens // (cols * len(blocks))
    aux = jnp.concatenate([block[:, channels:] for block in blocks], axis=0)
    return Scan(
        row_order(cols, lines, member),
        lines,
        aux[:, :heads],
        bias_ref[0:1, :heads],
        rates_ref[0:1, :],
        aux[:, heads : heads + state],
        aux[:, heads + state : heads + 2 * state],
    )


def col_scan(bias_ref, rates_ref, raw_ref, maps_ref, cols, heads, state):
    return Scan(
        column_order(cols),
        cols,
        raw_ref[:, heads:],
        bias_ref[0:1, heads:],
        rates_ref[1:2, :],
        maps_ref[:, 2 * state : 3 * state],
        maps_ref[:, 3 * state :],
    )


def write_state(scan, tokens_of, width, channels, s_ref, factor_ref):
    ends = scan.ends()
    if factor_ref:
        factor_ref[0][...] = ends
    ends = parts(ends, 2)
    into = scan.into()
    for first, count in strips(channels):
        pick = picks(scan.heads, width, first, count)
        values = (tokens_of(first, count) * dot(scan.grow, pick)).astype(BF16)
        s_ref[:, first : first + count] = (dot(into, values) * dot(ends, pick)).astype(BF16)


def row_state_kernel(bias_ref, rates_ref, *refs, group, axis, cols, heads, state, width):
    blocks, s_ref, factor_ref = refs[:group], refs[group], refs[group + 1 :]
    member = mod(lax.axis_index(axis), group)
    scan = row_scan(bias_ref, rates_ref, blocks, member, cols, heads, state)
    tokens_of = lambda first, count: jnp.concatenate(
        [block[:, first : first + count] for block in blocks], axis=0
    ).astype(F32)
    write_state(scan, tokens_of, width, s_ref.shape[1], s_ref, factor_ref)


def col_state_kernel(bias_ref, rates_ref, x_ref, raw_ref, maps_ref, s_ref, *factor_ref, cols, heads, state, width):
    scan = col_scan(bias_ref, rates_ref, raw_ref, maps_ref, cols, heads, state)
    tokens_of = lambda first, count: x_ref[:, first : first + count].astype(F32)
    write_state(scan, tokens_of, width, s_ref.shape[1], s_ref, factor_ref)


def row_out_kernel(bias_ref, rates_ref, s_ref, *refs, group, axis, cols, heads, state, width):
    blocks, outs = refs[:group], refs[group:]
    member = mod(lax.axis_index(axis), group)
    scan = row_scan(bias_ref, rates_ref, blocks, member, cols, heads, state)
    mix = scan.mix()
    rows = blocks[0].shape[0]
    for first, count in strips(s_ref.shape[1]):
        pick = picks(heads, width, first, count)
        part = slice(first, first + count)
        x = jnp.concatenate([block[:, part] for block in blocks], axis=0).astype(F32)
        values = (x * dot(scan.grow, pick)).astype(BF16)
        y = dot(mix, jnp.concatenate([values, s_ref[:, part]], axis=0)) * dot(scan.fade, pick)
        for s in range(group):
            outs[s][:, part] = y[s * rows : (s + 1) * rows].astype(BF16)


def col_out_kernel(bias_ref, rates_ref, s_ref, x_ref, raw_ref, maps_ref, skip_ref, w_ref, *, cols, heads, state, width):
    scan = col_scan(bias_ref, rates_ref, raw_ref, maps_ref, cols, heads, state)
    mix = scan.mix()
    for first, count in strips(s_ref.shape[1]):
        pick = picks(heads, width, first, count)
        part = slice(first, first + count)
        x = x_ref[:, part].astype(F32)
        values = (x * dot(scan.grow, pick)).astype(BF16)
        y = dot(mix, jnp.concatenate([values, s_ref[:, part]], axis=0)) * dot(scan.fade, pick)
        w_ref[:, part] = y + skip_ref[:, part] * x


def final_kernel(w_ref, gate_ref, gain_ref, *refs, group, axis):
    rows_of, out_ref = refs[:-1], refs[-1]
    pieces = len(rows_of) // group
    rows, channels = rows_of[0].shape
    member = mod(lax.axis_index(axis), group)
    for piece in range(pieces):
        for s in range(group):
            first = (jnp.bitwise_xor(member, s) * pieces + piece) * rows
            part = pl.ds(pl.multiple_of(first, rows), rows)
            gate = gate_ref[part, :].astype(F32)
            v = (rows_of[piece * group + s][...].astype(F32) + w_ref[part, :]) * (gate / (1.0 + jnp.exp(-gate)))
            power = jnp.sum(v * v, axis=1, keepdims=True) / channels
            out_ref[part, :] = (v * lax.rsqrt(power + 1e-5) * gain_ref[...]).astype(BF16)


def call(kernel, out_shape, flops, moved):
    return pl.pallas_call(
        kernel,
        out_shape=out_shape,
        compiler_params=pltpu.CompilerParams(vmem_limit_bytes=32 * 1024 * 1024),
        cost_estimate=pl.CostEstimate(flops=flops, bytes_accessed=moved, transcendentals=0),
    )


def entering_states(made, axis, size, stride, width):
    ends = made[0]
    onward = [(i, i + stride) for i in range(size - stride)]
    if not onward:
        return jnp.zeros_like(ends)
    entering = lax.ppermute(ends, axis, onward)
    for _ in range(size // stride - 2):
        factor = jnp.repeat(made[1], width, axis=1)
        entering = lax.ppermute(
            (ends.astype(F32) + factor * entering.astype(F32)).astype(BF16), axis, onward
        )
    return entering


def body(x_in, gate_in, proj_bc, dt_raw, step_index, step_table, rates, skip, norm_gain, *, row_count, col_count):
    _, tile_rows, cols, channels = x_in.shape
    heads = skip.shape[0]
    width = channels // heads
    state = proj_bc.shape[-1] // 4
    tokens = tile_rows * cols
    group = GROUP
    while col_count % group:
        group //= 2
    share = tokens // group // PIECES
    lines = share // cols

    x = x_in.reshape(tokens, channels)
    gate = gate_in.reshape(tokens, channels)
    maps = proj_bc.reshape(tokens, 4 * state)
    raw = dt_raw.reshape(tokens, 2 * heads)
    sizes = dict(cols=cols, heads=heads, state=state, width=width)
    shared = dict(group=group, axis="col")
    shape = jax.ShapeDtypeStruct

    full = lambda *dims: pl.BlockSpec(dims, lambda i, index: (0,) * len(dims))
    packed = pl.pallas_call(
        functools.partial(pack_kernel, heads=heads, state=state, **shared),
        grid_spec=pltpu.PrefetchScalarGridSpec(
            num_scalar_prefetch=1,
            grid=(1,),
            in_specs=[
                full(tokens, channels),
                full(tokens, 2 * heads),
                full(tokens, 4 * state),
                pl.BlockSpec((2 * heads, LANES), lambda i, index: (0, index[0] // LANES)),
            ],
            out_specs=[full(8, 2 * heads)] + [full(share, channels + LANES)] * (group * PIECES),
        ),
        out_shape=[shape((8, 2 * heads), F32)] + [shape((share, channels + LANES), BF16)] * (group * PIECES),
        compiler_params=pltpu.CompilerParams(vmem_limit_bytes=32 * 1024 * 1024),
        cost_estimate=pl.CostEstimate(flops=0, bytes_accessed=4 * tokens * channels, transcendentals=0),
    )(step_index, x, raw, maps, step_table.T)
    bias, packed = packed[0], packed[1:]

    def exchange(blocks):
        return [blocks[0]] + [
            lax.ppermute(blocks[s], "col", [(i, i ^ s) for i in range(col_count)]) for s in range(1, group)
        ]

    def state_shapes(places, count):
        return [shape((places, channels), BF16)] + [shape((places, heads), F32)] * (count > 2)

    got = [exchange(packed[piece * group : (piece + 1) * group]) for piece in range(PIECES)]

    col_made = call(
        functools.partial(col_state_kernel, **sizes),
        state_shapes(cols * state, row_count),
        2 * cols * state * tokens * channels,
        2 * tokens * channels,
    )(bias, rates, x, raw, maps)
    col_entering = entering_states(col_made, "row", row_count, 1, width)

    row_entering = []
    for piece in range(PIECES):
        made = call(
            functools.partial(row_state_kernel, **sizes, **shared),
            state_shapes(lines * state, col_count // group),
            2 * lines * state * group * share * channels,
            2 * group * share * channels,
        )(bias, rates, *got[piece])
        row_entering.append(entering_states(made, "col", col_count, group, width))

    w = call(
        functools.partial(col_out_kernel, **sizes),
        shape((tokens, channels), F32),
        2 * tokens * tokens * channels,
        8 * tokens * channels,
    )(bias, rates, col_entering, x, raw, maps, jnp.repeat(skip, width).reshape(1, channels))

    back = []
    for piece in range(PIECES):
        y_row = call(
            functools.partial(row_out_kernel, **sizes, **shared),
            [shape((share, channels), BF16)] * group,
            2 * (group * share) ** 2 * channels,
            4 * group * share * channels,
        )(bias, rates, row_entering[piece], *got[piece])
        back += exchange(y_row)

    mixed = call(
        functools.partial(final_kernel, **shared),
        shape((tokens, channels), BF16),
        10 * tokens * channels,
        10 * tokens * channels,
    )(w, gate, norm_gain.reshape(1, channels), *back)
    return mixed.reshape(x_in.shape)


def solution(mesh):
    tile = P("img", "row", "col", None)
    return jax.shard_map(
        functools.partial(body, row_count=mesh.shape["row"], col_count=mesh.shape["col"]),
        mesh=mesh,
        in_specs=(tile, tile, tile, tile, P("img"), P(), P(), P(), P()),
        out_specs=tile,
        check_vma=False,
    )
```

time: 147 us -> 53.1 us (0.36)
  matrix products: 33 us -> 0 us
  local copies, waits for them, and re-layouts: 30.4 us -> 4.61 us
  waiting for transfers between devices: 27.9 us -> 3.34 us
  other arithmetic: 15.1 us -> 0 us
  between operations: 14.5 us -> 0.88 us
  starting transfers between devices: 20.7 us -> 33.8 us
  Pallas kernels: 0 us -> 10.1 us
  blocking collectives: 4.38 us -> 0 us
    ppermute x0 -> x15, starting transfers between devices: none -> 33.8 us  [the longest x12 21.3 us: exchange(): lax.ppermute(blocks[s], 'col', [(i, i ^ s) for i in range(col_count)])]
    dot_general x9 -> x0, matrix products: 33 us -> none  [the longest x1 11.7 us: body(): jnp.einsum('lsn,lhpn->lshp', col_maps[..., state:].astype(jnp.float32), s...]
    all_to_all x4 -> x0, waiting for transfers between devices: 27.9 us -> none  [the longest x1 18.8 us: body(): lax.all_to_all(row_result, 'col', split_axis=1, concat_axis=0, tiled=True)]
    all_to_all x4 -> x0, starting transfers between devices: 20.7 us -> none  [the longest x1 7.28 us: body(): lax.all_to_all(sent_rows[1], 'col', split_axis=0, concat_axis=1, tiled=True)]
    pallas_call x0 -> x8, Pallas kernels: none -> 10.1 us  [the longest x2 2.5 us: body(): call(functools.partial(row_out_kernel, **sizes, **shared), [shape((share,...]
    convert_element_type x6 -> x0, local copies, waits for them, and re-layouts: 9.11 us -> none  [the longest x2 4.9 us: prepare(): tokens.astype(jnp.float32)]
    reshape x3 -> x1, local copies, waits for them, and re-layouts: 8.27 us -> 0.01 us  [body(): norm_gain.reshape(1, channels)]
    convert_element_type x5 -> x0, other arithmetic: 7.54 us -> none  [the longest x2 4.99 us: prepare(): tokens.astype(jnp.float32)]
  transfers between devices with their start and end apart: 5 -> 15, of which waited for: 3 -> 2; matrix products, arithmetic and copies ran while one was open for 28% -> 0% of each run, Pallas kernels for 0% -> 16%
where the time goes in v2:
time: 53.1 us; the launch traced here: 52.8 us
  starting transfers between devices  33.8 us (64%)
  Pallas kernels  10.1 us (19%)
  local copies, waits for them, and re-layouts  4.61 us (9%)
  waiting for transfers between devices  3.34 us (6%)
  between operations  0.88 us (2%)
    ppermute x12, starting transfers between devices, exchange(): lax.ppermute(blocks[s], 'col', [(i, i ^ s) for i in range(col_count)])  21.3 us
    ppermute x3, starting transfers between devices, entering_states(): entering = lax.ppermute(ends, axis, onward)  12.5 us
    unnamed x24, local copies, waits for them, and re-layouts  4.46 us
    ppermute x12, waiting for transfers between devices, exchange(): lax.ppermute(blocks[s], 'col', [(i, i ^ s) for i in range(col_count)])  3.33 us
    pallas_call x2, Pallas kernels, body(): call(functools.partial(row_out_kernel, **sizes, **shared), [shape((share,...  2.5 us
    pallas_call x2, Pallas kernels, body(): call(functools.partial(row_state_kernel, **sizes, **shared), state_shapes...  2.22 us
    pallas_call x1, Pallas kernels, body(): call(functools.partial(col_out_kernel, **sizes), shape((tokens, channels)...  1.95 us
    pallas_call x1, Pallas kernels, body(): call(functools.partial(final_kernel, **shared), shape((tokens, channels),...  1.76 us
  transfers between devices with their start and end apart: 15, of which 2 were waited for; matrix products, arithmetic and copies ran while one was open for 0% of the time, Pallas kernels for 16%

profile of v2, /device:TPU:0, one launch (start us, length us, event | category | flops | bytes accessed | tf_op | source)
XLA Modules:
  0.0 52.8 jit_solution(5800267056552585249)
XLA Ops:
  0.7 0.0 copy-start
  0.7 1.1 %copy-done = bf16[1,32,8,1536]{3,2,1,0:T(8,128)(2,1)S(1)} copy-done((bf16[1,32,8,1536]{3,2,1,0:T(8,128)(2,1)S(1)}, bf16[1,32,8,1536]{3,2,1,0:T(8,128)(2,1)}, u32[]{:S(2)}) %copy-start) | copy-done | bytes 786456
  1.8 0.0 copy-start.3
  1.8 0.8 %copy-done.3 = bf16[1,32,8,48]{3,2,1,0:T(8,128)(2,1)S(1)} copy-done((bf16[1,32,8,48]{3,2,1,0:T(8,128)(2,1)S(1)}, bf16[1,32,8,48]{3,2,1,0:T(8,128)(2,1)}, u32[]{:S(2)}) %copy-start.3) | copy-done | bytes 24600
  2.6 0.0 copy-start.5
  2.6 0.8 %copy-done.5 = bf16[1,32,8,64]{3,2,1,0:T(8,128)(2,1)S(1)} copy-done((bf16[1,32,8,64]{3,2,1,0:T(8,128)(2,1)S(1)}, bf16[1,32,8,64]{3,2,1,0:T(8,128)(2,1)}, u32[]{:S(2)}) %copy-start.5) | copy-done | bytes 32792
  3.5 0.0 copy-start.7
  3.5 0.9 %copy-done.7 = f32[1000,48]{0,1:T(8,128)S(1)} copy-done((f32[1000,48]{0,1:T(8,128)S(1)}, f32[1000,48]{0,1:T(8,128)}, u32[]{:S(2)}) %copy-start.7) | copy-done | bytes 192024
  4.4 0.1 shard_map.91
  4.5 3.0 %collective-permute-start.1 = (bf16[32,1664]{1,0:T(8,128)(2,1)S(1)}, bf16[32,1664]{1,0:T(8,128)(2,1)S(1)}, u32[]{:S(2)}, u32[]{:S(2)}) collective-permute-start(bf16[32,1664]{1,0:T(8,128)(2,1)S(1)} %get-tuple-element.24), channel_id=1, source_target_pairs={{0,2},{2,0},{4,6},{6,4},{8,10},{10,8},{12,14},{14,12},{1,3},{3,1},... | collective-permute-start | bytes 319496 | tf_op jit(solution)/shard_map/ppermute | solution.py:305
  7.6 1.6 %collective-permute-start.2 = (bf16[32,1664]{1,0:T(8,128)(2,1)S(1)}, bf16[32,1664]{1,0:T(8,128)(2,1)S(1)}, u32[]{:S(2)}, u32[]{:S(2)}) collective-permute-start(bf16[32,1664]{1,0:T(8,128)(2,1)S(1)} %get-tuple-element.25), channel_id=1, source_target_pairs={{0,4},{2,6},{4,0},{6,2},{8,12},{10,14},{12,8},{14,10},{1,5},{3,7},... | collective-permute-start | bytes 319496 | tf_op jit(solution)/shard_map/ppermute | solution.py:305
  9.1 0.0 collective-permute-start.3
  9.2 0.0 copy-start.8
  9.2 0.7 %copy-done.8 = f32[2,24]{1,0:T(2,128)S(1)} copy-done((f32[2,24]{1,0:T(2,128)S(1)}, f32[2,24]{1,0:T(2,128)}, u32[]{:S(2)}) %copy-start.8) | copy-done | bytes 216
  9.8 1.6 %shard_map.92 = bf16[128,1536]{1,0:T(8,128)(2,1)S(1)} custom-call(f32[8,48]{1,0:T(8,128)S(1)} %get-tuple-element.22.bias_ref, f32[2,24]{1,0:T(2,128)S(1)} %copy-done.8, bf16[256,1536]{1,0:T(8,128)(2,1)S(1)} %bitcast.7, bf16[256,48]{1,0:T(8,128)(2,1)S(1)} %bitcast.11, bf16[256,64]{1,0:T(8,128)(2,1)S(1)} %bitcast.14), custom_call_target="tpu_custom_call" | custom-call | flops 100663296 | bytes 786432 | tf_op jit(solution)/shard_map/pallas_call | solution.py:313
  11.4 0.0 copy-start.10
  11.4 0.0 copy-start.11
  11.4 0.0 copy-start.1
  11.4 0.0 copy-start.4
  11.4 0.0 copy-start.6
  11.5 0.0 copy-start.9
  11.5 3.9 %collective-permute-start = (bf16[128,1536]{1,0:T(8,128)(2,1)S(1)}, bf16[128,1536]{1,0:T(8,128)(2,1)S(1)}, u32[]{:S(2)}, u32[]{:S(2)}) collective-permute-start(bf16[128,1536]{1,0:T(8,128)(2,1)S(1)} %shard_map.92), channel_id=1, source_target_pairs={{0,16},{1,17},{2,18},{3,19},{4,20},{5,21},{6,22},{7,23},{8,24},{9,... | collective-permute-start | bytes 1179656 | tf_op jit(solution)/shard_map/ppermute | solution.py:254
  15.4 1.6 %collective-permute-start.8 = (bf16[32,1664]{1,0:T(8,128)(2,1)S(1)}, bf16[32,1664]{1,0:T(8,128)(2,1)S(1)}, u32[]{:S(2)}, u32[]{:S(2)}) collective-permute-start(bf16[32,1664]{1,0:T(8,128)(2,1)S(1)} %get-tuple-element.32), channel_id=1, source_target_pairs={{0,2},{2,0},{4,6},{6,4},{8,10},{10,8},{12,14},{14,12},{1,3},{3,1},... | collective-permute-start | bytes 319496 | tf_op jit(solution)/shard_map/ppermute | solution.py:305
  17.0 0.0 collective-permute-done.1.refs_1_
  17.0 1.6 %collective-permute-start.9 = (bf16[32,1664]{1,0:T(8,128)(2,1)S(1)}, bf16[32,1664]{1,0:T(8,128)(2,1)S(1)}, u32[]{:S(2)}, u32[]{:S(2)}) collective-permute-start(bf16[32,1664]{1,0:T(8,128)(2,1)S(1)} %get-tuple-element.33), channel_id=1, source_target_pairs={{0,4},{2,6},{4,0},{6,2},{8,12},{10,14},{12,8},{14,10},{1,5},{3,7},... | collective-permute-start | bytes 319496 | tf_op jit(solution)/shard_map/ppermute | solution.py:305
  18.6 0.0 collective-permute-done.2.refs_2_
  18.6 0.4 collective-permute-start.10
  19.0 0.0 collective-permute-done.3.refs_3_
  19.0 1.1 %shard_map.94 = bf16[64,1536]{1,0:T(8,128)(2,1)S(1)} custom-call(f32[8,48]{1,0:T(8,128)S(1)} %get-tuple-element.22.bias_ref, f32[2,24]{1,0:T(2,128)S(1)} %copy-done.8, bf16[32,1664]{1,0:T(8,128)(2,1)S(1)} %get-tuple-element.23.refs_0_, bf16[32,1664]{1,0:T(8,128)(2,1)S(1)} %collective-permute-done.1.refs_1_, ...), custom_call_target="tpu_custom_call" | custom-call | flops 25165824 | bytes 393216 | tf_op jit(solution)/shard_map/pallas_call | solution.py:323
  20.1 4.5 %collective-permute-start.4 = (bf16[64,1536]{1,0:T(8,128)(2,1)S(1)}, bf16[64,1536]{1,0:T(8,128)(2,1)S(1)}, u32[]{:S(2)}, u32[]{:S(2)}) collective-permute-start(bf16[64,1536]{1,0:T(8,128)(2,1)S(1)} %shard_map.94), channel_id=1, source_target_pairs={{0,8},{2,10},{4,12},{6,14},{1,9},{3,11},{5,13},{7,15},{16,24},{18,... | collective-permute-start | bytes 589832 | tf_op jit(solution)/shard_map/ppermute | solution.py:254
  24.6 0.0 collective-permute-done.8.refs_1_
  24.6 0.0 collective-permute-done.9.refs_2_
  24.6 0.0 collective-permute-done.10.refs_3_
  24.6 1.1 %shard_map.96 = bf16[64,1536]{1,0:T(8,128)(2,1)S(1)} custom-call(f32[8,48]{1,0:T(8,128)S(1)} %get-tuple-element.22.bias_ref, f32[2,24]{1,0:T(2,128)S(1)} %copy-done.8, bf16[32,1664]{1,0:T(8,128)(2,1)S(1)} %get-tuple-element.31.refs_0_, bf16[32,1664]{1,0:T(8,128)(2,1)S(1)} %collective-permute-done.8.refs_1_, ...), custom_call_target="tpu_custom_call" | custom-call | flops 25165824 | bytes 393216 | tf_op jit(solution)/shard_map/pallas_call | solution.py:323
  25.7 4.0 %collective-permute-start.11 = (bf16[64,1536]{1,0:T(8,128)(2,1)S(1)}, bf16[64,1536]{1,0:T(8,128)(2,1)S(1)}, u32[]{:S(2)}, u32[]{:S(2)}) collective-permute-start(bf16[64,1536]{1,0:T(8,128)(2,1)S(1)} %shard_map.96), channel_id=1, source_target_pairs={{0,8},{2,10},{4,12},{6,14},{1,9},{3,11},{5,13},{7,15},{16,24},{18,... | collective-permute-start | bytes 589832 | tf_op jit(solution)/shard_map/ppermute | solution.py:254
  29.8 0.0 collective-permute-done.4.s_ref
  29.8 1.2 %shard_map.95 = (bf16[32,1536]{1,0:T(8,128)(2,1)S(1)}, bf16[32,1536]{1,0:T(8,128)(2,1)S(1)}, bf16[32,1536]{1,0:T(8,128)(2,1)S(1)}, bf16[32,1536]{1,0:T(8,128)(2,1)S(1)}) custom-call(f32[8,48]{1,0:T(8,128)S(1)} %get-tuple-element.22.bias_ref, f32[2,24]{1,0:T(2,128)S(1)} %copy-done.8, bf16[64,1536]{1,0:T(8,128)(2,1)S(1)} %collective-permute-done.4.s_ref, ...), custom_call_target="tpu_custom_call" | custom-call | flops 50331648 | bytes 786432 | tf_op jit(solution)/shard_map/pallas_call | solution.py:340
  31.1 1.3 %collective-permute-start.5 = (bf16[32,1536]{1,0:T(8,128)(2,1)S(1)}, bf16[32,1536]{1,0:T(8,128)(2,1)S(1)}, u32[]{:S(2)}, u32[]{:S(2)}) collective-permute-start(bf16[32,1536]{1,0:T(8,128)(2,1)S(1)} %get-tuple-element.28), channel_id=1, source_target_pairs={{0,2},{2,0},{4,6},{6,4},{8,10},{10,8},{12,14},{14,12},{1,3},{3,1},... | collective-permute-start | bytes 294920 | tf_op jit(solution)/shard_map/ppermute | solution.py:305
  32.4 8.2 %collective-permute-start.6 = (bf16[32,1536]{1,0:T(8,128)(2,1)S(1)}, bf16[32,1536]{1,0:T(8,128)(2,1)S(1)}, u32[]{:S(2)}, u32[]{:S(2)}) collective-permute-start(bf16[32,1536]{1,0:T(8,128)(2,1)S(1)} %get-tuple-element.29), channel_id=1, source_target_pairs={{0,4},{2,6},{4,0},{6,2},{8,12},{10,14},{12,8},{14,10},{1,5},{3,7},... | collective-permute-start | bytes 294920 | tf_op jit(solution)/shard_map/ppermute | solution.py:305
  40.6 0.0 collective-permute-start.7
  40.6 0.0 collective-permute-done.11.s_ref
  40.6 1.3 %shard_map.97 = (bf16[32,1536]{1,0:T(8,128)(2,1)S(1)}, bf16[32,1536]{1,0:T(8,128)(2,1)S(1)}, bf16[32,1536]{1,0:T(8,128)(2,1)S(1)}, bf16[32,1536]{1,0:T(8,128)(2,1)S(1)}) custom-call(f32[8,48]{1,0:T(8,128)S(1)} %get-tuple-element.22.bias_ref, f32[2,24]{1,0:T(2,128)S(1)} %copy-done.8, bf16[64,1536]{1,0:T(8,128)(2,1)S(1)} %collective-permute-done.11.s_ref, ...), custom_call_target="tpu_custom_call" | custom-call | flops 50331648 | bytes 786432 | tf_op jit(solution)/shard_map/pallas_call | solution.py:340
  41.9 0.0 copy-start.2
  41.9 1.5 %collective-permute-start.12 = (bf16[32,1536]{1,0:T(8,128)(2,1)S(1)}, bf16[32,1536]{1,0:T(8,128)(2,1)S(1)}, u32[]{:S(2)}, u32[]{:S(2)}) collective-permute-start(bf16[32,1536]{1,0:T(8,128)(2,1)S(1)} %get-tuple-element.36), channel_id=1, source_target_pairs={{0,2},{2,0},{4,6},{6,4},{8,10},{10,8},{12,14},{14,12},{1,3},{3,1},... | collective-permute-start | bytes 294920 | tf_op jit(solution)/shard_map/ppermute | solution.py:305
  43.4 0.0 collective-permute-done.s_ref
  43.4 2.0 %collective-permute-start.13 = (bf16[32,1536]{1,0:T(8,128)(2,1)S(1)}, bf16[32,1536]{1,0:T(8,128)(2,1)S(1)}, u32[]{:S(2)}, u32[]{:S(2)}) collective-permute-start(bf16[32,1536]{1,0:T(8,128)(2,1)S(1)} %get-tuple-element.37), channel_id=1, source_target_pairs={{0,4},{2,6},{4,0},{6,2},{8,12},{10,14},{12,8},{14,10},{1,5},{3,7},... | collective-permute-start | bytes 294920 | tf_op jit(solution)/shard_map/ppermute | solution.py:305
  45.5 0.0 collective-permute-done.5.refs_1_
  45.5 0.0 collective-permute-start.14
  45.5 0.0 copy-done.10
  45.5 0.0 copy-done.11
  45.5 0.1 broadcast_in_dim.3
  45.6 0.1 reshape_reshape.3.skip_ref
  45.7 0.0 copy-done.1
  45.7 0.0 copy-done.4
  45.7 0.0 copy-done.6
  45.7 0.0 copy-done.9
  45.7 2.0 %shard_map.93.w_ref = f32[256,1536]{1,0:T(8,128)S(1)} custom-call(f32[8,48]{1,0:T(8,128)S(1)} %get-tuple-element.22.bias_ref, f32[2,24]{1,0:T(2,128)S(1)} %copy-done.9, bf16[128,1536]{1,0:T(8,128)(2,1)S(1)} %collective-permute-done.s_ref, bf16[256,1536]{1,0:T(8,128)(2,1)S(1)} %bitcast.8, bf16[256,48]{1,0:T(8,128)(2,1)S(1)} %bitcast.12, ...), custom_call_target="tpu_custom_call" | custom-call | flops 201326592 | bytes 3145728 | tf_op jit(solution)/shard_map/pallas_call | solution.py:331
  47.7 0.0 collective-permute-done.6.refs_2_
  47.7 0.0 collective-permute-done.7.refs_3_
  47.7 0.6 %collective-permute-done.12.refs_5_ = bf16[32,1536]{1,0:T(8,128)(2,1)S(1)} collective-permute-done((bf16[32,1536]{1,0:T(8,128)(2,1)S(1)}, bf16[32,1536]{1,0:T(8,128)(2,1)S(1)}, u32[]{:S(2)}, u32[]{:S(2)}) %collective-permute-start.12) | collective-permute-done | bytes 98336 | tf_op jit(solution)/shard_map/ppermute | solution.py:305
  48.3 0.0 collective-permute-done.13.refs_6_
  48.3 2.7 %collective-permute-done.14.refs_7_ = bf16[32,1536]{1,0:T(8,128)(2,1)S(1)} collective-permute-done((bf16[32,1536]{1,0:T(8,128)(2,1)S(1)}, bf16[32,1536]{1,0:T(8,128)(2,1)S(1)}, u32[]{:S(2)}, u32[]{:S(2)}) %collective-permute-start.14) | collective-permute-done | bytes 98336 | tf_op jit(solution)/shard_map/ppermute | solution.py:305
  51.0 0.0 copy-done.2
  51.0 1.8 %shard_map.98 = bf16[256,1536]{1,0:T(8,128)(2,1)} custom-call(f32[256,1536]{1,0:T(8,128)S(1)} %shard_map.93.w_ref, bf16[256,1536]{1,0:T(8,128)(2,1)S(1)} %bitcast.9, f32[1,1536]{1,0:T(1,128)S(1)} %reshape.22.gain_ref, bf16[32,1536]{1,0:T(8,128)(2,1)S(1)} %get-tuple-element.27.refs_0_, bf16[32,1536]{1,0:T(8,128)(2,1)S(1)} %collective-permute-done.5.refs_1_, ...), custom_call_target="tpu_custom_call" | custom-call | flops 3932160 | bytes 3932160 | tf_op jit(solution)/shard_map/pallas_call | solution.py:348
  (1 shorter events, 0.0 us)
Async XLA Ops:
  0.7 1.1 %copy-start = (bf16[1,32,8,1536]{3,2,1,0:T(8,128)(2,1)S(1)}, bf16[1,32,8,1536]{3,2,1,0:T(8,128)(2,1)}, u32[]{:S(2)}) copy-start(bf16[1,32,8,1536]{3,2,1,0:T(8,128)(2,1)} %param.9) | copy-start | bytes 2359300
  1.8 0.8 %copy-start.3 = (bf16[1,32,8,48]{3,2,1,0:T(8,128)(2,1)S(1)}, bf16[1,32,8,48]{3,2,1,0:T(8,128)(2,1)}, u32[]{:S(2)}) copy-start(bf16[1,32,8,48]{3,2,1,0:T(8,128)(2,1)} %param.12) | copy-start | bytes 73732
  2.6 0.8 %copy-start.5 = (bf16[1,32,8,64]{3,2,1,0:T(8,128)(2,1)S(1)}, bf16[1,32,8,64]{3,2,1,0:T(8,128)(2,1)}, u32[]{:S(2)}) copy-start(bf16[1,32,8,64]{3,2,1,0:T(8,128)(2,1)} %param.11) | copy-start | bytes 98308
  3.5 0.9 %copy-start.7 = (f32[1000,48]{0,1:T(8,128)S(1)}, f32[1000,48]{0,1:T(8,128)}, u32[]{:S(2)}) copy-start(f32[1000,48]{0,1:T(8,128)} %param.14) | copy-start | bytes 576004
  4.5 12.4 %collective-permute-start.1 = (bf16[32,1664]{1,0:T(8,128)(2,1)S(1)}, bf16[32,1664]{1,0:T(8,128)(2,1)S(1)}, u32[]{:S(2)}, u32[]{:S(2)}) collective-permute-start(bf16[32,1664]{1,0:T(8,128)(2,1)S(1)} %get-tuple-element.24), channel_id=1, source_target_pairs={{0,2},{2,0},{4,6},{6,4},{8,10},{10,8},{12,14},{14,12},{1,3},{3,1},... | collective-permute-start | bytes 319496 | tf_op jit(solution)/shard_map/ppermute | solution.py:305
  7.6 11.0 %collective-permute-start.2 = (bf16[32,1664]{1,0:T(8,128)(2,1)S(1)}, bf16[32,1664]{1,0:T(8,128)(2,1)S(1)}, u32[]{:S(2)}, u32[]{:S(2)}) collective-permute-start(bf16[32,1664]{1,0:T(8,128)(2,1)S(1)} %get-tuple-element.25), channel_id=1, source_target_pairs={{0,4},{2,6},{4,0},{6,2},{8,12},{10,14},{12,8},{14,10},{1,5},{3,7},... | collective-permute-start | bytes 319496 | tf_op jit(solution)/shard_map/ppermute | solution.py:305
  9.1 9.8 %collective-permute-start.3 = (bf16[32,1664]{1,0:T(8,128)(2,1)S(1)}, bf16[32,1664]{1,0:T(8,128)(2,1)S(1)}, u32[]{:S(2)}, u32[]{:S(2)}) collective-permute-start(bf16[32,1664]{1,0:T(8,128)(2,1)S(1)} %get-tuple-element.26), channel_id=1, source_target_pairs={{0,6},{2,4},{4,2},{6,0},{8,14},{10,12},{12,10},{14,8},{1,7},{3,5},... | collective-permute-start | bytes 319496 | tf_op jit(solution)/shard_map/ppermute | solution.py:305
  9.2 0.7 %copy-start.8 = (f32[2,24]{1,0:T(2,128)S(1)}, f32[2,24]{1,0:T(2,128)}, u32[]{:S(2)}) copy-start(f32[2,24]{1,0:T(2,128)} %rates_ref.11) | copy-start | bytes 580
  11.4 34.1 %copy-start.10 = (f32[1536]{0:T(1024)S(1)}, f32[1536]{0:T(1024)}, u32[]{:S(2)}) copy-start(f32[1536]{0:T(1024)} %param.17) | copy-start | bytes 18436
  11.4 34.1 %copy-start.11 = (f32[24]{0:T(128)S(1)}, f32[24]{0:T(128)}, u32[]{:S(2)}) copy-start(f32[24]{0:T(128)} %param.16) | copy-start | bytes 292
  11.4 34.3 %copy-start.1 = (bf16[1,32,8,1536]{3,2,1,0:T(8,128)(2,1)S(1)}, bf16[1,32,8,1536]{3,2,1,0:T(8,128)(2,1)}, u32[]{:S(2)}) copy-start(bf16[1,32,8,1536]{3,2,1,0:T(8,128)(2,1)} %param.9) | copy-start | bytes 2359300
  11.4 34.2 %copy-start.4 = (bf16[1,32,8,48]{3,2,1,0:T(8,128)(2,1)S(1)}, bf16[1,32,8,48]{3,2,1,0:T(8,128)(2,1)}, u32[]{:S(2)}) copy-start(bf16[1,32,8,48]{3,2,1,0:T(8,128)(2,1)} %param.12) | copy-start | bytes 73732
  11.4 34.2 %copy-start.6 = (bf16[1,32,8,64]{3,2,1,0:T(8,128)(2,1)S(1)}, bf16[1,32,8,64]{3,2,1,0:T(8,128)(2,1)}, u32[]{:S(2)}) copy-start(bf16[1,32,8,64]{3,2,1,0:T(8,128)(2,1)} %param.11) | copy-start | bytes 98308
  11.5 34.2 %copy-start.9 = (f32[2,24]{1,0:T(2,128)S(1)}, f32[2,24]{1,0:T(2,128)}, u32[]{:S(2)}) copy-start(f32[2,24]{1,0:T(2,128)} %rates_ref.11) | copy-start | bytes 580
  11.5 32.0 %collective-permute-start = (bf16[128,1536]{1,0:T(8,128)(2,1)S(1)}, bf16[128,1536]{1,0:T(8,128)(2,1)S(1)}, u32[]{:S(2)}, u32[]{:S(2)}) collective-permute-start(bf16[128,1536]{1,0:T(8,128)(2,1)S(1)} %shard_map.92), channel_id=1, source_target_pairs={{0,16},{1,17},{2,18},{3,19},{4,20},{5,21},{6,22},{7,23},{8,24},{9,... | collective-permute-start | bytes 1179656 | tf_op jit(solution)/shard_map/ppermute | solution.py:254
  15.4 9.2 %collective-permute-start.8 = (bf16[32,1664]{1,0:T(8,128)(2,1)S(1)}, bf16[32,1664]{1,0:T(8,128)(2,1)S(1)}, u32[]{:S(2)}, u32[]{:S(2)}) collective-permute-start(bf16[32,1664]{1,0:T(8,128)(2,1)S(1)} %get-tuple-element.32), channel_id=1, source_target_pairs={{0,2},{2,0},{4,6},{6,4},{8,10},{10,8},{12,14},{14,12},{1,3},{3,1},... | collective-permute-start | bytes 319496 | tf_op jit(solution)/shard_map/ppermute | solution.py:305
  17.0 7.6 %collective-permute-start.9 = (bf16[32,1664]{1,0:T(8,128)(2,1)S(1)}, bf16[32,1664]{1,0:T(8,128)(2,1)S(1)}, u32[]{:S(2)}, u32[]{:S(2)}) collective-permute-start(bf16[32,1664]{1,0:T(8,128)(2,1)S(1)} %get-tuple-element.33), channel_id=1, source_target_pairs={{0,4},{2,6},{4,0},{6,2},{8,12},{10,14},{12,8},{14,10},{1,5},{3,7},... | collective-permute-start | bytes 319496 | tf_op jit(solution)/shard_map/ppermute | solution.py:305
  18.6 6.1 %collective-permute-start.10 = (bf16[32,1664]{1,0:T(8,128)(2,1)S(1)}, bf16[32,1664]{1,0:T(8,128)(2,1)S(1)}, u32[]{:S(2)}, u32[]{:S(2)}) collective-permute-start(bf16[32,1664]{1,0:T(8,128)(2,1)S(1)} %get-tuple-element.34), channel_id=1, source_target_pairs={{0,6},{2,4},{4,2},{6,0},{8,14},{10,12},{12,10},{14,8},{1,7},{3,5},... | collective-permute-start | bytes 319496 | tf_op jit(solution)/shard_map/ppermute | solution.py:305
  20.1 9.7 %collective-permute-start.4 = (bf16[64,1536]{1,0:T(8,128)(2,1)S(1)}, bf16[64,1536]{1,0:T(8,128)(2,1)S(1)}, u32[]{:S(2)}, u32[]{:S(2)}) collective-permute-start(bf16[64,1536]{1,0:T(8,128)(2,1)S(1)} %shard_map.94), channel_id=1, source_target_pairs={{0,8},{2,10},{4,12},{6,14},{1,9},{3,11},{5,13},{7,15},{16,24},{18,... | collective-permute-start | bytes 589832 | tf_op jit(solution)/shard_map/ppermute | solution.py:254
  25.7 14.9 %collective-permute-start.11 = (bf16[64,1536]{1,0:T(8,128)(2,1)S(1)}, bf16[64,1536]{1,0:T(8,128)(2,1)S(1)}, u32[]{:S(2)}, u32[]{:S(2)}) collective-permute-start(bf16[64,1536]{1,0:T(8,128)(2,1)S(1)} %shard_map.96), channel_id=1, source_target_pairs={{0,8},{2,10},{4,12},{6,14},{1,9},{3,11},{5,13},{7,15},{16,24},{18,... | collective-permute-start | bytes 589832 | tf_op jit(solution)/shard_map/ppermute | solution.py:254
  31.1 14.4 %collective-permute-start.5 = (bf16[32,1536]{1,0:T(8,128)(2,1)S(1)}, bf16[32,1536]{1,0:T(8,128)(2,1)S(1)}, u32[]{:S(2)}, u32[]{:S(2)}) collective-permute-start(bf16[32,1536]{1,0:T(8,128)(2,1)S(1)} %get-tuple-element.28), channel_id=1, source_target_pairs={{0,2},{2,0},{4,6},{6,4},{8,10},{10,8},{12,14},{14,12},{1,3},{3,1},... | collective-permute-start | bytes 294920 | tf_op jit(solution)/shard_map/ppermute | solution.py:305
  32.4 15.3 %collective-permute-start.6 = (bf16[32,1536]{1,0:T(8,128)(2,1)S(1)}, bf16[32,1536]{1,0:T(8,128)(2,1)S(1)}, u32[]{:S(2)}, u32[]{:S(2)}) collective-permute-start(bf16[32,1536]{1,0:T(8,128)(2,1)S(1)} %get-tuple-element.29), channel_id=1, source_target_pairs={{0,4},{2,6},{4,0},{6,2},{8,12},{10,14},{12,8},{14,10},{1,5},{3,7},... | collective-permute-start | bytes 294920 | tf_op jit(solution)/shard_map/ppermute | solution.py:305
  40.6 7.0 %collective-permute-start.7 = (bf16[32,1536]{1,0:T(8,128)(2,1)S(1)}, bf16[32,1536]{1,0:T(8,128)(2,1)S(1)}, u32[]{:S(2)}, u32[]{:S(2)}) collective-permute-start(bf16[32,1536]{1,0:T(8,128)(2,1)S(1)} %get-tuple-element.30), channel_id=1, source_target_pairs={{0,6},{2,4},{4,2},{6,0},{8,14},{10,12},{12,10},{14,8},{1,7},{3,5},... | collective-permute-start | bytes 294920 | tf_op jit(solution)/shard_map/ppermute | solution.py:305
  41.9 9.1 %copy-start.2 = (bf16[1,32,8,1536]{3,2,1,0:T(8,128)(2,1)S(1)}, bf16[1,32,8,1536]{3,2,1,0:T(8,128)(2,1)}, u32[]{:S(2)}) copy-start(bf16[1,32,8,1536]{3,2,1,0:T(8,128)(2,1)} %param.10) | copy-start | bytes 2359300
  41.9 6.3 %collective-permute-start.12 = (bf16[32,1536]{1,0:T(8,128)(2,1)S(1)}, bf16[32,1536]{1,0:T(8,128)(2,1)S(1)}, u32[]{:S(2)}, u32[]{:S(2)}) collective-permute-start(bf16[32,1536]{1,0:T(8,128)(2,1)S(1)} %get-tuple-element.36), channel_id=1, source_target_pairs={{0,2},{2,0},{4,6},{6,4},{8,10},{10,8},{12,14},{14,12},{1,3},{3,1},... | collective-permute-start | bytes 294920 | tf_op jit(solution)/shard_map/ppermute | solution.py:305
  43.4 4.8 %collective-permute-start.13 = (bf16[32,1536]{1,0:T(8,128)(2,1)S(1)}, bf16[32,1536]{1,0:T(8,128)(2,1)S(1)}, u32[]{:S(2)}, u32[]{:S(2)}) collective-permute-start(bf16[32,1536]{1,0:T(8,128)(2,1)S(1)} %get-tuple-element.37), channel_id=1, source_target_pairs={{0,4},{2,6},{4,0},{6,2},{8,12},{10,14},{12,8},{14,10},{1,5},{3,7},... | collective-permute-start | bytes 294920 | tf_op jit(solution)/shard_map/ppermute | solution.py:305
  45.5 5.5 %collective-permute-start.14 = (bf16[32,1536]{1,0:T(8,128)(2,1)S(1)}, bf16[32,1536]{1,0:T(8,128)(2,1)S(1)}, u32[]{:S(2)}, u32[]{:S(2)}) collective-permute-start(bf16[32,1536]{1,0:T(8,128)(2,1)S(1)} %get-tuple-element.38), channel_id=1, source_target_pairs={{0,6},{2,4},{4,2},{6,0},{8,14},{10,12},{12,10},{14,8},{1,7},{3,5},... | collective-permute-start | bytes 294920 | tf_op jit(solution)/shard_map/ppermute | solution.py:305

commit v3 on v2

--- a/solution.py
+++ b/solution.py
@@ -110,35 +110,53 @@
     return [(first, min(STRIP, channels - first)) for first in range(0, channels, STRIP)]
 
 
-def pack_kernel(index_ref, x_ref, raw_ref, maps_ref, table_ref, bias_ref, *sent, group, axis, heads, state):
+def pack_kernel(
+    index_ref, x_ref, raw_ref, maps_ref, table_ref, rates_ref, params_ref, *refs, group, axis, heads, state
+):
+    sent, (raw, maps, table, rates, sems) = refs[:-5], refs[-5:]
     member = mod(lax.axis_index(axis), group)
     pieces = len(sent) // group
     share = x_ref.shape[0] // group
     rows = share // pieces
     channels = x_ref.shape[1]
-    for s in range(group):
-        for piece in range(pieces):
+    small = [(raw_ref, raw), (maps_ref, maps), (table_ref, table), (rates_ref, rates)]
+    copies = [pltpu.make_async_copy(a, b, sems.at[i]) for i, (a, b) in enumerate(small)]
+    places = []
+    for piece in range(pieces):
+        for s in range(group):
             first = pl.multiple_of(jnp.bitwise_xor(member, s) * share + piece * rows, rows)
-            part = pl.ds(first, rows)
             out = sent[piece * group + s]
-            out[:, :channels] = x_ref[part, :]
-            used = heads + 2 * state
-            out[:, channels : channels + heads] = raw_ref[part, :heads]
-            out[:, channels + heads : channels + used] = maps_ref[part, : 2 * state]
-            out[:, channels + used :] = jnp.zeros((rows, LANES - used), BF16)
-    lanes = table_ref.shape[1]
-    mine = iota(table_ref.shape, 1) == mod(index_ref[0], lanes)
-    row = jnp.where(mine, table_ref[...], 0.0)
-    ones = jnp.ones((8, lanes), BF16)
-    total = jnp.zeros((8, row.shape[0]), F32)
+            places.append((out, pl.ds(first, rows)))
+            copies.append(
+                pltpu.make_async_copy(
+                    x_ref.at[pl.ds(first, rows), :], out.at[:, pl.ds(0, channels)], sems.at[len(copies)]
+                )
+            )
+    for copy in copies:
+        copy.start()
+    for copy in copies[: len(small)]:
+        copy.wait()
+    used = heads + 2 * state
+    for out, part in places:
+        out[:, channels : channels + heads] = raw[part, :heads]
+        out[:, channels + heads : channels + used] = maps[part, : 2 * state]
+        out[:, channels + used :] = jnp.zeros((rows, LANES - used), BF16)
+    row = jnp.where(iota(table.shape, 1) == index_ref[0], table[...], 0.0)
+    ones = jnp.ones((8, table.shape[1]), BF16)
+    bias = jnp.zeros((8, row.shape[0]), F32)
     for _ in range(3):
         term = row.astype(BF16)
         row = row - term.astype(F32)
-        total += lax.dot_general(ones, term, (((1,), (1,)), ((), ())), preferred_element_type=F32)
-    bias_ref[...] = total
-
-
-def row_scan(bias_ref, rates_ref, blocks, member, cols, heads, state):
+        bias += lax.dot_general(ones, term, (((1,), (1,)), ((), ())), preferred_element_type=F32)
+    params_ref[0:1, :] = bias[0:1, :]
+    params_ref[1:2, :heads] = rates[0:1, :]
+    params_ref[1:2, heads:] = rates[1:2, :]
+    params_ref[2:, :] = jnp.zeros((6, 2 * heads), F32)
+    for copy in copies[len(small) :]:
+        copy.wait()
+
+
+def row_scan(params_ref, blocks, member, cols, heads, state):
     channels = blocks[0].shape[1] - LANES
     tokens = blocks[0].shape[0] * len(blocks)
     lines = tokens // (cols * len(blocks))
@@ -147,20 +165,20 @@
         row_order(cols, lines, member),
         lines,
         aux[:, :heads],
-        bias_ref[0:1, :heads],
-        rates_ref[0:1, :],
+        params_ref[0:1, :heads],
+        params_ref[1:2, :heads],
         aux[:, heads : heads + state],
         aux[:, heads + state : heads + 2 * state],
     )
 
 
-def col_scan(bias_ref, rates_ref, raw_ref, maps_ref, cols, heads, state):
+def col_scan(params_ref, raw_ref, maps_ref, cols, heads, state):
     return Scan(
         column_order(cols),
         cols,
         raw_ref[:, heads:],
-        bias_ref[0:1, heads:],
-        rates_ref[1:2, :],
+        params_ref[0:1, heads:],
+        params_ref[1:2, heads:],
         maps_ref[:, 2 * state : 3 * state],
         maps_ref[:, 3 * state :],
     )
@@ -178,26 +196,26 @@
         s_ref[:, first : first + count] = (dot(into, values) * dot(ends, pick)).astype(BF16)
 
 
-def row_state_kernel(bias_ref, rates_ref, *refs, group, axis, cols, heads, state, width):
-    blocks, s_ref, factor_ref = refs[:group], refs[group], refs[group + 1 :]
+def row_state_kernel(params_ref, *refs, group, axis, cols, heads, state, width):
+    blocks, s_ref, factor_ref = refs[:group], refs[group + 1], refs[group + 2 :]
     member = mod(lax.axis_index(axis), group)
-    scan = row_scan(bias_ref, rates_ref, blocks, member, cols, heads, state)
+    scan = row_scan(params_ref, blocks, member, cols, heads, state)
     tokens_of = lambda first, count: jnp.concatenate(
         [block[:, first : first + count] for block in blocks], axis=0
     ).astype(F32)
     write_state(scan, tokens_of, width, s_ref.shape[1], s_ref, factor_ref)
 
 
-def col_state_kernel(bias_ref, rates_ref, x_ref, raw_ref, maps_ref, s_ref, *factor_ref, cols, heads, state, width):
-    scan = col_scan(bias_ref, rates_ref, raw_ref, maps_ref, cols, heads, state)
+def col_state_kernel(params_ref, x_ref, raw_ref, maps_ref, _, s_ref, *factor_ref, cols, heads, state, width):
+    scan = col_scan(params_ref, raw_ref, maps_ref, cols, heads, state)
     tokens_of = lambda first, count: x_ref[:, first : first + count].astype(F32)
     write_state(scan, tokens_of, width, s_ref.shape[1], s_ref, factor_ref)
 
 
-def row_out_kernel(bias_ref, rates_ref, s_ref, *refs, group, axis, cols, heads, state, width):
-    blocks, outs = refs[:group], refs[group:]
+def row_out_kernel(params_ref, s_ref, *refs, group, axis, cols, heads, state, width):
+    blocks, outs = refs[:group], refs[group + 1 :]
     member = mod(lax.axis_index(axis), group)
-    scan = row_scan(bias_ref, rates_ref, blocks, member, cols, heads, state)
+    scan = row_scan(params_ref, blocks, member, cols, heads, state)
     mix = scan.mix()
     rows = blocks[0].shape[0]
     for first, count in strips(s_ref.shape[1]):
@@ -210,8 +228,8 @@
             outs[s][:, part] = y[s * rows : (s + 1) * rows].astype(BF16)
 
 
-def col_out_kernel(bias_ref, rates_ref, s_ref, x_ref, raw_ref, maps_ref, skip_ref, w_ref, *, cols, heads, state, width):
-    scan = col_scan(bias_ref, rates_ref, raw_ref, maps_ref, cols, heads, state)
+def col_out_kernel(params_ref, s_ref, x_ref, raw_ref, maps_ref, skip_ref, w_ref, *, cols, heads, state, width):
+    scan = col_scan(params_ref, raw_ref, maps_ref, cols, heads, state)
     mix = scan.mix()
     for first, count in strips(s_ref.shape[1]):
         pick = picks(heads, width, first, count)
@@ -237,12 +255,18 @@
             out_ref[part, :] = (v * lax.rsqrt(power + 1e-5) * gain_ref[...]).astype(BF16)
 
 
-def call(kernel, out_shape, flops, moved):
+SMALL = pl.CostEstimate(flops=1024, bytes_accessed=1024, transcendentals=0)
+LONG = pl.CostEstimate(flops=2 * 10**10, bytes_accessed=1024, transcendentals=0)
+
+
+def call(kernel, out_shape, specs=None, cost=SMALL):
+    more = {} if specs is None else dict(in_specs=[spec or pl.BlockSpec() for spec in specs])
     return pl.pallas_call(
         kernel,
+        **more,
         out_shape=out_shape,
         compiler_params=pltpu.CompilerParams(vmem_limit_bytes=32 * 1024 * 1024),
-        cost_estimate=pl.CostEstimate(flops=flops, bytes_accessed=moved, transcendentals=0),
+        cost_estimate=cost,
     )
 
 
@@ -280,25 +304,29 @@
     shared = dict(group=group, axis="col")
     shape = jax.ShapeDtypeStruct
 
+    any_spec = pl.BlockSpec(memory_space=pl.ANY)
+    hbm_spec = pl.BlockSpec(memory_space=pltpu.HBM)
     full = lambda *dims: pl.BlockSpec(dims, lambda i, index: (0,) * len(dims))
     packed = pl.pallas_call(
         functools.partial(pack_kernel, heads=heads, state=state, **shared),
         grid_spec=pltpu.PrefetchScalarGridSpec(
             num_scalar_prefetch=1,
             grid=(1,),
-            in_specs=[
-                full(tokens, channels),
-                full(tokens, 2 * heads),
-                full(tokens, 4 * state),
-                pl.BlockSpec((2 * heads, LANES), lambda i, index: (0, index[0] // LANES)),
+            in_specs=[hbm_spec] * 5,
+            out_specs=[full(8, 2 * heads)] + [full(share, channels + LANES)] * (group * PIECES),
+            scratch_shapes=[
+                pltpu.VMEM(raw.shape, BF16),
+                pltpu.VMEM(maps.shape, BF16),
+                pltpu.VMEM(step_table.shape[::-1], F32),
+                pltpu.VMEM(rates.shape, F32),
+                pltpu.SemaphoreType.DMA((4 + group * PIECES,)),
             ],
-            out_specs=[full(8, 2 * heads)] + [full(share, channels + LANES)] * (group * PIECES),
         ),
-        out_shape=[shape((8, 2 * heads), F32)] + [shape((share, channels + LANES), BF16)] * (group * PIECES),
+        out_shape=[pltpu.VMEM((8, 2 * heads), F32)] + [pltpu.VMEM((share, channels + LANES), BF16)] * (group * PIECES),
         compiler_params=pltpu.CompilerParams(vmem_limit_bytes=32 * 1024 * 1024),
-        cost_estimate=pl.CostEstimate(flops=0, bytes_accessed=4 * tokens * channels, transcendentals=0),
-    )(step_index, x, raw, maps, step_table.T)
-    bias, packed = packed[0], packed[1:]
+        cost_estimate=SMALL,
+    )(step_index, *[pltpu.with_memory_space_constraint(a, pltpu.HBM) for a in (x, raw, maps, step_table.T, rates)])
+    params, packed = packed[0], packed[1:]
 
     def exchange(blocks):
         return [blocks[0]] + [
@@ -310,46 +338,43 @@
 
     got = [exchange(packed[piece * group : (piece + 1) * group]) for piece in range(PIECES)]
 
-    col_made = call(
-        functools.partial(col_state_kernel, **sizes),
-        state_shapes(cols * state, row_count),
-        2 * cols * state * tokens * channels,
-        2 * tokens * channels,
-    )(bias, rates, x, raw, maps)
-    col_entering = entering_states(col_made, "row", row_count, 1, width)
-
     row_entering = []
+    row_made = params
     for piece in range(PIECES):
         made = call(
             functools.partial(row_state_kernel, **sizes, **shared),
             state_shapes(lines * state, col_count // group),
-            2 * lines * state * group * share * channels,
-            2 * group * share * channels,
-        )(bias, rates, *got[piece])
+            specs=[None] * (1 + group) + [any_spec],
+        )(params, *got[piece], row_made)
+        row_made = made[0]
         row_entering.append(entering_states(made, "col", col_count, group, width))
+
+    col_made = call(
+        functools.partial(col_state_kernel, **sizes),
+        state_shapes(cols * state, row_count),
+            specs=[None] * 4 + [any_spec],
+    )(params, x, raw, maps, row_made)
+    col_entering = entering_states(col_made, "row", row_count, 1, width)
 
     w = call(
         functools.partial(col_out_kernel, **sizes),
         shape((tokens, channels), F32),
-        2 * tokens * tokens * channels,
-        8 * tokens * channels,
-    )(bias, rates, col_entering, x, raw, maps, jnp.repeat(skip, width).reshape(1, channels))
+    )(params, col_entering, x, raw, maps, jnp.repeat(skip, width).reshape(1, channels))
 
     back = []
+    y_row = [params]
     for piece in range(PIECES):
         y_row = call(
             functools.partial(row_out_kernel, **sizes, **shared),
             [shape((share, channels), BF16)] * group,
-            2 * (group * share) ** 2 * channels,
-            4 * group * share * channels,
-        )(bias, rates, row_entering[piece], *got[piece])
+            specs=[None] * (2 + group) + [any_spec],
+            cost=LONG if piece == PIECES - 1 else SMALL,
+        )(params, row_entering[piece], *got[piece], y_row[0])
         back += exchange(y_row)
 
     mixed = call(
         functools.partial(final_kernel, **shared),
         shape((tokens, channels), BF16),
-        10 * tokens * channels,
-        10 * tokens * channels,
     )(w, gate, norm_gain.reshape(1, channels), *back)
     return mixed.reshape(x_in.shape)
 

time: 53.1 us -> 47.3 us (0.89)
  starting transfers between devices: 33.8 us -> 28.5 us
  local copies, waits for them, and re-layouts: 4.61 us -> 0.18 us
  waiting for transfers between devices: 3.34 us -> 6.19 us
  Pallas kernels: 10.1 us -> 11.3 us
    unnamed x24 -> x12, local copies, waits for them, and re-layouts: 4.46 us -> 0.03 us
    ppermute x12, waiting for transfers between devices: 3.33 us -> 6.18 us  [exchange(): lax.ppermute(blocks[s], 'col', [(i, i ^ s) for i in range(col_count)])]
    ppermute x3, starting transfers between devices: 12.5 us -> 9.79 us  [entering_states(): entering = lax.ppermute(ends, axis, onward)]
    ppermute x12, starting transfers between devices: 21.3 us -> 18.7 us  [exchange(): lax.ppermute(blocks[s], 'col', [(i, i ^ s) for i in range(col_count)])]
    pallas_call x1, Pallas kernels: 0.14 us -> 1.43 us  [body(): pl.pallas_call(functools.partial(pack_kernel, heads=heads, state=state, *...]
  transfers between devices with their start and end apart: 15 -> 15, of which waited for: 2 -> 4; matrix products, arithmetic and copies ran while one was open for 0% -> 0% of each run, Pallas kernels for 16% -> 17%
where the time goes in v3:
time: 47.3 us; the launch traced here: 47.1 us
  starting transfers between devices  28.5 us (60%)
  Pallas kernels  11.3 us (24%)
  waiting for transfers between devices  6.19 us (13%)
  between operations  0.93 us (2%)
    ppermute x12, starting transfers between devices, exchange(): lax.ppermute(blocks[s], 'col', [(i, i ^ s) for i in range(col_count)])  18.7 us
    ppermute x3, starting transfers between devices, entering_states(): entering = lax.ppermute(ends, axis, onward)  9.79 us
    ppermute x12, waiting for transfers between devices, exchange(): lax.ppermute(blocks[s], 'col', [(i, i ^ s) for i in range(col_count)])  6.18 us
    pallas_call x2, Pallas kernels, body(): call(functools.partial(row_out_kernel, **sizes, **shared), [shape((share,...  2.51 us
    pallas_call x2, Pallas kernels, body(): call(functools.partial(row_state_kernel, **sizes, **shared), state_shapes...  2.2 us
    pallas_call x1, Pallas kernels, body(): call(functools.partial(col_out_kernel, **sizes), shape((tokens, channels)...  1.89 us
    pallas_call x1, Pallas kernels, body(): call(functools.partial(final_kernel, **shared), shape((tokens, channels),...  1.76 us
    pallas_call x1, Pallas kernels, body(): call(functools.partial(col_state_kernel, **sizes), state_shapes(cols * st...  1.49 us
  transfers between devices with their start and end apart: 15, of which 4 were waited for; matrix products, arithmetic and copies ran while one was open for 0% of the time, Pallas kernels for 17%

profile of v3, /device:TPU:0, one launch (start us, length us, event | category | flops | bytes accessed | tf_op | source)
XLA Modules:
  0.0 47.1 jit_solution(5734524087618976628)
XLA Ops:
  0.0 0.0 copy-start.2
  0.0 0.0 copy-start.3
  0.0 0.0 copy-start
  0.7 1.4 %shard_map.91 = (f32[8,48]{1,0:T(8,128)S(1)}, bf16[32,1664]{1,0:T(8,128)(2,1)S(1)}, bf16[32,1664]{1,0:T(8,128)(2,1)S(1)}, bf16[32,1664]{1,0:T(8,128)(2,1)S(1)}, ...) custom-call(s32[1]{0:T(128)S(6)} %copy.10.index_ref, ...), custom_call_target="tpu_custom_call" | custom-call | flops 1024 | bytes 1024 | tf_op jit(solution)/shard_map/pallas_call | solution.py:310
  2.2 3.0 %collective-permute-start.3 = (bf16[32,1664]{1,0:T(8,128)(2,1)S(1)}, bf16[32,1664]{1,0:T(8,128)(2,1)S(1)}, u32[]{:S(2)}, u32[]{:S(2)}) collective-permute-start(bf16[32,1664]{1,0:T(8,128)(2,1)S(1)} %get-tuple-element.28), channel_id=1, source_target_pairs={{0,2},{2,0},{4,6},{6,4},{8,10},{10,8},{12,14},{14,12},{1,3},{3,1},... | collective-permute-start | bytes 319496 | tf_op jit(solution)/shard_map/ppermute | solution.py:333
  5.2 1.6 %collective-permute-start.4 = (bf16[32,1664]{1,0:T(8,128)(2,1)S(1)}, bf16[32,1664]{1,0:T(8,128)(2,1)S(1)}, u32[]{:S(2)}, u32[]{:S(2)}) collective-permute-start(bf16[32,1664]{1,0:T(8,128)(2,1)S(1)} %get-tuple-element.29), channel_id=1, source_target_pairs={{0,4},{2,6},{4,0},{6,2},{8,12},{10,14},{12,8},{14,10},{1,5},{3,7},... | collective-permute-start | bytes 319496 | tf_op jit(solution)/shard_map/ppermute | solution.py:333
  6.8 0.0 collective-permute-start.5
  6.8 1.9 %collective-permute-start = (bf16[32,1664]{1,0:T(8,128)(2,1)S(1)}, bf16[32,1664]{1,0:T(8,128)(2,1)S(1)}, u32[]{:S(2)}, u32[]{:S(2)}) collective-permute-start(bf16[32,1664]{1,0:T(8,128)(2,1)S(1)} %get-tuple-element.24), channel_id=1, source_target_pairs={{0,2},{2,0},{4,6},{6,4},{8,10},{10,8},{12,14},{14,12},{1,3},{3,1},... | collective-permute-start | bytes 319496 | tf_op jit(solution)/shard_map/ppermute | solution.py:333
  8.7 1.6 %collective-permute-start.1 = (bf16[32,1664]{1,0:T(8,128)(2,1)S(1)}, bf16[32,1664]{1,0:T(8,128)(2,1)S(1)}, u32[]{:S(2)}, u32[]{:S(2)}) collective-permute-start(bf16[32,1664]{1,0:T(8,128)(2,1)S(1)} %get-tuple-element.25), channel_id=1, source_target_pairs={{0,4},{2,6},{4,0},{6,2},{8,12},{10,14},{12,8},{14,10},{1,5},{3,7},... | collective-permute-start | bytes 319496 | tf_op jit(solution)/shard_map/ppermute | solution.py:333
  10.3 0.0 collective-permute-done.3.refs_1_
  10.3 0.7 %collective-permute-start.2 = (bf16[32,1664]{1,0:T(8,128)(2,1)S(1)}, bf16[32,1664]{1,0:T(8,128)(2,1)S(1)}, u32[]{:S(2)}, u32[]{:S(2)}) collective-permute-start(bf16[32,1664]{1,0:T(8,128)(2,1)S(1)} %get-tuple-element.26), channel_id=1, source_target_pairs={{0,6},{2,4},{4,2},{6,0},{8,14},{10,12},{12,10},{14,8},{1,7},{3,5},... | collective-permute-start | bytes 319496 | tf_op jit(solution)/shard_map/ppermute | solution.py:333
  10.9 0.1 collective-permute-done.4.refs_2_
  11.1 2.6 %collective-permute-done.5.refs_3_ = bf16[32,1664]{1,0:T(8,128)(2,1)S(1)} collective-permute-done((bf16[32,1664]{1,0:T(8,128)(2,1)S(1)}, bf16[32,1664]{1,0:T(8,128)(2,1)S(1)}, u32[]{:S(2)}, u32[]{:S(2)}) %collective-permute-start.5) | collective-permute-done | bytes 106528 | tf_op jit(solution)/shard_map/ppermute | solution.py:333
  13.7 1.1 %shard_map.92.refs_4_ = bf16[64,1536]{1,0:T(8,128)(2,1)S(1)} custom-call(f32[8,48]{1,0:T(8,128)S(1)} %get-tuple-element.22.params_ref.refs_4_, bf16[32,1664]{1,0:T(8,128)(2,1)S(1)} %get-tuple-element.27.refs_0_, bf16[32,1664]{1,0:T(8,128)(2,1)S(1)} %collective-permute-done.3.refs_1_, bf16[32,1664]{1,0:T(8,128)(2,1)S(1)} %collective-permute-done.4.refs_2_, ...), custom_call_target="tpu_custom_call" | custom-call | flops 1024 | bytes 1024 | tf_op jit(solution)/shard_map/pallas_call | solution.py:344
  14.8 4.5 %collective-permute-start.7 = (bf16[64,1536]{1,0:T(8,128)(2,1)S(1)}, bf16[64,1536]{1,0:T(8,128)(2,1)S(1)}, u32[]{:S(2)}, u32[]{:S(2)}) collective-permute-start(bf16[64,1536]{1,0:T(8,128)(2,1)S(1)} %shard_map.92.refs_4_), channel_id=1, source_target_pairs={{0,8},{2,10},{4,12},{6,14},{1,9},{3,11},{5,13},{7,15},{16,24},{18,... | collective-permute-start | bytes 589832 | tf_op jit(solution)/shard_map/ppermute | solution.py:278
  19.3 0.0 collective-permute-done.refs_1_
  19.3 0.0 collective-permute-done.1.refs_2_
  19.3 0.0 collective-permute-done.2.refs_3_
  19.3 1.1 %shard_map.93._ = bf16[64,1536]{1,0:T(8,128)(2,1)S(1)} custom-call(f32[8,48]{1,0:T(8,128)S(1)} %get-tuple-element.22.params_ref.refs_4_, bf16[32,1664]{1,0:T(8,128)(2,1)S(1)} %get-tuple-element.23.refs_0_, bf16[32,1664]{1,0:T(8,128)(2,1)S(1)} %collective-permute-done.refs_1_, bf16[32,1664]{1,0:T(8,128)(2,1)S(1)} %collective-permute-done.1.refs_2_, ...), custom_call_target="tpu_custom_call" | custom-call | flops 1024 | bytes 1024 | tf_op jit(solution)/shard_map/pallas_call | solution.py:344
  20.4 1.9 %collective-permute-start.11 = (bf16[64,1536]{1,0:T(8,128)(2,1)S(1)}, bf16[64,1536]{1,0:T(8,128)(2,1)S(1)}, u32[]{:S(2)}, u32[]{:S(2)}) collective-permute-start(bf16[64,1536]{1,0:T(8,128)(2,1)S(1)} %shard_map.93._), channel_id=1, source_target_pairs={{0,8},{2,10},{4,12},{6,14},{1,9},{3,11},{5,13},{7,15},{16,24},{18,... | collective-permute-start | bytes 589832 | tf_op jit(solution)/shard_map/ppermute | solution.py:278
  22.3 0.0 copy-done.2
  22.3 0.0 copy-done.3
  22.4 0.0 copy-done
  22.4 1.5 %shard_map.94 = bf16[128,1536]{1,0:T(8,128)(2,1)S(1)} custom-call(f32[8,48]{1,0:T(8,128)S(1)} %get-tuple-element.22.params_ref.refs_4_, bf16[256,1536]{1,0:T(8,128)(2,1)S(1)} %bitcast.7, bf16[256,48]{1,0:T(8,128)(2,1)S(1)} %bitcast.11, bf16[256,64]{1,0:T(8,128)(2,1)S(1)} %bitcast.14, bf16[64,1536]{1,0:T(8,128)(2,1)S(1)} %shard_map.93._), custom_call_target="tpu_custom_call" | custom-call | flops 1024 | bytes 1024 | tf_op jit(solution)/shard_map/pallas_call | solution.py:352
  23.9 3.4 %collective-permute-start.6 = (bf16[128,1536]{1,0:T(8,128)(2,1)S(1)}, bf16[128,1536]{1,0:T(8,128)(2,1)S(1)}, u32[]{:S(2)}, u32[]{:S(2)}) collective-permute-start(bf16[128,1536]{1,0:T(8,128)(2,1)S(1)} %shard_map.94), channel_id=1, source_target_pairs={{0,16},{1,17},{2,18},{3,19},{4,20},{5,21},{6,22},{7,23},{8,24},{9,... | collective-permute-start | bytes 1179656 | tf_op jit(solution)/shard_map/ppermute | solution.py:278
  27.3 0.0 collective-permute-done.7.s_ref
  27.3 1.3 %shard_map.96 = (bf16[32,1536]{1,0:T(8,128)(2,1)S(1)}, bf16[32,1536]{1,0:T(8,128)(2,1)S(1)}, bf16[32,1536]{1,0:T(8,128)(2,1)S(1)}, bf16[32,1536]{1,0:T(8,128)(2,1)S(1)}) custom-call(f32[8,48]{1,0:T(8,128)S(1)} %get-tuple-element.22.params_ref.refs_4_, bf16[64,1536]{1,0:T(8,128)(2,1)S(1)} %collective-permute-done.7.s_ref, ...), custom_call_target="tpu_custom_call" | custom-call | flops 1024 | bytes 1024 | tf_op jit(solution)/shard_map/pallas_call | solution.py:367
  28.5 1.4 %collective-permute-start.8 = (bf16[32,1536]{1,0:T(8,128)(2,1)S(1)}, bf16[32,1536]{1,0:T(8,128)(2,1)S(1)}, u32[]{:S(2)}, u32[]{:S(2)}) collective-permute-start(bf16[32,1536]{1,0:T(8,128)(2,1)S(1)} %get-tuple-element.32), channel_id=1, source_target_pairs={{0,2},{2,0},{4,6},{6,4},{8,10},{10,8},{12,14},{14,12},{1,3},{3,1},... | collective-permute-start | bytes 294920 | tf_op jit(solution)/shard_map/ppermute | solution.py:333
  29.9 5.0 %collective-permute-start.9 = (bf16[32,1536]{1,0:T(8,128)(2,1)S(1)}, bf16[32,1536]{1,0:T(8,128)(2,1)S(1)}, u32[]{:S(2)}, u32[]{:S(2)}) collective-permute-start(bf16[32,1536]{1,0:T(8,128)(2,1)S(1)} %get-tuple-element.33), channel_id=1, source_target_pairs={{0,4},{2,6},{4,0},{6,2},{8,12},{10,14},{12,8},{14,10},{1,5},{3,7},... | collective-permute-start | bytes 294920 | tf_op jit(solution)/shard_map/ppermute | solution.py:333
  35.0 0.0 collective-permute-start.10
  35.0 0.0 collective-permute-done.11.s_ref
  35.0 0.0 copy-start.5
  35.0 0.0 copy-start.4
  35.0 1.3 %shard_map.97 = (bf16[32,1536]{1,0:T(8,128)(2,1)S(1)}, bf16[32,1536]{1,0:T(8,128)(2,1)S(1)}, bf16[32,1536]{1,0:T(8,128)(2,1)S(1)}, bf16[32,1536]{1,0:T(8,128)(2,1)S(1)}) custom-call(f32[8,48]{1,0:T(8,128)S(1)} %get-tuple-element.22.params_ref.refs_4_, bf16[64,1536]{1,0:T(8,128)(2,1)S(1)} %collective-permute-done.11.s_ref, ...), custom_call_target="tpu_custom_call" | custom-call | flops 20000000000 | bytes 1024 | tf_op jit(solution)/shard_map/pallas_call | solution.py:367
  36.3 0.0 copy-start.1
  36.3 1.5 %collective-permute-start.12 = (bf16[32,1536]{1,0:T(8,128)(2,1)S(1)}, bf16[32,1536]{1,0:T(8,128)(2,1)S(1)}, u32[]{:S(2)}, u32[]{:S(2)}) collective-permute-start(bf16[32,1536]{1,0:T(8,128)(2,1)S(1)} %get-tuple-element.36), channel_id=1, source_target_pairs={{0,2},{2,0},{4,6},{6,4},{8,10},{10,8},{12,14},{14,12},{1,3},{3,1},... | collective-permute-start | bytes 294920 | tf_op jit(solution)/shard_map/ppermute | solution.py:333
  37.8 0.0 collective-permute-done.8.refs_1_
  37.8 2.0 %collective-permute-start.13 = (bf16[32,1536]{1,0:T(8,128)(2,1)S(1)}, bf16[32,1536]{1,0:T(8,128)(2,1)S(1)}, u32[]{:S(2)}, u32[]{:S(2)}) collective-permute-start(bf16[32,1536]{1,0:T(8,128)(2,1)S(1)} %get-tuple-element.37), channel_id=1, source_target_pairs={{0,4},{2,6},{4,0},{6,2},{8,12},{10,14},{12,8},{14,10},{1,5},{3,7},... | collective-permute-start | bytes 294920 | tf_op jit(solution)/shard_map/ppermute | solution.py:333
  39.8 0.0 collective-permute-done.6.s_ref
  39.8 0.0 collective-permute-start.14
  39.9 0.0 copy-done.5
  39.9 0.1 broadcast_in_dim.3
  39.9 0.1 reshape_reshape.3.skip_ref
  40.0 0.0 copy-done.4
  40.0 1.9 %shard_map.95.w_ref = f32[256,1536]{1,0:T(8,128)S(1)} custom-call(f32[8,48]{1,0:T(8,128)S(1)} %get-tuple-element.22.params_ref.refs_4_, bf16[128,1536]{1,0:T(8,128)(2,1)S(1)} %collective-permute-done.6.s_ref, bf16[256,1536]{1,0:T(8,128)(2,1)S(1)} %bitcast.8, bf16[256,48]{1,0:T(8,128)(2,1)S(1)} %bitcast.12, bf16[256,64]{1,0:T(8,128)(2,1)S(1)} %bitcast.15, ...), custom_call_target="tpu_custom_call" | custom-call | flops 1024 | bytes 1024 | tf_op jit(solution)/shard_map/pallas_call | solution.py:359
  41.9 0.0 collective-permute-done.9.refs_2_
  41.9 0.0 collective-permute-done.10.refs_3_
  41.9 0.0 collective-permute-done.12.refs_5_
  42.0 0.5 %collective-permute-done.13.refs_6_ = bf16[32,1536]{1,0:T(8,128)(2,1)S(1)} collective-permute-done((bf16[32,1536]{1,0:T(8,128)(2,1)S(1)}, bf16[32,1536]{1,0:T(8,128)(2,1)S(1)}, u32[]{:S(2)}, u32[]{:S(2)}) %collective-permute-start.13) | collective-permute-done | bytes 98336 | tf_op jit(solution)/shard_map/ppermute | solution.py:333
  42.4 2.9 %collective-permute-done.14.refs_7_ = bf16[32,1536]{1,0:T(8,128)(2,1)S(1)} collective-permute-done((bf16[32,1536]{1,0:T(8,128)(2,1)S(1)}, bf16[32,1536]{1,0:T(8,128)(2,1)S(1)}, u32[]{:S(2)}, u32[]{:S(2)}) %collective-permute-start.14) | collective-permute-done | bytes 98336 | tf_op jit(solution)/shard_map/ppermute | solution.py:333
  45.3 0.0 copy-done.1
  45.4 1.8 %shard_map.98 = bf16[256,1536]{1,0:T(8,128)(2,1)} custom-call(f32[256,1536]{1,0:T(8,128)S(1)} %shard_map.95.w_ref, bf16[256,1536]{1,0:T(8,128)(2,1)S(1)} %bitcast.9, f32[1,1536]{1,0:T(1,128)S(1)} %reshape.22.gain_ref, bf16[32,1536]{1,0:T(8,128)(2,1)S(1)} %get-tuple-element.31.refs_4_.refs_0_, bf16[32,1536]{1,0:T(8,128)(2,1)S(1)} %collective-permute-done.8.refs_1_, ...), custom_call_target="tpu_custom_call" | custom-call | flops 1024 | bytes 1024 | tf_op jit(solution)/shard_map/pallas_call | solution.py:375
  (1 shorter events, 0.0 us)
Async XLA Ops:
  0.0 22.3 %copy-start.2 = (bf16[1,32,8,48]{3,2,1,0:T(8,128)(2,1)S(1)}, bf16[1,32,8,48]{3,2,1,0:T(8,128)(2,1)}, u32[]{:S(2)}) copy-start(bf16[1,32,8,48]{3,2,1,0:T(8,128)(2,1)} %param.12) | copy-start | bytes 73732
  0.0 22.3 %copy-start.3 = (bf16[1,32,8,64]{3,2,1,0:T(8,128)(2,1)S(1)}, bf16[1,32,8,64]{3,2,1,0:T(8,128)(2,1)}, u32[]{:S(2)}) copy-start(bf16[1,32,8,64]{3,2,1,0:T(8,128)(2,1)} %param.11) | copy-start | bytes 98308
  0.0 22.4 %copy-start = (bf16[1,32,8,1536]{3,2,1,0:T(8,128)(2,1)S(1)}, bf16[1,32,8,1536]{3,2,1,0:T(8,128)(2,1)}, u32[]{:S(2)}) copy-start(bf16[1,32,8,1536]{3,2,1,0:T(8,128)(2,1)} %param.9) | copy-start | bytes 2359300
  2.2 8.1 %collective-permute-start.3 = (bf16[32,1664]{1,0:T(8,128)(2,1)S(1)}, bf16[32,1664]{1,0:T(8,128)(2,1)S(1)}, u32[]{:S(2)}, u32[]{:S(2)}) collective-permute-start(bf16[32,1664]{1,0:T(8,128)(2,1)S(1)} %get-tuple-element.28), channel_id=1, source_target_pairs={{0,2},{2,0},{4,6},{6,4},{8,10},{10,8},{12,14},{14,12},{1,3},{3,1},... | collective-permute-start | bytes 319496 | tf_op jit(solution)/shard_map/ppermute | solution.py:333
  5.2 5.8 %collective-permute-start.4 = (bf16[32,1664]{1,0:T(8,128)(2,1)S(1)}, bf16[32,1664]{1,0:T(8,128)(2,1)S(1)}, u32[]{:S(2)}, u32[]{:S(2)}) collective-permute-start(bf16[32,1664]{1,0:T(8,128)(2,1)S(1)} %get-tuple-element.29), channel_id=1, source_target_pairs={{0,4},{2,6},{4,0},{6,2},{8,12},{10,14},{12,8},{14,10},{1,5},{3,7},... | collective-permute-start | bytes 319496 | tf_op jit(solution)/shard_map/ppermute | solution.py:333
  6.8 6.9 %collective-permute-start.5 = (bf16[32,1664]{1,0:T(8,128)(2,1)S(1)}, bf16[32,1664]{1,0:T(8,128)(2,1)S(1)}, u32[]{:S(2)}, u32[]{:S(2)}) collective-permute-start(bf16[32,1664]{1,0:T(8,128)(2,1)S(1)} %get-tuple-element.30), channel_id=1, source_target_pairs={{0,6},{2,4},{4,2},{6,0},{8,14},{10,12},{12,10},{14,8},{1,7},{3,5},... | collective-permute-start | bytes 319496 | tf_op jit(solution)/shard_map/ppermute | solution.py:333
  6.8 12.5 %collective-permute-start = (bf16[32,1664]{1,0:T(8,128)(2,1)S(1)}, bf16[32,1664]{1,0:T(8,128)(2,1)S(1)}, u32[]{:S(2)}, u32[]{:S(2)}) collective-permute-start(bf16[32,1664]{1,0:T(8,128)(2,1)S(1)} %get-tuple-element.24), channel_id=1, source_target_pairs={{0,2},{2,0},{4,6},{6,4},{8,10},{10,8},{12,14},{14,12},{1,3},{3,1},... | collective-permute-start | bytes 319496 | tf_op jit(solution)/shard_map/ppermute | solution.py:333
  8.7 10.6 %collective-permute-start.1 = (bf16[32,1664]{1,0:T(8,128)(2,1)S(1)}, bf16[32,1664]{1,0:T(8,128)(2,1)S(1)}, u32[]{:S(2)}, u32[]{:S(2)}) collective-permute-start(bf16[32,1664]{1,0:T(8,128)(2,1)S(1)} %get-tuple-element.25), channel_id=1, source_target_pairs={{0,4},{2,6},{4,0},{6,2},{8,12},{10,14},{12,8},{14,10},{1,5},{3,7},... | collective-permute-start | bytes 319496 | tf_op jit(solution)/shard_map/ppermute | solution.py:333
  10.3 9.0 %collective-permute-start.2 = (bf16[32,1664]{1,0:T(8,128)(2,1)S(1)}, bf16[32,1664]{1,0:T(8,128)(2,1)S(1)}, u32[]{:S(2)}, u32[]{:S(2)}) collective-permute-start(bf16[32,1664]{1,0:T(8,128)(2,1)S(1)} %get-tuple-element.26), channel_id=1, source_target_pairs={{0,6},{2,4},{4,2},{6,0},{8,14},{10,12},{12,10},{14,8},{1,7},{3,5},... | collective-permute-start | bytes 319496 | tf_op jit(solution)/shard_map/ppermute | solution.py:333
  14.8 12.5 %collective-permute-start.7 = (bf16[64,1536]{1,0:T(8,128)(2,1)S(1)}, bf16[64,1536]{1,0:T(8,128)(2,1)S(1)}, u32[]{:S(2)}, u32[]{:S(2)}) collective-permute-start(bf16[64,1536]{1,0:T(8,128)(2,1)S(1)} %shard_map.92.refs_4_), channel_id=1, source_target_pairs={{0,8},{2,10},{4,12},{6,14},{1,9},{3,11},{5,13},{7,15},{16,24},{18,... | collective-permute-start | bytes 589832 | tf_op jit(solution)/shard_map/ppermute | solution.py:278
  20.4 14.6 %collective-permute-start.11 = (bf16[64,1536]{1,0:T(8,128)(2,1)S(1)}, bf16[64,1536]{1,0:T(8,128)(2,1)S(1)}, u32[]{:S(2)}, u32[]{:S(2)}) collective-permute-start(bf16[64,1536]{1,0:T(8,128)(2,1)S(1)} %shard_map.93._), channel_id=1, source_target_pairs={{0,8},{2,10},{4,12},{6,14},{1,9},{3,11},{5,13},{7,15},{16,24},{18,... | collective-permute-start | bytes 589832 | tf_op jit(solution)/shard_map/ppermute | solution.py:278
  23.9 16.0 %collective-permute-start.6 = (bf16[128,1536]{1,0:T(8,128)(2,1)S(1)}, bf16[128,1536]{1,0:T(8,128)(2,1)S(1)}, u32[]{:S(2)}, u32[]{:S(2)}) collective-permute-start(bf16[128,1536]{1,0:T(8,128)(2,1)S(1)} %shard_map.94), channel_id=1, source_target_pairs={{0,16},{1,17},{2,18},{3,19},{4,20},{5,21},{6,22},{7,23},{8,24},{9,... | collective-permute-start | bytes 1179656 | tf_op jit(solution)/shard_map/ppermute | solution.py:278
  28.5 9.3 %collective-permute-start.8 = (bf16[32,1536]{1,0:T(8,128)(2,1)S(1)}, bf16[32,1536]{1,0:T(8,128)(2,1)S(1)}, u32[]{:S(2)}, u32[]{:S(2)}) collective-permute-start(bf16[32,1536]{1,0:T(8,128)(2,1)S(1)} %get-tuple-element.32), channel_id=1, source_target_pairs={{0,2},{2,0},{4,6},{6,4},{8,10},{10,8},{12,14},{14,12},{1,3},{3,1},... | collective-permute-start | bytes 294920 | tf_op jit(solution)/shard_map/ppermute | solution.py:333
  29.9 12.0 %collective-permute-start.9 = (bf16[32,1536]{1,0:T(8,128)(2,1)S(1)}, bf16[32,1536]{1,0:T(8,128)(2,1)S(1)}, u32[]{:S(2)}, u32[]{:S(2)}) collective-permute-start(bf16[32,1536]{1,0:T(8,128)(2,1)S(1)} %get-tuple-element.33), channel_id=1, source_target_pairs={{0,4},{2,6},{4,0},{6,2},{8,12},{10,14},{12,8},{14,10},{1,5},{3,7},... | collective-permute-start | bytes 294920 | tf_op jit(solution)/shard_map/ppermute | solution.py:333
  35.0 6.9 %collective-permute-start.10 = (bf16[32,1536]{1,0:T(8,128)(2,1)S(1)}, bf16[32,1536]{1,0:T(8,128)(2,1)S(1)}, u32[]{:S(2)}, u32[]{:S(2)}) collective-permute-start(bf16[32,1536]{1,0:T(8,128)(2,1)S(1)} %get-tuple-element.34), channel_id=1, source_target_pairs={{0,6},{2,4},{4,2},{6,0},{8,14},{10,12},{12,10},{14,8},{1,7},{3,5},... | collective-permute-start | bytes 294920 | tf_op jit(solution)/shard_map/ppermute | solution.py:333
  35.0 4.9 %copy-start.5 = (f32[24]{0:T(128)S(1)}, f32[24]{0:T(128)}, u32[]{:S(2)}) copy-start(f32[24]{0:T(128)} %param.16) | copy-start | bytes 292
  35.0 5.0 %copy-start.4 = (f32[1536]{0:T(1024)S(1)}, f32[1536]{0:T(1024)}, u32[]{:S(2)}) copy-start(f32[1536]{0:T(1024)} %param.17) | copy-start | bytes 18436
  36.3 9.1 %copy-start.1 = (bf16[1,32,8,1536]{3,2,1,0:T(8,128)(2,1)S(1)}, bf16[1,32,8,1536]{3,2,1,0:T(8,128)(2,1)}, u32[]{:S(2)}) copy-start(bf16[1,32,8,1536]{3,2,1,0:T(8,128)(2,1)} %param.10) | copy-start | bytes 2359300
  36.3 5.7 %collective-permute-start.12 = (bf16[32,1536]{1,0:T(8,128)(2,1)S(1)}, bf16[32,1536]{1,0:T(8,128)(2,1)S(1)}, u32[]{:S(2)}, u32[]{:S(2)}) collective-permute-start(bf16[32,1536]{1,0:T(8,128)(2,1)S(1)} %get-tuple-element.36), channel_id=1, source_target_pairs={{0,2},{2,0},{4,6},{6,4},{8,10},{10,8},{12,14},{14,12},{1,3},{3,1},... | collective-permute-start | bytes 294920 | tf_op jit(solution)/shard_map/ppermute | solution.py:333
  37.8 4.6 %collective-permute-start.13 = (bf16[32,1536]{1,0:T(8,128)(2,1)S(1)}, bf16[32,1536]{1,0:T(8,128)(2,1)S(1)}, u32[]{:S(2)}, u32[]{:S(2)}) collective-permute-start(bf16[32,1536]{1,0:T(8,128)(2,1)S(1)} %get-tuple-element.37), channel_id=1, source_target_pairs={{0,4},{2,6},{4,0},{6,2},{8,12},{10,14},{12,8},{14,10},{1,5},{3,7},... | collective-permute-start | bytes 294920 | tf_op jit(solution)/shard_map/ppermute | solution.py:333
  39.8 5.5 %collective-permute-start.14 = (bf16[32,1536]{1,0:T(8,128)(2,1)S(1)}, bf16[32,1536]{1,0:T(8,128)(2,1)S(1)}, u32[]{:S(2)}, u32[]{:S(2)}) collective-permute-start(bf16[32,1536]{1,0:T(8,128)(2,1)S(1)} %get-tuple-element.38), channel_id=1, source_target_pairs={{0,6},{2,4},{4,2},{6,0},{8,14},{10,12},{12,10},{14,8},{1,7},{3,5},... | collective-permute-start | bytes 294920 | tf_op jit(solution)/shard_map/ppermute | solution.py:333

commit v4 on v3

--- a/solution.py
+++ b/solution.py
@@ -98,10 +98,9 @@
     return lambda token: (mod(token, cols), div(token, cols))
 
 
-def row_order(cols, lines, member):
+def row_order(cols, lines):
     def order(token):
-        source = jnp.bitwise_xor(div(token, cols * lines), member)
-        return mod(div(token, cols), lines), source * cols + mod(token, cols)
+        return mod(div(token, cols), lines), div(token, cols * lines) * cols + mod(token, cols)
 
     return order
 
@@ -110,26 +109,22 @@
     return [(first, min(STRIP, channels - first)) for first in range(0, channels, STRIP)]
 
 
-def pack_kernel(
-    index_ref, x_ref, raw_ref, maps_ref, table_ref, rates_ref, params_ref, *refs, group, axis, heads, state
-):
-    sent, (raw, maps, table, rates, sems) = refs[:-5], refs[-5:]
-    member = mod(lax.axis_index(axis), group)
-    pieces = len(sent) // group
+def pack_kernel(index_ref, x_ref, raw_ref, maps_ref, table_ref, rates_ref, params_ref, *refs, group, heads, state):
+    sent, (index, raw, maps, table, rates, sems) = refs[:-6], refs[-6:]
     share = x_ref.shape[0] // group
-    rows = share // pieces
+    rows = share // len(sent)
     channels = x_ref.shape[1]
-    small = [(raw_ref, raw), (maps_ref, maps), (table_ref, table), (rates_ref, rates)]
+    small = [(index_ref, index), (raw_ref, raw), (maps_ref, maps), (table_ref, table), (rates_ref, rates)]
     copies = [pltpu.make_async_copy(a, b, sems.at[i]) for i, (a, b) in enumerate(small)]
     places = []
-    for piece in range(pieces):
-        for s in range(group):
-            first = pl.multiple_of(jnp.bitwise_xor(member, s) * share + piece * rows, rows)
-            out = sent[piece * group + s]
-            places.append((out, pl.ds(first, rows)))
+    for piece in range(len(sent)):
+        for member in range(group):
+            source = pl.ds(member * share + piece * rows, rows)
+            target = pl.ds(member * rows, rows)
+            places.append((sent[piece], target, source))
             copies.append(
                 pltpu.make_async_copy(
-                    x_ref.at[pl.ds(first, rows), :], out.at[:, pl.ds(0, channels)], sems.at[len(copies)]
+                    x_ref.at[source, :], sent[piece].at[target, pl.ds(0, channels)], sems.at[len(copies)]
                 )
             )
     for copy in copies:
@@ -137,11 +132,11 @@
     for copy in copies[: len(small)]:
         copy.wait()
     used = heads + 2 * state
-    for out, part in places:
-        out[:, channels : channels + heads] = raw[part, :heads]
-        out[:, channels + heads : channels + used] = maps[part, : 2 * state]
-        out[:, channels + used :] = jnp.zeros((rows, LANES - used), BF16)
-    row = jnp.where(iota(table.shape, 1) == index_ref[0], table[...], 0.0)
+    for out, target, source in places:
+        out[target, channels : channels + heads] = raw[source, :heads]
+        out[target, channels + heads : channels + used] = maps[source, : 2 * state]
+        out[target, channels + used :] = jnp.zeros((rows, LANES - used), BF16)
+    row = jnp.where(iota(table.shape, 1) == index[0], table[...], 0.0)
     ones = jnp.ones((8, table.shape[1]), BF16)
     bias = jnp.zeros((8, row.shape[0]), F32)
     for _ in range(3):
@@ -156,13 +151,13 @@
         copy.wait()
 
 
-def row_scan(params_ref, blocks, member, cols, heads, state):
-    channels = blocks[0].shape[1] - LANES
-    tokens = blocks[0].shape[0] * len(blocks)
-    lines = tokens // (cols * len(blocks))
-    aux = jnp.concatenate([block[:, channels:] for block in blocks], axis=0)
+def row_scan(params_ref, got_ref, group, cols, heads, state):
+    tokens = got_ref.shape[0]
+    channels = got_ref.shape[1] - LANES
+    lines = tokens // (cols * group)
+    aux = got_ref[:, channels:]
     return Scan(
-        row_order(cols, lines, member),
+        row_order(cols, lines),
         lines,
         aux[:, :heads],
         params_ref[0:1, :heads],
@@ -196,13 +191,9 @@
         s_ref[:, first : first + count] = (dot(into, values) * dot(ends, pick)).astype(BF16)
 
 
-def row_state_kernel(params_ref, *refs, group, axis, cols, heads, state, width):
-    blocks, s_ref, factor_ref = refs[:group], refs[group + 1], refs[group + 2 :]
-    member = mod(lax.axis_index(axis), group)
-    scan = row_scan(params_ref, blocks, member, cols, heads, state)
-    tokens_of = lambda first, count: jnp.concatenate(
-        [block[:, first : first + count] for block in blocks], axis=0
-    ).astype(F32)
+def row_state_kernel(params_ref, got_ref, _, s_ref, *factor_ref, group, cols, heads, state, width):
+    scan = row_scan(params_ref, got_ref, group, cols, heads, state)
+    tokens_of = lambda first, count: got_ref[:, first : first + count].astype(F32)
     write_state(scan, tokens_of, width, s_ref.shape[1], s_ref, factor_ref)
 
 
@@ -212,23 +203,18 @@
     write_state(scan, tokens_of, width, s_ref.shape[1], s_ref, factor_ref)
 
 
-def row_out_kernel(params_ref, s_ref, *refs, group, axis, cols, heads, state, width):
-    blocks, outs = refs[:group], refs[group + 1 :]
-    member = mod(lax.axis_index(axis), group)
-    scan = row_scan(params_ref, blocks, member, cols, heads, state)
+def row_out_kernel(params_ref, s_ref, got_ref, _, y_ref, *, group, cols, heads, state, width):
+    scan = row_scan(params_ref, got_ref, group, cols, heads, state)
     mix = scan.mix()
-    rows = blocks[0].shape[0]
     for first, count in strips(s_ref.shape[1]):
         pick = picks(heads, width, first, count)
         part = slice(first, first + count)
-        x = jnp.concatenate([block[:, part] for block in blocks], axis=0).astype(F32)
-        values = (x * dot(scan.grow, pick)).astype(BF16)
+        values = (got_ref[:, part].astype(F32) * dot(scan.grow, pick)).astype(BF16)
         y = dot(mix, jnp.concatenate([values, s_ref[:, part]], axis=0)) * dot(scan.fade, pick)
-        for s in range(group):
-            outs[s][:, part] = y[s * rows : (s + 1) * rows].astype(BF16)
-
-
-def col_out_kernel(params_ref, s_ref, x_ref, raw_ref, maps_ref, skip_ref, w_ref, *, cols, heads, state, width):
+        y_ref[:, part] = y.astype(BF16)
+
+
+def col_out_kernel(params_ref, s_ref, x_ref, raw_ref, maps_ref, gate_ref, skip_ref, w_ref, g_ref, *, cols, heads, state, width):
     scan = col_scan(params_ref, raw_ref, maps_ref, cols, heads, state)
     mix = scan.mix()
     for first, count in strips(s_ref.shape[1]):
@@ -238,19 +224,20 @@
         values = (x * dot(scan.grow, pick)).astype(BF16)
         y = dot(mix, jnp.concatenate([values, s_ref[:, part]], axis=0)) * dot(scan.fade, pick)
         w_ref[:, part] = y + skip_ref[:, part] * x
-
-
-def final_kernel(w_ref, gate_ref, gain_ref, *refs, group, axis):
-    rows_of, out_ref = refs[:-1], refs[-1]
-    pieces = len(rows_of) // group
-    rows, channels = rows_of[0].shape
-    member = mod(lax.axis_index(axis), group)
-    for piece in range(pieces):
-        for s in range(group):
-            first = (jnp.bitwise_xor(member, s) * pieces + piece) * rows
-            part = pl.ds(pl.multiple_of(first, rows), rows)
-            gate = gate_ref[part, :].astype(F32)
-            v = (rows_of[piece * group + s][...].astype(F32) + w_ref[part, :]) * (gate / (1.0 + jnp.exp(-gate)))
+        gate = gate_ref[:, part].astype(F32)
+        g_ref[:, part] = gate / (1.0 + jnp.exp(-gate))
+
+
+def final_kernel(w_ref, g_ref, gain_ref, *refs, group):
+    back, out_ref = refs[:-1], refs[-1]
+    rows = back[0].shape[0] // group
+    channels = back[0].shape[1]
+    for member in range(group):
+        for piece in range(len(back)):
+            first = (member * len(back) + piece) * rows
+            part = slice(first, first + rows)
+            row = back[piece][member * rows : (member + 1) * rows, :].astype(F32)
+            v = (row + w_ref[part, :]) * g_ref[part, :]
             power = jnp.sum(v * v, axis=1, keepdims=True) / channels
             out_ref[part, :] = (v * lax.rsqrt(power + 1e-5) * gain_ref[...]).astype(BF16)
 
@@ -293,89 +280,81 @@
     group = GROUP
     while col_count % group:
         group //= 2
-    share = tokens // group // PIECES
-    lines = share // cols
+    share = tokens // PIECES
+    lines = share // group // cols
+    groups = [list(range(i, i + group)) for i in range(0, col_count, group)]
 
     x = x_in.reshape(tokens, channels)
     gate = gate_in.reshape(tokens, channels)
     maps = proj_bc.reshape(tokens, 4 * state)
     raw = dt_raw.reshape(tokens, 2 * heads)
     sizes = dict(cols=cols, heads=heads, state=state, width=width)
-    shared = dict(group=group, axis="col")
     shape = jax.ShapeDtypeStruct
 
     any_spec = pl.BlockSpec(memory_space=pl.ANY)
-    hbm_spec = pl.BlockSpec(memory_space=pltpu.HBM)
-    full = lambda *dims: pl.BlockSpec(dims, lambda i, index: (0,) * len(dims))
-    packed = pl.pallas_call(
-        functools.partial(pack_kernel, heads=heads, state=state, **shared),
-        grid_spec=pltpu.PrefetchScalarGridSpec(
-            num_scalar_prefetch=1,
-            grid=(1,),
-            in_specs=[hbm_spec] * 5,
-            out_specs=[full(8, 2 * heads)] + [full(share, channels + LANES)] * (group * PIECES),
-            scratch_shapes=[
-                pltpu.VMEM(raw.shape, BF16),
-                pltpu.VMEM(maps.shape, BF16),
-                pltpu.VMEM(step_table.shape[::-1], F32),
-                pltpu.VMEM(rates.shape, F32),
-                pltpu.SemaphoreType.DMA((4 + group * PIECES,)),
-            ],
-        ),
-        out_shape=[pltpu.VMEM((8, 2 * heads), F32)] + [pltpu.VMEM((share, channels + LANES), BF16)] * (group * PIECES),
+    given = (step_index, x, raw, maps, step_table.T, rates)
+    params, *packed = pl.pallas_call(
+        functools.partial(pack_kernel, group=group, heads=heads, state=state),
+        in_specs=[any_spec] + [pl.BlockSpec(memory_space=pltpu.HBM)] * (len(given) - 1),
+        out_shape=[pltpu.VMEM((8, 2 * heads), F32)] + [pltpu.VMEM((share, channels + LANES), BF16)] * PIECES,
+        scratch_shapes=[
+            pltpu.SMEM(step_index.shape, jnp.int32),
+            pltpu.VMEM(raw.shape, BF16),
+            pltpu.VMEM(maps.shape, BF16),
+            pltpu.VMEM(step_table.shape[::-1], F32),
+            pltpu.VMEM(rates.shape, F32),
+            pltpu.SemaphoreType.DMA((len(given) - 1 + group * PIECES,)),
+        ],
         compiler_params=pltpu.CompilerParams(vmem_limit_bytes=32 * 1024 * 1024),
         cost_estimate=SMALL,
-    )(step_index, *[pltpu.with_memory_space_constraint(a, pltpu.HBM) for a in (x, raw, maps, step_table.T, rates)])
-    params, packed = packed[0], packed[1:]
+    )(given[0], *[pltpu.with_memory_space_constraint(a, pltpu.HBM) for a in given[1:]])
 
     def exchange(blocks):
-        return [blocks[0]] + [
-            lax.ppermute(blocks[s], "col", [(i, i ^ s) for i in range(col_count)]) for s in range(1, group)
-        ]
+        return lax.all_to_all(blocks, "col", split_axis=0, concat_axis=0, axis_index_groups=groups, tiled=True)
 
     def state_shapes(places, count):
         return [shape((places, channels), BF16)] + [shape((places, heads), F32)] * (count > 2)
 
-    got = [exchange(packed[piece * group : (piece + 1) * group]) for piece in range(PIECES)]
+    got = [exchange(blocks) for blocks in packed]
 
     row_entering = []
     row_made = params
     for piece in range(PIECES):
         made = call(
-            functools.partial(row_state_kernel, **sizes, **shared),
+            functools.partial(row_state_kernel, group=group, **sizes),
             state_shapes(lines * state, col_count // group),
-            specs=[None] * (1 + group) + [any_spec],
-        )(params, *got[piece], row_made)
+            specs=[None] * 2 + [any_spec],
+        )(params, got[piece], row_made)
         row_made = made[0]
         row_entering.append(entering_states(made, "col", col_count, group, width))
 
     col_made = call(
         functools.partial(col_state_kernel, **sizes),
         state_shapes(cols * state, row_count),
-            specs=[None] * 4 + [any_spec],
+        specs=[None] * 4 + [any_spec],
     )(params, x, raw, maps, row_made)
     col_entering = entering_states(col_made, "row", row_count, 1, width)
 
-    w = call(
+    w, silu = call(
         functools.partial(col_out_kernel, **sizes),
-        shape((tokens, channels), F32),
-    )(params, col_entering, x, raw, maps, jnp.repeat(skip, width).reshape(1, channels))
+        [shape((tokens, channels), F32)] * 2,
+    )(params, col_entering, x, raw, maps, gate, jnp.repeat(skip, width).reshape(1, channels))
 
     back = []
-    y_row = [params]
+    y_row = params
     for piece in range(PIECES):
         y_row = call(
-            functools.partial(row_out_kernel, **sizes, **shared),
-            [shape((share, channels), BF16)] * group,
-            specs=[None] * (2 + group) + [any_spec],
+            functools.partial(row_out_kernel, group=group, **sizes),
+            shape((share, channels), BF16),
+            specs=[None] * 3 + [any_spec],
             cost=LONG if piece == PIECES - 1 else SMALL,
-        )(params, row_entering[piece], *got[piece], y_row[0])
-        back += exchange(y_row)
+        )(params, row_entering[piece], got[piece], y_row)
+        back.append(exchange(y_row))
 
     mixed = call(
-        functools.partial(final_kernel, **shared),
+        functools.partial(final_kernel, group=group),
         shape((tokens, channels), BF16),
-    )(w, gate, norm_gain.reshape(1, channels), *back)
+    )(w, silu, norm_gain.reshape(1, channels), *back)
     return mixed.reshape(x_in.shape)
 
 

time: 47.3 us -> 72.7 us (1.54); the launches traced: 47.1 us -> 71.5 us
  blocking collectives: 0 us -> 12.8 us
  local copies, waits for them, and re-layouts: 0.18 us -> 5.62 us
  waiting for transfers between devices: 6.19 us -> 9.9 us
  Pallas kernels: 11.3 us -> 13.3 us
    ppermute x12 -> x0, starting transfers between devices: 18.7 us -> none  [exchange(): lax.ppermute(blocks[s], 'col', [(i, i ^ s) for i in range(col_count)])]
    all_to_all x0 -> x3, starting transfers between devices: none -> 16.7 us  [exchange(): lax.all_to_all(blocks, 'col', split_axis=0, concat_axis=0, axis_index_gro...]
    all_to_all x0 -> x1, blocking collectives: none -> 12.8 us  [exchange(): lax.all_to_all(blocks, 'col', split_axis=0, concat_axis=0, axis_index_gro...]
    ppermute x12 -> x0, waiting for transfers between devices: 6.18 us -> none  [exchange(): lax.ppermute(blocks[s], 'col', [(i, i ^ s) for i in range(col_count)])]
    ppermute x3, waiting for transfers between devices: 0.01 us -> 5.68 us  [entering_states(): entering = lax.ppermute(ends, axis, onward)]
    unnamed x12 -> x20, local copies, waits for them, and re-layouts: 0.03 us -> 5.47 us
    all_to_all x0 -> x3, waiting for transfers between devices: none -> 4.22 us  [exchange(): lax.all_to_all(blocks, 'col', split_axis=0, concat_axis=0, axis_index_gro...]
    ppermute x3, starting transfers between devices: 9.79 us -> 12.5 us  [entering_states(): entering = lax.ppermute(ends, axis, onward)]
  transfers between devices with their start and end apart: 15 -> 6, of which waited for: 4 -> 3; matrix products, arithmetic and copies ran while one was open for 0% -> 0% of each run, Pallas kernels for 17% -> 14%
where the time goes in v4:
time: 72.7 us; the launch traced here: 71.5 us
  starting transfers between devices  29.1 us (40%)
  Pallas kernels  13.3 us (18%)
  blocking collectives  12.8 us (18%)
  waiting for transfers between devices  9.9 us (14%)
  local copies, waits for them, and re-layouts  5.62 us (8%)
  between operations  0.82 us (1%)
    all_to_all x3, starting transfers between devices, exchange(): lax.all_to_all(blocks, 'col', split_axis=0, concat_axis=0, axis_index_gro...  16.7 us
    all_to_all x1, blocking collectives, exchange(): lax.all_to_all(blocks, 'col', split_axis=0, concat_axis=0, axis_index_gro...  12.8 us
    ppermute x3, starting transfers between devices, entering_states(): entering = lax.ppermute(ends, axis, onward)  12.5 us
    ppermute x3, waiting for transfers between devices, entering_states(): entering = lax.ppermute(ends, axis, onward)  5.68 us
    unnamed x20, local copies, waits for them, and re-layouts  5.47 us
    all_to_all x3, waiting for transfers between devices, exchange(): lax.all_to_all(blocks, 'col', split_axis=0, concat_axis=0, axis_index_gro...  4.22 us
    pallas_call x2, Pallas kernels, body(): call(functools.partial(row_out_kernel, group=group, **sizes), shape((shar...  4.03 us
    pallas_call x2, Pallas kernels, body(): call(functools.partial(row_state_kernel, group=group, **sizes), state_sha...  2.22 us
  transfers between devices with their start and end apart: 6, of which 3 were waited for; matrix products, arithmetic and copies ran while one was open for 0% of the time, Pallas kernels for 14%

profile of v4, /device:TPU:0, one launch (start us, length us, event | category | flops | bytes accessed | tf_op | source)
XLA Modules:
  0.0 71.5 jit_solution(1116071276273950465)
XLA Ops:
  0.7 2.2 %shard_map.91 = (f32[8,48]{1,0:T(8,128)S(1)}, bf16[128,1664]{1,0:T(8,128)(2,1)S(1)}, bf16[128,1664]{1,0:T(8,128)(2,1)}) custom-call(s32[1]{0:T(128)S(6)} %copy.10.index_ref, bf16[256,1536]{1,0:T(8,128)(2,1)} %bitcast.14, bf16[256,48]{1,0:T(8,128)(2,1)} %bitcast.24, bf16[256,64]{1,0:T(8,128)(2,1)} %bitcast.27, f32[48,1000]{1,0:T(8,128)} %bitcast.31, ...), custom_call_target="tpu_custom_call" | custom-call | flops 1024 | bytes 1024 | tf_op jit(solution)/shard_map/pallas_call | solution.py:296
  2.9 12.8 %all_to_all.44 = bf16[4,32,1664]{2,1,0:T(8,128)(2,1)S(1)} all-to-all(bf16[4,32,1664]{2,1,0:T(8,128)(2,1)S(1)} %bitcast.30), channel_id=1, replica_groups={{0,2,4,6},{8,10,12,14},{1,3,5,7},{9,11,13,15},{16,18,20,22},{24,26,28,3..., dimensions={0} | all-to-all | bytes 851968 | tf_op jit(solution)/shard_map/all_to_all | solution.py:313
  15.6 3.5 %all-to-all-start = ((bf16[4,32,1664]{2,1,0:T(8,128)(2,1)}), bf16[4,32,1664]{2,1,0:T(8,128)(2,1)S(1)}, u32[]{:S(2)}, u32[]{:S(2)}) async-start(bf16[4,32,1664]{2,1,0:T(8,128)(2,1)} %bitcast.4), calls=%async_computation | async-start | bytes 851968 | tf_op jit(solution)/shard_map/all_to_all | solution.py:313
  19.1 1.1 %shard_map.92._ = bf16[64,1536]{1,0:T(8,128)(2,1)S(1)} custom-call(f32[8,48]{1,0:T(8,128)S(1)} %get-tuple-element.10.params_ref._, bf16[128,1664]{1,0:T(8,128)(2,1)S(1)} %bitcast.17, f32[8,48]{1,0:T(8,128)S(1)} %get-tuple-element.10.params_ref._), custom_call_target="tpu_custom_call" | custom-call | flops 1024 | bytes 1024 | tf_op jit(solution)/shard_map/pallas_call | solution.py:323
  20.2 4.5 %collective-permute-start.1 = (bf16[64,1536]{1,0:T(8,128)(2,1)S(1)}, bf16[64,1536]{1,0:T(8,128)(2,1)S(1)}, u32[]{:S(2)}, u32[]{:S(2)}) collective-permute-start(bf16[64,1536]{1,0:T(8,128)(2,1)S(1)} %shard_map.92._), channel_id=1, source_target_pairs={{0,8},{2,10},{4,12},{6,14},{1,9},{3,11},{5,13},{7,15},{16,24},{18,... | collective-permute-start | bytes 589832 | tf_op jit(solution)/shard_map/ppermute | solution.py:265
  24.7 0.4 all-to-all-done
  25.1 1.1 %shard_map.93._ = bf16[64,1536]{1,0:T(8,128)(2,1)S(1)} custom-call(f32[8,48]{1,0:T(8,128)S(1)} %get-tuple-element.10.params_ref._, bf16[128,1664]{1,0:T(8,128)(2,1)S(1)} %bitcast.19, bf16[64,1536]{1,0:T(8,128)(2,1)S(1)} %shard_map.92._), custom_call_target="tpu_custom_call" | custom-call | flops 1024 | bytes 1024 | tf_op jit(solution)/shard_map/pallas_call | solution.py:323
  26.3 4.5 %collective-permute-start.2 = (bf16[64,1536]{1,0:T(8,128)(2,1)S(1)}, bf16[64,1536]{1,0:T(8,128)(2,1)S(1)}, u32[]{:S(2)}, u32[]{:S(2)}) collective-permute-start(bf16[64,1536]{1,0:T(8,128)(2,1)S(1)} %shard_map.93._), channel_id=1, source_target_pairs={{0,8},{2,10},{4,12},{6,14},{1,9},{3,11},{5,13},{7,15},{16,24},{18,... | collective-permute-start | bytes 589832 | tf_op jit(solution)/shard_map/ppermute | solution.py:265
  30.8 0.0 collective-permute-done.1.s_ref
  30.8 2.0 %shard_map.96._ = bf16[128,1536]{1,0:T(8,128)(2,1)} custom-call(f32[8,48]{1,0:T(8,128)S(1)} %get-tuple-element.10.params_ref._, bf16[64,1536]{1,0:T(8,128)(2,1)S(1)} %collective-permute-done.1.s_ref, bf16[128,1664]{1,0:T(8,128)(2,1)S(1)} %bitcast.18, f32[8,48]{1,0:T(8,128)S(1)} %get-tuple-element.10.params_ref._), custom_call_target="tpu_custom_call" | custom-call | flops 1024 | bytes 1024 | tf_op jit(solution)/shard_map/pallas_call | solution.py:346
  32.8 9.8 %all-to-all-start.2 = ((bf16[4,32,1536]{2,1,0:T(8,128)(2,1)}), bf16[4,32,1536]{2,1,0:T(8,128)(2,1)S(1)}, u32[]{:S(2)}, u32[]{:S(2)}) async-start(bf16[4,32,1536]{2,1,0:T(8,128)(2,1)} %bitcast.9), calls=%async_computation.2 | async-start | bytes 786432 | tf_op jit(solution)/shard_map/all_to_all | solution.py:313
  42.5 0.0 copy-start
  42.5 0.0 copy-start.4
  42.5 0.0 copy-start.5
  42.5 0.0 collective-permute-done.2.s_ref
  42.5 2.0 %shard_map.97 = bf16[128,1536]{1,0:T(8,128)(2,1)} custom-call(f32[8,48]{1,0:T(8,128)S(1)} %get-tuple-element.10.params_ref._, bf16[64,1536]{1,0:T(8,128)(2,1)S(1)} %collective-permute-done.2.s_ref, bf16[128,1664]{1,0:T(8,128)(2,1)S(1)} %bitcast.20, bf16[128,1536]{1,0:T(8,128)(2,1)} %shard_map.96._), custom_call_target="tpu_custom_call" | custom-call | flops 20000000000 | bytes 1024 | tf_op jit(solution)/shard_map/pallas_call | solution.py:346
  44.6 0.0 copy-start.8
  44.6 0.0 copy-start.9
  44.6 3.8 %all-to-all-done.2 = bf16[4,32,1536]{2,1,0:T(8,128)(2,1)S(1)} async-done(((bf16[4,32,1536]{2,1,0:T(8,128)(2,1)}), bf16[4,32,1536]{2,1,0:T(8,128)(2,1)S(1)}, u32[]{:S(2)}, u32[]{:S(2)}) %all-to-all-start.2) | async-done | bytes 393248 | tf_op jit(solution)/shard_map/all_to_all | solution.py:313
  48.4 3.5 %all-to-all-start.3 = ((bf16[4,32,1536]{2,1,0:T(8,128)(2,1)}), bf16[4,32,1536]{2,1,0:T(8,128)(2,1)S(1)}, u32[]{:S(2)}, u32[]{:S(2)}) async-start(bf16[4,32,1536]{2,1,0:T(8,128)(2,1)} %bitcast.11), calls=%async_computation.3 | async-start | bytes 786432 | tf_op jit(solution)/shard_map/all_to_all | solution.py:313
  51.9 0.0 copy-done
  51.9 0.0 copy-done.4
  51.9 0.0 copy-done.5
  51.9 1.5 %shard_map.94 = bf16[128,1536]{1,0:T(8,128)(2,1)S(1)} custom-call(f32[8,48]{1,0:T(8,128)S(1)} %get-tuple-element.10.params_ref._, bf16[256,1536]{1,0:T(8,128)(2,1)S(1)} %bitcast.15, bf16[256,48]{1,0:T(8,128)(2,1)S(1)} %bitcast.25, bf16[256,64]{1,0:T(8,128)(2,1)S(1)} %bitcast.28, bf16[64,1536]{1,0:T(8,128)(2,1)S(1)} %shard_map.93._), custom_call_target="tpu_custom_call" | custom-call | flops 1024 | bytes 1024 | tf_op jit(solution)/shard_map/pallas_call | solution.py:331
  53.4 3.4 %collective-permute-start = (bf16[128,1536]{1,0:T(8,128)(2,1)S(1)}, bf16[128,1536]{1,0:T(8,128)(2,1)S(1)}, u32[]{:S(2)}, u32[]{:S(2)}) collective-permute-start(bf16[128,1536]{1,0:T(8,128)(2,1)S(1)} %shard_map.94), channel_id=1, source_target_pairs={{0,16},{1,17},{2,18},{3,19},{4,20},{5,21},{6,22},{7,23},{8,24},{9,... | collective-permute-start | bytes 1179656 | tf_op jit(solution)/shard_map/ppermute | solution.py:265
  56.8 0.0 copy-done.8
  56.9 0.0 copy-done.9
  56.9 0.1 broadcast_in_dim.3
  56.9 0.1 reshape_reshape.3.skip_ref
  57.0 5.7 %collective-permute-done.s_ref = bf16[128,1536]{1,0:T(8,128)(2,1)S(1)} collective-permute-done((bf16[128,1536]{1,0:T(8,128)(2,1)S(1)}, bf16[128,1536]{1,0:T(8,128)(2,1)S(1)}, u32[]{:S(2)}, u32[]{:S(2)}) %collective-permute-start) | collective-permute-done | bytes 393248 | tf_op jit(solution)/shard_map/ppermute | solution.py:265
  62.7 0.0 copy-start.6
  62.7 0.7 %copy-done.6 = bf16[128,1536]{1,0:T(8,128)(2,1)} copy-done((bf16[128,1536]{1,0:T(8,128)(2,1)}, bf16[128,1536]{1,0:T(8,128)(2,1)S(1)}, u32[]{:S(2)}) %copy-start.6) | copy-done | bytes 393240
  63.4 0.0 copy-start.3
  63.4 1.1 %copy-done.3 = bf16[1,32,8,1536]{3,2,1,0:T(8,128)(2,1)S(1)} copy-done((bf16[1,32,8,1536]{3,2,1,0:T(8,128)(2,1)S(1)}, bf16[1,32,8,1536]{3,2,1,0:T(8,128)(2,1)}, u32[]{:S(2)}) %copy-start.3) | copy-done | bytes 786456
  64.6 0.0 copy-start.7
  64.6 1.0 %copy-done.7 = bf16[128,1536]{1,0:T(8,128)(2,1)S(1)} copy-done((bf16[128,1536]{1,0:T(8,128)(2,1)S(1)}, bf16[128,1536]{1,0:T(8,128)(2,1)}, u32[]{:S(2)}) %copy-start.7) | copy-done | bytes 393240
  65.6 2.1 %shard_map.95 = (f32[256,1536]{1,0:T(8,128)S(1)}, f32[256,1536]{1,0:T(8,128)S(1)}) custom-call(f32[8,48]{1,0:T(8,128)S(1)} %get-tuple-element.10.params_ref._, bf16[128,1536]{1,0:T(8,128)(2,1)S(1)} %copy-done.7, bf16[256,1536]{1,0:T(8,128)(2,1)S(1)} %bitcast.16, bf16[256,48]{1,0:T(8,128)(2,1)S(1)} %bitcast.26, bf16[256,64]{1,0:T(8,128)(2,1)S(1)} %bitcast.29, ...), custom_call_target="tpu_custom_call" | custom-call | flops 1024 | bytes 1024 | tf_op jit(solution)/shard_map/pallas_call | solution.py:338
  67.6 0.0 copy-start.1
  67.6 1.2 %copy-done.1 = f32[256,1536]{1,0:T(8,128)} copy-done((f32[256,1536]{1,0:T(8,128)}, f32[256,1536]{1,0:T(8,128)S(1)}, u32[]{:S(2)}) %copy-start.1) | copy-done | bytes 1572888
  68.8 0.0 all-to-all-done.3
  68.8 0.0 copy-start.2
  68.8 1.4 %copy-done.2 = f32[256,1536]{1,0:T(8,128)S(1)} copy-done((f32[256,1536]{1,0:T(8,128)S(1)}, f32[256,1536]{1,0:T(8,128)}, u32[]{:S(2)}) %copy-start.2) | copy-done | bytes 1572888
  70.2 1.3 %shard_map.98 = bf16[256,1536]{1,0:T(8,128)(2,1)} custom-call(f32[256,1536]{1,0:T(8,128)S(1)} %get-tuple-element.13.w_ref, f32[256,1536]{1,0:T(8,128)S(1)} %copy-done.2, f32[1,1536]{1,0:T(1,128)S(1)} %reshape.30.gain_ref, bf16[128,1536]{1,0:T(8,128)(2,1)S(1)} %bitcast.21, bf16[128,1536]{1,0:T(8,128)(2,1)S(1)} %bitcast.22), custom_call_target="tpu_custom_call" | custom-call | flops 1024 | bytes 1024 | tf_op jit(solution)/shard_map/pallas_call | solution.py:354
  (1 shorter events, 0.0 us)
Async XLA Ops:
  15.6 9.5 %all-to-all-start = ((bf16[4,32,1664]{2,1,0:T(8,128)(2,1)}), bf16[4,32,1664]{2,1,0:T(8,128)(2,1)S(1)}, u32[]{:S(2)}, u32[]{:S(2)}) async-start(bf16[4,32,1664]{2,1,0:T(8,128)(2,1)} %bitcast.4), calls=%async_computation | async-start | bytes 851968 | tf_op jit(solution)/shard_map/all_to_all | solution.py:313
  20.2 10.5 %collective-permute-start.1 = (bf16[64,1536]{1,0:T(8,128)(2,1)S(1)}, bf16[64,1536]{1,0:T(8,128)(2,1)S(1)}, u32[]{:S(2)}, u32[]{:S(2)}) collective-permute-start(bf16[64,1536]{1,0:T(8,128)(2,1)S(1)} %shard_map.92._), channel_id=1, source_target_pairs={{0,8},{2,10},{4,12},{6,14},{1,9},{3,11},{5,13},{7,15},{16,24},{18,... | collective-permute-start | bytes 589832 | tf_op jit(solution)/shard_map/ppermute | solution.py:265
  26.3 16.3 %collective-permute-start.2 = (bf16[64,1536]{1,0:T(8,128)(2,1)S(1)}, bf16[64,1536]{1,0:T(8,128)(2,1)S(1)}, u32[]{:S(2)}, u32[]{:S(2)}) collective-permute-start(bf16[64,1536]{1,0:T(8,128)(2,1)S(1)} %shard_map.93._), channel_id=1, source_target_pairs={{0,8},{2,10},{4,12},{6,14},{1,9},{3,11},{5,13},{7,15},{16,24},{18,... | collective-permute-start | bytes 589832 | tf_op jit(solution)/shard_map/ppermute | solution.py:265
  32.8 15.6 %all-to-all-start.2 = ((bf16[4,32,1536]{2,1,0:T(8,128)(2,1)}), bf16[4,32,1536]{2,1,0:T(8,128)(2,1)S(1)}, u32[]{:S(2)}, u32[]{:S(2)}) async-start(bf16[4,32,1536]{2,1,0:T(8,128)(2,1)} %bitcast.9), calls=%async_computation.2 | async-start | bytes 786432 | tf_op jit(solution)/shard_map/all_to_all | solution.py:313
  42.5 9.3 %copy-start = (bf16[1,32,8,1536]{3,2,1,0:T(8,128)(2,1)S(1)}, bf16[1,32,8,1536]{3,2,1,0:T(8,128)(2,1)}, u32[]{:S(2)}) copy-start(bf16[1,32,8,1536]{3,2,1,0:T(8,128)(2,1)} %param.9) | copy-start | bytes 2359300
  42.5 9.4 %copy-start.4 = (bf16[1,32,8,48]{3,2,1,0:T(8,128)(2,1)S(1)}, bf16[1,32,8,48]{3,2,1,0:T(8,128)(2,1)}, u32[]{:S(2)}) copy-start(bf16[1,32,8,48]{3,2,1,0:T(8,128)(2,1)} %param.12) | copy-start | bytes 73732
  42.5 9.4 %copy-start.5 = (bf16[1,32,8,64]{3,2,1,0:T(8,128)(2,1)S(1)}, bf16[1,32,8,64]{3,2,1,0:T(8,128)(2,1)}, u32[]{:S(2)}) copy-start(bf16[1,32,8,64]{3,2,1,0:T(8,128)(2,1)} %param.11) | copy-start | bytes 98308
  44.6 12.3 %copy-start.8 = (f32[1536]{0:T(1024)S(1)}, f32[1536]{0:T(1024)}, u32[]{:S(2)}) copy-start(f32[1536]{0:T(1024)} %param.17) | copy-start | bytes 18436
  44.6 12.3 %copy-start.9 = (f32[24]{0:T(128)S(1)}, f32[24]{0:T(128)}, u32[]{:S(2)}) copy-start(f32[24]{0:T(128)} %param.16) | copy-start | bytes 292
  48.4 20.4 %all-to-all-start.3 = ((bf16[4,32,1536]{2,1,0:T(8,128)(2,1)}), bf16[4,32,1536]{2,1,0:T(8,128)(2,1)S(1)}, u32[]{:S(2)}, u32[]{:S(2)}) async-start(bf16[4,32,1536]{2,1,0:T(8,128)(2,1)} %bitcast.11), calls=%async_computation.3 | async-start | bytes 786432 | tf_op jit(solution)/shard_map/all_to_all | solution.py:313
  53.4 9.3 %collective-permute-start = (bf16[128,1536]{1,0:T(8,128)(2,1)S(1)}, bf16[128,1536]{1,0:T(8,128)(2,1)S(1)}, u32[]{:S(2)}, u32[]{:S(2)}) collective-permute-start(bf16[128,1536]{1,0:T(8,128)(2,1)S(1)} %shard_map.94), channel_id=1, source_target_pairs={{0,16},{1,17},{2,18},{3,19},{4,20},{5,21},{6,22},{7,23},{8,24},{9,... | collective-permute-start | bytes 1179656 | tf_op jit(solution)/shard_map/ppermute | solution.py:265
  62.7 0.7 %copy-start.6 = (bf16[128,1536]{1,0:T(8,128)(2,1)}, bf16[128,1536]{1,0:T(8,128)(2,1)S(1)}, u32[]{:S(2)}) copy-start(bf16[128,1536]{1,0:T(8,128)(2,1)S(1)} %collective-permute-done.s_ref) | copy-start | bytes 1179652
  63.4 1.1 %copy-start.3 = (bf16[1,32,8,1536]{3,2,1,0:T(8,128)(2,1)S(1)}, bf16[1,32,8,1536]{3,2,1,0:T(8,128)(2,1)}, u32[]{:S(2)}) copy-start(bf16[1,32,8,1536]{3,2,1,0:T(8,128)(2,1)} %param.10) | copy-start | bytes 2359300
  64.6 1.0 %copy-start.7 = (bf16[128,1536]{1,0:T(8,128)(2,1)S(1)}, bf16[128,1536]{1,0:T(8,128)(2,1)}, u32[]{:S(2)}) copy-start(bf16[128,1536]{1,0:T(8,128)(2,1)} %copy-done.6) | copy-start | bytes 1179652
  67.6 1.2 %copy-start.1 = (f32[256,1536]{1,0:T(8,128)}, f32[256,1536]{1,0:T(8,128)S(1)}, u32[]{:S(2)}) copy-start(f32[256,1536]{1,0:T(8,128)S(1)} %get-tuple-element.14.g_ref) | copy-start | bytes 4718596
  68.8 1.4 %copy-start.2 = (f32[256,1536]{1,0:T(8,128)S(1)}, f32[256,1536]{1,0:T(8,128)}, u32[]{:S(2)}) copy-start(f32[256,1536]{1,0:T(8,128)} %copy-done.1) | copy-start | bytes 4718596

commit v5 on v3

--- a/solution.py
+++ b/solution.py
@@ -86,12 +86,13 @@
     def into(self):
         return widen(self.b_map, self.line, self.lines).astype(F32).T.astype(BF16)
 
-    def mix(self):
+    def mix(self, follows):
         scores = lax.dot_general(
             self.c_map, self.b_map, (((1,), (1,)), ((), ())), preferred_element_type=F32
         )
         within = jnp.where(self.lower, scores, 0.0).astype(BF16)
-        return jnp.concatenate([within, widen(self.c_map, self.line, self.lines)], axis=1)
+        entering = widen(self.c_map, self.line, self.lines)
+        return jnp.concatenate([within, jnp.where(follows, entering, 0)], axis=1)
 
 
 def column_order(cols):
@@ -216,7 +217,7 @@
     blocks, outs = refs[:group], refs[group + 1 :]
     member = mod(lax.axis_index(axis), group)
     scan = row_scan(params_ref, blocks, member, cols, heads, state)
-    mix = scan.mix()
+    mix = scan.mix(lax.axis_index(axis) >= group)
     rows = blocks[0].shape[0]
     for first, count in strips(s_ref.shape[1]):
         pick = picks(heads, width, first, count)
@@ -228,9 +229,9 @@
             outs[s][:, part] = y[s * rows : (s + 1) * rows].astype(BF16)
 
 
-def col_out_kernel(params_ref, s_ref, x_ref, raw_ref, maps_ref, skip_ref, w_ref, *, cols, heads, state, width):
+def col_out_kernel(params_ref, s_ref, x_ref, raw_ref, maps_ref, gate_ref, skip_ref, w_ref, g_ref, *, cols, heads, state, width):
     scan = col_scan(params_ref, raw_ref, maps_ref, cols, heads, state)
-    mix = scan.mix()
+    mix = scan.mix(lax.axis_index("row") > 0)
     for first, count in strips(s_ref.shape[1]):
         pick = picks(heads, width, first, count)
         part = slice(first, first + count)
@@ -238,9 +239,11 @@
         values = (x * dot(scan.grow, pick)).astype(BF16)
         y = dot(mix, jnp.concatenate([values, s_ref[:, part]], axis=0)) * dot(scan.fade, pick)
         w_ref[:, part] = y + skip_ref[:, part] * x
-
-
-def final_kernel(w_ref, gate_ref, gain_ref, *refs, group, axis):
+        gate = gate_ref[:, part].astype(F32)
+        g_ref[:, part] = gate / (1.0 + jnp.exp(-gate))
+
+
+def final_kernel(w_ref, g_ref, gain_ref, *refs, group, axis):
     rows_of, out_ref = refs[:-1], refs[-1]
     pieces = len(rows_of) // group
     rows, channels = rows_of[0].shape
@@ -249,8 +252,7 @@
         for s in range(group):
             first = (jnp.bitwise_xor(member, s) * pieces + piece) * rows
             part = pl.ds(pl.multiple_of(first, rows), rows)
-            gate = gate_ref[part, :].astype(F32)
-            v = (rows_of[piece * group + s][...].astype(F32) + w_ref[part, :]) * (gate / (1.0 + jnp.exp(-gate)))
+            v = (rows_of[piece * group + s][...].astype(F32) + w_ref[part, :]) * g_ref[part, :]
             power = jnp.sum(v * v, axis=1, keepdims=True) / channels
             out_ref[part, :] = (v * lax.rsqrt(power + 1e-5) * gain_ref[...]).astype(BF16)
 
@@ -272,12 +274,13 @@
 
 def entering_states(made, axis, size, stride, width):
     ends = made[0]
-    onward = [(i, i + stride) for i in range(size - stride)]
-    if not onward:
-        return jnp.zeros_like(ends)
+    if size == stride:
+        return ends
+    onward = [(i, (i + stride) % size) for i in range(size)]
     entering = lax.ppermute(ends, axis, onward)
     for _ in range(size // stride - 2):
-        factor = jnp.repeat(made[1], width, axis=1)
+        follows = (lax.axis_index(axis) >= stride).astype(F32)
+        factor = follows * jnp.repeat(made[1], width, axis=1)
         entering = lax.ppermute(
             (ends.astype(F32) + factor * entering.astype(F32)).astype(BF16), axis, onward
         )
@@ -356,10 +359,10 @@
     )(params, x, raw, maps, row_made)
     col_entering = entering_states(col_made, "row", row_count, 1, width)
 
-    w = call(
+    w, silu = call(
         functools.partial(col_out_kernel, **sizes),
-        shape((tokens, channels), F32),
-    )(params, col_entering, x, raw, maps, jnp.repeat(skip, width).reshape(1, channels))
+        [shape((tokens, channels), F32)] * 2,
+    )(params, col_entering, x, raw, maps, gate, jnp.repeat(skip, width).reshape(1, channels))
 
     back = []
     y_row = [params]
@@ -375,7 +378,7 @@
     mixed = call(
         functools.partial(final_kernel, **shared),
         shape((tokens, channels), BF16),
-    )(w, gate, norm_gain.reshape(1, channels), *back)
+    )(w, silu, norm_gain.reshape(1, channels), *back)
     return mixed.reshape(x_in.shape)
 
 

time: 47.3 us -> 45.7 us (0.966)
  starting transfers between devices: 28.5 us -> 22.9 us
  waiting for transfers between devices: 6.19 us -> 10.6 us
    ppermute x3, waiting for transfers between devices: 0.01 us -> 5.91 us  [entering_states(): entering = lax.ppermute(ends, axis, onward)]
    ppermute x12, starting transfers between devices: 18.7 us -> 15.9 us  [exchange(): lax.ppermute(blocks[s], 'col', [(i, i ^ s) for i in range(col_count)])]
    ppermute x3, starting transfers between devices: 9.79 us -> 7 us  [entering_states(): entering = lax.ppermute(ends, axis, onward)]
    ppermute x12, waiting for transfers between devices: 6.18 us -> 4.68 us  [exchange(): lax.ppermute(blocks[s], 'col', [(i, i ^ s) for i in range(col_count)])]
  transfers between devices with their start and end apart: 15 -> 15, of which waited for: 4 -> 5; matrix products, arithmetic and copies ran while one was open for 0% -> 0% of each run, Pallas kernels for 17% -> 18%
where the time goes in v5:
time: 45.7 us; the launch traced here: 45.5 us
  starting transfers between devices  22.9 us (50%)
  Pallas kernels  11 us (24%)
  waiting for transfers between devices  10.6 us (23%)
  between operations  0.85 us (2%)
    ppermute x12, starting transfers between devices, exchange(): lax.ppermute(blocks[s], 'col', [(i, i ^ s) for i in range(col_count)])  15.9 us
    ppermute x3, starting transfers between devices, entering_states(): entering = lax.ppermute(ends, axis, onward)  7 us
    ppermute x3, waiting for transfers between devices, entering_states(): entering = lax.ppermute(ends, axis, onward)  5.91 us
    ppermute x12, waiting for transfers between devices, exchange(): lax.ppermute(blocks[s], 'col', [(i, i ^ s) for i in range(col_count)])  4.68 us
    pallas_call x2, Pallas kernels, body(): call(functools.partial(row_out_kernel, **sizes, **shared), [shape((share,...  2.5 us
    pallas_call x2, Pallas kernels, body(): call(functools.partial(row_state_kernel, **sizes, **shared), state_shapes...  2.2 us
    pallas_call x1, Pallas kernels, body(): call(functools.partial(col_out_kernel, **sizes), [shape((tokens, channels...  2.06 us
    pallas_call x1, Pallas kernels, body(): call(functools.partial(col_state_kernel, **sizes), state_shapes(cols * st...  1.49 us
  transfers between devices with their start and end apart: 15, of which 5 were waited for; matrix products, arithmetic and copies ran while one was open for 0% of the time, Pallas kernels for 18%

profile of v5, /device:TPU:0, one launch (start us, length us, event | category | flops | bytes accessed | tf_op | source)
XLA Modules:
  0.0 45.5 jit_solution(13048097210180282299)
XLA Ops:
  0.0 0.0 copy-start.2
  0.0 0.0 copy-start.3
  0.0 0.0 copy-start
  0.7 1.4 %shard_map.91 = (f32[8,48]{1,0:T(8,128)S(1)}, bf16[32,1664]{1,0:T(8,128)(2,1)S(1)}, bf16[32,1664]{1,0:T(8,128)(2,1)S(1)}, bf16[32,1664]{1,0:T(8,128)(2,1)S(1)}, ...) custom-call(s32[1]{0:T(128)S(6)} %copy.10.index_ref, ...), custom_call_target="tpu_custom_call" | custom-call | flops 1024 | bytes 1024 | tf_op jit(solution)/shard_map/pallas_call | solution.py:313
  2.2 3.0 %collective-permute-start.3 = (bf16[32,1664]{1,0:T(8,128)(2,1)S(1)}, bf16[32,1664]{1,0:T(8,128)(2,1)S(1)}, u32[]{:S(2)}, u32[]{:S(2)}) collective-permute-start(bf16[32,1664]{1,0:T(8,128)(2,1)S(1)} %get-tuple-element.30), channel_id=1, source_target_pairs={{0,2},{2,0},{4,6},{6,4},{8,10},{10,8},{12,14},{14,12},{1,3},{3,1},... | collective-permute-start | bytes 319496 | tf_op jit(solution)/shard_map/ppermute | solution.py:336
  5.2 1.6 %collective-permute-start.4 = (bf16[32,1664]{1,0:T(8,128)(2,1)S(1)}, bf16[32,1664]{1,0:T(8,128)(2,1)S(1)}, u32[]{:S(2)}, u32[]{:S(2)}) collective-permute-start(bf16[32,1664]{1,0:T(8,128)(2,1)S(1)} %get-tuple-element.31), channel_id=1, source_target_pairs={{0,4},{2,6},{4,0},{6,2},{8,12},{10,14},{12,8},{14,10},{1,5},{3,7},... | collective-permute-start | bytes 319496 | tf_op jit(solution)/shard_map/ppermute | solution.py:336
  6.8 0.0 collective-permute-start.5
  6.8 1.9 %collective-permute-start = (bf16[32,1664]{1,0:T(8,128)(2,1)S(1)}, bf16[32,1664]{1,0:T(8,128)(2,1)S(1)}, u32[]{:S(2)}, u32[]{:S(2)}) collective-permute-start(bf16[32,1664]{1,0:T(8,128)(2,1)S(1)} %get-tuple-element.26), channel_id=1, source_target_pairs={{0,2},{2,0},{4,6},{6,4},{8,10},{10,8},{12,14},{14,12},{1,3},{3,1},... | collective-permute-start | bytes 319496 | tf_op jit(solution)/shard_map/ppermute | solution.py:336
  8.7 1.6 %collective-permute-start.1 = (bf16[32,1664]{1,0:T(8,128)(2,1)S(1)}, bf16[32,1664]{1,0:T(8,128)(2,1)S(1)}, u32[]{:S(2)}, u32[]{:S(2)}) collective-permute-start(bf16[32,1664]{1,0:T(8,128)(2,1)S(1)} %get-tuple-element.27), channel_id=1, source_target_pairs={{0,4},{2,6},{4,0},{6,2},{8,12},{10,14},{12,8},{14,10},{1,5},{3,7},... | collective-permute-start | bytes 319496 | tf_op jit(solution)/shard_map/ppermute | solution.py:336
  10.3 0.0 collective-permute-done.3.refs_1_
  10.3 0.7 %collective-permute-start.2 = (bf16[32,1664]{1,0:T(8,128)(2,1)S(1)}, bf16[32,1664]{1,0:T(8,128)(2,1)S(1)}, u32[]{:S(2)}, u32[]{:S(2)}) collective-permute-start(bf16[32,1664]{1,0:T(8,128)(2,1)S(1)} %get-tuple-element.28), channel_id=1, source_target_pairs={{0,6},{2,4},{4,2},{6,0},{8,14},{10,12},{12,10},{14,8},{1,7},{3,5},... | collective-permute-start | bytes 319496 | tf_op jit(solution)/shard_map/ppermute | solution.py:336
  10.9 0.1 collective-permute-done.4.refs_2_
  11.1 2.6 %collective-permute-done.5.refs_3_ = bf16[32,1664]{1,0:T(8,128)(2,1)S(1)} collective-permute-done((bf16[32,1664]{1,0:T(8,128)(2,1)S(1)}, bf16[32,1664]{1,0:T(8,128)(2,1)S(1)}, u32[]{:S(2)}, u32[]{:S(2)}) %collective-permute-start.5) | collective-permute-done | bytes 106528 | tf_op jit(solution)/shard_map/ppermute | solution.py:336
  13.7 1.1 %shard_map.92.refs_4_ = bf16[64,1536]{1,0:T(8,128)(2,1)S(1)} custom-call(f32[8,48]{1,0:T(8,128)S(1)} %get-tuple-element.24.params_ref.refs_4_, bf16[32,1664]{1,0:T(8,128)(2,1)S(1)} %get-tuple-element.29.refs_0_, bf16[32,1664]{1,0:T(8,128)(2,1)S(1)} %collective-permute-done.3.refs_1_, bf16[32,1664]{1,0:T(8,128)(2,1)S(1)} %collective-permute-done.4.refs_2_, ...), custom_call_target="tpu_custom_call" | custom-call | flops 1024 | bytes 1024 | tf_op jit(solution)/shard_map/pallas_call | solution.py:347
  14.8 2.6 %collective-permute-start.7 = (bf16[64,1536]{1,0:T(8,128)(2,1)S(1)}, bf16[64,1536]{1,0:T(8,128)(2,1)S(1)}, u32[]{:S(2)}, u32[]{:S(2)}) collective-permute-start(bf16[64,1536]{1,0:T(8,128)(2,1)S(1)} %shard_map.92.refs_4_), channel_id=1, source_target_pairs={{0,8},{2,10},{4,12},{6,14},{8,0},{10,2},{12,4},{14,6},{1,9},{3,11}... | collective-permute-start | bytes 589832 | tf_op jit(solution)/shard_map/ppermute | solution.py:280
  17.4 0.0 collective-permute-done.refs_1_
  17.4 0.0 collective-permute-done.1.refs_2_
  17.4 0.6 %collective-permute-done.2.refs_3_ = bf16[32,1664]{1,0:T(8,128)(2,1)S(1)} collective-permute-done((bf16[32,1664]{1,0:T(8,128)(2,1)S(1)}, bf16[32,1664]{1,0:T(8,128)(2,1)S(1)}, u32[]{:S(2)}, u32[]{:S(2)}) %collective-permute-start.2) | collective-permute-done | bytes 106528 | tf_op jit(solution)/shard_map/ppermute | solution.py:336
  18.0 1.1 %shard_map.93._ = bf16[64,1536]{1,0:T(8,128)(2,1)S(1)} custom-call(f32[8,48]{1,0:T(8,128)S(1)} %get-tuple-element.24.params_ref.refs_4_, bf16[32,1664]{1,0:T(8,128)(2,1)S(1)} %get-tuple-element.25.refs_0_, bf16[32,1664]{1,0:T(8,128)(2,1)S(1)} %collective-permute-done.refs_1_, bf16[32,1664]{1,0:T(8,128)(2,1)S(1)} %collective-permute-done.1.refs_2_, ...), custom_call_target="tpu_custom_call" | custom-call | flops 1024 | bytes 1024 | tf_op jit(solution)/shard_map/pallas_call | solution.py:347
  19.1 2.9 %collective-permute-start.11 = (bf16[64,1536]{1,0:T(8,128)(2,1)S(1)}, bf16[64,1536]{1,0:T(8,128)(2,1)S(1)}, u32[]{:S(2)}, u32[]{:S(2)}) collective-permute-start(bf16[64,1536]{1,0:T(8,128)(2,1)S(1)} %shard_map.93._), channel_id=1, source_target_pairs={{0,8},{2,10},{4,12},{6,14},{8,0},{10,2},{12,4},{14,6},{1,9},{3,11}... | collective-permute-start | bytes 589832 | tf_op jit(solution)/shard_map/ppermute | solution.py:280
  21.9 0.0 copy-done.2
  21.9 0.0 copy-done.3
  21.9 0.0 copy-done
  21.9 1.5 %shard_map.94 = bf16[128,1536]{1,0:T(8,128)(2,1)S(1)} custom-call(f32[8,48]{1,0:T(8,128)S(1)} %get-tuple-element.24.params_ref.refs_4_, bf16[256,1536]{1,0:T(8,128)(2,1)S(1)} %bitcast.7, bf16[256,48]{1,0:T(8,128)(2,1)S(1)} %bitcast.11, bf16[256,64]{1,0:T(8,128)(2,1)S(1)} %bitcast.14, bf16[64,1536]{1,0:T(8,128)(2,1)S(1)} %shard_map.93._), custom_call_target="tpu_custom_call" | custom-call | flops 1024 | bytes 1024 | tf_op jit(solution)/shard_map/pallas_call | solution.py:355
  23.4 1.5 %collective-permute-start.6 = (bf16[128,1536]{1,0:T(8,128)(2,1)S(1)}, bf16[128,1536]{1,0:T(8,128)(2,1)S(1)}, u32[]{:S(2)}, u32[]{:S(2)}) collective-permute-start(bf16[128,1536]{1,0:T(8,128)(2,1)S(1)} %shard_map.94), channel_id=1, source_target_pairs={{0,16},{16,0},{1,17},{17,1},{2,18},{18,2},{3,19},{19,3},{4,20},{20... | collective-permute-start | bytes 1179656 | tf_op jit(solution)/shard_map/ppermute | solution.py:280
  25.0 5.9 %collective-permute-done.7.s_ref = bf16[64,1536]{1,0:T(8,128)(2,1)S(1)} collective-permute-done((bf16[64,1536]{1,0:T(8,128)(2,1)S(1)}, bf16[64,1536]{1,0:T(8,128)(2,1)S(1)}, u32[]{:S(2)}, u32[]{:S(2)}) %collective-permute-start.7) | collective-permute-done | bytes 196640 | tf_op jit(solution)/shard_map/ppermute | solution.py:280
  30.9 1.2 %shard_map.96 = (bf16[32,1536]{1,0:T(8,128)(2,1)S(1)}, bf16[32,1536]{1,0:T(8,128)(2,1)S(1)}, bf16[32,1536]{1,0:T(8,128)(2,1)S(1)}, bf16[32,1536]{1,0:T(8,128)(2,1)S(1)}) custom-call(f32[8,48]{1,0:T(8,128)S(1)} %get-tuple-element.24.params_ref.refs_4_, bf16[64,1536]{1,0:T(8,128)(2,1)S(1)} %collective-permute-done.7.s_ref, ...), custom_call_target="tpu_custom_call" | custom-call | flops 1024 | bytes 1024 | tf_op jit(solution)/shard_map/pallas_call | solution.py:370
  32.1 0.8 %collective-permute-start.8 = (bf16[32,1536]{1,0:T(8,128)(2,1)S(1)}, bf16[32,1536]{1,0:T(8,128)(2,1)S(1)}, u32[]{:S(2)}, u32[]{:S(2)}) collective-permute-start(bf16[32,1536]{1,0:T(8,128)(2,1)S(1)} %get-tuple-element.36), channel_id=1, source_target_pairs={{0,2},{2,0},{4,6},{6,4},{8,10},{10,8},{12,14},{14,12},{1,3},{3,1},... | collective-permute-start | bytes 294920 | tf_op jit(solution)/shard_map/ppermute | solution.py:336
  33.0 0.2 collective-permute-start.9
  33.1 2.5 %collective-permute-start.10 = (bf16[32,1536]{1,0:T(8,128)(2,1)S(1)}, bf16[32,1536]{1,0:T(8,128)(2,1)S(1)}, u32[]{:S(2)}, u32[]{:S(2)}) collective-permute-start(bf16[32,1536]{1,0:T(8,128)(2,1)S(1)} %get-tuple-element.38), channel_id=1, source_target_pairs={{0,6},{2,4},{4,2},{6,0},{8,14},{10,12},{12,10},{14,8},{1,7},{3,5},... | collective-permute-start | bytes 294920 | tf_op jit(solution)/shard_map/ppermute | solution.py:336
  35.7 0.0 collective-permute-done.11.s_ref
  35.7 0.0 copy-start.4
  35.7 0.0 copy-start.5
  35.7 0.0 copy-start.1
  35.7 1.3 %shard_map.97 = (bf16[32,1536]{1,0:T(8,128)(2,1)S(1)}, bf16[32,1536]{1,0:T(8,128)(2,1)S(1)}, bf16[32,1536]{1,0:T(8,128)(2,1)S(1)}, bf16[32,1536]{1,0:T(8,128)(2,1)S(1)}) custom-call(f32[8,48]{1,0:T(8,128)S(1)} %get-tuple-element.24.params_ref.refs_4_, bf16[64,1536]{1,0:T(8,128)(2,1)S(1)} %collective-permute-done.11.s_ref, ...), custom_call_target="tpu_custom_call" | custom-call | flops 20000000000 | bytes 1024 | tf_op jit(solution)/shard_map/pallas_call | solution.py:370
  37.0 0.8 %collective-permute-start.12 = (bf16[32,1536]{1,0:T(8,128)(2,1)S(1)}, bf16[32,1536]{1,0:T(8,128)(2,1)S(1)}, u32[]{:S(2)}, u32[]{:S(2)}) collective-permute-start(bf16[32,1536]{1,0:T(8,128)(2,1)S(1)} %get-tuple-element.40), channel_id=1, source_target_pairs={{0,2},{2,0},{4,6},{6,4},{8,10},{10,8},{12,14},{14,12},{1,3},{3,1},... | collective-permute-start | bytes 294920 | tf_op jit(solution)/shard_map/ppermute | solution.py:336
  37.8 0.0 collective-permute-done.8.refs_1_
  37.8 0.2 collective-permute-start.13
  38.0 0.0 collective-permute-done.6.s_ref
  38.0 2.5 %collective-permute-start.14 = (bf16[32,1536]{1,0:T(8,128)(2,1)S(1)}, bf16[32,1536]{1,0:T(8,128)(2,1)S(1)}, u32[]{:S(2)}, u32[]{:S(2)}) collective-permute-start(bf16[32,1536]{1,0:T(8,128)(2,1)S(1)} %get-tuple-element.42), channel_id=1, source_target_pairs={{0,6},{2,4},{4,2},{6,0},{8,14},{10,12},{12,10},{14,8},{1,7},{3,5},... | collective-permute-start | bytes 294920 | tf_op jit(solution)/shard_map/ppermute | solution.py:336
  40.5 0.0 copy-done.4
  40.5 0.0 copy-done.5
  40.5 0.1 broadcast_in_dim.3
  40.6 0.1 reshape_reshape.3.skip_ref
  40.7 0.0 copy-done.1
  40.7 2.1 %shard_map.95 = (f32[256,1536]{1,0:T(8,128)S(1)}, f32[256,1536]{1,0:T(8,128)S(1)}) custom-call(f32[8,48]{1,0:T(8,128)S(1)} %get-tuple-element.24.params_ref.refs_4_, bf16[128,1536]{1,0:T(8,128)(2,1)S(1)} %collective-permute-done.6.s_ref, bf16[256,1536]{1,0:T(8,128)(2,1)S(1)} %bitcast.8, bf16[256,48]{1,0:T(8,128)(2,1)S(1)} %bitcast.12, ...), custom_call_target="tpu_custom_call" | custom-call | flops 1024 | bytes 1024 | tf_op jit(solution)/shard_map/pallas_call | solution.py:362
  42.8 0.0 collective-permute-done.9.refs_2_
  42.8 0.0 collective-permute-done.10.refs_3_
  42.8 0.0 collective-permute-done.12.refs_5_
  42.8 0.0 collective-permute-done.13.refs_6_
  42.8 1.4 %collective-permute-done.14.refs_7_ = bf16[32,1536]{1,0:T(8,128)(2,1)S(1)} collective-permute-done((bf16[32,1536]{1,0:T(8,128)(2,1)S(1)}, bf16[32,1536]{1,0:T(8,128)(2,1)S(1)}, u32[]{:S(2)}, u32[]{:S(2)}) %collective-permute-start.14) | collective-permute-done | bytes 98336 | tf_op jit(solution)/shard_map/ppermute | solution.py:336
  44.2 1.3 %shard_map.98 = bf16[256,1536]{1,0:T(8,128)(2,1)} custom-call(f32[256,1536]{1,0:T(8,128)S(1)} %get-tuple-element.33.w_ref, f32[256,1536]{1,0:T(8,128)S(1)} %get-tuple-element.34.g_ref, f32[1,1536]{1,0:T(1,128)S(1)} %reshape.22.gain_ref, bf16[32,1536]{1,0:T(8,128)(2,1)S(1)} %get-tuple-element.35.refs_4_.refs_0_, ...), custom_call_target="tpu_custom_call" | custom-call | flops 1024 | bytes 1024 | tf_op jit(solution)/shard_map/pallas_call | solution.py:378
  (1 shorter events, 0.0 us)
Async XLA Ops:
  0.0 21.9 %copy-start.2 = (bf16[1,32,8,48]{3,2,1,0:T(8,128)(2,1)S(1)}, bf16[1,32,8,48]{3,2,1,0:T(8,128)(2,1)}, u32[]{:S(2)}) copy-start(bf16[1,32,8,48]{3,2,1,0:T(8,128)(2,1)} %param.12) | copy-start | bytes 73732
  0.0 21.9 %copy-start.3 = (bf16[1,32,8,64]{3,2,1,0:T(8,128)(2,1)S(1)}, bf16[1,32,8,64]{3,2,1,0:T(8,128)(2,1)}, u32[]{:S(2)}) copy-start(bf16[1,32,8,64]{3,2,1,0:T(8,128)(2,1)} %param.11) | copy-start | bytes 98308
  0.0 21.9 %copy-start = (bf16[1,32,8,1536]{3,2,1,0:T(8,128)(2,1)S(1)}, bf16[1,32,8,1536]{3,2,1,0:T(8,128)(2,1)}, u32[]{:S(2)}) copy-start(bf16[1,32,8,1536]{3,2,1,0:T(8,128)(2,1)} %param.9) | copy-start | bytes 2359300
  2.2 8.1 %collective-permute-start.3 = (bf16[32,1664]{1,0:T(8,128)(2,1)S(1)}, bf16[32,1664]{1,0:T(8,128)(2,1)S(1)}, u32[]{:S(2)}, u32[]{:S(2)}) collective-permute-start(bf16[32,1664]{1,0:T(8,128)(2,1)S(1)} %get-tuple-element.30), channel_id=1, source_target_pairs={{0,2},{2,0},{4,6},{6,4},{8,10},{10,8},{12,14},{14,12},{1,3},{3,1},... | collective-permute-start | bytes 319496 | tf_op jit(solution)/shard_map/ppermute | solution.py:336
  5.2 5.8 %collective-permute-start.4 = (bf16[32,1664]{1,0:T(8,128)(2,1)S(1)}, bf16[32,1664]{1,0:T(8,128)(2,1)S(1)}, u32[]{:S(2)}, u32[]{:S(2)}) collective-permute-start(bf16[32,1664]{1,0:T(8,128)(2,1)S(1)} %get-tuple-element.31), channel_id=1, source_target_pairs={{0,4},{2,6},{4,0},{6,2},{8,12},{10,14},{12,8},{14,10},{1,5},{3,7},... | collective-permute-start | bytes 319496 | tf_op jit(solution)/shard_map/ppermute | solution.py:336
  6.8 6.9 %collective-permute-start.5 = (bf16[32,1664]{1,0:T(8,128)(2,1)S(1)}, bf16[32,1664]{1,0:T(8,128)(2,1)S(1)}, u32[]{:S(2)}, u32[]{:S(2)}) collective-permute-start(bf16[32,1664]{1,0:T(8,128)(2,1)S(1)} %get-tuple-element.32), channel_id=1, source_target_pairs={{0,6},{2,4},{4,2},{6,0},{8,14},{10,12},{12,10},{14,8},{1,7},{3,5},... | collective-permute-start | bytes 319496 | tf_op jit(solution)/shard_map/ppermute | solution.py:336
  6.8 10.6 %collective-permute-start = (bf16[32,1664]{1,0:T(8,128)(2,1)S(1)}, bf16[32,1664]{1,0:T(8,128)(2,1)S(1)}, u32[]{:S(2)}, u32[]{:S(2)}) collective-permute-start(bf16[32,1664]{1,0:T(8,128)(2,1)S(1)} %get-tuple-element.26), channel_id=1, source_target_pairs={{0,2},{2,0},{4,6},{6,4},{8,10},{10,8},{12,14},{14,12},{1,3},{3,1},... | collective-permute-start | bytes 319496 | tf_op jit(solution)/shard_map/ppermute | solution.py:336
  8.7 8.7 %collective-permute-start.1 = (bf16[32,1664]{1,0:T(8,128)(2,1)S(1)}, bf16[32,1664]{1,0:T(8,128)(2,1)S(1)}, u32[]{:S(2)}, u32[]{:S(2)}) collective-permute-start(bf16[32,1664]{1,0:T(8,128)(2,1)S(1)} %get-tuple-element.27), channel_id=1, source_target_pairs={{0,4},{2,6},{4,0},{6,2},{8,12},{10,14},{12,8},{14,10},{1,5},{3,7},... | collective-permute-start | bytes 319496 | tf_op jit(solution)/shard_map/ppermute | solution.py:336
  10.3 7.7 %collective-permute-start.2 = (bf16[32,1664]{1,0:T(8,128)(2,1)S(1)}, bf16[32,1664]{1,0:T(8,128)(2,1)S(1)}, u32[]{:S(2)}, u32[]{:S(2)}) collective-permute-start(bf16[32,1664]{1,0:T(8,128)(2,1)S(1)} %get-tuple-element.28), channel_id=1, source_target_pairs={{0,6},{2,4},{4,2},{6,0},{8,14},{10,12},{12,10},{14,8},{1,7},{3,5},... | collective-permute-start | bytes 319496 | tf_op jit(solution)/shard_map/ppermute | solution.py:336
  14.8 16.1 %collective-permute-start.7 = (bf16[64,1536]{1,0:T(8,128)(2,1)S(1)}, bf16[64,1536]{1,0:T(8,128)(2,1)S(1)}, u32[]{:S(2)}, u32[]{:S(2)}) collective-permute-start(bf16[64,1536]{1,0:T(8,128)(2,1)S(1)} %shard_map.92.refs_4_), channel_id=1, source_target_pairs={{0,8},{2,10},{4,12},{6,14},{8,0},{10,2},{12,4},{14,6},{1,9},{3,11}... | collective-permute-start | bytes 589832 | tf_op jit(solution)/shard_map/ppermute | solution.py:280
  19.1 16.6 %collective-permute-start.11 = (bf16[64,1536]{1,0:T(8,128)(2,1)S(1)}, bf16[64,1536]{1,0:T(8,128)(2,1)S(1)}, u32[]{:S(2)}, u32[]{:S(2)}) collective-permute-start(bf16[64,1536]{1,0:T(8,128)(2,1)S(1)} %shard_map.93._), channel_id=1, source_target_pairs={{0,8},{2,10},{4,12},{6,14},{8,0},{10,2},{12,4},{14,6},{1,9},{3,11}... | collective-permute-start | bytes 589832 | tf_op jit(solution)/shard_map/ppermute | solution.py:280
  23.4 14.6 %collective-permute-start.6 = (bf16[128,1536]{1,0:T(8,128)(2,1)S(1)}, bf16[128,1536]{1,0:T(8,128)(2,1)S(1)}, u32[]{:S(2)}, u32[]{:S(2)}) collective-permute-start(bf16[128,1536]{1,0:T(8,128)(2,1)S(1)} %shard_map.94), channel_id=1, source_target_pairs={{0,16},{16,0},{1,17},{17,1},{2,18},{18,2},{3,19},{19,3},{4,20},{20... | collective-permute-start | bytes 1179656 | tf_op jit(solution)/shard_map/ppermute | solution.py:280
  32.1 5.7 %collective-permute-start.8 = (bf16[32,1536]{1,0:T(8,128)(2,1)S(1)}, bf16[32,1536]{1,0:T(8,128)(2,1)S(1)}, u32[]{:S(2)}, u32[]{:S(2)}) collective-permute-start(bf16[32,1536]{1,0:T(8,128)(2,1)S(1)} %get-tuple-element.36), channel_id=1, source_target_pairs={{0,2},{2,0},{4,6},{6,4},{8,10},{10,8},{12,14},{14,12},{1,3},{3,1},... | collective-permute-start | bytes 294920 | tf_op jit(solution)/shard_map/ppermute | solution.py:336
  33.0 9.8 %collective-permute-start.9 = (bf16[32,1536]{1,0:T(8,128)(2,1)S(1)}, bf16[32,1536]{1,0:T(8,128)(2,1)S(1)}, u32[]{:S(2)}, u32[]{:S(2)}) collective-permute-start(bf16[32,1536]{1,0:T(8,128)(2,1)S(1)} %get-tuple-element.37), channel_id=1, source_target_pairs={{0,4},{2,6},{4,0},{6,2},{8,12},{10,14},{12,8},{14,10},{1,5},{3,7},... | collective-permute-start | bytes 294920 | tf_op jit(solution)/shard_map/ppermute | solution.py:336
  33.1 9.6 %collective-permute-start.10 = (bf16[32,1536]{1,0:T(8,128)(2,1)S(1)}, bf16[32,1536]{1,0:T(8,128)(2,1)S(1)}, u32[]{:S(2)}, u32[]{:S(2)}) collective-permute-start(bf16[32,1536]{1,0:T(8,128)(2,1)S(1)} %get-tuple-element.38), channel_id=1, source_target_pairs={{0,6},{2,4},{4,2},{6,0},{8,14},{10,12},{12,10},{14,8},{1,7},{3,5},... | collective-permute-start | bytes 294920 | tf_op jit(solution)/shard_map/ppermute | solution.py:336
  35.7 4.8 %copy-start.4 = (f32[1536]{0:T(1024)S(1)}, f32[1536]{0:T(1024)}, u32[]{:S(2)}) copy-start(f32[1536]{0:T(1024)} %param.17) | copy-start | bytes 18436
  35.7 4.8 %copy-start.5 = (f32[24]{0:T(128)S(1)}, f32[24]{0:T(128)}, u32[]{:S(2)}) copy-start(f32[24]{0:T(128)} %param.16) | copy-start | bytes 292
  35.7 5.0 %copy-start.1 = (bf16[1,32,8,1536]{3,2,1,0:T(8,128)(2,1)S(1)}, bf16[1,32,8,1536]{3,2,1,0:T(8,128)(2,1)}, u32[]{:S(2)}) copy-start(bf16[1,32,8,1536]{3,2,1,0:T(8,128)(2,1)} %param.10) | copy-start | bytes 2359300
  37.0 5.8 %collective-permute-start.12 = (bf16[32,1536]{1,0:T(8,128)(2,1)S(1)}, bf16[32,1536]{1,0:T(8,128)(2,1)S(1)}, u32[]{:S(2)}, u32[]{:S(2)}) collective-permute-start(bf16[32,1536]{1,0:T(8,128)(2,1)S(1)} %get-tuple-element.40), channel_id=1, source_target_pairs={{0,2},{2,0},{4,6},{6,4},{8,10},{10,8},{12,14},{14,12},{1,3},{3,1},... | collective-permute-start | bytes 294920 | tf_op jit(solution)/shard_map/ppermute | solution.py:336
  37.8 5.0 %collective-permute-start.13 = (bf16[32,1536]{1,0:T(8,128)(2,1)S(1)}, bf16[32,1536]{1,0:T(8,128)(2,1)S(1)}, u32[]{:S(2)}, u32[]{:S(2)}) collective-permute-start(bf16[32,1536]{1,0:T(8,128)(2,1)S(1)} %get-tuple-element.41), channel_id=1, source_target_pairs={{0,4},{2,6},{4,0},{6,2},{8,12},{10,14},{12,8},{14,10},{1,5},{3,7},... | collective-permute-start | bytes 294920 | tf_op jit(solution)/shard_map/ppermute | solution.py:336
  38.0 6.2 %collective-permute-start.14 = (bf16[32,1536]{1,0:T(8,128)(2,1)S(1)}, bf16[32,1536]{1,0:T(8,128)(2,1)S(1)}, u32[]{:S(2)}, u32[]{:S(2)}) collective-permute-start(bf16[32,1536]{1,0:T(8,128)(2,1)S(1)} %get-tuple-element.42), channel_id=1, source_target_pairs={{0,6},{2,4},{4,2},{6,0},{8,14},{10,12},{12,10},{14,8},{1,7},{3,5},... | collective-permute-start | bytes 294920 | tf_op jit(solution)/shard_map/ppermute | solution.py:336

commit v6 on v5

--- a/solution.py
+++ b/solution.py
@@ -111,37 +111,38 @@
     return [(first, min(STRIP, channels - first)) for first in range(0, channels, STRIP)]
 
 
-def pack_kernel(
-    index_ref, x_ref, raw_ref, maps_ref, table_ref, rates_ref, params_ref, *refs, group, axis, heads, state
-):
-    sent, (raw, maps, table, rates, sems) = refs[:-5], refs[-5:]
-    member = mod(lax.axis_index(axis), group)
-    pieces = len(sent) // group
-    share = x_ref.shape[0] // group
+def pack_places(sent, piece, pieces, share, axis):
+    member = mod(lax.axis_index(axis), len(sent))
     rows = share // pieces
-    channels = x_ref.shape[1]
-    small = [(raw_ref, raw), (maps_ref, maps), (table_ref, table), (rates_ref, rates)]
-    copies = [pltpu.make_async_copy(a, b, sems.at[i]) for i, (a, b) in enumerate(small)]
-    places = []
-    for piece in range(pieces):
-        for s in range(group):
-            first = pl.multiple_of(jnp.bitwise_xor(member, s) * share + piece * rows, rows)
-            out = sent[piece * group + s]
-            places.append((out, pl.ds(first, rows)))
-            copies.append(
-                pltpu.make_async_copy(
-                    x_ref.at[pl.ds(first, rows), :], out.at[:, pl.ds(0, channels)], sems.at[len(copies)]
-                )
-            )
-    for copy in copies:
-        copy.start()
-    for copy in copies[: len(small)]:
-        copy.wait()
+    return [
+        (out, pl.ds(pl.multiple_of(jnp.bitwise_xor(member, s) * share + piece * rows, rows), rows))
+        for s, out in enumerate(sent)
+    ]
+
+
+def pack_aux(places, raw, maps, channels, heads, state):
     used = heads + 2 * state
     for out, part in places:
         out[:, channels : channels + heads] = raw[part, :heads]
         out[:, channels + heads : channels + used] = maps[part, : 2 * state]
-        out[:, channels + used :] = jnp.zeros((rows, LANES - used), BF16)
+        out[:, channels + used :] = jnp.zeros((out.shape[0], LANES - used), BF16)
+
+
+def first_pack_kernel(
+    index_ref, x_ref, raw_ref, maps_ref, table_ref, rates_ref, params_ref, *refs, pieces, axis, heads, state
+):
+    sent, (raw, maps, table, rates, sems) = refs[:-5], refs[-5:]
+    channels = x_ref.shape[1]
+    places = pack_places(sent, 0, pieces, x_ref.shape[0] // len(sent), axis)
+    moved = [(raw_ref, raw), (maps_ref, maps), (table_ref, table), (rates_ref, rates)]
+    small = len(moved)
+    moved += [(x_ref.at[part, :], out.at[:, pl.ds(0, channels)]) for out, part in places]
+    copies = [pltpu.make_async_copy(a, b, sems.at[i]) for i, (a, b) in enumerate(moved)]
+    for copy in copies:
+        copy.start()
+    for copy in copies[:small]:
+        copy.wait()
+    pack_aux(places, raw, maps, channels, heads, state)
     row = jnp.where(iota(table.shape, 1) == index_ref[0], table[...], 0.0)
     ones = jnp.ones((8, table.shape[1]), BF16)
     bias = jnp.zeros((8, row.shape[0]), F32)
@@ -153,8 +154,16 @@
     params_ref[1:2, :heads] = rates[0:1, :]
     params_ref[1:2, heads:] = rates[1:2, :]
     params_ref[2:, :] = jnp.zeros((6, 2 * heads), F32)
-    for copy in copies[len(small) :]:
+    for copy in copies[small:]:
         copy.wait()
+
+
+def pack_kernel(x_ref, raw_ref, maps_ref, _, *sent, piece, pieces, axis, heads, state):
+    channels = x_ref.shape[1]
+    places = pack_places(sent, piece, pieces, x_ref.shape[0] // len(sent), axis)
+    for out, part in places:
+        out[:, :channels] = x_ref[part, :]
+    pack_aux(places, raw_ref, maps_ref, channels, heads, state)
 
 
 def row_scan(params_ref, blocks, member, cols, heads, state):
@@ -310,54 +319,64 @@
     any_spec = pl.BlockSpec(memory_space=pl.ANY)
     hbm_spec = pl.BlockSpec(memory_space=pltpu.HBM)
     full = lambda *dims: pl.BlockSpec(dims, lambda i, index: (0,) * len(dims))
-    packed = pl.pallas_call(
-        functools.partial(pack_kernel, heads=heads, state=state, **shared),
+    block = shape((share, channels + LANES), BF16)
+    given = [x, raw, maps, step_table.T, rates]
+    params, *packed = pl.pallas_call(
+        functools.partial(first_pack_kernel, pieces=PIECES, heads=heads, state=state, axis="col"),
         grid_spec=pltpu.PrefetchScalarGridSpec(
             num_scalar_prefetch=1,
             grid=(1,),
-            in_specs=[hbm_spec] * 5,
-            out_specs=[full(8, 2 * heads)] + [full(share, channels + LANES)] * (group * PIECES),
+            in_specs=[hbm_spec] * len(given),
+            out_specs=[full(8, 2 * heads)] + [full(*block.shape)] * group,
             scratch_shapes=[
                 pltpu.VMEM(raw.shape, BF16),
                 pltpu.VMEM(maps.shape, BF16),
                 pltpu.VMEM(step_table.shape[::-1], F32),
                 pltpu.VMEM(rates.shape, F32),
-                pltpu.SemaphoreType.DMA((4 + group * PIECES,)),
+                pltpu.SemaphoreType.DMA((len(given) - 1 + group,)),
             ],
         ),
-        out_shape=[pltpu.VMEM((8, 2 * heads), F32)] + [pltpu.VMEM((share, channels + LANES), BF16)] * (group * PIECES),
+        out_shape=[pltpu.VMEM((8, 2 * heads), F32)] + [pltpu.VMEM(block.shape, BF16)] * group,
         compiler_params=pltpu.CompilerParams(vmem_limit_bytes=32 * 1024 * 1024),
         cost_estimate=SMALL,
-    )(step_index, *[pltpu.with_memory_space_constraint(a, pltpu.HBM) for a in (x, raw, maps, step_table.T, rates)])
-    params, packed = packed[0], packed[1:]
+    )(step_index, *[pltpu.with_memory_space_constraint(a, pltpu.HBM) for a in given])
 
     def exchange(blocks):
-        return [blocks[0]] + [
-            lax.ppermute(blocks[s], "col", [(i, i ^ s) for i in range(col_count)]) for s in range(1, group)
-        ]
+        got = {0: blocks[0]}
+        for s in reversed(range(1, group)):
+            got[s] = lax.ppermute(blocks[s], "col", [(i, i ^ s) for i in range(col_count)])
+        return [got[s] for s in range(group)]
 
     def state_shapes(places, count):
         return [shape((places, channels), BF16)] + [shape((places, heads), F32)] * (count > 2)
 
-    got = [exchange(packed[piece * group : (piece + 1) * group]) for piece in range(PIECES)]
-
+    got = []
     row_entering = []
-    row_made = params
     for piece in range(PIECES):
+        before = params
+        if piece:
+            packed = call(
+                functools.partial(pack_kernel, piece=piece, pieces=PIECES, heads=heads, state=state, axis="col"),
+                [block] * group,
+                specs=[None] * 3 + [any_spec],
+            )(x, raw, maps, made[0])
+            before = packed[0]
+        got.append(exchange(packed))
+        if piece == PIECES - 1:
+            col_made = call(
+                functools.partial(col_state_kernel, **sizes),
+                state_shapes(cols * state, row_count),
+                specs=[None] * 4 + [any_spec],
+                cost=LONG,
+            )(params, x, raw, maps, before)
+            col_entering = entering_states(col_made, "row", row_count, 1, width)
+            before = col_made[0]
         made = call(
             functools.partial(row_state_kernel, **sizes, **shared),
             state_shapes(lines * state, col_count // group),
             specs=[None] * (1 + group) + [any_spec],
-        )(params, *got[piece], row_made)
-        row_made = made[0]
+        )(params, *got[piece], before)
         row_entering.append(entering_states(made, "col", col_count, group, width))
-
-    col_made = call(
-        functools.partial(col_state_kernel, **sizes),
-        state_shapes(cols * state, row_count),
-            specs=[None] * 4 + [any_spec],
-    )(params, x, raw, maps, row_made)
-    col_entering = entering_states(col_made, "row", row_count, 1, width)
 
     w, silu = call(
         functools.partial(col_out_kernel, **sizes),

time: 45.7 us -> 46.5 us (1.018)
  waiting for transfers between devices: 10.6 us -> 14.4 us
  starting transfers between devices: 22.9 us -> 19.9 us
    ppermute x12, waiting for transfers between devices: 4.68 us -> 11.9 us  [exchange(): lax.ppermute(blocks[s], 'col', [(i, i ^ s) for i in range(col_count)])]
    ppermute x3, waiting for transfers between devices: 5.91 us -> 2.59 us  [entering_states(): entering = lax.ppermute(ends, axis, onward)]
    ppermute x3, starting transfers between devices: 7 us -> 4.27 us  [entering_states(): entering = lax.ppermute(ends, axis, onward)]
    pallas_call x1 -> x2, Pallas kernels: 1.43 us -> 1.39 us  [the longest x1 1.28 us: body(): pl.pallas_call(functools.partial(first_pack_kernel, pieces=PIECES, heads=...]
  transfers between devices with their start and end apart: 15 -> 15, of which waited for: 5 -> 8; matrix products, arithmetic and copies ran while one was open for 0% -> 0% of each run, Pallas kernels for 18% -> 16%
where the time goes in v6:
time: 46.5 us; the launch traced here: 46.4 us
  starting transfers between devices  19.9 us (43%)
  waiting for transfers between devices  14.4 us (31%)
  Pallas kernels  11 us (24%)
  between operations  0.85 us (2%)
    ppermute x12, starting transfers between devices, exchange(): lax.ppermute(blocks[s], 'col', [(i, i ^ s) for i in range(col_count)])  15.6 us
    ppermute x12, waiting for transfers between devices, exchange(): lax.ppermute(blocks[s], 'col', [(i, i ^ s) for i in range(col_count)])  11.9 us
    ppermute x3, starting transfers between devices, entering_states(): entering = lax.ppermute(ends, axis, onward)  4.27 us
    ppermute x3, waiting for transfers between devices, entering_states(): entering = lax.ppermute(ends, axis, onward)  2.59 us
    pallas_call x2, Pallas kernels, body(): call(functools.partial(row_out_kernel, **sizes, **shared), [shape((share,...  2.5 us
    pallas_call x2, Pallas kernels, body(): call(functools.partial(row_state_kernel, **sizes, **shared), state_shapes...  2.22 us
    pallas_call x1, Pallas kernels, body(): call(functools.partial(col_out_kernel, **sizes), [shape((tokens, channels...  2.05 us
    pallas_call x1, Pallas kernels, body(): call(functools.partial(col_state_kernel, **sizes), state_shapes(cols * st...  1.47 us
  transfers between devices with their start and end apart: 15, of which 8 were waited for; matrix products, arithmetic and copies ran while one was open for 0% of the time, Pallas kernels for 16%

profile of v6, /device:TPU:0, one launch (start us, length us, event | category | flops | bytes accessed | tf_op | source)
XLA Modules:
  0.0 46.4 jit_solution(6138329929316978095)
XLA Ops:
  0.0 0.0 copy-start.2
  0.0 0.0 copy-start.3
  0.0 0.0 copy-start
  0.7 1.3 %shard_map.91 = (f32[8,48]{1,0:T(8,128)S(1)}, bf16[32,1664]{1,0:T(8,128)(2,1)S(1)}, bf16[32,1664]{1,0:T(8,128)(2,1)S(1)}, bf16[32,1664]{1,0:T(8,128)(2,1)S(1)}, bf16[32,1664]{1,0:T(8,128)(2,1)S(1)}) custom-call(s32[1]{0:T(128)S(6)} %copy.10.index_ref, bf16[256,1536]{1,0:T(8,128)(2,1)} %bitcast.6, bf16[256,48]{1,0:T(8,128)(2,1)} %bitcast.11, ...), custom_call_target="tpu_custom_call" | custom-call | flops 1024 | bytes 1024 | tf_op jit(solution)/shard_map/pallas_call | solution.py:324
  2.0 3.0 %collective-permute-start = (bf16[32,1664]{1,0:T(8,128)(2,1)S(1)}, bf16[32,1664]{1,0:T(8,128)(2,1)S(1)}, u32[]{:S(2)}, u32[]{:S(2)}) collective-permute-start(bf16[32,1664]{1,0:T(8,128)(2,1)S(1)} %get-tuple-element.26), channel_id=1, source_target_pairs={{0,2},{2,0},{4,6},{6,4},{8,10},{10,8},{12,14},{14,12},{1,3},{3,1},... | collective-permute-start | bytes 319496 | tf_op jit(solution)/shard_map/ppermute | solution.py:347
  5.1 1.6 %collective-permute-start.1 = (bf16[32,1664]{1,0:T(8,128)(2,1)S(1)}, bf16[32,1664]{1,0:T(8,128)(2,1)S(1)}, u32[]{:S(2)}, u32[]{:S(2)}) collective-permute-start(bf16[32,1664]{1,0:T(8,128)(2,1)S(1)} %get-tuple-element.27), channel_id=1, source_target_pairs={{0,4},{2,6},{4,0},{6,2},{8,12},{10,14},{12,8},{14,10},{1,5},{3,7},... | collective-permute-start | bytes 319496 | tf_op jit(solution)/shard_map/ppermute | solution.py:347
  6.6 0.0 collective-permute-start.2
  6.6 1.4 %collective-permute-done.refs_1_ = bf16[32,1664]{1,0:T(8,128)(2,1)S(1)} collective-permute-done((bf16[32,1664]{1,0:T(8,128)(2,1)S(1)}, bf16[32,1664]{1,0:T(8,128)(2,1)S(1)}, u32[]{:S(2)}, u32[]{:S(2)}) %collective-permute-start) | collective-permute-done | bytes 106528 | tf_op jit(solution)/shard_map/ppermute | solution.py:347
  8.0 2.7 %collective-permute-done.1.refs_2_ = bf16[32,1664]{1,0:T(8,128)(2,1)S(1)} collective-permute-done((bf16[32,1664]{1,0:T(8,128)(2,1)S(1)}, bf16[32,1664]{1,0:T(8,128)(2,1)S(1)}, u32[]{:S(2)}, u32[]{:S(2)}) %collective-permute-start.1) | collective-permute-done | bytes 106528 | tf_op jit(solution)/shard_map/ppermute | solution.py:347
  10.7 1.5 %collective-permute-done.2.refs_3_ = bf16[32,1664]{1,0:T(8,128)(2,1)S(1)} collective-permute-done((bf16[32,1664]{1,0:T(8,128)(2,1)S(1)}, bf16[32,1664]{1,0:T(8,128)(2,1)S(1)}, u32[]{:S(2)}, u32[]{:S(2)}) %collective-permute-start.2) | collective-permute-done | bytes 106528 | tf_op jit(solution)/shard_map/ppermute | solution.py:347
  12.2 1.1 %shard_map.92._ = bf16[64,1536]{1,0:T(8,128)(2,1)S(1)} custom-call(f32[8,48]{1,0:T(8,128)S(1)} %get-tuple-element.24.params_ref.refs_4_, bf16[32,1664]{1,0:T(8,128)(2,1)S(1)} %get-tuple-element.25.refs_0_, bf16[32,1664]{1,0:T(8,128)(2,1)S(1)} %collective-permute-done.refs_1_, bf16[32,1664]{1,0:T(8,128)(2,1)S(1)} %collective-permute-done.1.refs_2_, ...), custom_call_target="tpu_custom_call" | custom-call | flops 1024 | bytes 1024 | tf_op jit(solution)/shard_map/pallas_call | solution.py:374
  13.3 2.7 %collective-permute-start.4 = (bf16[64,1536]{1,0:T(8,128)(2,1)S(1)}, bf16[64,1536]{1,0:T(8,128)(2,1)S(1)}, u32[]{:S(2)}, u32[]{:S(2)}) collective-permute-start(bf16[64,1536]{1,0:T(8,128)(2,1)S(1)} %shard_map.92._), channel_id=1, source_target_pairs={{0,8},{2,10},{4,12},{6,14},{8,0},{10,2},{12,4},{14,6},{1,9},{3,11}... | collective-permute-start | bytes 589832 | tf_op jit(solution)/shard_map/ppermute | solution.py:289
  16.0 0.0 copy-done.2
  16.0 0.0 copy-done.3
  16.0 0.0 copy-done
  16.0 0.1 shard_map.93
  16.1 1.1 %collective-permute-start.8 = (bf16[32,1664]{1,0:T(8,128)(2,1)S(1)}, bf16[32,1664]{1,0:T(8,128)(2,1)S(1)}, u32[]{:S(2)}, u32[]{:S(2)}) collective-permute-start(bf16[32,1664]{1,0:T(8,128)(2,1)S(1)} %get-tuple-element.36), channel_id=1, source_target_pairs={{0,2},{2,0},{4,6},{6,4},{8,10},{10,8},{12,14},{14,12},{1,3},{3,1},... | collective-permute-start | bytes 319496 | tf_op jit(solution)/shard_map/ppermute | solution.py:347
  17.3 1.5 %collective-permute-start.9 = (bf16[32,1664]{1,0:T(8,128)(2,1)S(1)}, bf16[32,1664]{1,0:T(8,128)(2,1)S(1)}, u32[]{:S(2)}, u32[]{:S(2)}) collective-permute-start(bf16[32,1664]{1,0:T(8,128)(2,1)S(1)} %get-tuple-element.37), channel_id=1, source_target_pairs={{0,4},{2,6},{4,0},{6,2},{8,12},{10,14},{12,8},{14,10},{1,5},{3,7},... | collective-permute-start | bytes 319496 | tf_op jit(solution)/shard_map/ppermute | solution.py:347
  18.8 0.9 %collective-permute-start.10 = (bf16[32,1664]{1,0:T(8,128)(2,1)S(1)}, bf16[32,1664]{1,0:T(8,128)(2,1)S(1)}, u32[]{:S(2)}, u32[]{:S(2)}) collective-permute-start(bf16[32,1664]{1,0:T(8,128)(2,1)S(1)} %get-tuple-element.38), channel_id=1, source_target_pairs={{0,6},{2,4},{4,2},{6,0},{8,14},{10,12},{12,10},{14,8},{1,7},{3,5},... | collective-permute-start | bytes 319496 | tf_op jit(solution)/shard_map/ppermute | solution.py:347
  19.7 1.5 %shard_map.94.refs_4_ = bf16[128,1536]{1,0:T(8,128)(2,1)S(1)} custom-call(f32[8,48]{1,0:T(8,128)S(1)} %get-tuple-element.24.params_ref.refs_4_, bf16[256,1536]{1,0:T(8,128)(2,1)S(1)} %bitcast.8, bf16[256,48]{1,0:T(8,128)(2,1)S(1)} %bitcast.13, bf16[256,64]{1,0:T(8,128)(2,1)S(1)} %bitcast.17, bf16[32,1664]{1,0:T(8,128)(2,1)S(1)} %get-tuple-element.29._.refs_0_), custom_call_target="tpu_custom_call" | custom-call | flops 20000000000 | bytes 1024 | tf_op jit(solution)/shard_map/pallas_call | solution.py:366
  21.2 0.4 collective-permute-done.8.refs_1_
  21.6 3.3 %collective-permute-done.9.refs_2_ = bf16[32,1664]{1,0:T(8,128)(2,1)S(1)} collective-permute-done((bf16[32,1664]{1,0:T(8,128)(2,1)S(1)}, bf16[32,1664]{1,0:T(8,128)(2,1)S(1)}, u32[]{:S(2)}, u32[]{:S(2)}) %collective-permute-start.9) | collective-permute-done | bytes 106528 | tf_op jit(solution)/shard_map/ppermute | solution.py:347
  24.9 1.1 %collective-permute-done.10.refs_3_ = bf16[32,1664]{1,0:T(8,128)(2,1)S(1)} collective-permute-done((bf16[32,1664]{1,0:T(8,128)(2,1)S(1)}, bf16[32,1664]{1,0:T(8,128)(2,1)S(1)}, u32[]{:S(2)}, u32[]{:S(2)}) %collective-permute-start.10) | collective-permute-done | bytes 106528 | tf_op jit(solution)/shard_map/ppermute | solution.py:347
  26.0 1.1 %shard_map.97 = bf16[64,1536]{1,0:T(8,128)(2,1)S(1)} custom-call(f32[8,48]{1,0:T(8,128)S(1)} %get-tuple-element.24.params_ref.refs_4_, bf16[32,1664]{1,0:T(8,128)(2,1)S(1)} %get-tuple-element.29._.refs_0_, bf16[32,1664]{1,0:T(8,128)(2,1)S(1)} %collective-permute-done.8.refs_1_, bf16[32,1664]{1,0:T(8,128)(2,1)S(1)} %collective-permute-done.9.refs_2_, ...), custom_call_target="tpu_custom_call" | custom-call | flops 1024 | bytes 1024 | tf_op jit(solution)/shard_map/pallas_call | solution.py:374
  27.2 0.1 collective-permute-start.11
  27.3 1.5 %collective-permute-start.3 = (bf16[128,1536]{1,0:T(8,128)(2,1)S(1)}, bf16[128,1536]{1,0:T(8,128)(2,1)S(1)}, u32[]{:S(2)}, u32[]{:S(2)}) collective-permute-start(bf16[128,1536]{1,0:T(8,128)(2,1)S(1)} %shard_map.94.refs_4_), channel_id=1, source_target_pairs={{0,16},{16,0},{1,17},{17,1},{2,18},{18,2},{3,19},{19,3},{4,20},{20... | collective-permute-start | bytes 1179656 | tf_op jit(solution)/shard_map/ppermute | solution.py:289
  28.8 0.0 collective-permute-done.4.s_ref
  28.8 1.3 %shard_map.96 = (bf16[32,1536]{1,0:T(8,128)(2,1)S(1)}, bf16[32,1536]{1,0:T(8,128)(2,1)S(1)}, bf16[32,1536]{1,0:T(8,128)(2,1)S(1)}, bf16[32,1536]{1,0:T(8,128)(2,1)S(1)}) custom-call(f32[8,48]{1,0:T(8,128)S(1)} %get-tuple-element.24.params_ref.refs_4_, bf16[64,1536]{1,0:T(8,128)(2,1)S(1)} %collective-permute-done.4.s_ref, ...), custom_call_target="tpu_custom_call" | custom-call | flops 1024 | bytes 1024 | tf_op jit(solution)/shard_map/pallas_call | solution.py:389
  30.0 1.6 %collective-permute-start.5 = (bf16[32,1536]{1,0:T(8,128)(2,1)S(1)}, bf16[32,1536]{1,0:T(8,128)(2,1)S(1)}, u32[]{:S(2)}, u32[]{:S(2)}) collective-permute-start(bf16[32,1536]{1,0:T(8,128)(2,1)S(1)} %get-tuple-element.33), channel_id=1, source_target_pairs={{0,2},{2,0},{4,6},{6,4},{8,10},{10,8},{12,14},{14,12},{1,3},{3,1},... | collective-permute-start | bytes 294920 | tf_op jit(solution)/shard_map/ppermute | solution.py:347
  31.6 1.7 %collective-permute-start.6 = (bf16[32,1536]{1,0:T(8,128)(2,1)S(1)}, bf16[32,1536]{1,0:T(8,128)(2,1)S(1)}, u32[]{:S(2)}, u32[]{:S(2)}) collective-permute-start(bf16[32,1536]{1,0:T(8,128)(2,1)S(1)} %get-tuple-element.34), channel_id=1, source_target_pairs={{0,4},{2,6},{4,0},{6,2},{8,12},{10,14},{12,8},{14,10},{1,5},{3,7},... | collective-permute-start | bytes 294920 | tf_op jit(solution)/shard_map/ppermute | solution.py:347
  33.3 0.7 %collective-permute-start.7 = (bf16[32,1536]{1,0:T(8,128)(2,1)S(1)}, bf16[32,1536]{1,0:T(8,128)(2,1)S(1)}, u32[]{:S(2)}, u32[]{:S(2)}) collective-permute-start(bf16[32,1536]{1,0:T(8,128)(2,1)S(1)} %get-tuple-element.35), channel_id=1, source_target_pairs={{0,6},{2,4},{4,2},{6,0},{8,14},{10,12},{12,10},{14,8},{1,7},{3,5},... | collective-permute-start | bytes 294920 | tf_op jit(solution)/shard_map/ppermute | solution.py:347
  34.0 2.6 %collective-permute-done.11.s_ref = bf16[64,1536]{1,0:T(8,128)(2,1)S(1)} collective-permute-done((bf16[64,1536]{1,0:T(8,128)(2,1)S(1)}, bf16[64,1536]{1,0:T(8,128)(2,1)S(1)}, u32[]{:S(2)}, u32[]{:S(2)}) %collective-permute-start.11) | collective-permute-done | bytes 196640 | tf_op jit(solution)/shard_map/ppermute | solution.py:289
  36.5 0.0 copy-start.4
  36.5 0.0 copy-start.5
  36.6 0.0 copy-start.1
  36.6 1.2 %shard_map.98 = (bf16[32,1536]{1,0:T(8,128)(2,1)S(1)}, bf16[32,1536]{1,0:T(8,128)(2,1)S(1)}, bf16[32,1536]{1,0:T(8,128)(2,1)S(1)}, bf16[32,1536]{1,0:T(8,128)(2,1)S(1)}) custom-call(f32[8,48]{1,0:T(8,128)S(1)} %get-tuple-element.24.params_ref.refs_4_, bf16[64,1536]{1,0:T(8,128)(2,1)S(1)} %collective-permute-done.11.s_ref, ...), custom_call_target="tpu_custom_call" | custom-call | flops 20000000000 | bytes 1024 | tf_op jit(solution)/shard_map/pallas_call | solution.py:389
  37.8 0.7 %collective-permute-start.12 = (bf16[32,1536]{1,0:T(8,128)(2,1)S(1)}, bf16[32,1536]{1,0:T(8,128)(2,1)S(1)}, u32[]{:S(2)}, u32[]{:S(2)}) collective-permute-start(bf16[32,1536]{1,0:T(8,128)(2,1)S(1)} %get-tuple-element.40), channel_id=1, source_target_pairs={{0,2},{2,0},{4,6},{6,4},{8,10},{10,8},{12,14},{14,12},{1,3},{3,1},... | collective-permute-start | bytes 294920 | tf_op jit(solution)/shard_map/ppermute | solution.py:347
  38.5 0.0 collective-permute-done.5.refs_1_
  38.5 0.0 collective-permute-start.13
  38.5 0.0 collective-permute-done.3.s_ref
  38.5 2.8 %collective-permute-start.14 = (bf16[32,1536]{1,0:T(8,128)(2,1)S(1)}, bf16[32,1536]{1,0:T(8,128)(2,1)S(1)}, u32[]{:S(2)}, u32[]{:S(2)}) collective-permute-start(bf16[32,1536]{1,0:T(8,128)(2,1)S(1)} %get-tuple-element.42), channel_id=1, source_target_pairs={{0,6},{2,4},{4,2},{6,0},{8,14},{10,12},{12,10},{14,8},{1,7},{3,5},... | collective-permute-start | bytes 294920 | tf_op jit(solution)/shard_map/ppermute | solution.py:347
  41.4 0.0 copy-done.4
  41.4 0.0 copy-done.5
  41.4 0.1 broadcast_in_dim.3
  41.5 0.1 reshape_reshape.3.skip_ref
  41.5 0.0 copy-done.1
  41.5 2.0 %shard_map.95 = (f32[256,1536]{1,0:T(8,128)S(1)}, f32[256,1536]{1,0:T(8,128)S(1)}) custom-call(f32[8,48]{1,0:T(8,128)S(1)} %get-tuple-element.24.params_ref.refs_4_, bf16[128,1536]{1,0:T(8,128)(2,1)S(1)} %collective-permute-done.3.s_ref, bf16[256,1536]{1,0:T(8,128)(2,1)S(1)} %bitcast.9, bf16[256,48]{1,0:T(8,128)(2,1)S(1)} %bitcast.14, ...), custom_call_target="tpu_custom_call" | custom-call | flops 1024 | bytes 1024 | tf_op jit(solution)/shard_map/pallas_call | solution.py:381
  43.6 0.0 collective-permute-done.6.refs_2_
  43.6 0.0 collective-permute-done.7.refs_3_
  43.6 0.0 collective-permute-done.12.refs_5_
  43.6 0.0 collective-permute-done.13.refs_6_
  43.6 1.4 %collective-permute-done.14.refs_7_ = bf16[32,1536]{1,0:T(8,128)(2,1)S(1)} collective-permute-done((bf16[32,1536]{1,0:T(8,128)(2,1)S(1)}, bf16[32,1536]{1,0:T(8,128)(2,1)S(1)}, u32[]{:S(2)}, u32[]{:S(2)}) %collective-permute-start.14) | collective-permute-done | bytes 98336 | tf_op jit(solution)/shard_map/ppermute | solution.py:347
  45.0 1.3 %shard_map.99 = bf16[256,1536]{1,0:T(8,128)(2,1)} custom-call(f32[256,1536]{1,0:T(8,128)S(1)} %get-tuple-element.30.w_ref, f32[256,1536]{1,0:T(8,128)S(1)} %get-tuple-element.31.g_ref, f32[1,1536]{1,0:T(1,128)S(1)} %reshape.22.gain_ref, bf16[32,1536]{1,0:T(8,128)(2,1)S(1)} %get-tuple-element.32.refs_4_.refs_0_, ...), custom_call_target="tpu_custom_call" | custom-call | flops 1024 | bytes 1024 | tf_op jit(solution)/shard_map/pallas_call | solution.py:397
  (1 shorter events, 0.0 us)
Async XLA Ops:
  0.0 16.0 %copy-start.2 = (bf16[1,32,8,48]{3,2,1,0:T(8,128)(2,1)S(1)}, bf16[1,32,8,48]{3,2,1,0:T(8,128)(2,1)}, u32[]{:S(2)}) copy-start(bf16[1,32,8,48]{3,2,1,0:T(8,128)(2,1)} %param.12) | copy-start | bytes 73732
  0.0 16.0 %copy-start.3 = (bf16[1,32,8,64]{3,2,1,0:T(8,128)(2,1)S(1)}, bf16[1,32,8,64]{3,2,1,0:T(8,128)(2,1)}, u32[]{:S(2)}) copy-start(bf16[1,32,8,64]{3,2,1,0:T(8,128)(2,1)} %param.11) | copy-start | bytes 98308
  0.0 16.0 %copy-start = (bf16[1,32,8,1536]{3,2,1,0:T(8,128)(2,1)S(1)}, bf16[1,32,8,1536]{3,2,1,0:T(8,128)(2,1)}, u32[]{:S(2)}) copy-start(bf16[1,32,8,1536]{3,2,1,0:T(8,128)(2,1)} %param.9) | copy-start | bytes 2359300
  2.0 6.0 %collective-permute-start = (bf16[32,1664]{1,0:T(8,128)(2,1)S(1)}, bf16[32,1664]{1,0:T(8,128)(2,1)S(1)}, u32[]{:S(2)}, u32[]{:S(2)}) collective-permute-start(bf16[32,1664]{1,0:T(8,128)(2,1)S(1)} %get-tuple-element.26), channel_id=1, source_target_pairs={{0,2},{2,0},{4,6},{6,4},{8,10},{10,8},{12,14},{14,12},{1,3},{3,1},... | collective-permute-start | bytes 319496 | tf_op jit(solution)/shard_map/ppermute | solution.py:347
  5.1 5.7 %collective-permute-start.1 = (bf16[32,1664]{1,0:T(8,128)(2,1)S(1)}, bf16[32,1664]{1,0:T(8,128)(2,1)S(1)}, u32[]{:S(2)}, u32[]{:S(2)}) collective-permute-start(bf16[32,1664]{1,0:T(8,128)(2,1)S(1)} %get-tuple-element.27), channel_id=1, source_target_pairs={{0,4},{2,6},{4,0},{6,2},{8,12},{10,14},{12,8},{14,10},{1,5},{3,7},... | collective-permute-start | bytes 319496 | tf_op jit(solution)/shard_map/ppermute | solution.py:347
  6.6 5.6 %collective-permute-start.2 = (bf16[32,1664]{1,0:T(8,128)(2,1)S(1)}, bf16[32,1664]{1,0:T(8,128)(2,1)S(1)}, u32[]{:S(2)}, u32[]{:S(2)}) collective-permute-start(bf16[32,1664]{1,0:T(8,128)(2,1)S(1)} %get-tuple-element.28), channel_id=1, source_target_pairs={{0,6},{2,4},{4,2},{6,0},{8,14},{10,12},{12,10},{14,8},{1,7},{3,5},... | collective-permute-start | bytes 319496 | tf_op jit(solution)/shard_map/ppermute | solution.py:347
  13.3 15.4 %collective-permute-start.4 = (bf16[64,1536]{1,0:T(8,128)(2,1)S(1)}, bf16[64,1536]{1,0:T(8,128)(2,1)S(1)}, u32[]{:S(2)}, u32[]{:S(2)}) collective-permute-start(bf16[64,1536]{1,0:T(8,128)(2,1)S(1)} %shard_map.92._), channel_id=1, source_target_pairs={{0,8},{2,10},{4,12},{6,14},{8,0},{10,2},{12,4},{14,6},{1,9},{3,11}... | collective-permute-start | bytes 589832 | tf_op jit(solution)/shard_map/ppermute | solution.py:289
  16.1 5.4 %collective-permute-start.8 = (bf16[32,1664]{1,0:T(8,128)(2,1)S(1)}, bf16[32,1664]{1,0:T(8,128)(2,1)S(1)}, u32[]{:S(2)}, u32[]{:S(2)}) collective-permute-start(bf16[32,1664]{1,0:T(8,128)(2,1)S(1)} %get-tuple-element.36), channel_id=1, source_target_pairs={{0,2},{2,0},{4,6},{6,4},{8,10},{10,8},{12,14},{14,12},{1,3},{3,1},... | collective-permute-start | bytes 319496 | tf_op jit(solution)/shard_map/ppermute | solution.py:347
  17.3 7.6 %collective-permute-start.9 = (bf16[32,1664]{1,0:T(8,128)(2,1)S(1)}, bf16[32,1664]{1,0:T(8,128)(2,1)S(1)}, u32[]{:S(2)}, u32[]{:S(2)}) collective-permute-start(bf16[32,1664]{1,0:T(8,128)(2,1)S(1)} %get-tuple-element.37), channel_id=1, source_target_pairs={{0,4},{2,6},{4,0},{6,2},{8,12},{10,14},{12,8},{14,10},{1,5},{3,7},... | collective-permute-start | bytes 319496 | tf_op jit(solution)/shard_map/ppermute | solution.py:347
  18.8 7.3 %collective-permute-start.10 = (bf16[32,1664]{1,0:T(8,128)(2,1)S(1)}, bf16[32,1664]{1,0:T(8,128)(2,1)S(1)}, u32[]{:S(2)}, u32[]{:S(2)}) collective-permute-start(bf16[32,1664]{1,0:T(8,128)(2,1)S(1)} %get-tuple-element.38), channel_id=1, source_target_pairs={{0,6},{2,4},{4,2},{6,0},{8,14},{10,12},{12,10},{14,8},{1,7},{3,5},... | collective-permute-start | bytes 319496 | tf_op jit(solution)/shard_map/ppermute | solution.py:347
  27.2 9.4 %collective-permute-start.11 = (bf16[64,1536]{1,0:T(8,128)(2,1)S(1)}, bf16[64,1536]{1,0:T(8,128)(2,1)S(1)}, u32[]{:S(2)}, u32[]{:S(2)}) collective-permute-start(bf16[64,1536]{1,0:T(8,128)(2,1)S(1)} %shard_map.97), channel_id=1, source_target_pairs={{0,8},{2,10},{4,12},{6,14},{8,0},{10,2},{12,4},{14,6},{1,9},{3,11}... | collective-permute-start | bytes 589832 | tf_op jit(solution)/shard_map/ppermute | solution.py:289
  27.3 11.3 %collective-permute-start.3 = (bf16[128,1536]{1,0:T(8,128)(2,1)S(1)}, bf16[128,1536]{1,0:T(8,128)(2,1)S(1)}, u32[]{:S(2)}, u32[]{:S(2)}) collective-permute-start(bf16[128,1536]{1,0:T(8,128)(2,1)S(1)} %shard_map.94.refs_4_), channel_id=1, source_target_pairs={{0,16},{16,0},{1,17},{17,1},{2,18},{18,2},{3,19},{19,3},{4,20},{20... | collective-permute-start | bytes 1179656 | tf_op jit(solution)/shard_map/ppermute | solution.py:289
  30.0 8.5 %collective-permute-start.5 = (bf16[32,1536]{1,0:T(8,128)(2,1)S(1)}, bf16[32,1536]{1,0:T(8,128)(2,1)S(1)}, u32[]{:S(2)}, u32[]{:S(2)}) collective-permute-start(bf16[32,1536]{1,0:T(8,128)(2,1)S(1)} %get-tuple-element.33), channel_id=1, source_target_pairs={{0,2},{2,0},{4,6},{6,4},{8,10},{10,8},{12,14},{14,12},{1,3},{3,1},... | collective-permute-start | bytes 294920 | tf_op jit(solution)/shard_map/ppermute | solution.py:347
  31.6 12.0 %collective-permute-start.6 = (bf16[32,1536]{1,0:T(8,128)(2,1)S(1)}, bf16[32,1536]{1,0:T(8,128)(2,1)S(1)}, u32[]{:S(2)}, u32[]{:S(2)}) collective-permute-start(bf16[32,1536]{1,0:T(8,128)(2,1)S(1)} %get-tuple-element.34), channel_id=1, source_target_pairs={{0,4},{2,6},{4,0},{6,2},{8,12},{10,14},{12,8},{14,10},{1,5},{3,7},... | collective-permute-start | bytes 294920 | tf_op jit(solution)/shard_map/ppermute | solution.py:347
  33.3 10.3 %collective-permute-start.7 = (bf16[32,1536]{1,0:T(8,128)(2,1)S(1)}, bf16[32,1536]{1,0:T(8,128)(2,1)S(1)}, u32[]{:S(2)}, u32[]{:S(2)}) collective-permute-start(bf16[32,1536]{1,0:T(8,128)(2,1)S(1)} %get-tuple-element.35), channel_id=1, source_target_pairs={{0,6},{2,4},{4,2},{6,0},{8,14},{10,12},{12,10},{14,8},{1,7},{3,5},... | collective-permute-start | bytes 294920 | tf_op jit(solution)/shard_map/ppermute | solution.py:347
  36.5 4.8 %copy-start.4 = (f32[1536]{0:T(1024)S(1)}, f32[1536]{0:T(1024)}, u32[]{:S(2)}) copy-start(f32[1536]{0:T(1024)} %param.17) | copy-start | bytes 18436
  36.5 4.8 %copy-start.5 = (f32[24]{0:T(128)S(1)}, f32[24]{0:T(128)}, u32[]{:S(2)}) copy-start(f32[24]{0:T(128)} %param.16) | copy-start | bytes 292
  36.6 5.0 %copy-start.1 = (bf16[1,32,8,1536]{3,2,1,0:T(8,128)(2,1)S(1)}, bf16[1,32,8,1536]{3,2,1,0:T(8,128)(2,1)}, u32[]{:S(2)}) copy-start(bf16[1,32,8,1536]{3,2,1,0:T(8,128)(2,1)} %param.10) | copy-start | bytes 2359300
  37.8 5.8 %collective-permute-start.12 = (bf16[32,1536]{1,0:T(8,128)(2,1)S(1)}, bf16[32,1536]{1,0:T(8,128)(2,1)S(1)}, u32[]{:S(2)}, u32[]{:S(2)}) collective-permute-start(bf16[32,1536]{1,0:T(8,128)(2,1)S(1)} %get-tuple-element.40), channel_id=1, source_target_pairs={{0,2},{2,0},{4,6},{6,4},{8,10},{10,8},{12,14},{14,12},{1,3},{3,1},... | collective-permute-start | bytes 294920 | tf_op jit(solution)/shard_map/ppermute | solution.py:347
  38.5 5.1 %collective-permute-start.13 = (bf16[32,1536]{1,0:T(8,128)(2,1)S(1)}, bf16[32,1536]{1,0:T(8,128)(2,1)S(1)}, u32[]{:S(2)}, u32[]{:S(2)}) collective-permute-start(bf16[32,1536]{1,0:T(8,128)(2,1)S(1)} %get-tuple-element.41), channel_id=1, source_target_pairs={{0,4},{2,6},{4,0},{6,2},{8,12},{10,14},{12,8},{14,10},{1,5},{3,7},... | collective-permute-start | bytes 294920 | tf_op jit(solution)/shard_map/ppermute | solution.py:347
  38.5 6.5 %collective-permute-start.14 = (bf16[32,1536]{1,0:T(8,128)(2,1)S(1)}, bf16[32,1536]{1,0:T(8,128)(2,1)S(1)}, u32[]{:S(2)}, u32[]{:S(2)}) collective-permute-start(bf16[32,1536]{1,0:T(8,128)(2,1)S(1)} %get-tuple-element.42), channel_id=1, source_target_pairs={{0,6},{2,4},{4,2},{6,0},{8,14},{10,12},{12,10},{14,8},{1,7},{3,5},... | collective-permute-start | bytes 294920 | tf_op jit(solution)/shard_map/ppermute | solution.py:347

commit v7 on v5

--- a/solution.py
+++ b/solution.py
@@ -9,7 +9,7 @@
 
 LANES = 128
 GROUP = 4
-PIECES = 2
+LATER = 4
 STRIP = 512
 F32 = jnp.float32
 BF16 = jnp.bfloat16
@@ -112,49 +112,51 @@
 
 
 def pack_kernel(
-    index_ref, x_ref, raw_ref, maps_ref, table_ref, rates_ref, params_ref, *refs, group, axis, heads, state
+    x_ref, raw_ref, maps_ref, table_ref, rates_ref, raw, maps, table, rates, *refs, group, axis, heads, state
 ):
-    sent, (raw, maps, table, rates, sems) = refs[:-5], refs[-5:]
+    sent, sems = refs[:-1], refs[-1]
+    channels = x_ref.shape[1]
+    share = x_ref.shape[0] // group
     member = mod(lax.axis_index(axis), group)
-    pieces = len(sent) // group
-    share = x_ref.shape[0] // group
-    rows = share // pieces
-    channels = x_ref.shape[1]
-    small = [(raw_ref, raw), (maps_ref, maps), (table_ref, table), (rates_ref, rates)]
-    copies = [pltpu.make_async_copy(a, b, sems.at[i]) for i, (a, b) in enumerate(small)]
+    moved = [(raw_ref, raw), (maps_ref, maps)]
     places = []
-    for piece in range(pieces):
-        for s in range(group):
-            first = pl.multiple_of(jnp.bitwise_xor(member, s) * share + piece * rows, rows)
-            out = sent[piece * group + s]
-            places.append((out, pl.ds(first, rows)))
-            copies.append(
-                pltpu.make_async_copy(
-                    x_ref.at[pl.ds(first, rows), :], out.at[:, pl.ds(0, channels)], sems.at[len(copies)]
-                )
-            )
+    offset = 0
+    for i, out in enumerate(sent):
+        rows = out.shape[0]
+        first = jnp.bitwise_xor(member, i % group) * share + offset
+        part = pl.ds(pl.multiple_of(first, 16), rows)
+        places.append((out, part))
+        moved.append((x_ref.at[part, :], out.at[:, pl.ds(0, channels)]))
+        if i % group == group - 1:
+            offset += rows
+    moved += [(table_ref, table), (rates_ref, rates)]
+    copies = [pltpu.make_async_copy(a, b, sems.at[i]) for i, (a, b) in enumerate(moved)]
     for copy in copies:
         copy.start()
-    for copy in copies[: len(small)]:
+    for copy in copies[:2]:
         copy.wait()
     used = heads + 2 * state
     for out, part in places:
         out[:, channels : channels + heads] = raw[part, :heads]
         out[:, channels + heads : channels + used] = maps[part, : 2 * state]
-        out[:, channels + used :] = jnp.zeros((rows, LANES - used), BF16)
-    row = jnp.where(iota(table.shape, 1) == index_ref[0], table[...], 0.0)
-    ones = jnp.ones((8, table.shape[1]), BF16)
+        out[:, channels + used :] = jnp.zeros((out.shape[0], LANES - used), BF16)
+    for copy in copies[2:]:
+        copy.wait()
+
+
+def params_kernel(index_ref, table_ref, rates_ref, params_ref):
+    heads = rates_ref.shape[1]
+    row = jnp.where(iota(table_ref.shape, 1) == index_ref[0], table_ref[...], 0.0)
+    ones = jnp.ones((8, table_ref.shape[1]), BF16)
     bias = jnp.zeros((8, row.shape[0]), F32)
     for _ in range(3):
         term = row.astype(BF16)
         row = row - term.astype(F32)
         bias += lax.dot_general(ones, term, (((1,), (1,)), ((), ())), preferred_element_type=F32)
     params_ref[0:1, :] = bias[0:1, :]
-    params_ref[1:2, :heads] = rates[0:1, :]
-    params_ref[1:2, heads:] = rates[1:2, :]
+    params_ref[1:2, :heads] = rates_ref[0:1, :]
+    params_ref[1:2, heads:] = rates_ref[1:2, :]
     params_ref[2:, :] = jnp.zeros((6, 2 * heads), F32)
-    for copy in copies[len(small) :]:
-        copy.wait()
 
 
 def row_scan(params_ref, blocks, member, cols, heads, state):
@@ -207,7 +209,7 @@
     write_state(scan, tokens_of, width, s_ref.shape[1], s_ref, factor_ref)
 
 
-def col_state_kernel(params_ref, x_ref, raw_ref, maps_ref, _, s_ref, *factor_ref, cols, heads, state, width):
+def col_state_kernel(params_ref, x_ref, raw_ref, maps_ref, s_ref, *factor_ref, cols, heads, state, width):
     scan = col_scan(params_ref, raw_ref, maps_ref, cols, heads, state)
     tokens_of = lambda first, count: x_ref[:, first : first + count].astype(F32)
     write_state(scan, tokens_of, width, s_ref.shape[1], s_ref, factor_ref)
@@ -243,32 +245,35 @@
         g_ref[:, part] = gate / (1.0 + jnp.exp(-gate))
 
 
-def final_kernel(w_ref, g_ref, gain_ref, *refs, group, axis):
-    rows_of, out_ref = refs[:-1], refs[-1]
-    pieces = len(rows_of) // group
-    rows, channels = rows_of[0].shape
+def final_kernel(w_ref, g_ref, gain_ref, *refs, group, axis, offset, share):
+    blocks, (out_ref, made, sems) = refs[:group], refs[-3:]
+    rows, channels = blocks[0].shape
     member = mod(lax.axis_index(axis), group)
-    for piece in range(pieces):
-        for s in range(group):
-            first = (jnp.bitwise_xor(member, s) * pieces + piece) * rows
-            part = pl.ds(pl.multiple_of(first, rows), rows)
-            v = (rows_of[piece * group + s][...].astype(F32) + w_ref[part, :]) * g_ref[part, :]
-            power = jnp.sum(v * v, axis=1, keepdims=True) / channels
-            out_ref[part, :] = (v * lax.rsqrt(power + 1e-5) * gain_ref[...]).astype(BF16)
+    copies = []
+    for s in range(group):
+        part = pl.ds(pl.multiple_of(jnp.bitwise_xor(member, s) * share + offset, 16), rows)
+        v = (blocks[s][...].astype(F32) + w_ref[part, :]) * g_ref[part, :]
+        power = jnp.sum(v * v, axis=1, keepdims=True) / channels
+        made[s] = (v * lax.rsqrt(power + 1e-5) * gain_ref[...]).astype(BF16)
+        copies.append(pltpu.make_async_copy(made.at[s], out_ref.at[part, :], sems.at[s]))
+        copies[-1].start()
+    for copy in copies:
+        copy.wait()
 
 
 SMALL = pl.CostEstimate(flops=1024, bytes_accessed=1024, transcendentals=0)
 LONG = pl.CostEstimate(flops=2 * 10**10, bytes_accessed=1024, transcendentals=0)
 
 
-def call(kernel, out_shape, specs=None, cost=SMALL):
-    more = {} if specs is None else dict(in_specs=[spec or pl.BlockSpec() for spec in specs])
+def call(kernel, out_shape, specs=None, cost=SMALL, **more):
+    if specs is not None:
+        more["in_specs"] = [spec or pl.BlockSpec() for spec in specs]
     return pl.pallas_call(
         kernel,
-        **more,
         out_shape=out_shape,
         compiler_params=pltpu.CompilerParams(vmem_limit_bytes=32 * 1024 * 1024),
         cost_estimate=cost,
+        **more,
     )
 
 
@@ -296,8 +301,9 @@
     group = GROUP
     while col_count % group:
         group //= 2
-    share = tokens // group // PIECES
-    lines = share // cols
+    share = tokens // group
+    later = max(share // LATER, 16)
+    pieces = [share - later, later]
 
     x = x_in.reshape(tokens, channels)
     gate = gate_in.reshape(tokens, channels)
@@ -306,30 +312,33 @@
     sizes = dict(cols=cols, heads=heads, state=state, width=width)
     shared = dict(group=group, axis="col")
     shape = jax.ShapeDtypeStruct
-
     any_spec = pl.BlockSpec(memory_space=pl.ANY)
-    hbm_spec = pl.BlockSpec(memory_space=pltpu.HBM)
-    full = lambda *dims: pl.BlockSpec(dims, lambda i, index: (0,) * len(dims))
-    packed = pl.pallas_call(
+
+    given = [x, raw, maps, step_table.T, rates]
+    raw, maps, table, rates, *packed = pl.pallas_call(
         functools.partial(pack_kernel, heads=heads, state=state, **shared),
+        in_specs=[pl.BlockSpec(memory_space=pltpu.HBM)] * len(given),
+        out_shape=[pltpu.VMEM(a.shape, a.dtype) for a in given[1:]]
+        + [pltpu.VMEM((rows, channels + LANES), BF16) for rows in pieces for _ in range(group)],
+        scratch_shapes=[pltpu.SemaphoreType.DMA((len(given) - 1 + group * len(pieces),))],
+        compiler_params=pltpu.CompilerParams(vmem_limit_bytes=32 * 1024 * 1024),
+        cost_estimate=SMALL,
+    )(*[pltpu.with_memory_space_constraint(a, pltpu.HBM) for a in given])
+    index, rates = lax.optimization_barrier((step_index, rates))
+    params = pl.pallas_call(
+        params_kernel,
         grid_spec=pltpu.PrefetchScalarGridSpec(
             num_scalar_prefetch=1,
             grid=(1,),
-            in_specs=[hbm_spec] * 5,
-            out_specs=[full(8, 2 * heads)] + [full(share, channels + LANES)] * (group * PIECES),
-            scratch_shapes=[
-                pltpu.VMEM(raw.shape, BF16),
-                pltpu.VMEM(maps.shape, BF16),
-                pltpu.VMEM(step_table.shape[::-1], F32),
-                pltpu.VMEM(rates.shape, F32),
-                pltpu.SemaphoreType.DMA((4 + group * PIECES,)),
+            in_specs=[
+                pl.BlockSpec(table.shape, lambda i, index: (0, 0)),
+                pl.BlockSpec(rates.shape, lambda i, index: (0, 0)),
             ],
+            out_specs=pl.BlockSpec((8, 2 * heads), lambda i, index: (0, 0)),
         ),
-        out_shape=[pltpu.VMEM((8, 2 * heads), F32)] + [pltpu.VMEM((share, channels + LANES), BF16)] * (group * PIECES),
-        compiler_params=pltpu.CompilerParams(vmem_limit_bytes=32 * 1024 * 1024),
+        out_shape=shape((8, 2 * heads), F32),
         cost_estimate=SMALL,
-    )(step_index, *[pltpu.with_memory_space_constraint(a, pltpu.HBM) for a in (x, raw, maps, step_table.T, rates)])
-    params, packed = packed[0], packed[1:]
+    )(index, table, rates)
 
     def exchange(blocks):
         return [blocks[0]] + [
@@ -339,25 +348,23 @@
     def state_shapes(places, count):
         return [shape((places, channels), BF16)] + [shape((places, heads), F32)] * (count > 2)
 
-    got = [exchange(packed[piece * group : (piece + 1) * group]) for piece in range(PIECES)]
-
-    row_entering = []
-    row_made = params
-    for piece in range(PIECES):
-        made = call(
-            functools.partial(row_state_kernel, **sizes, **shared),
-            state_shapes(lines * state, col_count // group),
-            specs=[None] * (1 + group) + [any_spec],
-        )(params, *got[piece], row_made)
-        row_made = made[0]
-        row_entering.append(entering_states(made, "col", col_count, group, width))
-
+    got = [exchange(packed[i * group : (i + 1) * group]) for i in range(len(pieces))]
     col_made = call(
         functools.partial(col_state_kernel, **sizes),
         state_shapes(cols * state, row_count),
-            specs=[None] * 4 + [any_spec],
-    )(params, x, raw, maps, row_made)
+    )(params, x, raw, maps)
     col_entering = entering_states(col_made, "row", row_count, 1, width)
+    row_entering = []
+    before = col_made[0]
+    for i, rows in enumerate(pieces):
+        made = call(
+            functools.partial(row_state_kernel, **sizes, **shared),
+            state_shapes(rows // cols * state, col_count // group),
+            specs=[None] * (1 + group) + [any_spec],
+            cost=LONG if i else SMALL,
+        )(params, *got[i], before)
+        before = made[0]
+        row_entering.append(entering_states(made, "col", col_count, group, width))
 
     w, silu = call(
         functools.partial(col_out_kernel, **sizes),
@@ -365,20 +372,28 @@
     )(params, col_entering, x, raw, maps, gate, jnp.repeat(skip, width).reshape(1, channels))
 
     back = []
-    y_row = [params]
-    for piece in range(PIECES):
+    before = w
+    for i, rows in enumerate(pieces):
         y_row = call(
             functools.partial(row_out_kernel, **sizes, **shared),
-            [shape((share, channels), BF16)] * group,
+            [shape((rows, channels), BF16)] * group,
             specs=[None] * (2 + group) + [any_spec],
-            cost=LONG if piece == PIECES - 1 else SMALL,
-        )(params, row_entering[piece], *got[piece], y_row[0])
-        back += exchange(y_row)
-
-    mixed = call(
-        functools.partial(final_kernel, **shared),
-        shape((tokens, channels), BF16),
-    )(w, silu, norm_gain.reshape(1, channels), *back)
+            cost=LONG if i else SMALL,
+        )(params, row_entering[i], *got[i], before)
+        back.append(exchange(y_row))
+        before = y_row[0]
+
+    mixed = None
+    for i, rows in enumerate(pieces):
+        more = [] if mixed is None else [mixed]
+        mixed = call(
+            functools.partial(final_kernel, offset=sum(pieces[:i]), share=share, **shared),
+            shape((tokens, channels), BF16),
+            specs=[None] * (3 + group) + [any_spec] * len(more),
+            out_specs=any_spec,
+            scratch_shapes=[pltpu.VMEM((group, rows, channels), BF16), pltpu.SemaphoreType.DMA((group,))],
+            input_output_aliases={3 + group: 0} if more else {},
+        )(w, silu, norm_gain.reshape(1, channels), *back[i], *more)
     return mixed.reshape(x_in.shape)
 
 

time: 45.7 us -> 53.9 us (1.18)
  local copies, waits for them, and re-layouts: 0.18 us -> 5.68 us
  Pallas kernels: 11 us -> 14.9 us
  starting transfers between devices: 22.9 us -> 20.4 us
  waiting for transfers between devices: 10.6 us -> 11.7 us
    unnamed x12 -> x38, local copies, waits for them, and re-layouts: 0.02 us -> 5.52 us
    ppermute x3, starting transfers between devices: 7 us -> 4.47 us  [entering_states(): entering = lax.ppermute(ends, axis, onward)]
    pallas_call x3 -> x5, Pallas kernels: 3.84 us -> 6.3 us  [the longest x2 2.61 us: body(): call(functools.partial(row_out_kernel, **sizes, **shared), [shape((rows,...]
    pallas_call x2, Pallas kernels: 2.2 us -> 3.57 us  [body(): call(functools.partial(row_state_kernel, **sizes, **shared), state_shapes...]
    ppermute x12, waiting for transfers between devices: 4.68 us -> 5.68 us  [exchange(): lax.ppermute(blocks[s], 'col', [(i, i ^ s) for i in range(col_count)])]
  transfers between devices with their start and end apart: 15 -> 15, of which waited for: 5 -> 4; matrix products, arithmetic and copies ran while one was open for 0% -> 0% of each run, Pallas kernels for 18% -> 23%
where the time goes in v7:
time: 53.9 us; the launch traced here: 53.6 us
  starting transfers between devices  20.4 us (38%)
  Pallas kernels  14.9 us (28%)
  waiting for transfers between devices  11.7 us (22%)
  local copies, waits for them, and re-layouts  5.68 us (11%)
  between operations  0.84 us (2%)
    ppermute x12, starting transfers between devices, exchange(): lax.ppermute(blocks[s], 'col', [(i, i ^ s) for i in range(col_count)])  16 us
    ppermute x3, waiting for transfers between devices, entering_states(): entering = lax.ppermute(ends, axis, onward)  6.02 us
    ppermute x12, waiting for transfers between devices, exchange(): lax.ppermute(blocks[s], 'col', [(i, i ^ s) for i in range(col_count)])  5.68 us
    unnamed x38, local copies, waits for them, and re-layouts  5.52 us
    ppermute x3, starting transfers between devices, entering_states(): entering = lax.ppermute(ends, axis, onward)  4.47 us
    pallas_call x2, Pallas kernels, body(): call(functools.partial(row_state_kernel, **sizes, **shared), state_shapes...  3.57 us
    pallas_call x2, Pallas kernels, body(): call(functools.partial(row_out_kernel, **sizes, **shared), [shape((rows,...  2.61 us
    pallas_call x1, Pallas kernels, body(): call(functools.partial(col_out_kernel, **sizes), [shape((tokens, channels...  2.05 us
  transfers between devices with their start and end apart: 15, of which 4 were waited for; matrix products, arithmetic and copies ran while one was open for 0% of the time, Pallas kernels for 23%

profile of v7, /device:TPU:0, one launch (start us, length us, event | category | flops | bytes accessed | tf_op | source)
XLA Modules:
  0.0 53.6 jit_solution(6994073280282893940)
XLA Ops:
  0.0 1.5 %shard_map.91 = (bf16[256,48]{1,0:T(8,128)(2,1)S(1)}, bf16[256,64]{1,0:T(8,128)(2,1)S(1)}, f32[48,1000]{1,0:T(8,128)S(1)}, f32[2,24]{1,0:T(2,128)S(1)}, bf16[48,...) custom-call(bf16[256,1536]{1,0:T(8,128)(2,1)} %bitcast.6, ...), custom_call_target="tpu_custom_call" | custom-call | flops 1024 | bytes 1024 | tf_op jit(solution)/shard_map/pallas_call | solution.py:318
  1.5 0.0 copy-start.2
  1.5 0.7 %copy-done.2 = f32[48,1000]{1,0:T(8,128)} copy-done((f32[48,1000]{1,0:T(8,128)}, f32[48,1000]{1,0:T(8,128)S(1)}, u32[]{:S(2)}) %copy-start.2) | copy-done | bytes 192024
  2.2 3.0 %collective-permute-start.4 = (bf16[48,1664]{1,0:T(8,128)(2,1)S(1)}, bf16[48,1664]{1,0:T(8,128)(2,1)S(1)}, u32[]{:S(2)}, u32[]{:S(2)}) collective-permute-start(bf16[48,1664]{1,0:T(8,128)(2,1)S(1)} %get-tuple-element.42), channel_id=1, source_target_pairs={{0,2},{2,0},{4,6},{6,4},{8,10},{10,8},{12,14},{14,12},{1,3},{3,1},... | collective-permute-start | bytes 479240 | tf_op jit(solution)/shard_map/ppermute | solution.py:345
  5.1 1.6 %collective-permute-start.5 = (bf16[48,1664]{1,0:T(8,128)(2,1)S(1)}, bf16[48,1664]{1,0:T(8,128)(2,1)S(1)}, u32[]{:S(2)}, u32[]{:S(2)}) collective-permute-start(bf16[48,1664]{1,0:T(8,128)(2,1)S(1)} %get-tuple-element.43), channel_id=1, source_target_pairs={{0,4},{2,6},{4,0},{6,2},{8,12},{10,14},{12,8},{14,10},{1,5},{3,7},... | collective-permute-start | bytes 479240 | tf_op jit(solution)/shard_map/ppermute | solution.py:345
  6.7 0.0 collective-permute-start.6
  6.7 1.9 %collective-permute-start.1 = (bf16[16,1664]{1,0:T(8,128)(2,1)S(1)}, bf16[16,1664]{1,0:T(8,128)(2,1)S(1)}, u32[]{:S(2)}, u32[]{:S(2)}) collective-permute-start(bf16[16,1664]{1,0:T(8,128)(2,1)S(1)} %get-tuple-element.38), channel_id=1, source_target_pairs={{0,2},{2,0},{4,6},{6,4},{8,10},{10,8},{12,14},{14,12},{1,3},{3,1},... | collective-permute-start | bytes 159752 | tf_op jit(solution)/shard_map/ppermute | solution.py:345
  8.6 1.6 %collective-permute-start.2 = (bf16[16,1664]{1,0:T(8,128)(2,1)S(1)}, bf16[16,1664]{1,0:T(8,128)(2,1)S(1)}, u32[]{:S(2)}, u32[]{:S(2)}) collective-permute-start(bf16[16,1664]{1,0:T(8,128)(2,1)S(1)} %get-tuple-element.39), channel_id=1, source_target_pairs={{0,4},{2,6},{4,0},{6,2},{8,12},{10,14},{12,8},{14,10},{1,5},{3,7},... | collective-permute-start | bytes 159752 | tf_op jit(solution)/shard_map/ppermute | solution.py:345
  10.2 0.0 collective-permute-done.4.refs_1_
  10.2 0.0 copy-done.6
  10.2 3.2 %collective-permute-start.3 = (bf16[16,1664]{1,0:T(8,128)(2,1)S(1)}, bf16[16,1664]{1,0:T(8,128)(2,1)S(1)}, u32[]{:S(2)}, u32[]{:S(2)}) collective-permute-start(bf16[16,1664]{1,0:T(8,128)(2,1)S(1)} %get-tuple-element.40), channel_id=1, source_target_pairs={{0,6},{2,4},{4,2},{6,0},{8,14},{10,12},{12,10},{14,8},{1,7},{3,5},... | collective-permute-start | bytes 159752 | tf_op jit(solution)/shard_map/ppermute | solution.py:345
  14.1 1.7 %shard_map.92.params_ref = f32[8,48]{1,0:T(8,128)} custom-call(s32[1]{0:T(128)S(6)} %copy.12.index_ref, f32[48,1000]{1,0:T(8,128)} %copy-done.2, f32[2,24]{1,0:T(2,128)} %copy-done.6), custom_call_target="tpu_custom_call" | custom-call | flops 1024 | bytes 1024 | tf_op jit(solution)/shard_map/pallas_call | solution.py:328
  15.8 0.0 copy-done
  15.8 0.7 %copy-done.3 = f32[8,48]{1,0:T(8,128)S(1)} copy-done((f32[8,48]{1,0:T(8,128)S(1)}, f32[8,48]{1,0:T(8,128)}, u32[]{:S(2)}) %copy-start.3) | copy-done | bytes 1560
  16.5 1.5 %shard_map.93.refs_4_ = bf16[128,1536]{1,0:T(8,128)(2,1)S(1)} custom-call(f32[8,48]{1,0:T(8,128)S(1)} %copy-done.3, bf16[256,1536]{1,0:T(8,128)(2,1)S(1)} %bitcast.7, bf16[256,48]{1,0:T(8,128)(2,1)S(1)} %get-tuple-element.33.raw_ref, bf16[256,64]{1,0:T(8,128)(2,1)S(1)} %get-tuple-element.34.maps_ref), custom_call_target="tpu_custom_call" | custom-call | flops 1024 | bytes 1024 | tf_op jit(solution)/shard_map/pallas_call | solution.py:352
  18.0 0.0 collective-permute-done.5.refs_2_
  18.0 1.6 %collective-permute-start = (bf16[128,1536]{1,0:T(8,128)(2,1)S(1)}, bf16[128,1536]{1,0:T(8,128)(2,1)S(1)}, u32[]{:S(2)}, u32[]{:S(2)}) collective-permute-start(bf16[128,1536]{1,0:T(8,128)(2,1)S(1)} %shard_map.93.refs_4_), channel_id=1, source_target_pairs={{0,16},{16,0},{1,17},{17,1},{2,18},{18,2},{3,19},{19,3},{4,20},{20... | collective-permute-start | bytes 1179656 | tf_op jit(solution)/shard_map/ppermute | solution.py:285
  19.5 0.0 collective-permute-done.6.refs_3_
  19.5 0.7 %copy-done.4 = f32[8,48]{1,0:T(8,128)S(1)} copy-done((f32[8,48]{1,0:T(8,128)S(1)}, f32[8,48]{1,0:T(8,128)}, u32[]{:S(2)}) %copy-start.4) | copy-done | bytes 1560
  20.2 2.0 %shard_map.95.refs_4_ = bf16[96,1536]{1,0:T(8,128)(2,1)} custom-call(f32[8,48]{1,0:T(8,128)S(1)} %copy-done.4, bf16[48,1664]{1,0:T(8,128)(2,1)S(1)} %get-tuple-element.41.refs_0_, bf16[48,1664]{1,0:T(8,128)(2,1)S(1)} %collective-permute-done.4.refs_1_, bf16[48,1664]{1,0:T(8,128)(2,1)S(1)} %collective-permute-done.5.refs_2_, ...), custom_call_target="tpu_custom_call" | custom-call | flops 1024 | bytes 1024 | tf_op jit(solution)/shard_map/pallas_call | solution.py:360
  22.2 2.6 %collective-permute-start.8 = (bf16[96,1536]{1,0:T(8,128)(2,1)}, bf16[96,1536]{1,0:T(8,128)(2,1)S(1)}, u32[]{:S(2)}, u32[]{:S(2)}) collective-permute-start(bf16[96,1536]{1,0:T(8,128)(2,1)} %shard_map.95.refs_4_), channel_id=1, source_target_pairs={{0,8},{2,10},{4,12},{6,14},{8,0},{10,2},{12,4},{14,6},{1,9},{3,11}... | collective-permute-start | bytes 884744 | tf_op jit(solution)/shard_map/ppermute | solution.py:285
  24.8 0.0 collective-permute-done.1.refs_1_
  24.8 0.0 collective-permute-done.2.refs_2_
  24.8 0.6 %copy-done.11 = bf16[16,1664]{1,0:T(8,128)(2,1)} copy-done((bf16[16,1664]{1,0:T(8,128)(2,1)}, bf16[16,1664]{1,0:T(8,128)(2,1)S(1)}, u32[]{:S(2)}) %copy-start.11) | copy-done | bytes 53272
  25.4 0.0 collective-permute-done.3.refs_3_
  25.4 0.6 %copy-done.14 = bf16[16,1664]{1,0:T(8,128)(2,1)} copy-done((bf16[16,1664]{1,0:T(8,128)(2,1)}, bf16[16,1664]{1,0:T(8,128)(2,1)S(1)}, u32[]{:S(2)}) %copy-start.14) | copy-done | bytes 53272
  26.0 0.0 copy-done.7
  26.0 0.0 copy-done.5
  26.0 0.8 %copy-done.12 = bf16[16,1664]{1,0:T(8,128)(2,1)S(1)} copy-done((bf16[16,1664]{1,0:T(8,128)(2,1)S(1)}, bf16[16,1664]{1,0:T(8,128)(2,1)}, u32[]{:S(2)}) %copy-start.12) | copy-done | bytes 53272
  26.8 0.8 %copy-done.15 = bf16[16,1664]{1,0:T(8,128)(2,1)S(1)} copy-done((bf16[16,1664]{1,0:T(8,128)(2,1)S(1)}, bf16[16,1664]{1,0:T(8,128)(2,1)}, u32[]{:S(2)}) %copy-start.15) | copy-done | bytes 53272
  27.6 1.6 %shard_map.96 = bf16[32,1536]{1,0:T(8,128)(2,1)} custom-call(f32[8,48]{1,0:T(8,128)S(1)} %copy-done.5, bf16[16,1664]{1,0:T(8,128)(2,1)S(1)} %get-tuple-element.37.refs_0_, bf16[16,1664]{1,0:T(8,128)(2,1)S(1)} %collective-permute-done.1.refs_1_, bf16[16,1664]{1,0:T(8,128)(2,1)S(1)} %copy-done.12, bf16[16,1664]{1,0:T(8,128)(2,1)S(1)} %copy-done.15, ...), custom_call_target="tpu_custom_call" | custom-call | flops 20000000000 | bytes 1024 | tf_op jit(solution)/shard_map/pallas_call | solution.py:360
  29.2 0.6 %copy-done.9 = bf16[16,1664]{1,0:T(8,128)(2,1)} copy-done((bf16[16,1664]{1,0:T(8,128)(2,1)}, bf16[16,1664]{1,0:T(8,128)(2,1)S(1)}, u32[]{:S(2)}) %copy-start.9) | copy-done | bytes 53272
  29.8 0.3 collective-permute-start.7
  30.2 0.0 copy-done.18
  30.2 0.1 broadcast_in_dim.3
  30.3 0.1 reshape_reshape.3.skip_ref
  30.3 0.0 collective-permute-done.s_ref
  30.3 0.0 copy-done.1
  30.4 2.1 %shard_map.94 = (f32[256,1536]{1,0:T(8,128)S(1)}, f32[256,1536]{1,0:T(8,128)S(1)}) custom-call(f32[8,48]{1,0:T(8,128)S(1)} %copy-done.5, bf16[128,1536]{1,0:T(8,128)(2,1)S(1)} %collective-permute-done.s_ref, bf16[256,1536]{1,0:T(8,128)(2,1)S(1)} %bitcast.8, bf16[256,48]{1,0:T(8,128)(2,1)S(1)} %get-tuple-element.33.raw_ref, ...), custom_call_target="tpu_custom_call" | custom-call | flops 1024 | bytes 1024 | tf_op jit(solution)/shard_map/pallas_call | solution.py:369
  32.4 0.0 copy-start.8
  32.4 0.0 copy-start.10
  32.4 0.0 copy-start.13
  32.5 6.0 %collective-permute-done.8.s_ref = bf16[96,1536]{1,0:T(8,128)(2,1)S(1)} collective-permute-done((bf16[96,1536]{1,0:T(8,128)(2,1)}, bf16[96,1536]{1,0:T(8,128)(2,1)S(1)}, u32[]{:S(2)}, u32[]{:S(2)}) %collective-permute-start.8) | collective-permute-done | bytes 294944 | tf_op jit(solution)/shard_map/ppermute | solution.py:285
  38.5 1.6 %shard_map.97 = (bf16[48,1536]{1,0:T(8,128)(2,1)S(1)}, bf16[48,1536]{1,0:T(8,128)(2,1)S(1)}, bf16[48,1536]{1,0:T(8,128)(2,1)S(1)}, bf16[48,1536]{1,0:T(8,128)(2,1)S(1)}) custom-call(f32[8,48]{1,0:T(8,128)S(1)} %copy-done.5, bf16[96,1536]{1,0:T(8,128)(2,1)S(1)} %collective-permute-done.8.s_ref, bf16[48,1664]{1,0:T(8,128)(2,1)S(1)} %get-tuple-element.41.refs_0_, ...), custom_call_target="tpu_custom_call" | custom-call | flops 1024 | bytes 1024 | tf_op jit(solution)/shard_map/pallas_call | solution.py:377
  40.0 0.2 collective-permute-start.12
  40.3 0.4 collective-permute-start.13
  40.7 2.9 %collective-permute-start.14 = (bf16[48,1536]{1,0:T(8,128)(2,1)S(1)}, bf16[48,1536]{1,0:T(8,128)(2,1)S(1)}, u32[]{:S(2)}, u32[]{:S(2)}) collective-permute-start(bf16[48,1536]{1,0:T(8,128)(2,1)S(1)} %get-tuple-element.52), channel_id=1, source_target_pairs={{0,6},{2,4},{4,2},{6,0},{8,14},{10,12},{12,10},{14,8},{1,7},{3,5},... | collective-permute-start | bytes 442376 | tf_op jit(solution)/shard_map/ppermute | solution.py:345
  43.6 0.0 collective-permute-done.7.s_ref
  43.6 0.0 copy-done.13
  43.6 0.0 copy-done.16
  43.6 0.0 copy-start.17
  43.6 1.0 %shard_map.98 = (bf16[16,1536]{1,0:T(8,128)(2,1)S(1)}, bf16[16,1536]{1,0:T(8,128)(2,1)S(1)}, bf16[16,1536]{1,0:T(8,128)(2,1)S(1)}, bf16[16,1536]{1,0:T(8,128)(2,1)S(1)}) custom-call(f32[8,48]{1,0:T(8,128)S(1)} %copy-done.5, bf16[32,1536]{1,0:T(8,128)(2,1)S(1)} %collective-permute-done.7.s_ref, bf16[16,1664]{1,0:T(8,128)(2,1)S(1)} %copy-done.8, ...), custom_call_target="tpu_custom_call" | custom-call | flops 20000000000 | bytes 1024 | tf_op jit(solution)/shard_map/pallas_call | solution.py:377
  44.7 0.2 collective-permute-start.9
  44.9 0.4 collective-permute-start.10
  45.3 2.4 %collective-permute-done.12.refs_1_ = bf16[48,1536]{1,0:T(8,128)(2,1)S(1)} collective-permute-done((bf16[48,1536]{1,0:T(8,128)(2,1)S(1)}, bf16[48,1536]{1,0:T(8,128)(2,1)S(1)}, u32[]{:S(2)}, u32[]{:S(2)}) %collective-permute-start.12) | collective-permute-done | bytes 147488 | tf_op jit(solution)/shard_map/ppermute | solution.py:345
  47.7 0.5 collective-permute-start.11
  48.2 0.0 copy-done.17
  48.3 0.0 collective-permute-done.13.refs_2_
  48.3 1.2 %collective-permute-done.14.refs_3_ = bf16[48,1536]{1,0:T(8,128)(2,1)S(1)} collective-permute-done((bf16[48,1536]{1,0:T(8,128)(2,1)S(1)}, bf16[48,1536]{1,0:T(8,128)(2,1)S(1)}, u32[]{:S(2)}, u32[]{:S(2)}) %collective-permute-start.14) | collective-permute-done | bytes 147488 | tf_op jit(solution)/shard_map/ppermute | solution.py:345
  49.5 1.1 %shard_map.99.refs_4_ = bf16[256,1536]{1,0:T(8,128)(2,1)} custom-call(f32[256,1536]{1,0:T(8,128)S(1)} %get-tuple-element.35.refs_4_.w_ref, f32[256,1536]{1,0:T(8,128)S(1)} %get-tuple-element.36.g_ref, f32[1,1536]{1,0:T(1,128)S(1)} %reshape.23.gain_ref, bf16[48,1536]{1,0:T(8,128)(2,1)S(1)} %get-tuple-element.45.refs_4_.refs_0_, ...), custom_call_target="tpu_custom_call" | custom-call | flops 1024 | bytes 1024 | tf_op jit(solution)/shard_map/pallas_call | solution.py:389
  50.6 0.0 collective-permute-done.9.refs_1_
  50.7 0.0 collective-permute-done.10.refs_2_
  50.7 2.1 %collective-permute-done.11.refs_3_ = bf16[16,1536]{1,0:T(8,128)(2,1)S(1)} collective-permute-done((bf16[16,1536]{1,0:T(8,128)(2,1)S(1)}, bf16[16,1536]{1,0:T(8,128)(2,1)S(1)}, u32[]{:S(2)}, u32[]{:S(2)}) %collective-permute-start.11) | collective-permute-done | bytes 49184 | tf_op jit(solution)/shard_map/ppermute | solution.py:345
  52.7 0.8 %shard_map.100 = bf16[256,1536]{1,0:T(8,128)(2,1)} custom-call(f32[256,1536]{1,0:T(8,128)S(1)} %get-tuple-element.35.refs_4_.w_ref, f32[256,1536]{1,0:T(8,128)S(1)} %get-tuple-element.36.g_ref, f32[1,1536]{1,0:T(1,128)S(1)} %reshape.23.gain_ref, bf16[16,1536]{1,0:T(8,128)(2,1)S(1)} %get-tuple-element.46.refs_0_, ...), custom_call_target="tpu_custom_call", output_to_operand_aliasing={{}: (7, {})} | custom-call | flops 1024 | bytes 1024 | tf_op jit(solution)/shard_map/pallas_call | solution.py:389
  (17 shorter events, 0.0 us)
Async XLA Ops:
  0.0 15.8 %copy-start = (bf16[1,32,8,1536]{3,2,1,0:T(8,128)(2,1)S(1)}, bf16[1,32,8,1536]{3,2,1,0:T(8,128)(2,1)}, u32[]{:S(2)}) copy-start(bf16[1,32,8,1536]{3,2,1,0:T(8,128)(2,1)} %param.9) | copy-start | bytes 2359300
  1.5 0.7 %copy-start.2 = (f32[48,1000]{1,0:T(8,128)}, f32[48,1000]{1,0:T(8,128)S(1)}, u32[]{:S(2)}) copy-start(f32[48,1000]{1,0:T(8,128)S(1)} %get-tuple-element.31.table_ref) | copy-start | bytes 576004
  2.2 8.0 %copy-start.6 = (f32[2,24]{1,0:T(2,128)}, f32[2,24]{1,0:T(2,128)S(1)}, u32[]{:S(2)}) copy-start(f32[2,24]{1,0:T(2,128)S(1)} %get-tuple-element.32.rates_ref) | copy-start | bytes 580
  2.2 23.8 %copy-start.7 = (bf16[16,1664]{1,0:T(8,128)(2,1)}, bf16[16,1664]{1,0:T(8,128)(2,1)S(1)}, u32[]{:S(2)}) copy-start(bf16[16,1664]{1,0:T(8,128)(2,1)S(1)} %get-tuple-element.37.refs_0_) | copy-start | bytes 159748
  2.2 8.0 %collective-permute-start.4 = (bf16[48,1664]{1,0:T(8,128)(2,1)S(1)}, bf16[48,1664]{1,0:T(8,128)(2,1)S(1)}, u32[]{:S(2)}, u32[]{:S(2)}) collective-permute-start(bf16[48,1664]{1,0:T(8,128)(2,1)S(1)} %get-tuple-element.42), channel_id=1, source_target_pairs={{0,2},{2,0},{4,6},{6,4},{8,10},{10,8},{12,14},{14,12},{1,3},{3,1},... | collective-permute-start | bytes 479240 | tf_op jit(solution)/shard_map/ppermute | solution.py:345
  5.1 12.8 %collective-permute-start.5 = (bf16[48,1664]{1,0:T(8,128)(2,1)S(1)}, bf16[48,1664]{1,0:T(8,128)(2,1)S(1)}, u32[]{:S(2)}, u32[]{:S(2)}) collective-permute-start(bf16[48,1664]{1,0:T(8,128)(2,1)S(1)} %get-tuple-element.43), channel_id=1, source_target_pairs={{0,4},{2,6},{4,0},{6,2},{8,12},{10,14},{12,8},{14,10},{1,5},{3,7},... | collective-permute-start | bytes 479240 | tf_op jit(solution)/shard_map/ppermute | solution.py:345
  6.7 12.8 %collective-permute-start.6 = (bf16[48,1664]{1,0:T(8,128)(2,1)S(1)}, bf16[48,1664]{1,0:T(8,128)(2,1)S(1)}, u32[]{:S(2)}, u32[]{:S(2)}) collective-permute-start(bf16[48,1664]{1,0:T(8,128)(2,1)S(1)} %get-tuple-element.44), channel_id=1, source_target_pairs={{0,6},{2,4},{4,2},{6,0},{8,14},{10,12},{12,10},{14,8},{1,7},{3,5},... | collective-permute-start | bytes 479240 | tf_op jit(solution)/shard_map/ppermute | solution.py:345
  6.7 18.0 %collective-permute-start.1 = (bf16[16,1664]{1,0:T(8,128)(2,1)S(1)}, bf16[16,1664]{1,0:T(8,128)(2,1)S(1)}, u32[]{:S(2)}, u32[]{:S(2)}) collective-permute-start(bf16[16,1664]{1,0:T(8,128)(2,1)S(1)} %get-tuple-element.38), channel_id=1, source_target_pairs={{0,2},{2,0},{4,6},{6,4},{8,10},{10,8},{12,14},{14,12},{1,3},{3,1},... | collective-permute-start | bytes 159752 | tf_op jit(solution)/shard_map/ppermute | solution.py:345
  8.6 16.1 %collective-permute-start.2 = (bf16[16,1664]{1,0:T(8,128)(2,1)S(1)}, bf16[16,1664]{1,0:T(8,128)(2,1)S(1)}, u32[]{:S(2)}, u32[]{:S(2)}) collective-permute-start(bf16[16,1664]{1,0:T(8,128)(2,1)S(1)} %get-tuple-element.39), channel_id=1, source_target_pairs={{0,4},{2,6},{4,0},{6,2},{8,12},{10,14},{12,8},{14,10},{1,5},{3,7},... | collective-permute-start | bytes 159752 | tf_op jit(solution)/shard_map/ppermute | solution.py:345
  10.2 15.2 %collective-permute-start.3 = (bf16[16,1664]{1,0:T(8,128)(2,1)S(1)}, bf16[16,1664]{1,0:T(8,128)(2,1)S(1)}, u32[]{:S(2)}, u32[]{:S(2)}) collective-permute-start(bf16[16,1664]{1,0:T(8,128)(2,1)S(1)} %get-tuple-element.40), channel_id=1, source_target_pairs={{0,6},{2,4},{4,2},{6,0},{8,14},{10,12},{12,10},{14,8},{1,7},{3,5},... | collective-permute-start | bytes 159752 | tf_op jit(solution)/shard_map/ppermute | solution.py:345
  15.8 0.7 %copy-start.3 = (f32[8,48]{1,0:T(8,128)S(1)}, f32[8,48]{1,0:T(8,128)}, u32[]{:S(2)}) copy-start(f32[8,48]{1,0:T(8,128)} %shard_map.92.params_ref) | copy-start | bytes 4612
  16.5 9.5 %copy-start.5 = (f32[8,48]{1,0:T(8,128)S(1)}, f32[8,48]{1,0:T(8,128)}, u32[]{:S(2)}) copy-start(f32[8,48]{1,0:T(8,128)} %shard_map.92.params_ref) | copy-start | bytes 4612
  18.0 12.4 %collective-permute-start = (bf16[128,1536]{1,0:T(8,128)(2,1)S(1)}, bf16[128,1536]{1,0:T(8,128)(2,1)S(1)}, u32[]{:S(2)}, u32[]{:S(2)}) collective-permute-start(bf16[128,1536]{1,0:T(8,128)(2,1)S(1)} %shard_map.93.refs_4_), channel_id=1, source_target_pairs={{0,16},{16,0},{1,17},{17,1},{2,18},{18,2},{3,19},{19,3},{4,20},{20... | collective-permute-start | bytes 1179656 | tf_op jit(solution)/shard_map/ppermute | solution.py:285
  19.5 0.7 %copy-start.4 = (f32[8,48]{1,0:T(8,128)S(1)}, f32[8,48]{1,0:T(8,128)}, u32[]{:S(2)}) copy-start(f32[8,48]{1,0:T(8,128)} %shard_map.92.params_ref) | copy-start | bytes 4612
  22.2 16.3 %collective-permute-start.8 = (bf16[96,1536]{1,0:T(8,128)(2,1)}, bf16[96,1536]{1,0:T(8,128)(2,1)S(1)}, u32[]{:S(2)}, u32[]{:S(2)}) collective-permute-start(bf16[96,1536]{1,0:T(8,128)(2,1)} %shard_map.95.refs_4_), channel_id=1, source_target_pairs={{0,8},{2,10},{4,12},{6,14},{8,0},{10,2},{12,4},{14,6},{1,9},{3,11}... | collective-permute-start | bytes 884744 | tf_op jit(solution)/shard_map/ppermute | solution.py:285
  24.8 0.6 %copy-start.11 = (bf16[16,1664]{1,0:T(8,128)(2,1)}, bf16[16,1664]{1,0:T(8,128)(2,1)S(1)}, u32[]{:S(2)}) copy-start(bf16[16,1664]{1,0:T(8,128)(2,1)S(1)} %collective-permute-done.2.refs_2_) | copy-start | bytes 159748
  25.4 0.6 %copy-start.14 = (bf16[16,1664]{1,0:T(8,128)(2,1)}, bf16[16,1664]{1,0:T(8,128)(2,1)S(1)}, u32[]{:S(2)}) copy-start(bf16[16,1664]{1,0:T(8,128)(2,1)S(1)} %collective-permute-done.3.refs_3_) | copy-start | bytes 159748
  26.0 0.8 %copy-start.12 = (bf16[16,1664]{1,0:T(8,128)(2,1)S(1)}, bf16[16,1664]{1,0:T(8,128)(2,1)}, u32[]{:S(2)}) copy-start(bf16[16,1664]{1,0:T(8,128)(2,1)} %copy-done.11) | copy-start | bytes 159748
  26.8 0.8 %copy-start.15 = (bf16[16,1664]{1,0:T(8,128)(2,1)S(1)}, bf16[16,1664]{1,0:T(8,128)(2,1)}, u32[]{:S(2)}) copy-start(bf16[16,1664]{1,0:T(8,128)(2,1)} %copy-done.14) | copy-start | bytes 159748
  27.6 2.6 %copy-start.18 = (f32[24]{0:T(128)S(1)}, f32[24]{0:T(128)}, u32[]{:S(2)}) copy-start(f32[24]{0:T(128)} %param.16) | copy-start | bytes 292
  27.6 2.7 %copy-start.1 = (bf16[1,32,8,1536]{3,2,1,0:T(8,128)(2,1)S(1)}, bf16[1,32,8,1536]{3,2,1,0:T(8,128)(2,1)}, u32[]{:S(2)}) copy-start(bf16[1,32,8,1536]{3,2,1,0:T(8,128)(2,1)} %param.10) | copy-start | bytes 2359300
  29.2 0.6 %copy-start.9 = (bf16[16,1664]{1,0:T(8,128)(2,1)}, bf16[16,1664]{1,0:T(8,128)(2,1)S(1)}, u32[]{:S(2)}) copy-start(bf16[16,1664]{1,0:T(8,128)(2,1)S(1)} %collective-permute-done.1.refs_1_) | copy-start | bytes 159748
  29.8 13.8 %collective-permute-start.7 = (bf16[32,1536]{1,0:T(8,128)(2,1)}, bf16[32,1536]{1,0:T(8,128)(2,1)S(1)}, u32[]{:S(2)}, u32[]{:S(2)}) collective-permute-start(bf16[32,1536]{1,0:T(8,128)(2,1)} %shard_map.96), channel_id=1, source_target_pairs={{0,8},{2,10},{4,12},{6,14},{8,0},{10,2},{12,4},{14,6},{1,9},{3,11}... | collective-permute-start | bytes 294920 | tf_op jit(solution)/shard_map/ppermute | solution.py:285
  32.4 11.2 %copy-start.8 = (bf16[16,1664]{1,0:T(8,128)(2,1)S(1)}, bf16[16,1664]{1,0:T(8,128)(2,1)}, u32[]{:S(2)}) copy-start(bf16[16,1664]{1,0:T(8,128)(2,1)} %copy-done.7) | copy-start | bytes 159748
  32.4 11.2 %copy-start.10 = (bf16[16,1664]{1,0:T(8,128)(2,1)S(1)}, bf16[16,1664]{1,0:T(8,128)(2,1)}, u32[]{:S(2)}) copy-start(bf16[16,1664]{1,0:T(8,128)(2,1)} %copy-done.9) | copy-start | bytes 159748
  32.4 11.2 %copy-start.13 = (bf16[16,1664]{1,0:T(8,128)(2,1)S(1)}, bf16[16,1664]{1,0:T(8,128)(2,1)}, u32[]{:S(2)}) copy-start(bf16[16,1664]{1,0:T(8,128)(2,1)} %copy-done.11) | copy-start | bytes 159748
  32.4 11.2 %copy-start.16 = (bf16[16,1664]{1,0:T(8,128)(2,1)S(1)}, bf16[16,1664]{1,0:T(8,128)(2,1)}, u32[]{:S(2)}) copy-start(bf16[16,1664]{1,0:T(8,128)(2,1)} %copy-done.14) | copy-start | bytes 159748
  40.0 7.7 %collective-permute-start.12 = (bf16[48,1536]{1,0:T(8,128)(2,1)S(1)}, bf16[48,1536]{1,0:T(8,128)(2,1)S(1)}, u32[]{:S(2)}, u32[]{:S(2)}) collective-permute-start(bf16[48,1536]{1,0:T(8,128)(2,1)S(1)} %get-tuple-element.50), channel_id=1, source_target_pairs={{0,2},{2,0},{4,6},{6,4},{8,10},{10,8},{12,14},{14,12},{1,3},{3,1},... | collective-permute-start | bytes 442376 | tf_op jit(solution)/shard_map/ppermute | solution.py:345
  40.3 8.0 %collective-permute-start.13 = (bf16[48,1536]{1,0:T(8,128)(2,1)S(1)}, bf16[48,1536]{1,0:T(8,128)(2,1)S(1)}, u32[]{:S(2)}, u32[]{:S(2)}) collective-permute-start(bf16[48,1536]{1,0:T(8,128)(2,1)S(1)} %get-tuple-element.51), channel_id=1, source_target_pairs={{0,4},{2,6},{4,0},{6,2},{8,12},{10,14},{12,8},{14,10},{1,5},{3,7},... | collective-permute-start | bytes 442376 | tf_op jit(solution)/shard_map/ppermute | solution.py:345
  40.7 8.8 %collective-permute-start.14 = (bf16[48,1536]{1,0:T(8,128)(2,1)S(1)}, bf16[48,1536]{1,0:T(8,128)(2,1)S(1)}, u32[]{:S(2)}, u32[]{:S(2)}) collective-permute-start(bf16[48,1536]{1,0:T(8,128)(2,1)S(1)} %get-tuple-element.52), channel_id=1, source_target_pairs={{0,6},{2,4},{4,2},{6,0},{8,14},{10,12},{12,10},{14,8},{1,7},{3,5},... | collective-permute-start | bytes 442376 | tf_op jit(solution)/shard_map/ppermute | solution.py:345
  43.6 4.6 %copy-start.17 = (f32[1536]{0:T(1024)S(1)}, f32[1536]{0:T(1024)}, u32[]{:S(2)}) copy-start(f32[1536]{0:T(1024)} %param.17) | copy-start | bytes 18436
  44.7 6.0 %collective-permute-start.9 = (bf16[16,1536]{1,0:T(8,128)(2,1)S(1)}, bf16[16,1536]{1,0:T(8,128)(2,1)S(1)}, u32[]{:S(2)}, u32[]{:S(2)}) collective-permute-start(bf16[16,1536]{1,0:T(8,128)(2,1)S(1)} %get-tuple-element.47), channel_id=1, source_target_pairs={{0,2},{2,0},{4,6},{6,4},{8,10},{10,8},{12,14},{14,12},{1,3},{3,1},... | collective-permute-start | bytes 147464 | tf_op jit(solution)/shard_map/ppermute | solution.py:345
  44.9 5.8 %collective-permute-start.10 = (bf16[16,1536]{1,0:T(8,128)(2,1)S(1)}, bf16[16,1536]{1,0:T(8,128)(2,1)S(1)}, u32[]{:S(2)}, u32[]{:S(2)}) collective-permute-start(bf16[16,1536]{1,0:T(8,128)(2,1)S(1)} %get-tuple-element.48), channel_id=1, source_target_pairs={{0,4},{2,6},{4,0},{6,2},{8,12},{10,14},{12,8},{14,10},{1,5},{3,7},... | collective-permute-start | bytes 147464 | tf_op jit(solution)/shard_map/ppermute | solution.py:345
  47.7 5.0 %collective-permute-start.11 = (bf16[16,1536]{1,0:T(8,128)(2,1)S(1)}, bf16[16,1536]{1,0:T(8,128)(2,1)S(1)}, u32[]{:S(2)}, u32[]{:S(2)}) collective-permute-start(bf16[16,1536]{1,0:T(8,128)(2,1)S(1)} %get-tuple-element.49), channel_id=1, source_target_pairs={{0,6},{2,4},{4,2},{6,0},{8,14},{10,12},{12,10},{14,8},{1,7},{3,5},... | collective-permute-start | bytes 147464 | tf_op jit(solution)/shard_map/ppermute | solution.py:345

commit v8 on v7

--- a/solution.py
+++ b/solution.py
@@ -11,6 +11,7 @@
 GROUP = 4
 LATER = 4
 STRIP = 512
+VMEM_LIMIT = 24 * 1024 * 1024
 F32 = jnp.float32
 BF16 = jnp.bfloat16
 
@@ -271,7 +272,7 @@
     return pl.pallas_call(
         kernel,
         out_shape=out_shape,
-        compiler_params=pltpu.CompilerParams(vmem_limit_bytes=32 * 1024 * 1024),
+        compiler_params=pltpu.CompilerParams(vmem_limit_bytes=VMEM_LIMIT),
         cost_estimate=cost,
         **more,
     )
@@ -321,7 +322,7 @@
         out_shape=[pltpu.VMEM(a.shape, a.dtype) for a in given[1:]]
         + [pltpu.VMEM((rows, channels + LANES), BF16) for rows in pieces for _ in range(group)],
         scratch_shapes=[pltpu.SemaphoreType.DMA((len(given) - 1 + group * len(pieces),))],
-        compiler_params=pltpu.CompilerParams(vmem_limit_bytes=32 * 1024 * 1024),
+        compiler_params=pltpu.CompilerParams(vmem_limit_bytes=VMEM_LIMIT),
         cost_estimate=SMALL,
     )(*[pltpu.with_memory_space_constraint(a, pltpu.HBM) for a in given])
     index, rates = lax.optimization_barrier((step_index, rates))
@@ -337,6 +338,7 @@
             out_specs=pl.BlockSpec((8, 2 * heads), lambda i, index: (0, 0)),
         ),
         out_shape=shape((8, 2 * heads), F32),
+        compiler_params=pltpu.CompilerParams(vmem_limit_bytes=VMEM_LIMIT),
         cost_estimate=SMALL,
     )(index, table, rates)
 

time: 53.9 us -> 50.2 us (0.931)
  local copies, waits for them, and re-layouts: 5.68 us -> 0.21 us
  waiting for transfers between devices: 11.7 us -> 14.9 us
  Pallas kernels: 14.9 us -> 13.4 us
    unnamed x38 -> x24, local copies, waits for them, and re-layouts: 5.52 us -> 0.06 us
    ppermute x3, waiting for transfers between devices: 6.02 us -> 9.35 us  [entering_states(): entering = lax.ppermute(ends, axis, onward)]
    pallas_call x1, Pallas kernels: 1.71 us -> 0.18 us  [body(): pl.pallas_call(params_kernel, grid_spec=pltpu.PrefetchScalarGridSpec(num_...]
  transfers between devices with their start and end apart: 15 -> 15, of which waited for: 4 -> 4; matrix products, arithmetic and copies ran while one was open for 0% -> 0% of each run, Pallas kernels for 23% -> 22%
where the time goes in v8:
time: 50.2 us; the launch traced here: 50.1 us
  starting transfers between devices  20.6 us (41%)
  waiting for transfers between devices  14.9 us (30%)
  Pallas kernels  13.4 us (27%)
  between operations  0.88 us (2%)
    ppermute x12, starting transfers between devices, exchange(): lax.ppermute(blocks[s], 'col', [(i, i ^ s) for i in range(col_count)])  16.1 us
    ppermute x3, waiting for transfers between devices, entering_states(): entering = lax.ppermute(ends, axis, onward)  9.35 us
    ppermute x12, waiting for transfers between devices, exchange(): lax.ppermute(blocks[s], 'col', [(i, i ^ s) for i in range(col_count)])  5.59 us
    ppermute x3, starting transfers between devices, entering_states(): entering = lax.ppermute(ends, axis, onward)  4.56 us
    pallas_call x2, Pallas kernels, body(): call(functools.partial(row_state_kernel, **sizes, **shared), state_shapes...  3.59 us
    pallas_call x2, Pallas kernels, body(): call(functools.partial(row_out_kernel, **sizes, **shared), [shape((rows,...  2.62 us
    pallas_call x1, Pallas kernels, body(): call(functools.partial(col_out_kernel, **sizes), [shape((tokens, channels...  2.06 us
    pallas_call x2, Pallas kernels, body(): call(functools.partial(final_kernel, offset=sum(pieces[:i]), share=share,...  1.98 us
  transfers between devices with their start and end apart: 15, of which 4 were waited for; matrix products, arithmetic and copies ran while one was open for 0% of the time, Pallas kernels for 22%

profile of v8, /device:TPU:0, one launch (start us, length us, event | category | flops | bytes accessed | tf_op | source)
XLA Modules:
  0.0 50.1 jit_solution(1421916733401336954)
XLA Ops:
  0.0 1.5 %shard_map.91 = (bf16[256,48]{1,0:T(8,128)(2,1)S(1)}, bf16[256,64]{1,0:T(8,128)(2,1)S(1)}, f32[48,1000]{1,0:T(8,128)S(1)}, f32[2,24]{1,0:T(2,128)S(1)}, bf16[48,...) custom-call(bf16[256,1536]{1,0:T(8,128)(2,1)} %bitcast.6, ...), custom_call_target="tpu_custom_call" | custom-call | flops 1024 | bytes 1024 | tf_op jit(solution)/shard_map/pallas_call | solution.py:319
  1.5 0.0 copy-start.2
  1.5 3.0 %collective-permute-start.4 = (bf16[48,1664]{1,0:T(8,128)(2,1)S(1)}, bf16[48,1664]{1,0:T(8,128)(2,1)S(1)}, u32[]{:S(2)}, u32[]{:S(2)}) collective-permute-start(bf16[48,1664]{1,0:T(8,128)(2,1)S(1)} %get-tuple-element.42), channel_id=1, source_target_pairs={{0,2},{2,0},{4,6},{6,4},{8,10},{10,8},{12,14},{14,12},{1,3},{3,1},... | collective-permute-start | bytes 479240 | tf_op jit(solution)/shard_map/ppermute | solution.py:347
  4.5 1.6 %collective-permute-start.5 = (bf16[48,1664]{1,0:T(8,128)(2,1)S(1)}, bf16[48,1664]{1,0:T(8,128)(2,1)S(1)}, u32[]{:S(2)}, u32[]{:S(2)}) collective-permute-start(bf16[48,1664]{1,0:T(8,128)(2,1)S(1)} %get-tuple-element.43), channel_id=1, source_target_pairs={{0,4},{2,6},{4,0},{6,2},{8,12},{10,14},{12,8},{14,10},{1,5},{3,7},... | collective-permute-start | bytes 479240 | tf_op jit(solution)/shard_map/ppermute | solution.py:347
  6.1 0.0 collective-permute-start.6
  6.1 1.9 %collective-permute-start.1 = (bf16[16,1664]{1,0:T(8,128)(2,1)S(1)}, bf16[16,1664]{1,0:T(8,128)(2,1)S(1)}, u32[]{:S(2)}, u32[]{:S(2)}) collective-permute-start(bf16[16,1664]{1,0:T(8,128)(2,1)S(1)} %get-tuple-element.38), channel_id=1, source_target_pairs={{0,2},{2,0},{4,6},{6,4},{8,10},{10,8},{12,14},{14,12},{1,3},{3,1},... | collective-permute-start | bytes 159752 | tf_op jit(solution)/shard_map/ppermute | solution.py:347
  8.0 1.6 %collective-permute-start.2 = (bf16[16,1664]{1,0:T(8,128)(2,1)S(1)}, bf16[16,1664]{1,0:T(8,128)(2,1)S(1)}, u32[]{:S(2)}, u32[]{:S(2)}) collective-permute-start(bf16[16,1664]{1,0:T(8,128)(2,1)S(1)} %get-tuple-element.39), channel_id=1, source_target_pairs={{0,4},{2,6},{4,0},{6,2},{8,12},{10,14},{12,8},{14,10},{1,5},{3,7},... | collective-permute-start | bytes 159752 | tf_op jit(solution)/shard_map/ppermute | solution.py:347
  9.6 0.0 collective-permute-done.4.refs_1_
  9.6 3.2 %collective-permute-start.3 = (bf16[16,1664]{1,0:T(8,128)(2,1)S(1)}, bf16[16,1664]{1,0:T(8,128)(2,1)S(1)}, u32[]{:S(2)}, u32[]{:S(2)}) collective-permute-start(bf16[16,1664]{1,0:T(8,128)(2,1)S(1)} %get-tuple-element.40), channel_id=1, source_target_pairs={{0,6},{2,4},{4,2},{6,0},{8,14},{10,12},{12,10},{14,8},{1,7},{3,5},... | collective-permute-start | bytes 159752 | tf_op jit(solution)/shard_map/ppermute | solution.py:347
  13.5 0.2 shard_map.92.params_ref
  13.7 0.0 copy-done
  13.7 1.5 %shard_map.93.refs_4_ = bf16[128,1536]{1,0:T(8,128)(2,1)S(1)} custom-call(f32[8,48]{1,0:T(8,128)S(1)} %shard_map.92.params_ref, bf16[256,1536]{1,0:T(8,128)(2,1)S(1)} %bitcast.7, bf16[256,48]{1,0:T(8,128)(2,1)S(1)} %get-tuple-element.33.raw_ref, bf16[256,64]{1,0:T(8,128)(2,1)S(1)} %get-tuple-element.34.maps_ref), custom_call_target="tpu_custom_call" | custom-call | flops 1024 | bytes 1024 | tf_op jit(solution)/shard_map/pallas_call | solution.py:354
  15.2 0.0 collective-permute-done.5.refs_2_
  15.2 1.6 %collective-permute-start = (bf16[128,1536]{1,0:T(8,128)(2,1)S(1)}, bf16[128,1536]{1,0:T(8,128)(2,1)S(1)}, u32[]{:S(2)}, u32[]{:S(2)}) collective-permute-start(bf16[128,1536]{1,0:T(8,128)(2,1)S(1)} %shard_map.93.refs_4_), channel_id=1, source_target_pairs={{0,16},{16,0},{1,17},{17,1},{2,18},{18,2},{3,19},{19,3},{4,20},{20... | collective-permute-start | bytes 1179656 | tf_op jit(solution)/shard_map/ppermute | solution.py:286
  16.7 0.0 collective-permute-done.6.refs_3_
  16.7 2.0 %shard_map.95.refs_4_ = bf16[96,1536]{1,0:T(8,128)(2,1)} custom-call(f32[8,48]{1,0:T(8,128)S(1)} %shard_map.92.params_ref, bf16[48,1664]{1,0:T(8,128)(2,1)S(1)} %get-tuple-element.41.refs_0_, bf16[48,1664]{1,0:T(8,128)(2,1)S(1)} %collective-permute-done.4.refs_1_, bf16[48,1664]{1,0:T(8,128)(2,1)S(1)} %collective-permute-done.5.refs_2_, ...), custom_call_target="tpu_custom_call" | custom-call | flops 1024 | bytes 1024 | tf_op jit(solution)/shard_map/pallas_call | solution.py:362
  18.7 2.6 %collective-permute-start.8 = (bf16[96,1536]{1,0:T(8,128)(2,1)}, bf16[96,1536]{1,0:T(8,128)(2,1)S(1)}, u32[]{:S(2)}, u32[]{:S(2)}) collective-permute-start(bf16[96,1536]{1,0:T(8,128)(2,1)} %shard_map.95.refs_4_), channel_id=1, source_target_pairs={{0,8},{2,10},{4,12},{6,14},{8,0},{10,2},{12,4},{14,6},{1,9},{3,11}... | collective-permute-start | bytes 884744 | tf_op jit(solution)/shard_map/ppermute | solution.py:286
  21.3 0.0 collective-permute-done.1.refs_1_
  21.3 0.0 collective-permute-done.2.refs_2_
  21.3 0.0 copy-start.6
  21.3 0.0 collective-permute-done.3.refs_3_
  21.3 0.0 copy-start.8
  21.3 0.0 copy-start.11
  21.3 0.0 copy-start.1
  21.4 1.6 %shard_map.96 = bf16[32,1536]{1,0:T(8,128)(2,1)} custom-call(f32[8,48]{1,0:T(8,128)S(1)} %shard_map.92.params_ref, bf16[16,1664]{1,0:T(8,128)(2,1)S(1)} %get-tuple-element.37.refs_0_, bf16[16,1664]{1,0:T(8,128)(2,1)S(1)} %collective-permute-done.1.refs_1_, bf16[16,1664]{1,0:T(8,128)(2,1)S(1)} %collective-permute-done.2.refs_2_, ...), custom_call_target="tpu_custom_call" | custom-call | flops 20000000000 | bytes 1024 | tf_op jit(solution)/shard_map/pallas_call | solution.py:362
  23.0 0.0 copy-done.2
  23.0 0.0 copy-done.4
  23.0 0.0 copy-done.6
  23.0 0.0 copy-done.8
  23.0 0.4 collective-permute-start.7
  23.4 0.0 copy-done.11
  23.4 0.1 broadcast_in_dim.3
  23.5 0.1 reshape_reshape.3.skip_ref
  23.6 0.0 collective-permute-done.s_ref
  23.6 0.0 copy-done.1
  23.6 2.1 %shard_map.94 = (f32[256,1536]{1,0:T(8,128)S(1)}, f32[256,1536]{1,0:T(8,128)S(1)}) custom-call(f32[8,48]{1,0:T(8,128)S(1)} %shard_map.92.params_ref, bf16[128,1536]{1,0:T(8,128)(2,1)S(1)} %collective-permute-done.s_ref, bf16[256,1536]{1,0:T(8,128)(2,1)S(1)} %bitcast.8, bf16[256,48]{1,0:T(8,128)(2,1)S(1)} %get-tuple-element.33.raw_ref, ...), custom_call_target="tpu_custom_call" | custom-call | flops 1024 | bytes 1024 | tf_op jit(solution)/shard_map/pallas_call | solution.py:371
  25.6 0.0 copy-start.3
  25.7 0.0 copy-start.5
  25.7 0.0 copy-start.7
  25.7 0.0 copy-start.9
  25.7 9.3 %collective-permute-done.8.s_ref = bf16[96,1536]{1,0:T(8,128)(2,1)S(1)} collective-permute-done((bf16[96,1536]{1,0:T(8,128)(2,1)}, bf16[96,1536]{1,0:T(8,128)(2,1)S(1)}, u32[]{:S(2)}, u32[]{:S(2)}) %collective-permute-start.8) | collective-permute-done | bytes 294944 | tf_op jit(solution)/shard_map/ppermute | solution.py:286
  35.0 1.6 %shard_map.97 = (bf16[48,1536]{1,0:T(8,128)(2,1)S(1)}, bf16[48,1536]{1,0:T(8,128)(2,1)S(1)}, bf16[48,1536]{1,0:T(8,128)(2,1)S(1)}, bf16[48,1536]{1,0:T(8,128)(2,1)S(1)}) custom-call(f32[8,48]{1,0:T(8,128)S(1)} %shard_map.92.params_ref, bf16[96,1536]{1,0:T(8,128)(2,1)S(1)} %collective-permute-done.8.s_ref, bf16[48,1664]{1,0:T(8,128)(2,1)S(1)} %get-tuple-element.41.refs_0_, ...), custom_call_target="tpu_custom_call" | custom-call | flops 1024 | bytes 1024 | tf_op jit(solution)/shard_map/pallas_call | solution.py:379
  36.6 0.5 collective-permute-start.12
  37.1 0.1 collective-permute-start.13
  37.2 2.9 %collective-permute-start.14 = (bf16[48,1536]{1,0:T(8,128)(2,1)S(1)}, bf16[48,1536]{1,0:T(8,128)(2,1)S(1)}, u32[]{:S(2)}, u32[]{:S(2)}) collective-permute-start(bf16[48,1536]{1,0:T(8,128)(2,1)S(1)} %get-tuple-element.52), channel_id=1, source_target_pairs={{0,6},{2,4},{4,2},{6,0},{8,14},{10,12},{12,10},{14,8},{1,7},{3,5},... | collective-permute-start | bytes 442376 | tf_op jit(solution)/shard_map/ppermute | solution.py:347
  40.2 0.0 collective-permute-done.7.s_ref
  40.2 0.0 copy-done.3
  40.2 0.0 copy-done.5
  40.2 0.0 copy-done.7
  40.2 0.0 copy-done.9
  40.2 0.0 copy-start.10
  40.2 1.0 %shard_map.98 = (bf16[16,1536]{1,0:T(8,128)(2,1)S(1)}, bf16[16,1536]{1,0:T(8,128)(2,1)S(1)}, bf16[16,1536]{1,0:T(8,128)(2,1)S(1)}, bf16[16,1536]{1,0:T(8,128)(2,1)S(1)}) custom-call(f32[8,48]{1,0:T(8,128)S(1)} %shard_map.92.params_ref, bf16[32,1536]{1,0:T(8,128)(2,1)S(1)} %collective-permute-done.7.s_ref, bf16[16,1664]{1,0:T(8,128)(2,1)S(1)} %copy-done.3, ...), custom_call_target="tpu_custom_call" | custom-call | flops 20000000000 | bytes 1024 | tf_op jit(solution)/shard_map/pallas_call | solution.py:379
  41.3 0.5 collective-permute-start.9
  41.7 0.2 collective-permute-start.10
  41.9 2.3 %collective-permute-done.12.refs_1_ = bf16[48,1536]{1,0:T(8,128)(2,1)S(1)} collective-permute-done((bf16[48,1536]{1,0:T(8,128)(2,1)S(1)}, bf16[48,1536]{1,0:T(8,128)(2,1)S(1)}, u32[]{:S(2)}, u32[]{:S(2)}) %collective-permute-start.12) | collective-permute-done | bytes 147488 | tf_op jit(solution)/shard_map/ppermute | solution.py:347
  44.2 0.6 %collective-permute-start.11 = (bf16[16,1536]{1,0:T(8,128)(2,1)S(1)}, bf16[16,1536]{1,0:T(8,128)(2,1)S(1)}, u32[]{:S(2)}, u32[]{:S(2)}) collective-permute-start(bf16[16,1536]{1,0:T(8,128)(2,1)S(1)} %get-tuple-element.49), channel_id=1, source_target_pairs={{0,6},{2,4},{4,2},{6,0},{8,14},{10,12},{12,10},{14,8},{1,7},{3,5},... | collective-permute-start | bytes 147464 | tf_op jit(solution)/shard_map/ppermute | solution.py:347
  44.8 0.0 copy-done.10
  44.8 0.0 collective-permute-done.13.refs_2_
  44.8 1.2 %collective-permute-done.14.refs_3_ = bf16[48,1536]{1,0:T(8,128)(2,1)S(1)} collective-permute-done((bf16[48,1536]{1,0:T(8,128)(2,1)S(1)}, bf16[48,1536]{1,0:T(8,128)(2,1)S(1)}, u32[]{:S(2)}, u32[]{:S(2)}) %collective-permute-start.14) | collective-permute-done | bytes 147488 | tf_op jit(solution)/shard_map/ppermute | solution.py:347
  46.0 1.1 %shard_map.99.refs_4_ = bf16[256,1536]{1,0:T(8,128)(2,1)} custom-call(f32[256,1536]{1,0:T(8,128)S(1)} %get-tuple-element.35.refs_4_.w_ref, f32[256,1536]{1,0:T(8,128)S(1)} %get-tuple-element.36.g_ref, f32[1,1536]{1,0:T(1,128)S(1)} %reshape.23.gain_ref, bf16[48,1536]{1,0:T(8,128)(2,1)S(1)} %get-tuple-element.45.refs_4_.refs_0_, ...), custom_call_target="tpu_custom_call" | custom-call | flops 1024 | bytes 1024 | tf_op jit(solution)/shard_map/pallas_call | solution.py:391
  47.2 0.0 collective-permute-done.9.refs_1_
  47.2 0.0 collective-permute-done.10.refs_2_
  47.2 2.0 %collective-permute-done.11.refs_3_ = bf16[16,1536]{1,0:T(8,128)(2,1)S(1)} collective-permute-done((bf16[16,1536]{1,0:T(8,128)(2,1)S(1)}, bf16[16,1536]{1,0:T(8,128)(2,1)S(1)}, u32[]{:S(2)}, u32[]{:S(2)}) %collective-permute-start.11) | collective-permute-done | bytes 49184 | tf_op jit(solution)/shard_map/ppermute | solution.py:347
  49.2 0.8 %shard_map.100 = bf16[256,1536]{1,0:T(8,128)(2,1)} custom-call(f32[256,1536]{1,0:T(8,128)S(1)} %get-tuple-element.35.refs_4_.w_ref, f32[256,1536]{1,0:T(8,128)S(1)} %get-tuple-element.36.g_ref, f32[1,1536]{1,0:T(1,128)S(1)} %reshape.23.gain_ref, bf16[16,1536]{1,0:T(8,128)(2,1)S(1)} %get-tuple-element.46.refs_0_, ...), custom_call_target="tpu_custom_call", output_to_operand_aliasing={{}: (7, {})} | custom-call | flops 1024 | bytes 1024 | tf_op jit(solution)/shard_map/pallas_call | solution.py:391
  (3 shorter events, 0.0 us)
Async XLA Ops:
  0.0 13.7 %copy-start = (bf16[1,32,8,1536]{3,2,1,0:T(8,128)(2,1)S(1)}, bf16[1,32,8,1536]{3,2,1,0:T(8,128)(2,1)}, u32[]{:S(2)}) copy-start(bf16[1,32,8,1536]{3,2,1,0:T(8,128)(2,1)} %param.9) | copy-start | bytes 2359300
  1.5 21.5 %copy-start.2 = (bf16[16,1664]{1,0:T(8,128)(2,1)}, bf16[16,1664]{1,0:T(8,128)(2,1)S(1)}, u32[]{:S(2)}) copy-start(bf16[16,1664]{1,0:T(8,128)(2,1)S(1)} %get-tuple-element.37.refs_0_) | copy-start | bytes 159748
  1.5 8.1 %collective-permute-start.4 = (bf16[48,1664]{1,0:T(8,128)(2,1)S(1)}, bf16[48,1664]{1,0:T(8,128)(2,1)S(1)}, u32[]{:S(2)}, u32[]{:S(2)}) collective-permute-start(bf16[48,1664]{1,0:T(8,128)(2,1)S(1)} %get-tuple-element.42), channel_id=1, source_target_pairs={{0,2},{2,0},{4,6},{6,4},{8,10},{10,8},{12,14},{14,12},{1,3},{3,1},... | collective-permute-start | bytes 479240 | tf_op jit(solution)/shard_map/ppermute | solution.py:347
  4.5 10.6 %collective-permute-start.5 = (bf16[48,1664]{1,0:T(8,128)(2,1)S(1)}, bf16[48,1664]{1,0:T(8,128)(2,1)S(1)}, u32[]{:S(2)}, u32[]{:S(2)}) collective-permute-start(bf16[48,1664]{1,0:T(8,128)(2,1)S(1)} %get-tuple-element.43), channel_id=1, source_target_pairs={{0,4},{2,6},{4,0},{6,2},{8,12},{10,14},{12,8},{14,10},{1,5},{3,7},... | collective-permute-start | bytes 479240 | tf_op jit(solution)/shard_map/ppermute | solution.py:347
  6.1 10.6 %collective-permute-start.6 = (bf16[48,1664]{1,0:T(8,128)(2,1)S(1)}, bf16[48,1664]{1,0:T(8,128)(2,1)S(1)}, u32[]{:S(2)}, u32[]{:S(2)}) collective-permute-start(bf16[48,1664]{1,0:T(8,128)(2,1)S(1)} %get-tuple-element.44), channel_id=1, source_target_pairs={{0,6},{2,4},{4,2},{6,0},{8,14},{10,12},{12,10},{14,8},{1,7},{3,5},... | collective-permute-start | bytes 479240 | tf_op jit(solution)/shard_map/ppermute | solution.py:347
  6.1 15.2 %collective-permute-start.1 = (bf16[16,1664]{1,0:T(8,128)(2,1)S(1)}, bf16[16,1664]{1,0:T(8,128)(2,1)S(1)}, u32[]{:S(2)}, u32[]{:S(2)}) collective-permute-start(bf16[16,1664]{1,0:T(8,128)(2,1)S(1)} %get-tuple-element.38), channel_id=1, source_target_pairs={{0,2},{2,0},{4,6},{6,4},{8,10},{10,8},{12,14},{14,12},{1,3},{3,1},... | collective-permute-start | bytes 159752 | tf_op jit(solution)/shard_map/ppermute | solution.py:347
  8.0 13.3 %collective-permute-start.2 = (bf16[16,1664]{1,0:T(8,128)(2,1)S(1)}, bf16[16,1664]{1,0:T(8,128)(2,1)S(1)}, u32[]{:S(2)}, u32[]{:S(2)}) collective-permute-start(bf16[16,1664]{1,0:T(8,128)(2,1)S(1)} %get-tuple-element.39), channel_id=1, source_target_pairs={{0,4},{2,6},{4,0},{6,2},{8,12},{10,14},{12,8},{14,10},{1,5},{3,7},... | collective-permute-start | bytes 159752 | tf_op jit(solution)/shard_map/ppermute | solution.py:347
  9.6 11.7 %collective-permute-start.3 = (bf16[16,1664]{1,0:T(8,128)(2,1)S(1)}, bf16[16,1664]{1,0:T(8,128)(2,1)S(1)}, u32[]{:S(2)}, u32[]{:S(2)}) collective-permute-start(bf16[16,1664]{1,0:T(8,128)(2,1)S(1)} %get-tuple-element.40), channel_id=1, source_target_pairs={{0,6},{2,4},{4,2},{6,0},{8,14},{10,12},{12,10},{14,8},{1,7},{3,5},... | collective-permute-start | bytes 159752 | tf_op jit(solution)/shard_map/ppermute | solution.py:347
  15.2 8.4 %collective-permute-start = (bf16[128,1536]{1,0:T(8,128)(2,1)S(1)}, bf16[128,1536]{1,0:T(8,128)(2,1)S(1)}, u32[]{:S(2)}, u32[]{:S(2)}) collective-permute-start(bf16[128,1536]{1,0:T(8,128)(2,1)S(1)} %shard_map.93.refs_4_), channel_id=1, source_target_pairs={{0,16},{16,0},{1,17},{17,1},{2,18},{18,2},{3,19},{19,3},{4,20},{20... | collective-permute-start | bytes 1179656 | tf_op jit(solution)/shard_map/ppermute | solution.py:286
  18.7 16.3 %collective-permute-start.8 = (bf16[96,1536]{1,0:T(8,128)(2,1)}, bf16[96,1536]{1,0:T(8,128)(2,1)S(1)}, u32[]{:S(2)}, u32[]{:S(2)}) collective-permute-start(bf16[96,1536]{1,0:T(8,128)(2,1)} %shard_map.95.refs_4_), channel_id=1, source_target_pairs={{0,8},{2,10},{4,12},{6,14},{8,0},{10,2},{12,4},{14,6},{1,9},{3,11}... | collective-permute-start | bytes 884744 | tf_op jit(solution)/shard_map/ppermute | solution.py:286
  21.3 1.7 %copy-start.4 = (bf16[16,1664]{1,0:T(8,128)(2,1)}, bf16[16,1664]{1,0:T(8,128)(2,1)S(1)}, u32[]{:S(2)}) copy-start(bf16[16,1664]{1,0:T(8,128)(2,1)S(1)} %collective-permute-done.1.refs_1_) | copy-start | bytes 159748
  21.3 1.7 %copy-start.6 = (bf16[16,1664]{1,0:T(8,128)(2,1)}, bf16[16,1664]{1,0:T(8,128)(2,1)S(1)}, u32[]{:S(2)}) copy-start(bf16[16,1664]{1,0:T(8,128)(2,1)S(1)} %collective-permute-done.2.refs_2_) | copy-start | bytes 159748
  21.3 1.7 %copy-start.8 = (bf16[16,1664]{1,0:T(8,128)(2,1)}, bf16[16,1664]{1,0:T(8,128)(2,1)S(1)}, u32[]{:S(2)}) copy-start(bf16[16,1664]{1,0:T(8,128)(2,1)S(1)} %collective-permute-done.3.refs_3_) | copy-start | bytes 159748
  21.3 2.1 %copy-start.11 = (f32[24]{0:T(128)S(1)}, f32[24]{0:T(128)}, u32[]{:S(2)}) copy-start(f32[24]{0:T(128)} %param.16) | copy-start | bytes 292
  21.3 2.2 %copy-start.1 = (bf16[1,32,8,1536]{3,2,1,0:T(8,128)(2,1)S(1)}, bf16[1,32,8,1536]{3,2,1,0:T(8,128)(2,1)}, u32[]{:S(2)}) copy-start(bf16[1,32,8,1536]{3,2,1,0:T(8,128)(2,1)} %param.10) | copy-start | bytes 2359300
  23.0 17.2 %collective-permute-start.7 = (bf16[32,1536]{1,0:T(8,128)(2,1)}, bf16[32,1536]{1,0:T(8,128)(2,1)S(1)}, u32[]{:S(2)}, u32[]{:S(2)}) collective-permute-start(bf16[32,1536]{1,0:T(8,128)(2,1)} %shard_map.96), channel_id=1, source_target_pairs={{0,8},{2,10},{4,12},{6,14},{8,0},{10,2},{12,4},{14,6},{1,9},{3,11}... | collective-permute-start | bytes 294920 | tf_op jit(solution)/shard_map/ppermute | solution.py:286
  25.6 14.5 %copy-start.3 = (bf16[16,1664]{1,0:T(8,128)(2,1)S(1)}, bf16[16,1664]{1,0:T(8,128)(2,1)}, u32[]{:S(2)}) copy-start(bf16[16,1664]{1,0:T(8,128)(2,1)} %copy-done.2) | copy-start | bytes 159748
  25.7 14.5 %copy-start.5 = (bf16[16,1664]{1,0:T(8,128)(2,1)S(1)}, bf16[16,1664]{1,0:T(8,128)(2,1)}, u32[]{:S(2)}) copy-start(bf16[16,1664]{1,0:T(8,128)(2,1)} %copy-done.4) | copy-start | bytes 159748
  25.7 14.5 %copy-start.7 = (bf16[16,1664]{1,0:T(8,128)(2,1)S(1)}, bf16[16,1664]{1,0:T(8,128)(2,1)}, u32[]{:S(2)}) copy-start(bf16[16,1664]{1,0:T(8,128)(2,1)} %copy-done.6) | copy-start | bytes 159748
  25.7 14.5 %copy-start.9 = (bf16[16,1664]{1,0:T(8,128)(2,1)S(1)}, bf16[16,1664]{1,0:T(8,128)(2,1)}, u32[]{:S(2)}) copy-start(bf16[16,1664]{1,0:T(8,128)(2,1)} %copy-done.8) | copy-start | bytes 159748
  36.6 7.6 %collective-permute-start.12 = (bf16[48,1536]{1,0:T(8,128)(2,1)S(1)}, bf16[48,1536]{1,0:T(8,128)(2,1)S(1)}, u32[]{:S(2)}, u32[]{:S(2)}) collective-permute-start(bf16[48,1536]{1,0:T(8,128)(2,1)S(1)} %get-tuple-element.50), channel_id=1, source_target_pairs={{0,2},{2,0},{4,6},{6,4},{8,10},{10,8},{12,14},{14,12},{1,3},{3,1},... | collective-permute-start | bytes 442376 | tf_op jit(solution)/shard_map/ppermute | solution.py:347
  37.1 7.7 %collective-permute-start.13 = (bf16[48,1536]{1,0:T(8,128)(2,1)S(1)}, bf16[48,1536]{1,0:T(8,128)(2,1)S(1)}, u32[]{:S(2)}, u32[]{:S(2)}) collective-permute-start(bf16[48,1536]{1,0:T(8,128)(2,1)S(1)} %get-tuple-element.51), channel_id=1, source_target_pairs={{0,4},{2,6},{4,0},{6,2},{8,12},{10,14},{12,8},{14,10},{1,5},{3,7},... | collective-permute-start | bytes 442376 | tf_op jit(solution)/shard_map/ppermute | solution.py:347
  37.2 8.8 %collective-permute-start.14 = (bf16[48,1536]{1,0:T(8,128)(2,1)S(1)}, bf16[48,1536]{1,0:T(8,128)(2,1)S(1)}, u32[]{:S(2)}, u32[]{:S(2)}) collective-permute-start(bf16[48,1536]{1,0:T(8,128)(2,1)S(1)} %get-tuple-element.52), channel_id=1, source_target_pairs={{0,6},{2,4},{4,2},{6,0},{8,14},{10,12},{12,10},{14,8},{1,7},{3,5},... | collective-permute-start | bytes 442376 | tf_op jit(solution)/shard_map/ppermute | solution.py:347
  40.2 4.6 %copy-start.10 = (f32[1536]{0:T(1024)S(1)}, f32[1536]{0:T(1024)}, u32[]{:S(2)}) copy-start(f32[1536]{0:T(1024)} %param.17) | copy-start | bytes 18436
  41.3 5.9 %collective-permute-start.9 = (bf16[16,1536]{1,0:T(8,128)(2,1)S(1)}, bf16[16,1536]{1,0:T(8,128)(2,1)S(1)}, u32[]{:S(2)}, u32[]{:S(2)}) collective-permute-start(bf16[16,1536]{1,0:T(8,128)(2,1)S(1)} %get-tuple-element.47), channel_id=1, source_target_pairs={{0,2},{2,0},{4,6},{6,4},{8,10},{10,8},{12,14},{14,12},{1,3},{3,1},... | collective-permute-start | bytes 147464 | tf_op jit(solution)/shard_map/ppermute | solution.py:347
  41.7 5.5 %collective-permute-start.10 = (bf16[16,1536]{1,0:T(8,128)(2,1)S(1)}, bf16[16,1536]{1,0:T(8,128)(2,1)S(1)}, u32[]{:S(2)}, u32[]{:S(2)}) collective-permute-start(bf16[16,1536]{1,0:T(8,128)(2,1)S(1)} %get-tuple-element.48), channel_id=1, source_target_pairs={{0,4},{2,6},{4,0},{6,2},{8,12},{10,14},{12,8},{14,10},{1,5},{3,7},... | collective-permute-start | bytes 147464 | tf_op jit(solution)/shard_map/ppermute | solution.py:347
  44.2 5.0 %collective-permute-start.11 = (bf16[16,1536]{1,0:T(8,128)(2,1)S(1)}, bf16[16,1536]{1,0:T(8,128)(2,1)S(1)}, u32[]{:S(2)}, u32[]{:S(2)}) collective-permute-start(bf16[16,1536]{1,0:T(8,128)(2,1)S(1)} %get-tuple-element.49), channel_id=1, source_target_pairs={{0,6},{2,4},{4,2},{6,0},{8,14},{10,12},{12,10},{14,8},{1,7},{3,5},... | collective-permute-start | bytes 147464 | tf_op jit(solution)/shard_map/ppermute | solution.py:347

commit v9 on v8

--- a/solution.py
+++ b/solution.py
@@ -9,7 +9,7 @@
 
 LANES = 128
 GROUP = 4
-LATER = 4
+PIECES = ((4,), (4,))
 STRIP = 512
 VMEM_LIMIT = 24 * 1024 * 1024
 F32 = jnp.float32
@@ -188,7 +188,7 @@
     )
 
 
-def write_state(scan, tokens_of, width, channels, s_ref, factor_ref):
+def write_state(scan, tokens_of, width, channels, s_refs, factor_ref):
     ends = scan.ends()
     if factor_ref:
         factor_ref[0][...] = ends
@@ -197,35 +197,40 @@
     for first, count in strips(channels):
         pick = picks(scan.heads, width, first, count)
         values = (tokens_of(first, count) * dot(scan.grow, pick)).astype(BF16)
-        s_ref[:, first : first + count] = (dot(into, values) * dot(ends, pick)).astype(BF16)
-
-
-def row_state_kernel(params_ref, *refs, group, axis, cols, heads, state, width):
-    blocks, s_ref, factor_ref = refs[:group], refs[group + 1], refs[group + 2 :]
+        made = (dot(into, values) * dot(ends, pick)).astype(BF16)
+        row = 0
+        for s_ref in s_refs:
+            s_ref[:, first : first + count] = made[row : row + s_ref.shape[0]]
+            row += s_ref.shape[0]
+
+
+def row_state_kernel(params_ref, *refs, group, count, axis, cols, heads, state, width):
+    blocks, s_refs, factor_ref = refs[:group], refs[group + 1 : group + 1 + count], refs[group + 1 + count :]
     member = mod(lax.axis_index(axis), group)
-    scan = row_scan(params_ref, blocks, member, cols, heads, state)
+    scan = row_scan(params_ref, [block[...] for block in blocks], member, cols, heads, state)
     tokens_of = lambda first, count: jnp.concatenate(
         [block[:, first : first + count] for block in blocks], axis=0
     ).astype(F32)
-    write_state(scan, tokens_of, width, s_ref.shape[1], s_ref, factor_ref)
-
-
-def col_state_kernel(params_ref, x_ref, raw_ref, maps_ref, s_ref, *factor_ref, cols, heads, state, width):
+    write_state(scan, tokens_of, width, s_refs[0].shape[1], s_refs, factor_ref)
+
+
+def col_state_kernel(params_ref, x_ref, raw_ref, maps_ref, _, s_ref, *factor_ref, cols, heads, state, width):
     scan = col_scan(params_ref, raw_ref, maps_ref, cols, heads, state)
     tokens_of = lambda first, count: x_ref[:, first : first + count].astype(F32)
-    write_state(scan, tokens_of, width, s_ref.shape[1], s_ref, factor_ref)
-
-
-def row_out_kernel(params_ref, s_ref, *refs, group, axis, cols, heads, state, width):
+    write_state(scan, tokens_of, width, s_ref.shape[1], [s_ref], factor_ref)
+
+
+def row_out_kernel(params_ref, s_ref, *refs, group, offset, axis, cols, heads, state, width):
     blocks, outs = refs[:group], refs[group + 1 :]
+    rows = outs[0].shape[0]
+    mine = slice(offset, offset + rows)
     member = mod(lax.axis_index(axis), group)
-    scan = row_scan(params_ref, blocks, member, cols, heads, state)
+    scan = row_scan(params_ref, [block[mine, :] for block in blocks], member, cols, heads, state)
     mix = scan.mix(lax.axis_index(axis) >= group)
-    rows = blocks[0].shape[0]
     for first, count in strips(s_ref.shape[1]):
         pick = picks(heads, width, first, count)
         part = slice(first, first + count)
-        x = jnp.concatenate([block[:, part] for block in blocks], axis=0).astype(F32)
+        x = jnp.concatenate([block[mine, part] for block in blocks], axis=0).astype(F32)
         values = (x * dot(scan.grow, pick)).astype(BF16)
         y = dot(mix, jnp.concatenate([values, s_ref[:, part]], axis=0)) * dot(scan.fade, pick)
         for s in range(group):
@@ -262,34 +267,31 @@
         copy.wait()
 
 
-SMALL = pl.CostEstimate(flops=1024, bytes_accessed=1024, transcendentals=0)
-LONG = pl.CostEstimate(flops=2 * 10**10, bytes_accessed=1024, transcendentals=0)
-
-
-def call(kernel, out_shape, specs=None, cost=SMALL, **more):
+def cost(micros):
+    return pl.CostEstimate(flops=1024 + int(micros * 10**9), bytes_accessed=1024, transcendentals=0)
+
+
+def call(kernel, out_shape, micros, specs=None, **more):
     if specs is not None:
         more["in_specs"] = [spec or pl.BlockSpec() for spec in specs]
     return pl.pallas_call(
         kernel,
         out_shape=out_shape,
         compiler_params=pltpu.CompilerParams(vmem_limit_bytes=VMEM_LIMIT),
-        cost_estimate=cost,
+        cost_estimate=cost(micros),
         **more,
     )
 
 
-def entering_states(made, axis, size, stride, width):
-    ends = made[0]
+def entering_states(ends, factor, axis, size, stride, width):
     if size == stride:
         return ends
     onward = [(i, (i + stride) % size) for i in range(size)]
     entering = lax.ppermute(ends, axis, onward)
     for _ in range(size // stride - 2):
         follows = (lax.axis_index(axis) >= stride).astype(F32)
-        factor = follows * jnp.repeat(made[1], width, axis=1)
-        entering = lax.ppermute(
-            (ends.astype(F32) + factor * entering.astype(F32)).astype(BF16), axis, onward
-        )
+        decayed = follows * jnp.repeat(factor[0], width, axis=1) * entering.astype(F32)
+        entering = lax.ppermute((ends.astype(F32) + decayed).astype(BF16), axis, onward)
     return entering
 
 
@@ -303,8 +305,7 @@
     while col_count % group:
         group //= 2
     share = tokens // group
-    later = max(share // LATER, 16)
-    pieces = [share - later, later]
+    pieces = [[eighths * share // 8 for eighths in piece] for piece in PIECES]
 
     x = x_in.reshape(tokens, channels)
     gate = gate_in.reshape(tokens, channels)
@@ -320,10 +321,10 @@
         functools.partial(pack_kernel, heads=heads, state=state, **shared),
         in_specs=[pl.BlockSpec(memory_space=pltpu.HBM)] * len(given),
         out_shape=[pltpu.VMEM(a.shape, a.dtype) for a in given[1:]]
-        + [pltpu.VMEM((rows, channels + LANES), BF16) for rows in pieces for _ in range(group)],
+        + [pltpu.VMEM((sum(piece), channels + LANES), BF16) for piece in pieces for _ in range(group)],
         scratch_shapes=[pltpu.SemaphoreType.DMA((len(given) - 1 + group * len(pieces),))],
         compiler_params=pltpu.CompilerParams(vmem_limit_bytes=VMEM_LIMIT),
-        cost_estimate=SMALL,
+        cost_estimate=cost(1),
     )(*[pltpu.with_memory_space_constraint(a, pltpu.HBM) for a in given])
     index, rates = lax.optimization_barrier((step_index, rates))
     params = pl.pallas_call(
@@ -339,7 +340,7 @@
         ),
         out_shape=shape((8, 2 * heads), F32),
         compiler_params=pltpu.CompilerParams(vmem_limit_bytes=VMEM_LIMIT),
-        cost_estimate=SMALL,
+        cost_estimate=cost(0),
     )(index, table, rates)
 
     def exchange(blocks):
@@ -348,54 +349,66 @@
         ]
 
     def state_shapes(places, count):
-        return [shape((places, channels), BF16)] + [shape((places, heads), F32)] * (count > 2)
+        states = [pltpu.VMEM((rows, channels), BF16) for rows in places]
+        return states + [shape((sum(places), heads), F32)] * (count > 2)
 
     got = [exchange(packed[i * group : (i + 1) * group]) for i in range(len(pieces))]
+    before = params
+    parts_of = []
+    for i, piece in enumerate(pieces):
+        places = [rows // cols * state for rows in piece]
+        made = call(
+            functools.partial(row_state_kernel, count=len(piece), **sizes, **shared),
+            state_shapes(places, col_count // group),
+            0,
+            specs=[None] * (1 + group) + [any_spec],
+        )(params, *got[i], before)
+        before = made[0]
+        for j, rows in enumerate(piece):
+            first = sum(places[:j])
+            factor = [f[first : first + places[j]] for f in made[len(piece) :]]
+            entering = entering_states(made[j], factor, "col", col_count, group, width)
+            offset = sum(piece[:j])
+            parts_of.append((i, offset, sum(map(sum, pieces[:i])) + offset, rows, entering))
+
     col_made = call(
         functools.partial(col_state_kernel, **sizes),
-        state_shapes(cols * state, row_count),
-    )(params, x, raw, maps)
-    col_entering = entering_states(col_made, "row", row_count, 1, width)
-    row_entering = []
-    before = col_made[0]
-    for i, rows in enumerate(pieces):
-        made = call(
-            functools.partial(row_state_kernel, **sizes, **shared),
-            state_shapes(rows // cols * state, col_count // group),
-            specs=[None] * (1 + group) + [any_spec],
-            cost=LONG if i else SMALL,
-        )(params, *got[i], before)
-        before = made[0]
-        row_entering.append(entering_states(made, "col", col_count, group, width))
+        state_shapes([cols * state], row_count),
+        0,
+        specs=[None] * 4 + [any_spec],
+    )(params, x, raw, maps, before)
+    col_entering = entering_states(col_made[0], col_made[1:], "row", row_count, 1, width)
 
     w, silu = call(
         functools.partial(col_out_kernel, **sizes),
-        [shape((tokens, channels), F32)] * 2,
+        [pltpu.VMEM((tokens, channels), F32)] * 2,
+        0,
     )(params, col_entering, x, raw, maps, gate, jnp.repeat(skip, width).reshape(1, channels))
 
     back = []
-    before = w
-    for i, rows in enumerate(pieces):
+    before = params
+    for i, offset, _, rows, entering in parts_of:
         y_row = call(
-            functools.partial(row_out_kernel, **sizes, **shared),
-            [shape((rows, channels), BF16)] * group,
+            functools.partial(row_out_kernel, offset=offset, **sizes, **shared),
+            [pltpu.VMEM((rows, channels), BF16)] * group,
+            20 if len(back) == len(parts_of) - 1 else 0,
             specs=[None] * (2 + group) + [any_spec],
-            cost=LONG if i else SMALL,
-        )(params, row_entering[i], *got[i], before)
+        )(params, entering, *got[i], before)
         back.append(exchange(y_row))
         before = y_row[0]
 
     mixed = None
-    for i, rows in enumerate(pieces):
+    for (_, _, first, rows, _), blocks in zip(parts_of, back):
         more = [] if mixed is None else [mixed]
         mixed = call(
-            functools.partial(final_kernel, offset=sum(pieces[:i]), share=share, **shared),
+            functools.partial(final_kernel, offset=first, share=share, **shared),
             shape((tokens, channels), BF16),
+            0,
             specs=[None] * (3 + group) + [any_spec] * len(more),
             out_specs=any_spec,
             scratch_shapes=[pltpu.VMEM((group, rows, channels), BF16), pltpu.SemaphoreType.DMA((group,))],
             input_output_aliases={3 + group: 0} if more else {},
-        )(w, silu, norm_gain.reshape(1, channels), *back[i], *more)
+        )(w, silu, norm_gain.reshape(1, channels), *blocks, *more)
     return mixed.reshape(x_in.shape)
 
 

time: 50.2 us -> 44.5 us (0.89)
  waiting for transfers between devices: 14.9 us -> 8.81 us
  starting transfers between devices: 20.6 us -> 22.9 us
  Pallas kernels: 13.4 us -> 11.7 us
    ppermute x3, waiting for transfers between devices: 9.35 us -> 5.91 us  [entering_states(): entering = lax.ppermute(ends, axis, onward)]
    ppermute x12, waiting for transfers between devices: 5.59 us -> 2.9 us  [exchange(): lax.ppermute(blocks[s], 'col', [(i, i ^ s) for i in range(col_count)])]
    ppermute x3, starting transfers between devices: 4.56 us -> 7 us  [entering_states(): entering = lax.ppermute(ends, axis, onward)]
    pallas_call x8, Pallas kernels: 11.7 us -> 10.2 us  [the longest x2 2.5 us: body(): call(functools.partial(row_out_kernel, offset=offset, **sizes, **shared),...]
  transfers between devices with their start and end apart: 15 -> 15, of which waited for: 4 -> 4; matrix products, arithmetic and copies ran while one was open for 0% -> 0% of each run, Pallas kernels for 22% -> 21%
where the time goes in v9:
time: 44.5 us; the launch traced here: 44.4 us
  starting transfers between devices  22.9 us (51%)
  Pallas kernels  11.7 us (26%)
  waiting for transfers between devices  8.81 us (20%)
  between operations  0.79 us (2%)
    ppermute x12, starting transfers between devices, exchange(): lax.ppermute(blocks[s], 'col', [(i, i ^ s) for i in range(col_count)])  15.9 us
    ppermute x3, starting transfers between devices, entering_states(): entering = lax.ppermute(ends, axis, onward)  7 us
    ppermute x3, waiting for transfers between devices, entering_states(): entering = lax.ppermute(ends, axis, onward)  5.91 us
    ppermute x12, waiting for transfers between devices, exchange(): lax.ppermute(blocks[s], 'col', [(i, i ^ s) for i in range(col_count)])  2.9 us
    pallas_call x2, Pallas kernels, body(): call(functools.partial(row_out_kernel, offset=offset, **sizes, **shared),...  2.5 us
    pallas_call x2, Pallas kernels, body(): call(functools.partial(row_state_kernel, count=len(piece), **sizes, **sha...  2.2 us
    pallas_call x1, Pallas kernels, body(): call(functools.partial(col_out_kernel, **sizes), [pltpu.VMEM((tokens, cha...  2.06 us
    pallas_call x2, Pallas kernels, body(): call(functools.partial(final_kernel, offset=first, share=share, **shared)...  1.91 us
  transfers between devices with their start and end apart: 15, of which 4 were waited for; matrix products, arithmetic and copies ran while one was open for 0% of the time, Pallas kernels for 21%

profile of v9, /device:TPU:0, one launch (start us, length us, event | category | flops | bytes accessed | tf_op | source)
XLA Modules:
  0.0 44.4 jit_solution(6589245961016849127)
XLA Ops:
  0.0 1.4 %shard_map.91 = (bf16[256,48]{1,0:T(8,128)(2,1)S(1)}, bf16[256,64]{1,0:T(8,128)(2,1)S(1)}, f32[48,1000]{1,0:T(8,128)S(1)}, f32[2,24]{1,0:T(2,128)S(1)}, bf16[32,...) custom-call(bf16[256,1536]{1,0:T(8,128)(2,1)} %bitcast.6, ...), custom_call_target="tpu_custom_call" | custom-call | flops 1000001024 | bytes 1024 | tf_op jit(solution)/shard_map/pallas_call | solution.py:320
  1.4 0.0 copy-start
  1.4 3.0 %collective-permute-start.3 = (bf16[32,1664]{1,0:T(8,128)(2,1)S(1)}, bf16[32,1664]{1,0:T(8,128)(2,1)S(1)}, u32[]{:S(2)}, u32[]{:S(2)}) collective-permute-start(bf16[32,1664]{1,0:T(8,128)(2,1)S(1)} %get-tuple-element.40), channel_id=1, source_target_pairs={{0,2},{2,0},{4,6},{6,4},{8,10},{10,8},{12,14},{14,12},{1,3},{3,1},... | collective-permute-start | bytes 319496 | tf_op jit(solution)/shard_map/ppermute | solution.py:348
  4.5 1.6 %collective-permute-start.4 = (bf16[32,1664]{1,0:T(8,128)(2,1)S(1)}, bf16[32,1664]{1,0:T(8,128)(2,1)S(1)}, u32[]{:S(2)}, u32[]{:S(2)}) collective-permute-start(bf16[32,1664]{1,0:T(8,128)(2,1)S(1)} %get-tuple-element.41), channel_id=1, source_target_pairs={{0,4},{2,6},{4,0},{6,2},{8,12},{10,14},{12,8},{14,10},{1,5},{3,7},... | collective-permute-start | bytes 319496 | tf_op jit(solution)/shard_map/ppermute | solution.py:348
  6.0 0.0 collective-permute-start.5
  6.0 1.9 %collective-permute-start = (bf16[32,1664]{1,0:T(8,128)(2,1)S(1)}, bf16[32,1664]{1,0:T(8,128)(2,1)S(1)}, u32[]{:S(2)}, u32[]{:S(2)}) collective-permute-start(bf16[32,1664]{1,0:T(8,128)(2,1)S(1)} %get-tuple-element.36), channel_id=1, source_target_pairs={{0,2},{2,0},{4,6},{6,4},{8,10},{10,8},{12,14},{14,12},{1,3},{3,1},... | collective-permute-start | bytes 319496 | tf_op jit(solution)/shard_map/ppermute | solution.py:348
  8.0 1.6 %collective-permute-start.1 = (bf16[32,1664]{1,0:T(8,128)(2,1)S(1)}, bf16[32,1664]{1,0:T(8,128)(2,1)S(1)}, u32[]{:S(2)}, u32[]{:S(2)}) collective-permute-start(bf16[32,1664]{1,0:T(8,128)(2,1)S(1)} %get-tuple-element.37), channel_id=1, source_target_pairs={{0,4},{2,6},{4,0},{6,2},{8,12},{10,14},{12,8},{14,10},{1,5},{3,7},... | collective-permute-start | bytes 319496 | tf_op jit(solution)/shard_map/ppermute | solution.py:348
  9.5 0.0 collective-permute-done.3.refs_1_
  9.5 0.7 %collective-permute-start.2 = (bf16[32,1664]{1,0:T(8,128)(2,1)S(1)}, bf16[32,1664]{1,0:T(8,128)(2,1)S(1)}, u32[]{:S(2)}, u32[]{:S(2)}) collective-permute-start(bf16[32,1664]{1,0:T(8,128)(2,1)S(1)} %get-tuple-element.38), channel_id=1, source_target_pairs={{0,6},{2,4},{4,2},{6,0},{8,14},{10,12},{12,10},{14,8},{1,7},{3,5},... | collective-permute-start | bytes 319496 | tf_op jit(solution)/shard_map/ppermute | solution.py:348
  10.8 0.2 shard_map.92.params_ref.refs_4_
  11.0 0.0 collective-permute-done.4.refs_2_
  11.0 1.9 %collective-permute-done.5.refs_3_ = bf16[32,1664]{1,0:T(8,128)(2,1)S(1)} collective-permute-done((bf16[32,1664]{1,0:T(8,128)(2,1)S(1)}, bf16[32,1664]{1,0:T(8,128)(2,1)S(1)}, u32[]{:S(2)}, u32[]{:S(2)}) %collective-permute-start.5) | collective-permute-done | bytes 106528 | tf_op jit(solution)/shard_map/ppermute | solution.py:348
  13.0 1.1 %shard_map.93.refs_4_ = bf16[64,1536]{1,0:T(8,128)(2,1)S(1)} custom-call(f32[8,48]{1,0:T(8,128)S(1)} %shard_map.92.params_ref.refs_4_, bf16[32,1664]{1,0:T(8,128)(2,1)S(1)} %get-tuple-element.39.refs_0_, bf16[32,1664]{1,0:T(8,128)(2,1)S(1)} %collective-permute-done.3.refs_1_, bf16[32,1664]{1,0:T(8,128)(2,1)S(1)} %collective-permute-done.4.refs_2_, ...), custom_call_target="tpu_custom_call" | custom-call | flops 1024 | bytes 1024 | tf_op jit(solution)/shard_map/pallas_call | solution.py:360
  14.1 2.6 %collective-permute-start.8 = (bf16[64,1536]{1,0:T(8,128)(2,1)S(1)}, bf16[64,1536]{1,0:T(8,128)(2,1)S(1)}, u32[]{:S(2)}, u32[]{:S(2)}) collective-permute-start(bf16[64,1536]{1,0:T(8,128)(2,1)S(1)} %shard_map.93.refs_4_), channel_id=1, source_target_pairs={{0,8},{2,10},{4,12},{6,14},{8,0},{10,2},{12,4},{14,6},{1,9},{3,11}... | collective-permute-start | bytes 589832 | tf_op jit(solution)/shard_map/ppermute | solution.py:290
  16.7 0.0 collective-permute-done.refs_1_
  16.7 0.0 collective-permute-done.1.refs_2_
  16.7 0.6 %collective-permute-done.2.refs_3_ = bf16[32,1664]{1,0:T(8,128)(2,1)S(1)} collective-permute-done((bf16[32,1664]{1,0:T(8,128)(2,1)S(1)}, bf16[32,1664]{1,0:T(8,128)(2,1)S(1)}, u32[]{:S(2)}, u32[]{:S(2)}) %collective-permute-start.2) | collective-permute-done | bytes 106528 | tf_op jit(solution)/shard_map/ppermute | solution.py:348
  17.2 1.1 %shard_map.94._ = bf16[64,1536]{1,0:T(8,128)(2,1)S(1)} custom-call(f32[8,48]{1,0:T(8,128)S(1)} %shard_map.92.params_ref.refs_4_, bf16[32,1664]{1,0:T(8,128)(2,1)S(1)} %get-tuple-element.35.refs_0_, bf16[32,1664]{1,0:T(8,128)(2,1)S(1)} %collective-permute-done.refs_1_, bf16[32,1664]{1,0:T(8,128)(2,1)S(1)} %collective-permute-done.1.refs_2_, ...), custom_call_target="tpu_custom_call" | custom-call | flops 1024 | bytes 1024 | tf_op jit(solution)/shard_map/pallas_call | solution.py:360
  18.4 2.8 %collective-permute-start.7 = (bf16[64,1536]{1,0:T(8,128)(2,1)S(1)}, bf16[64,1536]{1,0:T(8,128)(2,1)S(1)}, u32[]{:S(2)}, u32[]{:S(2)}) collective-permute-start(bf16[64,1536]{1,0:T(8,128)(2,1)S(1)} %shard_map.94._), channel_id=1, source_target_pairs={{0,8},{2,10},{4,12},{6,14},{8,0},{10,2},{12,4},{14,6},{1,9},{3,11}... | collective-permute-start | bytes 589832 | tf_op jit(solution)/shard_map/ppermute | solution.py:290
  21.2 0.0 copy-done
  21.2 1.5 %shard_map.95 = bf16[128,1536]{1,0:T(8,128)(2,1)S(1)} custom-call(f32[8,48]{1,0:T(8,128)S(1)} %shard_map.92.params_ref.refs_4_, bf16[256,1536]{1,0:T(8,128)(2,1)S(1)} %bitcast.7, bf16[256,48]{1,0:T(8,128)(2,1)S(1)} %get-tuple-element.33.raw_ref, bf16[256,64]{1,0:T(8,128)(2,1)S(1)} %get-tuple-element.34.maps_ref, bf16[64,1536]{1,0:T(8,128)(2,1)S(1)} %shard_map.94._), custom_call_target="tpu_custom_call" | custom-call | flops 1024 | bytes 1024 | tf_op jit(solution)/shard_map/pallas_call | solution.py:374
  22.7 1.6 %collective-permute-start.6 = (bf16[128,1536]{1,0:T(8,128)(2,1)S(1)}, bf16[128,1536]{1,0:T(8,128)(2,1)S(1)}, u32[]{:S(2)}, u32[]{:S(2)}) collective-permute-start(bf16[128,1536]{1,0:T(8,128)(2,1)S(1)} %shard_map.95), channel_id=1, source_target_pairs={{0,16},{16,0},{1,17},{17,1},{2,18},{18,2},{3,19},{19,3},{4,20},{20... | collective-permute-start | bytes 1179656 | tf_op jit(solution)/shard_map/ppermute | solution.py:290
  24.2 5.9 %collective-permute-done.8.s_ref = bf16[64,1536]{1,0:T(8,128)(2,1)S(1)} collective-permute-done((bf16[64,1536]{1,0:T(8,128)(2,1)S(1)}, bf16[64,1536]{1,0:T(8,128)(2,1)S(1)}, u32[]{:S(2)}, u32[]{:S(2)}) %collective-permute-start.8) | collective-permute-done | bytes 196640 | tf_op jit(solution)/shard_map/ppermute | solution.py:290
  30.1 1.2 %shard_map.97 = (bf16[32,1536]{1,0:T(8,128)(2,1)S(1)}, bf16[32,1536]{1,0:T(8,128)(2,1)S(1)}, bf16[32,1536]{1,0:T(8,128)(2,1)S(1)}, bf16[32,1536]{1,0:T(8,128)(2,1)S(1)}) custom-call(f32[8,48]{1,0:T(8,128)S(1)} %shard_map.92.params_ref.refs_4_, bf16[64,1536]{1,0:T(8,128)(2,1)S(1)} %collective-permute-done.8.s_ref, ...), custom_call_target="tpu_custom_call" | custom-call | flops 1024 | bytes 1024 | tf_op jit(solution)/shard_map/pallas_call | solution.py:391
  31.4 0.8 %collective-permute-start.12 = (bf16[32,1536]{1,0:T(8,128)(2,1)S(1)}, bf16[32,1536]{1,0:T(8,128)(2,1)S(1)}, u32[]{:S(2)}, u32[]{:S(2)}) collective-permute-start(bf16[32,1536]{1,0:T(8,128)(2,1)S(1)} %get-tuple-element.50), channel_id=1, source_target_pairs={{0,2},{2,0},{4,6},{6,4},{8,10},{10,8},{12,14},{14,12},{1,3},{3,1},... | collective-permute-start | bytes 294920 | tf_op jit(solution)/shard_map/ppermute | solution.py:348
  32.2 0.2 collective-permute-start.13
  32.4 2.5 %collective-permute-start.14 = (bf16[32,1536]{1,0:T(8,128)(2,1)S(1)}, bf16[32,1536]{1,0:T(8,128)(2,1)S(1)}, u32[]{:S(2)}, u32[]{:S(2)}) collective-permute-start(bf16[32,1536]{1,0:T(8,128)(2,1)S(1)} %get-tuple-element.52), channel_id=1, source_target_pairs={{0,6},{2,4},{4,2},{6,0},{8,14},{10,12},{12,10},{14,8},{1,7},{3,5},... | collective-permute-start | bytes 294920 | tf_op jit(solution)/shard_map/ppermute | solution.py:348
  34.9 0.0 collective-permute-done.7.s_ref
  34.9 0.0 copy-start.2
  34.9 0.0 copy-start.3
  34.9 0.0 copy-start.1
  35.0 1.3 %shard_map.98 = (bf16[32,1536]{1,0:T(8,128)(2,1)S(1)}, bf16[32,1536]{1,0:T(8,128)(2,1)S(1)}, bf16[32,1536]{1,0:T(8,128)(2,1)S(1)}, bf16[32,1536]{1,0:T(8,128)(2,1)S(1)}) custom-call(f32[8,48]{1,0:T(8,128)S(1)} %shard_map.92.params_ref.refs_4_, bf16[64,1536]{1,0:T(8,128)(2,1)S(1)} %collective-permute-done.7.s_ref, ...), custom_call_target="tpu_custom_call" | custom-call | flops 20000002048 | bytes 1024 | tf_op jit(solution)/shard_map/pallas_call | solution.py:391
  36.2 0.8 %collective-permute-start.9 = (bf16[32,1536]{1,0:T(8,128)(2,1)S(1)}, bf16[32,1536]{1,0:T(8,128)(2,1)S(1)}, u32[]{:S(2)}, u32[]{:S(2)}) collective-permute-start(bf16[32,1536]{1,0:T(8,128)(2,1)S(1)} %get-tuple-element.47), channel_id=1, source_target_pairs={{0,2},{2,0},{4,6},{6,4},{8,10},{10,8},{12,14},{14,12},{1,3},{3,1},... | collective-permute-start | bytes 294920 | tf_op jit(solution)/shard_map/ppermute | solution.py:348
  37.1 0.0 collective-permute-done.12.refs_1_
  37.1 0.2 collective-permute-start.10
  37.3 0.0 collective-permute-done.6.s_ref
  37.3 2.5 %collective-permute-start.11 = (bf16[32,1536]{1,0:T(8,128)(2,1)S(1)}, bf16[32,1536]{1,0:T(8,128)(2,1)S(1)}, u32[]{:S(2)}, u32[]{:S(2)}) collective-permute-start(bf16[32,1536]{1,0:T(8,128)(2,1)S(1)} %get-tuple-element.49), channel_id=1, source_target_pairs={{0,6},{2,4},{4,2},{6,0},{8,14},{10,12},{12,10},{14,8},{1,7},{3,5},... | collective-permute-start | bytes 294920 | tf_op jit(solution)/shard_map/ppermute | solution.py:348
  39.8 0.0 copy-done.2
  39.8 0.0 copy-done.3
  39.8 0.1 broadcast_in_dim.3
  39.9 0.1 reshape_reshape.3.skip_ref
  40.0 0.0 copy-done.1
  40.0 2.1 %shard_map.96 = (f32[256,1536]{1,0:T(8,128)S(1)}, f32[256,1536]{1,0:T(8,128)S(1)}) custom-call(f32[8,48]{1,0:T(8,128)S(1)} %shard_map.92.params_ref.refs_4_, bf16[128,1536]{1,0:T(8,128)(2,1)S(1)} %collective-permute-done.6.s_ref, bf16[256,1536]{1,0:T(8,128)(2,1)S(1)} %bitcast.8, bf16[256,48]{1,0:T(8,128)(2,1)S(1)} %get-tuple-element.33.raw_ref, ...), custom_call_target="tpu_custom_call" | custom-call | flops 1024 | bytes 1024 | tf_op jit(solution)/shard_map/pallas_call | solution.py:382
  42.0 0.0 collective-permute-done.13.refs_2_
  42.0 0.0 collective-permute-done.14.refs_3_
  42.0 1.0 %shard_map.99.refs_4_ = bf16[256,1536]{1,0:T(8,128)(2,1)} custom-call(f32[256,1536]{1,0:T(8,128)S(1)} %get-tuple-element.43.w_ref, f32[256,1536]{1,0:T(8,128)S(1)} %get-tuple-element.44.g_ref, f32[1,1536]{1,0:T(1,128)S(1)} %reshape.23.gain_ref, bf16[32,1536]{1,0:T(8,128)(2,1)S(1)} %get-tuple-element.45.refs_4_.refs_0_, ...), custom_call_target="tpu_custom_call" | custom-call | flops 1024 | bytes 1024 | tf_op jit(solution)/shard_map/pallas_call | solution.py:403
  43.0 0.0 collective-permute-done.9.refs_1_
  43.0 0.0 collective-permute-done.10.refs_2_
  43.0 0.4 collective-permute-done.11.refs_3_
  43.4 1.0 %shard_map.100 = bf16[256,1536]{1,0:T(8,128)(2,1)} custom-call(f32[256,1536]{1,0:T(8,128)S(1)} %get-tuple-element.43.w_ref, f32[256,1536]{1,0:T(8,128)S(1)} %get-tuple-element.44.g_ref, f32[1,1536]{1,0:T(1,128)S(1)} %reshape.23.gain_ref, bf16[32,1536]{1,0:T(8,128)(2,1)S(1)} %get-tuple-element.46.refs_0_, ...), custom_call_target="tpu_custom_call", output_to_operand_aliasing={{}: (7, {})} | custom-call | flops 1024 | bytes 1024 | tf_op jit(solution)/shard_map/pallas_call | solution.py:403
  (1 shorter events, 0.0 us)
Async XLA Ops:
  1.4 19.8 %copy-start = (bf16[1,32,8,1536]{3,2,1,0:T(8,128)(2,1)S(1)}, bf16[1,32,8,1536]{3,2,1,0:T(8,128)(2,1)}, u32[]{:S(2)}) copy-start(bf16[1,32,8,1536]{3,2,1,0:T(8,128)(2,1)} %param.9) | copy-start | bytes 2359300
  1.4 8.1 %collective-permute-start.3 = (bf16[32,1664]{1,0:T(8,128)(2,1)S(1)}, bf16[32,1664]{1,0:T(8,128)(2,1)S(1)}, u32[]{:S(2)}, u32[]{:S(2)}) collective-permute-start(bf16[32,1664]{1,0:T(8,128)(2,1)S(1)} %get-tuple-element.40), channel_id=1, source_target_pairs={{0,2},{2,0},{4,6},{6,4},{8,10},{10,8},{12,14},{14,12},{1,3},{3,1},... | collective-permute-start | bytes 319496 | tf_op jit(solution)/shard_map/ppermute | solution.py:348
  4.5 6.6 %collective-permute-start.4 = (bf16[32,1664]{1,0:T(8,128)(2,1)S(1)}, bf16[32,1664]{1,0:T(8,128)(2,1)S(1)}, u32[]{:S(2)}, u32[]{:S(2)}) collective-permute-start(bf16[32,1664]{1,0:T(8,128)(2,1)S(1)} %get-tuple-element.41), channel_id=1, source_target_pairs={{0,4},{2,6},{4,0},{6,2},{8,12},{10,14},{12,8},{14,10},{1,5},{3,7},... | collective-permute-start | bytes 319496 | tf_op jit(solution)/shard_map/ppermute | solution.py:348
  6.0 6.9 %collective-permute-start.5 = (bf16[32,1664]{1,0:T(8,128)(2,1)S(1)}, bf16[32,1664]{1,0:T(8,128)(2,1)S(1)}, u32[]{:S(2)}, u32[]{:S(2)}) collective-permute-start(bf16[32,1664]{1,0:T(8,128)(2,1)S(1)} %get-tuple-element.42), channel_id=1, source_target_pairs={{0,6},{2,4},{4,2},{6,0},{8,14},{10,12},{12,10},{14,8},{1,7},{3,5},... | collective-permute-start | bytes 319496 | tf_op jit(solution)/shard_map/ppermute | solution.py:348
  6.0 10.6 %collective-permute-start = (bf16[32,1664]{1,0:T(8,128)(2,1)S(1)}, bf16[32,1664]{1,0:T(8,128)(2,1)S(1)}, u32[]{:S(2)}, u32[]{:S(2)}) collective-permute-start(bf16[32,1664]{1,0:T(8,128)(2,1)S(1)} %get-tuple-element.36), channel_id=1, source_target_pairs={{0,2},{2,0},{4,6},{6,4},{8,10},{10,8},{12,14},{14,12},{1,3},{3,1},... | collective-permute-start | bytes 319496 | tf_op jit(solution)/shard_map/ppermute | solution.py:348
  8.0 8.7 %collective-permute-start.1 = (bf16[32,1664]{1,0:T(8,128)(2,1)S(1)}, bf16[32,1664]{1,0:T(8,128)(2,1)S(1)}, u32[]{:S(2)}, u32[]{:S(2)}) collective-permute-start(bf16[32,1664]{1,0:T(8,128)(2,1)S(1)} %get-tuple-element.37), channel_id=1, source_target_pairs={{0,4},{2,6},{4,0},{6,2},{8,12},{10,14},{12,8},{14,10},{1,5},{3,7},... | collective-permute-start | bytes 319496 | tf_op jit(solution)/shard_map/ppermute | solution.py:348
  9.5 7.7 %collective-permute-start.2 = (bf16[32,1664]{1,0:T(8,128)(2,1)S(1)}, bf16[32,1664]{1,0:T(8,128)(2,1)S(1)}, u32[]{:S(2)}, u32[]{:S(2)}) collective-permute-start(bf16[32,1664]{1,0:T(8,128)(2,1)S(1)} %get-tuple-element.38), channel_id=1, source_target_pairs={{0,6},{2,4},{4,2},{6,0},{8,14},{10,12},{12,10},{14,8},{1,7},{3,5},... | collective-permute-start | bytes 319496 | tf_op jit(solution)/shard_map/ppermute | solution.py:348
  14.1 16.1 %collective-permute-start.8 = (bf16[64,1536]{1,0:T(8,128)(2,1)S(1)}, bf16[64,1536]{1,0:T(8,128)(2,1)S(1)}, u32[]{:S(2)}, u32[]{:S(2)}) collective-permute-start(bf16[64,1536]{1,0:T(8,128)(2,1)S(1)} %shard_map.93.refs_4_), channel_id=1, source_target_pairs={{0,8},{2,10},{4,12},{6,14},{8,0},{10,2},{12,4},{14,6},{1,9},{3,11}... | collective-permute-start | bytes 589832 | tf_op jit(solution)/shard_map/ppermute | solution.py:290
  18.4 16.6 %collective-permute-start.7 = (bf16[64,1536]{1,0:T(8,128)(2,1)S(1)}, bf16[64,1536]{1,0:T(8,128)(2,1)S(1)}, u32[]{:S(2)}, u32[]{:S(2)}) collective-permute-start(bf16[64,1536]{1,0:T(8,128)(2,1)S(1)} %shard_map.94._), channel_id=1, source_target_pairs={{0,8},{2,10},{4,12},{6,14},{8,0},{10,2},{12,4},{14,6},{1,9},{3,11}... | collective-permute-start | bytes 589832 | tf_op jit(solution)/shard_map/ppermute | solution.py:290
  22.7 14.6 %collective-permute-start.6 = (bf16[128,1536]{1,0:T(8,128)(2,1)S(1)}, bf16[128,1536]{1,0:T(8,128)(2,1)S(1)}, u32[]{:S(2)}, u32[]{:S(2)}) collective-permute-start(bf16[128,1536]{1,0:T(8,128)(2,1)S(1)} %shard_map.95), channel_id=1, source_target_pairs={{0,16},{16,0},{1,17},{17,1},{2,18},{18,2},{3,19},{19,3},{4,20},{20... | collective-permute-start | bytes 1179656 | tf_op jit(solution)/shard_map/ppermute | solution.py:290
  31.4 5.7 %collective-permute-start.12 = (bf16[32,1536]{1,0:T(8,128)(2,1)S(1)}, bf16[32,1536]{1,0:T(8,128)(2,1)S(1)}, u32[]{:S(2)}, u32[]{:S(2)}) collective-permute-start(bf16[32,1536]{1,0:T(8,128)(2,1)S(1)} %get-tuple-element.50), channel_id=1, source_target_pairs={{0,2},{2,0},{4,6},{6,4},{8,10},{10,8},{12,14},{14,12},{1,3},{3,1},... | collective-permute-start | bytes 294920 | tf_op jit(solution)/shard_map/ppermute | solution.py:348
  32.2 9.8 %collective-permute-start.13 = (bf16[32,1536]{1,0:T(8,128)(2,1)S(1)}, bf16[32,1536]{1,0:T(8,128)(2,1)S(1)}, u32[]{:S(2)}, u32[]{:S(2)}) collective-permute-start(bf16[32,1536]{1,0:T(8,128)(2,1)S(1)} %get-tuple-element.51), channel_id=1, source_target_pairs={{0,4},{2,6},{4,0},{6,2},{8,12},{10,14},{12,8},{14,10},{1,5},{3,7},... | collective-permute-start | bytes 294920 | tf_op jit(solution)/shard_map/ppermute | solution.py:348
  32.4 9.6 %collective-permute-start.14 = (bf16[32,1536]{1,0:T(8,128)(2,1)S(1)}, bf16[32,1536]{1,0:T(8,128)(2,1)S(1)}, u32[]{:S(2)}, u32[]{:S(2)}) collective-permute-start(bf16[32,1536]{1,0:T(8,128)(2,1)S(1)} %get-tuple-element.52), channel_id=1, source_target_pairs={{0,6},{2,4},{4,2},{6,0},{8,14},{10,12},{12,10},{14,8},{1,7},{3,5},... | collective-permute-start | bytes 294920 | tf_op jit(solution)/shard_map/ppermute | solution.py:348
  34.9 4.8 %copy-start.2 = (f32[1536]{0:T(1024)S(1)}, f32[1536]{0:T(1024)}, u32[]{:S(2)}) copy-start(f32[1536]{0:T(1024)} %param.17) | copy-start | bytes 18436
  34.9 4.8 %copy-start.3 = (f32[24]{0:T(128)S(1)}, f32[24]{0:T(128)}, u32[]{:S(2)}) copy-start(f32[24]{0:T(128)} %param.16) | copy-start | bytes 292
  34.9 5.0 %copy-start.1 = (bf16[1,32,8,1536]{3,2,1,0:T(8,128)(2,1)S(1)}, bf16[1,32,8,1536]{3,2,1,0:T(8,128)(2,1)}, u32[]{:S(2)}) copy-start(bf16[1,32,8,1536]{3,2,1,0:T(8,128)(2,1)} %param.10) | copy-start | bytes 2359300
  36.2 6.8 %collective-permute-start.9 = (bf16[32,1536]{1,0:T(8,128)(2,1)S(1)}, bf16[32,1536]{1,0:T(8,128)(2,1)S(1)}, u32[]{:S(2)}, u32[]{:S(2)}) collective-permute-start(bf16[32,1536]{1,0:T(8,128)(2,1)S(1)} %get-tuple-element.47), channel_id=1, source_target_pairs={{0,2},{2,0},{4,6},{6,4},{8,10},{10,8},{12,14},{14,12},{1,3},{3,1},... | collective-permute-start | bytes 294920 | tf_op jit(solution)/shard_map/ppermute | solution.py:348
  37.1 6.0 %collective-permute-start.10 = (bf16[32,1536]{1,0:T(8,128)(2,1)S(1)}, bf16[32,1536]{1,0:T(8,128)(2,1)S(1)}, u32[]{:S(2)}, u32[]{:S(2)}) collective-permute-start(bf16[32,1536]{1,0:T(8,128)(2,1)S(1)} %get-tuple-element.48), channel_id=1, source_target_pairs={{0,4},{2,6},{4,0},{6,2},{8,12},{10,14},{12,8},{14,10},{1,5},{3,7},... | collective-permute-start | bytes 294920 | tf_op jit(solution)/shard_map/ppermute | solution.py:348
  37.3 6.2 %collective-permute-start.11 = (bf16[32,1536]{1,0:T(8,128)(2,1)S(1)}, bf16[32,1536]{1,0:T(8,128)(2,1)S(1)}, u32[]{:S(2)}, u32[]{:S(2)}) collective-permute-start(bf16[32,1536]{1,0:T(8,128)(2,1)S(1)} %get-tuple-element.49), channel_id=1, source_target_pairs={{0,6},{2,4},{4,2},{6,0},{8,14},{10,12},{12,10},{14,8},{1,7},{3,5},... | collective-permute-start | bytes 294920 | tf_op jit(solution)/shard_map/ppermute | solution.py:348

commit v10 on v9

--- a/solution.py
+++ b/solution.py
@@ -87,22 +87,27 @@
     def into(self):
         return widen(self.b_map, self.line, self.lines).astype(F32).T.astype(BF16)
 
-    def mix(self, follows):
+    def within(self):
         scores = lax.dot_general(
             self.c_map, self.b_map, (((1,), (1,)), ((), ())), preferred_element_type=F32
         )
-        within = jnp.where(self.lower, scores, 0.0).astype(BF16)
-        entering = widen(self.c_map, self.line, self.lines)
-        return jnp.concatenate([within, jnp.where(follows, entering, 0)], axis=1)
+        return jnp.where(self.lower, scores, 0.0).astype(BF16)
+
+    def entry(self, follows):
+        return jnp.where(follows, widen(self.c_map, self.line, self.lines), 0)
+
+
+def partner(member, i, group):
+    return member ^ ((group - i) & (group - 1))
 
 
 def column_order(cols):
     return lambda token: (mod(token, cols), div(token, cols))
 
 
-def row_order(cols, lines, member):
+def row_order(cols, lines, member, group):
     def order(token):
-        source = jnp.bitwise_xor(div(token, cols * lines), member)
+        source = partner(member, div(token, cols * lines), group)
         return mod(div(token, cols), lines), source * cols + mod(token, cols)
 
     return order
@@ -124,7 +129,7 @@
     offset = 0
     for i, out in enumerate(sent):
         rows = out.shape[0]
-        first = jnp.bitwise_xor(member, i % group) * share + offset
+        first = partner(member, i % group, group) * share + offset
         part = pl.ds(pl.multiple_of(first, 16), rows)
         places.append((out, part))
         moved.append((x_ref.at[part, :], out.at[:, pl.ds(0, channels)]))
@@ -166,7 +171,7 @@
     lines = tokens // (cols * len(blocks))
     aux = jnp.concatenate([block[:, channels:] for block in blocks], axis=0)
     return Scan(
-        row_order(cols, lines, member),
+        row_order(cols, lines, member, len(blocks)),
         lines,
         aux[:, :heads],
         params_ref[0:1, :heads],
@@ -220,26 +225,36 @@
     write_state(scan, tokens_of, width, s_ref.shape[1], [s_ref], factor_ref)
 
 
-def row_out_kernel(params_ref, s_ref, *refs, group, offset, axis, cols, heads, state, width):
-    blocks, outs = refs[:group], refs[group + 1 :]
-    rows = outs[0].shape[0]
+def row_local_kernel(params_ref, *refs, group, offset, axis, cols, heads, state, width):
+    blocks, (y_ref, fade_ref, entry_ref) = refs[:group], refs[group + 1 :]
+    rows = y_ref.shape[0] // group
     mine = slice(offset, offset + rows)
     member = mod(lax.axis_index(axis), group)
     scan = row_scan(params_ref, [block[mine, :] for block in blocks], member, cols, heads, state)
-    mix = scan.mix(lax.axis_index(axis) >= group)
-    for first, count in strips(s_ref.shape[1]):
+    mix = scan.within()
+    fade_ref[...] = scan.fade
+    entry_ref[...] = scan.entry(lax.axis_index(axis) >= group)
+    for first, count in strips(y_ref.shape[1]):
         pick = picks(heads, width, first, count)
         part = slice(first, first + count)
         x = jnp.concatenate([block[mine, part] for block in blocks], axis=0).astype(F32)
         values = (x * dot(scan.grow, pick)).astype(BF16)
-        y = dot(mix, jnp.concatenate([values, s_ref[:, part]], axis=0)) * dot(scan.fade, pick)
-        for s in range(group):
-            outs[s][:, part] = y[s * rows : (s + 1) * rows].astype(BF16)
+        y_ref[:, part] = dot(mix, values) * dot(scan.fade, pick)
+
+
+def row_out_kernel(s_ref, y_ref, fade_ref, entry_ref, _, *outs, heads, width):
+    rows = outs[0].shape[0]
+    for first, count in strips(s_ref.shape[1]):
+        pick = picks(heads, width, first, count)
+        part = slice(first, first + count)
+        y = y_ref[:, part] + dot(entry_ref[...], s_ref[:, part]) * dot(fade_ref[...], pick)
+        for i, out in enumerate(outs):
+            out[:, part] = y[i * rows : (i + 1) * rows].astype(BF16)
 
 
 def col_out_kernel(params_ref, s_ref, x_ref, raw_ref, maps_ref, gate_ref, skip_ref, w_ref, g_ref, *, cols, heads, state, width):
     scan = col_scan(params_ref, raw_ref, maps_ref, cols, heads, state)
-    mix = scan.mix(lax.axis_index("row") > 0)
+    mix = jnp.concatenate([scan.within(), scan.entry(lax.axis_index("row") > 0)], axis=1)
     for first, count in strips(s_ref.shape[1]):
         pick = picks(heads, width, first, count)
         part = slice(first, first + count)
@@ -257,7 +272,7 @@
     member = mod(lax.axis_index(axis), group)
     copies = []
     for s in range(group):
-        part = pl.ds(pl.multiple_of(jnp.bitwise_xor(member, s) * share + offset, 16), rows)
+        part = pl.ds(pl.multiple_of(partner(member, s, group) * share + offset, 16), rows)
         v = (blocks[s][...].astype(F32) + w_ref[part, :]) * g_ref[part, :]
         power = jnp.sum(v * v, axis=1, keepdims=True) / channels
         made[s] = (v * lax.rsqrt(power + 1e-5) * gain_ref[...]).astype(BF16)
@@ -345,7 +360,8 @@
 
     def exchange(blocks):
         return [blocks[0]] + [
-            lax.ppermute(blocks[s], "col", [(i, i ^ s) for i in range(col_count)]) for s in range(1, group)
+            lax.ppermute(blocks[i], "col", [(at, partner(at, i, group)) for at in range(col_count)])
+            for i in range(1, group)
         ]
 
     def state_shapes(places, count):
@@ -364,6 +380,15 @@
             specs=[None] * (1 + group) + [any_spec],
         )(params, *got[i], before)
         before = made[0]
+        if i == 0:
+            col_made = call(
+                functools.partial(col_state_kernel, **sizes),
+                state_shapes([cols * state], row_count),
+                0,
+                specs=[None] * 4 + [any_spec],
+            )(params, x, raw, maps, before)
+            col_entering = entering_states(col_made[0], col_made[1:], "row", row_count, 1, width)
+            before = col_made[0]
         for j, rows in enumerate(piece):
             first = sum(places[:j])
             factor = [f[first : first + places[j]] for f in made[len(piece) :]]
@@ -371,29 +396,37 @@
             offset = sum(piece[:j])
             parts_of.append((i, offset, sum(map(sum, pieces[:i])) + offset, rows, entering))
 
-    col_made = call(
-        functools.partial(col_state_kernel, **sizes),
-        state_shapes([cols * state], row_count),
-        0,
-        specs=[None] * 4 + [any_spec],
-    )(params, x, raw, maps, before)
-    col_entering = entering_states(col_made[0], col_made[1:], "row", row_count, 1, width)
-
     w, silu = call(
         functools.partial(col_out_kernel, **sizes),
         [pltpu.VMEM((tokens, channels), F32)] * 2,
         0,
     )(params, col_entering, x, raw, maps, gate, jnp.repeat(skip, width).reshape(1, channels))
 
+    local = []
+    for i, offset, _, rows, _ in parts_of:
+        places = rows // cols * state
+        local.append(
+            call(
+                functools.partial(row_local_kernel, offset=offset, **sizes, **shared),
+                [
+                    pltpu.VMEM((group * rows, channels), F32),
+                    pltpu.VMEM((group * rows, 2 * heads), BF16),
+                    pltpu.VMEM((group * rows, places), BF16),
+                ],
+                0,
+                specs=[None] * (1 + group) + [any_spec],
+            )(params, *got[i], before)
+        )
+    before = params
+
     back = []
-    before = params
-    for i, offset, _, rows, entering in parts_of:
+    for (_, _, _, rows, entering), known in zip(parts_of, local):
         y_row = call(
-            functools.partial(row_out_kernel, offset=offset, **sizes, **shared),
+            functools.partial(row_out_kernel, heads=heads, width=width),
             [pltpu.VMEM((rows, channels), BF16)] * group,
             20 if len(back) == len(parts_of) - 1 else 0,
-            specs=[None] * (2 + group) + [any_spec],
-        )(params, entering, *got[i], before)
+            specs=[None] * 4 + [any_spec],
+        )(entering, *known, before)
         back.append(exchange(y_row))
         before = y_row[0]
 

time: 44.5 us -> 43 us (0.966)
  starting transfers between devices: 22.9 us -> 20.6 us
  Pallas kernels: 11.7 us -> 12.5 us
    ppermute x3, starting transfers between devices: 7 us -> 4.82 us  [entering_states(): entering = lax.ppermute(ends, axis, onward)]
    ppermute x12, waiting for transfers between devices: 2.9 us -> 3.84 us  [exchange(): lax.ppermute(blocks[i], 'col', [(at, partner(at, i, group)) for at in ran...]
    ppermute x3, waiting for transfers between devices: 5.91 us -> 5.06 us  [entering_states(): entering = lax.ppermute(ends, axis, onward)]
    pallas_call x2 -> x4, Pallas kernels: 2.5 us -> 3.15 us  [the longest x2 2.46 us: body(): call(functools.partial(row_local_kernel, offset=offset, **sizes, **shared...]
  transfers between devices with their start and end apart: 15 -> 15, of which waited for: 4 -> 5; matrix products, arithmetic and copies ran while one was open for 0% -> 0% of each run, Pallas kernels for 21% -> 23%
where the time goes in v10:
time: 43 us; the launch traced here: 42.9 us
  starting transfers between devices  20.6 us (48%)
  Pallas kernels  12.5 us (29%)
  waiting for transfers between devices  8.9 us (21%)
  between operations  0.8 us (2%)
    ppermute x12, starting transfers between devices, exchange(): lax.ppermute(blocks[i], 'col', [(at, partner(at, i, group)) for at in ran...  15.7 us
    ppermute x3, waiting for transfers between devices, entering_states(): entering = lax.ppermute(ends, axis, onward)  5.06 us
    ppermute x3, starting transfers between devices, entering_states(): entering = lax.ppermute(ends, axis, onward)  4.82 us
    ppermute x12, waiting for transfers between devices, exchange(): lax.ppermute(blocks[i], 'col', [(at, partner(at, i, group)) for at in ran...  3.84 us
    pallas_call x2, Pallas kernels, body(): call(functools.partial(row_local_kernel, offset=offset, **sizes, **shared...  2.46 us
    pallas_call x2, Pallas kernels, body(): call(functools.partial(row_state_kernel, count=len(piece), **sizes, **sha...  2.22 us
    pallas_call x1, Pallas kernels, body(): call(functools.partial(col_out_kernel, **sizes), [pltpu.VMEM((tokens, cha...  2.05 us
    pallas_call x2, Pallas kernels, body(): call(functools.partial(final_kernel, offset=first, share=share, **shared)...  1.91 us
  transfers between devices with their start and end apart: 15, of which 5 were waited for; matrix products, arithmetic and copies ran while one was open for 0% of the time, Pallas kernels for 23%

profile of v10, /device:TPU:0, one launch (start us, length us, event | category | flops | bytes accessed | tf_op | source)
XLA Modules:
  0.0 42.9 jit_solution(15577195495775547713)
XLA Ops:
  0.0 0.0 copy-start
  0.0 1.5 %shard_map.91 = (bf16[256,48]{1,0:T(8,128)(2,1)S(1)}, bf16[256,64]{1,0:T(8,128)(2,1)S(1)}, f32[48,1000]{1,0:T(8,128)S(1)}, f32[2,24]{1,0:T(2,128)S(1)}, bf16[32,...) custom-call(bf16[256,1536]{1,0:T(8,128)(2,1)} %bitcast.6, ...), custom_call_target="tpu_custom_call" | custom-call | flops 1000001024 | bytes 1024 | tf_op jit(solution)/shard_map/pallas_call | solution.py:335
  1.5 4.0 %collective-permute-start = (bf16[32,1664]{1,0:T(8,128)(2,1)S(1)}, bf16[32,1664]{1,0:T(8,128)(2,1)S(1)}, u32[]{:S(2)}, u32[]{:S(2)}) collective-permute-start(bf16[32,1664]{1,0:T(8,128)(2,1)S(1)} %get-tuple-element.42), channel_id=1, source_target_pairs={{0,6},{2,4},{4,2},{6,0},{8,14},{10,12},{12,10},{14,8},{1,7},{3,5},... | collective-permute-start | bytes 319496 | tf_op jit(solution)/shard_map/ppermute | solution.py:363
  5.5 0.4 %collective-permute-start.1 = (bf16[32,1664]{1,0:T(8,128)(2,1)S(1)}, bf16[32,1664]{1,0:T(8,128)(2,1)S(1)}, u32[]{:S(2)}, u32[]{:S(2)}) collective-permute-start(bf16[32,1664]{1,0:T(8,128)(2,1)S(1)} %get-tuple-element.43), channel_id=1, source_target_pairs={{0,4},{2,6},{4,0},{6,2},{8,12},{10,14},{12,8},{14,10},{1,5},{3,7},... | collective-permute-start | bytes 319496 | tf_op jit(solution)/shard_map/ppermute | solution.py:363
  6.0 0.2 collective-permute-start.2
  6.2 2.8 %collective-permute-start.4 = (bf16[32,1664]{1,0:T(8,128)(2,1)S(1)}, bf16[32,1664]{1,0:T(8,128)(2,1)S(1)}, u32[]{:S(2)}, u32[]{:S(2)}) collective-permute-start(bf16[32,1664]{1,0:T(8,128)(2,1)S(1)} %get-tuple-element.48), channel_id=1, source_target_pairs={{0,6},{2,4},{4,2},{6,0},{8,14},{10,12},{12,10},{14,8},{1,7},{3,5},... | collective-permute-start | bytes 319496 | tf_op jit(solution)/shard_map/ppermute | solution.py:363
  9.0 0.4 %collective-permute-start.5 = (bf16[32,1664]{1,0:T(8,128)(2,1)S(1)}, bf16[32,1664]{1,0:T(8,128)(2,1)S(1)}, u32[]{:S(2)}, u32[]{:S(2)}) collective-permute-start(bf16[32,1664]{1,0:T(8,128)(2,1)S(1)} %get-tuple-element.49), channel_id=1, source_target_pairs={{0,4},{2,6},{4,0},{6,2},{8,12},{10,14},{12,8},{14,10},{1,5},{3,7},... | collective-permute-start | bytes 319496 | tf_op jit(solution)/shard_map/ppermute | solution.py:363
  9.5 0.0 collective-permute-done.refs_1_
  9.5 1.6 %collective-permute-start.6 = (bf16[32,1664]{1,0:T(8,128)(2,1)S(1)}, bf16[32,1664]{1,0:T(8,128)(2,1)S(1)}, u32[]{:S(2)}, u32[]{:S(2)}) collective-permute-start(bf16[32,1664]{1,0:T(8,128)(2,1)S(1)} %get-tuple-element.50), channel_id=1, source_target_pairs={{0,2},{2,0},{4,6},{6,4},{8,10},{10,8},{12,14},{14,12},{1,3},{3,1},... | collective-permute-start | bytes 319496 | tf_op jit(solution)/shard_map/ppermute | solution.py:363
  11.8 0.2 shard_map.92.params_ref.refs_4_._
  11.9 0.0 collective-permute-done.1.refs_2_
  11.9 1.8 %collective-permute-done.2.refs_3_ = bf16[32,1664]{1,0:T(8,128)(2,1)S(1)} collective-permute-done((bf16[32,1664]{1,0:T(8,128)(2,1)S(1)}, bf16[32,1664]{1,0:T(8,128)(2,1)S(1)}, u32[]{:S(2)}, u32[]{:S(2)}) %collective-permute-start.2) | collective-permute-done | bytes 106528 | tf_op jit(solution)/shard_map/ppermute | solution.py:363
  13.7 1.1 %shard_map.93._ = bf16[64,1536]{1,0:T(8,128)(2,1)S(1)} custom-call(f32[8,48]{1,0:T(8,128)S(1)} %shard_map.92.params_ref.refs_4_._, bf16[32,1664]{1,0:T(8,128)(2,1)S(1)} %get-tuple-element.41.refs_0_, bf16[32,1664]{1,0:T(8,128)(2,1)S(1)} %collective-permute-done.refs_1_, bf16[32,1664]{1,0:T(8,128)(2,1)S(1)} %collective-permute-done.1.refs_2_, ...), custom_call_target="tpu_custom_call" | custom-call | flops 1024 | bytes 1024 | tf_op jit(solution)/shard_map/pallas_call | solution.py:376
  14.8 3.0 %collective-permute-start.8 = (bf16[64,1536]{1,0:T(8,128)(2,1)S(1)}, bf16[64,1536]{1,0:T(8,128)(2,1)S(1)}, u32[]{:S(2)}, u32[]{:S(2)}) collective-permute-start(bf16[64,1536]{1,0:T(8,128)(2,1)S(1)} %shard_map.93._), channel_id=1, source_target_pairs={{0,8},{2,10},{4,12},{6,14},{8,0},{10,2},{12,4},{14,6},{1,9},{3,11}... | collective-permute-start | bytes 589832 | tf_op jit(solution)/shard_map/ppermute | solution.py:305
  17.8 0.0 copy-done
  17.8 1.5 %shard_map.94.refs_4_ = bf16[128,1536]{1,0:T(8,128)(2,1)S(1)} custom-call(f32[8,48]{1,0:T(8,128)S(1)} %shard_map.92.params_ref.refs_4_._, bf16[256,1536]{1,0:T(8,128)(2,1)S(1)} %bitcast.7, bf16[256,48]{1,0:T(8,128)(2,1)S(1)} %get-tuple-element.39.raw_ref, bf16[256,64]{1,0:T(8,128)(2,1)S(1)} %get-tuple-element.40.maps_ref, bf16[64,1536]{1,0:T(8,128)(2,1)S(1)} %shard_map.93._), custom_call_target="tpu_custom_call" | custom-call | flops 1024 | bytes 1024 | tf_op jit(solution)/shard_map/pallas_call | solution.py:384
  19.3 0.0 collective-permute-done.4.refs_1_
  19.3 0.0 collective-permute-done.5.refs_2_
  19.3 0.0 collective-permute-done.6.refs_3_
  19.3 1.1 %shard_map.96.refs_4_ = bf16[64,1536]{1,0:T(8,128)(2,1)S(1)} custom-call(f32[8,48]{1,0:T(8,128)S(1)} %shard_map.92.params_ref.refs_4_._, bf16[32,1664]{1,0:T(8,128)(2,1)S(1)} %get-tuple-element.47.refs_0_, bf16[32,1664]{1,0:T(8,128)(2,1)S(1)} %collective-permute-done.4.refs_1_, bf16[32,1664]{1,0:T(8,128)(2,1)S(1)} %collective-permute-done.5.refs_2_, ...), custom_call_target="tpu_custom_call" | custom-call | flops 1024 | bytes 1024 | tf_op jit(solution)/shard_map/pallas_call | solution.py:376
  20.4 0.1 collective-permute-start.7
  20.5 1.8 %collective-permute-start.3 = (bf16[128,1536]{1,0:T(8,128)(2,1)S(1)}, bf16[128,1536]{1,0:T(8,128)(2,1)S(1)}, u32[]{:S(2)}, u32[]{:S(2)}) collective-permute-start(bf16[128,1536]{1,0:T(8,128)(2,1)S(1)} %shard_map.94.refs_4_), channel_id=1, source_target_pairs={{0,16},{16,0},{1,17},{17,1},{2,18},{18,2},{3,19},{19,3},{4,20},{20... | collective-permute-start | bytes 1179656 | tf_op jit(solution)/shard_map/ppermute | solution.py:305
  22.3 1.2 %shard_map.98 = (f32[128,1536]{1,0:T(8,128)S(1)}, bf16[128,48]{1,0:T(8,128)(2,1)S(1)}, bf16[128,64]{1,0:T(8,128)(2,1)S(1)}) custom-call(f32[8,48]{1,0:T(8,128)S(1)} %shard_map.92.params_ref.refs_4_._, bf16[32,1664]{1,0:T(8,128)(2,1)S(1)} %get-tuple-element.41.refs_0_, bf16[32,1664]{1,0:T(8,128)(2,1)S(1)} %collective-permute-done.refs_1_, ...), custom_call_target="tpu_custom_call" | custom-call | flops 1024 | bytes 1024 | tf_op jit(solution)/shard_map/pallas_call | solution.py:409
  23.5 1.2 %shard_map.97 = (f32[128,1536]{1,0:T(8,128)S(1)}, bf16[128,48]{1,0:T(8,128)(2,1)S(1)}, bf16[128,64]{1,0:T(8,128)(2,1)S(1)}) custom-call(f32[8,48]{1,0:T(8,128)S(1)} %shard_map.92.params_ref.refs_4_._, bf16[32,1664]{1,0:T(8,128)(2,1)S(1)} %get-tuple-element.47.refs_0_, bf16[32,1664]{1,0:T(8,128)(2,1)S(1)} %collective-permute-done.4.refs_1_, ...), custom_call_target="tpu_custom_call" | custom-call | flops 1024 | bytes 1024 | tf_op jit(solution)/shard_map/pallas_call | solution.py:409
  24.8 5.1 %collective-permute-done.8.s_ref = bf16[64,1536]{1,0:T(8,128)(2,1)S(1)} collective-permute-done((bf16[64,1536]{1,0:T(8,128)(2,1)S(1)}, bf16[64,1536]{1,0:T(8,128)(2,1)S(1)}, u32[]{:S(2)}, u32[]{:S(2)}) %collective-permute-start.8) | collective-permute-done | bytes 196640 | tf_op jit(solution)/shard_map/ppermute | solution.py:305
  29.8 0.3 shard_map.99
  30.2 1.5 %collective-permute-start.12 = (bf16[32,1536]{1,0:T(8,128)(2,1)S(1)}, bf16[32,1536]{1,0:T(8,128)(2,1)S(1)}, u32[]{:S(2)}, u32[]{:S(2)}) collective-permute-start(bf16[32,1536]{1,0:T(8,128)(2,1)S(1)} %get-tuple-element.62), channel_id=1, source_target_pairs={{0,6},{2,4},{4,2},{6,0},{8,14},{10,12},{12,10},{14,8},{1,7},{3,5},... | collective-permute-start | bytes 294920 | tf_op jit(solution)/shard_map/ppermute | solution.py:363
  31.6 1.2 %collective-permute-start.13 = (bf16[32,1536]{1,0:T(8,128)(2,1)S(1)}, bf16[32,1536]{1,0:T(8,128)(2,1)S(1)}, u32[]{:S(2)}, u32[]{:S(2)}) collective-permute-start(bf16[32,1536]{1,0:T(8,128)(2,1)S(1)} %get-tuple-element.63), channel_id=1, source_target_pairs={{0,4},{2,6},{4,0},{6,2},{8,12},{10,14},{12,8},{14,10},{1,5},{3,7},... | collective-permute-start | bytes 294920 | tf_op jit(solution)/shard_map/ppermute | solution.py:363
  32.9 0.8 %collective-permute-start.14 = (bf16[32,1536]{1,0:T(8,128)(2,1)S(1)}, bf16[32,1536]{1,0:T(8,128)(2,1)S(1)}, u32[]{:S(2)}, u32[]{:S(2)}) collective-permute-start(bf16[32,1536]{1,0:T(8,128)(2,1)S(1)} %get-tuple-element.64), channel_id=1, source_target_pairs={{0,2},{2,0},{4,6},{6,4},{8,10},{10,8},{12,14},{14,12},{1,3},{3,1},... | collective-permute-start | bytes 294920 | tf_op jit(solution)/shard_map/ppermute | solution.py:363
  33.7 0.0 collective-permute-done.7.s_ref
  33.7 0.0 copy-start.2
  33.7 0.0 copy-start.3
  33.7 0.0 copy-start.1
  33.7 0.3 shard_map.100
  34.1 1.5 %collective-permute-start.9 = (bf16[32,1536]{1,0:T(8,128)(2,1)S(1)}, bf16[32,1536]{1,0:T(8,128)(2,1)S(1)}, u32[]{:S(2)}, u32[]{:S(2)}) collective-permute-start(bf16[32,1536]{1,0:T(8,128)(2,1)S(1)} %get-tuple-element.59), channel_id=1, source_target_pairs={{0,6},{2,4},{4,2},{6,0},{8,14},{10,12},{12,10},{14,8},{1,7},{3,5},... | collective-permute-start | bytes 294920 | tf_op jit(solution)/shard_map/ppermute | solution.py:363
  35.6 1.4 %collective-permute-done.12.refs_1_ = bf16[32,1536]{1,0:T(8,128)(2,1)S(1)} collective-permute-done((bf16[32,1536]{1,0:T(8,128)(2,1)S(1)}, bf16[32,1536]{1,0:T(8,128)(2,1)S(1)}, u32[]{:S(2)}, u32[]{:S(2)}) %collective-permute-start.12) | collective-permute-done | bytes 98336 | tf_op jit(solution)/shard_map/ppermute | solution.py:363
  36.9 0.0 collective-permute-start.10
  36.9 0.0 collective-permute-done.3.s_ref
  36.9 1.1 %collective-permute-start.11 = (bf16[32,1536]{1,0:T(8,128)(2,1)S(1)}, bf16[32,1536]{1,0:T(8,128)(2,1)S(1)}, u32[]{:S(2)}, u32[]{:S(2)}) collective-permute-start(bf16[32,1536]{1,0:T(8,128)(2,1)S(1)} %get-tuple-element.61), channel_id=1, source_target_pairs={{0,2},{2,0},{4,6},{6,4},{8,10},{10,8},{12,14},{14,12},{1,3},{3,1},... | collective-permute-start | bytes 294920 | tf_op jit(solution)/shard_map/ppermute | solution.py:363
  38.0 0.0 copy-done.2
  38.0 0.0 copy-done.3
  38.0 0.1 broadcast_in_dim.3
  38.1 0.1 reshape_reshape.3.skip_ref
  38.2 0.0 copy-done.1
  38.2 2.0 %shard_map.95 = (f32[256,1536]{1,0:T(8,128)S(1)}, f32[256,1536]{1,0:T(8,128)S(1)}) custom-call(f32[8,48]{1,0:T(8,128)S(1)} %shard_map.92.params_ref.refs_4_._, bf16[128,1536]{1,0:T(8,128)(2,1)S(1)} %collective-permute-done.3.s_ref, bf16[256,1536]{1,0:T(8,128)(2,1)S(1)} %bitcast.8, bf16[256,48]{1,0:T(8,128)(2,1)S(1)} %get-tuple-element.39.raw_ref, ...), custom_call_target="tpu_custom_call" | custom-call | flops 1024 | bytes 1024 | tf_op jit(solution)/shard_map/pallas_call | solution.py:399
  40.2 0.0 collective-permute-done.13.refs_2_
  40.2 0.0 collective-permute-done.14.refs_3_
  40.3 1.0 %shard_map.101.refs_4_ = bf16[256,1536]{1,0:T(8,128)(2,1)} custom-call(f32[256,1536]{1,0:T(8,128)S(1)} %get-tuple-element.45.w_ref, f32[256,1536]{1,0:T(8,128)S(1)} %get-tuple-element.46.g_ref, f32[1,1536]{1,0:T(1,128)S(1)} %reshape.23.gain_ref, bf16[32,1536]{1,0:T(8,128)(2,1)S(1)} %get-tuple-element.57._.refs_0_, ...), custom_call_target="tpu_custom_call" | custom-call | flops 1024 | bytes 1024 | tf_op jit(solution)/shard_map/pallas_call | solution.py:436
  41.2 0.0 collective-permute-done.9.refs_1_
  41.2 0.3 collective-permute-done.10.refs_2_
  41.5 0.4 collective-permute-done.11.refs_3_
  41.9 1.0 %shard_map.102 = bf16[256,1536]{1,0:T(8,128)(2,1)} custom-call(f32[256,1536]{1,0:T(8,128)S(1)} %get-tuple-element.45.w_ref, f32[256,1536]{1,0:T(8,128)S(1)} %get-tuple-element.46.g_ref, f32[1,1536]{1,0:T(1,128)S(1)} %reshape.23.gain_ref, bf16[32,1536]{1,0:T(8,128)(2,1)S(1)} %get-tuple-element.58.refs_0_, ...), custom_call_target="tpu_custom_call", output_to_operand_aliasing={{}: (7, {})} | custom-call | flops 1024 | bytes 1024 | tf_op jit(solution)/shard_map/pallas_call | solution.py:436
  (1 shorter events, 0.0 us)
Async XLA Ops:
  0.0 17.8 %copy-start = (bf16[1,32,8,1536]{3,2,1,0:T(8,128)(2,1)S(1)}, bf16[1,32,8,1536]{3,2,1,0:T(8,128)(2,1)}, u32[]{:S(2)}) copy-start(bf16[1,32,8,1536]{3,2,1,0:T(8,128)(2,1)} %param.9) | copy-start | bytes 2359300
  1.5 8.0 %collective-permute-start = (bf16[32,1664]{1,0:T(8,128)(2,1)S(1)}, bf16[32,1664]{1,0:T(8,128)(2,1)S(1)}, u32[]{:S(2)}, u32[]{:S(2)}) collective-permute-start(bf16[32,1664]{1,0:T(8,128)(2,1)S(1)} %get-tuple-element.42), channel_id=1, source_target_pairs={{0,6},{2,4},{4,2},{6,0},{8,14},{10,12},{12,10},{14,8},{1,7},{3,5},... | collective-permute-start | bytes 319496 | tf_op jit(solution)/shard_map/ppermute | solution.py:363
  5.5 6.4 %collective-permute-start.1 = (bf16[32,1664]{1,0:T(8,128)(2,1)S(1)}, bf16[32,1664]{1,0:T(8,128)(2,1)S(1)}, u32[]{:S(2)}, u32[]{:S(2)}) collective-permute-start(bf16[32,1664]{1,0:T(8,128)(2,1)S(1)} %get-tuple-element.43), channel_id=1, source_target_pairs={{0,4},{2,6},{4,0},{6,2},{8,12},{10,14},{12,8},{14,10},{1,5},{3,7},... | collective-permute-start | bytes 319496 | tf_op jit(solution)/shard_map/ppermute | solution.py:363
  6.0 7.7 %collective-permute-start.2 = (bf16[32,1664]{1,0:T(8,128)(2,1)S(1)}, bf16[32,1664]{1,0:T(8,128)(2,1)S(1)}, u32[]{:S(2)}, u32[]{:S(2)}) collective-permute-start(bf16[32,1664]{1,0:T(8,128)(2,1)S(1)} %get-tuple-element.44), channel_id=1, source_target_pairs={{0,2},{2,0},{4,6},{6,4},{8,10},{10,8},{12,14},{14,12},{1,3},{3,1},... | collective-permute-start | bytes 319496 | tf_op jit(solution)/shard_map/ppermute | solution.py:363
  6.2 13.1 %collective-permute-start.4 = (bf16[32,1664]{1,0:T(8,128)(2,1)S(1)}, bf16[32,1664]{1,0:T(8,128)(2,1)S(1)}, u32[]{:S(2)}, u32[]{:S(2)}) collective-permute-start(bf16[32,1664]{1,0:T(8,128)(2,1)S(1)} %get-tuple-element.48), channel_id=1, source_target_pairs={{0,6},{2,4},{4,2},{6,0},{8,14},{10,12},{12,10},{14,8},{1,7},{3,5},... | collective-permute-start | bytes 319496 | tf_op jit(solution)/shard_map/ppermute | solution.py:363
  9.0 10.2 %collective-permute-start.5 = (bf16[32,1664]{1,0:T(8,128)(2,1)S(1)}, bf16[32,1664]{1,0:T(8,128)(2,1)S(1)}, u32[]{:S(2)}, u32[]{:S(2)}) collective-permute-start(bf16[32,1664]{1,0:T(8,128)(2,1)S(1)} %get-tuple-element.49), channel_id=1, source_target_pairs={{0,4},{2,6},{4,0},{6,2},{8,12},{10,14},{12,8},{14,10},{1,5},{3,7},... | collective-permute-start | bytes 319496 | tf_op jit(solution)/shard_map/ppermute | solution.py:363
  9.5 9.8 %collective-permute-start.6 = (bf16[32,1664]{1,0:T(8,128)(2,1)S(1)}, bf16[32,1664]{1,0:T(8,128)(2,1)S(1)}, u32[]{:S(2)}, u32[]{:S(2)}) collective-permute-start(bf16[32,1664]{1,0:T(8,128)(2,1)S(1)} %get-tuple-element.50), channel_id=1, source_target_pairs={{0,2},{2,0},{4,6},{6,4},{8,10},{10,8},{12,14},{14,12},{1,3},{3,1},... | collective-permute-start | bytes 319496 | tf_op jit(solution)/shard_map/ppermute | solution.py:363
  14.8 15.0 %collective-permute-start.8 = (bf16[64,1536]{1,0:T(8,128)(2,1)S(1)}, bf16[64,1536]{1,0:T(8,128)(2,1)S(1)}, u32[]{:S(2)}, u32[]{:S(2)}) collective-permute-start(bf16[64,1536]{1,0:T(8,128)(2,1)S(1)} %shard_map.93._), channel_id=1, source_target_pairs={{0,8},{2,10},{4,12},{6,14},{8,0},{10,2},{12,4},{14,6},{1,9},{3,11}... | collective-permute-start | bytes 589832 | tf_op jit(solution)/shard_map/ppermute | solution.py:305
  20.4 13.3 %collective-permute-start.7 = (bf16[64,1536]{1,0:T(8,128)(2,1)S(1)}, bf16[64,1536]{1,0:T(8,128)(2,1)S(1)}, u32[]{:S(2)}, u32[]{:S(2)}) collective-permute-start(bf16[64,1536]{1,0:T(8,128)(2,1)S(1)} %shard_map.96.refs_4_), channel_id=1, source_target_pairs={{0,8},{2,10},{4,12},{6,14},{8,0},{10,2},{12,4},{14,6},{1,9},{3,11}... | collective-permute-start | bytes 589832 | tf_op jit(solution)/shard_map/ppermute | solution.py:305
  20.5 16.4 %collective-permute-start.3 = (bf16[128,1536]{1,0:T(8,128)(2,1)S(1)}, bf16[128,1536]{1,0:T(8,128)(2,1)S(1)}, u32[]{:S(2)}, u32[]{:S(2)}) collective-permute-start(bf16[128,1536]{1,0:T(8,128)(2,1)S(1)} %shard_map.94.refs_4_), channel_id=1, source_target_pairs={{0,16},{16,0},{1,17},{17,1},{2,18},{18,2},{3,19},{19,3},{4,20},{20... | collective-permute-start | bytes 1179656 | tf_op jit(solution)/shard_map/ppermute | solution.py:305
  30.2 6.7 %collective-permute-start.12 = (bf16[32,1536]{1,0:T(8,128)(2,1)S(1)}, bf16[32,1536]{1,0:T(8,128)(2,1)S(1)}, u32[]{:S(2)}, u32[]{:S(2)}) collective-permute-start(bf16[32,1536]{1,0:T(8,128)(2,1)S(1)} %get-tuple-element.62), channel_id=1, source_target_pairs={{0,6},{2,4},{4,2},{6,0},{8,14},{10,12},{12,10},{14,8},{1,7},{3,5},... | collective-permute-start | bytes 294920 | tf_op jit(solution)/shard_map/ppermute | solution.py:363
  31.6 8.6 %collective-permute-start.13 = (bf16[32,1536]{1,0:T(8,128)(2,1)S(1)}, bf16[32,1536]{1,0:T(8,128)(2,1)S(1)}, u32[]{:S(2)}, u32[]{:S(2)}) collective-permute-start(bf16[32,1536]{1,0:T(8,128)(2,1)S(1)} %get-tuple-element.63), channel_id=1, source_target_pairs={{0,4},{2,6},{4,0},{6,2},{8,12},{10,14},{12,8},{14,10},{1,5},{3,7},... | collective-permute-start | bytes 294920 | tf_op jit(solution)/shard_map/ppermute | solution.py:363
  32.9 7.4 %collective-permute-start.14 = (bf16[32,1536]{1,0:T(8,128)(2,1)S(1)}, bf16[32,1536]{1,0:T(8,128)(2,1)S(1)}, u32[]{:S(2)}, u32[]{:S(2)}) collective-permute-start(bf16[32,1536]{1,0:T(8,128)(2,1)S(1)} %get-tuple-element.64), channel_id=1, source_target_pairs={{0,2},{2,0},{4,6},{6,4},{8,10},{10,8},{12,14},{14,12},{1,3},{3,1},... | collective-permute-start | bytes 294920 | tf_op jit(solution)/shard_map/ppermute | solution.py:363
  33.7 4.3 %copy-start.2 = (f32[1536]{0:T(1024)S(1)}, f32[1536]{0:T(1024)}, u32[]{:S(2)}) copy-start(f32[1536]{0:T(1024)} %param.17) | copy-start | bytes 18436
  33.7 4.3 %copy-start.3 = (f32[24]{0:T(128)S(1)}, f32[24]{0:T(128)}, u32[]{:S(2)}) copy-start(f32[24]{0:T(128)} %param.16) | copy-start | bytes 292
  33.7 4.5 %copy-start.1 = (bf16[1,32,8,1536]{3,2,1,0:T(8,128)(2,1)S(1)}, bf16[1,32,8,1536]{3,2,1,0:T(8,128)(2,1)}, u32[]{:S(2)}) copy-start(bf16[1,32,8,1536]{3,2,1,0:T(8,128)(2,1)} %param.10) | copy-start | bytes 2359300
  34.1 7.1 %collective-permute-start.9 = (bf16[32,1536]{1,0:T(8,128)(2,1)S(1)}, bf16[32,1536]{1,0:T(8,128)(2,1)S(1)}, u32[]{:S(2)}, u32[]{:S(2)}) collective-permute-start(bf16[32,1536]{1,0:T(8,128)(2,1)S(1)} %get-tuple-element.59), channel_id=1, source_target_pairs={{0,6},{2,4},{4,2},{6,0},{8,14},{10,12},{12,10},{14,8},{1,7},{3,5},... | collective-permute-start | bytes 294920 | tf_op jit(solution)/shard_map/ppermute | solution.py:363
  36.9 4.6 %collective-permute-start.10 = (bf16[32,1536]{1,0:T(8,128)(2,1)S(1)}, bf16[32,1536]{1,0:T(8,128)(2,1)S(1)}, u32[]{:S(2)}, u32[]{:S(2)}) collective-permute-start(bf16[32,1536]{1,0:T(8,128)(2,1)S(1)} %get-tuple-element.60), channel_id=1, source_target_pairs={{0,4},{2,6},{4,0},{6,2},{8,12},{10,14},{12,8},{14,10},{1,5},{3,7},... | collective-permute-start | bytes 294920 | tf_op jit(solution)/shard_map/ppermute | solution.py:363
  36.9 5.0 %collective-permute-start.11 = (bf16[32,1536]{1,0:T(8,128)(2,1)S(1)}, bf16[32,1536]{1,0:T(8,128)(2,1)S(1)}, u32[]{:S(2)}, u32[]{:S(2)}) collective-permute-start(bf16[32,1536]{1,0:T(8,128)(2,1)S(1)} %get-tuple-element.61), channel_id=1, source_target_pairs={{0,2},{2,0},{4,6},{6,4},{8,10},{10,8},{12,14},{14,12},{1,3},{3,1},... | collective-permute-start | bytes 294920 | tf_op jit(solution)/shard_map/ppermute | solution.py:363

commit v11 on v10

--- a/solution.py
+++ b/solution.py
@@ -98,7 +98,7 @@
 
 
 def partner(member, i, group):
-    return member ^ ((group - i) & (group - 1))
+    return member ^ i
 
 
 def column_order(cols):
@@ -373,10 +373,32 @@
     parts_of = []
     for i, piece in enumerate(pieces):
         places = [rows // cols * state for rows in piece]
+        offsets = [sum(piece[:j]) for j in range(len(piece))]
+
+        def of_own(before, i=i, piece=piece, places=places, offsets=offsets):
+            known = []
+            for offset, rows, count in zip(offsets, piece, places):
+                known.append(
+                    call(
+                        functools.partial(row_local_kernel, offset=offset, **sizes, **shared),
+                        [
+                            pltpu.VMEM((group * rows, channels), F32),
+                            pltpu.VMEM((group * rows, 2 * heads), BF16),
+                            pltpu.VMEM((group * rows, count), BF16),
+                        ],
+                        5,
+                        specs=[None] * (1 + group) + [any_spec],
+                    )(params, *got[i], before)
+                )
+                before = known[-1][1]
+            return known, before
+
+        if i:
+            known, before = of_own(before)
         made = call(
             functools.partial(row_state_kernel, count=len(piece), **sizes, **shared),
             state_shapes(places, col_count // group),
-            0,
+            0 if i else 0,
             specs=[None] * (1 + group) + [any_spec],
         )(params, *got[i], before)
         before = made[0]
@@ -388,13 +410,12 @@
                 specs=[None] * 4 + [any_spec],
             )(params, x, raw, maps, before)
             col_entering = entering_states(col_made[0], col_made[1:], "row", row_count, 1, width)
-            before = col_made[0]
+            known, before = of_own(col_made[0])
         for j, rows in enumerate(piece):
             first = sum(places[:j])
             factor = [f[first : first + places[j]] for f in made[len(piece) :]]
             entering = entering_states(made[j], factor, "col", col_count, group, width)
-            offset = sum(piece[:j])
-            parts_of.append((i, offset, sum(map(sum, pieces[:i])) + offset, rows, entering))
+            parts_of.append((sum(map(sum, pieces[:i])) + offsets[j], rows, known[j], entering))
 
     w, silu = call(
         functools.partial(col_out_kernel, **sizes),
@@ -402,36 +423,20 @@
         0,
     )(params, col_entering, x, raw, maps, gate, jnp.repeat(skip, width).reshape(1, channels))
 
-    local = []
-    for i, offset, _, rows, _ in parts_of:
-        places = rows // cols * state
-        local.append(
-            call(
-                functools.partial(row_local_kernel, offset=offset, **sizes, **shared),
-                [
-                    pltpu.VMEM((group * rows, channels), F32),
-                    pltpu.VMEM((group * rows, 2 * heads), BF16),
-                    pltpu.VMEM((group * rows, places), BF16),
-                ],
-                0,
-                specs=[None] * (1 + group) + [any_spec],
-            )(params, *got[i], before)
-        )
-    before = params
-
     back = []
-    for (_, _, _, rows, entering), known in zip(parts_of, local):
+    before = w
+    for _, rows, known, entering in parts_of:
         y_row = call(
             functools.partial(row_out_kernel, heads=heads, width=width),
             [pltpu.VMEM((rows, channels), BF16)] * group,
-            20 if len(back) == len(parts_of) - 1 else 0,
+            20 if back else 0,
             specs=[None] * 4 + [any_spec],
         )(entering, *known, before)
         back.append(exchange(y_row))
         before = y_row[0]
 
     mixed = None
-    for (_, _, first, rows, _), blocks in zip(parts_of, back):
+    for (first, rows, _, _), blocks in zip(parts_of, back):
         more = [] if mixed is None else [mixed]
         mixed = call(
             functools.partial(final_kernel, offset=first, share=share, **shared),

time: 43 us -> 44.2 us (1.028)
  waiting for transfers between devices: 8.9 us -> 5.52 us
  Pallas kernels: 12.5 us -> 15.1 us
  local copies, waits for them, and re-layouts: 0.17 us -> 2.38 us
  starting transfers between devices: 20.6 us -> 20.1 us
    ppermute x3, waiting for transfers between devices: 5.06 us -> 0.27 us  [entering_states(): entering = lax.ppermute(ends, axis, onward)]
    pallas_call x2, Pallas kernels: 0.69 us -> 2.62 us  [body(): call(functools.partial(row_out_kernel, heads=heads, width=width), [pltpu....]
    ppermute x12, waiting for transfers between devices: 3.84 us -> 5.25 us  [exchange(): lax.ppermute(blocks[i], 'col', [(at, partner(at, i, group)) for at in ran...]
    unnamed x8 -> x20, local copies, waits for them, and re-layouts: 0.01 us -> 0.92 us
    another operation x1, local copies, waits for them, and re-layouts: 0.08 us -> 0.78 us  [body(): jnp.repeat(skip, width).reshape(1, channels)]
    pallas_call x2, Pallas kernels: 2.22 us -> 2.9 us  [body(): call(functools.partial(row_state_kernel, count=len(piece), **sizes, **sha...]
    broadcast_in_dim x1, local copies, waits for them, and re-layouts: 0.07 us -> 0.67 us  [body(): jnp.repeat(skip, width).reshape(1, channels)]
    ppermute x12, starting transfers between devices: 15.7 us -> 15.2 us  [exchange(): lax.ppermute(blocks[i], 'col', [(at, partner(at, i, group)) for at in ran...]
  transfers between devices with their start and end apart: 15 -> 15, of which waited for: 5 -> 5; matrix products, arithmetic and copies ran while one was open for 0% -> 3% of each run, Pallas kernels for 23% -> 29%
where the time goes in v11:
time: 44.2 us; the launch traced here: 44 us
  starting transfers between devices  20.1 us (45%)
  Pallas kernels  15.1 us (34%)
  waiting for transfers between devices  5.52 us (12%)
  local copies, waits for them, and re-layouts  2.38 us (5%)
  between operations  0.87 us (2%)
    ppermute x12, starting transfers between devices, exchange(): lax.ppermute(blocks[i], 'col', [(at, partner(at, i, group)) for at in ran...  15.2 us
    ppermute x12, waiting for transfers between devices, exchange(): lax.ppermute(blocks[i], 'col', [(at, partner(at, i, group)) for at in ran...  5.25 us
    ppermute x3, starting transfers between devices, entering_states(): entering = lax.ppermute(ends, axis, onward)  4.9 us
    pallas_call x2, Pallas kernels, body(): call(functools.partial(row_state_kernel, count=len(piece), **sizes, **sha...  2.9 us
    pallas_call x2, Pallas kernels, body(): call(functools.partial(row_out_kernel, heads=heads, width=width), [pltpu....  2.62 us
    pallas_call x2, Pallas kernels, of_own(): call(functools.partial(row_local_kernel, offset=offset, **sizes, **shared...  2.45 us
    pallas_call x1, Pallas kernels, body(): call(functools.partial(col_out_kernel, **sizes), [pltpu.VMEM((tokens, cha...  2.05 us
    pallas_call x2, Pallas kernels, body(): call(functools.partial(final_kernel, offset=first, share=share, **shared)...  1.92 us
  transfers between devices with their start and end apart: 15, of which 5 were waited for; matrix products, arithmetic and copies ran while one was open for 3% of the time, Pallas kernels for 29%

profile of v11, /device:TPU:0, one launch (start us, length us, event | category | flops | bytes accessed | tf_op | source)
XLA Modules:
  0.0 44.0 jit_solution(12304028282125157952)
XLA Ops:
  0.0 0.0 copy-start
  0.0 1.5 %shard_map.91 = (bf16[256,48]{1,0:T(8,128)(2,1)S(1)}, bf16[256,64]{1,0:T(8,128)(2,1)S(1)}, f32[48,1000]{1,0:T(8,128)S(1)}, f32[2,24]{1,0:T(2,128)S(1)}, bf16[32,...) custom-call(bf16[256,1536]{1,0:T(8,128)(2,1)} %bitcast.6, ...), custom_call_target="tpu_custom_call" | custom-call | flops 1000001024 | bytes 1024 | tf_op jit(solution)/shard_map/pallas_call | solution.py:335
  1.5 3.0 %collective-permute-start = (bf16[32,1664]{1,0:T(8,128)(2,1)S(1)}, bf16[32,1664]{1,0:T(8,128)(2,1)S(1)}, u32[]{:S(2)}, u32[]{:S(2)}) collective-permute-start(bf16[32,1664]{1,0:T(8,128)(2,1)S(1)} %get-tuple-element.42), channel_id=1, source_target_pairs={{0,2},{2,0},{4,6},{6,4},{8,10},{10,8},{12,14},{14,12},{1,3},{3,1},... | collective-permute-start | bytes 319496 | tf_op jit(solution)/shard_map/ppermute | solution.py:363
  4.5 1.6 %collective-permute-start.1 = (bf16[32,1664]{1,0:T(8,128)(2,1)S(1)}, bf16[32,1664]{1,0:T(8,128)(2,1)S(1)}, u32[]{:S(2)}, u32[]{:S(2)}) collective-permute-start(bf16[32,1664]{1,0:T(8,128)(2,1)S(1)} %get-tuple-element.43), channel_id=1, source_target_pairs={{0,4},{2,6},{4,0},{6,2},{8,12},{10,14},{12,8},{14,10},{1,5},{3,7},... | collective-permute-start | bytes 319496 | tf_op jit(solution)/shard_map/ppermute | solution.py:363
  6.1 0.0 collective-permute-start.2
  6.1 1.9 %collective-permute-start.4 = (bf16[32,1664]{1,0:T(8,128)(2,1)S(1)}, bf16[32,1664]{1,0:T(8,128)(2,1)S(1)}, u32[]{:S(2)}, u32[]{:S(2)}) collective-permute-start(bf16[32,1664]{1,0:T(8,128)(2,1)S(1)} %get-tuple-element.48), channel_id=1, source_target_pairs={{0,2},{2,0},{4,6},{6,4},{8,10},{10,8},{12,14},{14,12},{1,3},{3,1},... | collective-permute-start | bytes 319496 | tf_op jit(solution)/shard_map/ppermute | solution.py:363
  8.0 1.6 %collective-permute-start.5 = (bf16[32,1664]{1,0:T(8,128)(2,1)S(1)}, bf16[32,1664]{1,0:T(8,128)(2,1)S(1)}, u32[]{:S(2)}, u32[]{:S(2)}) collective-permute-start(bf16[32,1664]{1,0:T(8,128)(2,1)S(1)} %get-tuple-element.49), channel_id=1, source_target_pairs={{0,4},{2,6},{4,0},{6,2},{8,12},{10,14},{12,8},{14,10},{1,5},{3,7},... | collective-permute-start | bytes 319496 | tf_op jit(solution)/shard_map/ppermute | solution.py:363
  10.2 0.2 shard_map.92.params_ref.refs_4_
  10.4 0.0 collective-permute-done.refs_1_
  10.4 0.0 collective-permute-start.6
  10.4 0.0 collective-permute-done.1.refs_2_
  10.5 2.0 %collective-permute-done.2.refs_3_ = bf16[32,1664]{1,0:T(8,128)(2,1)S(1)} collective-permute-done((bf16[32,1664]{1,0:T(8,128)(2,1)S(1)}, bf16[32,1664]{1,0:T(8,128)(2,1)S(1)}, u32[]{:S(2)}, u32[]{:S(2)}) %collective-permute-start.2) | collective-permute-done | bytes 106528 | tf_op jit(solution)/shard_map/ppermute | solution.py:363
  12.4 1.1 %shard_map.93._ = bf16[64,1536]{1,0:T(8,128)(2,1)S(1)} custom-call(f32[8,48]{1,0:T(8,128)S(1)} %shard_map.92.params_ref.refs_4_, bf16[32,1664]{1,0:T(8,128)(2,1)S(1)} %get-tuple-element.41.refs_0_, bf16[32,1664]{1,0:T(8,128)(2,1)S(1)} %collective-permute-done.refs_1_, bf16[32,1664]{1,0:T(8,128)(2,1)S(1)} %collective-permute-done.1.refs_2_, ...), custom_call_target="tpu_custom_call" | custom-call | flops 1024 | bytes 1024 | tf_op jit(solution)/shard_map/pallas_call | solution.py:398
  13.6 3.0 %collective-permute-start.8 = (bf16[64,1536]{1,0:T(8,128)(2,1)S(1)}, bf16[64,1536]{1,0:T(8,128)(2,1)}, u32[]{:S(2)}, u32[]{:S(2)}) collective-permute-start(bf16[64,1536]{1,0:T(8,128)(2,1)S(1)} %shard_map.93._), channel_id=1, source_target_pairs={{0,8},{2,10},{4,12},{6,14},{8,0},{10,2},{12,4},{14,6},{1,9},{3,11}... | collective-permute-start | bytes 589832 | tf_op jit(solution)/shard_map/ppermute | solution.py:305
  16.6 0.0 copy-done
  16.6 1.5 %shard_map.94.refs_4_ = bf16[128,1536]{1,0:T(8,128)(2,1)S(1)} custom-call(f32[8,48]{1,0:T(8,128)S(1)} %shard_map.92.params_ref.refs_4_, bf16[256,1536]{1,0:T(8,128)(2,1)S(1)} %bitcast.7, bf16[256,48]{1,0:T(8,128)(2,1)S(1)} %get-tuple-element.39.raw_ref, bf16[256,64]{1,0:T(8,128)(2,1)S(1)} %get-tuple-element.40.maps_ref, bf16[64,1536]{1,0:T(8,128)(2,1)S(1)} %shard_map.93._), custom_call_target="tpu_custom_call" | custom-call | flops 1024 | bytes 1024 | tf_op jit(solution)/shard_map/pallas_call | solution.py:406
  18.1 1.6 %collective-permute-start.3 = (bf16[128,1536]{1,0:T(8,128)(2,1)S(1)}, bf16[128,1536]{1,0:T(8,128)(2,1)S(1)}, u32[]{:S(2)}, u32[]{:S(2)}) collective-permute-start(bf16[128,1536]{1,0:T(8,128)(2,1)S(1)} %shard_map.94.refs_4_), channel_id=1, source_target_pairs={{0,16},{16,0},{1,17},{17,1},{2,18},{18,2},{3,19},{19,3},{4,20},{20... | collective-permute-start | bytes 1179656 | tf_op jit(solution)/shard_map/ppermute | solution.py:305
  19.6 1.2 %shard_map.96 = (f32[128,1536]{1,0:T(8,128)S(1)}, bf16[128,48]{1,0:T(8,128)(2,1)S(1)}, bf16[128,64]{1,0:T(8,128)(2,1)S(1)}) custom-call(f32[8,48]{1,0:T(8,128)S(1)} %shard_map.92.params_ref.refs_4_, bf16[32,1664]{1,0:T(8,128)(2,1)S(1)} %get-tuple-element.41.refs_0_, bf16[32,1664]{1,0:T(8,128)(2,1)S(1)} %collective-permute-done.refs_1_, ...), custom_call_target="tpu_custom_call" | custom-call | flops 5000001024 | bytes 1024 | tf_op jit(solution)/shard_map/pallas_call | solution.py:382
  20.8 0.0 collective-permute-done.4.refs_1_
  20.8 0.0 collective-permute-done.5.refs_2_
  20.9 0.0 collective-permute-done.6.refs_3_
  20.9 0.0 copy-start.9
  20.9 0.0 copy-start.1
  20.9 1.2 %shard_map.97 = (f32[128,1536]{1,0:T(8,128)S(1)}, bf16[128,48]{1,0:T(8,128)(2,1)S(1)}, bf16[128,64]{1,0:T(8,128)(2,1)S(1)}) custom-call(f32[8,48]{1,0:T(8,128)S(1)} %shard_map.92.params_ref.refs_4_, bf16[32,1664]{1,0:T(8,128)(2,1)S(1)} %get-tuple-element.47.refs_0_, bf16[32,1664]{1,0:T(8,128)(2,1)S(1)} %collective-permute-done.4.refs_1_, ...), custom_call_target="tpu_custom_call" | custom-call | flops 5000001024 | bytes 1024 | tf_op jit(solution)/shard_map/pallas_call | solution.py:382
  22.1 0.0 copy-start.4
  22.1 0.9 %copy-done.4 = f32[128,1536]{1,0:T(8,128)} copy-done((f32[128,1536]{1,0:T(8,128)}, f32[128,1536]{1,0:T(8,128)S(1)}, u32[]{:S(2)}) %copy-start.4) | copy-done | bytes 786456
  23.0 0.0 copy-start.2
  23.0 0.0 copy-start.6
  23.0 1.8 %shard_map.98 = bf16[64,1536]{1,0:T(8,128)(2,1)} custom-call(f32[8,48]{1,0:T(8,128)S(1)} %shard_map.92.params_ref.refs_4_, bf16[32,1664]{1,0:T(8,128)(2,1)S(1)} %get-tuple-element.47.refs_0_, bf16[32,1664]{1,0:T(8,128)(2,1)S(1)} %collective-permute-done.4.refs_1_, bf16[32,1664]{1,0:T(8,128)(2,1)S(1)} %collective-permute-done.5.refs_2_, ...), custom_call_target="tpu_custom_call" | custom-call | flops 1024 | bytes 1024 | tf_op jit(solution)/shard_map/pallas_call | solution.py:398
  24.8 0.0 copy-done.2
  24.8 0.3 collective-permute-start.7
  25.2 0.0 copy-done.6
  25.2 0.0 copy-done.9
  25.2 0.7 %broadcast_in_dim.3 = f32[24,64]{1,0:T(8,128)} broadcast(f32[24]{0:T(128)S(1)} %copy-done.9), dimensions={0} | broadcast | bytes 6240 | tf_op jit(solution)/shard_map/broadcast_in_dim | solution.py:424
  25.8 0.8 %reshape_reshape.3.skip_ref = f32[1,1536]{1,0:T(1,128)S(1)} reshape(f32[24,64]{1,0:T(8,128)} %broadcast_in_dim.3) | data formatting | bytes 12288 | tf_op jit(solution)/shard_map/reshape;reshape | solution.py:424
  26.6 0.0 collective-permute-done.3.s_ref
  26.6 0.0 copy-done.1
  26.6 2.1 %shard_map.95 = (f32[256,1536]{1,0:T(8,128)S(1)}, f32[256,1536]{1,0:T(8,128)S(1)}) custom-call(f32[8,48]{1,0:T(8,128)S(1)} %shard_map.92.params_ref.refs_4_, bf16[128,1536]{1,0:T(8,128)(2,1)S(1)} %collective-permute-done.3.s_ref, bf16[256,1536]{1,0:T(8,128)(2,1)S(1)} %bitcast.8, bf16[256,48]{1,0:T(8,128)(2,1)S(1)} %get-tuple-element.39.raw_ref, ...), custom_call_target="tpu_custom_call" | custom-call | flops 1024 | bytes 1024 | tf_op jit(solution)/shard_map/pallas_call | solution.py:420
  28.7 0.0 copy-start.3
  28.7 0.0 copy-start.5
  28.7 0.0 copy-start.7
  28.7 0.0 collective-permute-done.8.s_ref
  28.7 1.3 %shard_map.99 = (bf16[32,1536]{1,0:T(8,128)(2,1)S(1)}, bf16[32,1536]{1,0:T(8,128)(2,1)S(1)}, bf16[32,1536]{1,0:T(8,128)(2,1)S(1)}, bf16[32,1536]{1,0:T(8,128)(2,1)S(1)}) custom-call(bf16[64,1536]{1,0:T(8,128)(2,1)} %collective-permute-done.8.s_ref, f32[128,1536]{1,0:T(8,128)S(1)} %get-tuple-element.55.y_ref, ...), custom_call_target="tpu_custom_call" | custom-call | flops 1024 | bytes 1024 | tf_op jit(solution)/shard_map/pallas_call | solution.py:429
  30.1 1.4 %collective-permute-start.12 = (bf16[32,1536]{1,0:T(8,128)(2,1)S(1)}, bf16[32,1536]{1,0:T(8,128)(2,1)S(1)}, u32[]{:S(2)}, u32[]{:S(2)}) collective-permute-start(bf16[32,1536]{1,0:T(8,128)(2,1)S(1)} %get-tuple-element.62), channel_id=1, source_target_pairs={{0,2},{2,0},{4,6},{6,4},{8,10},{10,8},{12,14},{14,12},{1,3},{3,1},... | collective-permute-start | bytes 294920 | tf_op jit(solution)/shard_map/ppermute | solution.py:363
  31.4 1.6 %collective-permute-start.13 = (bf16[32,1536]{1,0:T(8,128)(2,1)S(1)}, bf16[32,1536]{1,0:T(8,128)(2,1)S(1)}, u32[]{:S(2)}, u32[]{:S(2)}) collective-permute-start(bf16[32,1536]{1,0:T(8,128)(2,1)S(1)} %get-tuple-element.63), channel_id=1, source_target_pairs={{0,4},{2,6},{4,0},{6,2},{8,12},{10,14},{12,8},{14,10},{1,5},{3,7},... | collective-permute-start | bytes 294920 | tf_op jit(solution)/shard_map/ppermute | solution.py:363
  33.1 0.6 %collective-permute-start.14 = (bf16[32,1536]{1,0:T(8,128)(2,1)S(1)}, bf16[32,1536]{1,0:T(8,128)(2,1)S(1)}, u32[]{:S(2)}, u32[]{:S(2)}) collective-permute-start(bf16[32,1536]{1,0:T(8,128)(2,1)S(1)} %get-tuple-element.64), channel_id=1, source_target_pairs={{0,6},{2,4},{4,2},{6,0},{8,14},{10,12},{12,10},{14,8},{1,7},{3,5},... | collective-permute-start | bytes 294920 | tf_op jit(solution)/shard_map/ppermute | solution.py:363
  33.6 0.3 collective-permute-done.7.s_ref
  33.9 0.0 copy-done.3
  33.9 0.0 copy-done.5
  33.9 0.0 copy-done.7
  33.9 0.0 copy-start.8
  33.9 1.3 %shard_map.100 = (bf16[32,1536]{1,0:T(8,128)(2,1)S(1)}, bf16[32,1536]{1,0:T(8,128)(2,1)S(1)}, bf16[32,1536]{1,0:T(8,128)(2,1)S(1)}, bf16[32,1536]{1,0:T(8,128)(2,1)S(1)}) custom-call(bf16[64,1536]{1,0:T(8,128)(2,1)} %collective-permute-done.7.s_ref, f32[128,1536]{1,0:T(8,128)S(1)} %copy-done.5, bf16[128,48]{1,0:T(8,128)(2,1)S(1)} %copy-done.3, ...), custom_call_target="tpu_custom_call" | custom-call | flops 20000002048 | bytes 1024 | tf_op jit(solution)/shard_map/pallas_call | solution.py:429
  35.2 1.2 %collective-permute-start.10 = (bf16[32,1536]{1,0:T(8,128)(2,1)S(1)}, bf16[32,1536]{1,0:T(8,128)(2,1)S(1)}, u32[]{:S(2)}, u32[]{:S(2)}) collective-permute-start(bf16[32,1536]{1,0:T(8,128)(2,1)S(1)} %get-tuple-element.60), channel_id=1, source_target_pairs={{0,4},{2,6},{4,0},{6,2},{8,12},{10,14},{12,8},{14,10},{1,5},{3,7},... | collective-permute-start | bytes 294920 | tf_op jit(solution)/shard_map/ppermute | solution.py:363
  36.4 1.6 %collective-permute-start.11 = (bf16[32,1536]{1,0:T(8,128)(2,1)S(1)}, bf16[32,1536]{1,0:T(8,128)(2,1)S(1)}, u32[]{:S(2)}, u32[]{:S(2)}) collective-permute-start(bf16[32,1536]{1,0:T(8,128)(2,1)S(1)} %get-tuple-element.61), channel_id=1, source_target_pairs={{0,6},{2,4},{4,2},{6,0},{8,14},{10,12},{12,10},{14,8},{1,7},{3,5},... | collective-permute-start | bytes 294920 | tf_op jit(solution)/shard_map/ppermute | solution.py:363
  38.1 0.0 collective-permute-done.12.refs_1_
  38.1 0.7 %collective-permute-start.9 = (bf16[32,1536]{1,0:T(8,128)(2,1)S(1)}, bf16[32,1536]{1,0:T(8,128)(2,1)S(1)}, u32[]{:S(2)}, u32[]{:S(2)}) collective-permute-start(bf16[32,1536]{1,0:T(8,128)(2,1)S(1)} %get-tuple-element.59), channel_id=1, source_target_pairs={{0,2},{2,0},{4,6},{6,4},{8,10},{10,8},{12,14},{14,12},{1,3},{3,1},... | collective-permute-start | bytes 294920 | tf_op jit(solution)/shard_map/ppermute | solution.py:363
  38.8 0.0 copy-done.8
  38.8 0.0 collective-permute-done.13.refs_2_
  38.8 0.0 collective-permute-done.14.refs_3_
  38.8 1.0 %shard_map.101.refs_4_ = bf16[256,1536]{1,0:T(8,128)(2,1)} custom-call(f32[256,1536]{1,0:T(8,128)S(1)} %get-tuple-element.45._.w_ref, f32[256,1536]{1,0:T(8,128)S(1)} %get-tuple-element.46.g_ref, f32[1,1536]{1,0:T(1,128)S(1)} %reshape.23.gain_ref, bf16[32,1536]{1,0:T(8,128)(2,1)S(1)} %get-tuple-element.57._.refs_0_, ...), custom_call_target="tpu_custom_call" | custom-call | flops 1024 | bytes 1024 | tf_op jit(solution)/shard_map/pallas_call | solution.py:441
  39.8 0.1 collective-permute-done.10.refs_2_
  39.9 2.1 %collective-permute-done.11.refs_3_ = bf16[32,1536]{1,0:T(8,128)(2,1)S(1)} collective-permute-done((bf16[32,1536]{1,0:T(8,128)(2,1)S(1)}, bf16[32,1536]{1,0:T(8,128)(2,1)S(1)}, u32[]{:S(2)}, u32[]{:S(2)}) %collective-permute-start.11) | collective-permute-done | bytes 98336 | tf_op jit(solution)/shard_map/ppermute | solution.py:363
  42.0 1.0 %collective-permute-done.9.refs_1_ = bf16[32,1536]{1,0:T(8,128)(2,1)S(1)} collective-permute-done((bf16[32,1536]{1,0:T(8,128)(2,1)S(1)}, bf16[32,1536]{1,0:T(8,128)(2,1)S(1)}, u32[]{:S(2)}, u32[]{:S(2)}) %collective-permute-start.9) | collective-permute-done | bytes 98336 | tf_op jit(solution)/shard_map/ppermute | solution.py:363
  43.0 1.0 %shard_map.102 = bf16[256,1536]{1,0:T(8,128)(2,1)} custom-call(f32[256,1536]{1,0:T(8,128)S(1)} %get-tuple-element.45._.w_ref, f32[256,1536]{1,0:T(8,128)S(1)} %get-tuple-element.46.g_ref, f32[1,1536]{1,0:T(1,128)S(1)} %reshape.23.gain_ref, bf16[32,1536]{1,0:T(8,128)(2,1)S(1)} %get-tuple-element.58.refs_0_, ...), custom_call_target="tpu_custom_call", output_to_operand_aliasing={{}: (7, {})} | custom-call | flops 1024 | bytes 1024 | tf_op jit(solution)/shard_map/pallas_call | solution.py:441
  (1 shorter events, 0.0 us)
Async XLA Ops:
  0.0 16.6 %copy-start = (bf16[1,32,8,1536]{3,2,1,0:T(8,128)(2,1)S(1)}, bf16[1,32,8,1536]{3,2,1,0:T(8,128)(2,1)}, u32[]{:S(2)}) copy-start(bf16[1,32,8,1536]{3,2,1,0:T(8,128)(2,1)} %param.9) | copy-start | bytes 2359300
  1.5 8.9 %collective-permute-start = (bf16[32,1664]{1,0:T(8,128)(2,1)S(1)}, bf16[32,1664]{1,0:T(8,128)(2,1)S(1)}, u32[]{:S(2)}, u32[]{:S(2)}) collective-permute-start(bf16[32,1664]{1,0:T(8,128)(2,1)S(1)} %get-tuple-element.42), channel_id=1, source_target_pairs={{0,2},{2,0},{4,6},{6,4},{8,10},{10,8},{12,14},{14,12},{1,3},{3,1},... | collective-permute-start | bytes 319496 | tf_op jit(solution)/shard_map/ppermute | solution.py:363
  4.5 5.9 %collective-permute-start.1 = (bf16[32,1664]{1,0:T(8,128)(2,1)S(1)}, bf16[32,1664]{1,0:T(8,128)(2,1)S(1)}, u32[]{:S(2)}, u32[]{:S(2)}) collective-permute-start(bf16[32,1664]{1,0:T(8,128)(2,1)S(1)} %get-tuple-element.43), channel_id=1, source_target_pairs={{0,4},{2,6},{4,0},{6,2},{8,12},{10,14},{12,8},{14,10},{1,5},{3,7},... | collective-permute-start | bytes 319496 | tf_op jit(solution)/shard_map/ppermute | solution.py:363
  6.1 6.3 %collective-permute-start.2 = (bf16[32,1664]{1,0:T(8,128)(2,1)S(1)}, bf16[32,1664]{1,0:T(8,128)(2,1)S(1)}, u32[]{:S(2)}, u32[]{:S(2)}) collective-permute-start(bf16[32,1664]{1,0:T(8,128)(2,1)S(1)} %get-tuple-element.44), channel_id=1, source_target_pairs={{0,6},{2,4},{4,2},{6,0},{8,14},{10,12},{12,10},{14,8},{1,7},{3,5},... | collective-permute-start | bytes 319496 | tf_op jit(solution)/shard_map/ppermute | solution.py:363
  6.1 14.7 %collective-permute-start.4 = (bf16[32,1664]{1,0:T(8,128)(2,1)S(1)}, bf16[32,1664]{1,0:T(8,128)(2,1)S(1)}, u32[]{:S(2)}, u32[]{:S(2)}) collective-permute-start(bf16[32,1664]{1,0:T(8,128)(2,1)S(1)} %get-tuple-element.48), channel_id=1, source_target_pairs={{0,2},{2,0},{4,6},{6,4},{8,10},{10,8},{12,14},{14,12},{1,3},{3,1},... | collective-permute-start | bytes 319496 | tf_op jit(solution)/shard_map/ppermute | solution.py:363
  8.0 12.8 %collective-permute-start.5 = (bf16[32,1664]{1,0:T(8,128)(2,1)S(1)}, bf16[32,1664]{1,0:T(8,128)(2,1)S(1)}, u32[]{:S(2)}, u32[]{:S(2)}) collective-permute-start(bf16[32,1664]{1,0:T(8,128)(2,1)S(1)} %get-tuple-element.49), channel_id=1, source_target_pairs={{0,4},{2,6},{4,0},{6,2},{8,12},{10,14},{12,8},{14,10},{1,5},{3,7},... | collective-permute-start | bytes 319496 | tf_op jit(solution)/shard_map/ppermute | solution.py:363
  10.4 10.4 %collective-permute-start.6 = (bf16[32,1664]{1,0:T(8,128)(2,1)S(1)}, bf16[32,1664]{1,0:T(8,128)(2,1)S(1)}, u32[]{:S(2)}, u32[]{:S(2)}) collective-permute-start(bf16[32,1664]{1,0:T(8,128)(2,1)S(1)} %get-tuple-element.50), channel_id=1, source_target_pairs={{0,6},{2,4},{4,2},{6,0},{8,14},{10,12},{12,10},{14,8},{1,7},{3,5},... | collective-permute-start | bytes 319496 | tf_op jit(solution)/shard_map/ppermute | solution.py:363
  13.6 15.2 %collective-permute-start.8 = (bf16[64,1536]{1,0:T(8,128)(2,1)S(1)}, bf16[64,1536]{1,0:T(8,128)(2,1)}, u32[]{:S(2)}, u32[]{:S(2)}) collective-permute-start(bf16[64,1536]{1,0:T(8,128)(2,1)S(1)} %shard_map.93._), channel_id=1, source_target_pairs={{0,8},{2,10},{4,12},{6,14},{8,0},{10,2},{12,4},{14,6},{1,9},{3,11}... | collective-permute-start | bytes 589832 | tf_op jit(solution)/shard_map/ppermute | solution.py:305
  18.1 8.6 %collective-permute-start.3 = (bf16[128,1536]{1,0:T(8,128)(2,1)S(1)}, bf16[128,1536]{1,0:T(8,128)(2,1)S(1)}, u32[]{:S(2)}, u32[]{:S(2)}) collective-permute-start(bf16[128,1536]{1,0:T(8,128)(2,1)S(1)} %shard_map.94.refs_4_), channel_id=1, source_target_pairs={{0,16},{16,0},{1,17},{17,1},{2,18},{18,2},{3,19},{19,3},{4,20},{20... | collective-permute-start | bytes 1179656 | tf_op jit(solution)/shard_map/ppermute | solution.py:305
  20.9 4.3 %copy-start.9 = (f32[24]{0:T(128)S(1)}, f32[24]{0:T(128)}, u32[]{:S(2)}) copy-start(f32[24]{0:T(128)} %param.16) | copy-start | bytes 292
  20.9 5.7 %copy-start.1 = (bf16[1,32,8,1536]{3,2,1,0:T(8,128)(2,1)S(1)}, bf16[1,32,8,1536]{3,2,1,0:T(8,128)(2,1)}, u32[]{:S(2)}) copy-start(bf16[1,32,8,1536]{3,2,1,0:T(8,128)(2,1)} %param.10) | copy-start | bytes 2359300
  22.1 0.9 %copy-start.4 = (f32[128,1536]{1,0:T(8,128)}, f32[128,1536]{1,0:T(8,128)S(1)}, u32[]{:S(2)}) copy-start(f32[128,1536]{1,0:T(8,128)S(1)} %get-tuple-element.53.y_ref) | copy-start | bytes 2359300
  23.0 1.8 %copy-start.2 = (bf16[128,48]{1,0:T(8,128)(2,1)}, bf16[128,48]{1,0:T(8,128)(2,1)S(1)}, u32[]{:S(2)}) copy-start(bf16[128,48]{1,0:T(8,128)(2,1)S(1)} %get-tuple-element.52.refs_4_.fade_ref) | copy-start | bytes 36868
  23.0 2.1 %copy-start.6 = (bf16[128,64]{1,0:T(8,128)(2,1)}, bf16[128,64]{1,0:T(8,128)(2,1)S(1)}, u32[]{:S(2)}) copy-start(bf16[128,64]{1,0:T(8,128)(2,1)S(1)} %get-tuple-element.54.entry_ref) | copy-start | bytes 49156
  24.8 9.1 %collective-permute-start.7 = (bf16[64,1536]{1,0:T(8,128)(2,1)}, bf16[64,1536]{1,0:T(8,128)(2,1)}, u32[]{:S(2)}, u32[]{:S(2)}) collective-permute-start(bf16[64,1536]{1,0:T(8,128)(2,1)} %shard_map.98), channel_id=1, source_target_pairs={{0,8},{2,10},{4,12},{6,14},{8,0},{10,2},{12,4},{14,6},{1,9},{3,11}... | collective-permute-start | bytes 589832 | tf_op jit(solution)/shard_map/ppermute | solution.py:305
  28.7 5.2 %copy-start.3 = (bf16[128,48]{1,0:T(8,128)(2,1)S(1)}, bf16[128,48]{1,0:T(8,128)(2,1)}, u32[]{:S(2)}) copy-start(bf16[128,48]{1,0:T(8,128)(2,1)} %copy-done.2) | copy-start | bytes 36868
  28.7 5.2 %copy-start.5 = (f32[128,1536]{1,0:T(8,128)S(1)}, f32[128,1536]{1,0:T(8,128)}, u32[]{:S(2)}) copy-start(f32[128,1536]{1,0:T(8,128)} %copy-done.4) | copy-start | bytes 2359300
  28.7 5.2 %copy-start.7 = (bf16[128,64]{1,0:T(8,128)(2,1)S(1)}, bf16[128,64]{1,0:T(8,128)(2,1)}, u32[]{:S(2)}) copy-start(bf16[128,64]{1,0:T(8,128)(2,1)} %copy-done.6) | copy-start | bytes 49156
  30.1 8.0 %collective-permute-start.12 = (bf16[32,1536]{1,0:T(8,128)(2,1)S(1)}, bf16[32,1536]{1,0:T(8,128)(2,1)S(1)}, u32[]{:S(2)}, u32[]{:S(2)}) collective-permute-start(bf16[32,1536]{1,0:T(8,128)(2,1)S(1)} %get-tuple-element.62), channel_id=1, source_target_pairs={{0,2},{2,0},{4,6},{6,4},{8,10},{10,8},{12,14},{14,12},{1,3},{3,1},... | collective-permute-start | bytes 294920 | tf_op jit(solution)/shard_map/ppermute | solution.py:363
  31.4 7.3 %collective-permute-start.13 = (bf16[32,1536]{1,0:T(8,128)(2,1)S(1)}, bf16[32,1536]{1,0:T(8,128)(2,1)S(1)}, u32[]{:S(2)}, u32[]{:S(2)}) collective-permute-start(bf16[32,1536]{1,0:T(8,128)(2,1)S(1)} %get-tuple-element.63), channel_id=1, source_target_pairs={{0,4},{2,6},{4,0},{6,2},{8,12},{10,14},{12,8},{14,10},{1,5},{3,7},... | collective-permute-start | bytes 294920 | tf_op jit(solution)/shard_map/ppermute | solution.py:363
  33.1 5.7 %collective-permute-start.14 = (bf16[32,1536]{1,0:T(8,128)(2,1)S(1)}, bf16[32,1536]{1,0:T(8,128)(2,1)S(1)}, u32[]{:S(2)}, u32[]{:S(2)}) collective-permute-start(bf16[32,1536]{1,0:T(8,128)(2,1)S(1)} %get-tuple-element.64), channel_id=1, source_target_pairs={{0,6},{2,4},{4,2},{6,0},{8,14},{10,12},{12,10},{14,8},{1,7},{3,5},... | collective-permute-start | bytes 294920 | tf_op jit(solution)/shard_map/ppermute | solution.py:363
  33.9 4.9 %copy-start.8 = (f32[1536]{0:T(1024)S(1)}, f32[1536]{0:T(1024)}, u32[]{:S(2)}) copy-start(f32[1536]{0:T(1024)} %param.17) | copy-start | bytes 18436
  35.2 4.7 %collective-permute-start.10 = (bf16[32,1536]{1,0:T(8,128)(2,1)S(1)}, bf16[32,1536]{1,0:T(8,128)(2,1)S(1)}, u32[]{:S(2)}, u32[]{:S(2)}) collective-permute-start(bf16[32,1536]{1,0:T(8,128)(2,1)S(1)} %get-tuple-element.60), channel_id=1, source_target_pairs={{0,4},{2,6},{4,0},{6,2},{8,12},{10,14},{12,8},{14,10},{1,5},{3,7},... | collective-permute-start | bytes 294920 | tf_op jit(solution)/shard_map/ppermute | solution.py:363
  36.4 5.5 %collective-permute-start.11 = (bf16[32,1536]{1,0:T(8,128)(2,1)S(1)}, bf16[32,1536]{1,0:T(8,128)(2,1)S(1)}, u32[]{:S(2)}, u32[]{:S(2)}) collective-permute-start(bf16[32,1536]{1,0:T(8,128)(2,1)S(1)} %get-tuple-element.61), channel_id=1, source_target_pairs={{0,6},{2,4},{4,2},{6,0},{8,14},{10,12},{12,10},{14,8},{1,7},{3,5},... | collective-permute-start | bytes 294920 | tf_op jit(solution)/shard_map/ppermute | solution.py:363
  38.1 4.9 %collective-permute-start.9 = (bf16[32,1536]{1,0:T(8,128)(2,1)S(1)}, bf16[32,1536]{1,0:T(8,128)(2,1)S(1)}, u32[]{:S(2)}, u32[]{:S(2)}) collective-permute-start(bf16[32,1536]{1,0:T(8,128)(2,1)S(1)} %get-tuple-element.59), channel_id=1, source_target_pairs={{0,2},{2,0},{4,6},{6,4},{8,10},{10,8},{12,14},{14,12},{1,3},{3,1},... | collective-permute-start | bytes 294920 | tf_op jit(solution)/shard_map/ppermute | solution.py:363

commit v12 on v11

--- a/solution.py
+++ b/solution.py
@@ -11,7 +11,7 @@
 GROUP = 4
 PIECES = ((4,), (4,))
 STRIP = 512
-VMEM_LIMIT = 24 * 1024 * 1024
+VMEM_LIMIT = 16 * 1024 * 1024
 F32 = jnp.float32
 BF16 = jnp.bfloat16
 
@@ -386,7 +386,7 @@
                             pltpu.VMEM((group * rows, 2 * heads), BF16),
                             pltpu.VMEM((group * rows, count), BF16),
                         ],
-                        5,
+                        2,
                         specs=[None] * (1 + group) + [any_spec],
                     )(params, *got[i], before)
                 )

time: 44.2 us -> 44.2 us (level)
  no operation moved by 1% of the time
where the time goes in v12:
time: 44.2 us; the launch traced here: 44 us
  starting transfers between devices  20.1 us (45%)
  Pallas kernels  15.1 us (34%)
  waiting for transfers between devices  5.52 us (12%)
  local copies, waits for them, and re-layouts  2.38 us (5%)
  between operations  0.87 us (2%)
    ppermute x12, starting transfers between devices, exchange(): lax.ppermute(blocks[i], 'col', [(at, partner(at, i, group)) for at in ran...  15.2 us
    ppermute x12, waiting for transfers between devices, exchange(): lax.ppermute(blocks[i], 'col', [(at, partner(at, i, group)) for at in ran...  5.25 us
    ppermute x3, starting transfers between devices, entering_states(): entering = lax.ppermute(ends, axis, onward)  4.9 us
    pallas_call x2, Pallas kernels, body(): call(functools.partial(row_state_kernel, count=len(piece), **sizes, **sha...  2.9 us
    pallas_call x2, Pallas kernels, body(): call(functools.partial(row_out_kernel, heads=heads, width=width), [pltpu....  2.62 us
    pallas_call x2, Pallas kernels, of_own(): call(functools.partial(row_local_kernel, offset=offset, **sizes, **shared...  2.45 us
    pallas_call x1, Pallas kernels, body(): call(functools.partial(col_out_kernel, **sizes), [pltpu.VMEM((tokens, cha...  2.05 us
    pallas_call x2, Pallas kernels, body(): call(functools.partial(final_kernel, offset=first, share=share, **shared)...  1.92 us
  transfers between devices with their start and end apart: 15, of which 5 were waited for; matrix products, arithmetic and copies ran while one was open for 3% of the time, Pallas kernels for 29%

profile of v12, /device:TPU:0, one launch (start us, length us, event | category | flops | bytes accessed | tf_op | source)
XLA Modules:
  0.0 44.0 jit_solution(17609843913620549041)
XLA Ops:
  0.0 0.0 copy-start
  0.0 1.5 %shard_map.91 = (bf16[256,48]{1,0:T(8,128)(2,1)S(1)}, bf16[256,64]{1,0:T(8,128)(2,1)S(1)}, f32[48,1000]{1,0:T(8,128)S(1)}, f32[2,24]{1,0:T(2,128)S(1)}, bf16[32,...) custom-call(bf16[256,1536]{1,0:T(8,128)(2,1)} %bitcast.6, ...), custom_call_target="tpu_custom_call" | custom-call | flops 1000001024 | bytes 1024 | tf_op jit(solution)/shard_map/pallas_call | solution.py:335
  1.5 3.0 %collective-permute-start = (bf16[32,1664]{1,0:T(8,128)(2,1)S(1)}, bf16[32,1664]{1,0:T(8,128)(2,1)S(1)}, u32[]{:S(2)}, u32[]{:S(2)}) collective-permute-start(bf16[32,1664]{1,0:T(8,128)(2,1)S(1)} %get-tuple-element.42), channel_id=1, source_target_pairs={{0,2},{2,0},{4,6},{6,4},{8,10},{10,8},{12,14},{14,12},{1,3},{3,1},... | collective-permute-start | bytes 319496 | tf_op jit(solution)/shard_map/ppermute | solution.py:363
  4.5 1.6 %collective-permute-start.1 = (bf16[32,1664]{1,0:T(8,128)(2,1)S(1)}, bf16[32,1664]{1,0:T(8,128)(2,1)S(1)}, u32[]{:S(2)}, u32[]{:S(2)}) collective-permute-start(bf16[32,1664]{1,0:T(8,128)(2,1)S(1)} %get-tuple-element.43), channel_id=1, source_target_pairs={{0,4},{2,6},{4,0},{6,2},{8,12},{10,14},{12,8},{14,10},{1,5},{3,7},... | collective-permute-start | bytes 319496 | tf_op jit(solution)/shard_map/ppermute | solution.py:363
  6.1 0.0 collective-permute-start.2
  6.1 1.9 %collective-permute-start.4 = (bf16[32,1664]{1,0:T(8,128)(2,1)S(1)}, bf16[32,1664]{1,0:T(8,128)(2,1)S(1)}, u32[]{:S(2)}, u32[]{:S(2)}) collective-permute-start(bf16[32,1664]{1,0:T(8,128)(2,1)S(1)} %get-tuple-element.48), channel_id=1, source_target_pairs={{0,2},{2,0},{4,6},{6,4},{8,10},{10,8},{12,14},{14,12},{1,3},{3,1},... | collective-permute-start | bytes 319496 | tf_op jit(solution)/shard_map/ppermute | solution.py:363
  8.0 1.6 %collective-permute-start.5 = (bf16[32,1664]{1,0:T(8,128)(2,1)S(1)}, bf16[32,1664]{1,0:T(8,128)(2,1)S(1)}, u32[]{:S(2)}, u32[]{:S(2)}) collective-permute-start(bf16[32,1664]{1,0:T(8,128)(2,1)S(1)} %get-tuple-element.49), channel_id=1, source_target_pairs={{0,4},{2,6},{4,0},{6,2},{8,12},{10,14},{12,8},{14,10},{1,5},{3,7},... | collective-permute-start | bytes 319496 | tf_op jit(solution)/shard_map/ppermute | solution.py:363
  10.2 0.2 shard_map.92.params_ref.refs_4_
  10.4 0.0 collective-permute-done.refs_1_
  10.4 0.0 collective-permute-start.6
  10.4 0.0 collective-permute-done.1.refs_2_
  10.5 2.0 %collective-permute-done.2.refs_3_ = bf16[32,1664]{1,0:T(8,128)(2,1)S(1)} collective-permute-done((bf16[32,1664]{1,0:T(8,128)(2,1)S(1)}, bf16[32,1664]{1,0:T(8,128)(2,1)S(1)}, u32[]{:S(2)}, u32[]{:S(2)}) %collective-permute-start.2) | collective-permute-done | bytes 106528 | tf_op jit(solution)/shard_map/ppermute | solution.py:363
  12.4 1.1 %shard_map.93._ = bf16[64,1536]{1,0:T(8,128)(2,1)S(1)} custom-call(f32[8,48]{1,0:T(8,128)S(1)} %shard_map.92.params_ref.refs_4_, bf16[32,1664]{1,0:T(8,128)(2,1)S(1)} %get-tuple-element.41.refs_0_, bf16[32,1664]{1,0:T(8,128)(2,1)S(1)} %collective-permute-done.refs_1_, bf16[32,1664]{1,0:T(8,128)(2,1)S(1)} %collective-permute-done.1.refs_2_, ...), custom_call_target="tpu_custom_call" | custom-call | flops 1024 | bytes 1024 | tf_op jit(solution)/shard_map/pallas_call | solution.py:398
  13.6 3.0 %collective-permute-start.8 = (bf16[64,1536]{1,0:T(8,128)(2,1)S(1)}, bf16[64,1536]{1,0:T(8,128)(2,1)}, u32[]{:S(2)}, u32[]{:S(2)}) collective-permute-start(bf16[64,1536]{1,0:T(8,128)(2,1)S(1)} %shard_map.93._), channel_id=1, source_target_pairs={{0,8},{2,10},{4,12},{6,14},{8,0},{10,2},{12,4},{14,6},{1,9},{3,11}... | collective-permute-start | bytes 589832 | tf_op jit(solution)/shard_map/ppermute | solution.py:305
  16.6 0.0 copy-done
  16.6 1.5 %shard_map.94.refs_4_ = bf16[128,1536]{1,0:T(8,128)(2,1)S(1)} custom-call(f32[8,48]{1,0:T(8,128)S(1)} %shard_map.92.params_ref.refs_4_, bf16[256,1536]{1,0:T(8,128)(2,1)S(1)} %bitcast.7, bf16[256,48]{1,0:T(8,128)(2,1)S(1)} %get-tuple-element.39.raw_ref, bf16[256,64]{1,0:T(8,128)(2,1)S(1)} %get-tuple-element.40.maps_ref, bf16[64,1536]{1,0:T(8,128)(2,1)S(1)} %shard_map.93._), custom_call_target="tpu_custom_call" | custom-call | flops 1024 | bytes 1024 | tf_op jit(solution)/shard_map/pallas_call | solution.py:406
  18.1 1.6 %collective-permute-start.3 = (bf16[128,1536]{1,0:T(8,128)(2,1)S(1)}, bf16[128,1536]{1,0:T(8,128)(2,1)S(1)}, u32[]{:S(2)}, u32[]{:S(2)}) collective-permute-start(bf16[128,1536]{1,0:T(8,128)(2,1)S(1)} %shard_map.94.refs_4_), channel_id=1, source_target_pairs={{0,16},{16,0},{1,17},{17,1},{2,18},{18,2},{3,19},{19,3},{4,20},{20... | collective-permute-start | bytes 1179656 | tf_op jit(solution)/shard_map/ppermute | solution.py:305
  19.6 1.2 %shard_map.96 = (f32[128,1536]{1,0:T(8,128)S(1)}, bf16[128,48]{1,0:T(8,128)(2,1)S(1)}, bf16[128,64]{1,0:T(8,128)(2,1)S(1)}) custom-call(f32[8,48]{1,0:T(8,128)S(1)} %shard_map.92.params_ref.refs_4_, bf16[32,1664]{1,0:T(8,128)(2,1)S(1)} %get-tuple-element.41.refs_0_, bf16[32,1664]{1,0:T(8,128)(2,1)S(1)} %collective-permute-done.refs_1_, ...), custom_call_target="tpu_custom_call" | custom-call | flops 2000001024 | bytes 1024 | tf_op jit(solution)/shard_map/pallas_call | solution.py:382
  20.8 0.0 collective-permute-done.4.refs_1_
  20.8 0.0 collective-permute-done.5.refs_2_
  20.9 0.0 collective-permute-done.6.refs_3_
  20.9 0.0 copy-start.9
  20.9 0.0 copy-start.1
  20.9 1.2 %shard_map.97 = (f32[128,1536]{1,0:T(8,128)S(1)}, bf16[128,48]{1,0:T(8,128)(2,1)S(1)}, bf16[128,64]{1,0:T(8,128)(2,1)S(1)}) custom-call(f32[8,48]{1,0:T(8,128)S(1)} %shard_map.92.params_ref.refs_4_, bf16[32,1664]{1,0:T(8,128)(2,1)S(1)} %get-tuple-element.47.refs_0_, bf16[32,1664]{1,0:T(8,128)(2,1)S(1)} %collective-permute-done.4.refs_1_, ...), custom_call_target="tpu_custom_call" | custom-call | flops 2000001024 | bytes 1024 | tf_op jit(solution)/shard_map/pallas_call | solution.py:382
  22.1 0.0 copy-start.4
  22.1 0.9 %copy-done.4 = f32[128,1536]{1,0:T(8,128)} copy-done((f32[128,1536]{1,0:T(8,128)}, f32[128,1536]{1,0:T(8,128)S(1)}, u32[]{:S(2)}) %copy-start.4) | copy-done | bytes 786456
  23.0 0.0 copy-start.2
  23.0 0.0 copy-start.6
  23.0 1.8 %shard_map.98 = bf16[64,1536]{1,0:T(8,128)(2,1)} custom-call(f32[8,48]{1,0:T(8,128)S(1)} %shard_map.92.params_ref.refs_4_, bf16[32,1664]{1,0:T(8,128)(2,1)S(1)} %get-tuple-element.47.refs_0_, bf16[32,1664]{1,0:T(8,128)(2,1)S(1)} %collective-permute-done.4.refs_1_, bf16[32,1664]{1,0:T(8,128)(2,1)S(1)} %collective-permute-done.5.refs_2_, ...), custom_call_target="tpu_custom_call" | custom-call | flops 1024 | bytes 1024 | tf_op jit(solution)/shard_map/pallas_call | solution.py:398
  24.8 0.0 copy-done.2
  24.8 0.3 collective-permute-start.7
  25.2 0.0 copy-done.6
  25.2 0.0 copy-done.9
  25.2 0.7 %broadcast_in_dim.3 = f32[24,64]{1,0:T(8,128)} broadcast(f32[24]{0:T(128)S(1)} %copy-done.9), dimensions={0} | broadcast | bytes 6240 | tf_op jit(solution)/shard_map/broadcast_in_dim | solution.py:424
  25.8 0.8 %reshape_reshape.3.skip_ref = f32[1,1536]{1,0:T(1,128)S(1)} reshape(f32[24,64]{1,0:T(8,128)} %broadcast_in_dim.3) | data formatting | bytes 12288 | tf_op jit(solution)/shard_map/reshape;reshape | solution.py:424
  26.6 0.0 collective-permute-done.3.s_ref
  26.6 0.0 copy-done.1
  26.6 2.1 %shard_map.95 = (f32[256,1536]{1,0:T(8,128)S(1)}, f32[256,1536]{1,0:T(8,128)S(1)}) custom-call(f32[8,48]{1,0:T(8,128)S(1)} %shard_map.92.params_ref.refs_4_, bf16[128,1536]{1,0:T(8,128)(2,1)S(1)} %collective-permute-done.3.s_ref, bf16[256,1536]{1,0:T(8,128)(2,1)S(1)} %bitcast.8, bf16[256,48]{1,0:T(8,128)(2,1)S(1)} %get-tuple-element.39.raw_ref, ...), custom_call_target="tpu_custom_call" | custom-call | flops 1024 | bytes 1024 | tf_op jit(solution)/shard_map/pallas_call | solution.py:420
  28.7 0.0 copy-start.3
  28.7 0.0 copy-start.5
  28.7 0.0 copy-start.7
  28.7 0.0 collective-permute-done.8.s_ref
  28.7 1.3 %shard_map.99 = (bf16[32,1536]{1,0:T(8,128)(2,1)S(1)}, bf16[32,1536]{1,0:T(8,128)(2,1)S(1)}, bf16[32,1536]{1,0:T(8,128)(2,1)S(1)}, bf16[32,1536]{1,0:T(8,128)(2,1)S(1)}) custom-call(bf16[64,1536]{1,0:T(8,128)(2,1)} %collective-permute-done.8.s_ref, f32[128,1536]{1,0:T(8,128)S(1)} %get-tuple-element.55.y_ref, ...), custom_call_target="tpu_custom_call" | custom-call | flops 1024 | bytes 1024 | tf_op jit(solution)/shard_map/pallas_call | solution.py:429
  30.1 1.4 %collective-permute-start.12 = (bf16[32,1536]{1,0:T(8,128)(2,1)S(1)}, bf16[32,1536]{1,0:T(8,128)(2,1)S(1)}, u32[]{:S(2)}, u32[]{:S(2)}) collective-permute-start(bf16[32,1536]{1,0:T(8,128)(2,1)S(1)} %get-tuple-element.62), channel_id=1, source_target_pairs={{0,2},{2,0},{4,6},{6,4},{8,10},{10,8},{12,14},{14,12},{1,3},{3,1},... | collective-permute-start | bytes 294920 | tf_op jit(solution)/shard_map/ppermute | solution.py:363
  31.4 1.6 %collective-permute-start.13 = (bf16[32,1536]{1,0:T(8,128)(2,1)S(1)}, bf16[32,1536]{1,0:T(8,128)(2,1)S(1)}, u32[]{:S(2)}, u32[]{:S(2)}) collective-permute-start(bf16[32,1536]{1,0:T(8,128)(2,1)S(1)} %get-tuple-element.63), channel_id=1, source_target_pairs={{0,4},{2,6},{4,0},{6,2},{8,12},{10,14},{12,8},{14,10},{1,5},{3,7},... | collective-permute-start | bytes 294920 | tf_op jit(solution)/shard_map/ppermute | solution.py:363
  33.1 0.6 %collective-permute-start.14 = (bf16[32,1536]{1,0:T(8,128)(2,1)S(1)}, bf16[32,1536]{1,0:T(8,128)(2,1)S(1)}, u32[]{:S(2)}, u32[]{:S(2)}) collective-permute-start(bf16[32,1536]{1,0:T(8,128)(2,1)S(1)} %get-tuple-element.64), channel_id=1, source_target_pairs={{0,6},{2,4},{4,2},{6,0},{8,14},{10,12},{12,10},{14,8},{1,7},{3,5},... | collective-permute-start | bytes 294920 | tf_op jit(solution)/shard_map/ppermute | solution.py:363
  33.6 0.3 collective-permute-done.7.s_ref
  33.9 0.0 copy-done.3
  33.9 0.0 copy-done.5
  33.9 0.0 copy-done.7
  33.9 0.0 copy-start.8
  33.9 1.3 %shard_map.100 = (bf16[32,1536]{1,0:T(8,128)(2,1)S(1)}, bf16[32,1536]{1,0:T(8,128)(2,1)S(1)}, bf16[32,1536]{1,0:T(8,128)(2,1)S(1)}, bf16[32,1536]{1,0:T(8,128)(2,1)S(1)}) custom-call(bf16[64,1536]{1,0:T(8,128)(2,1)} %collective-permute-done.7.s_ref, f32[128,1536]{1,0:T(8,128)S(1)} %copy-done.5, bf16[128,48]{1,0:T(8,128)(2,1)S(1)} %copy-done.3, ...), custom_call_target="tpu_custom_call" | custom-call | flops 20000002048 | bytes 1024 | tf_op jit(solution)/shard_map/pallas_call | solution.py:429
  35.2 1.2 %collective-permute-start.10 = (bf16[32,1536]{1,0:T(8,128)(2,1)S(1)}, bf16[32,1536]{1,0:T(8,128)(2,1)S(1)}, u32[]{:S(2)}, u32[]{:S(2)}) collective-permute-start(bf16[32,1536]{1,0:T(8,128)(2,1)S(1)} %get-tuple-element.60), channel_id=1, source_target_pairs={{0,4},{2,6},{4,0},{6,2},{8,12},{10,14},{12,8},{14,10},{1,5},{3,7},... | collective-permute-start | bytes 294920 | tf_op jit(solution)/shard_map/ppermute | solution.py:363
  36.4 1.6 %collective-permute-start.11 = (bf16[32,1536]{1,0:T(8,128)(2,1)S(1)}, bf16[32,1536]{1,0:T(8,128)(2,1)S(1)}, u32[]{:S(2)}, u32[]{:S(2)}) collective-permute-start(bf16[32,1536]{1,0:T(8,128)(2,1)S(1)} %get-tuple-element.61), channel_id=1, source_target_pairs={{0,6},{2,4},{4,2},{6,0},{8,14},{10,12},{12,10},{14,8},{1,7},{3,5},... | collective-permute-start | bytes 294920 | tf_op jit(solution)/shard_map/ppermute | solution.py:363
  38.1 0.0 collective-permute-done.12.refs_1_
  38.1 0.7 %collective-permute-start.9 = (bf16[32,1536]{1,0:T(8,128)(2,1)S(1)}, bf16[32,1536]{1,0:T(8,128)(2,1)S(1)}, u32[]{:S(2)}, u32[]{:S(2)}) collective-permute-start(bf16[32,1536]{1,0:T(8,128)(2,1)S(1)} %get-tuple-element.59), channel_id=1, source_target_pairs={{0,2},{2,0},{4,6},{6,4},{8,10},{10,8},{12,14},{14,12},{1,3},{3,1},... | collective-permute-start | bytes 294920 | tf_op jit(solution)/shard_map/ppermute | solution.py:363
  38.8 0.0 copy-done.8
  38.8 0.0 collective-permute-done.13.refs_2_
  38.8 0.0 collective-permute-done.14.refs_3_
  38.8 1.0 %shard_map.101.refs_4_ = bf16[256,1536]{1,0:T(8,128)(2,1)} custom-call(f32[256,1536]{1,0:T(8,128)S(1)} %get-tuple-element.45._.w_ref, f32[256,1536]{1,0:T(8,128)S(1)} %get-tuple-element.46.g_ref, f32[1,1536]{1,0:T(1,128)S(1)} %reshape.23.gain_ref, bf16[32,1536]{1,0:T(8,128)(2,1)S(1)} %get-tuple-element.57._.refs_0_, ...), custom_call_target="tpu_custom_call" | custom-call | flops 1024 | bytes 1024 | tf_op jit(solution)/shard_map/pallas_call | solution.py:441
  39.8 0.1 collective-permute-done.10.refs_2_
  39.9 2.1 %collective-permute-done.11.refs_3_ = bf16[32,1536]{1,0:T(8,128)(2,1)S(1)} collective-permute-done((bf16[32,1536]{1,0:T(8,128)(2,1)S(1)}, bf16[32,1536]{1,0:T(8,128)(2,1)S(1)}, u32[]{:S(2)}, u32[]{:S(2)}) %collective-permute-start.11) | collective-permute-done | bytes 98336 | tf_op jit(solution)/shard_map/ppermute | solution.py:363
  42.0 1.0 %collective-permute-done.9.refs_1_ = bf16[32,1536]{1,0:T(8,128)(2,1)S(1)} collective-permute-done((bf16[32,1536]{1,0:T(8,128)(2,1)S(1)}, bf16[32,1536]{1,0:T(8,128)(2,1)S(1)}, u32[]{:S(2)}, u32[]{:S(2)}) %collective-permute-start.9) | collective-permute-done | bytes 98336 | tf_op jit(solution)/shard_map/ppermute | solution.py:363
  43.0 1.0 %shard_map.102 = bf16[256,1536]{1,0:T(8,128)(2,1)} custom-call(f32[256,1536]{1,0:T(8,128)S(1)} %get-tuple-element.45._.w_ref, f32[256,1536]{1,0:T(8,128)S(1)} %get-tuple-element.46.g_ref, f32[1,1536]{1,0:T(1,128)S(1)} %reshape.23.gain_ref, bf16[32,1536]{1,0:T(8,128)(2,1)S(1)} %get-tuple-element.58.refs_0_, ...), custom_call_target="tpu_custom_call", output_to_operand_aliasing={{}: (7, {})} | custom-call | flops 1024 | bytes 1024 | tf_op jit(solution)/shard_map/pallas_call | solution.py:441
  (1 shorter events, 0.0 us)
Async XLA Ops:
  0.0 16.6 %copy-start = (bf16[1,32,8,1536]{3,2,1,0:T(8,128)(2,1)S(1)}, bf16[1,32,8,1536]{3,2,1,0:T(8,128)(2,1)}, u32[]{:S(2)}) copy-start(bf16[1,32,8,1536]{3,2,1,0:T(8,128)(2,1)} %param.9) | copy-start | bytes 2359300
  1.5 8.9 %collective-permute-start = (bf16[32,1664]{1,0:T(8,128)(2,1)S(1)}, bf16[32,1664]{1,0:T(8,128)(2,1)S(1)}, u32[]{:S(2)}, u32[]{:S(2)}) collective-permute-start(bf16[32,1664]{1,0:T(8,128)(2,1)S(1)} %get-tuple-element.42), channel_id=1, source_target_pairs={{0,2},{2,0},{4,6},{6,4},{8,10},{10,8},{12,14},{14,12},{1,3},{3,1},... | collective-permute-start | bytes 319496 | tf_op jit(solution)/shard_map/ppermute | solution.py:363
  4.5 5.9 %collective-permute-start.1 = (bf16[32,1664]{1,0:T(8,128)(2,1)S(1)}, bf16[32,1664]{1,0:T(8,128)(2,1)S(1)}, u32[]{:S(2)}, u32[]{:S(2)}) collective-permute-start(bf16[32,1664]{1,0:T(8,128)(2,1)S(1)} %get-tuple-element.43), channel_id=1, source_target_pairs={{0,4},{2,6},{4,0},{6,2},{8,12},{10,14},{12,8},{14,10},{1,5},{3,7},... | collective-permute-start | bytes 319496 | tf_op jit(solution)/shard_map/ppermute | solution.py:363
  6.1 6.3 %collective-permute-start.2 = (bf16[32,1664]{1,0:T(8,128)(2,1)S(1)}, bf16[32,1664]{1,0:T(8,128)(2,1)S(1)}, u32[]{:S(2)}, u32[]{:S(2)}) collective-permute-start(bf16[32,1664]{1,0:T(8,128)(2,1)S(1)} %get-tuple-element.44), channel_id=1, source_target_pairs={{0,6},{2,4},{4,2},{6,0},{8,14},{10,12},{12,10},{14,8},{1,7},{3,5},... | collective-permute-start | bytes 319496 | tf_op jit(solution)/shard_map/ppermute | solution.py:363
  6.1 14.7 %collective-permute-start.4 = (bf16[32,1664]{1,0:T(8,128)(2,1)S(1)}, bf16[32,1664]{1,0:T(8,128)(2,1)S(1)}, u32[]{:S(2)}, u32[]{:S(2)}) collective-permute-start(bf16[32,1664]{1,0:T(8,128)(2,1)S(1)} %get-tuple-element.48), channel_id=1, source_target_pairs={{0,2},{2,0},{4,6},{6,4},{8,10},{10,8},{12,14},{14,12},{1,3},{3,1},... | collective-permute-start | bytes 319496 | tf_op jit(solution)/shard_map/ppermute | solution.py:363
  8.0 12.8 %collective-permute-start.5 = (bf16[32,1664]{1,0:T(8,128)(2,1)S(1)}, bf16[32,1664]{1,0:T(8,128)(2,1)S(1)}, u32[]{:S(2)}, u32[]{:S(2)}) collective-permute-start(bf16[32,1664]{1,0:T(8,128)(2,1)S(1)} %get-tuple-element.49), channel_id=1, source_target_pairs={{0,4},{2,6},{4,0},{6,2},{8,12},{10,14},{12,8},{14,10},{1,5},{3,7},... | collective-permute-start | bytes 319496 | tf_op jit(solution)/shard_map/ppermute | solution.py:363
  10.4 10.4 %collective-permute-start.6 = (bf16[32,1664]{1,0:T(8,128)(2,1)S(1)}, bf16[32,1664]{1,0:T(8,128)(2,1)S(1)}, u32[]{:S(2)}, u32[]{:S(2)}) collective-permute-start(bf16[32,1664]{1,0:T(8,128)(2,1)S(1)} %get-tuple-element.50), channel_id=1, source_target_pairs={{0,6},{2,4},{4,2},{6,0},{8,14},{10,12},{12,10},{14,8},{1,7},{3,5},... | collective-permute-start | bytes 319496 | tf_op jit(solution)/shard_map/ppermute | solution.py:363
  13.6 15.2 %collective-permute-start.8 = (bf16[64,1536]{1,0:T(8,128)(2,1)S(1)}, bf16[64,1536]{1,0:T(8,128)(2,1)}, u32[]{:S(2)}, u32[]{:S(2)}) collective-permute-start(bf16[64,1536]{1,0:T(8,128)(2,1)S(1)} %shard_map.93._), channel_id=1, source_target_pairs={{0,8},{2,10},{4,12},{6,14},{8,0},{10,2},{12,4},{14,6},{1,9},{3,11}... | collective-permute-start | bytes 589832 | tf_op jit(solution)/shard_map/ppermute | solution.py:305
  18.1 8.6 %collective-permute-start.3 = (bf16[128,1536]{1,0:T(8,128)(2,1)S(1)}, bf16[128,1536]{1,0:T(8,128)(2,1)S(1)}, u32[]{:S(2)}, u32[]{:S(2)}) collective-permute-start(bf16[128,1536]{1,0:T(8,128)(2,1)S(1)} %shard_map.94.refs_4_), channel_id=1, source_target_pairs={{0,16},{16,0},{1,17},{17,1},{2,18},{18,2},{3,19},{19,3},{4,20},{20... | collective-permute-start | bytes 1179656 | tf_op jit(solution)/shard_map/ppermute | solution.py:305
  20.9 4.3 %copy-start.9 = (f32[24]{0:T(128)S(1)}, f32[24]{0:T(128)}, u32[]{:S(2)}) copy-start(f32[24]{0:T(128)} %param.16) | copy-start | bytes 292
  20.9 5.7 %copy-start.1 = (bf16[1,32,8,1536]{3,2,1,0:T(8,128)(2,1)S(1)}, bf16[1,32,8,1536]{3,2,1,0:T(8,128)(2,1)}, u32[]{:S(2)}) copy-start(bf16[1,32,8,1536]{3,2,1,0:T(8,128)(2,1)} %param.10) | copy-start | bytes 2359300
  22.1 0.9 %copy-start.4 = (f32[128,1536]{1,0:T(8,128)}, f32[128,1536]{1,0:T(8,128)S(1)}, u32[]{:S(2)}) copy-start(f32[128,1536]{1,0:T(8,128)S(1)} %get-tuple-element.53.y_ref) | copy-start | bytes 2359300
  23.0 1.8 %copy-start.2 = (bf16[128,48]{1,0:T(8,128)(2,1)}, bf16[128,48]{1,0:T(8,128)(2,1)S(1)}, u32[]{:S(2)}) copy-start(bf16[128,48]{1,0:T(8,128)(2,1)S(1)} %get-tuple-element.52.refs_4_.fade_ref) | copy-start | bytes 36868
  23.0 2.1 %copy-start.6 = (bf16[128,64]{1,0:T(8,128)(2,1)}, bf16[128,64]{1,0:T(8,128)(2,1)S(1)}, u32[]{:S(2)}) copy-start(bf16[128,64]{1,0:T(8,128)(2,1)S(1)} %get-tuple-element.54.entry_ref) | copy-start | bytes 49156
  24.8 9.1 %collective-permute-start.7 = (bf16[64,1536]{1,0:T(8,128)(2,1)}, bf16[64,1536]{1,0:T(8,128)(2,1)}, u32[]{:S(2)}, u32[]{:S(2)}) collective-permute-start(bf16[64,1536]{1,0:T(8,128)(2,1)} %shard_map.98), channel_id=1, source_target_pairs={{0,8},{2,10},{4,12},{6,14},{8,0},{10,2},{12,4},{14,6},{1,9},{3,11}... | collective-permute-start | bytes 589832 | tf_op jit(solution)/shard_map/ppermute | solution.py:305
  28.7 5.2 %copy-start.3 = (bf16[128,48]{1,0:T(8,128)(2,1)S(1)}, bf16[128,48]{1,0:T(8,128)(2,1)}, u32[]{:S(2)}) copy-start(bf16[128,48]{1,0:T(8,128)(2,1)} %copy-done.2) | copy-start | bytes 36868
  28.7 5.2 %copy-start.5 = (f32[128,1536]{1,0:T(8,128)S(1)}, f32[128,1536]{1,0:T(8,128)}, u32[]{:S(2)}) copy-start(f32[128,1536]{1,0:T(8,128)} %copy-done.4) | copy-start | bytes 2359300
  28.7 5.2 %copy-start.7 = (bf16[128,64]{1,0:T(8,128)(2,1)S(1)}, bf16[128,64]{1,0:T(8,128)(2,1)}, u32[]{:S(2)}) copy-start(bf16[128,64]{1,0:T(8,128)(2,1)} %copy-done.6) | copy-start | bytes 49156
  30.1 8.0 %collective-permute-start.12 = (bf16[32,1536]{1,0:T(8,128)(2,1)S(1)}, bf16[32,1536]{1,0:T(8,128)(2,1)S(1)}, u32[]{:S(2)}, u32[]{:S(2)}) collective-permute-start(bf16[32,1536]{1,0:T(8,128)(2,1)S(1)} %get-tuple-element.62), channel_id=1, source_target_pairs={{0,2},{2,0},{4,6},{6,4},{8,10},{10,8},{12,14},{14,12},{1,3},{3,1},... | collective-permute-start | bytes 294920 | tf_op jit(solution)/shard_map/ppermute | solution.py:363
  31.4 7.3 %collective-permute-start.13 = (bf16[32,1536]{1,0:T(8,128)(2,1)S(1)}, bf16[32,1536]{1,0:T(8,128)(2,1)S(1)}, u32[]{:S(2)}, u32[]{:S(2)}) collective-permute-start(bf16[32,1536]{1,0:T(8,128)(2,1)S(1)} %get-tuple-element.63), channel_id=1, source_target_pairs={{0,4},{2,6},{4,0},{6,2},{8,12},{10,14},{12,8},{14,10},{1,5},{3,7},... | collective-permute-start | bytes 294920 | tf_op jit(solution)/shard_map/ppermute | solution.py:363
  33.1 5.7 %collective-permute-start.14 = (bf16[32,1536]{1,0:T(8,128)(2,1)S(1)}, bf16[32,1536]{1,0:T(8,128)(2,1)S(1)}, u32[]{:S(2)}, u32[]{:S(2)}) collective-permute-start(bf16[32,1536]{1,0:T(8,128)(2,1)S(1)} %get-tuple-element.64), channel_id=1, source_target_pairs={{0,6},{2,4},{4,2},{6,0},{8,14},{10,12},{12,10},{14,8},{1,7},{3,5},... | collective-permute-start | bytes 294920 | tf_op jit(solution)/shard_map/ppermute | solution.py:363
  33.9 4.9 %copy-start.8 = (f32[1536]{0:T(1024)S(1)}, f32[1536]{0:T(1024)}, u32[]{:S(2)}) copy-start(f32[1536]{0:T(1024)} %param.17) | copy-start | bytes 18436
  35.2 4.7 %collective-permute-start.10 = (bf16[32,1536]{1,0:T(8,128)(2,1)S(1)}, bf16[32,1536]{1,0:T(8,128)(2,1)S(1)}, u32[]{:S(2)}, u32[]{:S(2)}) collective-permute-start(bf16[32,1536]{1,0:T(8,128)(2,1)S(1)} %get-tuple-element.60), channel_id=1, source_target_pairs={{0,4},{2,6},{4,0},{6,2},{8,12},{10,14},{12,8},{14,10},{1,5},{3,7},... | collective-permute-start | bytes 294920 | tf_op jit(solution)/shard_map/ppermute | solution.py:363
  36.4 5.5 %collective-permute-start.11 = (bf16[32,1536]{1,0:T(8,128)(2,1)S(1)}, bf16[32,1536]{1,0:T(8,128)(2,1)S(1)}, u32[]{:S(2)}, u32[]{:S(2)}) collective-permute-start(bf16[32,1536]{1,0:T(8,128)(2,1)S(1)} %get-tuple-element.61), channel_id=1, source_target_pairs={{0,6},{2,4},{4,2},{6,0},{8,14},{10,12},{12,10},{14,8},{1,7},{3,5},... | collective-permute-start | bytes 294920 | tf_op jit(solution)/shard_map/ppermute | solution.py:363
  38.1 4.9 %collective-permute-start.9 = (bf16[32,1536]{1,0:T(8,128)(2,1)S(1)}, bf16[32,1536]{1,0:T(8,128)(2,1)S(1)}, u32[]{:S(2)}, u32[]{:S(2)}) collective-permute-start(bf16[32,1536]{1,0:T(8,128)(2,1)S(1)} %get-tuple-element.59), channel_id=1, source_target_pairs={{0,2},{2,0},{4,6},{6,4},{8,10},{10,8},{12,14},{14,12},{1,3},{3,1},... | collective-permute-start | bytes 294920 | tf_op jit(solution)/shard_map/ppermute | solution.py:363

commit v13 on v12

--- a/solution.py
+++ b/solution.py
@@ -255,13 +255,14 @@
 def col_out_kernel(params_ref, s_ref, x_ref, raw_ref, maps_ref, gate_ref, skip_ref, w_ref, g_ref, *, cols, heads, state, width):
     scan = col_scan(params_ref, raw_ref, maps_ref, cols, heads, state)
     mix = jnp.concatenate([scan.within(), scan.entry(lax.axis_index("row") > 0)], axis=1)
+    skips = parts(jnp.broadcast_to(skip_ref[...], (8, heads)), 2)
     for first, count in strips(s_ref.shape[1]):
         pick = picks(heads, width, first, count)
         part = slice(first, first + count)
         x = x_ref[:, part].astype(F32)
         values = (x * dot(scan.grow, pick)).astype(BF16)
         y = dot(mix, jnp.concatenate([values, s_ref[:, part]], axis=0)) * dot(scan.fade, pick)
-        w_ref[:, part] = y + skip_ref[:, part] * x
+        w_ref[:, part] = y + dot(skips, pick)[0:1, :] * x
         gate = gate_ref[:, part].astype(F32)
         g_ref[:, part] = gate / (1.0 + jnp.exp(-gate))
 
@@ -421,7 +422,7 @@
         functools.partial(col_out_kernel, **sizes),
         [pltpu.VMEM((tokens, channels), F32)] * 2,
         0,
-    )(params, col_entering, x, raw, maps, gate, jnp.repeat(skip, width).reshape(1, channels))
+    )(params, col_entering, x, raw, maps, gate, skip.reshape(1, heads))
 
     back = []
     before = w

time: 44.2 us -> 41.7 us (0.943)
  local copies, waits for them, and re-layouts: 2.38 us -> 0.03 us
  Pallas kernels: 15.1 us -> 12.8 us
  waiting for transfers between devices: 5.52 us -> 7.77 us
    ppermute x3, waiting for transfers between devices: 0.27 us -> 2.6 us  [entering_states(): entering = lax.ppermute(ends, axis, onward)]
    pallas_call x2, Pallas kernels: 2.62 us -> 0.7 us  [body(): call(functools.partial(row_out_kernel, heads=heads, width=width), [pltpu....]
    unnamed x20 -> x8, local copies, waits for them, and re-layouts: 0.92 us -> 0.02 us
    another operation x1 -> x0, local copies, waits for them, and re-layouts: 0.78 us -> none  [body(): jnp.repeat(skip, width).reshape(1, channels)]
    pallas_call x2, Pallas kernels: 2.9 us -> 2.23 us  [body(): call(functools.partial(row_state_kernel, count=len(piece), **sizes, **sha...]
    broadcast_in_dim x1 -> x0, local copies, waits for them, and re-layouts: 0.67 us -> none  [body(): jnp.repeat(skip, width).reshape(1, channels)]
  transfers between devices with their start and end apart: 15 -> 15, of which waited for: 5 -> 5; matrix products, arithmetic and copies ran while one was open for 3% -> 0% of each run, Pallas kernels for 29% -> 25%
where the time goes in v13:
time: 41.7 us; the launch traced here: 41.6 us
  starting transfers between devices  20.2 us (48%)
  Pallas kernels  12.8 us (31%)
  waiting for transfers between devices  7.77 us (19%)
  between operations  0.83 us (2%)
    ppermute x12, starting transfers between devices, exchange(): lax.ppermute(blocks[i], 'col', [(at, partner(at, i, group)) for at in ran...  15.2 us
    ppermute x12, waiting for transfers between devices, exchange(): lax.ppermute(blocks[i], 'col', [(at, partner(at, i, group)) for at in ran...  5.17 us
    ppermute x3, starting transfers between devices, entering_states(): entering = lax.ppermute(ends, axis, onward)  4.99 us
    ppermute x3, waiting for transfers between devices, entering_states(): entering = lax.ppermute(ends, axis, onward)  2.6 us
    pallas_call x2, Pallas kernels, of_own(): call(functools.partial(row_local_kernel, offset=offset, **sizes, **shared...  2.43 us
    pallas_call x1, Pallas kernels, body(): call(functools.partial(col_out_kernel, **sizes), [pltpu.VMEM((tokens, cha...  2.38 us
    pallas_call x2, Pallas kernels, body(): call(functools.partial(row_state_kernel, count=len(piece), **sizes, **sha...  2.23 us
    pallas_call x2, Pallas kernels, body(): call(functools.partial(final_kernel, offset=first, share=share, **shared)...  1.89 us
  transfers between devices with their start and end apart: 15, of which 5 were waited for; matrix products, arithmetic and copies ran while one was open for 0% of the time, Pallas kernels for 25%

profile of v13, /device:TPU:0, one launch (start us, length us, event | category | flops | bytes accessed | tf_op | source)
XLA Modules:
  0.0 41.6 jit_solution(11236025612497637873)
XLA Ops:
  0.0 0.0 copy-start
  0.0 1.5 %shard_map.91 = (bf16[256,48]{1,0:T(8,128)(2,1)S(1)}, bf16[256,64]{1,0:T(8,128)(2,1)S(1)}, f32[48,1000]{1,0:T(8,128)S(1)}, f32[2,24]{1,0:T(2,128)S(1)}, bf16[32,...) custom-call(bf16[256,1536]{1,0:T(8,128)(2,1)} %bitcast.7, ...), custom_call_target="tpu_custom_call" | custom-call | flops 1000001024 | bytes 1024 | tf_op jit(solution)/shard_map/pallas_call | solution.py:336
  1.5 3.0 %collective-permute-start = (bf16[32,1664]{1,0:T(8,128)(2,1)S(1)}, bf16[32,1664]{1,0:T(8,128)(2,1)S(1)}, u32[]{:S(2)}, u32[]{:S(2)}) collective-permute-start(bf16[32,1664]{1,0:T(8,128)(2,1)S(1)} %get-tuple-element.42), channel_id=1, source_target_pairs={{0,2},{2,0},{4,6},{6,4},{8,10},{10,8},{12,14},{14,12},{1,3},{3,1},... | collective-permute-start | bytes 319496 | tf_op jit(solution)/shard_map/ppermute | solution.py:364
  4.5 1.6 %collective-permute-start.1 = (bf16[32,1664]{1,0:T(8,128)(2,1)S(1)}, bf16[32,1664]{1,0:T(8,128)(2,1)S(1)}, u32[]{:S(2)}, u32[]{:S(2)}) collective-permute-start(bf16[32,1664]{1,0:T(8,128)(2,1)S(1)} %get-tuple-element.43), channel_id=1, source_target_pairs={{0,4},{2,6},{4,0},{6,2},{8,12},{10,14},{12,8},{14,10},{1,5},{3,7},... | collective-permute-start | bytes 319496 | tf_op jit(solution)/shard_map/ppermute | solution.py:364
  6.1 0.0 collective-permute-start.2
  6.1 1.9 %collective-permute-start.4 = (bf16[32,1664]{1,0:T(8,128)(2,1)S(1)}, bf16[32,1664]{1,0:T(8,128)(2,1)S(1)}, u32[]{:S(2)}, u32[]{:S(2)}) collective-permute-start(bf16[32,1664]{1,0:T(8,128)(2,1)S(1)} %get-tuple-element.48), channel_id=1, source_target_pairs={{0,2},{2,0},{4,6},{6,4},{8,10},{10,8},{12,14},{14,12},{1,3},{3,1},... | collective-permute-start | bytes 319496 | tf_op jit(solution)/shard_map/ppermute | solution.py:364
  8.0 1.6 %collective-permute-start.5 = (bf16[32,1664]{1,0:T(8,128)(2,1)S(1)}, bf16[32,1664]{1,0:T(8,128)(2,1)S(1)}, u32[]{:S(2)}, u32[]{:S(2)}) collective-permute-start(bf16[32,1664]{1,0:T(8,128)(2,1)S(1)} %get-tuple-element.49), channel_id=1, source_target_pairs={{0,4},{2,6},{4,0},{6,2},{8,12},{10,14},{12,8},{14,10},{1,5},{3,7},... | collective-permute-start | bytes 319496 | tf_op jit(solution)/shard_map/ppermute | solution.py:364
  10.2 0.2 shard_map.92.params_ref.refs_4_
  10.4 0.0 collective-permute-done.refs_1_
  10.4 0.0 collective-permute-start.6
  10.4 0.0 collective-permute-done.1.refs_2_
  10.5 2.0 %collective-permute-done.2.refs_3_ = bf16[32,1664]{1,0:T(8,128)(2,1)S(1)} collective-permute-done((bf16[32,1664]{1,0:T(8,128)(2,1)S(1)}, bf16[32,1664]{1,0:T(8,128)(2,1)S(1)}, u32[]{:S(2)}, u32[]{:S(2)}) %collective-permute-start.2) | collective-permute-done | bytes 106528 | tf_op jit(solution)/shard_map/ppermute | solution.py:364
  12.4 1.1 %shard_map.93._ = bf16[64,1536]{1,0:T(8,128)(2,1)S(1)} custom-call(f32[8,48]{1,0:T(8,128)S(1)} %shard_map.92.params_ref.refs_4_, bf16[32,1664]{1,0:T(8,128)(2,1)S(1)} %get-tuple-element.41.refs_0_, bf16[32,1664]{1,0:T(8,128)(2,1)S(1)} %collective-permute-done.refs_1_, bf16[32,1664]{1,0:T(8,128)(2,1)S(1)} %collective-permute-done.1.refs_2_, ...), custom_call_target="tpu_custom_call" | custom-call | flops 1024 | bytes 1024 | tf_op jit(solution)/shard_map/pallas_call | solution.py:399
  13.6 3.0 %collective-permute-start.8 = (bf16[64,1536]{1,0:T(8,128)(2,1)S(1)}, bf16[64,1536]{1,0:T(8,128)(2,1)S(1)}, u32[]{:S(2)}, u32[]{:S(2)}) collective-permute-start(bf16[64,1536]{1,0:T(8,128)(2,1)S(1)} %shard_map.93._), channel_id=1, source_target_pairs={{0,8},{2,10},{4,12},{6,14},{8,0},{10,2},{12,4},{14,6},{1,9},{3,11}... | collective-permute-start | bytes 589832 | tf_op jit(solution)/shard_map/ppermute | solution.py:306
  16.6 0.0 copy-done
  16.6 1.5 %shard_map.94.refs_4_ = bf16[128,1536]{1,0:T(8,128)(2,1)S(1)} custom-call(f32[8,48]{1,0:T(8,128)S(1)} %shard_map.92.params_ref.refs_4_, bf16[256,1536]{1,0:T(8,128)(2,1)S(1)} %bitcast.8, bf16[256,48]{1,0:T(8,128)(2,1)S(1)} %get-tuple-element.39.raw_ref, bf16[256,64]{1,0:T(8,128)(2,1)S(1)} %get-tuple-element.40.maps_ref, bf16[64,1536]{1,0:T(8,128)(2,1)S(1)} %shard_map.93._), custom_call_target="tpu_custom_call" | custom-call | flops 1024 | bytes 1024 | tf_op jit(solution)/shard_map/pallas_call | solution.py:407
  18.1 1.5 %collective-permute-start.3 = (bf16[128,1536]{1,0:T(8,128)(2,1)S(1)}, bf16[128,1536]{1,0:T(8,128)(2,1)S(1)}, u32[]{:S(2)}, u32[]{:S(2)}) collective-permute-start(bf16[128,1536]{1,0:T(8,128)(2,1)S(1)} %shard_map.94.refs_4_), channel_id=1, source_target_pairs={{0,16},{16,0},{1,17},{17,1},{2,18},{18,2},{3,19},{19,3},{4,20},{20... | collective-permute-start | bytes 1179656 | tf_op jit(solution)/shard_map/ppermute | solution.py:306
  19.6 1.2 %shard_map.96 = (f32[128,1536]{1,0:T(8,128)S(1)}, bf16[128,48]{1,0:T(8,128)(2,1)S(1)}, bf16[128,64]{1,0:T(8,128)(2,1)S(1)}) custom-call(f32[8,48]{1,0:T(8,128)S(1)} %shard_map.92.params_ref.refs_4_, bf16[32,1664]{1,0:T(8,128)(2,1)S(1)} %get-tuple-element.41.refs_0_, bf16[32,1664]{1,0:T(8,128)(2,1)S(1)} %collective-permute-done.refs_1_, ...), custom_call_target="tpu_custom_call" | custom-call | flops 2000001024 | bytes 1024 | tf_op jit(solution)/shard_map/pallas_call | solution.py:383
  20.8 0.0 collective-permute-done.4.refs_1_
  20.8 0.0 collective-permute-done.5.refs_2_
  20.8 0.0 collective-permute-done.6.refs_3_
  20.8 0.0 copy-start.1
  20.8 0.0 copy-start.2
  20.9 1.2 %shard_map.97 = (f32[128,1536]{1,0:T(8,128)S(1)}, bf16[128,48]{1,0:T(8,128)(2,1)S(1)}, bf16[128,64]{1,0:T(8,128)(2,1)S(1)}) custom-call(f32[8,48]{1,0:T(8,128)S(1)} %shard_map.92.params_ref.refs_4_, bf16[32,1664]{1,0:T(8,128)(2,1)S(1)} %get-tuple-element.47.refs_0_, bf16[32,1664]{1,0:T(8,128)(2,1)S(1)} %collective-permute-done.4.refs_1_, ...), custom_call_target="tpu_custom_call" | custom-call | flops 2000001024 | bytes 1024 | tf_op jit(solution)/shard_map/pallas_call | solution.py:383
  22.1 1.1 %shard_map.98 = bf16[64,1536]{1,0:T(8,128)(2,1)S(1)} custom-call(f32[8,48]{1,0:T(8,128)S(1)} %shard_map.92.params_ref.refs_4_, bf16[32,1664]{1,0:T(8,128)(2,1)S(1)} %get-tuple-element.47.refs_0_, bf16[32,1664]{1,0:T(8,128)(2,1)S(1)} %collective-permute-done.4.refs_1_, bf16[32,1664]{1,0:T(8,128)(2,1)S(1)} %collective-permute-done.5.refs_2_, ...), custom_call_target="tpu_custom_call" | custom-call | flops 1024 | bytes 1024 | tf_op jit(solution)/shard_map/pallas_call | solution.py:399
  23.2 0.5 %collective-permute-start.7 = (bf16[64,1536]{1,0:T(8,128)(2,1)S(1)}, bf16[64,1536]{1,0:T(8,128)(2,1)S(1)}, u32[]{:S(2)}, u32[]{:S(2)}) collective-permute-start(bf16[64,1536]{1,0:T(8,128)(2,1)S(1)} %shard_map.98), channel_id=1, source_target_pairs={{0,8},{2,10},{4,12},{6,14},{8,0},{10,2},{12,4},{14,6},{1,9},{3,11}... | collective-permute-start | bytes 589832 | tf_op jit(solution)/shard_map/ppermute | solution.py:306
  23.7 2.6 %collective-permute-done.3.s_ref = bf16[128,1536]{1,0:T(8,128)(2,1)S(1)} collective-permute-done((bf16[128,1536]{1,0:T(8,128)(2,1)S(1)}, bf16[128,1536]{1,0:T(8,128)(2,1)S(1)}, u32[]{:S(2)}, u32[]{:S(2)}) %collective-permute-start.3) | collective-permute-done | bytes 393248 | tf_op jit(solution)/shard_map/ppermute | solution.py:306
  26.3 0.0 copy-done.1
  26.3 0.0 copy-done.2
  26.3 2.4 %shard_map.95 = (f32[256,1536]{1,0:T(8,128)S(1)}, f32[256,1536]{1,0:T(8,128)S(1)}) custom-call(f32[8,48]{1,0:T(8,128)S(1)} %shard_map.92.params_ref.refs_4_, bf16[128,1536]{1,0:T(8,128)(2,1)S(1)} %collective-permute-done.3.s_ref, bf16[256,1536]{1,0:T(8,128)(2,1)S(1)} %bitcast.9, bf16[256,48]{1,0:T(8,128)(2,1)S(1)} %get-tuple-element.39.raw_ref, ...), custom_call_target="tpu_custom_call" | custom-call | flops 1024 | bytes 1024 | tf_op jit(solution)/shard_map/pallas_call | solution.py:421
  28.6 0.0 collective-permute-done.8.s_ref
  28.7 0.3 shard_map.99
  29.0 1.2 %collective-permute-start.12 = (bf16[32,1536]{1,0:T(8,128)(2,1)S(1)}, bf16[32,1536]{1,0:T(8,128)(2,1)S(1)}, u32[]{:S(2)}, u32[]{:S(2)}) collective-permute-start(bf16[32,1536]{1,0:T(8,128)(2,1)S(1)} %get-tuple-element.62), channel_id=1, source_target_pairs={{0,2},{2,0},{4,6},{6,4},{8,10},{10,8},{12,14},{14,12},{1,3},{3,1},... | collective-permute-start | bytes 294920 | tf_op jit(solution)/shard_map/ppermute | solution.py:364
  30.2 1.5 %collective-permute-start.13 = (bf16[32,1536]{1,0:T(8,128)(2,1)S(1)}, bf16[32,1536]{1,0:T(8,128)(2,1)S(1)}, u32[]{:S(2)}, u32[]{:S(2)}) collective-permute-start(bf16[32,1536]{1,0:T(8,128)(2,1)S(1)} %get-tuple-element.63), channel_id=1, source_target_pairs={{0,4},{2,6},{4,0},{6,2},{8,12},{10,14},{12,8},{14,10},{1,5},{3,7},... | collective-permute-start | bytes 294920 | tf_op jit(solution)/shard_map/ppermute | solution.py:364
  31.7 0.9 %collective-permute-start.14 = (bf16[32,1536]{1,0:T(8,128)(2,1)S(1)}, bf16[32,1536]{1,0:T(8,128)(2,1)S(1)}, u32[]{:S(2)}, u32[]{:S(2)}) collective-permute-start(bf16[32,1536]{1,0:T(8,128)(2,1)S(1)} %get-tuple-element.64), channel_id=1, source_target_pairs={{0,6},{2,4},{4,2},{6,0},{8,14},{10,12},{12,10},{14,8},{1,7},{3,5},... | collective-permute-start | bytes 294920 | tf_op jit(solution)/shard_map/ppermute | solution.py:364
  32.6 0.0 collective-permute-done.7.s_ref
  32.6 0.0 copy-start.3
  32.6 0.3 shard_map.100
  32.9 1.1 %collective-permute-start.10 = (bf16[32,1536]{1,0:T(8,128)(2,1)S(1)}, bf16[32,1536]{1,0:T(8,128)(2,1)S(1)}, u32[]{:S(2)}, u32[]{:S(2)}) collective-permute-start(bf16[32,1536]{1,0:T(8,128)(2,1)S(1)} %get-tuple-element.60), channel_id=1, source_target_pairs={{0,4},{2,6},{4,0},{6,2},{8,12},{10,14},{12,8},{14,10},{1,5},{3,7},... | collective-permute-start | bytes 294920 | tf_op jit(solution)/shard_map/ppermute | solution.py:364
  34.1 1.5 %collective-permute-start.11 = (bf16[32,1536]{1,0:T(8,128)(2,1)S(1)}, bf16[32,1536]{1,0:T(8,128)(2,1)S(1)}, u32[]{:S(2)}, u32[]{:S(2)}) collective-permute-start(bf16[32,1536]{1,0:T(8,128)(2,1)S(1)} %get-tuple-element.61), channel_id=1, source_target_pairs={{0,6},{2,4},{4,2},{6,0},{8,14},{10,12},{12,10},{14,8},{1,7},{3,5},... | collective-permute-start | bytes 294920 | tf_op jit(solution)/shard_map/ppermute | solution.py:364
  35.6 0.0 collective-permute-done.12.refs_1_
  35.6 0.9 %collective-permute-start.9 = (bf16[32,1536]{1,0:T(8,128)(2,1)S(1)}, bf16[32,1536]{1,0:T(8,128)(2,1)S(1)}, u32[]{:S(2)}, u32[]{:S(2)}) collective-permute-start(bf16[32,1536]{1,0:T(8,128)(2,1)S(1)} %get-tuple-element.59), channel_id=1, source_target_pairs={{0,2},{2,0},{4,6},{6,4},{8,10},{10,8},{12,14},{14,12},{1,3},{3,1},... | collective-permute-start | bytes 294920 | tf_op jit(solution)/shard_map/ppermute | solution.py:364
  36.5 0.0 copy-done.3
  36.5 0.0 collective-permute-done.13.refs_2_
  36.5 0.7 %collective-permute-done.14.refs_3_ = bf16[32,1536]{1,0:T(8,128)(2,1)S(1)} collective-permute-done((bf16[32,1536]{1,0:T(8,128)(2,1)S(1)}, bf16[32,1536]{1,0:T(8,128)(2,1)S(1)}, u32[]{:S(2)}, u32[]{:S(2)}) %collective-permute-start.14) | collective-permute-done | bytes 98336 | tf_op jit(solution)/shard_map/ppermute | solution.py:364
  37.2 0.9 %shard_map.101.refs_4_ = bf16[256,1536]{1,0:T(8,128)(2,1)} custom-call(f32[256,1536]{1,0:T(8,128)S(1)} %get-tuple-element.45._.w_ref, f32[256,1536]{1,0:T(8,128)S(1)} %get-tuple-element.46.g_ref, f32[1,1536]{1,0:T(1,128)S(1)} %reshape.27.gain_ref, bf16[32,1536]{1,0:T(8,128)(2,1)S(1)} %get-tuple-element.57._.refs_0_, ...), custom_call_target="tpu_custom_call" | custom-call | flops 1024 | bytes 1024 | tf_op jit(solution)/shard_map/pallas_call | solution.py:442
  38.1 0.0 collective-permute-done.10.refs_2_
  38.2 1.5 %collective-permute-done.11.refs_3_ = bf16[32,1536]{1,0:T(8,128)(2,1)S(1)} collective-permute-done((bf16[32,1536]{1,0:T(8,128)(2,1)S(1)}, bf16[32,1536]{1,0:T(8,128)(2,1)S(1)}, u32[]{:S(2)}, u32[]{:S(2)}) %collective-permute-start.11) | collective-permute-done | bytes 98336 | tf_op jit(solution)/shard_map/ppermute | solution.py:364
  39.6 1.0 %collective-permute-done.9.refs_1_ = bf16[32,1536]{1,0:T(8,128)(2,1)S(1)} collective-permute-done((bf16[32,1536]{1,0:T(8,128)(2,1)S(1)}, bf16[32,1536]{1,0:T(8,128)(2,1)S(1)}, u32[]{:S(2)}, u32[]{:S(2)}) %collective-permute-start.9) | collective-permute-done | bytes 98336 | tf_op jit(solution)/shard_map/ppermute | solution.py:364
  40.6 0.9 %shard_map.102 = bf16[256,1536]{1,0:T(8,128)(2,1)} custom-call(f32[256,1536]{1,0:T(8,128)S(1)} %get-tuple-element.45._.w_ref, f32[256,1536]{1,0:T(8,128)S(1)} %get-tuple-element.46.g_ref, f32[1,1536]{1,0:T(1,128)S(1)} %reshape.27.gain_ref, bf16[32,1536]{1,0:T(8,128)(2,1)S(1)} %get-tuple-element.58.refs_0_, ...), custom_call_target="tpu_custom_call", output_to_operand_aliasing={{}: (7, {})} | custom-call | flops 1024 | bytes 1024 | tf_op jit(solution)/shard_map/pallas_call | solution.py:442
  (1 shorter events, 0.0 us)
Async XLA Ops:
  0.0 16.6 %copy-start = (bf16[1,32,8,1536]{3,2,1,0:T(8,128)(2,1)S(1)}, bf16[1,32,8,1536]{3,2,1,0:T(8,128)(2,1)}, u32[]{:S(2)}) copy-start(bf16[1,32,8,1536]{3,2,1,0:T(8,128)(2,1)} %param.9) | copy-start | bytes 2359300
  1.5 8.9 %collective-permute-start = (bf16[32,1664]{1,0:T(8,128)(2,1)S(1)}, bf16[32,1664]{1,0:T(8,128)(2,1)S(1)}, u32[]{:S(2)}, u32[]{:S(2)}) collective-permute-start(bf16[32,1664]{1,0:T(8,128)(2,1)S(1)} %get-tuple-element.42), channel_id=1, source_target_pairs={{0,2},{2,0},{4,6},{6,4},{8,10},{10,8},{12,14},{14,12},{1,3},{3,1},... | collective-permute-start | bytes 319496 | tf_op jit(solution)/shard_map/ppermute | solution.py:364
  4.5 5.9 %collective-permute-start.1 = (bf16[32,1664]{1,0:T(8,128)(2,1)S(1)}, bf16[32,1664]{1,0:T(8,128)(2,1)S(1)}, u32[]{:S(2)}, u32[]{:S(2)}) collective-permute-start(bf16[32,1664]{1,0:T(8,128)(2,1)S(1)} %get-tuple-element.43), channel_id=1, source_target_pairs={{0,4},{2,6},{4,0},{6,2},{8,12},{10,14},{12,8},{14,10},{1,5},{3,7},... | collective-permute-start | bytes 319496 | tf_op jit(solution)/shard_map/ppermute | solution.py:364
  6.1 6.3 %collective-permute-start.2 = (bf16[32,1664]{1,0:T(8,128)(2,1)S(1)}, bf16[32,1664]{1,0:T(8,128)(2,1)S(1)}, u32[]{:S(2)}, u32[]{:S(2)}) collective-permute-start(bf16[32,1664]{1,0:T(8,128)(2,1)S(1)} %get-tuple-element.44), channel_id=1, source_target_pairs={{0,6},{2,4},{4,2},{6,0},{8,14},{10,12},{12,10},{14,8},{1,7},{3,5},... | collective-permute-start | bytes 319496 | tf_op jit(solution)/shard_map/ppermute | solution.py:364
  6.1 14.7 %collective-permute-start.4 = (bf16[32,1664]{1,0:T(8,128)(2,1)S(1)}, bf16[32,1664]{1,0:T(8,128)(2,1)S(1)}, u32[]{:S(2)}, u32[]{:S(2)}) collective-permute-start(bf16[32,1664]{1,0:T(8,128)(2,1)S(1)} %get-tuple-element.48), channel_id=1, source_target_pairs={{0,2},{2,0},{4,6},{6,4},{8,10},{10,8},{12,14},{14,12},{1,3},{3,1},... | collective-permute-start | bytes 319496 | tf_op jit(solution)/shard_map/ppermute | solution.py:364
  8.0 12.8 %collective-permute-start.5 = (bf16[32,1664]{1,0:T(8,128)(2,1)S(1)}, bf16[32,1664]{1,0:T(8,128)(2,1)S(1)}, u32[]{:S(2)}, u32[]{:S(2)}) collective-permute-start(bf16[32,1664]{1,0:T(8,128)(2,1)S(1)} %get-tuple-element.49), channel_id=1, source_target_pairs={{0,4},{2,6},{4,0},{6,2},{8,12},{10,14},{12,8},{14,10},{1,5},{3,7},... | collective-permute-start | bytes 319496 | tf_op jit(solution)/shard_map/ppermute | solution.py:364
  10.4 10.4 %collective-permute-start.6 = (bf16[32,1664]{1,0:T(8,128)(2,1)S(1)}, bf16[32,1664]{1,0:T(8,128)(2,1)S(1)}, u32[]{:S(2)}, u32[]{:S(2)}) collective-permute-start(bf16[32,1664]{1,0:T(8,128)(2,1)S(1)} %get-tuple-element.50), channel_id=1, source_target_pairs={{0,6},{2,4},{4,2},{6,0},{8,14},{10,12},{12,10},{14,8},{1,7},{3,5},... | collective-permute-start | bytes 319496 | tf_op jit(solution)/shard_map/ppermute | solution.py:364
  13.6 15.1 %collective-permute-start.8 = (bf16[64,1536]{1,0:T(8,128)(2,1)S(1)}, bf16[64,1536]{1,0:T(8,128)(2,1)S(1)}, u32[]{:S(2)}, u32[]{:S(2)}) collective-permute-start(bf16[64,1536]{1,0:T(8,128)(2,1)S(1)} %shard_map.93._), channel_id=1, source_target_pairs={{0,8},{2,10},{4,12},{6,14},{8,0},{10,2},{12,4},{14,6},{1,9},{3,11}... | collective-permute-start | bytes 589832 | tf_op jit(solution)/shard_map/ppermute | solution.py:306
  18.1 8.2 %collective-permute-start.3 = (bf16[128,1536]{1,0:T(8,128)(2,1)S(1)}, bf16[128,1536]{1,0:T(8,128)(2,1)S(1)}, u32[]{:S(2)}, u32[]{:S(2)}) collective-permute-start(bf16[128,1536]{1,0:T(8,128)(2,1)S(1)} %shard_map.94.refs_4_), channel_id=1, source_target_pairs={{0,16},{16,0},{1,17},{17,1},{2,18},{18,2},{3,19},{19,3},{4,20},{20... | collective-permute-start | bytes 1179656 | tf_op jit(solution)/shard_map/ppermute | solution.py:306
  20.8 5.4 %copy-start.1 = (bf16[1,32,8,1536]{3,2,1,0:T(8,128)(2,1)S(1)}, bf16[1,32,8,1536]{3,2,1,0:T(8,128)(2,1)}, u32[]{:S(2)}) copy-start(bf16[1,32,8,1536]{3,2,1,0:T(8,128)(2,1)} %param.10) | copy-start | bytes 2359300
  20.8 5.4 %copy-start.2 = (f32[24]{0:T(128)S(1)}, f32[24]{0:T(128)}, u32[]{:S(2)}) copy-start(f32[24]{0:T(128)} %param.16) | copy-start | bytes 292
  23.2 9.4 %collective-permute-start.7 = (bf16[64,1536]{1,0:T(8,128)(2,1)S(1)}, bf16[64,1536]{1,0:T(8,128)(2,1)S(1)}, u32[]{:S(2)}, u32[]{:S(2)}) collective-permute-start(bf16[64,1536]{1,0:T(8,128)(2,1)S(1)} %shard_map.98), channel_id=1, source_target_pairs={{0,8},{2,10},{4,12},{6,14},{8,0},{10,2},{12,4},{14,6},{1,9},{3,11}... | collective-permute-start | bytes 589832 | tf_op jit(solution)/shard_map/ppermute | solution.py:306
  29.0 6.6 %collective-permute-start.12 = (bf16[32,1536]{1,0:T(8,128)(2,1)S(1)}, bf16[32,1536]{1,0:T(8,128)(2,1)S(1)}, u32[]{:S(2)}, u32[]{:S(2)}) collective-permute-start(bf16[32,1536]{1,0:T(8,128)(2,1)S(1)} %get-tuple-element.62), channel_id=1, source_target_pairs={{0,2},{2,0},{4,6},{6,4},{8,10},{10,8},{12,14},{14,12},{1,3},{3,1},... | collective-permute-start | bytes 294920 | tf_op jit(solution)/shard_map/ppermute | solution.py:364
  30.2 6.3 %collective-permute-start.13 = (bf16[32,1536]{1,0:T(8,128)(2,1)S(1)}, bf16[32,1536]{1,0:T(8,128)(2,1)S(1)}, u32[]{:S(2)}, u32[]{:S(2)}) collective-permute-start(bf16[32,1536]{1,0:T(8,128)(2,1)S(1)} %get-tuple-element.63), channel_id=1, source_target_pairs={{0,4},{2,6},{4,0},{6,2},{8,12},{10,14},{12,8},{14,10},{1,5},{3,7},... | collective-permute-start | bytes 294920 | tf_op jit(solution)/shard_map/ppermute | solution.py:364
  31.7 5.5 %collective-permute-start.14 = (bf16[32,1536]{1,0:T(8,128)(2,1)S(1)}, bf16[32,1536]{1,0:T(8,128)(2,1)S(1)}, u32[]{:S(2)}, u32[]{:S(2)}) collective-permute-start(bf16[32,1536]{1,0:T(8,128)(2,1)S(1)} %get-tuple-element.64), channel_id=1, source_target_pairs={{0,6},{2,4},{4,2},{6,0},{8,14},{10,12},{12,10},{14,8},{1,7},{3,5},... | collective-permute-start | bytes 294920 | tf_op jit(solution)/shard_map/ppermute | solution.py:364
  32.6 3.9 %copy-start.3 = (f32[1536]{0:T(1024)S(1)}, f32[1536]{0:T(1024)}, u32[]{:S(2)}) copy-start(f32[1536]{0:T(1024)} %param.17) | copy-start | bytes 18436
  32.9 5.2 %collective-permute-start.10 = (bf16[32,1536]{1,0:T(8,128)(2,1)S(1)}, bf16[32,1536]{1,0:T(8,128)(2,1)S(1)}, u32[]{:S(2)}, u32[]{:S(2)}) collective-permute-start(bf16[32,1536]{1,0:T(8,128)(2,1)S(1)} %get-tuple-element.60), channel_id=1, source_target_pairs={{0,4},{2,6},{4,0},{6,2},{8,12},{10,14},{12,8},{14,10},{1,5},{3,7},... | collective-permute-start | bytes 294920 | tf_op jit(solution)/shard_map/ppermute | solution.py:364
  34.1 5.6 %collective-permute-start.11 = (bf16[32,1536]{1,0:T(8,128)(2,1)S(1)}, bf16[32,1536]{1,0:T(8,128)(2,1)S(1)}, u32[]{:S(2)}, u32[]{:S(2)}) collective-permute-start(bf16[32,1536]{1,0:T(8,128)(2,1)S(1)} %get-tuple-element.61), channel_id=1, source_target_pairs={{0,6},{2,4},{4,2},{6,0},{8,14},{10,12},{12,10},{14,8},{1,7},{3,5},... | collective-permute-start | bytes 294920 | tf_op jit(solution)/shard_map/ppermute | solution.py:364
  35.6 5.1 %collective-permute-start.9 = (bf16[32,1536]{1,0:T(8,128)(2,1)S(1)}, bf16[32,1536]{1,0:T(8,128)(2,1)S(1)}, u32[]{:S(2)}, u32[]{:S(2)}) collective-permute-start(bf16[32,1536]{1,0:T(8,128)(2,1)S(1)} %get-tuple-element.59), channel_id=1, source_target_pairs={{0,2},{2,0},{4,6},{6,4},{8,10},{10,8},{12,14},{14,12},{1,3},{3,1},... | collective-permute-start | bytes 294920 | tf_op jit(solution)/shard_map/ppermute | solution.py:364

commit v14 on v13

--- a/solution.py
+++ b/solution.py
@@ -252,19 +252,30 @@
             out[:, part] = y[i * rows : (i + 1) * rows].astype(BF16)
 
 
-def col_out_kernel(params_ref, s_ref, x_ref, raw_ref, maps_ref, gate_ref, skip_ref, w_ref, g_ref, *, cols, heads, state, width):
+def col_local_kernel(
+    params_ref, x_ref, raw_ref, maps_ref, gate_ref, skip_ref, _, y_ref, g_ref, fade_ref, entry_ref,
+    *, cols, heads, state, width
+):
     scan = col_scan(params_ref, raw_ref, maps_ref, cols, heads, state)
-    mix = jnp.concatenate([scan.within(), scan.entry(lax.axis_index("row") > 0)], axis=1)
+    mix = scan.within()
+    fade_ref[...] = scan.fade
+    entry_ref[...] = scan.entry(lax.axis_index("row") > 0)
     skips = parts(jnp.broadcast_to(skip_ref[...], (8, heads)), 2)
-    for first, count in strips(s_ref.shape[1]):
+    for first, count in strips(x_ref.shape[1]):
         pick = picks(heads, width, first, count)
         part = slice(first, first + count)
         x = x_ref[:, part].astype(F32)
         values = (x * dot(scan.grow, pick)).astype(BF16)
-        y = dot(mix, jnp.concatenate([values, s_ref[:, part]], axis=0)) * dot(scan.fade, pick)
-        w_ref[:, part] = y + dot(skips, pick)[0:1, :] * x
+        y_ref[:, part] = dot(mix, values) * dot(scan.fade, pick) + dot(skips, pick)[0:1, :] * x
         gate = gate_ref[:, part].astype(F32)
         g_ref[:, part] = gate / (1.0 + jnp.exp(-gate))
+
+
+def col_out_kernel(s_ref, y_ref, fade_ref, entry_ref, w_ref, *, heads, width):
+    for first, count in strips(s_ref.shape[1]):
+        pick = picks(heads, width, first, count)
+        part = slice(first, first + count)
+        w_ref[:, part] = y_ref[:, part] + dot(entry_ref[...], s_ref[:, part]) * dot(fade_ref[...], pick)
 
 
 def final_kernel(w_ref, g_ref, gain_ref, *refs, group, axis, offset, share):
@@ -418,19 +429,30 @@
             entering = entering_states(made[j], factor, "col", col_count, group, width)
             parts_of.append((sum(map(sum, pieces[:i])) + offsets[j], rows, known[j], entering))
 
-    w, silu = call(
-        functools.partial(col_out_kernel, **sizes),
-        [pltpu.VMEM((tokens, channels), F32)] * 2,
+    y_col, silu, *known = call(
+        functools.partial(col_local_kernel, **sizes),
+        [
+            pltpu.VMEM((tokens, channels), F32),
+            pltpu.VMEM((tokens, channels), F32),
+            pltpu.VMEM((tokens, 2 * heads), BF16),
+            pltpu.VMEM((tokens, cols * state), BF16),
+        ],
         0,
-    )(params, col_entering, x, raw, maps, gate, skip.reshape(1, heads))
+        specs=[None] * 6 + [any_spec],
+    )(params, x, raw, maps, gate, skip.reshape(1, heads), before)
+    w = call(
+        functools.partial(col_out_kernel, heads=heads, width=width),
+        pltpu.VMEM((tokens, channels), F32),
+        0,
+    )(col_entering, y_col, *known)
 
     back = []
-    before = w
+    before = y_col
     for _, rows, known, entering in parts_of:
         y_row = call(
             functools.partial(row_out_kernel, heads=heads, width=width),
             [pltpu.VMEM((rows, channels), BF16)] * group,
-            20 if back else 0,
+            0,
             specs=[None] * 4 + [any_spec],
         )(entering, *known, before)
         back.append(exchange(y_row))

time: 41.7 us -> 42.7 us (1.024)
  the two profiles are of different devices: /device:TPU:0 before, /device:TPU:22 now
where the time goes in v14:
time: 42.7 us; the launch traced here: 42.6 us
  starting transfers between devices  22.9 us (54%)
  Pallas kernels  13.1 us (31%)
  waiting for transfers between devices  5.73 us (13%)
  between operations  0.84 us (2%)
    ppermute x12, starting transfers between devices, exchange(): lax.ppermute(blocks[i], 'col', [(at, partner(at, i, group)) for at in ran...  19.2 us
    ppermute x12, waiting for transfers between devices, exchange(): lax.ppermute(blocks[i], 'col', [(at, partner(at, i, group)) for at in ran...  5.72 us
    ppermute x3, starting transfers between devices, entering_states(): entering = lax.ppermute(ends, axis, onward)  3.67 us
    pallas_call x2, Pallas kernels, of_own(): call(functools.partial(row_local_kernel, offset=offset, **sizes, **shared...  2.43 us
    pallas_call x2, Pallas kernels, body(): call(functools.partial(row_state_kernel, count=len(piece), **sizes, **sha...  2.22 us
    pallas_call x1, Pallas kernels, body(): call(functools.partial(col_local_kernel, **sizes), [pltpu.VMEM((tokens, c...  2.16 us
    pallas_call x2, Pallas kernels, body(): call(functools.partial(final_kernel, offset=first, share=share, **shared)...  1.89 us
    pallas_call x1, Pallas kernels, body(): call(functools.partial(col_state_kernel, **sizes), state_shapes([cols * s...  1.48 us
  transfers between devices with their start and end apart: 15, of which 3 were waited for; matrix products, arithmetic and copies ran while one was open for 0% of the time, Pallas kernels for 25%

profile of v14, /device:TPU:22, one launch (start us, length us, event | category | flops | bytes accessed | tf_op | source)
XLA Modules:
  0.0 42.6 jit_solution(9551385398269052367)
XLA Ops:
  0.0 0.0 copy-start
  0.0 1.5 %shard_map.91 = (bf16[256,48]{1,0:T(8,128)(2,1)S(1)}, bf16[256,64]{1,0:T(8,128)(2,1)S(1)}, f32[48,1000]{1,0:T(8,128)S(1)}, f32[2,24]{1,0:T(2,128)S(1)}, bf16[32,...) custom-call(bf16[256,1536]{1,0:T(8,128)(2,1)} %bitcast.7, ...), custom_call_target="tpu_custom_call" | custom-call | flops 1000001024 | bytes 1024 | tf_op jit(solution)/shard_map/pallas_call | solution.py:347
  1.5 0.6 %collective-permute-start = (bf16[32,1664]{1,0:T(8,128)(2,1)S(1)}, bf16[32,1664]{1,0:T(8,128)(2,1)S(1)}, u32[]{:S(2)}, u32[]{:S(2)}) collective-permute-start(bf16[32,1664]{1,0:T(8,128)(2,1)S(1)} %get-tuple-element.44), channel_id=1, source_target_pairs={{0,2},{2,0},{4,6},{6,4},{8,10},{10,8},{12,14},{14,12},{1,3},{3,1},... | collective-permute-start | bytes 319496 | tf_op jit(solution)/shard_map/ppermute | solution.py:375
  2.1 1.6 %collective-permute-start.1 = (bf16[32,1664]{1,0:T(8,128)(2,1)S(1)}, bf16[32,1664]{1,0:T(8,128)(2,1)S(1)}, u32[]{:S(2)}, u32[]{:S(2)}) collective-permute-start(bf16[32,1664]{1,0:T(8,128)(2,1)S(1)} %get-tuple-element.45), channel_id=1, source_target_pairs={{0,4},{2,6},{4,0},{6,2},{8,12},{10,14},{12,8},{14,10},{1,5},{3,7},... | collective-permute-start | bytes 319496 | tf_op jit(solution)/shard_map/ppermute | solution.py:375
  3.6 1.4 %collective-permute-start.2 = (bf16[32,1664]{1,0:T(8,128)(2,1)S(1)}, bf16[32,1664]{1,0:T(8,128)(2,1)S(1)}, u32[]{:S(2)}, u32[]{:S(2)}) collective-permute-start(bf16[32,1664]{1,0:T(8,128)(2,1)S(1)} %get-tuple-element.46), channel_id=1, source_target_pairs={{0,6},{2,4},{4,2},{6,0},{8,14},{10,12},{12,10},{14,8},{1,7},{3,5},... | collective-permute-start | bytes 319496 | tf_op jit(solution)/shard_map/ppermute | solution.py:375
  5.0 0.5 %collective-permute-start.4 = (bf16[32,1664]{1,0:T(8,128)(2,1)S(1)}, bf16[32,1664]{1,0:T(8,128)(2,1)S(1)}, u32[]{:S(2)}, u32[]{:S(2)}) collective-permute-start(bf16[32,1664]{1,0:T(8,128)(2,1)S(1)} %get-tuple-element.48), channel_id=1, source_target_pairs={{0,2},{2,0},{4,6},{6,4},{8,10},{10,8},{12,14},{14,12},{1,3},{3,1},... | collective-permute-start | bytes 319496 | tf_op jit(solution)/shard_map/ppermute | solution.py:375
  5.5 1.6 %collective-permute-start.5 = (bf16[32,1664]{1,0:T(8,128)(2,1)S(1)}, bf16[32,1664]{1,0:T(8,128)(2,1)S(1)}, u32[]{:S(2)}, u32[]{:S(2)}) collective-permute-start(bf16[32,1664]{1,0:T(8,128)(2,1)S(1)} %get-tuple-element.49), channel_id=1, source_target_pairs={{0,4},{2,6},{4,0},{6,2},{8,12},{10,14},{12,8},{14,10},{1,5},{3,7},... | collective-permute-start | bytes 319496 | tf_op jit(solution)/shard_map/ppermute | solution.py:375
  7.8 0.2 shard_map.92.params_ref.refs_4_
  8.0 0.0 collective-permute-done.refs_1_
  8.0 1.4 %collective-permute-start.6 = (bf16[32,1664]{1,0:T(8,128)(2,1)S(1)}, bf16[32,1664]{1,0:T(8,128)(2,1)S(1)}, u32[]{:S(2)}, u32[]{:S(2)}) collective-permute-start(bf16[32,1664]{1,0:T(8,128)(2,1)S(1)} %get-tuple-element.50), channel_id=1, source_target_pairs={{0,6},{2,4},{4,2},{6,0},{8,14},{10,12},{12,10},{14,8},{1,7},{3,5},... | collective-permute-start | bytes 319496 | tf_op jit(solution)/shard_map/ppermute | solution.py:375
  9.4 0.0 collective-permute-done.1.refs_2_
  9.4 1.8 %collective-permute-done.2.refs_3_ = bf16[32,1664]{1,0:T(8,128)(2,1)S(1)} collective-permute-done((bf16[32,1664]{1,0:T(8,128)(2,1)S(1)}, bf16[32,1664]{1,0:T(8,128)(2,1)S(1)}, u32[]{:S(2)}, u32[]{:S(2)}) %collective-permute-start.2) | collective-permute-done | bytes 106528 | tf_op jit(solution)/shard_map/ppermute | solution.py:375
  11.2 1.1 %shard_map.93._ = bf16[64,1536]{1,0:T(8,128)(2,1)S(1)} custom-call(f32[8,48]{1,0:T(8,128)S(1)} %shard_map.92.params_ref.refs_4_, bf16[32,1664]{1,0:T(8,128)(2,1)S(1)} %get-tuple-element.43.refs_0_, bf16[32,1664]{1,0:T(8,128)(2,1)S(1)} %collective-permute-done.refs_1_, bf16[32,1664]{1,0:T(8,128)(2,1)S(1)} %collective-permute-done.1.refs_2_, ...), custom_call_target="tpu_custom_call" | custom-call | flops 1024 | bytes 1024 | tf_op jit(solution)/shard_map/pallas_call | solution.py:410
  12.3 0.4 collective-permute-start.8
  12.7 0.0 copy-done
  12.7 1.5 %shard_map.94.refs_4_ = bf16[128,1536]{1,0:T(8,128)(2,1)S(1)} custom-call(f32[8,48]{1,0:T(8,128)S(1)} %shard_map.92.params_ref.refs_4_, bf16[256,1536]{1,0:T(8,128)(2,1)S(1)} %bitcast.8, bf16[256,48]{1,0:T(8,128)(2,1)S(1)} %get-tuple-element.41.raw_ref, bf16[256,64]{1,0:T(8,128)(2,1)S(1)} %get-tuple-element.42.maps_ref, bf16[64,1536]{1,0:T(8,128)(2,1)S(1)} %shard_map.93._), custom_call_target="tpu_custom_call" | custom-call | flops 1024 | bytes 1024 | tf_op jit(solution)/shard_map/pallas_call | solution.py:418
  14.2 0.6 %collective-permute-start.3 = (bf16[128,1536]{1,0:T(8,128)(2,1)S(1)}, bf16[128,1536]{1,0:T(8,128)(2,1)S(1)}, u32[]{:S(2)}, u32[]{:S(2)}) collective-permute-start(bf16[128,1536]{1,0:T(8,128)(2,1)S(1)} %shard_map.94.refs_4_), channel_id=1, source_target_pairs={{0,16},{16,0},{1,17},{17,1},{2,18},{18,2},{3,19},{19,3},{4,20},{20... | collective-permute-start | bytes 1179656 | tf_op jit(solution)/shard_map/ppermute | solution.py:317
  14.8 1.2 %shard_map.95 = (f32[128,1536]{1,0:T(8,128)S(1)}, bf16[128,48]{1,0:T(8,128)(2,1)S(1)}, bf16[128,64]{1,0:T(8,128)(2,1)S(1)}) custom-call(f32[8,48]{1,0:T(8,128)S(1)} %shard_map.92.params_ref.refs_4_, bf16[32,1664]{1,0:T(8,128)(2,1)S(1)} %get-tuple-element.43.refs_0_, bf16[32,1664]{1,0:T(8,128)(2,1)S(1)} %collective-permute-done.refs_1_, ...), custom_call_target="tpu_custom_call" | custom-call | flops 2000001024 | bytes 1024 | tf_op jit(solution)/shard_map/pallas_call | solution.py:394
  16.0 0.0 collective-permute-done.4.refs_1_
  16.0 0.0 collective-permute-done.5.refs_2_
  16.0 0.0 collective-permute-done.6.refs_3_
  16.0 0.0 copy-start.1
  16.0 0.0 copy-start.2
  16.0 1.2 %shard_map.96 = (f32[128,1536]{1,0:T(8,128)S(1)}, bf16[128,48]{1,0:T(8,128)(2,1)S(1)}, bf16[128,64]{1,0:T(8,128)(2,1)S(1)}) custom-call(f32[8,48]{1,0:T(8,128)S(1)} %shard_map.92.params_ref.refs_4_, bf16[32,1664]{1,0:T(8,128)(2,1)S(1)} %get-tuple-element.47.refs_0_, bf16[32,1664]{1,0:T(8,128)(2,1)S(1)} %collective-permute-done.4.refs_1_, ...), custom_call_target="tpu_custom_call" | custom-call | flops 2000001024 | bytes 1024 | tf_op jit(solution)/shard_map/pallas_call | solution.py:394
  17.3 1.1 %shard_map.97._ = bf16[64,1536]{1,0:T(8,128)(2,1)S(1)} custom-call(f32[8,48]{1,0:T(8,128)S(1)} %shard_map.92.params_ref.refs_4_, bf16[32,1664]{1,0:T(8,128)(2,1)S(1)} %get-tuple-element.47.refs_0_, bf16[32,1664]{1,0:T(8,128)(2,1)S(1)} %collective-permute-done.4.refs_1_, bf16[32,1664]{1,0:T(8,128)(2,1)S(1)} %collective-permute-done.5.refs_2_, ...), custom_call_target="tpu_custom_call" | custom-call | flops 1024 | bytes 1024 | tf_op jit(solution)/shard_map/pallas_call | solution.py:410
  18.4 2.7 %collective-permute-start.7 = (bf16[64,1536]{1,0:T(8,128)(2,1)S(1)}, bf16[64,1536]{1,0:T(8,128)(2,1)S(1)}, u32[]{:S(2)}, u32[]{:S(2)}) collective-permute-start(bf16[64,1536]{1,0:T(8,128)(2,1)S(1)} %shard_map.97._), channel_id=1, source_target_pairs={{0,8},{2,10},{4,12},{6,14},{8,0},{10,2},{12,4},{14,6},{1,9},{3,11}... | collective-permute-start | bytes 589832 | tf_op jit(solution)/shard_map/ppermute | solution.py:317
  21.1 0.0 copy-done.1
  21.1 0.0 copy-done.2
  21.1 2.2 %shard_map.98 = (f32[256,1536]{1,0:T(8,128)S(1)}, f32[256,1536]{1,0:T(8,128)S(1)}, bf16[256,48]{1,0:T(8,128)(2,1)S(1)}, bf16[256,128]{1,0:T(8,128)(2,1)S(1)}) custom-call(f32[8,48]{1,0:T(8,128)S(1)} %shard_map.92.params_ref.refs_4_, bf16[256,1536]{1,0:T(8,128)(2,1)S(1)} %bitcast.9, bf16[256,48]{1,0:T(8,128)(2,1)S(1)} %get-tuple-element.41.raw_ref, ...), custom_call_target="tpu_custom_call" | custom-call | flops 1024 | bytes 1024 | tf_op jit(solution)/shard_map/pallas_call | solution.py:432
  23.2 0.0 collective-permute-done.8.s_ref
  23.2 0.0 copy-start.3
  23.3 0.4 shard_map.100
  23.6 0.7 %collective-permute-start.12 = (bf16[32,1536]{1,0:T(8,128)(2,1)S(1)}, bf16[32,1536]{1,0:T(8,128)(2,1)S(1)}, u32[]{:S(2)}, u32[]{:S(2)}) collective-permute-start(bf16[32,1536]{1,0:T(8,128)(2,1)S(1)} %get-tuple-element.66), channel_id=1, source_target_pairs={{0,2},{2,0},{4,6},{6,4},{8,10},{10,8},{12,14},{14,12},{1,3},{3,1},... | collective-permute-start | bytes 294920 | tf_op jit(solution)/shard_map/ppermute | solution.py:375
  24.4 5.7 %collective-permute-start.13 = (bf16[32,1536]{1,0:T(8,128)(2,1)S(1)}, bf16[32,1536]{1,0:T(8,128)(2,1)S(1)}, u32[]{:S(2)}, u32[]{:S(2)}) collective-permute-start(bf16[32,1536]{1,0:T(8,128)(2,1)S(1)} %get-tuple-element.67), channel_id=1, source_target_pairs={{0,4},{2,6},{4,0},{6,2},{8,12},{10,14},{12,8},{14,10},{1,5},{3,7},... | collective-permute-start | bytes 294920 | tf_op jit(solution)/shard_map/ppermute | solution.py:375
  30.1 0.9 %collective-permute-start.14 = (bf16[32,1536]{1,0:T(8,128)(2,1)S(1)}, bf16[32,1536]{1,0:T(8,128)(2,1)S(1)}, u32[]{:S(2)}, u32[]{:S(2)}) collective-permute-start(bf16[32,1536]{1,0:T(8,128)(2,1)S(1)} %get-tuple-element.68), channel_id=1, source_target_pairs={{0,6},{2,4},{4,2},{6,0},{8,14},{10,12},{12,10},{14,8},{1,7},{3,5},... | collective-permute-start | bytes 294920 | tf_op jit(solution)/shard_map/ppermute | solution.py:375
  30.9 0.0 collective-permute-done.7.s_ref
  31.0 0.3 shard_map.101
  31.3 0.6 %collective-permute-start.9 = (bf16[32,1536]{1,0:T(8,128)(2,1)S(1)}, bf16[32,1536]{1,0:T(8,128)(2,1)S(1)}, u32[]{:S(2)}, u32[]{:S(2)}) collective-permute-start(bf16[32,1536]{1,0:T(8,128)(2,1)S(1)} %get-tuple-element.63), channel_id=1, source_target_pairs={{0,2},{2,0},{4,6},{6,4},{8,10},{10,8},{12,14},{14,12},{1,3},{3,1},... | collective-permute-start | bytes 294920 | tf_op jit(solution)/shard_map/ppermute | solution.py:375
  31.9 0.0 collective-permute-done.12.refs_1_
  31.9 4.2 %collective-permute-start.10 = (bf16[32,1536]{1,0:T(8,128)(2,1)S(1)}, bf16[32,1536]{1,0:T(8,128)(2,1)S(1)}, u32[]{:S(2)}, u32[]{:S(2)}) collective-permute-start(bf16[32,1536]{1,0:T(8,128)(2,1)S(1)} %get-tuple-element.64), channel_id=1, source_target_pairs={{0,4},{2,6},{4,0},{6,2},{8,12},{10,14},{12,8},{14,10},{1,5},{3,7},... | collective-permute-start | bytes 294920 | tf_op jit(solution)/shard_map/ppermute | solution.py:375
  36.1 0.0 collective-permute-done.3.s_ref
  36.1 0.0 collective-permute-start.11
  36.1 0.0 copy-done.3
  36.2 0.6 %shard_map.99.w_ref = f32[256,1536]{1,0:T(8,128)S(1)} custom-call(bf16[128,1536]{1,0:T(8,128)(2,1)S(1)} %collective-permute-done.3.s_ref, f32[256,1536]{1,0:T(8,128)S(1)} %get-tuple-element.53.y_ref._, bf16[256,48]{1,0:T(8,128)(2,1)S(1)} %get-tuple-element.54.fade_ref, bf16[256,128]{1,0:T(8,128)(2,1)S(1)} %get-tuple-element.55.entry_ref), custom_call_target="tpu_custom_call" | custom-call | flops 1024 | bytes 1024 | tf_op jit(solution)/shard_map/pallas_call | solution.py:443
  36.7 0.0 collective-permute-done.13.refs_2_
  36.8 0.0 collective-permute-done.14.refs_3_
  36.8 0.9 %shard_map.102.refs_4_ = bf16[256,1536]{1,0:T(8,128)(2,1)} custom-call(f32[256,1536]{1,0:T(8,128)S(1)} %shard_map.99.w_ref, f32[256,1536]{1,0:T(8,128)S(1)} %get-tuple-element.56.g_ref, f32[1,1536]{1,0:T(1,128)S(1)} %reshape.27.gain_ref, bf16[32,1536]{1,0:T(8,128)(2,1)S(1)} %get-tuple-element.61._.refs_0_, ...), custom_call_target="tpu_custom_call" | custom-call | flops 1024 | bytes 1024 | tf_op jit(solution)/shard_map/pallas_call | solution.py:464
  37.7 0.0 collective-permute-done.9.refs_1_
  37.7 1.0 %collective-permute-done.10.refs_2_ = bf16[32,1536]{1,0:T(8,128)(2,1)S(1)} collective-permute-done((bf16[32,1536]{1,0:T(8,128)(2,1)S(1)}, bf16[32,1536]{1,0:T(8,128)(2,1)S(1)}, u32[]{:S(2)}, u32[]{:S(2)}) %collective-permute-start.10) | collective-permute-done | bytes 98336 | tf_op jit(solution)/shard_map/ppermute | solution.py:375
  38.7 2.9 %collective-permute-done.11.refs_3_ = bf16[32,1536]{1,0:T(8,128)(2,1)S(1)} collective-permute-done((bf16[32,1536]{1,0:T(8,128)(2,1)S(1)}, bf16[32,1536]{1,0:T(8,128)(2,1)S(1)}, u32[]{:S(2)}, u32[]{:S(2)}) %collective-permute-start.11) | collective-permute-done | bytes 98336 | tf_op jit(solution)/shard_map/ppermute | solution.py:375
  41.6 0.9 %shard_map.103 = bf16[256,1536]{1,0:T(8,128)(2,1)} custom-call(f32[256,1536]{1,0:T(8,128)S(1)} %shard_map.99.w_ref, f32[256,1536]{1,0:T(8,128)S(1)} %get-tuple-element.56.g_ref, f32[1,1536]{1,0:T(1,128)S(1)} %reshape.27.gain_ref, bf16[32,1536]{1,0:T(8,128)(2,1)S(1)} %get-tuple-element.62.refs_0_, ...), custom_call_target="tpu_custom_call", output_to_operand_aliasing={{}: (7, {})} | custom-call | flops 1024 | bytes 1024 | tf_op jit(solution)/shard_map/pallas_call | solution.py:464
  (1 shorter events, 0.0 us)
Async XLA Ops:
  0.0 12.7 %copy-start = (bf16[1,32,8,1536]{3,2,1,0:T(8,128)(2,1)S(1)}, bf16[1,32,8,1536]{3,2,1,0:T(8,128)(2,1)}, u32[]{:S(2)}) copy-start(bf16[1,32,8,1536]{3,2,1,0:T(8,128)(2,1)} %param.9) | copy-start | bytes 2359300
  1.5 6.5 %collective-permute-start = (bf16[32,1664]{1,0:T(8,128)(2,1)S(1)}, bf16[32,1664]{1,0:T(8,128)(2,1)S(1)}, u32[]{:S(2)}, u32[]{:S(2)}) collective-permute-start(bf16[32,1664]{1,0:T(8,128)(2,1)S(1)} %get-tuple-element.44), channel_id=1, source_target_pairs={{0,2},{2,0},{4,6},{6,4},{8,10},{10,8},{12,14},{14,12},{1,3},{3,1},... | collective-permute-start | bytes 319496 | tf_op jit(solution)/shard_map/ppermute | solution.py:375
  2.1 7.3 %collective-permute-start.1 = (bf16[32,1664]{1,0:T(8,128)(2,1)S(1)}, bf16[32,1664]{1,0:T(8,128)(2,1)S(1)}, u32[]{:S(2)}, u32[]{:S(2)}) collective-permute-start(bf16[32,1664]{1,0:T(8,128)(2,1)S(1)} %get-tuple-element.45), channel_id=1, source_target_pairs={{0,4},{2,6},{4,0},{6,2},{8,12},{10,14},{12,8},{14,10},{1,5},{3,7},... | collective-permute-start | bytes 319496 | tf_op jit(solution)/shard_map/ppermute | solution.py:375
  3.6 7.5 %collective-permute-start.2 = (bf16[32,1664]{1,0:T(8,128)(2,1)S(1)}, bf16[32,1664]{1,0:T(8,128)(2,1)S(1)}, u32[]{:S(2)}, u32[]{:S(2)}) collective-permute-start(bf16[32,1664]{1,0:T(8,128)(2,1)S(1)} %get-tuple-element.46), channel_id=1, source_target_pairs={{0,6},{2,4},{4,2},{6,0},{8,14},{10,12},{12,10},{14,8},{1,7},{3,5},... | collective-permute-start | bytes 319496 | tf_op jit(solution)/shard_map/ppermute | solution.py:375
  5.0 10.9 %collective-permute-start.4 = (bf16[32,1664]{1,0:T(8,128)(2,1)S(1)}, bf16[32,1664]{1,0:T(8,128)(2,1)S(1)}, u32[]{:S(2)}, u32[]{:S(2)}) collective-permute-start(bf16[32,1664]{1,0:T(8,128)(2,1)S(1)} %get-tuple-element.48), channel_id=1, source_target_pairs={{0,2},{2,0},{4,6},{6,4},{8,10},{10,8},{12,14},{14,12},{1,3},{3,1},... | collective-permute-start | bytes 319496 | tf_op jit(solution)/shard_map/ppermute | solution.py:375
  5.5 10.4 %collective-permute-start.5 = (bf16[32,1664]{1,0:T(8,128)(2,1)S(1)}, bf16[32,1664]{1,0:T(8,128)(2,1)S(1)}, u32[]{:S(2)}, u32[]{:S(2)}) collective-permute-start(bf16[32,1664]{1,0:T(8,128)(2,1)S(1)} %get-tuple-element.49), channel_id=1, source_target_pairs={{0,4},{2,6},{4,0},{6,2},{8,12},{10,14},{12,8},{14,10},{1,5},{3,7},... | collective-permute-start | bytes 319496 | tf_op jit(solution)/shard_map/ppermute | solution.py:375
  8.0 8.0 %collective-permute-start.6 = (bf16[32,1664]{1,0:T(8,128)(2,1)S(1)}, bf16[32,1664]{1,0:T(8,128)(2,1)S(1)}, u32[]{:S(2)}, u32[]{:S(2)}) collective-permute-start(bf16[32,1664]{1,0:T(8,128)(2,1)S(1)} %get-tuple-element.50), channel_id=1, source_target_pairs={{0,6},{2,4},{4,2},{6,0},{8,14},{10,12},{12,10},{14,8},{1,7},{3,5},... | collective-permute-start | bytes 319496 | tf_op jit(solution)/shard_map/ppermute | solution.py:375
  12.3 11.0 %collective-permute-start.8 = (bf16[64,1536]{1,0:T(8,128)(2,1)S(1)}, bf16[64,1536]{1,0:T(8,128)(2,1)S(1)}, u32[]{:S(2)}, u32[]{:S(2)}) collective-permute-start(bf16[64,1536]{1,0:T(8,128)(2,1)S(1)} %shard_map.93._), channel_id=1, source_target_pairs={{0,8},{2,10},{4,12},{6,14},{8,0},{10,2},{12,4},{14,6},{1,9},{3,11}... | collective-permute-start | bytes 589832 | tf_op jit(solution)/shard_map/ppermute | solution.py:317
  14.2 22.0 %collective-permute-start.3 = (bf16[128,1536]{1,0:T(8,128)(2,1)S(1)}, bf16[128,1536]{1,0:T(8,128)(2,1)S(1)}, u32[]{:S(2)}, u32[]{:S(2)}) collective-permute-start(bf16[128,1536]{1,0:T(8,128)(2,1)S(1)} %shard_map.94.refs_4_), channel_id=1, source_target_pairs={{0,16},{16,0},{1,17},{17,1},{2,18},{18,2},{3,19},{19,3},{4,20},{20... | collective-permute-start | bytes 1179656 | tf_op jit(solution)/shard_map/ppermute | solution.py:317
  16.0 5.1 %copy-start.1 = (bf16[1,32,8,1536]{3,2,1,0:T(8,128)(2,1)S(1)}, bf16[1,32,8,1536]{3,2,1,0:T(8,128)(2,1)}, u32[]{:S(2)}) copy-start(bf16[1,32,8,1536]{3,2,1,0:T(8,128)(2,1)} %param.10) | copy-start | bytes 2359300
  16.0 5.0 %copy-start.2 = (f32[24]{0:T(128)S(1)}, f32[24]{0:T(128)}, u32[]{:S(2)}) copy-start(f32[24]{0:T(128)} %param.16) | copy-start | bytes 292
  18.4 12.6 %collective-permute-start.7 = (bf16[64,1536]{1,0:T(8,128)(2,1)S(1)}, bf16[64,1536]{1,0:T(8,128)(2,1)S(1)}, u32[]{:S(2)}, u32[]{:S(2)}) collective-permute-start(bf16[64,1536]{1,0:T(8,128)(2,1)S(1)} %shard_map.97._), channel_id=1, source_target_pairs={{0,8},{2,10},{4,12},{6,14},{8,0},{10,2},{12,4},{14,6},{1,9},{3,11}... | collective-permute-start | bytes 589832 | tf_op jit(solution)/shard_map/ppermute | solution.py:317
  23.2 12.9 %copy-start.3 = (f32[1536]{0:T(1024)S(1)}, f32[1536]{0:T(1024)}, u32[]{:S(2)}) copy-start(f32[1536]{0:T(1024)} %param.17) | copy-start | bytes 18436
  23.6 8.3 %collective-permute-start.12 = (bf16[32,1536]{1,0:T(8,128)(2,1)S(1)}, bf16[32,1536]{1,0:T(8,128)(2,1)S(1)}, u32[]{:S(2)}, u32[]{:S(2)}) collective-permute-start(bf16[32,1536]{1,0:T(8,128)(2,1)S(1)} %get-tuple-element.66), channel_id=1, source_target_pairs={{0,2},{2,0},{4,6},{6,4},{8,10},{10,8},{12,14},{14,12},{1,3},{3,1},... | collective-permute-start | bytes 294920 | tf_op jit(solution)/shard_map/ppermute | solution.py:375
  24.4 12.4 %collective-permute-start.13 = (bf16[32,1536]{1,0:T(8,128)(2,1)S(1)}, bf16[32,1536]{1,0:T(8,128)(2,1)S(1)}, u32[]{:S(2)}, u32[]{:S(2)}) collective-permute-start(bf16[32,1536]{1,0:T(8,128)(2,1)S(1)} %get-tuple-element.67), channel_id=1, source_target_pairs={{0,4},{2,6},{4,0},{6,2},{8,12},{10,14},{12,8},{14,10},{1,5},{3,7},... | collective-permute-start | bytes 294920 | tf_op jit(solution)/shard_map/ppermute | solution.py:375
  30.1 6.7 %collective-permute-start.14 = (bf16[32,1536]{1,0:T(8,128)(2,1)S(1)}, bf16[32,1536]{1,0:T(8,128)(2,1)S(1)}, u32[]{:S(2)}, u32[]{:S(2)}) collective-permute-start(bf16[32,1536]{1,0:T(8,128)(2,1)S(1)} %get-tuple-element.68), channel_id=1, source_target_pairs={{0,6},{2,4},{4,2},{6,0},{8,14},{10,12},{12,10},{14,8},{1,7},{3,5},... | collective-permute-start | bytes 294920 | tf_op jit(solution)/shard_map/ppermute | solution.py:375
  31.3 6.4 %collective-permute-start.9 = (bf16[32,1536]{1,0:T(8,128)(2,1)S(1)}, bf16[32,1536]{1,0:T(8,128)(2,1)S(1)}, u32[]{:S(2)}, u32[]{:S(2)}) collective-permute-start(bf16[32,1536]{1,0:T(8,128)(2,1)S(1)} %get-tuple-element.63), channel_id=1, source_target_pairs={{0,2},{2,0},{4,6},{6,4},{8,10},{10,8},{12,14},{14,12},{1,3},{3,1},... | collective-permute-start | bytes 294920 | tf_op jit(solution)/shard_map/ppermute | solution.py:375
  31.9 6.8 %collective-permute-start.10 = (bf16[32,1536]{1,0:T(8,128)(2,1)S(1)}, bf16[32,1536]{1,0:T(8,128)(2,1)S(1)}, u32[]{:S(2)}, u32[]{:S(2)}) collective-permute-start(bf16[32,1536]{1,0:T(8,128)(2,1)S(1)} %get-tuple-element.64), channel_id=1, source_target_pairs={{0,4},{2,6},{4,0},{6,2},{8,12},{10,14},{12,8},{14,10},{1,5},{3,7},... | collective-permute-start | bytes 294920 | tf_op jit(solution)/shard_map/ppermute | solution.py:375
  36.1 5.5 %collective-permute-start.11 = (bf16[32,1536]{1,0:T(8,128)(2,1)S(1)}, bf16[32,1536]{1,0:T(8,128)(2,1)S(1)}, u32[]{:S(2)}, u32[]{:S(2)}) collective-permute-start(bf16[32,1536]{1,0:T(8,128)(2,1)S(1)} %get-tuple-element.65), channel_id=1, source_target_pairs={{0,6},{2,4},{4,2},{6,0},{8,14},{10,12},{12,10},{14,8},{1,7},{3,5},... | collective-permute-start | bytes 294920 | tf_op jit(solution)/shard_map/ppermute | solution.py:375

commit v15 on v14

--- a/solution.py
+++ b/solution.py
@@ -456,7 +456,7 @@
             specs=[None] * 4 + [any_spec],
         )(entering, *known, before)
         back.append(exchange(y_row))
-        before = y_row[0]
+        before = col_entering
 
     mixed = None
     for (first, rows, _, _), blocks in zip(parts_of, back):

time: 42.7 us -> 41.5 us (0.972)
  the two profiles are of different devices: /device:TPU:22 before, /device:TPU:0 now
where the time goes in v15:
time: 41.5 us; the launch traced here: 40.8 us
  starting transfers between devices  20.8 us (50%)
  Pallas kernels  13.1 us (32%)
  waiting for transfers between devices  6.09 us (15%)
  between operations  0.84 us (2%)
    ppermute x12, starting transfers between devices, exchange(): lax.ppermute(blocks[i], 'col', [(at, partner(at, i, group)) for at in ran...  15.8 us
    ppermute x3, starting transfers between devices, entering_states(): entering = lax.ppermute(ends, axis, onward)  4.95 us
    ppermute x12, waiting for transfers between devices, exchange(): lax.ppermute(blocks[i], 'col', [(at, partner(at, i, group)) for at in ran...  4.93 us
    pallas_call x2, Pallas kernels, of_own(): call(functools.partial(row_local_kernel, offset=offset, **sizes, **shared...  2.44 us
    pallas_call x2, Pallas kernels, body(): call(functools.partial(row_state_kernel, count=len(piece), **sizes, **sha...  2.22 us
    pallas_call x1, Pallas kernels, body(): call(functools.partial(col_local_kernel, **sizes), [pltpu.VMEM((tokens, c...  2.16 us
    pallas_call x2, Pallas kernels, body(): call(functools.partial(final_kernel, offset=first, share=share, **shared)...  1.89 us
    pallas_call x1, Pallas kernels, body(): call(functools.partial(col_state_kernel, **sizes), state_shapes([cols * s...  1.48 us
  transfers between devices with their start and end apart: 15, of which 5 were waited for; matrix products, arithmetic and copies ran while one was open for 0% of the time, Pallas kernels for 26%

profile of v15, /device:TPU:0, one launch (start us, length us, event | category | flops | bytes accessed | tf_op | source)
XLA Modules:
  0.0 40.8 jit_solution(310913354811592889)
XLA Ops:
  0.0 0.0 copy-start
  0.0 1.5 %shard_map.91 = (bf16[256,48]{1,0:T(8,128)(2,1)S(1)}, bf16[256,64]{1,0:T(8,128)(2,1)S(1)}, f32[48,1000]{1,0:T(8,128)S(1)}, f32[2,24]{1,0:T(2,128)S(1)}, bf16[32,...) custom-call(bf16[256,1536]{1,0:T(8,128)(2,1)} %bitcast.7, ...), custom_call_target="tpu_custom_call" | custom-call | flops 1000001024 | bytes 1024 | tf_op jit(solution)/shard_map/pallas_call | solution.py:347
  1.5 3.0 %collective-permute-start = (bf16[32,1664]{1,0:T(8,128)(2,1)S(1)}, bf16[32,1664]{1,0:T(8,128)(2,1)S(1)}, u32[]{:S(2)}, u32[]{:S(2)}) collective-permute-start(bf16[32,1664]{1,0:T(8,128)(2,1)S(1)} %get-tuple-element.44), channel_id=1, source_target_pairs={{0,2},{2,0},{4,6},{6,4},{8,10},{10,8},{12,14},{14,12},{1,3},{3,1},... | collective-permute-start | bytes 319496 | tf_op jit(solution)/shard_map/ppermute | solution.py:375
  4.5 1.6 %collective-permute-start.1 = (bf16[32,1664]{1,0:T(8,128)(2,1)S(1)}, bf16[32,1664]{1,0:T(8,128)(2,1)S(1)}, u32[]{:S(2)}, u32[]{:S(2)}) collective-permute-start(bf16[32,1664]{1,0:T(8,128)(2,1)S(1)} %get-tuple-element.45), channel_id=1, source_target_pairs={{0,4},{2,6},{4,0},{6,2},{8,12},{10,14},{12,8},{14,10},{1,5},{3,7},... | collective-permute-start | bytes 319496 | tf_op jit(solution)/shard_map/ppermute | solution.py:375
  6.1 0.0 collective-permute-start.2
  6.1 1.9 %collective-permute-start.4 = (bf16[32,1664]{1,0:T(8,128)(2,1)S(1)}, bf16[32,1664]{1,0:T(8,128)(2,1)S(1)}, u32[]{:S(2)}, u32[]{:S(2)}) collective-permute-start(bf16[32,1664]{1,0:T(8,128)(2,1)S(1)} %get-tuple-element.48), channel_id=1, source_target_pairs={{0,2},{2,0},{4,6},{6,4},{8,10},{10,8},{12,14},{14,12},{1,3},{3,1},... | collective-permute-start | bytes 319496 | tf_op jit(solution)/shard_map/ppermute | solution.py:375
  8.0 1.6 %collective-permute-start.5 = (bf16[32,1664]{1,0:T(8,128)(2,1)S(1)}, bf16[32,1664]{1,0:T(8,128)(2,1)S(1)}, u32[]{:S(2)}, u32[]{:S(2)}) collective-permute-start(bf16[32,1664]{1,0:T(8,128)(2,1)S(1)} %get-tuple-element.49), channel_id=1, source_target_pairs={{0,4},{2,6},{4,0},{6,2},{8,12},{10,14},{12,8},{14,10},{1,5},{3,7},... | collective-permute-start | bytes 319496 | tf_op jit(solution)/shard_map/ppermute | solution.py:375
  10.2 0.2 shard_map.92.params_ref.refs_4_
  10.4 0.0 collective-permute-done.refs_1_
  10.4 0.0 collective-permute-start.6
  10.4 0.0 collective-permute-done.1.refs_2_
  10.5 2.0 %collective-permute-done.2.refs_3_ = bf16[32,1664]{1,0:T(8,128)(2,1)S(1)} collective-permute-done((bf16[32,1664]{1,0:T(8,128)(2,1)S(1)}, bf16[32,1664]{1,0:T(8,128)(2,1)S(1)}, u32[]{:S(2)}, u32[]{:S(2)}) %collective-permute-start.2) | collective-permute-done | bytes 106528 | tf_op jit(solution)/shard_map/ppermute | solution.py:375
  12.4 1.1 %shard_map.93._ = bf16[64,1536]{1,0:T(8,128)(2,1)S(1)} custom-call(f32[8,48]{1,0:T(8,128)S(1)} %shard_map.92.params_ref.refs_4_, bf16[32,1664]{1,0:T(8,128)(2,1)S(1)} %get-tuple-element.43.refs_0_, bf16[32,1664]{1,0:T(8,128)(2,1)S(1)} %collective-permute-done.refs_1_, bf16[32,1664]{1,0:T(8,128)(2,1)S(1)} %collective-permute-done.1.refs_2_, ...), custom_call_target="tpu_custom_call" | custom-call | flops 1024 | bytes 1024 | tf_op jit(solution)/shard_map/pallas_call | solution.py:410
  13.6 3.0 %collective-permute-start.11 = (bf16[64,1536]{1,0:T(8,128)(2,1)S(1)}, bf16[64,1536]{1,0:T(8,128)(2,1)S(1)}, u32[]{:S(2)}, u32[]{:S(2)}) collective-permute-start(bf16[64,1536]{1,0:T(8,128)(2,1)S(1)} %shard_map.93._), channel_id=1, source_target_pairs={{0,8},{2,10},{4,12},{6,14},{8,0},{10,2},{12,4},{14,6},{1,9},{3,11}... | collective-permute-start | bytes 589832 | tf_op jit(solution)/shard_map/ppermute | solution.py:317
  16.6 0.0 copy-done
  16.6 1.5 %shard_map.94.refs_4_ = bf16[128,1536]{1,0:T(8,128)(2,1)S(1)} custom-call(f32[8,48]{1,0:T(8,128)S(1)} %shard_map.92.params_ref.refs_4_, bf16[256,1536]{1,0:T(8,128)(2,1)S(1)} %bitcast.8, bf16[256,48]{1,0:T(8,128)(2,1)S(1)} %get-tuple-element.41.raw_ref, bf16[256,64]{1,0:T(8,128)(2,1)S(1)} %get-tuple-element.42.maps_ref, bf16[64,1536]{1,0:T(8,128)(2,1)S(1)} %shard_map.93._), custom_call_target="tpu_custom_call" | custom-call | flops 1024 | bytes 1024 | tf_op jit(solution)/shard_map/pallas_call | solution.py:418
  18.1 1.5 %collective-permute-start.3 = (bf16[128,1536]{1,0:T(8,128)(2,1)S(1)}, bf16[128,1536]{1,0:T(8,128)(2,1)S(1)}, u32[]{:S(2)}, u32[]{:S(2)}) collective-permute-start(bf16[128,1536]{1,0:T(8,128)(2,1)S(1)} %shard_map.94.refs_4_), channel_id=1, source_target_pairs={{0,16},{16,0},{1,17},{17,1},{2,18},{18,2},{3,19},{19,3},{4,20},{20... | collective-permute-start | bytes 1179656 | tf_op jit(solution)/shard_map/ppermute | solution.py:317
  19.6 1.2 %shard_map.95 = (f32[128,1536]{1,0:T(8,128)S(1)}, bf16[128,48]{1,0:T(8,128)(2,1)S(1)}, bf16[128,64]{1,0:T(8,128)(2,1)S(1)}) custom-call(f32[8,48]{1,0:T(8,128)S(1)} %shard_map.92.params_ref.refs_4_, bf16[32,1664]{1,0:T(8,128)(2,1)S(1)} %get-tuple-element.43.refs_0_, bf16[32,1664]{1,0:T(8,128)(2,1)S(1)} %collective-permute-done.refs_1_, ...), custom_call_target="tpu_custom_call" | custom-call | flops 2000001024 | bytes 1024 | tf_op jit(solution)/shard_map/pallas_call | solution.py:394
  20.8 0.0 collective-permute-done.4.refs_1_
  20.8 0.0 collective-permute-done.5.refs_2_
  20.8 0.0 collective-permute-done.6.refs_3_
  20.9 0.0 copy-start.1
  20.9 0.0 copy-start.2
  20.9 1.2 %shard_map.96 = (f32[128,1536]{1,0:T(8,128)S(1)}, bf16[128,48]{1,0:T(8,128)(2,1)S(1)}, bf16[128,64]{1,0:T(8,128)(2,1)S(1)}) custom-call(f32[8,48]{1,0:T(8,128)S(1)} %shard_map.92.params_ref.refs_4_, bf16[32,1664]{1,0:T(8,128)(2,1)S(1)} %get-tuple-element.47.refs_0_, bf16[32,1664]{1,0:T(8,128)(2,1)S(1)} %collective-permute-done.4.refs_1_, ...), custom_call_target="tpu_custom_call" | custom-call | flops 2000001024 | bytes 1024 | tf_op jit(solution)/shard_map/pallas_call | solution.py:394
  22.1 1.1 %shard_map.97._ = bf16[64,1536]{1,0:T(8,128)(2,1)S(1)} custom-call(f32[8,48]{1,0:T(8,128)S(1)} %shard_map.92.params_ref.refs_4_, bf16[32,1664]{1,0:T(8,128)(2,1)S(1)} %get-tuple-element.47.refs_0_, bf16[32,1664]{1,0:T(8,128)(2,1)S(1)} %collective-permute-done.4.refs_1_, bf16[32,1664]{1,0:T(8,128)(2,1)S(1)} %collective-permute-done.5.refs_2_, ...), custom_call_target="tpu_custom_call" | custom-call | flops 1024 | bytes 1024 | tf_op jit(solution)/shard_map/pallas_call | solution.py:410
  23.2 0.4 collective-permute-start.7
  23.6 0.0 copy-done.1
  23.6 0.0 copy-done.2
  23.6 2.2 %shard_map.98 = (f32[256,1536]{1,0:T(8,128)S(1)}, f32[256,1536]{1,0:T(8,128)S(1)}, bf16[256,48]{1,0:T(8,128)(2,1)S(1)}, bf16[256,128]{1,0:T(8,128)(2,1)S(1)}) custom-call(f32[8,48]{1,0:T(8,128)S(1)} %shard_map.92.params_ref.refs_4_, bf16[256,1536]{1,0:T(8,128)(2,1)S(1)} %bitcast.9, bf16[256,48]{1,0:T(8,128)(2,1)S(1)} %get-tuple-element.41.raw_ref, ...), custom_call_target="tpu_custom_call" | custom-call | flops 1024 | bytes 1024 | tf_op jit(solution)/shard_map/pallas_call | solution.py:432
  25.8 0.0 collective-permute-done.11.s_ref
  25.8 0.0 copy-start.3
  25.8 0.4 shard_map.101
  26.2 1.4 %collective-permute-start.12 = (bf16[32,1536]{1,0:T(8,128)(2,1)S(1)}, bf16[32,1536]{1,0:T(8,128)(2,1)S(1)}, u32[]{:S(2)}, u32[]{:S(2)}) collective-permute-start(bf16[32,1536]{1,0:T(8,128)(2,1)S(1)} %get-tuple-element.66), channel_id=1, source_target_pairs={{0,2},{2,0},{4,6},{6,4},{8,10},{10,8},{12,14},{14,12},{1,3},{3,1},... | collective-permute-start | bytes 294920 | tf_op jit(solution)/shard_map/ppermute | solution.py:375
  27.6 2.6 %collective-permute-start.13 = (bf16[32,1536]{1,0:T(8,128)(2,1)S(1)}, bf16[32,1536]{1,0:T(8,128)(2,1)S(1)}, u32[]{:S(2)}, u32[]{:S(2)}) collective-permute-start(bf16[32,1536]{1,0:T(8,128)(2,1)S(1)} %get-tuple-element.67), channel_id=1, source_target_pairs={{0,4},{2,6},{4,0},{6,2},{8,12},{10,14},{12,8},{14,10},{1,5},{3,7},... | collective-permute-start | bytes 294920 | tf_op jit(solution)/shard_map/ppermute | solution.py:375
  30.2 0.1 collective-permute-start.14
  30.3 1.2 %collective-permute-done.7.s_ref = bf16[64,1536]{1,0:T(8,128)(2,1)S(1)} collective-permute-done((bf16[64,1536]{1,0:T(8,128)(2,1)S(1)}, bf16[64,1536]{1,0:T(8,128)(2,1)S(1)}, u32[]{:S(2)}, u32[]{:S(2)}) %collective-permute-start.7) | collective-permute-done | bytes 196640 | tf_op jit(solution)/shard_map/ppermute | solution.py:317
  31.5 0.0 collective-permute-done.3.s_ref._
  31.5 0.3 shard_map.100
  31.8 1.2 %collective-permute-start.8 = (bf16[32,1536]{1,0:T(8,128)(2,1)S(1)}, bf16[32,1536]{1,0:T(8,128)(2,1)S(1)}, u32[]{:S(2)}, u32[]{:S(2)}) collective-permute-start(bf16[32,1536]{1,0:T(8,128)(2,1)S(1)} %get-tuple-element.60), channel_id=1, source_target_pairs={{0,2},{2,0},{4,6},{6,4},{8,10},{10,8},{12,14},{14,12},{1,3},{3,1},... | collective-permute-start | bytes 294920 | tf_op jit(solution)/shard_map/ppermute | solution.py:375
  33.1 1.3 %collective-permute-start.9 = (bf16[32,1536]{1,0:T(8,128)(2,1)S(1)}, bf16[32,1536]{1,0:T(8,128)(2,1)S(1)}, u32[]{:S(2)}, u32[]{:S(2)}) collective-permute-start(bf16[32,1536]{1,0:T(8,128)(2,1)S(1)} %get-tuple-element.61), channel_id=1, source_target_pairs={{0,4},{2,6},{4,0},{6,2},{8,12},{10,14},{12,8},{14,10},{1,5},{3,7},... | collective-permute-start | bytes 294920 | tf_op jit(solution)/shard_map/ppermute | solution.py:375
  34.4 0.0 collective-permute-done.12.refs_1_
  34.4 1.0 %collective-permute-start.10 = (bf16[32,1536]{1,0:T(8,128)(2,1)S(1)}, bf16[32,1536]{1,0:T(8,128)(2,1)S(1)}, u32[]{:S(2)}, u32[]{:S(2)}) collective-permute-start(bf16[32,1536]{1,0:T(8,128)(2,1)S(1)} %get-tuple-element.62), channel_id=1, source_target_pairs={{0,6},{2,4},{4,2},{6,0},{8,14},{10,12},{12,10},{14,8},{1,7},{3,5},... | collective-permute-start | bytes 294920 | tf_op jit(solution)/shard_map/ppermute | solution.py:375
  35.4 0.0 copy-done.3
  35.4 0.6 %shard_map.99.w_ref = f32[256,1536]{1,0:T(8,128)S(1)} custom-call(bf16[128,1536]{1,0:T(8,128)(2,1)S(1)} %collective-permute-done.3.s_ref._, f32[256,1536]{1,0:T(8,128)S(1)} %get-tuple-element.53.y_ref._, bf16[256,48]{1,0:T(8,128)(2,1)S(1)} %get-tuple-element.54.fade_ref, bf16[256,128]{1,0:T(8,128)(2,1)S(1)} %get-tuple-element.55.entry_ref), custom_call_target="tpu_custom_call" | custom-call | flops 1024 | bytes 1024 | tf_op jit(solution)/shard_map/pallas_call | solution.py:443
  36.0 0.0 collective-permute-done.13.refs_2_
  36.0 0.5 %collective-permute-done.14.refs_3_ = bf16[32,1536]{1,0:T(8,128)(2,1)S(1)} collective-permute-done((bf16[32,1536]{1,0:T(8,128)(2,1)S(1)}, bf16[32,1536]{1,0:T(8,128)(2,1)S(1)}, u32[]{:S(2)}, u32[]{:S(2)}) %collective-permute-start.14) | collective-permute-done | bytes 98336 | tf_op jit(solution)/shard_map/ppermute | solution.py:375
  36.5 0.9 %shard_map.102.refs_4_ = bf16[256,1536]{1,0:T(8,128)(2,1)} custom-call(f32[256,1536]{1,0:T(8,128)S(1)} %shard_map.99.w_ref, f32[256,1536]{1,0:T(8,128)S(1)} %get-tuple-element.56.g_ref, f32[1,1536]{1,0:T(1,128)S(1)} %reshape.27.gain_ref, bf16[32,1536]{1,0:T(8,128)(2,1)S(1)} %get-tuple-element.65.refs_0_, ...), custom_call_target="tpu_custom_call" | custom-call | flops 1024 | bytes 1024 | tf_op jit(solution)/shard_map/pallas_call | solution.py:464
  37.4 0.0 collective-permute-done.8.refs_1_
  37.4 0.3 collective-permute-done.9.refs_2_
  37.7 2.2 %collective-permute-done.10.refs_3_ = bf16[32,1536]{1,0:T(8,128)(2,1)S(1)} collective-permute-done((bf16[32,1536]{1,0:T(8,128)(2,1)S(1)}, bf16[32,1536]{1,0:T(8,128)(2,1)S(1)}, u32[]{:S(2)}, u32[]{:S(2)}) %collective-permute-start.10) | collective-permute-done | bytes 98336 | tf_op jit(solution)/shard_map/ppermute | solution.py:375
  39.9 0.9 %shard_map.103 = bf16[256,1536]{1,0:T(8,128)(2,1)} custom-call(f32[256,1536]{1,0:T(8,128)S(1)} %shard_map.99.w_ref, f32[256,1536]{1,0:T(8,128)S(1)} %get-tuple-element.56.g_ref, f32[1,1536]{1,0:T(1,128)S(1)} %reshape.27.gain_ref, bf16[32,1536]{1,0:T(8,128)(2,1)S(1)} %get-tuple-element.59.refs_0_, ...), custom_call_target="tpu_custom_call", output_to_operand_aliasing={{}: (7, {})} | custom-call | flops 1024 | bytes 1024 | tf_op jit(solution)/shard_map/pallas_call | solution.py:464
  (1 shorter events, 0.0 us)
Async XLA Ops:
  0.0 16.6 %copy-start = (bf16[1,32,8,1536]{3,2,1,0:T(8,128)(2,1)S(1)}, bf16[1,32,8,1536]{3,2,1,0:T(8,128)(2,1)}, u32[]{:S(2)}) copy-start(bf16[1,32,8,1536]{3,2,1,0:T(8,128)(2,1)} %param.9) | copy-start | bytes 2359300
  1.5 8.9 %collective-permute-start = (bf16[32,1664]{1,0:T(8,128)(2,1)S(1)}, bf16[32,1664]{1,0:T(8,128)(2,1)S(1)}, u32[]{:S(2)}, u32[]{:S(2)}) collective-permute-start(bf16[32,1664]{1,0:T(8,128)(2,1)S(1)} %get-tuple-element.44), channel_id=1, source_target_pairs={{0,2},{2,0},{4,6},{6,4},{8,10},{10,8},{12,14},{14,12},{1,3},{3,1},... | collective-permute-start | bytes 319496 | tf_op jit(solution)/shard_map/ppermute | solution.py:375
  4.5 5.9 %collective-permute-start.1 = (bf16[32,1664]{1,0:T(8,128)(2,1)S(1)}, bf16[32,1664]{1,0:T(8,128)(2,1)S(1)}, u32[]{:S(2)}, u32[]{:S(2)}) collective-permute-start(bf16[32,1664]{1,0:T(8,128)(2,1)S(1)} %get-tuple-element.45), channel_id=1, source_target_pairs={{0,4},{2,6},{4,0},{6,2},{8,12},{10,14},{12,8},{14,10},{1,5},{3,7},... | collective-permute-start | bytes 319496 | tf_op jit(solution)/shard_map/ppermute | solution.py:375
  6.1 6.3 %collective-permute-start.2 = (bf16[32,1664]{1,0:T(8,128)(2,1)S(1)}, bf16[32,1664]{1,0:T(8,128)(2,1)S(1)}, u32[]{:S(2)}, u32[]{:S(2)}) collective-permute-start(bf16[32,1664]{1,0:T(8,128)(2,1)S(1)} %get-tuple-element.46), channel_id=1, source_target_pairs={{0,6},{2,4},{4,2},{6,0},{8,14},{10,12},{12,10},{14,8},{1,7},{3,5},... | collective-permute-start | bytes 319496 | tf_op jit(solution)/shard_map/ppermute | solution.py:375
  6.1 14.7 %collective-permute-start.4 = (bf16[32,1664]{1,0:T(8,128)(2,1)S(1)}, bf16[32,1664]{1,0:T(8,128)(2,1)S(1)}, u32[]{:S(2)}, u32[]{:S(2)}) collective-permute-start(bf16[32,1664]{1,0:T(8,128)(2,1)S(1)} %get-tuple-element.48), channel_id=1, source_target_pairs={{0,2},{2,0},{4,6},{6,4},{8,10},{10,8},{12,14},{14,12},{1,3},{3,1},... | collective-permute-start | bytes 319496 | tf_op jit(solution)/shard_map/ppermute | solution.py:375
  8.0 12.8 %collective-permute-start.5 = (bf16[32,1664]{1,0:T(8,128)(2,1)S(1)}, bf16[32,1664]{1,0:T(8,128)(2,1)S(1)}, u32[]{:S(2)}, u32[]{:S(2)}) collective-permute-start(bf16[32,1664]{1,0:T(8,128)(2,1)S(1)} %get-tuple-element.49), channel_id=1, source_target_pairs={{0,4},{2,6},{4,0},{6,2},{8,12},{10,14},{12,8},{14,10},{1,5},{3,7},... | collective-permute-start | bytes 319496 | tf_op jit(solution)/shard_map/ppermute | solution.py:375
  10.4 10.4 %collective-permute-start.6 = (bf16[32,1664]{1,0:T(8,128)(2,1)S(1)}, bf16[32,1664]{1,0:T(8,128)(2,1)S(1)}, u32[]{:S(2)}, u32[]{:S(2)}) collective-permute-start(bf16[32,1664]{1,0:T(8,128)(2,1)S(1)} %get-tuple-element.50), channel_id=1, source_target_pairs={{0,6},{2,4},{4,2},{6,0},{8,14},{10,12},{12,10},{14,8},{1,7},{3,5},... | collective-permute-start | bytes 319496 | tf_op jit(solution)/shard_map/ppermute | solution.py:375
  13.6 12.3 %collective-permute-start.11 = (bf16[64,1536]{1,0:T(8,128)(2,1)S(1)}, bf16[64,1536]{1,0:T(8,128)(2,1)S(1)}, u32[]{:S(2)}, u32[]{:S(2)}) collective-permute-start(bf16[64,1536]{1,0:T(8,128)(2,1)S(1)} %shard_map.93._), channel_id=1, source_target_pairs={{0,8},{2,10},{4,12},{6,14},{8,0},{10,2},{12,4},{14,6},{1,9},{3,11}... | collective-permute-start | bytes 589832 | tf_op jit(solution)/shard_map/ppermute | solution.py:317
  18.1 13.4 %collective-permute-start.3 = (bf16[128,1536]{1,0:T(8,128)(2,1)S(1)}, bf16[128,1536]{1,0:T(8,128)(2,1)S(1)}, u32[]{:S(2)}, u32[]{:S(2)}) collective-permute-start(bf16[128,1536]{1,0:T(8,128)(2,1)S(1)} %shard_map.94.refs_4_), channel_id=1, source_target_pairs={{0,16},{16,0},{1,17},{17,1},{2,18},{18,2},{3,19},{19,3},{4,20},{20... | collective-permute-start | bytes 1179656 | tf_op jit(solution)/shard_map/ppermute | solution.py:317
  20.9 2.8 %copy-start.1 = (bf16[1,32,8,1536]{3,2,1,0:T(8,128)(2,1)S(1)}, bf16[1,32,8,1536]{3,2,1,0:T(8,128)(2,1)}, u32[]{:S(2)}) copy-start(bf16[1,32,8,1536]{3,2,1,0:T(8,128)(2,1)} %param.10) | copy-start | bytes 2359300
  20.9 2.8 %copy-start.2 = (f32[24]{0:T(128)S(1)}, f32[24]{0:T(128)}, u32[]{:S(2)}) copy-start(f32[24]{0:T(128)} %param.16) | copy-start | bytes 292
  23.2 8.3 %collective-permute-start.7 = (bf16[64,1536]{1,0:T(8,128)(2,1)S(1)}, bf16[64,1536]{1,0:T(8,128)(2,1)S(1)}, u32[]{:S(2)}, u32[]{:S(2)}) collective-permute-start(bf16[64,1536]{1,0:T(8,128)(2,1)S(1)} %shard_map.97._), channel_id=1, source_target_pairs={{0,8},{2,10},{4,12},{6,14},{8,0},{10,2},{12,4},{14,6},{1,9},{3,11}... | collective-permute-start | bytes 589832 | tf_op jit(solution)/shard_map/ppermute | solution.py:317
  25.8 9.6 %copy-start.3 = (f32[1536]{0:T(1024)S(1)}, f32[1536]{0:T(1024)}, u32[]{:S(2)}) copy-start(f32[1536]{0:T(1024)} %param.17) | copy-start | bytes 18436
  26.2 8.2 %collective-permute-start.12 = (bf16[32,1536]{1,0:T(8,128)(2,1)S(1)}, bf16[32,1536]{1,0:T(8,128)(2,1)S(1)}, u32[]{:S(2)}, u32[]{:S(2)}) collective-permute-start(bf16[32,1536]{1,0:T(8,128)(2,1)S(1)} %get-tuple-element.66), channel_id=1, source_target_pairs={{0,2},{2,0},{4,6},{6,4},{8,10},{10,8},{12,14},{14,12},{1,3},{3,1},... | collective-permute-start | bytes 294920 | tf_op jit(solution)/shard_map/ppermute | solution.py:375
  27.6 8.4 %collective-permute-start.13 = (bf16[32,1536]{1,0:T(8,128)(2,1)S(1)}, bf16[32,1536]{1,0:T(8,128)(2,1)S(1)}, u32[]{:S(2)}, u32[]{:S(2)}) collective-permute-start(bf16[32,1536]{1,0:T(8,128)(2,1)S(1)} %get-tuple-element.67), channel_id=1, source_target_pairs={{0,4},{2,6},{4,0},{6,2},{8,12},{10,14},{12,8},{14,10},{1,5},{3,7},... | collective-permute-start | bytes 294920 | tf_op jit(solution)/shard_map/ppermute | solution.py:375
  30.2 6.2 %collective-permute-start.14 = (bf16[32,1536]{1,0:T(8,128)(2,1)S(1)}, bf16[32,1536]{1,0:T(8,128)(2,1)S(1)}, u32[]{:S(2)}, u32[]{:S(2)}) collective-permute-start(bf16[32,1536]{1,0:T(8,128)(2,1)S(1)} %get-tuple-element.68), channel_id=1, source_target_pairs={{0,6},{2,4},{4,2},{6,0},{8,14},{10,12},{12,10},{14,8},{1,7},{3,5},... | collective-permute-start | bytes 294920 | tf_op jit(solution)/shard_map/ppermute | solution.py:375
  31.8 5.6 %collective-permute-start.8 = (bf16[32,1536]{1,0:T(8,128)(2,1)S(1)}, bf16[32,1536]{1,0:T(8,128)(2,1)S(1)}, u32[]{:S(2)}, u32[]{:S(2)}) collective-permute-start(bf16[32,1536]{1,0:T(8,128)(2,1)S(1)} %get-tuple-element.60), channel_id=1, source_target_pairs={{0,2},{2,0},{4,6},{6,4},{8,10},{10,8},{12,14},{14,12},{1,3},{3,1},... | collective-permute-start | bytes 294920 | tf_op jit(solution)/shard_map/ppermute | solution.py:375
  33.1 4.6 %collective-permute-start.9 = (bf16[32,1536]{1,0:T(8,128)(2,1)S(1)}, bf16[32,1536]{1,0:T(8,128)(2,1)S(1)}, u32[]{:S(2)}, u32[]{:S(2)}) collective-permute-start(bf16[32,1536]{1,0:T(8,128)(2,1)S(1)} %get-tuple-element.61), channel_id=1, source_target_pairs={{0,4},{2,6},{4,0},{6,2},{8,12},{10,14},{12,8},{14,10},{1,5},{3,7},... | collective-permute-start | bytes 294920 | tf_op jit(solution)/shard_map/ppermute | solution.py:375
  34.4 5.5 %collective-permute-start.10 = (bf16[32,1536]{1,0:T(8,128)(2,1)S(1)}, bf16[32,1536]{1,0:T(8,128)(2,1)S(1)}, u32[]{:S(2)}, u32[]{:S(2)}) collective-permute-start(bf16[32,1536]{1,0:T(8,128)(2,1)S(1)} %get-tuple-element.62), channel_id=1, source_target_pairs={{0,6},{2,4},{4,2},{6,0},{8,14},{10,12},{12,10},{14,8},{1,7},{3,5},... | collective-permute-start | bytes 294920 | tf_op jit(solution)/shard_map/ppermute | solution.py:375

commit v16 on v15

--- a/solution.py
+++ b/solution.py
@@ -117,37 +117,49 @@
     return [(first, min(STRIP, channels - first)) for first in range(0, channels, STRIP)]
 
 
-def pack_kernel(
-    x_ref, raw_ref, maps_ref, table_ref, rates_ref, raw, maps, table, rates, *refs, group, axis, heads, state
+def pack_places(sent, x_ref, offset, axis):
+    group = len(sent)
+    share = x_ref.shape[0] // group
+    member = mod(lax.axis_index(axis), group)
+    return [
+        (out, pl.ds(pl.multiple_of(partner(member, i, group) * share + offset, 16), out.shape[0]))
+        for i, out in enumerate(sent)
+    ]
+
+
+def pack_aux(places, raw, maps, channels, heads, state):
+    used = heads + 2 * state
+    for out, part in places:
+        out[:, channels : channels + heads] = raw[part, :heads]
+        out[:, channels + heads : channels + used] = maps[part, : 2 * state]
+        out[:, channels + used :] = jnp.zeros((out.shape[0], LANES - used), BF16)
+
+
+def first_pack_kernel(
+    x_ref, raw_ref, maps_ref, table_ref, rates_ref, raw, maps, table, rates, *refs, offset, axis, heads, state
 ):
     sent, sems = refs[:-1], refs[-1]
     channels = x_ref.shape[1]
-    share = x_ref.shape[0] // group
-    member = mod(lax.axis_index(axis), group)
+    places = pack_places(sent, x_ref, offset, axis)
     moved = [(raw_ref, raw), (maps_ref, maps)]
-    places = []
-    offset = 0
-    for i, out in enumerate(sent):
-        rows = out.shape[0]
-        first = partner(member, i % group, group) * share + offset
-        part = pl.ds(pl.multiple_of(first, 16), rows)
-        places.append((out, part))
-        moved.append((x_ref.at[part, :], out.at[:, pl.ds(0, channels)]))
-        if i % group == group - 1:
-            offset += rows
+    moved += [(x_ref.at[part, :], out.at[:, pl.ds(0, channels)]) for out, part in places]
     moved += [(table_ref, table), (rates_ref, rates)]
     copies = [pltpu.make_async_copy(a, b, sems.at[i]) for i, (a, b) in enumerate(moved)]
     for copy in copies:
         copy.start()
     for copy in copies[:2]:
         copy.wait()
-    used = heads + 2 * state
-    for out, part in places:
-        out[:, channels : channels + heads] = raw[part, :heads]
-        out[:, channels + heads : channels + used] = maps[part, : 2 * state]
-        out[:, channels + used :] = jnp.zeros((out.shape[0], LANES - used), BF16)
+    pack_aux(places, raw, maps, channels, heads, state)
     for copy in copies[2:]:
         copy.wait()
+
+
+def pack_kernel(x_ref, raw_ref, maps_ref, *sent, offset, axis, heads, state):
+    channels = x_ref.shape[1]
+    places = pack_places(sent, x_ref, offset, axis)
+    for out, part in places:
+        out[:, :channels] = x_ref[part, :]
+    pack_aux(places, raw_ref, maps_ref, channels, heads, state)
 
 
 def params_kernel(index_ref, table_ref, rates_ref, params_ref):
@@ -278,17 +290,18 @@
         w_ref[:, part] = y_ref[:, part] + dot(entry_ref[...], s_ref[:, part]) * dot(fade_ref[...], pick)
 
 
-def final_kernel(w_ref, g_ref, gain_ref, *refs, group, axis, offset, share):
-    blocks, (out_ref, made, sems) = refs[:group], refs[-3:]
+def final_kernel(w_ref, g_ref, gain_ref, *refs, which, offset, group, axis, share):
+    blocks, (out_ref, made, sems) = refs[-3 - len(which) : -3], refs[-3:]
     rows, channels = blocks[0].shape
     member = mod(lax.axis_index(axis), group)
     copies = []
-    for s in range(group):
-        part = pl.ds(pl.multiple_of(partner(member, s, group) * share + offset, 16), rows)
-        v = (blocks[s][...].astype(F32) + w_ref[part, :]) * g_ref[part, :]
+    for i, block in zip(which, blocks):
+        part = pl.ds(pl.multiple_of(partner(member, i, group) * share + offset, 16), rows)
+        v = (block[...].astype(F32) + w_ref[part, :]) * g_ref[part, :]
         power = jnp.sum(v * v, axis=1, keepdims=True) / channels
-        made[s] = (v * lax.rsqrt(power + 1e-5) * gain_ref[...]).astype(BF16)
-        copies.append(pltpu.make_async_copy(made.at[s], out_ref.at[part, :], sems.at[s]))
+        at = len(copies)
+        made[at] = (v * lax.rsqrt(power + 1e-5) * gain_ref[...]).astype(BF16)
+        copies.append(pltpu.make_async_copy(made.at[at], out_ref.at[part, :], sems.at[at]))
         copies[-1].start()
     for copy in copies:
         copy.wait()
@@ -344,15 +357,21 @@
     any_spec = pl.BlockSpec(memory_space=pl.ANY)
 
     given = [x, raw, maps, step_table.T, rates]
-    raw, maps, table, rates, *packed = pl.pallas_call(
-        functools.partial(pack_kernel, heads=heads, state=state, **shared),
-        in_specs=[pl.BlockSpec(memory_space=pltpu.HBM)] * len(given),
-        out_shape=[pltpu.VMEM(a.shape, a.dtype) for a in given[1:]]
-        + [pltpu.VMEM((sum(piece), channels + LANES), BF16) for piece in pieces for _ in range(group)],
-        scratch_shapes=[pltpu.SemaphoreType.DMA((len(given) - 1 + group * len(pieces),))],
-        compiler_params=pltpu.CompilerParams(vmem_limit_bytes=VMEM_LIMIT),
-        cost_estimate=cost(1),
+    blocks_of = lambda piece: [pltpu.VMEM((sum(piece), channels + LANES), BF16)] * group
+    packing = dict(axis="col", heads=heads, state=state)
+    raw, maps, table, rates, *packed = call(
+        functools.partial(first_pack_kernel, offset=0, **packing),
+        [pltpu.VMEM(a.shape, a.dtype) for a in given[1:]] + blocks_of(pieces[0]),
+        0,
+        specs=[pl.BlockSpec(memory_space=pltpu.HBM)] * len(given),
+        scratch_shapes=[pltpu.SemaphoreType.DMA((len(given) - 1 + group,))],
     )(*[pltpu.with_memory_space_constraint(a, pltpu.HBM) for a in given])
+    for i in range(1, len(pieces)):
+        packed += call(
+            functools.partial(pack_kernel, offset=sum(map(sum, pieces[:i])), **packing),
+            blocks_of(pieces[i]),
+            0,
+        )(x, raw, maps)
     index, rates = lax.optimization_barrier((step_index, rates))
     params = pl.pallas_call(
         params_kernel,
@@ -458,18 +477,25 @@
         back.append(exchange(y_row))
         before = col_entering
 
+    order = list(range(group))
+    stages = [(i, order) for i in range(len(parts_of) - 1)]
+    stages += [(len(parts_of) - 1, order[:1] + order[:1:-1]), (len(parts_of) - 1, order[1:2])]
     mixed = None
-    for (first, rows, _, _), blocks in zip(parts_of, back):
+    for i, which in stages:
+        first, rows = parts_of[i][:2]
         more = [] if mixed is None else [mixed]
         mixed = call(
-            functools.partial(final_kernel, offset=first, share=share, **shared),
+            functools.partial(final_kernel, which=which, offset=first, share=share, **shared),
             shape((tokens, channels), BF16),
             0,
-            specs=[None] * (3 + group) + [any_spec] * len(more),
+            specs=[None] * 3 + [any_spec] * len(more) + [None] * len(which),
             out_specs=any_spec,
-            scratch_shapes=[pltpu.VMEM((group, rows, channels), BF16), pltpu.SemaphoreType.DMA((group,))],
-            input_output_aliases={3 + group: 0} if more else {},
-        )(w, silu, norm_gain.reshape(1, channels), *blocks, *more)
+            scratch_shapes=[
+                pltpu.VMEM((len(which), rows, channels), BF16),
+                pltpu.SemaphoreType.DMA((len(which),)),
+            ],
+            input_output_aliases={3: 0} if more else {},
+        )(w, silu, norm_gain.reshape(1, channels), *more, *[back[i][j] for j in which])
     return mixed.reshape(x_in.shape)
 
 

time: 41.5 us -> 43.7 us (1.053)
  starting transfers between devices: 20.8 us -> 22.4 us
  Pallas kernels: 13.1 us -> 13.8 us
    ppermute x12, starting transfers between devices: 15.8 us -> 17.8 us  [exchange(): lax.ppermute(blocks[i], 'col', [(at, partner(at, i, group)) for at in ran...]
    ppermute x3, waiting for transfers between devices: 1.16 us -> 3.1 us  [entering_states(): entering = lax.ppermute(ends, axis, onward)]
    ppermute x12, waiting for transfers between devices: 4.93 us -> 3.21 us  [exchange(): lax.ppermute(blocks[i], 'col', [(at, partner(at, i, group)) for at in ran...]
    pallas_call x3 -> x5, Pallas kernels: 3.37 us -> 4.05 us  [the longest x3 2.62 us: body(): call(functools.partial(final_kernel, which=which, offset=first, share=sha...]
  transfers between devices with their start and end apart: 15 -> 15, of which waited for: 5 -> 4; matrix products, arithmetic and copies ran while one was open for 0% -> 0% of each run, Pallas kernels for 26% -> 27%
where the time goes in v16:
time: 43.7 us; the launch traced here: 43.4 us
  starting transfers between devices  22.4 us (51%)
  Pallas kernels  13.8 us (32%)
  waiting for transfers between devices  6.31 us (14%)
  between operations  0.83 us (2%)
    ppermute x12, starting transfers between devices, exchange(): lax.ppermute(blocks[i], 'col', [(at, partner(at, i, group)) for at in ran...  17.8 us
    ppermute x3, starting transfers between devices, entering_states(): entering = lax.ppermute(ends, axis, onward)  4.53 us
    ppermute x12, waiting for transfers between devices, exchange(): lax.ppermute(blocks[i], 'col', [(at, partner(at, i, group)) for at in ran...  3.21 us
    ppermute x3, waiting for transfers between devices, entering_states(): entering = lax.ppermute(ends, axis, onward)  3.1 us
    pallas_call x3, Pallas kernels, body(): call(functools.partial(final_kernel, which=which, offset=first, share=sha...  2.62 us
    pallas_call x2, Pallas kernels, of_own(): call(functools.partial(row_local_kernel, offset=offset, **sizes, **shared...  2.46 us
    pallas_call x2, Pallas kernels, body(): call(functools.partial(row_state_kernel, count=len(piece), **sizes, **sha...  2.22 us
    pallas_call x1, Pallas kernels, body(): call(functools.partial(col_local_kernel, **sizes), [pltpu.VMEM((tokens, c...  2.17 us
  transfers between devices with their start and end apart: 15, of which 4 were waited for; matrix products, arithmetic and copies ran while one was open for 0% of the time, Pallas kernels for 27%

profile of v16, /device:TPU:0, one launch (start us, length us, event | category | flops | bytes accessed | tf_op | source)
XLA Modules:
  0.0 43.4 jit_solution(14946071109565914570)
XLA Ops:
  0.0 0.0 copy-start
  0.0 1.3 %shard_map.91 = (bf16[256,48]{1,0:T(8,128)(2,1)S(1)}, bf16[256,64]{1,0:T(8,128)(2,1)S(1)}, f32[48,1000]{1,0:T(8,128)S(1)}, f32[2,24]{1,0:T(2,128)S(1)}, bf16[32,...) custom-call(bf16[256,1536]{1,0:T(8,128)(2,1)} %bitcast.7, ...), custom_call_target="tpu_custom_call" | custom-call | flops 1024 | bytes 1024 | tf_op jit(solution)/shard_map/pallas_call | solution.py:362
  1.3 3.0 %collective-permute-start = (bf16[32,1664]{1,0:T(8,128)(2,1)S(1)}, bf16[32,1664]{1,0:T(8,128)(2,1)S(1)}, u32[]{:S(2)}, u32[]{:S(2)}) collective-permute-start(bf16[32,1664]{1,0:T(8,128)(2,1)S(1)} %get-tuple-element.44), channel_id=1, source_target_pairs={{0,2},{2,0},{4,6},{6,4},{8,10},{10,8},{12,14},{14,12},{1,3},{3,1},... | collective-permute-start | bytes 319496 | tf_op jit(solution)/shard_map/ppermute | solution.py:394
  4.4 1.6 %collective-permute-start.1 = (bf16[32,1664]{1,0:T(8,128)(2,1)S(1)}, bf16[32,1664]{1,0:T(8,128)(2,1)S(1)}, u32[]{:S(2)}, u32[]{:S(2)}) collective-permute-start(bf16[32,1664]{1,0:T(8,128)(2,1)S(1)} %get-tuple-element.45), channel_id=1, source_target_pairs={{0,4},{2,6},{4,0},{6,2},{8,12},{10,14},{12,8},{14,10},{1,5},{3,7},... | collective-permute-start | bytes 319496 | tf_op jit(solution)/shard_map/ppermute | solution.py:394
  5.9 0.0 collective-permute-start.2
  5.9 0.0 copy-done
  5.9 0.1 shard_map.95
  6.0 2.0 %collective-permute-start.4 = (bf16[32,1664]{1,0:T(8,128)(2,1)S(1)}, bf16[32,1664]{1,0:T(8,128)(2,1)S(1)}, u32[]{:S(2)}, u32[]{:S(2)}) collective-permute-start(bf16[32,1664]{1,0:T(8,128)(2,1)S(1)} %get-tuple-element.48), channel_id=1, source_target_pairs={{0,2},{2,0},{4,6},{6,4},{8,10},{10,8},{12,14},{14,12},{1,3},{3,1},... | collective-permute-start | bytes 319496 | tf_op jit(solution)/shard_map/ppermute | solution.py:394
  8.0 1.6 %collective-permute-start.5 = (bf16[32,1664]{1,0:T(8,128)(2,1)S(1)}, bf16[32,1664]{1,0:T(8,128)(2,1)S(1)}, u32[]{:S(2)}, u32[]{:S(2)}) collective-permute-start(bf16[32,1664]{1,0:T(8,128)(2,1)S(1)} %get-tuple-element.49), channel_id=1, source_target_pairs={{0,4},{2,6},{4,0},{6,2},{8,12},{10,14},{12,8},{14,10},{1,5},{3,7},... | collective-permute-start | bytes 319496 | tf_op jit(solution)/shard_map/ppermute | solution.py:394
  10.2 0.2 shard_map.92.params_ref.refs_4_
  10.4 0.0 collective-permute-done.refs_1_
  10.4 0.0 collective-permute-done.1.refs_2_
  10.4 1.8 %collective-permute-done.2.refs_3_ = bf16[32,1664]{1,0:T(8,128)(2,1)S(1)} collective-permute-done((bf16[32,1664]{1,0:T(8,128)(2,1)S(1)}, bf16[32,1664]{1,0:T(8,128)(2,1)S(1)}, u32[]{:S(2)}, u32[]{:S(2)}) %collective-permute-start.2) | collective-permute-done | bytes 106528 | tf_op jit(solution)/shard_map/ppermute | solution.py:394
  12.3 1.1 %shard_map.93._ = bf16[64,1536]{1,0:T(8,128)(2,1)S(1)} custom-call(f32[8,48]{1,0:T(8,128)S(1)} %shard_map.92.params_ref.refs_4_, bf16[32,1664]{1,0:T(8,128)(2,1)S(1)} %get-tuple-element.43.refs_0_, bf16[32,1664]{1,0:T(8,128)(2,1)S(1)} %collective-permute-done.refs_1_, bf16[32,1664]{1,0:T(8,128)(2,1)S(1)} %collective-permute-done.1.refs_2_, ...), custom_call_target="tpu_custom_call" | custom-call | flops 1024 | bytes 1024 | tf_op jit(solution)/shard_map/pallas_call | solution.py:429
  13.4 2.6 %collective-permute-start.6 = (bf16[32,1664]{1,0:T(8,128)(2,1)S(1)}, bf16[32,1664]{1,0:T(8,128)(2,1)S(1)}, u32[]{:S(2)}, u32[]{:S(2)}) collective-permute-start(bf16[32,1664]{1,0:T(8,128)(2,1)S(1)} %get-tuple-element.50), channel_id=1, source_target_pairs={{0,6},{2,4},{4,2},{6,0},{8,14},{10,12},{12,10},{14,8},{1,7},{3,5},... | collective-permute-start | bytes 319496 | tf_op jit(solution)/shard_map/ppermute | solution.py:394
  16.0 1.5 %shard_map.94.refs_4_ = bf16[128,1536]{1,0:T(8,128)(2,1)S(1)} custom-call(f32[8,48]{1,0:T(8,128)S(1)} %shard_map.92.params_ref.refs_4_, bf16[256,1536]{1,0:T(8,128)(2,1)S(1)} %bitcast.9, bf16[256,48]{1,0:T(8,128)(2,1)S(1)} %get-tuple-element.41.raw_ref, bf16[256,64]{1,0:T(8,128)(2,1)S(1)} %get-tuple-element.42.maps_ref, bf16[64,1536]{1,0:T(8,128)(2,1)S(1)} %shard_map.93._), custom_call_target="tpu_custom_call" | custom-call | flops 1024 | bytes 1024 | tf_op jit(solution)/shard_map/pallas_call | solution.py:437
  17.5 2.6 %collective-permute-start.7 = (bf16[64,1536]{1,0:T(8,128)(2,1)S(1)}, bf16[64,1536]{1,0:T(8,128)(2,1)S(1)}, u32[]{:S(2)}, u32[]{:S(2)}) collective-permute-start(bf16[64,1536]{1,0:T(8,128)(2,1)S(1)} %shard_map.93._), channel_id=1, source_target_pairs={{0,8},{2,10},{4,12},{6,14},{8,0},{10,2},{12,4},{14,6},{1,9},{3,11}... | collective-permute-start | bytes 589832 | tf_op jit(solution)/shard_map/ppermute | solution.py:330
  20.1 1.5 %collective-permute-start.3 = (bf16[128,1536]{1,0:T(8,128)(2,1)S(1)}, bf16[128,1536]{1,0:T(8,128)(2,1)S(1)}, u32[]{:S(2)}, u32[]{:S(2)}) collective-permute-start(bf16[128,1536]{1,0:T(8,128)(2,1)S(1)} %shard_map.94.refs_4_), channel_id=1, source_target_pairs={{0,16},{16,0},{1,17},{17,1},{2,18},{18,2},{3,19},{19,3},{4,20},{20... | collective-permute-start | bytes 1179656 | tf_op jit(solution)/shard_map/ppermute | solution.py:330
  21.6 1.2 %shard_map.96 = (f32[128,1536]{1,0:T(8,128)S(1)}, bf16[128,48]{1,0:T(8,128)(2,1)S(1)}, bf16[128,64]{1,0:T(8,128)(2,1)S(1)}) custom-call(f32[8,48]{1,0:T(8,128)S(1)} %shard_map.92.params_ref.refs_4_, bf16[32,1664]{1,0:T(8,128)(2,1)S(1)} %get-tuple-element.43.refs_0_, bf16[32,1664]{1,0:T(8,128)(2,1)S(1)} %collective-permute-done.refs_1_, ...), custom_call_target="tpu_custom_call" | custom-call | flops 2000001024 | bytes 1024 | tf_op jit(solution)/shard_map/pallas_call | solution.py:413
  22.9 0.0 collective-permute-done.4.refs_1_
  22.9 0.0 collective-permute-done.5.refs_2_
  22.9 0.0 collective-permute-done.6.refs_3_
  22.9 0.0 copy-start.1
  22.9 0.0 copy-start.2
  22.9 1.2 %shard_map.97 = (f32[128,1536]{1,0:T(8,128)S(1)}, bf16[128,48]{1,0:T(8,128)(2,1)S(1)}, bf16[128,64]{1,0:T(8,128)(2,1)S(1)}) custom-call(f32[8,48]{1,0:T(8,128)S(1)} %shard_map.92.params_ref.refs_4_, bf16[32,1664]{1,0:T(8,128)(2,1)S(1)} %get-tuple-element.47.refs_0_, bf16[32,1664]{1,0:T(8,128)(2,1)S(1)} %collective-permute-done.4.refs_1_, ...), custom_call_target="tpu_custom_call" | custom-call | flops 2000001024 | bytes 1024 | tf_op jit(solution)/shard_map/pallas_call | solution.py:413
  24.2 1.1 %shard_map.98._ = bf16[64,1536]{1,0:T(8,128)(2,1)S(1)} custom-call(f32[8,48]{1,0:T(8,128)S(1)} %shard_map.92.params_ref.refs_4_, bf16[32,1664]{1,0:T(8,128)(2,1)S(1)} %get-tuple-element.47.refs_0_, bf16[32,1664]{1,0:T(8,128)(2,1)S(1)} %collective-permute-done.4.refs_1_, bf16[32,1664]{1,0:T(8,128)(2,1)S(1)} %collective-permute-done.5.refs_2_, ...), custom_call_target="tpu_custom_call" | custom-call | flops 1024 | bytes 1024 | tf_op jit(solution)/shard_map/pallas_call | solution.py:429
  25.3 0.4 collective-permute-start.11
  25.7 0.0 copy-done.1
  25.7 0.0 copy-done.2
  25.7 2.2 %shard_map.99 = (f32[256,1536]{1,0:T(8,128)S(1)}, f32[256,1536]{1,0:T(8,128)S(1)}, bf16[256,48]{1,0:T(8,128)(2,1)S(1)}, bf16[256,128]{1,0:T(8,128)(2,1)S(1)}) custom-call(f32[8,48]{1,0:T(8,128)S(1)} %shard_map.92.params_ref.refs_4_, bf16[256,1536]{1,0:T(8,128)(2,1)S(1)} %bitcast.10, bf16[256,48]{1,0:T(8,128)(2,1)S(1)} %get-tuple-element.41.raw_ref, ...), custom_call_target="tpu_custom_call" | custom-call | flops 1024 | bytes 1024 | tf_op jit(solution)/shard_map/pallas_call | solution.py:451
  27.8 1.8 %collective-permute-done.7.s_ref = bf16[64,1536]{1,0:T(8,128)(2,1)S(1)} collective-permute-done((bf16[64,1536]{1,0:T(8,128)(2,1)S(1)}, bf16[64,1536]{1,0:T(8,128)(2,1)S(1)}, u32[]{:S(2)}, u32[]{:S(2)}) %collective-permute-start.7) | collective-permute-done | bytes 196640 | tf_op jit(solution)/shard_map/ppermute | solution.py:330
  29.6 0.0 copy-start.3
  29.6 0.3 shard_map.101
  30.0 2.7 %collective-permute-start.10 = (bf16[32,1536]{1,0:T(8,128)(2,1)S(1)}, bf16[32,1536]{1,0:T(8,128)(2,1)S(1)}, u32[]{:S(2)}, u32[]{:S(2)}) collective-permute-start(bf16[32,1536]{1,0:T(8,128)(2,1)S(1)} %get-tuple-element.62), channel_id=1, source_target_pairs={{0,6},{2,4},{4,2},{6,0},{8,14},{10,12},{12,10},{14,8},{1,7},{3,5},... | collective-permute-start | bytes 294920 | tf_op jit(solution)/shard_map/ppermute | solution.py:394
  32.7 0.2 collective-permute-start.8
  32.9 0.6 %collective-permute-start.9 = (bf16[32,1536]{1,0:T(8,128)(2,1)S(1)}, bf16[32,1536]{1,0:T(8,128)(2,1)S(1)}, u32[]{:S(2)}, u32[]{:S(2)}) collective-permute-start(bf16[32,1536]{1,0:T(8,128)(2,1)S(1)} %get-tuple-element.61), channel_id=1, source_target_pairs={{0,4},{2,6},{4,0},{6,2},{8,12},{10,14},{12,8},{14,10},{1,5},{3,7},... | collective-permute-start | bytes 294920 | tf_op jit(solution)/shard_map/ppermute | solution.py:394
  33.5 1.3 %collective-permute-done.11.s_ref = bf16[64,1536]{1,0:T(8,128)(2,1)S(1)} collective-permute-done((bf16[64,1536]{1,0:T(8,128)(2,1)S(1)}, bf16[64,1536]{1,0:T(8,128)(2,1)S(1)}, u32[]{:S(2)}, u32[]{:S(2)}) %collective-permute-start.11) | collective-permute-done | bytes 196640 | tf_op jit(solution)/shard_map/ppermute | solution.py:330
  34.9 0.0 collective-permute-done.3.s_ref._
  34.9 0.3 shard_map.103
  35.2 1.4 %collective-permute-start.12 = (bf16[32,1536]{1,0:T(8,128)(2,1)S(1)}, bf16[32,1536]{1,0:T(8,128)(2,1)S(1)}, u32[]{:S(2)}, u32[]{:S(2)}) collective-permute-start(bf16[32,1536]{1,0:T(8,128)(2,1)S(1)} %get-tuple-element.66), channel_id=1, source_target_pairs={{0,6},{2,4},{4,2},{6,0},{8,14},{10,12},{12,10},{14,8},{1,7},{3,5},... | collective-permute-start | bytes 294920 | tf_op jit(solution)/shard_map/ppermute | solution.py:394
  36.6 0.5 %collective-permute-start.13 = (bf16[32,1536]{1,0:T(8,128)(2,1)S(1)}, bf16[32,1536]{1,0:T(8,128)(2,1)S(1)}, u32[]{:S(2)}, u32[]{:S(2)}) collective-permute-start(bf16[32,1536]{1,0:T(8,128)(2,1)S(1)} %get-tuple-element.67), channel_id=1, source_target_pairs={{0,4},{2,6},{4,0},{6,2},{8,12},{10,14},{12,8},{14,10},{1,5},{3,7},... | collective-permute-start | bytes 294920 | tf_op jit(solution)/shard_map/ppermute | solution.py:394
  37.1 0.0 collective-permute-done.10.refs_3_
  37.1 1.6 %collective-permute-start.14 = (bf16[32,1536]{1,0:T(8,128)(2,1)S(1)}, bf16[32,1536]{1,0:T(8,128)(2,1)S(1)}, u32[]{:S(2)}, u32[]{:S(2)}) collective-permute-start(bf16[32,1536]{1,0:T(8,128)(2,1)S(1)} %get-tuple-element.68), channel_id=1, source_target_pairs={{0,2},{2,0},{4,6},{6,4},{8,10},{10,8},{12,14},{14,12},{1,3},{3,1},... | collective-permute-start | bytes 294920 | tf_op jit(solution)/shard_map/ppermute | solution.py:394
  38.8 0.0 copy-done.3
  38.8 0.6 %shard_map.100.w_ref = f32[256,1536]{1,0:T(8,128)S(1)} custom-call(bf16[128,1536]{1,0:T(8,128)(2,1)S(1)} %collective-permute-done.3.s_ref._, f32[256,1536]{1,0:T(8,128)S(1)} %get-tuple-element.53.y_ref._, bf16[256,48]{1,0:T(8,128)(2,1)S(1)} %get-tuple-element.54.fade_ref, bf16[256,128]{1,0:T(8,128)(2,1)S(1)} %get-tuple-element.55.entry_ref), custom_call_target="tpu_custom_call" | custom-call | flops 1024 | bytes 1024 | tf_op jit(solution)/shard_map/pallas_call | solution.py:462
  39.4 0.0 collective-permute-done.8.refs_1_
  39.4 0.0 collective-permute-done.9.refs_2_
  39.4 0.9 %shard_map.102.refs_0_ = bf16[256,1536]{1,0:T(8,128)(2,1)} custom-call(f32[256,1536]{1,0:T(8,128)S(1)} %shard_map.100.w_ref, f32[256,1536]{1,0:T(8,128)S(1)} %get-tuple-element.56.g_ref, f32[1,1536]{1,0:T(1,128)S(1)} %reshape.28.gain_ref, bf16[32,1536]{1,0:T(8,128)(2,1)S(1)} %get-tuple-element.59.refs_0_, ...), custom_call_target="tpu_custom_call" | custom-call | flops 1024 | bytes 1024 | tf_op jit(solution)/shard_map/pallas_call | solution.py:487
  40.3 1.3 %collective-permute-done.12.refs_2_ = bf16[32,1536]{1,0:T(8,128)(2,1)S(1)} collective-permute-done((bf16[32,1536]{1,0:T(8,128)(2,1)S(1)}, bf16[32,1536]{1,0:T(8,128)(2,1)S(1)}, u32[]{:S(2)}, u32[]{:S(2)}) %collective-permute-start.12) | collective-permute-done | bytes 98336 | tf_op jit(solution)/shard_map/ppermute | solution.py:394
  41.7 0.0 collective-permute-done.13.refs_3_
  41.7 0.9 %shard_map.104.refs_0_ = bf16[256,1536]{1,0:T(8,128)(2,1)} custom-call(f32[256,1536]{1,0:T(8,128)S(1)} %shard_map.100.w_ref, f32[256,1536]{1,0:T(8,128)S(1)} %get-tuple-element.56.g_ref, f32[1,1536]{1,0:T(1,128)S(1)} %reshape.28.gain_ref, bf16[256,1536]{1,0:T(8,128)(2,1)} %shard_map.102.refs_0_, ...), custom_call_target="tpu_custom_call", output_to_operand_aliasing={{}: (3, {})} | custom-call | flops 1024 | bytes 1024 | tf_op jit(solution)/shard_map/pallas_call | solution.py:487
  42.6 0.0 collective-permute-done.14.refs_1_
  42.6 0.8 %shard_map.105 = bf16[256,1536]{1,0:T(8,128)(2,1)} custom-call(f32[256,1536]{1,0:T(8,128)S(1)} %shard_map.100.w_ref, f32[256,1536]{1,0:T(8,128)S(1)} %get-tuple-element.56.g_ref, f32[1,1536]{1,0:T(1,128)S(1)} %reshape.28.gain_ref, bf16[256,1536]{1,0:T(8,128)(2,1)} %shard_map.104.refs_0_, ...), custom_call_target="tpu_custom_call", output_to_operand_aliasing={{}: (3, {})} | custom-call | flops 1024 | bytes 1024 | tf_op jit(solution)/shard_map/pallas_call | solution.py:487
  (1 shorter events, 0.0 us)
Async XLA Ops:
  0.0 5.9 %copy-start = (bf16[1,32,8,1536]{3,2,1,0:T(8,128)(2,1)S(1)}, bf16[1,32,8,1536]{3,2,1,0:T(8,128)(2,1)}, u32[]{:S(2)}) copy-start(bf16[1,32,8,1536]{3,2,1,0:T(8,128)(2,1)} %param.9) | copy-start | bytes 2359300
  1.3 9.1 %collective-permute-start = (bf16[32,1664]{1,0:T(8,128)(2,1)S(1)}, bf16[32,1664]{1,0:T(8,128)(2,1)S(1)}, u32[]{:S(2)}, u32[]{:S(2)}) collective-permute-start(bf16[32,1664]{1,0:T(8,128)(2,1)S(1)} %get-tuple-element.44), channel_id=1, source_target_pairs={{0,2},{2,0},{4,6},{6,4},{8,10},{10,8},{12,14},{14,12},{1,3},{3,1},... | collective-permute-start | bytes 319496 | tf_op jit(solution)/shard_map/ppermute | solution.py:394
  4.4 6.1 %collective-permute-start.1 = (bf16[32,1664]{1,0:T(8,128)(2,1)S(1)}, bf16[32,1664]{1,0:T(8,128)(2,1)S(1)}, u32[]{:S(2)}, u32[]{:S(2)}) collective-permute-start(bf16[32,1664]{1,0:T(8,128)(2,1)S(1)} %get-tuple-element.45), channel_id=1, source_target_pairs={{0,4},{2,6},{4,0},{6,2},{8,12},{10,14},{12,8},{14,10},{1,5},{3,7},... | collective-permute-start | bytes 319496 | tf_op jit(solution)/shard_map/ppermute | solution.py:394
  5.9 6.3 %collective-permute-start.2 = (bf16[32,1664]{1,0:T(8,128)(2,1)S(1)}, bf16[32,1664]{1,0:T(8,128)(2,1)S(1)}, u32[]{:S(2)}, u32[]{:S(2)}) collective-permute-start(bf16[32,1664]{1,0:T(8,128)(2,1)S(1)} %get-tuple-element.46), channel_id=1, source_target_pairs={{0,6},{2,4},{4,2},{6,0},{8,14},{10,12},{12,10},{14,8},{1,7},{3,5},... | collective-permute-start | bytes 319496 | tf_op jit(solution)/shard_map/ppermute | solution.py:394
  6.0 16.8 %collective-permute-start.4 = (bf16[32,1664]{1,0:T(8,128)(2,1)S(1)}, bf16[32,1664]{1,0:T(8,128)(2,1)S(1)}, u32[]{:S(2)}, u32[]{:S(2)}) collective-permute-start(bf16[32,1664]{1,0:T(8,128)(2,1)S(1)} %get-tuple-element.48), channel_id=1, source_target_pairs={{0,2},{2,0},{4,6},{6,4},{8,10},{10,8},{12,14},{14,12},{1,3},{3,1},... | collective-permute-start | bytes 319496 | tf_op jit(solution)/shard_map/ppermute | solution.py:394
  8.0 14.9 %collective-permute-start.5 = (bf16[32,1664]{1,0:T(8,128)(2,1)S(1)}, bf16[32,1664]{1,0:T(8,128)(2,1)S(1)}, u32[]{:S(2)}, u32[]{:S(2)}) collective-permute-start(bf16[32,1664]{1,0:T(8,128)(2,1)S(1)} %get-tuple-element.49), channel_id=1, source_target_pairs={{0,4},{2,6},{4,0},{6,2},{8,12},{10,14},{12,8},{14,10},{1,5},{3,7},... | collective-permute-start | bytes 319496 | tf_op jit(solution)/shard_map/ppermute | solution.py:394
  13.4 9.5 %collective-permute-start.6 = (bf16[32,1664]{1,0:T(8,128)(2,1)S(1)}, bf16[32,1664]{1,0:T(8,128)(2,1)S(1)}, u32[]{:S(2)}, u32[]{:S(2)}) collective-permute-start(bf16[32,1664]{1,0:T(8,128)(2,1)S(1)} %get-tuple-element.50), channel_id=1, source_target_pairs={{0,6},{2,4},{4,2},{6,0},{8,14},{10,12},{12,10},{14,8},{1,7},{3,5},... | collective-permute-start | bytes 319496 | tf_op jit(solution)/shard_map/ppermute | solution.py:394
  17.5 12.1 %collective-permute-start.7 = (bf16[64,1536]{1,0:T(8,128)(2,1)S(1)}, bf16[64,1536]{1,0:T(8,128)(2,1)S(1)}, u32[]{:S(2)}, u32[]{:S(2)}) collective-permute-start(bf16[64,1536]{1,0:T(8,128)(2,1)S(1)} %shard_map.93._), channel_id=1, source_target_pairs={{0,8},{2,10},{4,12},{6,14},{8,0},{10,2},{12,4},{14,6},{1,9},{3,11}... | collective-permute-start | bytes 589832 | tf_op jit(solution)/shard_map/ppermute | solution.py:330
  20.1 14.7 %collective-permute-start.3 = (bf16[128,1536]{1,0:T(8,128)(2,1)S(1)}, bf16[128,1536]{1,0:T(8,128)(2,1)S(1)}, u32[]{:S(2)}, u32[]{:S(2)}) collective-permute-start(bf16[128,1536]{1,0:T(8,128)(2,1)S(1)} %shard_map.94.refs_4_), channel_id=1, source_target_pairs={{0,16},{16,0},{1,17},{17,1},{2,18},{18,2},{3,19},{19,3},{4,20},{20... | collective-permute-start | bytes 1179656 | tf_op jit(solution)/shard_map/ppermute | solution.py:330
  22.9 2.8 %copy-start.1 = (bf16[1,32,8,1536]{3,2,1,0:T(8,128)(2,1)S(1)}, bf16[1,32,8,1536]{3,2,1,0:T(8,128)(2,1)}, u32[]{:S(2)}) copy-start(bf16[1,32,8,1536]{3,2,1,0:T(8,128)(2,1)} %param.10) | copy-start | bytes 2359300
  22.9 2.8 %copy-start.2 = (f32[24]{0:T(128)S(1)}, f32[24]{0:T(128)}, u32[]{:S(2)}) copy-start(f32[24]{0:T(128)} %param.16) | copy-start | bytes 292
  25.3 9.6 %collective-permute-start.11 = (bf16[64,1536]{1,0:T(8,128)(2,1)S(1)}, bf16[64,1536]{1,0:T(8,128)(2,1)S(1)}, u32[]{:S(2)}, u32[]{:S(2)}) collective-permute-start(bf16[64,1536]{1,0:T(8,128)(2,1)S(1)} %shard_map.98._), channel_id=1, source_target_pairs={{0,8},{2,10},{4,12},{6,14},{8,0},{10,2},{12,4},{14,6},{1,9},{3,11}... | collective-permute-start | bytes 589832 | tf_op jit(solution)/shard_map/ppermute | solution.py:330
  29.6 9.1 %copy-start.3 = (f32[1536]{0:T(1024)S(1)}, f32[1536]{0:T(1024)}, u32[]{:S(2)}) copy-start(f32[1536]{0:T(1024)} %param.17) | copy-start | bytes 18436
  30.0 7.2 %collective-permute-start.10 = (bf16[32,1536]{1,0:T(8,128)(2,1)S(1)}, bf16[32,1536]{1,0:T(8,128)(2,1)S(1)}, u32[]{:S(2)}, u32[]{:S(2)}) collective-permute-start(bf16[32,1536]{1,0:T(8,128)(2,1)S(1)} %get-tuple-element.62), channel_id=1, source_target_pairs={{0,6},{2,4},{4,2},{6,0},{8,14},{10,12},{12,10},{14,8},{1,7},{3,5},... | collective-permute-start | bytes 294920 | tf_op jit(solution)/shard_map/ppermute | solution.py:394
  32.7 6.7 %collective-permute-start.8 = (bf16[32,1536]{1,0:T(8,128)(2,1)S(1)}, bf16[32,1536]{1,0:T(8,128)(2,1)S(1)}, u32[]{:S(2)}, u32[]{:S(2)}) collective-permute-start(bf16[32,1536]{1,0:T(8,128)(2,1)S(1)} %get-tuple-element.60), channel_id=1, source_target_pairs={{0,2},{2,0},{4,6},{6,4},{8,10},{10,8},{12,14},{14,12},{1,3},{3,1},... | collective-permute-start | bytes 294920 | tf_op jit(solution)/shard_map/ppermute | solution.py:394
  32.9 6.5 %collective-permute-start.9 = (bf16[32,1536]{1,0:T(8,128)(2,1)S(1)}, bf16[32,1536]{1,0:T(8,128)(2,1)S(1)}, u32[]{:S(2)}, u32[]{:S(2)}) collective-permute-start(bf16[32,1536]{1,0:T(8,128)(2,1)S(1)} %get-tuple-element.61), channel_id=1, source_target_pairs={{0,4},{2,6},{4,0},{6,2},{8,12},{10,14},{12,8},{14,10},{1,5},{3,7},... | collective-permute-start | bytes 294920 | tf_op jit(solution)/shard_map/ppermute | solution.py:394
  35.2 6.5 %collective-permute-start.12 = (bf16[32,1536]{1,0:T(8,128)(2,1)S(1)}, bf16[32,1536]{1,0:T(8,128)(2,1)S(1)}, u32[]{:S(2)}, u32[]{:S(2)}) collective-permute-start(bf16[32,1536]{1,0:T(8,128)(2,1)S(1)} %get-tuple-element.66), channel_id=1, source_target_pairs={{0,6},{2,4},{4,2},{6,0},{8,14},{10,12},{12,10},{14,8},{1,7},{3,5},... | collective-permute-start | bytes 294920 | tf_op jit(solution)/shard_map/ppermute | solution.py:394
  36.6 5.1 %collective-permute-start.13 = (bf16[32,1536]{1,0:T(8,128)(2,1)S(1)}, bf16[32,1536]{1,0:T(8,128)(2,1)S(1)}, u32[]{:S(2)}, u32[]{:S(2)}) collective-permute-start(bf16[32,1536]{1,0:T(8,128)(2,1)S(1)} %get-tuple-element.67), channel_id=1, source_target_pairs={{0,4},{2,6},{4,0},{6,2},{8,12},{10,14},{12,8},{14,10},{1,5},{3,7},... | collective-permute-start | bytes 294920 | tf_op jit(solution)/shard_map/ppermute | solution.py:394
  37.1 5.4 %collective-permute-start.14 = (bf16[32,1536]{1,0:T(8,128)(2,1)S(1)}, bf16[32,1536]{1,0:T(8,128)(2,1)S(1)}, u32[]{:S(2)}, u32[]{:S(2)}) collective-permute-start(bf16[32,1536]{1,0:T(8,128)(2,1)S(1)} %get-tuple-element.68), channel_id=1, source_target_pairs={{0,2},{2,0},{4,6},{6,4},{8,10},{10,8},{12,14},{14,12},{1,3},{3,1},... | collective-permute-start | bytes 294920 | tf_op jit(solution)/shard_map/ppermute | solution.py:394

commit v17 on v15

--- a/solution.py
+++ b/solution.py
@@ -278,17 +278,18 @@
         w_ref[:, part] = y_ref[:, part] + dot(entry_ref[...], s_ref[:, part]) * dot(fade_ref[...], pick)
 
 
-def final_kernel(w_ref, g_ref, gain_ref, *refs, group, axis, offset, share):
-    blocks, (out_ref, made, sems) = refs[:group], refs[-3:]
+def final_kernel(w_ref, g_ref, gain_ref, *refs, which, offset, group, axis, share):
+    blocks, (out_ref, made, sems) = refs[-3 - len(which) : -3], refs[-3:]
     rows, channels = blocks[0].shape
     member = mod(lax.axis_index(axis), group)
     copies = []
-    for s in range(group):
-        part = pl.ds(pl.multiple_of(partner(member, s, group) * share + offset, 16), rows)
-        v = (blocks[s][...].astype(F32) + w_ref[part, :]) * g_ref[part, :]
+    for i, block in zip(which, blocks):
+        part = pl.ds(pl.multiple_of(partner(member, i, group) * share + offset, 16), rows)
+        v = (block[...].astype(F32) + w_ref[part, :]) * g_ref[part, :]
         power = jnp.sum(v * v, axis=1, keepdims=True) / channels
-        made[s] = (v * lax.rsqrt(power + 1e-5) * gain_ref[...]).astype(BF16)
-        copies.append(pltpu.make_async_copy(made.at[s], out_ref.at[part, :], sems.at[s]))
+        at = len(copies)
+        made[at] = (v * lax.rsqrt(power + 1e-5) * gain_ref[...]).astype(BF16)
+        copies.append(pltpu.make_async_copy(made.at[at], out_ref.at[part, :], sems.at[at]))
         copies[-1].start()
     for copy in copies:
         copy.wait()
@@ -458,18 +459,23 @@
         back.append(exchange(y_row))
         before = col_entering
 
+    which = [0, *range(group - 1, 0, -1)]
     mixed = None
-    for (first, rows, _, _), blocks in zip(parts_of, back):
+    for i in range(len(parts_of)):
+        first, rows = parts_of[i][:2]
         more = [] if mixed is None else [mixed]
         mixed = call(
-            functools.partial(final_kernel, offset=first, share=share, **shared),
+            functools.partial(final_kernel, which=which, offset=first, share=share, **shared),
             shape((tokens, channels), BF16),
             0,
-            specs=[None] * (3 + group) + [any_spec] * len(more),
+            specs=[None] * 3 + [any_spec] * len(more) + [None] * len(which),
             out_specs=any_spec,
-            scratch_shapes=[pltpu.VMEM((group, rows, channels), BF16), pltpu.SemaphoreType.DMA((group,))],
-            input_output_aliases={3 + group: 0} if more else {},
-        )(w, silu, norm_gain.reshape(1, channels), *blocks, *more)
+            scratch_shapes=[
+                pltpu.VMEM((len(which), rows, channels), BF16),
+                pltpu.SemaphoreType.DMA((len(which),)),
+            ],
+            input_output_aliases={3: 0} if more else {},
+        )(w, silu, norm_gain.reshape(1, channels), *more, *[back[i][j] for j in which])
     return mixed.reshape(x_in.shape)
 
 

time: 41.5 us -> 41.1 us (level)
  the two profiles are of different devices: /device:TPU:0 before, /device:TPU:30 now
where the time goes in v17:
time: 41.1 us; the launch traced here: 40.9 us
  starting transfers between devices  16.4 us (40%)
  Pallas kernels  13.1 us (32%)
  waiting for transfers between devices  10.6 us (26%)
  between operations  0.81 us (2%)
    ppermute x12, starting transfers between devices, exchange(): lax.ppermute(blocks[i], 'col', [(at, partner(at, i, group)) for at in ran...  12.7 us
    ppermute x12, waiting for transfers between devices, exchange(): lax.ppermute(blocks[i], 'col', [(at, partner(at, i, group)) for at in ran...  6.41 us
    ppermute x3, waiting for transfers between devices, entering_states(): entering = lax.ppermute(ends, axis, onward)  4.21 us
    ppermute x3, starting transfers between devices, entering_states(): entering = lax.ppermute(ends, axis, onward)  3.68 us
    pallas_call x2, Pallas kernels, of_own(): call(functools.partial(row_local_kernel, offset=offset, **sizes, **shared...  2.43 us
    pallas_call x2, Pallas kernels, body(): call(functools.partial(row_state_kernel, count=len(piece), **sizes, **sha...  2.21 us
    pallas_call x1, Pallas kernels, body(): call(functools.partial(col_local_kernel, **sizes), [pltpu.VMEM((tokens, c...  2.15 us
    pallas_call x2, Pallas kernels, body(): call(functools.partial(final_kernel, which=which, offset=first, share=sha...  1.89 us
  transfers between devices with their start and end apart: 15, of which 6 were waited for; matrix products, arithmetic and copies ran while one was open for 0% of the time, Pallas kernels for 26%

profile of v17, /device:TPU:30, one launch (start us, length us, event | category | flops | bytes accessed | tf_op | source)
XLA Modules:
  0.0 40.9 jit_solution(2488534534680861447)
XLA Ops:
  0.0 0.0 copy-start
  0.0 1.5 %shard_map.91 = (bf16[256,48]{1,0:T(8,128)(2,1)S(1)}, bf16[256,64]{1,0:T(8,128)(2,1)S(1)}, f32[48,1000]{1,0:T(8,128)S(1)}, f32[2,24]{1,0:T(2,128)S(1)}, bf16[32,...) custom-call(bf16[256,1536]{1,0:T(8,128)(2,1)} %bitcast.7, ...), custom_call_target="tpu_custom_call" | custom-call | flops 1000001024 | bytes 1024 | tf_op jit(solution)/shard_map/pallas_call | solution.py:348
  1.5 0.6 %collective-permute-start = (bf16[32,1664]{1,0:T(8,128)(2,1)S(1)}, bf16[32,1664]{1,0:T(8,128)(2,1)S(1)}, u32[]{:S(2)}, u32[]{:S(2)}) collective-permute-start(bf16[32,1664]{1,0:T(8,128)(2,1)S(1)} %get-tuple-element.44), channel_id=1, source_target_pairs={{0,2},{2,0},{4,6},{6,4},{8,10},{10,8},{12,14},{14,12},{1,3},{3,1},... | collective-permute-start | bytes 319496 | tf_op jit(solution)/shard_map/ppermute | solution.py:376
  2.1 0.4 %collective-permute-start.1 = (bf16[32,1664]{1,0:T(8,128)(2,1)S(1)}, bf16[32,1664]{1,0:T(8,128)(2,1)S(1)}, u32[]{:S(2)}, u32[]{:S(2)}) collective-permute-start(bf16[32,1664]{1,0:T(8,128)(2,1)S(1)} %get-tuple-element.45), channel_id=1, source_target_pairs={{0,4},{2,6},{4,0},{6,2},{8,12},{10,14},{12,8},{14,10},{1,5},{3,7},... | collective-permute-start | bytes 319496 | tf_op jit(solution)/shard_map/ppermute | solution.py:376
  2.5 2.5 %collective-permute-start.2 = (bf16[32,1664]{1,0:T(8,128)(2,1)S(1)}, bf16[32,1664]{1,0:T(8,128)(2,1)S(1)}, u32[]{:S(2)}, u32[]{:S(2)}) collective-permute-start(bf16[32,1664]{1,0:T(8,128)(2,1)S(1)} %get-tuple-element.46), channel_id=1, source_target_pairs={{0,6},{2,4},{4,2},{6,0},{8,14},{10,12},{12,10},{14,8},{1,7},{3,5},... | collective-permute-start | bytes 319496 | tf_op jit(solution)/shard_map/ppermute | solution.py:376
  5.0 0.5 %collective-permute-start.4 = (bf16[32,1664]{1,0:T(8,128)(2,1)S(1)}, bf16[32,1664]{1,0:T(8,128)(2,1)S(1)}, u32[]{:S(2)}, u32[]{:S(2)}) collective-permute-start(bf16[32,1664]{1,0:T(8,128)(2,1)S(1)} %get-tuple-element.48), channel_id=1, source_target_pairs={{0,2},{2,0},{4,6},{6,4},{8,10},{10,8},{12,14},{14,12},{1,3},{3,1},... | collective-permute-start | bytes 319496 | tf_op jit(solution)/shard_map/ppermute | solution.py:376
  5.5 0.4 %collective-permute-start.5 = (bf16[32,1664]{1,0:T(8,128)(2,1)S(1)}, bf16[32,1664]{1,0:T(8,128)(2,1)S(1)}, u32[]{:S(2)}, u32[]{:S(2)}) collective-permute-start(bf16[32,1664]{1,0:T(8,128)(2,1)S(1)} %get-tuple-element.49), channel_id=1, source_target_pairs={{0,4},{2,6},{4,0},{6,2},{8,12},{10,14},{12,8},{14,10},{1,5},{3,7},... | collective-permute-start | bytes 319496 | tf_op jit(solution)/shard_map/ppermute | solution.py:376
  6.6 0.2 shard_map.92.params_ref.refs_4_
  6.8 0.0 collective-permute-done.refs_1_
  6.8 2.6 %collective-permute-start.6 = (bf16[32,1664]{1,0:T(8,128)(2,1)S(1)}, bf16[32,1664]{1,0:T(8,128)(2,1)S(1)}, u32[]{:S(2)}, u32[]{:S(2)}) collective-permute-start(bf16[32,1664]{1,0:T(8,128)(2,1)S(1)} %get-tuple-element.50), channel_id=1, source_target_pairs={{0,6},{2,4},{4,2},{6,0},{8,14},{10,12},{12,10},{14,8},{1,7},{3,5},... | collective-permute-start | bytes 319496 | tf_op jit(solution)/shard_map/ppermute | solution.py:376
  9.4 0.0 collective-permute-done.1.refs_2_
  9.4 1.8 %collective-permute-done.2.refs_3_ = bf16[32,1664]{1,0:T(8,128)(2,1)S(1)} collective-permute-done((bf16[32,1664]{1,0:T(8,128)(2,1)S(1)}, bf16[32,1664]{1,0:T(8,128)(2,1)S(1)}, u32[]{:S(2)}, u32[]{:S(2)}) %collective-permute-start.2) | collective-permute-done | bytes 106528 | tf_op jit(solution)/shard_map/ppermute | solution.py:376
  11.2 1.1 %shard_map.93._ = bf16[64,1536]{1,0:T(8,128)(2,1)S(1)} custom-call(f32[8,48]{1,0:T(8,128)S(1)} %shard_map.92.params_ref.refs_4_, bf16[32,1664]{1,0:T(8,128)(2,1)S(1)} %get-tuple-element.43.refs_0_, bf16[32,1664]{1,0:T(8,128)(2,1)S(1)} %collective-permute-done.refs_1_, bf16[32,1664]{1,0:T(8,128)(2,1)S(1)} %collective-permute-done.1.refs_2_, ...), custom_call_target="tpu_custom_call" | custom-call | flops 1024 | bytes 1024 | tf_op jit(solution)/shard_map/pallas_call | solution.py:411
  12.3 0.4 collective-permute-start.7
  12.7 0.0 copy-done
  12.7 1.5 %shard_map.94.refs_4_ = bf16[128,1536]{1,0:T(8,128)(2,1)S(1)} custom-call(f32[8,48]{1,0:T(8,128)S(1)} %shard_map.92.params_ref.refs_4_, bf16[256,1536]{1,0:T(8,128)(2,1)S(1)} %bitcast.8, bf16[256,48]{1,0:T(8,128)(2,1)S(1)} %get-tuple-element.41.raw_ref, bf16[256,64]{1,0:T(8,128)(2,1)S(1)} %get-tuple-element.42.maps_ref, bf16[64,1536]{1,0:T(8,128)(2,1)S(1)} %shard_map.93._), custom_call_target="tpu_custom_call" | custom-call | flops 1024 | bytes 1024 | tf_op jit(solution)/shard_map/pallas_call | solution.py:419
  14.2 0.6 %collective-permute-start.3 = (bf16[128,1536]{1,0:T(8,128)(2,1)S(1)}, bf16[128,1536]{1,0:T(8,128)(2,1)S(1)}, u32[]{:S(2)}, u32[]{:S(2)}) collective-permute-start(bf16[128,1536]{1,0:T(8,128)(2,1)S(1)} %shard_map.94.refs_4_), channel_id=1, source_target_pairs={{0,16},{16,0},{1,17},{17,1},{2,18},{18,2},{3,19},{19,3},{4,20},{20... | collective-permute-start | bytes 1179656 | tf_op jit(solution)/shard_map/ppermute | solution.py:318
  14.8 1.2 %shard_map.95 = (f32[128,1536]{1,0:T(8,128)S(1)}, bf16[128,48]{1,0:T(8,128)(2,1)S(1)}, bf16[128,64]{1,0:T(8,128)(2,1)S(1)}) custom-call(f32[8,48]{1,0:T(8,128)S(1)} %shard_map.92.params_ref.refs_4_, bf16[32,1664]{1,0:T(8,128)(2,1)S(1)} %get-tuple-element.43.refs_0_, bf16[32,1664]{1,0:T(8,128)(2,1)S(1)} %collective-permute-done.refs_1_, ...), custom_call_target="tpu_custom_call" | custom-call | flops 2000001024 | bytes 1024 | tf_op jit(solution)/shard_map/pallas_call | solution.py:395
  16.0 0.0 collective-permute-done.4.refs_1_
  16.0 0.0 collective-permute-done.5.refs_2_
  16.0 0.0 collective-permute-done.6.refs_3_
  16.0 0.0 copy-start.1
  16.1 0.0 copy-start.2
  16.1 1.2 %shard_map.96 = (f32[128,1536]{1,0:T(8,128)S(1)}, bf16[128,48]{1,0:T(8,128)(2,1)S(1)}, bf16[128,64]{1,0:T(8,128)(2,1)S(1)}) custom-call(f32[8,48]{1,0:T(8,128)S(1)} %shard_map.92.params_ref.refs_4_, bf16[32,1664]{1,0:T(8,128)(2,1)S(1)} %get-tuple-element.47.refs_0_, bf16[32,1664]{1,0:T(8,128)(2,1)S(1)} %collective-permute-done.4.refs_1_, ...), custom_call_target="tpu_custom_call" | custom-call | flops 2000001024 | bytes 1024 | tf_op jit(solution)/shard_map/pallas_call | solution.py:395
  17.3 1.1 %shard_map.97._ = bf16[64,1536]{1,0:T(8,128)(2,1)S(1)} custom-call(f32[8,48]{1,0:T(8,128)S(1)} %shard_map.92.params_ref.refs_4_, bf16[32,1664]{1,0:T(8,128)(2,1)S(1)} %get-tuple-element.47.refs_0_, bf16[32,1664]{1,0:T(8,128)(2,1)S(1)} %collective-permute-done.4.refs_1_, bf16[32,1664]{1,0:T(8,128)(2,1)S(1)} %collective-permute-done.5.refs_2_, ...), custom_call_target="tpu_custom_call" | custom-call | flops 1024 | bytes 1024 | tf_op jit(solution)/shard_map/pallas_call | solution.py:411
  18.4 2.7 %collective-permute-start.11 = (bf16[64,1536]{1,0:T(8,128)(2,1)S(1)}, bf16[64,1536]{1,0:T(8,128)(2,1)S(1)}, u32[]{:S(2)}, u32[]{:S(2)}) collective-permute-start(bf16[64,1536]{1,0:T(8,128)(2,1)S(1)} %shard_map.97._), channel_id=1, source_target_pairs={{0,8},{2,10},{4,12},{6,14},{8,0},{10,2},{12,4},{14,6},{1,9},{3,11}... | collective-permute-start | bytes 589832 | tf_op jit(solution)/shard_map/ppermute | solution.py:318
  21.1 0.0 copy-done.1
  21.1 0.0 copy-done.2
  21.1 2.1 %shard_map.98 = (f32[256,1536]{1,0:T(8,128)S(1)}, f32[256,1536]{1,0:T(8,128)S(1)}, bf16[256,48]{1,0:T(8,128)(2,1)S(1)}, bf16[256,128]{1,0:T(8,128)(2,1)S(1)}) custom-call(f32[8,48]{1,0:T(8,128)S(1)} %shard_map.92.params_ref.refs_4_, bf16[256,1536]{1,0:T(8,128)(2,1)S(1)} %bitcast.9, bf16[256,48]{1,0:T(8,128)(2,1)S(1)} %get-tuple-element.41.raw_ref, ...), custom_call_target="tpu_custom_call" | custom-call | flops 1024 | bytes 1024 | tf_op jit(solution)/shard_map/pallas_call | solution.py:433
  23.3 4.2 %collective-permute-done.7.s_ref = bf16[64,1536]{1,0:T(8,128)(2,1)S(1)} collective-permute-done((bf16[64,1536]{1,0:T(8,128)(2,1)S(1)}, bf16[64,1536]{1,0:T(8,128)(2,1)S(1)}, u32[]{:S(2)}, u32[]{:S(2)}) %collective-permute-start.7) | collective-permute-done | bytes 196640 | tf_op jit(solution)/shard_map/ppermute | solution.py:318
  27.5 0.0 copy-start.3
  27.5 0.3 shard_map.100
  27.8 0.6 %collective-permute-start.10 = (bf16[32,1536]{1,0:T(8,128)(2,1)S(1)}, bf16[32,1536]{1,0:T(8,128)(2,1)S(1)}, u32[]{:S(2)}, u32[]{:S(2)}) collective-permute-start(bf16[32,1536]{1,0:T(8,128)(2,1)S(1)} %get-tuple-element.62), channel_id=1, source_target_pairs={{0,2},{2,0},{4,6},{6,4},{8,10},{10,8},{12,14},{14,12},{1,3},{3,1},... | collective-permute-start | bytes 294920 | tf_op jit(solution)/shard_map/ppermute | solution.py:376
  28.5 0.0 collective-permute-start.8
  28.5 2.9 %collective-permute-start.9 = (bf16[32,1536]{1,0:T(8,128)(2,1)S(1)}, bf16[32,1536]{1,0:T(8,128)(2,1)S(1)}, u32[]{:S(2)}, u32[]{:S(2)}) collective-permute-start(bf16[32,1536]{1,0:T(8,128)(2,1)S(1)} %get-tuple-element.61), channel_id=1, source_target_pairs={{0,4},{2,6},{4,0},{6,2},{8,12},{10,14},{12,8},{14,10},{1,5},{3,7},... | collective-permute-start | bytes 294920 | tf_op jit(solution)/shard_map/ppermute | solution.py:376
  31.4 0.0 collective-permute-done.11.s_ref
  31.4 0.0 collective-permute-done.3.s_ref._
  31.4 0.3 shard_map.102
  31.8 0.1 collective-permute-start.12
  31.8 2.0 %collective-permute-start.13 = (bf16[32,1536]{1,0:T(8,128)(2,1)S(1)}, bf16[32,1536]{1,0:T(8,128)(2,1)S(1)}, u32[]{:S(2)}, u32[]{:S(2)}) collective-permute-start(bf16[32,1536]{1,0:T(8,128)(2,1)S(1)} %get-tuple-element.67), channel_id=1, source_target_pairs={{0,4},{2,6},{4,0},{6,2},{8,12},{10,14},{12,8},{14,10},{1,5},{3,7},... | collective-permute-start | bytes 294920 | tf_op jit(solution)/shard_map/ppermute | solution.py:376
  33.9 1.5 %collective-permute-done.10.refs_3_ = bf16[32,1536]{1,0:T(8,128)(2,1)S(1)} collective-permute-done((bf16[32,1536]{1,0:T(8,128)(2,1)S(1)}, bf16[32,1536]{1,0:T(8,128)(2,1)S(1)}, u32[]{:S(2)}, u32[]{:S(2)}) %collective-permute-start.10) | collective-permute-done | bytes 98336 | tf_op jit(solution)/shard_map/ppermute | solution.py:376
  35.4 0.0 collective-permute-start.14
  35.4 0.0 copy-done.3
  35.4 0.6 %shard_map.99.w_ref = f32[256,1536]{1,0:T(8,128)S(1)} custom-call(bf16[128,1536]{1,0:T(8,128)(2,1)S(1)} %collective-permute-done.3.s_ref._, f32[256,1536]{1,0:T(8,128)S(1)} %get-tuple-element.53.y_ref._, bf16[256,48]{1,0:T(8,128)(2,1)S(1)} %get-tuple-element.54.fade_ref, bf16[256,128]{1,0:T(8,128)(2,1)S(1)} %get-tuple-element.55.entry_ref), custom_call_target="tpu_custom_call" | custom-call | flops 1024 | bytes 1024 | tf_op jit(solution)/shard_map/pallas_call | solution.py:444
  36.0 0.0 collective-permute-done.8.refs_1_
  36.0 0.0 collective-permute-done.9.refs_2_
  36.0 0.9 %shard_map.101.refs_0_ = bf16[256,1536]{1,0:T(8,128)(2,1)} custom-call(f32[256,1536]{1,0:T(8,128)S(1)} %shard_map.99.w_ref, f32[256,1536]{1,0:T(8,128)S(1)} %get-tuple-element.56.g_ref, f32[1,1536]{1,0:T(1,128)S(1)} %reshape.27.gain_ref, bf16[32,1536]{1,0:T(8,128)(2,1)S(1)} %get-tuple-element.59.refs_0_, ...), custom_call_target="tpu_custom_call" | custom-call | flops 1024 | bytes 1024 | tf_op jit(solution)/shard_map/pallas_call | solution.py:467
  36.9 0.4 collective-permute-done.12.refs_2_
  37.3 0.7 %collective-permute-done.13.refs_3_ = bf16[32,1536]{1,0:T(8,128)(2,1)S(1)} collective-permute-done((bf16[32,1536]{1,0:T(8,128)(2,1)S(1)}, bf16[32,1536]{1,0:T(8,128)(2,1)S(1)}, u32[]{:S(2)}, u32[]{:S(2)}) %collective-permute-start.13) | collective-permute-done | bytes 98336 | tf_op jit(solution)/shard_map/ppermute | solution.py:376
  38.0 2.0 %collective-permute-done.14.refs_4_ = bf16[32,1536]{1,0:T(8,128)(2,1)S(1)} collective-permute-done((bf16[32,1536]{1,0:T(8,128)(2,1)S(1)}, bf16[32,1536]{1,0:T(8,128)(2,1)S(1)}, u32[]{:S(2)}, u32[]{:S(2)}) %collective-permute-start.14) | collective-permute-done | bytes 98336 | tf_op jit(solution)/shard_map/ppermute | solution.py:376
  40.0 0.9 %shard_map.103 = bf16[256,1536]{1,0:T(8,128)(2,1)} custom-call(f32[256,1536]{1,0:T(8,128)S(1)} %shard_map.99.w_ref, f32[256,1536]{1,0:T(8,128)S(1)} %get-tuple-element.56.g_ref, f32[1,1536]{1,0:T(1,128)S(1)} %reshape.27.gain_ref, bf16[256,1536]{1,0:T(8,128)(2,1)} %shard_map.101.refs_0_, ...), custom_call_target="tpu_custom_call", output_to_operand_aliasing={{}: (3, {})} | custom-call | flops 1024 | bytes 1024 | tf_op jit(solution)/shard_map/pallas_call | solution.py:467
  (1 shorter events, 0.0 us)
Async XLA Ops:
  0.0 12.7 %copy-start = (bf16[1,32,8,1536]{3,2,1,0:T(8,128)(2,1)S(1)}, bf16[1,32,8,1536]{3,2,1,0:T(8,128)(2,1)}, u32[]{:S(2)}) copy-start(bf16[1,32,8,1536]{3,2,1,0:T(8,128)(2,1)} %param.9) | copy-start | bytes 2359300
  1.5 5.3 %collective-permute-start = (bf16[32,1664]{1,0:T(8,128)(2,1)S(1)}, bf16[32,1664]{1,0:T(8,128)(2,1)S(1)}, u32[]{:S(2)}, u32[]{:S(2)}) collective-permute-start(bf16[32,1664]{1,0:T(8,128)(2,1)S(1)} %get-tuple-element.44), channel_id=1, source_target_pairs={{0,2},{2,0},{4,6},{6,4},{8,10},{10,8},{12,14},{14,12},{1,3},{3,1},... | collective-permute-start | bytes 319496 | tf_op jit(solution)/shard_map/ppermute | solution.py:376
  2.1 7.3 %collective-permute-start.1 = (bf16[32,1664]{1,0:T(8,128)(2,1)S(1)}, bf16[32,1664]{1,0:T(8,128)(2,1)S(1)}, u32[]{:S(2)}, u32[]{:S(2)}) collective-permute-start(bf16[32,1664]{1,0:T(8,128)(2,1)S(1)} %get-tuple-element.45), channel_id=1, source_target_pairs={{0,4},{2,6},{4,0},{6,2},{8,12},{10,14},{12,8},{14,10},{1,5},{3,7},... | collective-permute-start | bytes 319496 | tf_op jit(solution)/shard_map/ppermute | solution.py:376
  2.5 8.7 %collective-permute-start.2 = (bf16[32,1664]{1,0:T(8,128)(2,1)S(1)}, bf16[32,1664]{1,0:T(8,128)(2,1)S(1)}, u32[]{:S(2)}, u32[]{:S(2)}) collective-permute-start(bf16[32,1664]{1,0:T(8,128)(2,1)S(1)} %get-tuple-element.46), channel_id=1, source_target_pairs={{0,6},{2,4},{4,2},{6,0},{8,14},{10,12},{12,10},{14,8},{1,7},{3,5},... | collective-permute-start | bytes 319496 | tf_op jit(solution)/shard_map/ppermute | solution.py:376
  5.0 11.0 %collective-permute-start.4 = (bf16[32,1664]{1,0:T(8,128)(2,1)S(1)}, bf16[32,1664]{1,0:T(8,128)(2,1)S(1)}, u32[]{:S(2)}, u32[]{:S(2)}) collective-permute-start(bf16[32,1664]{1,0:T(8,128)(2,1)S(1)} %get-tuple-element.48), channel_id=1, source_target_pairs={{0,2},{2,0},{4,6},{6,4},{8,10},{10,8},{12,14},{14,12},{1,3},{3,1},... | collective-permute-start | bytes 319496 | tf_op jit(solution)/shard_map/ppermute | solution.py:376
  5.5 10.5 %collective-permute-start.5 = (bf16[32,1664]{1,0:T(8,128)(2,1)S(1)}, bf16[32,1664]{1,0:T(8,128)(2,1)S(1)}, u32[]{:S(2)}, u32[]{:S(2)}) collective-permute-start(bf16[32,1664]{1,0:T(8,128)(2,1)S(1)} %get-tuple-element.49), channel_id=1, source_target_pairs={{0,4},{2,6},{4,0},{6,2},{8,12},{10,14},{12,8},{14,10},{1,5},{3,7},... | collective-permute-start | bytes 319496 | tf_op jit(solution)/shard_map/ppermute | solution.py:376
  6.8 9.2 %collective-permute-start.6 = (bf16[32,1664]{1,0:T(8,128)(2,1)S(1)}, bf16[32,1664]{1,0:T(8,128)(2,1)S(1)}, u32[]{:S(2)}, u32[]{:S(2)}) collective-permute-start(bf16[32,1664]{1,0:T(8,128)(2,1)S(1)} %get-tuple-element.50), channel_id=1, source_target_pairs={{0,6},{2,4},{4,2},{6,0},{8,14},{10,12},{12,10},{14,8},{1,7},{3,5},... | collective-permute-start | bytes 319496 | tf_op jit(solution)/shard_map/ppermute | solution.py:376
  12.3 15.2 %collective-permute-start.7 = (bf16[64,1536]{1,0:T(8,128)(2,1)S(1)}, bf16[64,1536]{1,0:T(8,128)(2,1)S(1)}, u32[]{:S(2)}, u32[]{:S(2)}) collective-permute-start(bf16[64,1536]{1,0:T(8,128)(2,1)S(1)} %shard_map.93._), channel_id=1, source_target_pairs={{0,8},{2,10},{4,12},{6,14},{8,0},{10,2},{12,4},{14,6},{1,9},{3,11}... | collective-permute-start | bytes 589832 | tf_op jit(solution)/shard_map/ppermute | solution.py:318
  14.2 17.2 %collective-permute-start.3 = (bf16[128,1536]{1,0:T(8,128)(2,1)S(1)}, bf16[128,1536]{1,0:T(8,128)(2,1)S(1)}, u32[]{:S(2)}, u32[]{:S(2)}) collective-permute-start(bf16[128,1536]{1,0:T(8,128)(2,1)S(1)} %shard_map.94.refs_4_), channel_id=1, source_target_pairs={{0,16},{16,0},{1,17},{17,1},{2,18},{18,2},{3,19},{19,3},{4,20},{20... | collective-permute-start | bytes 1179656 | tf_op jit(solution)/shard_map/ppermute | solution.py:318
  16.0 5.1 %copy-start.1 = (bf16[1,32,8,1536]{3,2,1,0:T(8,128)(2,1)S(1)}, bf16[1,32,8,1536]{3,2,1,0:T(8,128)(2,1)}, u32[]{:S(2)}) copy-start(bf16[1,32,8,1536]{3,2,1,0:T(8,128)(2,1)} %param.10) | copy-start | bytes 2359300
  16.1 5.1 %copy-start.2 = (f32[24]{0:T(128)S(1)}, f32[24]{0:T(128)}, u32[]{:S(2)}) copy-start(f32[24]{0:T(128)} %param.16) | copy-start | bytes 292
  18.4 13.0 %collective-permute-start.11 = (bf16[64,1536]{1,0:T(8,128)(2,1)S(1)}, bf16[64,1536]{1,0:T(8,128)(2,1)S(1)}, u32[]{:S(2)}, u32[]{:S(2)}) collective-permute-start(bf16[64,1536]{1,0:T(8,128)(2,1)S(1)} %shard_map.97._), channel_id=1, source_target_pairs={{0,8},{2,10},{4,12},{6,14},{8,0},{10,2},{12,4},{14,6},{1,9},{3,11}... | collective-permute-start | bytes 589832 | tf_op jit(solution)/shard_map/ppermute | solution.py:318
  27.5 7.9 %copy-start.3 = (f32[1536]{0:T(1024)S(1)}, f32[1536]{0:T(1024)}, u32[]{:S(2)}) copy-start(f32[1536]{0:T(1024)} %param.17) | copy-start | bytes 18436
  27.8 7.5 %collective-permute-start.10 = (bf16[32,1536]{1,0:T(8,128)(2,1)S(1)}, bf16[32,1536]{1,0:T(8,128)(2,1)S(1)}, u32[]{:S(2)}, u32[]{:S(2)}) collective-permute-start(bf16[32,1536]{1,0:T(8,128)(2,1)S(1)} %get-tuple-element.62), channel_id=1, source_target_pairs={{0,2},{2,0},{4,6},{6,4},{8,10},{10,8},{12,14},{14,12},{1,3},{3,1},... | collective-permute-start | bytes 294920 | tf_op jit(solution)/shard_map/ppermute | solution.py:376
  28.5 7.5 %collective-permute-start.8 = (bf16[32,1536]{1,0:T(8,128)(2,1)S(1)}, bf16[32,1536]{1,0:T(8,128)(2,1)S(1)}, u32[]{:S(2)}, u32[]{:S(2)}) collective-permute-start(bf16[32,1536]{1,0:T(8,128)(2,1)S(1)} %get-tuple-element.60), channel_id=1, source_target_pairs={{0,6},{2,4},{4,2},{6,0},{8,14},{10,12},{12,10},{14,8},{1,7},{3,5},... | collective-permute-start | bytes 294920 | tf_op jit(solution)/shard_map/ppermute | solution.py:376
  28.5 7.5 %collective-permute-start.9 = (bf16[32,1536]{1,0:T(8,128)(2,1)S(1)}, bf16[32,1536]{1,0:T(8,128)(2,1)S(1)}, u32[]{:S(2)}, u32[]{:S(2)}) collective-permute-start(bf16[32,1536]{1,0:T(8,128)(2,1)S(1)} %get-tuple-element.61), channel_id=1, source_target_pairs={{0,4},{2,6},{4,0},{6,2},{8,12},{10,14},{12,8},{14,10},{1,5},{3,7},... | collective-permute-start | bytes 294920 | tf_op jit(solution)/shard_map/ppermute | solution.py:376
  31.8 5.6 %collective-permute-start.12 = (bf16[32,1536]{1,0:T(8,128)(2,1)S(1)}, bf16[32,1536]{1,0:T(8,128)(2,1)S(1)}, u32[]{:S(2)}, u32[]{:S(2)}) collective-permute-start(bf16[32,1536]{1,0:T(8,128)(2,1)S(1)} %get-tuple-element.66), channel_id=1, source_target_pairs={{0,6},{2,4},{4,2},{6,0},{8,14},{10,12},{12,10},{14,8},{1,7},{3,5},... | collective-permute-start | bytes 294920 | tf_op jit(solution)/shard_map/ppermute | solution.py:376
  31.8 6.2 %collective-permute-start.13 = (bf16[32,1536]{1,0:T(8,128)(2,1)S(1)}, bf16[32,1536]{1,0:T(8,128)(2,1)S(1)}, u32[]{:S(2)}, u32[]{:S(2)}) collective-permute-start(bf16[32,1536]{1,0:T(8,128)(2,1)S(1)} %get-tuple-element.67), channel_id=1, source_target_pairs={{0,4},{2,6},{4,0},{6,2},{8,12},{10,14},{12,8},{14,10},{1,5},{3,7},... | collective-permute-start | bytes 294920 | tf_op jit(solution)/shard_map/ppermute | solution.py:376
  35.4 4.6 %collective-permute-start.14 = (bf16[32,1536]{1,0:T(8,128)(2,1)S(1)}, bf16[32,1536]{1,0:T(8,128)(2,1)S(1)}, u32[]{:S(2)}, u32[]{:S(2)}) collective-permute-start(bf16[32,1536]{1,0:T(8,128)(2,1)S(1)} %get-tuple-element.68), channel_id=1, source_target_pairs={{0,2},{2,0},{4,6},{6,4},{8,10},{10,8},{12,14},{14,12},{1,3},{3,1},... | collective-permute-start | bytes 294920 | tf_op jit(solution)/shard_map/ppermute | solution.py:376

commit v18 on v17

--- a/solution.py
+++ b/solution.py
@@ -382,55 +382,51 @@
         return states + [shape((sum(places), heads), F32)] * (count > 2)
 
     got = [exchange(packed[i * group : (i + 1) * group]) for i in range(len(pieces))]
-    before = params
-    parts_of = []
-    for i, piece in enumerate(pieces):
-        places = [rows // cols * state for rows in piece]
-        offsets = [sum(piece[:j]) for j in range(len(piece))]
-
-        def of_own(before, i=i, piece=piece, places=places, offsets=offsets):
-            known = []
-            for offset, rows, count in zip(offsets, piece, places):
-                known.append(
-                    call(
-                        functools.partial(row_local_kernel, offset=offset, **sizes, **shared),
-                        [
-                            pltpu.VMEM((group * rows, channels), F32),
-                            pltpu.VMEM((group * rows, 2 * heads), BF16),
-                            pltpu.VMEM((group * rows, count), BF16),
-                        ],
-                        2,
-                        specs=[None] * (1 + group) + [any_spec],
-                    )(params, *got[i], before)
-                )
-                before = known[-1][1]
-            return known, before
-
-        if i:
-            known, before = of_own(before)
+
+    def own_rows(i, before):
+        known = []
+        for j, rows in enumerate(pieces[i]):
+            known.append(
+                call(
+                    functools.partial(row_local_kernel, offset=sum(pieces[i][:j]), **sizes, **shared),
+                    [
+                        pltpu.VMEM((group * rows, channels), F32),
+                        pltpu.VMEM((group * rows, 2 * heads), BF16),
+                        pltpu.VMEM((group * rows, rows // cols * state), BF16),
+                    ],
+                    2,
+                    specs=[None] * (1 + group) + [any_spec],
+                )(params, *got[i], before)
+            )
+            before = known[-1][1]
+        return known, before
+
+    def row_states(i, before):
+        places = [rows // cols * state for rows in pieces[i]]
         made = call(
-            functools.partial(row_state_kernel, count=len(piece), **sizes, **shared),
+            functools.partial(row_state_kernel, count=len(places), **sizes, **shared),
             state_shapes(places, col_count // group),
-            0 if i else 0,
+            0,
             specs=[None] * (1 + group) + [any_spec],
         )(params, *got[i], before)
-        before = made[0]
-        if i == 0:
-            col_made = call(
-                functools.partial(col_state_kernel, **sizes),
-                state_shapes([cols * state], row_count),
-                0,
-                specs=[None] * 4 + [any_spec],
-            )(params, x, raw, maps, before)
-            col_entering = entering_states(col_made[0], col_made[1:], "row", row_count, 1, width)
-            known, before = of_own(col_made[0])
-        for j, rows in enumerate(piece):
+        entering = []
+        for j, count in enumerate(places):
             first = sum(places[:j])
-            factor = [f[first : first + places[j]] for f in made[len(piece) :]]
-            entering = entering_states(made[j], factor, "col", col_count, group, width)
-            parts_of.append((sum(map(sum, pieces[:i])) + offsets[j], rows, known[j], entering))
-
-    y_col, silu, *known = call(
+            factor = [f[first : first + count] for f in made[len(places) :]]
+            entering.append(entering_states(made[j], factor, "col", col_count, group, width))
+        return entering, made[0]
+
+    known, entering = [None] * len(pieces), [None] * len(pieces)
+    entering[0], before = row_states(0, params)
+    col_made = call(
+        functools.partial(col_state_kernel, **sizes),
+        state_shapes([cols * state], row_count),
+        0,
+        specs=[None] * 4 + [any_spec],
+    )(params, x, raw, maps, before)
+    col_entering = entering_states(col_made[0], col_made[1:], "row", row_count, 1, width)
+    before = col_made[0]
+    y_col, silu, *col_known = call(
         functools.partial(col_local_kernel, **sizes),
         [
             pltpu.VMEM((tokens, channels), F32),
@@ -438,17 +434,26 @@
             pltpu.VMEM((tokens, 2 * heads), BF16),
             pltpu.VMEM((tokens, cols * state), BF16),
         ],
-        0,
+        2,
         specs=[None] * 6 + [any_spec],
     )(params, x, raw, maps, gate, skip.reshape(1, heads), before)
+    before = y_col
+    for i in range(1, len(pieces)):
+        known[i], before = own_rows(i, before)
+        entering[i], before = row_states(i, before)
+    known[0], before = own_rows(0, before)
     w = call(
         functools.partial(col_out_kernel, heads=heads, width=width),
         pltpu.VMEM((tokens, channels), F32),
         0,
-    )(col_entering, y_col, *known)
+    )(col_entering, y_col, *col_known)
+    parts_of = []
+    for i, piece in enumerate(pieces):
+        for j, rows in enumerate(piece):
+            first = sum(map(sum, pieces[:i])) + sum(piece[:j])
+            parts_of.append((first, rows, known[i][j], entering[i][j]))
 
     back = []
-    before = y_col
     for _, rows, known, entering in parts_of:
         y_row = call(
             functools.partial(row_out_kernel, heads=heads, width=width),

time: 41.1 us -> 42 us (1.022)
  the two profiles are of different devices: /device:TPU:30 before, /device:TPU:0 now
where the time goes in v18:
time: 42 us; the launch traced here: 41.8 us
  starting transfers between devices  20.2 us (48%)
  Pallas kernels  13.2 us (31%)
  waiting for transfers between devices  7.64 us (18%)
  between operations  0.83 us (2%)
    ppermute x12, starting transfers between devices, exchange(): lax.ppermute(blocks[i], 'col', [(at, partner(at, i, group)) for at in ran...  15.2 us
    ppermute x3, starting transfers between devices, entering_states(): entering = lax.ppermute(ends, axis, onward)  4.95 us
    ppermute x12, waiting for transfers between devices, exchange(): lax.ppermute(blocks[i], 'col', [(at, partner(at, i, group)) for at in ran...  4.23 us
    ppermute x3, waiting for transfers between devices, entering_states(): entering = lax.ppermute(ends, axis, onward)  3.41 us
    pallas_call x2, Pallas kernels, own_rows(): call(functools.partial(row_local_kernel, offset=sum(pieces[i][:j]), **siz...  2.46 us
    pallas_call x2, Pallas kernels, row_states(): call(functools.partial(row_state_kernel, count=len(places), **sizes, **sh...  2.22 us
    pallas_call x1, Pallas kernels, body(): call(functools.partial(col_local_kernel, **sizes), [pltpu.VMEM((tokens, c...  2.16 us
    pallas_call x2, Pallas kernels, body(): call(functools.partial(final_kernel, which=which, offset=first, share=sha...  1.89 us
  transfers between devices with their start and end apart: 15, of which 5 were waited for; matrix products, arithmetic and copies ran while one was open for 0% of the time, Pallas kernels for 26%

profile of v18, /device:TPU:0, one launch (start us, length us, event | category | flops | bytes accessed | tf_op | source)
XLA Modules:
  0.0 41.8 jit_solution(6400301955915194772)
XLA Ops:
  0.0 0.0 copy-start
  0.0 1.5 %shard_map.91 = (bf16[256,48]{1,0:T(8,128)(2,1)S(1)}, bf16[256,64]{1,0:T(8,128)(2,1)S(1)}, f32[48,1000]{1,0:T(8,128)S(1)}, f32[2,24]{1,0:T(2,128)S(1)}, bf16[32,...) custom-call(bf16[256,1536]{1,0:T(8,128)(2,1)} %bitcast.7, ...), custom_call_target="tpu_custom_call" | custom-call | flops 1000001024 | bytes 1024 | tf_op jit(solution)/shard_map/pallas_call | solution.py:348
  1.5 0.0 copy-start.1
  1.5 0.0 copy-start.2
  1.5 3.0 %collective-permute-start = (bf16[32,1664]{1,0:T(8,128)(2,1)S(1)}, bf16[32,1664]{1,0:T(8,128)(2,1)S(1)}, u32[]{:S(2)}, u32[]{:S(2)}) collective-permute-start(bf16[32,1664]{1,0:T(8,128)(2,1)S(1)} %get-tuple-element.44), channel_id=1, source_target_pairs={{0,2},{2,0},{4,6},{6,4},{8,10},{10,8},{12,14},{14,12},{1,3},{3,1},... | collective-permute-start | bytes 319496 | tf_op jit(solution)/shard_map/ppermute | solution.py:376
  4.5 1.6 %collective-permute-start.1 = (bf16[32,1664]{1,0:T(8,128)(2,1)S(1)}, bf16[32,1664]{1,0:T(8,128)(2,1)S(1)}, u32[]{:S(2)}, u32[]{:S(2)}) collective-permute-start(bf16[32,1664]{1,0:T(8,128)(2,1)S(1)} %get-tuple-element.45), channel_id=1, source_target_pairs={{0,4},{2,6},{4,0},{6,2},{8,12},{10,14},{12,8},{14,10},{1,5},{3,7},... | collective-permute-start | bytes 319496 | tf_op jit(solution)/shard_map/ppermute | solution.py:376
  6.1 0.0 collective-permute-start.2
  6.1 1.9 %collective-permute-start.5 = (bf16[32,1664]{1,0:T(8,128)(2,1)S(1)}, bf16[32,1664]{1,0:T(8,128)(2,1)S(1)}, u32[]{:S(2)}, u32[]{:S(2)}) collective-permute-start(bf16[32,1664]{1,0:T(8,128)(2,1)S(1)} %get-tuple-element.52), channel_id=1, source_target_pairs={{0,2},{2,0},{4,6},{6,4},{8,10},{10,8},{12,14},{14,12},{1,3},{3,1},... | collective-permute-start | bytes 319496 | tf_op jit(solution)/shard_map/ppermute | solution.py:376
  8.0 1.6 %collective-permute-start.6 = (bf16[32,1664]{1,0:T(8,128)(2,1)S(1)}, bf16[32,1664]{1,0:T(8,128)(2,1)S(1)}, u32[]{:S(2)}, u32[]{:S(2)}) collective-permute-start(bf16[32,1664]{1,0:T(8,128)(2,1)S(1)} %get-tuple-element.53), channel_id=1, source_target_pairs={{0,4},{2,6},{4,0},{6,2},{8,12},{10,14},{12,8},{14,10},{1,5},{3,7},... | collective-permute-start | bytes 319496 | tf_op jit(solution)/shard_map/ppermute | solution.py:376
  10.3 0.2 shard_map.92.params_ref.refs_4_
  10.4 0.0 collective-permute-done.refs_1_
  10.4 0.0 collective-permute-start.7
  10.5 0.0 collective-permute-done.1.refs_2_
  10.5 2.0 %collective-permute-done.2.refs_3_ = bf16[32,1664]{1,0:T(8,128)(2,1)S(1)} collective-permute-done((bf16[32,1664]{1,0:T(8,128)(2,1)S(1)}, bf16[32,1664]{1,0:T(8,128)(2,1)S(1)}, u32[]{:S(2)}, u32[]{:S(2)}) %collective-permute-start.2) | collective-permute-done | bytes 106528 | tf_op jit(solution)/shard_map/ppermute | solution.py:376
  12.5 1.1 %shard_map.93._ = bf16[64,1536]{1,0:T(8,128)(2,1)S(1)} custom-call(f32[8,48]{1,0:T(8,128)S(1)} %shard_map.92.params_ref.refs_4_, bf16[32,1664]{1,0:T(8,128)(2,1)S(1)} %get-tuple-element.43.refs_0_, bf16[32,1664]{1,0:T(8,128)(2,1)S(1)} %collective-permute-done.refs_1_, bf16[32,1664]{1,0:T(8,128)(2,1)S(1)} %collective-permute-done.1.refs_2_, ...), custom_call_target="tpu_custom_call" | custom-call | flops 1024 | bytes 1024 | tf_op jit(solution)/shard_map/pallas_call | solution.py:406
  13.6 3.0 %collective-permute-start.4 = (bf16[64,1536]{1,0:T(8,128)(2,1)S(1)}, bf16[64,1536]{1,0:T(8,128)(2,1)S(1)}, u32[]{:S(2)}, u32[]{:S(2)}) collective-permute-start(bf16[64,1536]{1,0:T(8,128)(2,1)S(1)} %shard_map.93._), channel_id=1, source_target_pairs={{0,8},{2,10},{4,12},{6,14},{8,0},{10,2},{12,4},{14,6},{1,9},{3,11}... | collective-permute-start | bytes 589832 | tf_op jit(solution)/shard_map/ppermute | solution.py:318
  16.6 0.0 copy-done
  16.6 1.5 %shard_map.94._ = bf16[128,1536]{1,0:T(8,128)(2,1)S(1)} custom-call(f32[8,48]{1,0:T(8,128)S(1)} %shard_map.92.params_ref.refs_4_, bf16[256,1536]{1,0:T(8,128)(2,1)S(1)} %bitcast.8, bf16[256,48]{1,0:T(8,128)(2,1)S(1)} %get-tuple-element.41.raw_ref, bf16[256,64]{1,0:T(8,128)(2,1)S(1)} %get-tuple-element.42.maps_ref, bf16[64,1536]{1,0:T(8,128)(2,1)S(1)} %shard_map.93._), custom_call_target="tpu_custom_call" | custom-call | flops 1024 | bytes 1024 | tf_op jit(solution)/shard_map/pallas_call | solution.py:421
  18.1 1.5 %collective-permute-start.3 = (bf16[128,1536]{1,0:T(8,128)(2,1)S(1)}, bf16[128,1536]{1,0:T(8,128)(2,1)S(1)}, u32[]{:S(2)}, u32[]{:S(2)}) collective-permute-start(bf16[128,1536]{1,0:T(8,128)(2,1)S(1)} %shard_map.94._), channel_id=1, source_target_pairs={{0,16},{16,0},{1,17},{17,1},{2,18},{18,2},{3,19},{19,3},{4,20},{20... | collective-permute-start | bytes 1179656 | tf_op jit(solution)/shard_map/ppermute | solution.py:318
  19.6 0.0 copy-done.1
  19.6 0.0 copy-done.2
  19.6 2.2 %shard_map.95 = (f32[256,1536]{1,0:T(8,128)S(1)}, f32[256,1536]{1,0:T(8,128)S(1)}, bf16[256,48]{1,0:T(8,128)(2,1)S(1)}, bf16[256,128]{1,0:T(8,128)(2,1)S(1)}) custom-call(f32[8,48]{1,0:T(8,128)S(1)} %shard_map.92.params_ref.refs_4_, bf16[256,1536]{1,0:T(8,128)(2,1)S(1)} %bitcast.9, bf16[256,48]{1,0:T(8,128)(2,1)S(1)} %get-tuple-element.41.raw_ref, ...), custom_call_target="tpu_custom_call" | custom-call | flops 2000001024 | bytes 1024 | tf_op jit(solution)/shard_map/pallas_call | solution.py:429
  21.8 0.0 collective-permute-done.5.refs_1_
  21.8 0.0 collective-permute-done.6.refs_2_
  21.8 0.0 collective-permute-done.7.refs_3_
  21.8 1.2 %shard_map.97 = (f32[128,1536]{1,0:T(8,128)S(1)}, bf16[128,48]{1,0:T(8,128)(2,1)S(1)}, bf16[128,64]{1,0:T(8,128)(2,1)S(1)}) custom-call(f32[8,48]{1,0:T(8,128)S(1)} %shard_map.92.params_ref.refs_4_, bf16[32,1664]{1,0:T(8,128)(2,1)S(1)} %get-tuple-element.51.refs_0_, bf16[32,1664]{1,0:T(8,128)(2,1)S(1)} %collective-permute-done.5.refs_1_, ...), custom_call_target="tpu_custom_call" | custom-call | flops 2000001024 | bytes 1024 | tf_op jit(solution)/shard_map/pallas_call | solution.py:390
  23.1 1.1 %shard_map.98.refs_4_ = bf16[64,1536]{1,0:T(8,128)(2,1)S(1)} custom-call(f32[8,48]{1,0:T(8,128)S(1)} %shard_map.92.params_ref.refs_4_, bf16[32,1664]{1,0:T(8,128)(2,1)S(1)} %get-tuple-element.51.refs_0_, bf16[32,1664]{1,0:T(8,128)(2,1)S(1)} %collective-permute-done.5.refs_1_, bf16[32,1664]{1,0:T(8,128)(2,1)S(1)} %collective-permute-done.6.refs_2_, ...), custom_call_target="tpu_custom_call" | custom-call | flops 1024 | bytes 1024 | tf_op jit(solution)/shard_map/pallas_call | solution.py:406
  24.2 0.4 collective-permute-start.11
  24.6 1.2 %shard_map.99 = (f32[128,1536]{1,0:T(8,128)S(1)}, bf16[128,48]{1,0:T(8,128)(2,1)S(1)}, bf16[128,64]{1,0:T(8,128)(2,1)S(1)}) custom-call(f32[8,48]{1,0:T(8,128)S(1)} %shard_map.92.params_ref.refs_4_, bf16[32,1664]{1,0:T(8,128)(2,1)S(1)} %get-tuple-element.43.refs_0_, bf16[32,1664]{1,0:T(8,128)(2,1)S(1)} %collective-permute-done.refs_1_, ...), custom_call_target="tpu_custom_call" | custom-call | flops 2000001024 | bytes 1024 | tf_op jit(solution)/shard_map/pallas_call | solution.py:390
  25.8 0.0 copy-start.3
  25.8 0.0 collective-permute-done.4.s_ref
  25.8 0.3 shard_map.100
  26.2 1.4 %collective-permute-start.10 = (bf16[32,1536]{1,0:T(8,128)(2,1)S(1)}, bf16[32,1536]{1,0:T(8,128)(2,1)S(1)}, u32[]{:S(2)}, u32[]{:S(2)}) collective-permute-start(bf16[32,1536]{1,0:T(8,128)(2,1)S(1)} %get-tuple-element.62), channel_id=1, source_target_pairs={{0,2},{2,0},{4,6},{6,4},{8,10},{10,8},{12,14},{14,12},{1,3},{3,1},... | collective-permute-start | bytes 294920 | tf_op jit(solution)/shard_map/ppermute | solution.py:376
  27.6 1.6 %collective-permute-start.8 = (bf16[32,1536]{1,0:T(8,128)(2,1)S(1)}, bf16[32,1536]{1,0:T(8,128)(2,1)S(1)}, u32[]{:S(2)}, u32[]{:S(2)}) collective-permute-start(bf16[32,1536]{1,0:T(8,128)(2,1)S(1)} %get-tuple-element.60), channel_id=1, source_target_pairs={{0,6},{2,4},{4,2},{6,0},{8,14},{10,12},{12,10},{14,8},{1,7},{3,5},... | collective-permute-start | bytes 294920 | tf_op jit(solution)/shard_map/ppermute | solution.py:376
  29.2 0.6 %collective-permute-start.9 = (bf16[32,1536]{1,0:T(8,128)(2,1)S(1)}, bf16[32,1536]{1,0:T(8,128)(2,1)S(1)}, u32[]{:S(2)}, u32[]{:S(2)}) collective-permute-start(bf16[32,1536]{1,0:T(8,128)(2,1)S(1)} %get-tuple-element.61), channel_id=1, source_target_pairs={{0,4},{2,6},{4,0},{6,2},{8,12},{10,14},{12,8},{14,10},{1,5},{3,7},... | collective-permute-start | bytes 294920 | tf_op jit(solution)/shard_map/ppermute | solution.py:376
  29.8 3.4 %collective-permute-done.11.s_ref = bf16[64,1536]{1,0:T(8,128)(2,1)S(1)} collective-permute-done((bf16[64,1536]{1,0:T(8,128)(2,1)S(1)}, bf16[64,1536]{1,0:T(8,128)(2,1)S(1)}, u32[]{:S(2)}, u32[]{:S(2)}) %collective-permute-start.11) | collective-permute-done | bytes 196640 | tf_op jit(solution)/shard_map/ppermute | solution.py:318
  33.2 0.0 collective-permute-done.3.s_ref._
  33.2 0.3 shard_map.102
  33.5 0.8 %collective-permute-start.12 = (bf16[32,1536]{1,0:T(8,128)(2,1)S(1)}, bf16[32,1536]{1,0:T(8,128)(2,1)S(1)}, u32[]{:S(2)}, u32[]{:S(2)}) collective-permute-start(bf16[32,1536]{1,0:T(8,128)(2,1)S(1)} %get-tuple-element.66), channel_id=1, source_target_pairs={{0,6},{2,4},{4,2},{6,0},{8,14},{10,12},{12,10},{14,8},{1,7},{3,5},... | collective-permute-start | bytes 294920 | tf_op jit(solution)/shard_map/ppermute | solution.py:376
  34.4 1.9 %collective-permute-start.13 = (bf16[32,1536]{1,0:T(8,128)(2,1)S(1)}, bf16[32,1536]{1,0:T(8,128)(2,1)S(1)}, u32[]{:S(2)}, u32[]{:S(2)}) collective-permute-start(bf16[32,1536]{1,0:T(8,128)(2,1)S(1)} %get-tuple-element.67), channel_id=1, source_target_pairs={{0,4},{2,6},{4,0},{6,2},{8,12},{10,14},{12,8},{14,10},{1,5},{3,7},... | collective-permute-start | bytes 294920 | tf_op jit(solution)/shard_map/ppermute | solution.py:376
  36.3 0.0 collective-permute-done.10.refs_3_
  36.3 0.8 %collective-permute-start.14 = (bf16[32,1536]{1,0:T(8,128)(2,1)S(1)}, bf16[32,1536]{1,0:T(8,128)(2,1)S(1)}, u32[]{:S(2)}, u32[]{:S(2)}) collective-permute-start(bf16[32,1536]{1,0:T(8,128)(2,1)S(1)} %get-tuple-element.68), channel_id=1, source_target_pairs={{0,2},{2,0},{4,6},{6,4},{8,10},{10,8},{12,14},{14,12},{1,3},{3,1},... | collective-permute-start | bytes 294920 | tf_op jit(solution)/shard_map/ppermute | solution.py:376
  37.1 0.0 copy-done.3
  37.1 0.6 %shard_map.96.w_ref = f32[256,1536]{1,0:T(8,128)S(1)} custom-call(bf16[128,1536]{1,0:T(8,128)(2,1)S(1)} %collective-permute-done.3.s_ref._, f32[256,1536]{1,0:T(8,128)S(1)} %get-tuple-element.47.y_ref.refs_4_, bf16[256,48]{1,0:T(8,128)(2,1)S(1)} %get-tuple-element.48.fade_ref, bf16[256,128]{1,0:T(8,128)(2,1)S(1)} %get-tuple-element.49.entry_ref), custom_call_target="tpu_custom_call" | custom-call | flops 1024 | bytes 1024 | tf_op jit(solution)/shard_map/pallas_call | solution.py:445
  37.7 0.0 collective-permute-done.8.refs_1_
  37.7 0.0 collective-permute-done.9.refs_2_
  37.7 0.9 %shard_map.101.refs_0_ = bf16[256,1536]{1,0:T(8,128)(2,1)} custom-call(f32[256,1536]{1,0:T(8,128)S(1)} %shard_map.96.w_ref, f32[256,1536]{1,0:T(8,128)S(1)} %get-tuple-element.50.g_ref, f32[1,1536]{1,0:T(1,128)S(1)} %reshape.27.gain_ref, bf16[32,1536]{1,0:T(8,128)(2,1)S(1)} %get-tuple-element.59.refs_0_, ...), custom_call_target="tpu_custom_call" | custom-call | flops 1024 | bytes 1024 | tf_op jit(solution)/shard_map/pallas_call | solution.py:472
  38.7 0.4 %collective-permute-done.12.refs_2_ = bf16[32,1536]{1,0:T(8,128)(2,1)S(1)} collective-permute-done((bf16[32,1536]{1,0:T(8,128)(2,1)S(1)}, bf16[32,1536]{1,0:T(8,128)(2,1)S(1)}, u32[]{:S(2)}, u32[]{:S(2)}) %collective-permute-start.12) | collective-permute-done | bytes 98336 | tf_op jit(solution)/shard_map/ppermute | solution.py:376
  39.1 0.8 %collective-permute-done.13.refs_3_ = bf16[32,1536]{1,0:T(8,128)(2,1)S(1)} collective-permute-done((bf16[32,1536]{1,0:T(8,128)(2,1)S(1)}, bf16[32,1536]{1,0:T(8,128)(2,1)S(1)}, u32[]{:S(2)}, u32[]{:S(2)}) %collective-permute-start.13) | collective-permute-done | bytes 98336 | tf_op jit(solution)/shard_map/ppermute | solution.py:376
  39.9 1.0 %collective-permute-done.14.refs_4_ = bf16[32,1536]{1,0:T(8,128)(2,1)S(1)} collective-permute-done((bf16[32,1536]{1,0:T(8,128)(2,1)S(1)}, bf16[32,1536]{1,0:T(8,128)(2,1)S(1)}, u32[]{:S(2)}, u32[]{:S(2)}) %collective-permute-start.14) | collective-permute-done | bytes 98336 | tf_op jit(solution)/shard_map/ppermute | solution.py:376
  40.9 0.9 %shard_map.103 = bf16[256,1536]{1,0:T(8,128)(2,1)} custom-call(f32[256,1536]{1,0:T(8,128)S(1)} %shard_map.96.w_ref, f32[256,1536]{1,0:T(8,128)S(1)} %get-tuple-element.50.g_ref, f32[1,1536]{1,0:T(1,128)S(1)} %reshape.27.gain_ref, bf16[256,1536]{1,0:T(8,128)(2,1)} %shard_map.101.refs_0_, ...), custom_call_target="tpu_custom_call", output_to_operand_aliasing={{}: (3, {})} | custom-call | flops 1024 | bytes 1024 | tf_op jit(solution)/shard_map/pallas_call | solution.py:472
  (1 shorter events, 0.0 us)
Async XLA Ops:
  0.0 16.6 %copy-start = (bf16[1,32,8,1536]{3,2,1,0:T(8,128)(2,1)S(1)}, bf16[1,32,8,1536]{3,2,1,0:T(8,128)(2,1)}, u32[]{:S(2)}) copy-start(bf16[1,32,8,1536]{3,2,1,0:T(8,128)(2,1)} %param.9) | copy-start | bytes 2359300
  1.5 18.1 %copy-start.1 = (bf16[1,32,8,1536]{3,2,1,0:T(8,128)(2,1)S(1)}, bf16[1,32,8,1536]{3,2,1,0:T(8,128)(2,1)}, u32[]{:S(2)}) copy-start(bf16[1,32,8,1536]{3,2,1,0:T(8,128)(2,1)} %param.10) | copy-start | bytes 2359300
  1.5 18.1 %copy-start.2 = (f32[24]{0:T(128)S(1)}, f32[24]{0:T(128)}, u32[]{:S(2)}) copy-start(f32[24]{0:T(128)} %param.16) | copy-start | bytes 292
  1.5 8.9 %collective-permute-start = (bf16[32,1664]{1,0:T(8,128)(2,1)S(1)}, bf16[32,1664]{1,0:T(8,128)(2,1)S(1)}, u32[]{:S(2)}, u32[]{:S(2)}) collective-permute-start(bf16[32,1664]{1,0:T(8,128)(2,1)S(1)} %get-tuple-element.44), channel_id=1, source_target_pairs={{0,2},{2,0},{4,6},{6,4},{8,10},{10,8},{12,14},{14,12},{1,3},{3,1},... | collective-permute-start | bytes 319496 | tf_op jit(solution)/shard_map/ppermute | solution.py:376
  4.5 5.9 %collective-permute-start.1 = (bf16[32,1664]{1,0:T(8,128)(2,1)S(1)}, bf16[32,1664]{1,0:T(8,128)(2,1)S(1)}, u32[]{:S(2)}, u32[]{:S(2)}) collective-permute-start(bf16[32,1664]{1,0:T(8,128)(2,1)S(1)} %get-tuple-element.45), channel_id=1, source_target_pairs={{0,4},{2,6},{4,0},{6,2},{8,12},{10,14},{12,8},{14,10},{1,5},{3,7},... | collective-permute-start | bytes 319496 | tf_op jit(solution)/shard_map/ppermute | solution.py:376
  6.1 6.3 %collective-permute-start.2 = (bf16[32,1664]{1,0:T(8,128)(2,1)S(1)}, bf16[32,1664]{1,0:T(8,128)(2,1)S(1)}, u32[]{:S(2)}, u32[]{:S(2)}) collective-permute-start(bf16[32,1664]{1,0:T(8,128)(2,1)S(1)} %get-tuple-element.46), channel_id=1, source_target_pairs={{0,6},{2,4},{4,2},{6,0},{8,14},{10,12},{12,10},{14,8},{1,7},{3,5},... | collective-permute-start | bytes 319496 | tf_op jit(solution)/shard_map/ppermute | solution.py:376
  6.1 15.7 %collective-permute-start.5 = (bf16[32,1664]{1,0:T(8,128)(2,1)S(1)}, bf16[32,1664]{1,0:T(8,128)(2,1)S(1)}, u32[]{:S(2)}, u32[]{:S(2)}) collective-permute-start(bf16[32,1664]{1,0:T(8,128)(2,1)S(1)} %get-tuple-element.52), channel_id=1, source_target_pairs={{0,2},{2,0},{4,6},{6,4},{8,10},{10,8},{12,14},{14,12},{1,3},{3,1},... | collective-permute-start | bytes 319496 | tf_op jit(solution)/shard_map/ppermute | solution.py:376
  8.0 13.8 %collective-permute-start.6 = (bf16[32,1664]{1,0:T(8,128)(2,1)S(1)}, bf16[32,1664]{1,0:T(8,128)(2,1)S(1)}, u32[]{:S(2)}, u32[]{:S(2)}) collective-permute-start(bf16[32,1664]{1,0:T(8,128)(2,1)S(1)} %get-tuple-element.53), channel_id=1, source_target_pairs={{0,4},{2,6},{4,0},{6,2},{8,12},{10,14},{12,8},{14,10},{1,5},{3,7},... | collective-permute-start | bytes 319496 | tf_op jit(solution)/shard_map/ppermute | solution.py:376
  10.4 11.4 %collective-permute-start.7 = (bf16[32,1664]{1,0:T(8,128)(2,1)S(1)}, bf16[32,1664]{1,0:T(8,128)(2,1)S(1)}, u32[]{:S(2)}, u32[]{:S(2)}) collective-permute-start(bf16[32,1664]{1,0:T(8,128)(2,1)S(1)} %get-tuple-element.54), channel_id=1, source_target_pairs={{0,6},{2,4},{4,2},{6,0},{8,14},{10,12},{12,10},{14,8},{1,7},{3,5},... | collective-permute-start | bytes 319496 | tf_op jit(solution)/shard_map/ppermute | solution.py:376
  13.6 12.3 %collective-permute-start.4 = (bf16[64,1536]{1,0:T(8,128)(2,1)S(1)}, bf16[64,1536]{1,0:T(8,128)(2,1)S(1)}, u32[]{:S(2)}, u32[]{:S(2)}) collective-permute-start(bf16[64,1536]{1,0:T(8,128)(2,1)S(1)} %shard_map.93._), channel_id=1, source_target_pairs={{0,8},{2,10},{4,12},{6,14},{8,0},{10,2},{12,4},{14,6},{1,9},{3,11}... | collective-permute-start | bytes 589832 | tf_op jit(solution)/shard_map/ppermute | solution.py:318
  18.1 15.1 %collective-permute-start.3 = (bf16[128,1536]{1,0:T(8,128)(2,1)S(1)}, bf16[128,1536]{1,0:T(8,128)(2,1)S(1)}, u32[]{:S(2)}, u32[]{:S(2)}) collective-permute-start(bf16[128,1536]{1,0:T(8,128)(2,1)S(1)} %shard_map.94._), channel_id=1, source_target_pairs={{0,16},{16,0},{1,17},{17,1},{2,18},{18,2},{3,19},{19,3},{4,20},{20... | collective-permute-start | bytes 1179656 | tf_op jit(solution)/shard_map/ppermute | solution.py:318
  24.2 9.0 %collective-permute-start.11 = (bf16[64,1536]{1,0:T(8,128)(2,1)S(1)}, bf16[64,1536]{1,0:T(8,128)(2,1)S(1)}, u32[]{:S(2)}, u32[]{:S(2)}) collective-permute-start(bf16[64,1536]{1,0:T(8,128)(2,1)S(1)} %shard_map.98.refs_4_), channel_id=1, source_target_pairs={{0,8},{2,10},{4,12},{6,14},{8,0},{10,2},{12,4},{14,6},{1,9},{3,11}... | collective-permute-start | bytes 589832 | tf_op jit(solution)/shard_map/ppermute | solution.py:318
  25.8 11.2 %copy-start.3 = (f32[1536]{0:T(1024)S(1)}, f32[1536]{0:T(1024)}, u32[]{:S(2)}) copy-start(f32[1536]{0:T(1024)} %param.17) | copy-start | bytes 18436
  26.2 10.1 %collective-permute-start.10 = (bf16[32,1536]{1,0:T(8,128)(2,1)S(1)}, bf16[32,1536]{1,0:T(8,128)(2,1)S(1)}, u32[]{:S(2)}, u32[]{:S(2)}) collective-permute-start(bf16[32,1536]{1,0:T(8,128)(2,1)S(1)} %get-tuple-element.62), channel_id=1, source_target_pairs={{0,2},{2,0},{4,6},{6,4},{8,10},{10,8},{12,14},{14,12},{1,3},{3,1},... | collective-permute-start | bytes 294920 | tf_op jit(solution)/shard_map/ppermute | solution.py:376
  27.6 10.1 %collective-permute-start.8 = (bf16[32,1536]{1,0:T(8,128)(2,1)S(1)}, bf16[32,1536]{1,0:T(8,128)(2,1)S(1)}, u32[]{:S(2)}, u32[]{:S(2)}) collective-permute-start(bf16[32,1536]{1,0:T(8,128)(2,1)S(1)} %get-tuple-element.60), channel_id=1, source_target_pairs={{0,6},{2,4},{4,2},{6,0},{8,14},{10,12},{12,10},{14,8},{1,7},{3,5},... | collective-permute-start | bytes 294920 | tf_op jit(solution)/shard_map/ppermute | solution.py:376
  29.2 8.5 %collective-permute-start.9 = (bf16[32,1536]{1,0:T(8,128)(2,1)S(1)}, bf16[32,1536]{1,0:T(8,128)(2,1)S(1)}, u32[]{:S(2)}, u32[]{:S(2)}) collective-permute-start(bf16[32,1536]{1,0:T(8,128)(2,1)S(1)} %get-tuple-element.61), channel_id=1, source_target_pairs={{0,4},{2,6},{4,0},{6,2},{8,12},{10,14},{12,8},{14,10},{1,5},{3,7},... | collective-permute-start | bytes 294920 | tf_op jit(solution)/shard_map/ppermute | solution.py:376
  33.5 5.6 %collective-permute-start.12 = (bf16[32,1536]{1,0:T(8,128)(2,1)S(1)}, bf16[32,1536]{1,0:T(8,128)(2,1)S(1)}, u32[]{:S(2)}, u32[]{:S(2)}) collective-permute-start(bf16[32,1536]{1,0:T(8,128)(2,1)S(1)} %get-tuple-element.66), channel_id=1, source_target_pairs={{0,6},{2,4},{4,2},{6,0},{8,14},{10,12},{12,10},{14,8},{1,7},{3,5},... | collective-permute-start | bytes 294920 | tf_op jit(solution)/shard_map/ppermute | solution.py:376
  34.4 5.6 %collective-permute-start.13 = (bf16[32,1536]{1,0:T(8,128)(2,1)S(1)}, bf16[32,1536]{1,0:T(8,128)(2,1)S(1)}, u32[]{:S(2)}, u32[]{:S(2)}) collective-permute-start(bf16[32,1536]{1,0:T(8,128)(2,1)S(1)} %get-tuple-element.67), channel_id=1, source_target_pairs={{0,4},{2,6},{4,0},{6,2},{8,12},{10,14},{12,8},{14,10},{1,5},{3,7},... | collective-permute-start | bytes 294920 | tf_op jit(solution)/shard_map/ppermute | solution.py:376
  36.3 4.6 %collective-permute-start.14 = (bf16[32,1536]{1,0:T(8,128)(2,1)S(1)}, bf16[32,1536]{1,0:T(8,128)(2,1)S(1)}, u32[]{:S(2)}, u32[]{:S(2)}) collective-permute-start(bf16[32,1536]{1,0:T(8,128)(2,1)S(1)} %get-tuple-element.68), channel_id=1, source_target_pairs={{0,2},{2,0},{4,6},{6,4},{8,10},{10,8},{12,14},{14,12},{1,3},{3,1},... | collective-permute-start | bytes 294920 | tf_op jit(solution)/shard_map/ppermute | solution.py:376

commit v19 on v18

--- a/solution.py
+++ b/solution.py
@@ -311,10 +311,10 @@
     )
 
 
-def entering_states(ends, factor, axis, size, stride, width):
+def entering_states(ends, factor, axis, size, stride, width, wrap=True):
     if size == stride:
         return ends
-    onward = [(i, (i + stride) % size) for i in range(size)]
+    onward = [(i, (i + stride) % size) for i in range(size if wrap else size - stride)]
     entering = lax.ppermute(ends, axis, onward)
     for _ in range(size // stride - 2):
         follows = (lax.axis_index(axis) >= stride).astype(F32)
@@ -413,7 +413,7 @@
         for j, count in enumerate(places):
             first = sum(places[:j])
             factor = [f[first : first + count] for f in made[len(places) :]]
-            entering.append(entering_states(made[j], factor, "col", col_count, group, width))
+            entering.append(entering_states(made[j], factor, "col", col_count, group, width, wrap=i == 0))
         return entering, made[0]
 
     known, entering = [None] * len(pieces), [None] * len(pieces)

time: 42 us -> 41.1 us (0.979)
  waiting for transfers between devices: 7.64 us -> 4.43 us
  starting transfers between devices: 20.2 us -> 22.5 us
    ppermute x3, waiting for transfers between devices: 3.41 us -> 0.06 us  [entering_states(): entering = lax.ppermute(ends, axis, onward)]
    ppermute x3, starting transfers between devices: 4.95 us -> 6.8 us  [entering_states(): entering = lax.ppermute(ends, axis, onward)]
    ppermute x12, starting transfers between devices: 15.2 us -> 15.7 us  [exchange(): lax.ppermute(blocks[i], 'col', [(at, partner(at, i, group)) for at in ran...]
where the time goes in v19:
time: 41.1 us; the launch traced here: 40.9 us
  starting transfers between devices  22.5 us (55%)
  Pallas kernels  13.1 us (32%)
  waiting for transfers between devices  4.43 us (11%)
  between operations  0.85 us (2%)
    ppermute x12, starting transfers between devices, exchange(): lax.ppermute(blocks[i], 'col', [(at, partner(at, i, group)) for at in ran...  15.7 us
    ppermute x3, starting transfers between devices, entering_states(): entering = lax.ppermute(ends, axis, onward)  6.8 us
    ppermute x12, waiting for transfers between devices, exchange(): lax.ppermute(blocks[i], 'col', [(at, partner(at, i, group)) for at in ran...  4.36 us
    pallas_call x2, Pallas kernels, own_rows(): call(functools.partial(row_local_kernel, offset=sum(pieces[i][:j]), **siz...  2.45 us
    pallas_call x2, Pallas kernels, row_states(): call(functools.partial(row_state_kernel, count=len(places), **sizes, **sh...  2.22 us
    pallas_call x1, Pallas kernels, body(): call(functools.partial(col_local_kernel, **sizes), [pltpu.VMEM((tokens, c...  2.16 us
    pallas_call x2, Pallas kernels, body(): call(functools.partial(final_kernel, which=which, offset=first, share=sha...  1.89 us
    pallas_call x1, Pallas kernels, body(): call(functools.partial(col_state_kernel, **sizes), state_shapes([cols * s...  1.48 us
  transfers between devices with their start and end apart: 15, of which 5 were waited for; matrix products, arithmetic and copies ran while one was open for 0% of the time, Pallas kernels for 26%

profile of v19, /device:TPU:0, one launch (start us, length us, event | category | flops | bytes accessed | tf_op | source)
XLA Modules:
  0.0 40.9 jit_solution(624398582030621640)
XLA Ops:
  0.0 0.0 copy-start
  0.0 1.5 %shard_map.91 = (bf16[256,48]{1,0:T(8,128)(2,1)S(1)}, bf16[256,64]{1,0:T(8,128)(2,1)S(1)}, f32[48,1000]{1,0:T(8,128)S(1)}, f32[2,24]{1,0:T(2,128)S(1)}, bf16[32,...) custom-call(bf16[256,1536]{1,0:T(8,128)(2,1)} %bitcast.7, ...), custom_call_target="tpu_custom_call" | custom-call | flops 1000001024 | bytes 1024 | tf_op jit(solution)/shard_map/pallas_call | solution.py:348
  1.5 0.0 copy-start.1
  1.5 0.0 copy-start.2
  1.5 3.0 %collective-permute-start = (bf16[32,1664]{1,0:T(8,128)(2,1)S(1)}, bf16[32,1664]{1,0:T(8,128)(2,1)S(1)}, u32[]{:S(2)}, u32[]{:S(2)}) collective-permute-start(bf16[32,1664]{1,0:T(8,128)(2,1)S(1)} %get-tuple-element.44), channel_id=1, source_target_pairs={{0,2},{2,0},{4,6},{6,4},{8,10},{10,8},{12,14},{14,12},{1,3},{3,1},... | collective-permute-start | bytes 319496 | tf_op jit(solution)/shard_map/ppermute | solution.py:376
  4.5 1.6 %collective-permute-start.1 = (bf16[32,1664]{1,0:T(8,128)(2,1)S(1)}, bf16[32,1664]{1,0:T(8,128)(2,1)S(1)}, u32[]{:S(2)}, u32[]{:S(2)}) collective-permute-start(bf16[32,1664]{1,0:T(8,128)(2,1)S(1)} %get-tuple-element.45), channel_id=1, source_target_pairs={{0,4},{2,6},{4,0},{6,2},{8,12},{10,14},{12,8},{14,10},{1,5},{3,7},... | collective-permute-start | bytes 319496 | tf_op jit(solution)/shard_map/ppermute | solution.py:376
  6.1 0.0 collective-permute-start.2
  6.1 1.9 %collective-permute-start.5 = (bf16[32,1664]{1,0:T(8,128)(2,1)S(1)}, bf16[32,1664]{1,0:T(8,128)(2,1)S(1)}, u32[]{:S(2)}, u32[]{:S(2)}) collective-permute-start(bf16[32,1664]{1,0:T(8,128)(2,1)S(1)} %get-tuple-element.52), channel_id=1, source_target_pairs={{0,2},{2,0},{4,6},{6,4},{8,10},{10,8},{12,14},{14,12},{1,3},{3,1},... | collective-permute-start | bytes 319496 | tf_op jit(solution)/shard_map/ppermute | solution.py:376
  8.0 1.6 %collective-permute-start.6 = (bf16[32,1664]{1,0:T(8,128)(2,1)S(1)}, bf16[32,1664]{1,0:T(8,128)(2,1)S(1)}, u32[]{:S(2)}, u32[]{:S(2)}) collective-permute-start(bf16[32,1664]{1,0:T(8,128)(2,1)S(1)} %get-tuple-element.53), channel_id=1, source_target_pairs={{0,4},{2,6},{4,0},{6,2},{8,12},{10,14},{12,8},{14,10},{1,5},{3,7},... | collective-permute-start | bytes 319496 | tf_op jit(solution)/shard_map/ppermute | solution.py:376
  10.3 0.2 shard_map.92.params_ref.refs_4_
  10.4 0.0 collective-permute-done.refs_1_
  10.4 0.0 collective-permute-start.7
  10.5 0.0 collective-permute-done.1.refs_2_
  10.5 2.0 %collective-permute-done.2.refs_3_ = bf16[32,1664]{1,0:T(8,128)(2,1)S(1)} collective-permute-done((bf16[32,1664]{1,0:T(8,128)(2,1)S(1)}, bf16[32,1664]{1,0:T(8,128)(2,1)S(1)}, u32[]{:S(2)}, u32[]{:S(2)}) %collective-permute-start.2) | collective-permute-done | bytes 106528 | tf_op jit(solution)/shard_map/ppermute | solution.py:376
  12.5 1.1 %shard_map.93._ = bf16[64,1536]{1,0:T(8,128)(2,1)S(1)} custom-call(f32[8,48]{1,0:T(8,128)S(1)} %shard_map.92.params_ref.refs_4_, bf16[32,1664]{1,0:T(8,128)(2,1)S(1)} %get-tuple-element.43.refs_0_, bf16[32,1664]{1,0:T(8,128)(2,1)S(1)} %collective-permute-done.refs_1_, bf16[32,1664]{1,0:T(8,128)(2,1)S(1)} %collective-permute-done.1.refs_2_, ...), custom_call_target="tpu_custom_call" | custom-call | flops 1024 | bytes 1024 | tf_op jit(solution)/shard_map/pallas_call | solution.py:406
  13.6 3.0 %collective-permute-start.4 = (bf16[64,1536]{1,0:T(8,128)(2,1)S(1)}, bf16[64,1536]{1,0:T(8,128)(2,1)S(1)}, u32[]{:S(2)}, u32[]{:S(2)}) collective-permute-start(bf16[64,1536]{1,0:T(8,128)(2,1)S(1)} %shard_map.93._), channel_id=1, source_target_pairs={{0,8},{2,10},{4,12},{6,14},{8,0},{10,2},{12,4},{14,6},{1,9},{3,11}... | collective-permute-start | bytes 589832 | tf_op jit(solution)/shard_map/ppermute | solution.py:318
  16.6 0.0 copy-done
  16.6 1.5 %shard_map.94._ = bf16[128,1536]{1,0:T(8,128)(2,1)S(1)} custom-call(f32[8,48]{1,0:T(8,128)S(1)} %shard_map.92.params_ref.refs_4_, bf16[256,1536]{1,0:T(8,128)(2,1)S(1)} %bitcast.8, bf16[256,48]{1,0:T(8,128)(2,1)S(1)} %get-tuple-element.41.raw_ref, bf16[256,64]{1,0:T(8,128)(2,1)S(1)} %get-tuple-element.42.maps_ref, bf16[64,1536]{1,0:T(8,128)(2,1)S(1)} %shard_map.93._), custom_call_target="tpu_custom_call" | custom-call | flops 1024 | bytes 1024 | tf_op jit(solution)/shard_map/pallas_call | solution.py:421
  18.1 1.5 %collective-permute-start.3 = (bf16[128,1536]{1,0:T(8,128)(2,1)S(1)}, bf16[128,1536]{1,0:T(8,128)(2,1)S(1)}, u32[]{:S(2)}, u32[]{:S(2)}) collective-permute-start(bf16[128,1536]{1,0:T(8,128)(2,1)S(1)} %shard_map.94._), channel_id=1, source_target_pairs={{0,16},{16,0},{1,17},{17,1},{2,18},{18,2},{3,19},{19,3},{4,20},{20... | collective-permute-start | bytes 1179656 | tf_op jit(solution)/shard_map/ppermute | solution.py:318
  19.6 0.0 copy-done.1
  19.6 0.0 copy-done.2
  19.6 2.2 %shard_map.95 = (f32[256,1536]{1,0:T(8,128)S(1)}, f32[256,1536]{1,0:T(8,128)S(1)}, bf16[256,48]{1,0:T(8,128)(2,1)S(1)}, bf16[256,128]{1,0:T(8,128)(2,1)S(1)}) custom-call(f32[8,48]{1,0:T(8,128)S(1)} %shard_map.92.params_ref.refs_4_, bf16[256,1536]{1,0:T(8,128)(2,1)S(1)} %bitcast.9, bf16[256,48]{1,0:T(8,128)(2,1)S(1)} %get-tuple-element.41.raw_ref, ...), custom_call_target="tpu_custom_call" | custom-call | flops 2000001024 | bytes 1024 | tf_op jit(solution)/shard_map/pallas_call | solution.py:429
  21.8 0.0 collective-permute-done.5.refs_1_
  21.8 0.0 collective-permute-done.6.refs_2_
  21.8 0.0 collective-permute-done.7.refs_3_
  21.8 1.2 %shard_map.97 = (f32[128,1536]{1,0:T(8,128)S(1)}, bf16[128,48]{1,0:T(8,128)(2,1)S(1)}, bf16[128,64]{1,0:T(8,128)(2,1)S(1)}) custom-call(f32[8,48]{1,0:T(8,128)S(1)} %shard_map.92.params_ref.refs_4_, bf16[32,1664]{1,0:T(8,128)(2,1)S(1)} %get-tuple-element.51.refs_0_, bf16[32,1664]{1,0:T(8,128)(2,1)S(1)} %collective-permute-done.5.refs_1_, ...), custom_call_target="tpu_custom_call" | custom-call | flops 2000001024 | bytes 1024 | tf_op jit(solution)/shard_map/pallas_call | solution.py:390
  23.1 1.1 %shard_map.98.refs_4_ = bf16[64,1536]{1,0:T(8,128)(2,1)S(1)} custom-call(f32[8,48]{1,0:T(8,128)S(1)} %shard_map.92.params_ref.refs_4_, bf16[32,1664]{1,0:T(8,128)(2,1)S(1)} %get-tuple-element.51.refs_0_, bf16[32,1664]{1,0:T(8,128)(2,1)S(1)} %collective-permute-done.5.refs_1_, bf16[32,1664]{1,0:T(8,128)(2,1)S(1)} %collective-permute-done.6.refs_2_, ...), custom_call_target="tpu_custom_call" | custom-call | flops 1024 | bytes 1024 | tf_op jit(solution)/shard_map/pallas_call | solution.py:406
  24.2 2.3 %collective-permute-start.11 = (bf16[64,1536]{1,0:T(8,128)(2,1)S(1)}, bf16[64,1536]{1,0:T(8,128)(2,1)S(1)}, u32[]{:S(2)}, u32[]{:S(2)}) collective-permute-start(bf16[64,1536]{1,0:T(8,128)(2,1)S(1)} %shard_map.98.refs_4_), channel_id=1, source_target_pairs={{0,8},{2,10},{4,12},{6,14},{1,9},{3,11},{5,13},{7,15},{16,24},{18,... | collective-permute-start | bytes 589832 | tf_op jit(solution)/shard_map/ppermute | solution.py:318
  26.4 1.2 %shard_map.99 = (f32[128,1536]{1,0:T(8,128)S(1)}, bf16[128,48]{1,0:T(8,128)(2,1)S(1)}, bf16[128,64]{1,0:T(8,128)(2,1)S(1)}) custom-call(f32[8,48]{1,0:T(8,128)S(1)} %shard_map.92.params_ref.refs_4_, bf16[32,1664]{1,0:T(8,128)(2,1)S(1)} %get-tuple-element.43.refs_0_, bf16[32,1664]{1,0:T(8,128)(2,1)S(1)} %collective-permute-done.refs_1_, ...), custom_call_target="tpu_custom_call" | custom-call | flops 2000001024 | bytes 1024 | tf_op jit(solution)/shard_map/pallas_call | solution.py:390
  27.7 0.0 copy-start.3
  27.7 0.0 collective-permute-done.4.s_ref
  27.7 0.3 shard_map.100
  28.0 1.4 %collective-permute-start.10 = (bf16[32,1536]{1,0:T(8,128)(2,1)S(1)}, bf16[32,1536]{1,0:T(8,128)(2,1)S(1)}, u32[]{:S(2)}, u32[]{:S(2)}) collective-permute-start(bf16[32,1536]{1,0:T(8,128)(2,1)S(1)} %get-tuple-element.62), channel_id=1, source_target_pairs={{0,2},{2,0},{4,6},{6,4},{8,10},{10,8},{12,14},{14,12},{1,3},{3,1},... | collective-permute-start | bytes 294920 | tf_op jit(solution)/shard_map/ppermute | solution.py:376
  29.4 1.6 %collective-permute-start.8 = (bf16[32,1536]{1,0:T(8,128)(2,1)S(1)}, bf16[32,1536]{1,0:T(8,128)(2,1)S(1)}, u32[]{:S(2)}, u32[]{:S(2)}) collective-permute-start(bf16[32,1536]{1,0:T(8,128)(2,1)S(1)} %get-tuple-element.60), channel_id=1, source_target_pairs={{0,6},{2,4},{4,2},{6,0},{8,14},{10,12},{12,10},{14,8},{1,7},{3,5},... | collective-permute-start | bytes 294920 | tf_op jit(solution)/shard_map/ppermute | solution.py:376
  31.0 0.6 %collective-permute-start.9 = (bf16[32,1536]{1,0:T(8,128)(2,1)S(1)}, bf16[32,1536]{1,0:T(8,128)(2,1)S(1)}, u32[]{:S(2)}, u32[]{:S(2)}) collective-permute-start(bf16[32,1536]{1,0:T(8,128)(2,1)S(1)} %get-tuple-element.61), channel_id=1, source_target_pairs={{0,4},{2,6},{4,0},{6,2},{8,12},{10,14},{12,8},{14,10},{1,5},{3,7},... | collective-permute-start | bytes 294920 | tf_op jit(solution)/shard_map/ppermute | solution.py:376
  31.6 0.1 collective-permute-done.11.s_ref
  31.7 0.0 collective-permute-done.3.s_ref._
  31.7 0.3 shard_map.102
  32.0 2.4 %collective-permute-start.12 = (bf16[32,1536]{1,0:T(8,128)(2,1)S(1)}, bf16[32,1536]{1,0:T(8,128)(2,1)S(1)}, u32[]{:S(2)}, u32[]{:S(2)}) collective-permute-start(bf16[32,1536]{1,0:T(8,128)(2,1)S(1)} %get-tuple-element.66), channel_id=1, source_target_pairs={{0,6},{2,4},{4,2},{6,0},{8,14},{10,12},{12,10},{14,8},{1,7},{3,5},... | collective-permute-start | bytes 294920 | tf_op jit(solution)/shard_map/ppermute | solution.py:376
  34.4 0.4 %collective-permute-start.13 = (bf16[32,1536]{1,0:T(8,128)(2,1)S(1)}, bf16[32,1536]{1,0:T(8,128)(2,1)S(1)}, u32[]{:S(2)}, u32[]{:S(2)}) collective-permute-start(bf16[32,1536]{1,0:T(8,128)(2,1)S(1)} %get-tuple-element.67), channel_id=1, source_target_pairs={{0,4},{2,6},{4,0},{6,2},{8,12},{10,14},{12,8},{14,10},{1,5},{3,7},... | collective-permute-start | bytes 294920 | tf_op jit(solution)/shard_map/ppermute | solution.py:376
  34.8 0.5 %collective-permute-done.10.refs_3_ = bf16[32,1536]{1,0:T(8,128)(2,1)S(1)} collective-permute-done((bf16[32,1536]{1,0:T(8,128)(2,1)S(1)}, bf16[32,1536]{1,0:T(8,128)(2,1)S(1)}, u32[]{:S(2)}, u32[]{:S(2)}) %collective-permute-start.10) | collective-permute-done | bytes 98336 | tf_op jit(solution)/shard_map/ppermute | solution.py:376
  35.4 1.2 %collective-permute-start.14 = (bf16[32,1536]{1,0:T(8,128)(2,1)S(1)}, bf16[32,1536]{1,0:T(8,128)(2,1)S(1)}, u32[]{:S(2)}, u32[]{:S(2)}) collective-permute-start(bf16[32,1536]{1,0:T(8,128)(2,1)S(1)} %get-tuple-element.68), channel_id=1, source_target_pairs={{0,2},{2,0},{4,6},{6,4},{8,10},{10,8},{12,14},{14,12},{1,3},{3,1},... | collective-permute-start | bytes 294920 | tf_op jit(solution)/shard_map/ppermute | solution.py:376
  36.5 0.0 copy-done.3
  36.5 0.6 %shard_map.96.w_ref = f32[256,1536]{1,0:T(8,128)S(1)} custom-call(bf16[128,1536]{1,0:T(8,128)(2,1)S(1)} %collective-permute-done.3.s_ref._, f32[256,1536]{1,0:T(8,128)S(1)} %get-tuple-element.47.y_ref.refs_4_, bf16[256,48]{1,0:T(8,128)(2,1)S(1)} %get-tuple-element.48.fade_ref, bf16[256,128]{1,0:T(8,128)(2,1)S(1)} %get-tuple-element.49.entry_ref), custom_call_target="tpu_custom_call" | custom-call | flops 1024 | bytes 1024 | tf_op jit(solution)/shard_map/pallas_call | solution.py:445
  37.1 0.0 collective-permute-done.8.refs_1_
  37.1 0.0 collective-permute-done.9.refs_2_
  37.2 0.9 %shard_map.101.refs_0_ = bf16[256,1536]{1,0:T(8,128)(2,1)} custom-call(f32[256,1536]{1,0:T(8,128)S(1)} %shard_map.96.w_ref, f32[256,1536]{1,0:T(8,128)S(1)} %get-tuple-element.50.g_ref, f32[1,1536]{1,0:T(1,128)S(1)} %reshape.27.gain_ref, bf16[32,1536]{1,0:T(8,128)(2,1)S(1)} %get-tuple-element.59.refs_0_, ...), custom_call_target="tpu_custom_call" | custom-call | flops 1024 | bytes 1024 | tf_op jit(solution)/shard_map/pallas_call | solution.py:472
  38.1 0.0 collective-permute-done.12.refs_2_
  38.1 0.9 %collective-permute-done.13.refs_3_ = bf16[32,1536]{1,0:T(8,128)(2,1)S(1)} collective-permute-done((bf16[32,1536]{1,0:T(8,128)(2,1)S(1)}, bf16[32,1536]{1,0:T(8,128)(2,1)S(1)}, u32[]{:S(2)}, u32[]{:S(2)}) %collective-permute-start.13) | collective-permute-done | bytes 98336 | tf_op jit(solution)/shard_map/ppermute | solution.py:376
  39.0 0.9 %collective-permute-done.14.refs_4_ = bf16[32,1536]{1,0:T(8,128)(2,1)S(1)} collective-permute-done((bf16[32,1536]{1,0:T(8,128)(2,1)S(1)}, bf16[32,1536]{1,0:T(8,128)(2,1)S(1)}, u32[]{:S(2)}, u32[]{:S(2)}) %collective-permute-start.14) | collective-permute-done | bytes 98336 | tf_op jit(solution)/shard_map/ppermute | solution.py:376
  40.0 0.9 %shard_map.103 = bf16[256,1536]{1,0:T(8,128)(2,1)} custom-call(f32[256,1536]{1,0:T(8,128)S(1)} %shard_map.96.w_ref, f32[256,1536]{1,0:T(8,128)S(1)} %get-tuple-element.50.g_ref, f32[1,1536]{1,0:T(1,128)S(1)} %reshape.27.gain_ref, bf16[256,1536]{1,0:T(8,128)(2,1)} %shard_map.101.refs_0_, ...), custom_call_target="tpu_custom_call", output_to_operand_aliasing={{}: (3, {})} | custom-call | flops 1024 | bytes 1024 | tf_op jit(solution)/shard_map/pallas_call | solution.py:472
  (1 shorter events, 0.0 us)
Async XLA Ops:
  0.0 16.6 %copy-start = (bf16[1,32,8,1536]{3,2,1,0:T(8,128)(2,1)S(1)}, bf16[1,32,8,1536]{3,2,1,0:T(8,128)(2,1)}, u32[]{:S(2)}) copy-start(bf16[1,32,8,1536]{3,2,1,0:T(8,128)(2,1)} %param.9) | copy-start | bytes 2359300
  1.5 18.1 %copy-start.1 = (bf16[1,32,8,1536]{3,2,1,0:T(8,128)(2,1)S(1)}, bf16[1,32,8,1536]{3,2,1,0:T(8,128)(2,1)}, u32[]{:S(2)}) copy-start(bf16[1,32,8,1536]{3,2,1,0:T(8,128)(2,1)} %param.10) | copy-start | bytes 2359300
  1.5 18.1 %copy-start.2 = (f32[24]{0:T(128)S(1)}, f32[24]{0:T(128)}, u32[]{:S(2)}) copy-start(f32[24]{0:T(128)} %param.16) | copy-start | bytes 292
  1.5 8.9 %collective-permute-start = (bf16[32,1664]{1,0:T(8,128)(2,1)S(1)}, bf16[32,1664]{1,0:T(8,128)(2,1)S(1)}, u32[]{:S(2)}, u32[]{:S(2)}) collective-permute-start(bf16[32,1664]{1,0:T(8,128)(2,1)S(1)} %get-tuple-element.44), channel_id=1, source_target_pairs={{0,2},{2,0},{4,6},{6,4},{8,10},{10,8},{12,14},{14,12},{1,3},{3,1},... | collective-permute-start | bytes 319496 | tf_op jit(solution)/shard_map/ppermute | solution.py:376
  4.5 5.9 %collective-permute-start.1 = (bf16[32,1664]{1,0:T(8,128)(2,1)S(1)}, bf16[32,1664]{1,0:T(8,128)(2,1)S(1)}, u32[]{:S(2)}, u32[]{:S(2)}) collective-permute-start(bf16[32,1664]{1,0:T(8,128)(2,1)S(1)} %get-tuple-element.45), channel_id=1, source_target_pairs={{0,4},{2,6},{4,0},{6,2},{8,12},{10,14},{12,8},{14,10},{1,5},{3,7},... | collective-permute-start | bytes 319496 | tf_op jit(solution)/shard_map/ppermute | solution.py:376
  6.1 6.3 %collective-permute-start.2 = (bf16[32,1664]{1,0:T(8,128)(2,1)S(1)}, bf16[32,1664]{1,0:T(8,128)(2,1)S(1)}, u32[]{:S(2)}, u32[]{:S(2)}) collective-permute-start(bf16[32,1664]{1,0:T(8,128)(2,1)S(1)} %get-tuple-element.46), channel_id=1, source_target_pairs={{0,6},{2,4},{4,2},{6,0},{8,14},{10,12},{12,10},{14,8},{1,7},{3,5},... | collective-permute-start | bytes 319496 | tf_op jit(solution)/shard_map/ppermute | solution.py:376
  6.1 15.7 %collective-permute-start.5 = (bf16[32,1664]{1,0:T(8,128)(2,1)S(1)}, bf16[32,1664]{1,0:T(8,128)(2,1)S(1)}, u32[]{:S(2)}, u32[]{:S(2)}) collective-permute-start(bf16[32,1664]{1,0:T(8,128)(2,1)S(1)} %get-tuple-element.52), channel_id=1, source_target_pairs={{0,2},{2,0},{4,6},{6,4},{8,10},{10,8},{12,14},{14,12},{1,3},{3,1},... | collective-permute-start | bytes 319496 | tf_op jit(solution)/shard_map/ppermute | solution.py:376
  8.0 13.8 %collective-permute-start.6 = (bf16[32,1664]{1,0:T(8,128)(2,1)S(1)}, bf16[32,1664]{1,0:T(8,128)(2,1)S(1)}, u32[]{:S(2)}, u32[]{:S(2)}) collective-permute-start(bf16[32,1664]{1,0:T(8,128)(2,1)S(1)} %get-tuple-element.53), channel_id=1, source_target_pairs={{0,4},{2,6},{4,0},{6,2},{8,12},{10,14},{12,8},{14,10},{1,5},{3,7},... | collective-permute-start | bytes 319496 | tf_op jit(solution)/shard_map/ppermute | solution.py:376
  10.4 11.4 %collective-permute-start.7 = (bf16[32,1664]{1,0:T(8,128)(2,1)S(1)}, bf16[32,1664]{1,0:T(8,128)(2,1)S(1)}, u32[]{:S(2)}, u32[]{:S(2)}) collective-permute-start(bf16[32,1664]{1,0:T(8,128)(2,1)S(1)} %get-tuple-element.54), channel_id=1, source_target_pairs={{0,6},{2,4},{4,2},{6,0},{8,14},{10,12},{12,10},{14,8},{1,7},{3,5},... | collective-permute-start | bytes 319496 | tf_op jit(solution)/shard_map/ppermute | solution.py:376
  13.6 14.1 %collective-permute-start.4 = (bf16[64,1536]{1,0:T(8,128)(2,1)S(1)}, bf16[64,1536]{1,0:T(8,128)(2,1)S(1)}, u32[]{:S(2)}, u32[]{:S(2)}) collective-permute-start(bf16[64,1536]{1,0:T(8,128)(2,1)S(1)} %shard_map.93._), channel_id=1, source_target_pairs={{0,8},{2,10},{4,12},{6,14},{8,0},{10,2},{12,4},{14,6},{1,9},{3,11}... | collective-permute-start | bytes 589832 | tf_op jit(solution)/shard_map/ppermute | solution.py:318
  18.1 13.6 %collective-permute-start.3 = (bf16[128,1536]{1,0:T(8,128)(2,1)S(1)}, bf16[128,1536]{1,0:T(8,128)(2,1)S(1)}, u32[]{:S(2)}, u32[]{:S(2)}) collective-permute-start(bf16[128,1536]{1,0:T(8,128)(2,1)S(1)} %shard_map.94._), channel_id=1, source_target_pairs={{0,16},{16,0},{1,17},{17,1},{2,18},{18,2},{3,19},{19,3},{4,20},{20... | collective-permute-start | bytes 1179656 | tf_op jit(solution)/shard_map/ppermute | solution.py:318
  24.2 7.5 %collective-permute-start.11 = (bf16[64,1536]{1,0:T(8,128)(2,1)S(1)}, bf16[64,1536]{1,0:T(8,128)(2,1)S(1)}, u32[]{:S(2)}, u32[]{:S(2)}) collective-permute-start(bf16[64,1536]{1,0:T(8,128)(2,1)S(1)} %shard_map.98.refs_4_), channel_id=1, source_target_pairs={{0,8},{2,10},{4,12},{6,14},{1,9},{3,11},{5,13},{7,15},{16,24},{18,... | collective-permute-start | bytes 589832 | tf_op jit(solution)/shard_map/ppermute | solution.py:318
  27.7 8.9 %copy-start.3 = (f32[1536]{0:T(1024)S(1)}, f32[1536]{0:T(1024)}, u32[]{:S(2)}) copy-start(f32[1536]{0:T(1024)} %param.17) | copy-start | bytes 18436
  28.0 7.3 %collective-permute-start.10 = (bf16[32,1536]{1,0:T(8,128)(2,1)S(1)}, bf16[32,1536]{1,0:T(8,128)(2,1)S(1)}, u32[]{:S(2)}, u32[]{:S(2)}) collective-permute-start(bf16[32,1536]{1,0:T(8,128)(2,1)S(1)} %get-tuple-element.62), channel_id=1, source_target_pairs={{0,2},{2,0},{4,6},{6,4},{8,10},{10,8},{12,14},{14,12},{1,3},{3,1},... | collective-permute-start | bytes 294920 | tf_op jit(solution)/shard_map/ppermute | solution.py:376
  29.4 7.7 %collective-permute-start.8 = (bf16[32,1536]{1,0:T(8,128)(2,1)S(1)}, bf16[32,1536]{1,0:T(8,128)(2,1)S(1)}, u32[]{:S(2)}, u32[]{:S(2)}) collective-permute-start(bf16[32,1536]{1,0:T(8,128)(2,1)S(1)} %get-tuple-element.60), channel_id=1, source_target_pairs={{0,6},{2,4},{4,2},{6,0},{8,14},{10,12},{12,10},{14,8},{1,7},{3,5},... | collective-permute-start | bytes 294920 | tf_op jit(solution)/shard_map/ppermute | solution.py:376
  31.0 6.1 %collective-permute-start.9 = (bf16[32,1536]{1,0:T(8,128)(2,1)S(1)}, bf16[32,1536]{1,0:T(8,128)(2,1)S(1)}, u32[]{:S(2)}, u32[]{:S(2)}) collective-permute-start(bf16[32,1536]{1,0:T(8,128)(2,1)S(1)} %get-tuple-element.61), channel_id=1, source_target_pairs={{0,4},{2,6},{4,0},{6,2},{8,12},{10,14},{12,8},{14,10},{1,5},{3,7},... | collective-permute-start | bytes 294920 | tf_op jit(solution)/shard_map/ppermute | solution.py:376
  32.0 6.1 %collective-permute-start.12 = (bf16[32,1536]{1,0:T(8,128)(2,1)S(1)}, bf16[32,1536]{1,0:T(8,128)(2,1)S(1)}, u32[]{:S(2)}, u32[]{:S(2)}) collective-permute-start(bf16[32,1536]{1,0:T(8,128)(2,1)S(1)} %get-tuple-element.66), channel_id=1, source_target_pairs={{0,6},{2,4},{4,2},{6,0},{8,14},{10,12},{12,10},{14,8},{1,7},{3,5},... | collective-permute-start | bytes 294920 | tf_op jit(solution)/shard_map/ppermute | solution.py:376
  34.4 4.6 %collective-permute-start.13 = (bf16[32,1536]{1,0:T(8,128)(2,1)S(1)}, bf16[32,1536]{1,0:T(8,128)(2,1)S(1)}, u32[]{:S(2)}, u32[]{:S(2)}) collective-permute-start(bf16[32,1536]{1,0:T(8,128)(2,1)S(1)} %get-tuple-element.67), channel_id=1, source_target_pairs={{0,4},{2,6},{4,0},{6,2},{8,12},{10,14},{12,8},{14,10},{1,5},{3,7},... | collective-permute-start | bytes 294920 | tf_op jit(solution)/shard_map/ppermute | solution.py:376
  35.4 4.6 %collective-permute-start.14 = (bf16[32,1536]{1,0:T(8,128)(2,1)S(1)}, bf16[32,1536]{1,0:T(8,128)(2,1)S(1)}, u32[]{:S(2)}, u32[]{:S(2)}) collective-permute-start(bf16[32,1536]{1,0:T(8,128)(2,1)S(1)} %get-tuple-element.68), channel_id=1, source_target_pairs={{0,2},{2,0},{4,6},{6,4},{8,10},{10,8},{12,14},{14,12},{1,3},{3,1},... | collective-permute-start | bytes 294920 | tf_op jit(solution)/shard_map/ppermute | solution.py:376

commit v20 on v19

--- a/solution.py
+++ b/solution.py
@@ -426,6 +426,10 @@
     )(params, x, raw, maps, before)
     col_entering = entering_states(col_made[0], col_made[1:], "row", row_count, 1, width)
     before = col_made[0]
+    known[0], before = own_rows(0, before)
+    for i in range(1, len(pieces)):
+        known[i], before = own_rows(i, before)
+        entering[i], before = row_states(i, before)
     y_col, silu, *col_known = call(
         functools.partial(col_local_kernel, **sizes),
         [
@@ -437,11 +441,6 @@
         2,
         specs=[None] * 6 + [any_spec],
     )(params, x, raw, maps, gate, skip.reshape(1, heads), before)
-    before = y_col
-    for i in range(1, len(pieces)):
-        known[i], before = own_rows(i, before)
-        entering[i], before = row_states(i, before)
-    known[0], before = own_rows(0, before)
     w = call(
         functools.partial(col_out_kernel, heads=heads, width=width),
         pltpu.VMEM((tokens, channels), F32),
@@ -454,6 +453,7 @@
             parts_of.append((first, rows, known[i][j], entering[i][j]))
 
     back = []
+    before = y_col
     for _, rows, known, entering in parts_of:
         y_row = call(
             functools.partial(row_out_kernel, heads=heads, width=width),

time: 41.1 us -> 41.1 us (level)
  transfers between devices with their start and end apart: 15 -> 15, of which waited for: 5 -> 4; matrix products, arithmetic and copies ran while one was open for 0% -> 0% of each run, Pallas kernels for 26% -> 26%
where the time goes in v20:
time: 41.1 us; the launch traced here: 41 us
  starting transfers between devices  22.5 us (55%)
  Pallas kernels  13.1 us (32%)
  waiting for transfers between devices  4.47 us (11%)
  between operations  0.87 us (2%)
    ppermute x12, starting transfers between devices, exchange(): lax.ppermute(blocks[i], 'col', [(at, partner(at, i, group)) for at in ran...  15.6 us
    ppermute x3, starting transfers between devices, entering_states(): entering = lax.ppermute(ends, axis, onward)  6.84 us
    ppermute x12, waiting for transfers between devices, exchange(): lax.ppermute(blocks[i], 'col', [(at, partner(at, i, group)) for at in ran...  4.46 us
    pallas_call x2, Pallas kernels, own_rows(): call(functools.partial(row_local_kernel, offset=sum(pieces[i][:j]), **siz...  2.43 us
    pallas_call x2, Pallas kernels, row_states(): call(functools.partial(row_state_kernel, count=len(places), **sizes, **sh...  2.23 us
    pallas_call x1, Pallas kernels, body(): call(functools.partial(col_local_kernel, **sizes), [pltpu.VMEM((tokens, c...  2.16 us
    pallas_call x2, Pallas kernels, body(): call(functools.partial(final_kernel, which=which, offset=first, share=sha...  1.9 us
    pallas_call x1, Pallas kernels, body(): call(functools.partial(col_state_kernel, **sizes), state_shapes([cols * s...  1.48 us
  transfers between devices with their start and end apart: 15, of which 4 were waited for; matrix products, arithmetic and copies ran while one was open for 0% of the time, Pallas kernels for 26%

profile of v20, /device:TPU:0, one launch (start us, length us, event | category | flops | bytes accessed | tf_op | source)
XLA Modules:
  0.0 41.0 jit_solution(6554184478170085999)
XLA Ops:
  0.0 0.0 copy-start
  0.0 1.5 %shard_map.91 = (bf16[256,48]{1,0:T(8,128)(2,1)S(1)}, bf16[256,64]{1,0:T(8,128)(2,1)S(1)}, f32[48,1000]{1,0:T(8,128)S(1)}, f32[2,24]{1,0:T(2,128)S(1)}, bf16[32,...) custom-call(bf16[256,1536]{1,0:T(8,128)(2,1)} %bitcast.7, ...), custom_call_target="tpu_custom_call" | custom-call | flops 1000001024 | bytes 1024 | tf_op jit(solution)/shard_map/pallas_call | solution.py:348
  1.5 3.0 %collective-permute-start = (bf16[32,1664]{1,0:T(8,128)(2,1)S(1)}, bf16[32,1664]{1,0:T(8,128)(2,1)S(1)}, u32[]{:S(2)}, u32[]{:S(2)}) collective-permute-start(bf16[32,1664]{1,0:T(8,128)(2,1)S(1)} %get-tuple-element.44), channel_id=1, source_target_pairs={{0,2},{2,0},{4,6},{6,4},{8,10},{10,8},{12,14},{14,12},{1,3},{3,1},... | collective-permute-start | bytes 319496 | tf_op jit(solution)/shard_map/ppermute | solution.py:376
  4.5 1.6 %collective-permute-start.1 = (bf16[32,1664]{1,0:T(8,128)(2,1)S(1)}, bf16[32,1664]{1,0:T(8,128)(2,1)S(1)}, u32[]{:S(2)}, u32[]{:S(2)}) collective-permute-start(bf16[32,1664]{1,0:T(8,128)(2,1)S(1)} %get-tuple-element.45), channel_id=1, source_target_pairs={{0,4},{2,6},{4,0},{6,2},{8,12},{10,14},{12,8},{14,10},{1,5},{3,7},... | collective-permute-start | bytes 319496 | tf_op jit(solution)/shard_map/ppermute | solution.py:376
  6.1 0.0 collective-permute-start.2
  6.1 1.9 %collective-permute-start.4 = (bf16[32,1664]{1,0:T(8,128)(2,1)S(1)}, bf16[32,1664]{1,0:T(8,128)(2,1)S(1)}, u32[]{:S(2)}, u32[]{:S(2)}) collective-permute-start(bf16[32,1664]{1,0:T(8,128)(2,1)S(1)} %get-tuple-element.48), channel_id=1, source_target_pairs={{0,2},{2,0},{4,6},{6,4},{8,10},{10,8},{12,14},{14,12},{1,3},{3,1},... | collective-permute-start | bytes 319496 | tf_op jit(solution)/shard_map/ppermute | solution.py:376
  8.0 1.6 %collective-permute-start.5 = (bf16[32,1664]{1,0:T(8,128)(2,1)S(1)}, bf16[32,1664]{1,0:T(8,128)(2,1)S(1)}, u32[]{:S(2)}, u32[]{:S(2)}) collective-permute-start(bf16[32,1664]{1,0:T(8,128)(2,1)S(1)} %get-tuple-element.49), channel_id=1, source_target_pairs={{0,4},{2,6},{4,0},{6,2},{8,12},{10,14},{12,8},{14,10},{1,5},{3,7},... | collective-permute-start | bytes 319496 | tf_op jit(solution)/shard_map/ppermute | solution.py:376
  10.2 0.2 shard_map.92.params_ref.refs_4_
  10.4 0.0 collective-permute-done.refs_1_
  10.4 0.0 collective-permute-start.6
  10.4 0.0 collective-permute-done.1.refs_2_
  10.5 2.0 %collective-permute-done.2.refs_3_ = bf16[32,1664]{1,0:T(8,128)(2,1)S(1)} collective-permute-done((bf16[32,1664]{1,0:T(8,128)(2,1)S(1)}, bf16[32,1664]{1,0:T(8,128)(2,1)S(1)}, u32[]{:S(2)}, u32[]{:S(2)}) %collective-permute-start.2) | collective-permute-done | bytes 106528 | tf_op jit(solution)/shard_map/ppermute | solution.py:376
  12.4 1.1 %shard_map.93._ = bf16[64,1536]{1,0:T(8,128)(2,1)S(1)} custom-call(f32[8,48]{1,0:T(8,128)S(1)} %shard_map.92.params_ref.refs_4_, bf16[32,1664]{1,0:T(8,128)(2,1)S(1)} %get-tuple-element.43.refs_0_, bf16[32,1664]{1,0:T(8,128)(2,1)S(1)} %collective-permute-done.refs_1_, bf16[32,1664]{1,0:T(8,128)(2,1)S(1)} %collective-permute-done.1.refs_2_, ...), custom_call_target="tpu_custom_call" | custom-call | flops 1024 | bytes 1024 | tf_op jit(solution)/shard_map/pallas_call | solution.py:406
  13.6 3.0 %collective-permute-start.7 = (bf16[64,1536]{1,0:T(8,128)(2,1)S(1)}, bf16[64,1536]{1,0:T(8,128)(2,1)S(1)}, u32[]{:S(2)}, u32[]{:S(2)}) collective-permute-start(bf16[64,1536]{1,0:T(8,128)(2,1)S(1)} %shard_map.93._), channel_id=1, source_target_pairs={{0,8},{2,10},{4,12},{6,14},{8,0},{10,2},{12,4},{14,6},{1,9},{3,11}... | collective-permute-start | bytes 589832 | tf_op jit(solution)/shard_map/ppermute | solution.py:318
  16.6 0.0 copy-done
  16.6 1.5 %shard_map.94.refs_4_ = bf16[128,1536]{1,0:T(8,128)(2,1)S(1)} custom-call(f32[8,48]{1,0:T(8,128)S(1)} %shard_map.92.params_ref.refs_4_, bf16[256,1536]{1,0:T(8,128)(2,1)S(1)} %bitcast.8, bf16[256,48]{1,0:T(8,128)(2,1)S(1)} %get-tuple-element.41.raw_ref, bf16[256,64]{1,0:T(8,128)(2,1)S(1)} %get-tuple-element.42.maps_ref, bf16[64,1536]{1,0:T(8,128)(2,1)S(1)} %shard_map.93._), custom_call_target="tpu_custom_call" | custom-call | flops 1024 | bytes 1024 | tf_op jit(solution)/shard_map/pallas_call | solution.py:421
  18.1 1.5 %collective-permute-start.3 = (bf16[128,1536]{1,0:T(8,128)(2,1)S(1)}, bf16[128,1536]{1,0:T(8,128)(2,1)S(1)}, u32[]{:S(2)}, u32[]{:S(2)}) collective-permute-start(bf16[128,1536]{1,0:T(8,128)(2,1)S(1)} %shard_map.94.refs_4_), channel_id=1, source_target_pairs={{0,16},{16,0},{1,17},{17,1},{2,18},{18,2},{3,19},{19,3},{4,20},{20... | collective-permute-start | bytes 1179656 | tf_op jit(solution)/shard_map/ppermute | solution.py:318
  19.6 1.2 %shard_map.95 = (f32[128,1536]{1,0:T(8,128)S(1)}, bf16[128,48]{1,0:T(8,128)(2,1)S(1)}, bf16[128,64]{1,0:T(8,128)(2,1)S(1)}) custom-call(f32[8,48]{1,0:T(8,128)S(1)} %shard_map.92.params_ref.refs_4_, bf16[32,1664]{1,0:T(8,128)(2,1)S(1)} %get-tuple-element.43.refs_0_, bf16[32,1664]{1,0:T(8,128)(2,1)S(1)} %collective-permute-done.refs_1_, ...), custom_call_target="tpu_custom_call" | custom-call | flops 2000001024 | bytes 1024 | tf_op jit(solution)/shard_map/pallas_call | solution.py:390
  20.8 0.0 collective-permute-done.4.refs_1_
  20.8 0.0 collective-permute-done.5.refs_2_
  20.8 0.0 collective-permute-done.6.refs_3_
  20.8 0.0 copy-start.1
  20.8 0.0 copy-start.2
  20.9 1.2 %shard_map.96 = (f32[128,1536]{1,0:T(8,128)S(1)}, bf16[128,48]{1,0:T(8,128)(2,1)S(1)}, bf16[128,64]{1,0:T(8,128)(2,1)S(1)}) custom-call(f32[8,48]{1,0:T(8,128)S(1)} %shard_map.92.params_ref.refs_4_, bf16[32,1664]{1,0:T(8,128)(2,1)S(1)} %get-tuple-element.47.refs_0_, bf16[32,1664]{1,0:T(8,128)(2,1)S(1)} %collective-permute-done.4.refs_1_, ...), custom_call_target="tpu_custom_call" | custom-call | flops 2000001024 | bytes 1024 | tf_op jit(solution)/shard_map/pallas_call | solution.py:390
  22.1 1.1 %shard_map.97._ = bf16[64,1536]{1,0:T(8,128)(2,1)S(1)} custom-call(f32[8,48]{1,0:T(8,128)S(1)} %shard_map.92.params_ref.refs_4_, bf16[32,1664]{1,0:T(8,128)(2,1)S(1)} %get-tuple-element.47.refs_0_, bf16[32,1664]{1,0:T(8,128)(2,1)S(1)} %collective-permute-done.4.refs_1_, bf16[32,1664]{1,0:T(8,128)(2,1)S(1)} %collective-permute-done.5.refs_2_, ...), custom_call_target="tpu_custom_call" | custom-call | flops 1024 | bytes 1024 | tf_op jit(solution)/shard_map/pallas_call | solution.py:406
  23.2 2.3 %collective-permute-start.11 = (bf16[64,1536]{1,0:T(8,128)(2,1)S(1)}, bf16[64,1536]{1,0:T(8,128)(2,1)S(1)}, u32[]{:S(2)}, u32[]{:S(2)}) collective-permute-start(bf16[64,1536]{1,0:T(8,128)(2,1)S(1)} %shard_map.97._), channel_id=1, source_target_pairs={{0,8},{2,10},{4,12},{6,14},{1,9},{3,11},{5,13},{7,15},{16,24},{18,... | collective-permute-start | bytes 589832 | tf_op jit(solution)/shard_map/ppermute | solution.py:318
  25.5 0.0 copy-done.1
  25.5 0.0 copy-done.2
  25.5 2.2 %shard_map.98 = (f32[256,1536]{1,0:T(8,128)S(1)}, f32[256,1536]{1,0:T(8,128)S(1)}, bf16[256,48]{1,0:T(8,128)(2,1)S(1)}, bf16[256,128]{1,0:T(8,128)(2,1)S(1)}) custom-call(f32[8,48]{1,0:T(8,128)S(1)} %shard_map.92.params_ref.refs_4_, bf16[256,1536]{1,0:T(8,128)(2,1)S(1)} %bitcast.9, bf16[256,48]{1,0:T(8,128)(2,1)S(1)} %get-tuple-element.41.raw_ref, ...), custom_call_target="tpu_custom_call" | custom-call | flops 2000001024 | bytes 1024 | tf_op jit(solution)/shard_map/pallas_call | solution.py:433
  27.7 0.0 collective-permute-done.7.s_ref
  27.7 0.0 copy-start.3
  27.7 0.3 shard_map.100
  28.1 1.4 %collective-permute-start.10 = (bf16[32,1536]{1,0:T(8,128)(2,1)S(1)}, bf16[32,1536]{1,0:T(8,128)(2,1)S(1)}, u32[]{:S(2)}, u32[]{:S(2)}) collective-permute-start(bf16[32,1536]{1,0:T(8,128)(2,1)S(1)} %get-tuple-element.62), channel_id=1, source_target_pairs={{0,2},{2,0},{4,6},{6,4},{8,10},{10,8},{12,14},{14,12},{1,3},{3,1},... | collective-permute-start | bytes 294920 | tf_op jit(solution)/shard_map/ppermute | solution.py:376
  29.5 1.5 %collective-permute-start.8 = (bf16[32,1536]{1,0:T(8,128)(2,1)S(1)}, bf16[32,1536]{1,0:T(8,128)(2,1)S(1)}, u32[]{:S(2)}, u32[]{:S(2)}) collective-permute-start(bf16[32,1536]{1,0:T(8,128)(2,1)S(1)} %get-tuple-element.60), channel_id=1, source_target_pairs={{0,6},{2,4},{4,2},{6,0},{8,14},{10,12},{12,10},{14,8},{1,7},{3,5},... | collective-permute-start | bytes 294920 | tf_op jit(solution)/shard_map/ppermute | solution.py:376
  31.0 0.6 %collective-permute-start.9 = (bf16[32,1536]{1,0:T(8,128)(2,1)S(1)}, bf16[32,1536]{1,0:T(8,128)(2,1)S(1)}, u32[]{:S(2)}, u32[]{:S(2)}) collective-permute-start(bf16[32,1536]{1,0:T(8,128)(2,1)S(1)} %get-tuple-element.61), channel_id=1, source_target_pairs={{0,4},{2,6},{4,0},{6,2},{8,12},{10,14},{12,8},{14,10},{1,5},{3,7},... | collective-permute-start | bytes 294920 | tf_op jit(solution)/shard_map/ppermute | solution.py:376
  31.6 0.0 collective-permute-done.11.s_ref
  31.6 0.0 collective-permute-done.3.s_ref._
  31.6 0.3 shard_map.102
  32.0 2.4 %collective-permute-start.12 = (bf16[32,1536]{1,0:T(8,128)(2,1)S(1)}, bf16[32,1536]{1,0:T(8,128)(2,1)S(1)}, u32[]{:S(2)}, u32[]{:S(2)}) collective-permute-start(bf16[32,1536]{1,0:T(8,128)(2,1)S(1)} %get-tuple-element.66), channel_id=1, source_target_pairs={{0,6},{2,4},{4,2},{6,0},{8,14},{10,12},{12,10},{14,8},{1,7},{3,5},... | collective-permute-start | bytes 294920 | tf_op jit(solution)/shard_map/ppermute | solution.py:376
  34.4 0.4 %collective-permute-start.13 = (bf16[32,1536]{1,0:T(8,128)(2,1)S(1)}, bf16[32,1536]{1,0:T(8,128)(2,1)S(1)}, u32[]{:S(2)}, u32[]{:S(2)}) collective-permute-start(bf16[32,1536]{1,0:T(8,128)(2,1)S(1)} %get-tuple-element.67), channel_id=1, source_target_pairs={{0,4},{2,6},{4,0},{6,2},{8,12},{10,14},{12,8},{14,10},{1,5},{3,7},... | collective-permute-start | bytes 294920 | tf_op jit(solution)/shard_map/ppermute | solution.py:376
  34.9 0.6 %collective-permute-done.10.refs_3_ = bf16[32,1536]{1,0:T(8,128)(2,1)S(1)} collective-permute-done((bf16[32,1536]{1,0:T(8,128)(2,1)S(1)}, bf16[32,1536]{1,0:T(8,128)(2,1)S(1)}, u32[]{:S(2)}, u32[]{:S(2)}) %collective-permute-start.10) | collective-permute-done | bytes 98336 | tf_op jit(solution)/shard_map/ppermute | solution.py:376
  35.4 1.1 %collective-permute-start.14 = (bf16[32,1536]{1,0:T(8,128)(2,1)S(1)}, bf16[32,1536]{1,0:T(8,128)(2,1)S(1)}, u32[]{:S(2)}, u32[]{:S(2)}) collective-permute-start(bf16[32,1536]{1,0:T(8,128)(2,1)S(1)} %get-tuple-element.68), channel_id=1, source_target_pairs={{0,2},{2,0},{4,6},{6,4},{8,10},{10,8},{12,14},{14,12},{1,3},{3,1},... | collective-permute-start | bytes 294920 | tf_op jit(solution)/shard_map/ppermute | solution.py:376
  36.5 0.0 copy-done.3
  36.5 0.6 %shard_map.99.w_ref = f32[256,1536]{1,0:T(8,128)S(1)} custom-call(bf16[128,1536]{1,0:T(8,128)(2,1)S(1)} %collective-permute-done.3.s_ref._, f32[256,1536]{1,0:T(8,128)S(1)} %get-tuple-element.53.y_ref._, bf16[256,48]{1,0:T(8,128)(2,1)S(1)} %get-tuple-element.54.fade_ref, bf16[256,128]{1,0:T(8,128)(2,1)S(1)} %get-tuple-element.55.entry_ref), custom_call_target="tpu_custom_call" | custom-call | flops 1024 | bytes 1024 | tf_op jit(solution)/shard_map/pallas_call | solution.py:444
  37.1 0.0 collective-permute-done.8.refs_1_
  37.1 0.0 collective-permute-done.9.refs_2_
  37.2 0.9 %shard_map.101.refs_0_ = bf16[256,1536]{1,0:T(8,128)(2,1)} custom-call(f32[256,1536]{1,0:T(8,128)S(1)} %shard_map.99.w_ref, f32[256,1536]{1,0:T(8,128)S(1)} %get-tuple-element.56.g_ref, f32[1,1536]{1,0:T(1,128)S(1)} %reshape.27.gain_ref, bf16[32,1536]{1,0:T(8,128)(2,1)S(1)} %get-tuple-element.59.refs_0_, ...), custom_call_target="tpu_custom_call" | custom-call | flops 1024 | bytes 1024 | tf_op jit(solution)/shard_map/pallas_call | solution.py:472
  38.1 0.0 collective-permute-done.12.refs_2_
  38.1 0.9 %collective-permute-done.13.refs_3_ = bf16[32,1536]{1,0:T(8,128)(2,1)S(1)} collective-permute-done((bf16[32,1536]{1,0:T(8,128)(2,1)S(1)}, bf16[32,1536]{1,0:T(8,128)(2,1)S(1)}, u32[]{:S(2)}, u32[]{:S(2)}) %collective-permute-start.13) | collective-permute-done | bytes 98336 | tf_op jit(solution)/shard_map/ppermute | solution.py:376
  39.0 1.0 %collective-permute-done.14.refs_4_ = bf16[32,1536]{1,0:T(8,128)(2,1)S(1)} collective-permute-done((bf16[32,1536]{1,0:T(8,128)(2,1)S(1)}, bf16[32,1536]{1,0:T(8,128)(2,1)S(1)}, u32[]{:S(2)}, u32[]{:S(2)}) %collective-permute-start.14) | collective-permute-done | bytes 98336 | tf_op jit(solution)/shard_map/ppermute | solution.py:376
  40.0 0.9 %shard_map.103 = bf16[256,1536]{1,0:T(8,128)(2,1)} custom-call(f32[256,1536]{1,0:T(8,128)S(1)} %shard_map.99.w_ref, f32[256,1536]{1,0:T(8,128)S(1)} %get-tuple-element.56.g_ref, f32[1,1536]{1,0:T(1,128)S(1)} %reshape.27.gain_ref, bf16[256,1536]{1,0:T(8,128)(2,1)} %shard_map.101.refs_0_, ...), custom_call_target="tpu_custom_call", output_to_operand_aliasing={{}: (3, {})} | custom-call | flops 1024 | bytes 1024 | tf_op jit(solution)/shard_map/pallas_call | solution.py:472
  (1 shorter events, 0.0 us)
Async XLA Ops:
  0.0 16.6 %copy-start = (bf16[1,32,8,1536]{3,2,1,0:T(8,128)(2,1)S(1)}, bf16[1,32,8,1536]{3,2,1,0:T(8,128)(2,1)}, u32[]{:S(2)}) copy-start(bf16[1,32,8,1536]{3,2,1,0:T(8,128)(2,1)} %param.9) | copy-start | bytes 2359300
  1.5 8.9 %collective-permute-start = (bf16[32,1664]{1,0:T(8,128)(2,1)S(1)}, bf16[32,1664]{1,0:T(8,128)(2,1)S(1)}, u32[]{:S(2)}, u32[]{:S(2)}) collective-permute-start(bf16[32,1664]{1,0:T(8,128)(2,1)S(1)} %get-tuple-element.44), channel_id=1, source_target_pairs={{0,2},{2,0},{4,6},{6,4},{8,10},{10,8},{12,14},{14,12},{1,3},{3,1},... | collective-permute-start | bytes 319496 | tf_op jit(solution)/shard_map/ppermute | solution.py:376
  4.5 5.9 %collective-permute-start.1 = (bf16[32,1664]{1,0:T(8,128)(2,1)S(1)}, bf16[32,1664]{1,0:T(8,128)(2,1)S(1)}, u32[]{:S(2)}, u32[]{:S(2)}) collective-permute-start(bf16[32,1664]{1,0:T(8,128)(2,1)S(1)} %get-tuple-element.45), channel_id=1, source_target_pairs={{0,4},{2,6},{4,0},{6,2},{8,12},{10,14},{12,8},{14,10},{1,5},{3,7},... | collective-permute-start | bytes 319496 | tf_op jit(solution)/shard_map/ppermute | solution.py:376
  6.1 6.3 %collective-permute-start.2 = (bf16[32,1664]{1,0:T(8,128)(2,1)S(1)}, bf16[32,1664]{1,0:T(8,128)(2,1)S(1)}, u32[]{:S(2)}, u32[]{:S(2)}) collective-permute-start(bf16[32,1664]{1,0:T(8,128)(2,1)S(1)} %get-tuple-element.46), channel_id=1, source_target_pairs={{0,6},{2,4},{4,2},{6,0},{8,14},{10,12},{12,10},{14,8},{1,7},{3,5},... | collective-permute-start | bytes 319496 | tf_op jit(solution)/shard_map/ppermute | solution.py:376
  6.1 14.7 %collective-permute-start.4 = (bf16[32,1664]{1,0:T(8,128)(2,1)S(1)}, bf16[32,1664]{1,0:T(8,128)(2,1)S(1)}, u32[]{:S(2)}, u32[]{:S(2)}) collective-permute-start(bf16[32,1664]{1,0:T(8,128)(2,1)S(1)} %get-tuple-element.48), channel_id=1, source_target_pairs={{0,2},{2,0},{4,6},{6,4},{8,10},{10,8},{12,14},{14,12},{1,3},{3,1},... | collective-permute-start | bytes 319496 | tf_op jit(solution)/shard_map/ppermute | solution.py:376
  8.0 12.8 %collective-permute-start.5 = (bf16[32,1664]{1,0:T(8,128)(2,1)S(1)}, bf16[32,1664]{1,0:T(8,128)(2,1)S(1)}, u32[]{:S(2)}, u32[]{:S(2)}) collective-permute-start(bf16[32,1664]{1,0:T(8,128)(2,1)S(1)} %get-tuple-element.49), channel_id=1, source_target_pairs={{0,4},{2,6},{4,0},{6,2},{8,12},{10,14},{12,8},{14,10},{1,5},{3,7},... | collective-permute-start | bytes 319496 | tf_op jit(solution)/shard_map/ppermute | solution.py:376
  10.4 10.4 %collective-permute-start.6 = (bf16[32,1664]{1,0:T(8,128)(2,1)S(1)}, bf16[32,1664]{1,0:T(8,128)(2,1)S(1)}, u32[]{:S(2)}, u32[]{:S(2)}) collective-permute-start(bf16[32,1664]{1,0:T(8,128)(2,1)S(1)} %get-tuple-element.50), channel_id=1, source_target_pairs={{0,6},{2,4},{4,2},{6,0},{8,14},{10,12},{12,10},{14,8},{1,7},{3,5},... | collective-permute-start | bytes 319496 | tf_op jit(solution)/shard_map/ppermute | solution.py:376
  13.6 14.2 %collective-permute-start.7 = (bf16[64,1536]{1,0:T(8,128)(2,1)S(1)}, bf16[64,1536]{1,0:T(8,128)(2,1)S(1)}, u32[]{:S(2)}, u32[]{:S(2)}) collective-permute-start(bf16[64,1536]{1,0:T(8,128)(2,1)S(1)} %shard_map.93._), channel_id=1, source_target_pairs={{0,8},{2,10},{4,12},{6,14},{8,0},{10,2},{12,4},{14,6},{1,9},{3,11}... | collective-permute-start | bytes 589832 | tf_op jit(solution)/shard_map/ppermute | solution.py:318
  18.1 13.6 %collective-permute-start.3 = (bf16[128,1536]{1,0:T(8,128)(2,1)S(1)}, bf16[128,1536]{1,0:T(8,128)(2,1)S(1)}, u32[]{:S(2)}, u32[]{:S(2)}) collective-permute-start(bf16[128,1536]{1,0:T(8,128)(2,1)S(1)} %shard_map.94.refs_4_), channel_id=1, source_target_pairs={{0,16},{16,0},{1,17},{17,1},{2,18},{18,2},{3,19},{19,3},{4,20},{20... | collective-permute-start | bytes 1179656 | tf_op jit(solution)/shard_map/ppermute | solution.py:318
  20.8 4.7 %copy-start.1 = (bf16[1,32,8,1536]{3,2,1,0:T(8,128)(2,1)S(1)}, bf16[1,32,8,1536]{3,2,1,0:T(8,128)(2,1)}, u32[]{:S(2)}) copy-start(bf16[1,32,8,1536]{3,2,1,0:T(8,128)(2,1)} %param.10) | copy-start | bytes 2359300
  20.8 4.7 %copy-start.2 = (f32[24]{0:T(128)S(1)}, f32[24]{0:T(128)}, u32[]{:S(2)}) copy-start(f32[24]{0:T(128)} %param.16) | copy-start | bytes 292
  23.2 8.4 %collective-permute-start.11 = (bf16[64,1536]{1,0:T(8,128)(2,1)S(1)}, bf16[64,1536]{1,0:T(8,128)(2,1)S(1)}, u32[]{:S(2)}, u32[]{:S(2)}) collective-permute-start(bf16[64,1536]{1,0:T(8,128)(2,1)S(1)} %shard_map.97._), channel_id=1, source_target_pairs={{0,8},{2,10},{4,12},{6,14},{1,9},{3,11},{5,13},{7,15},{16,24},{18,... | collective-permute-start | bytes 589832 | tf_op jit(solution)/shard_map/ppermute | solution.py:318
  27.7 8.8 %copy-start.3 = (f32[1536]{0:T(1024)S(1)}, f32[1536]{0:T(1024)}, u32[]{:S(2)}) copy-start(f32[1536]{0:T(1024)} %param.17) | copy-start | bytes 18436
  28.1 7.3 %collective-permute-start.10 = (bf16[32,1536]{1,0:T(8,128)(2,1)S(1)}, bf16[32,1536]{1,0:T(8,128)(2,1)S(1)}, u32[]{:S(2)}, u32[]{:S(2)}) collective-permute-start(bf16[32,1536]{1,0:T(8,128)(2,1)S(1)} %get-tuple-element.62), channel_id=1, source_target_pairs={{0,2},{2,0},{4,6},{6,4},{8,10},{10,8},{12,14},{14,12},{1,3},{3,1},... | collective-permute-start | bytes 294920 | tf_op jit(solution)/shard_map/ppermute | solution.py:376
  29.5 7.7 %collective-permute-start.8 = (bf16[32,1536]{1,0:T(8,128)(2,1)S(1)}, bf16[32,1536]{1,0:T(8,128)(2,1)S(1)}, u32[]{:S(2)}, u32[]{:S(2)}) collective-permute-start(bf16[32,1536]{1,0:T(8,128)(2,1)S(1)} %get-tuple-element.60), channel_id=1, source_target_pairs={{0,6},{2,4},{4,2},{6,0},{8,14},{10,12},{12,10},{14,8},{1,7},{3,5},... | collective-permute-start | bytes 294920 | tf_op jit(solution)/shard_map/ppermute | solution.py:376
  31.0 6.1 %collective-permute-start.9 = (bf16[32,1536]{1,0:T(8,128)(2,1)S(1)}, bf16[32,1536]{1,0:T(8,128)(2,1)S(1)}, u32[]{:S(2)}, u32[]{:S(2)}) collective-permute-start(bf16[32,1536]{1,0:T(8,128)(2,1)S(1)} %get-tuple-element.61), channel_id=1, source_target_pairs={{0,4},{2,6},{4,0},{6,2},{8,12},{10,14},{12,8},{14,10},{1,5},{3,7},... | collective-permute-start | bytes 294920 | tf_op jit(solution)/shard_map/ppermute | solution.py:376
  32.0 6.1 %collective-permute-start.12 = (bf16[32,1536]{1,0:T(8,128)(2,1)S(1)}, bf16[32,1536]{1,0:T(8,128)(2,1)S(1)}, u32[]{:S(2)}, u32[]{:S(2)}) collective-permute-start(bf16[32,1536]{1,0:T(8,128)(2,1)S(1)} %get-tuple-element.66), channel_id=1, source_target_pairs={{0,6},{2,4},{4,2},{6,0},{8,14},{10,12},{12,10},{14,8},{1,7},{3,5},... | collective-permute-start | bytes 294920 | tf_op jit(solution)/shard_map/ppermute | solution.py:376
  34.4 4.6 %collective-permute-start.13 = (bf16[32,1536]{1,0:T(8,128)(2,1)S(1)}, bf16[32,1536]{1,0:T(8,128)(2,1)S(1)}, u32[]{:S(2)}, u32[]{:S(2)}) collective-permute-start(bf16[32,1536]{1,0:T(8,128)(2,1)S(1)} %get-tuple-element.67), channel_id=1, source_target_pairs={{0,4},{2,6},{4,0},{6,2},{8,12},{10,14},{12,8},{14,10},{1,5},{3,7},... | collective-permute-start | bytes 294920 | tf_op jit(solution)/shard_map/ppermute | solution.py:376
  35.4 4.6 %collective-permute-start.14 = (bf16[32,1536]{1,0:T(8,128)(2,1)S(1)}, bf16[32,1536]{1,0:T(8,128)(2,1)S(1)}, u32[]{:S(2)}, u32[]{:S(2)}) collective-permute-start(bf16[32,1536]{1,0:T(8,128)(2,1)S(1)} %get-tuple-element.68), channel_id=1, source_target_pairs={{0,2},{2,0},{4,6},{6,4},{8,10},{10,8},{12,14},{14,12},{1,3},{3,1},... | collective-permute-start | bytes 294920 | tf_op jit(solution)/shard_map/ppermute | solution.py:376

commit v21 on v20

--- a/solution.py
+++ b/solution.py
@@ -242,7 +242,25 @@
         y_ref[:, part] = dot(mix, values) * dot(scan.fade, pick)
 
 
-def row_out_kernel(s_ref, y_ref, fade_ref, entry_ref, _, *outs, heads, width):
+def row_both_kernel(params_ref, *refs, group, axis, cols, heads, state, width):
+    blocks, (s_ref, y_ref, fade_ref, entry_ref) = refs[:group], refs[group + 1 :]
+    member = mod(lax.axis_index(axis), group)
+    scan = row_scan(params_ref, [block[...] for block in blocks], member, cols, heads, state)
+    into = scan.into()
+    ends = parts(scan.ends(), 2)
+    mix = scan.within()
+    fade_ref[...] = scan.fade
+    entry_ref[...] = scan.entry(lax.axis_index(axis) >= group)
+    for first, count in strips(y_ref.shape[1]):
+        pick = picks(heads, width, first, count)
+        part = slice(first, first + count)
+        x = jnp.concatenate([block[:, part] for block in blocks], axis=0).astype(F32)
+        values = (x * dot(scan.grow, pick)).astype(BF16)
+        s_ref[:, part] = (dot(into, values) * dot(ends, pick)).astype(BF16)
+        y_ref[:, part] = dot(mix, values) * dot(scan.fade, pick)
+
+
+def row_out_kernel(s_ref, y_ref, fade_ref, entry_ref, _, __, *outs, heads, width):
     rows = outs[0].shape[0]
     for first, count in strips(s_ref.shape[1]):
         pick = picks(heads, width, first, count)
@@ -428,24 +446,25 @@
     before = col_made[0]
     known[0], before = own_rows(0, before)
     for i in range(1, len(pieces)):
-        known[i], before = own_rows(i, before)
-        entering[i], before = row_states(i, before)
-    y_col, silu, *col_known = call(
-        functools.partial(col_local_kernel, **sizes),
-        [
-            pltpu.VMEM((tokens, channels), F32),
-            pltpu.VMEM((tokens, channels), F32),
-            pltpu.VMEM((tokens, 2 * heads), BF16),
-            pltpu.VMEM((tokens, cols * state), BF16),
-        ],
-        2,
-        specs=[None] * 6 + [any_spec],
-    )(params, x, raw, maps, gate, skip.reshape(1, heads), before)
-    w = call(
-        functools.partial(col_out_kernel, heads=heads, width=width),
-        pltpu.VMEM((tokens, channels), F32),
-        0,
-    )(col_entering, y_col, *col_known)
+        if len(pieces[i]) > 1 or col_count > 2 * group:
+            known[i], before = own_rows(i, before)
+            entering[i], before = row_states(i, before)
+            continue
+        rows = pieces[i][0]
+        places = rows // cols * state
+        made, *own = call(
+            functools.partial(row_both_kernel, **sizes, **shared),
+            [
+                pltpu.VMEM((places, channels), BF16),
+                pltpu.VMEM((group * rows, channels), F32),
+                pltpu.VMEM((group * rows, 2 * heads), BF16),
+                pltpu.VMEM((group * rows, places), BF16),
+            ],
+            2,
+            specs=[None] * (1 + group) + [any_spec],
+        )(params, *got[i], before)
+        known[i], before = [own], made
+        entering[i] = [entering_states(made, [], "col", col_count, group, width, wrap=False)]
     parts_of = []
     for i, piece in enumerate(pieces):
         for j, rows in enumerate(piece):
@@ -453,16 +472,34 @@
             parts_of.append((first, rows, known[i][j], entering[i][j]))
 
     back = []
-    before = y_col
     for _, rows, known, entering in parts_of:
         y_row = call(
             functools.partial(row_out_kernel, heads=heads, width=width),
             [pltpu.VMEM((rows, channels), BF16)] * group,
             0,
-            specs=[None] * 4 + [any_spec],
-        )(entering, *known, before)
+            specs=[None] * 4 + [any_spec] * 2,
+        )(entering, *known, before, col_entering if back else before)
         back.append(exchange(y_row))
-        before = col_entering
+        before = y_row[0]
+        if len(back) > 1:
+            continue
+        y_col, silu, *col_known = call(
+            functools.partial(col_local_kernel, **sizes),
+            [
+                pltpu.VMEM((tokens, channels), F32),
+                pltpu.VMEM((tokens, channels), F32),
+                pltpu.VMEM((tokens, 2 * heads), BF16),
+                pltpu.VMEM((tokens, cols * state), BF16),
+            ],
+            2,
+            specs=[None] * 6 + [any_spec],
+        )(params, x, raw, maps, gate, skip.reshape(1, heads), before)
+        w = call(
+            functools.partial(col_out_kernel, heads=heads, width=width),
+            pltpu.VMEM((tokens, channels), F32),
+            0,
+        )(col_entering, y_col, *col_known)
+        before = y_col
 
     which = [0, *range(group - 1, 0, -1)]
     mixed = None

time: 41.1 us -> 41.1 us (level)
  the two profiles are of different devices: /device:TPU:0 before, /device:TPU:26 now
where the time goes in v21:
time: 41.1 us; the launch traced here: 40.9 us
  starting transfers between devices  16.5 us (40%)
  Pallas kernels  12.1 us (29%)
  waiting for transfers between devices  11.4 us (28%)
  between operations  0.83 us (2%)
    ppermute x12, starting transfers between devices, exchange(): lax.ppermute(blocks[i], 'col', [(at, partner(at, i, group)) for at in ran...  14.2 us
    ppermute x3, waiting for transfers between devices, entering_states(): entering = lax.ppermute(ends, axis, onward)  7.64 us
    ppermute x12, waiting for transfers between devices, exchange(): lax.ppermute(blocks[i], 'col', [(at, partner(at, i, group)) for at in ran...  3.8 us
    ppermute x3, starting transfers between devices, entering_states(): entering = lax.ppermute(ends, axis, onward)  2.29 us
    pallas_call x1, Pallas kernels, body(): call(functools.partial(col_local_kernel, **sizes), [pltpu.VMEM((tokens, c...  2.16 us
    pallas_call x2, Pallas kernels, body(): call(functools.partial(final_kernel, which=which, offset=first, share=sha...  1.9 us
    pallas_call x1, Pallas kernels, body(): pl.pallas_call(functools.partial(pack_kernel, heads=heads, state=state, *...  1.48 us
    pallas_call x1, Pallas kernels, body(): call(functools.partial(col_state_kernel, **sizes), state_shapes([cols * s...  1.47 us
  transfers between devices with their start and end apart: 15, of which 5 were waited for; matrix products, arithmetic and copies ran while one was open for 0% of the time, Pallas kernels for 24%

profile of v21, /device:TPU:26, one launch (start us, length us, event | category | flops | bytes accessed | tf_op | source)
XLA Modules:
  0.0 40.9 jit_solution(5800288898293618953)
XLA Ops:
  0.0 0.0 copy-start
  0.0 1.5 %shard_map.91 = (bf16[256,48]{1,0:T(8,128)(2,1)S(1)}, bf16[256,64]{1,0:T(8,128)(2,1)S(1)}, f32[48,1000]{1,0:T(8,128)S(1)}, f32[2,24]{1,0:T(2,128)S(1)}, bf16[32,...) custom-call(bf16[256,1536]{1,0:T(8,128)(2,1)} %bitcast.7, ...), custom_call_target="tpu_custom_call" | custom-call | flops 1000001024 | bytes 1024 | tf_op jit(solution)/shard_map/pallas_call | solution.py:366
  1.5 1.6 %collective-permute-start = (bf16[32,1664]{1,0:T(8,128)(2,1)S(1)}, bf16[32,1664]{1,0:T(8,128)(2,1)S(1)}, u32[]{:S(2)}, u32[]{:S(2)}) collective-permute-start(bf16[32,1664]{1,0:T(8,128)(2,1)S(1)} %get-tuple-element.45), channel_id=1, source_target_pairs={{0,2},{2,0},{4,6},{6,4},{8,10},{10,8},{12,14},{14,12},{1,3},{3,1},... | collective-permute-start | bytes 319496 | tf_op jit(solution)/shard_map/ppermute | solution.py:394
  3.1 0.4 %collective-permute-start.1 = (bf16[32,1664]{1,0:T(8,128)(2,1)S(1)}, bf16[32,1664]{1,0:T(8,128)(2,1)S(1)}, u32[]{:S(2)}, u32[]{:S(2)}) collective-permute-start(bf16[32,1664]{1,0:T(8,128)(2,1)S(1)} %get-tuple-element.46), channel_id=1, source_target_pairs={{0,4},{2,6},{4,0},{6,2},{8,12},{10,14},{12,8},{14,10},{1,5},{3,7},... | collective-permute-start | bytes 319496 | tf_op jit(solution)/shard_map/ppermute | solution.py:394
  3.5 1.5 %collective-permute-start.2 = (bf16[32,1664]{1,0:T(8,128)(2,1)S(1)}, bf16[32,1664]{1,0:T(8,128)(2,1)S(1)}, u32[]{:S(2)}, u32[]{:S(2)}) collective-permute-start(bf16[32,1664]{1,0:T(8,128)(2,1)S(1)} %get-tuple-element.47), channel_id=1, source_target_pairs={{0,6},{2,4},{4,2},{6,0},{8,14},{10,12},{12,10},{14,8},{1,7},{3,5},... | collective-permute-start | bytes 319496 | tf_op jit(solution)/shard_map/ppermute | solution.py:394
  5.0 1.5 %collective-permute-start.5 = (bf16[32,1664]{1,0:T(8,128)(2,1)S(1)}, bf16[32,1664]{1,0:T(8,128)(2,1)S(1)}, u32[]{:S(2)}, u32[]{:S(2)}) collective-permute-start(bf16[32,1664]{1,0:T(8,128)(2,1)S(1)} %get-tuple-element.52), channel_id=1, source_target_pairs={{0,2},{2,0},{4,6},{6,4},{8,10},{10,8},{12,14},{14,12},{1,3},{3,1},... | collective-permute-start | bytes 319496 | tf_op jit(solution)/shard_map/ppermute | solution.py:394
  6.6 0.4 %collective-permute-start.6 = (bf16[32,1664]{1,0:T(8,128)(2,1)S(1)}, bf16[32,1664]{1,0:T(8,128)(2,1)S(1)}, u32[]{:S(2)}, u32[]{:S(2)}) collective-permute-start(bf16[32,1664]{1,0:T(8,128)(2,1)S(1)} %get-tuple-element.53), channel_id=1, source_target_pairs={{0,4},{2,6},{4,0},{6,2},{8,12},{10,14},{12,8},{14,10},{1,5},{3,7},... | collective-permute-start | bytes 319496 | tf_op jit(solution)/shard_map/ppermute | solution.py:394
  7.7 0.2 shard_map.92.params_ref.refs_4_
  7.8 0.0 collective-permute-done.refs_1_
  7.8 1.5 %collective-permute-start.7 = (bf16[32,1664]{1,0:T(8,128)(2,1)S(1)}, bf16[32,1664]{1,0:T(8,128)(2,1)S(1)}, u32[]{:S(2)}, u32[]{:S(2)}) collective-permute-start(bf16[32,1664]{1,0:T(8,128)(2,1)S(1)} %get-tuple-element.54), channel_id=1, source_target_pairs={{0,6},{2,4},{4,2},{6,0},{8,14},{10,12},{12,10},{14,8},{1,7},{3,5},... | collective-permute-start | bytes 319496 | tf_op jit(solution)/shard_map/ppermute | solution.py:394
  9.4 0.0 collective-permute-done.1.refs_2_
  9.4 1.8 %collective-permute-done.2.refs_3_ = bf16[32,1664]{1,0:T(8,128)(2,1)S(1)} collective-permute-done((bf16[32,1664]{1,0:T(8,128)(2,1)S(1)}, bf16[32,1664]{1,0:T(8,128)(2,1)S(1)}, u32[]{:S(2)}, u32[]{:S(2)}) %collective-permute-start.2) | collective-permute-done | bytes 106528 | tf_op jit(solution)/shard_map/ppermute | solution.py:394
  11.2 1.1 %shard_map.93._ = bf16[64,1536]{1,0:T(8,128)(2,1)S(1)} custom-call(f32[8,48]{1,0:T(8,128)S(1)} %shard_map.92.params_ref.refs_4_, bf16[32,1664]{1,0:T(8,128)(2,1)S(1)} %get-tuple-element.44.refs_0_, bf16[32,1664]{1,0:T(8,128)(2,1)S(1)} %collective-permute-done.refs_1_, bf16[32,1664]{1,0:T(8,128)(2,1)S(1)} %collective-permute-done.1.refs_2_, ...), custom_call_target="tpu_custom_call" | custom-call | flops 1024 | bytes 1024 | tf_op jit(solution)/shard_map/pallas_call | solution.py:424
  12.3 0.4 collective-permute-start.4
  12.7 0.0 copy-done
  12.7 1.5 %shard_map.94.refs_4_ = bf16[128,1536]{1,0:T(8,128)(2,1)S(1)} custom-call(f32[8,48]{1,0:T(8,128)S(1)} %shard_map.92.params_ref.refs_4_, bf16[256,1536]{1,0:T(8,128)(2,1)S(1)} %bitcast.8, bf16[256,48]{1,0:T(8,128)(2,1)S(1)} %get-tuple-element.42.raw_ref, bf16[256,64]{1,0:T(8,128)(2,1)S(1)} %get-tuple-element.43.maps_ref, bf16[64,1536]{1,0:T(8,128)(2,1)S(1)} %shard_map.93._), custom_call_target="tpu_custom_call" | custom-call | flops 1024 | bytes 1024 | tf_op jit(solution)/shard_map/pallas_call | solution.py:439
  14.2 0.6 %collective-permute-start.3 = (bf16[128,1536]{1,0:T(8,128)(2,1)S(1)}, bf16[128,1536]{1,0:T(8,128)(2,1)S(1)}, u32[]{:S(2)}, u32[]{:S(2)}) collective-permute-start(bf16[128,1536]{1,0:T(8,128)(2,1)S(1)} %shard_map.94.refs_4_), channel_id=1, source_target_pairs={{0,16},{16,0},{1,17},{17,1},{2,18},{18,2},{3,19},{19,3},{4,20},{20... | collective-permute-start | bytes 1179656 | tf_op jit(solution)/shard_map/ppermute | solution.py:336
  14.8 1.2 %shard_map.95 = (f32[128,1536]{1,0:T(8,128)S(1)}, bf16[128,48]{1,0:T(8,128)(2,1)S(1)}, bf16[128,64]{1,0:T(8,128)(2,1)S(1)}) custom-call(f32[8,48]{1,0:T(8,128)S(1)} %shard_map.92.params_ref.refs_4_, bf16[32,1664]{1,0:T(8,128)(2,1)S(1)} %get-tuple-element.44.refs_0_, bf16[32,1664]{1,0:T(8,128)(2,1)S(1)} %collective-permute-done.refs_1_, ...), custom_call_target="tpu_custom_call" | custom-call | flops 2000001024 | bytes 1024 | tf_op jit(solution)/shard_map/pallas_call | solution.py:408
  16.0 0.0 collective-permute-done.5.refs_1_
  16.0 0.0 collective-permute-done.6.refs_2_
  16.0 0.0 collective-permute-done.7.refs_3_
  16.1 0.0 copy-start.1
  16.1 0.0 copy-start.2
  16.1 1.4 %shard_map.96 = (bf16[64,1536]{1,0:T(8,128)(2,1)S(1)}, f32[128,1536]{1,0:T(8,128)S(1)}, bf16[128,48]{1,0:T(8,128)(2,1)S(1)}, bf16[128,64]{1,0:T(8,128)(2,1)S(1)}) custom-call(f32[8,48]{1,0:T(8,128)S(1)} %shard_map.92.params_ref.refs_4_, bf16[32,1664]{1,0:T(8,128)(2,1)S(1)} %get-tuple-element.51.refs_0_, bf16[32,1664]{1,0:T(8,128)(2,1)S(1)} %collective-permute-done.5.refs_1_, ...), custom_call_target="tpu_custom_call" | custom-call | flops 2000001024 | bytes 1024 | tf_op jit(solution)/shard_map/pallas_call | solution.py:455
  17.5 1.3 %collective-permute-start.11 = (bf16[64,1536]{1,0:T(8,128)(2,1)S(1)}, bf16[64,1536]{1,0:T(8,128)(2,1)S(1)}, u32[]{:S(2)}, u32[]{:S(2)}) collective-permute-start(bf16[64,1536]{1,0:T(8,128)(2,1)S(1)} %get-tuple-element.55._.__), channel_id=1, source_target_pairs={{0,8},{2,10},{4,12},{6,14},{1,9},{3,11},{5,13},{7,15},{16,24},{18,... | collective-permute-start | bytes 589832 | tf_op jit(solution)/shard_map/ppermute | solution.py:336
  18.8 7.6 %collective-permute-done.4.s_ref = bf16[64,1536]{1,0:T(8,128)(2,1)S(1)} collective-permute-done((bf16[64,1536]{1,0:T(8,128)(2,1)S(1)}, bf16[64,1536]{1,0:T(8,128)(2,1)S(1)}, u32[]{:S(2)}, u32[]{:S(2)}) %collective-permute-start.4) | collective-permute-done | bytes 196640 | tf_op jit(solution)/shard_map/ppermute | solution.py:336
  26.4 0.3 shard_map.97
  26.8 1.0 %collective-permute-start.10 = (bf16[32,1536]{1,0:T(8,128)(2,1)S(1)}, bf16[32,1536]{1,0:T(8,128)(2,1)S(1)}, u32[]{:S(2)}, u32[]{:S(2)}) collective-permute-start(bf16[32,1536]{1,0:T(8,128)(2,1)S(1)} %get-tuple-element.63), channel_id=1, source_target_pairs={{0,2},{2,0},{4,6},{6,4},{8,10},{10,8},{12,14},{14,12},{1,3},{3,1},... | collective-permute-start | bytes 294920 | tf_op jit(solution)/shard_map/ppermute | solution.py:394
  27.8 0.0 collective-permute-start.8
  27.8 2.6 %collective-permute-start.9 = (bf16[32,1536]{1,0:T(8,128)(2,1)S(1)}, bf16[32,1536]{1,0:T(8,128)(2,1)S(1)}, u32[]{:S(2)}, u32[]{:S(2)}) collective-permute-start(bf16[32,1536]{1,0:T(8,128)(2,1)S(1)} %get-tuple-element.62), channel_id=1, source_target_pairs={{0,4},{2,6},{4,0},{6,2},{8,12},{10,14},{12,8},{14,10},{1,5},{3,7},... | collective-permute-start | bytes 294920 | tf_op jit(solution)/shard_map/ppermute | solution.py:394
  30.3 0.0 copy-done.1
  30.3 0.0 copy-done.2
  30.3 2.2 %shard_map.98 = (f32[256,1536]{1,0:T(8,128)S(1)}, f32[256,1536]{1,0:T(8,128)S(1)}, bf16[256,48]{1,0:T(8,128)(2,1)S(1)}, bf16[256,128]{1,0:T(8,128)(2,1)S(1)}) custom-call(f32[8,48]{1,0:T(8,128)S(1)} %shard_map.92.params_ref.refs_4_, bf16[256,1536]{1,0:T(8,128)(2,1)S(1)} %bitcast.9, bf16[256,48]{1,0:T(8,128)(2,1)S(1)} %get-tuple-element.42.raw_ref, ...), custom_call_target="tpu_custom_call" | custom-call | flops 2000001024 | bytes 1024 | tf_op jit(solution)/shard_map/pallas_call | solution.py:486
  32.5 0.0 copy-start.3
  32.5 0.0 collective-permute-done.11.s_ref
  32.5 0.0 collective-permute-done.3.s_ref.__
  32.5 0.3 shard_map.101
  32.9 0.4 %collective-permute-start.12 = (bf16[32,1536]{1,0:T(8,128)(2,1)S(1)}, bf16[32,1536]{1,0:T(8,128)(2,1)S(1)}, u32[]{:S(2)}, u32[]{:S(2)}) collective-permute-start(bf16[32,1536]{1,0:T(8,128)(2,1)S(1)} %get-tuple-element.68), channel_id=1, source_target_pairs={{0,6},{2,4},{4,2},{6,0},{8,14},{10,12},{12,10},{14,8},{1,7},{3,5},... | collective-permute-start | bytes 294920 | tf_op jit(solution)/shard_map/ppermute | solution.py:394
  33.3 2.0 %collective-permute-start.13 = (bf16[32,1536]{1,0:T(8,128)(2,1)S(1)}, bf16[32,1536]{1,0:T(8,128)(2,1)S(1)}, u32[]{:S(2)}, u32[]{:S(2)}) collective-permute-start(bf16[32,1536]{1,0:T(8,128)(2,1)S(1)} %get-tuple-element.69), channel_id=1, source_target_pairs={{0,4},{2,6},{4,0},{6,2},{8,12},{10,14},{12,8},{14,10},{1,5},{3,7},... | collective-permute-start | bytes 294920 | tf_op jit(solution)/shard_map/ppermute | solution.py:394
  35.3 0.0 collective-permute-done.10.refs_3_
  35.3 1.1 %collective-permute-start.14 = (bf16[32,1536]{1,0:T(8,128)(2,1)S(1)}, bf16[32,1536]{1,0:T(8,128)(2,1)S(1)}, u32[]{:S(2)}, u32[]{:S(2)}) collective-permute-start(bf16[32,1536]{1,0:T(8,128)(2,1)S(1)} %get-tuple-element.70), channel_id=1, source_target_pairs={{0,2},{2,0},{4,6},{6,4},{8,10},{10,8},{12,14},{14,12},{1,3},{3,1},... | collective-permute-start | bytes 294920 | tf_op jit(solution)/shard_map/ppermute | solution.py:394
  36.4 0.0 copy-done.3
  36.4 0.6 %shard_map.99.w_ref = f32[256,1536]{1,0:T(8,128)S(1)} custom-call(bf16[128,1536]{1,0:T(8,128)(2,1)S(1)} %collective-permute-done.3.s_ref.__, f32[256,1536]{1,0:T(8,128)S(1)} %get-tuple-element.57.y_ref._, bf16[256,48]{1,0:T(8,128)(2,1)S(1)} %get-tuple-element.58.fade_ref, bf16[256,128]{1,0:T(8,128)(2,1)S(1)} %get-tuple-element.59.entry_ref), custom_call_target="tpu_custom_call" | custom-call | flops 1024 | bytes 1024 | tf_op jit(solution)/shard_map/pallas_call | solution.py:497
  37.0 0.0 collective-permute-done.8.refs_1_
  37.0 0.0 collective-permute-done.9.refs_2_
  37.0 1.0 %shard_map.100.refs_0_ = bf16[256,1536]{1,0:T(8,128)(2,1)} custom-call(f32[256,1536]{1,0:T(8,128)S(1)} %shard_map.99.w_ref, f32[256,1536]{1,0:T(8,128)S(1)} %get-tuple-element.60.g_ref, f32[1,1536]{1,0:T(1,128)S(1)} %reshape.27.gain_ref, bf16[32,1536]{1,0:T(8,128)(2,1)S(1)} %get-tuple-element.56._.refs_0_, ...), custom_call_target="tpu_custom_call" | custom-call | flops 1024 | bytes 1024 | tf_op jit(solution)/shard_map/pallas_call | solution.py:509
  38.0 0.5 %collective-permute-done.12.refs_2_ = bf16[32,1536]{1,0:T(8,128)(2,1)S(1)} collective-permute-done((bf16[32,1536]{1,0:T(8,128)(2,1)S(1)}, bf16[32,1536]{1,0:T(8,128)(2,1)S(1)}, u32[]{:S(2)}, u32[]{:S(2)}) %collective-permute-start.12) | collective-permute-done | bytes 98336 | tf_op jit(solution)/shard_map/ppermute | solution.py:394
  38.5 0.5 %collective-permute-done.13.refs_3_ = bf16[32,1536]{1,0:T(8,128)(2,1)S(1)} collective-permute-done((bf16[32,1536]{1,0:T(8,128)(2,1)S(1)}, bf16[32,1536]{1,0:T(8,128)(2,1)S(1)}, u32[]{:S(2)}, u32[]{:S(2)}) %collective-permute-start.13) | collective-permute-done | bytes 98336 | tf_op jit(solution)/shard_map/ppermute | solution.py:394
  39.0 1.0 %collective-permute-done.14.refs_4_ = bf16[32,1536]{1,0:T(8,128)(2,1)S(1)} collective-permute-done((bf16[32,1536]{1,0:T(8,128)(2,1)S(1)}, bf16[32,1536]{1,0:T(8,128)(2,1)S(1)}, u32[]{:S(2)}, u32[]{:S(2)}) %collective-permute-start.14) | collective-permute-done | bytes 98336 | tf_op jit(solution)/shard_map/ppermute | solution.py:394
  40.0 0.9 %shard_map.102 = bf16[256,1536]{1,0:T(8,128)(2,1)} custom-call(f32[256,1536]{1,0:T(8,128)S(1)} %shard_map.99.w_ref, f32[256,1536]{1,0:T(8,128)S(1)} %get-tuple-element.60.g_ref, f32[1,1536]{1,0:T(1,128)S(1)} %reshape.27.gain_ref, bf16[256,1536]{1,0:T(8,128)(2,1)} %shard_map.100.refs_0_, ...), custom_call_target="tpu_custom_call", output_to_operand_aliasing={{}: (3, {})} | custom-call | flops 1024 | bytes 1024 | tf_op jit(solution)/shard_map/pallas_call | solution.py:509
  (1 shorter events, 0.0 us)
Async XLA Ops:
  0.0 12.7 %copy-start = (bf16[1,32,8,1536]{3,2,1,0:T(8,128)(2,1)S(1)}, bf16[1,32,8,1536]{3,2,1,0:T(8,128)(2,1)}, u32[]{:S(2)}) copy-start(bf16[1,32,8,1536]{3,2,1,0:T(8,128)(2,1)} %param.9) | copy-start | bytes 2359300
  1.5 6.4 %collective-permute-start = (bf16[32,1664]{1,0:T(8,128)(2,1)S(1)}, bf16[32,1664]{1,0:T(8,128)(2,1)S(1)}, u32[]{:S(2)}, u32[]{:S(2)}) collective-permute-start(bf16[32,1664]{1,0:T(8,128)(2,1)S(1)} %get-tuple-element.45), channel_id=1, source_target_pairs={{0,2},{2,0},{4,6},{6,4},{8,10},{10,8},{12,14},{14,12},{1,3},{3,1},... | collective-permute-start | bytes 319496 | tf_op jit(solution)/shard_map/ppermute | solution.py:394
  3.1 6.3 %collective-permute-start.1 = (bf16[32,1664]{1,0:T(8,128)(2,1)S(1)}, bf16[32,1664]{1,0:T(8,128)(2,1)S(1)}, u32[]{:S(2)}, u32[]{:S(2)}) collective-permute-start(bf16[32,1664]{1,0:T(8,128)(2,1)S(1)} %get-tuple-element.46), channel_id=1, source_target_pairs={{0,4},{2,6},{4,0},{6,2},{8,12},{10,14},{12,8},{14,10},{1,5},{3,7},... | collective-permute-start | bytes 319496 | tf_op jit(solution)/shard_map/ppermute | solution.py:394
  3.5 7.7 %collective-permute-start.2 = (bf16[32,1664]{1,0:T(8,128)(2,1)S(1)}, bf16[32,1664]{1,0:T(8,128)(2,1)S(1)}, u32[]{:S(2)}, u32[]{:S(2)}) collective-permute-start(bf16[32,1664]{1,0:T(8,128)(2,1)S(1)} %get-tuple-element.47), channel_id=1, source_target_pairs={{0,6},{2,4},{4,2},{6,0},{8,14},{10,12},{12,10},{14,8},{1,7},{3,5},... | collective-permute-start | bytes 319496 | tf_op jit(solution)/shard_map/ppermute | solution.py:394
  5.0 11.0 %collective-permute-start.5 = (bf16[32,1664]{1,0:T(8,128)(2,1)S(1)}, bf16[32,1664]{1,0:T(8,128)(2,1)S(1)}, u32[]{:S(2)}, u32[]{:S(2)}) collective-permute-start(bf16[32,1664]{1,0:T(8,128)(2,1)S(1)} %get-tuple-element.52), channel_id=1, source_target_pairs={{0,2},{2,0},{4,6},{6,4},{8,10},{10,8},{12,14},{14,12},{1,3},{3,1},... | collective-permute-start | bytes 319496 | tf_op jit(solution)/shard_map/ppermute | solution.py:394
  6.6 9.5 %collective-permute-start.6 = (bf16[32,1664]{1,0:T(8,128)(2,1)S(1)}, bf16[32,1664]{1,0:T(8,128)(2,1)S(1)}, u32[]{:S(2)}, u32[]{:S(2)}) collective-permute-start(bf16[32,1664]{1,0:T(8,128)(2,1)S(1)} %get-tuple-element.53), channel_id=1, source_target_pairs={{0,4},{2,6},{4,0},{6,2},{8,12},{10,14},{12,8},{14,10},{1,5},{3,7},... | collective-permute-start | bytes 319496 | tf_op jit(solution)/shard_map/ppermute | solution.py:394
  7.8 8.2 %collective-permute-start.7 = (bf16[32,1664]{1,0:T(8,128)(2,1)S(1)}, bf16[32,1664]{1,0:T(8,128)(2,1)S(1)}, u32[]{:S(2)}, u32[]{:S(2)}) collective-permute-start(bf16[32,1664]{1,0:T(8,128)(2,1)S(1)} %get-tuple-element.54), channel_id=1, source_target_pairs={{0,6},{2,4},{4,2},{6,0},{8,14},{10,12},{12,10},{14,8},{1,7},{3,5},... | collective-permute-start | bytes 319496 | tf_op jit(solution)/shard_map/ppermute | solution.py:394
  12.3 14.1 %collective-permute-start.4 = (bf16[64,1536]{1,0:T(8,128)(2,1)S(1)}, bf16[64,1536]{1,0:T(8,128)(2,1)S(1)}, u32[]{:S(2)}, u32[]{:S(2)}) collective-permute-start(bf16[64,1536]{1,0:T(8,128)(2,1)S(1)} %shard_map.93._), channel_id=1, source_target_pairs={{0,8},{2,10},{4,12},{6,14},{8,0},{10,2},{12,4},{14,6},{1,9},{3,11}... | collective-permute-start | bytes 589832 | tf_op jit(solution)/shard_map/ppermute | solution.py:336
  14.2 18.3 %collective-permute-start.3 = (bf16[128,1536]{1,0:T(8,128)(2,1)S(1)}, bf16[128,1536]{1,0:T(8,128)(2,1)S(1)}, u32[]{:S(2)}, u32[]{:S(2)}) collective-permute-start(bf16[128,1536]{1,0:T(8,128)(2,1)S(1)} %shard_map.94.refs_4_), channel_id=1, source_target_pairs={{0,16},{16,0},{1,17},{17,1},{2,18},{18,2},{3,19},{19,3},{4,20},{20... | collective-permute-start | bytes 1179656 | tf_op jit(solution)/shard_map/ppermute | solution.py:336
  16.1 14.3 %copy-start.1 = (bf16[1,32,8,1536]{3,2,1,0:T(8,128)(2,1)S(1)}, bf16[1,32,8,1536]{3,2,1,0:T(8,128)(2,1)}, u32[]{:S(2)}) copy-start(bf16[1,32,8,1536]{3,2,1,0:T(8,128)(2,1)} %param.10) | copy-start | bytes 2359300
  16.1 14.3 %copy-start.2 = (f32[24]{0:T(128)S(1)}, f32[24]{0:T(128)}, u32[]{:S(2)}) copy-start(f32[24]{0:T(128)} %param.16) | copy-start | bytes 292
  17.5 15.0 %collective-permute-start.11 = (bf16[64,1536]{1,0:T(8,128)(2,1)S(1)}, bf16[64,1536]{1,0:T(8,128)(2,1)S(1)}, u32[]{:S(2)}, u32[]{:S(2)}) collective-permute-start(bf16[64,1536]{1,0:T(8,128)(2,1)S(1)} %get-tuple-element.55._.__), channel_id=1, source_target_pairs={{0,8},{2,10},{4,12},{6,14},{1,9},{3,11},{5,13},{7,15},{16,24},{18,... | collective-permute-start | bytes 589832 | tf_op jit(solution)/shard_map/ppermute | solution.py:336
  26.8 8.6 %collective-permute-start.10 = (bf16[32,1536]{1,0:T(8,128)(2,1)S(1)}, bf16[32,1536]{1,0:T(8,128)(2,1)S(1)}, u32[]{:S(2)}, u32[]{:S(2)}) collective-permute-start(bf16[32,1536]{1,0:T(8,128)(2,1)S(1)} %get-tuple-element.63), channel_id=1, source_target_pairs={{0,2},{2,0},{4,6},{6,4},{8,10},{10,8},{12,14},{14,12},{1,3},{3,1},... | collective-permute-start | bytes 294920 | tf_op jit(solution)/shard_map/ppermute | solution.py:394
  27.8 9.3 %collective-permute-start.8 = (bf16[32,1536]{1,0:T(8,128)(2,1)S(1)}, bf16[32,1536]{1,0:T(8,128)(2,1)S(1)}, u32[]{:S(2)}, u32[]{:S(2)}) collective-permute-start(bf16[32,1536]{1,0:T(8,128)(2,1)S(1)} %get-tuple-element.61), channel_id=1, source_target_pairs={{0,6},{2,4},{4,2},{6,0},{8,14},{10,12},{12,10},{14,8},{1,7},{3,5},... | collective-permute-start | bytes 294920 | tf_op jit(solution)/shard_map/ppermute | solution.py:394
  27.8 9.3 %collective-permute-start.9 = (bf16[32,1536]{1,0:T(8,128)(2,1)S(1)}, bf16[32,1536]{1,0:T(8,128)(2,1)S(1)}, u32[]{:S(2)}, u32[]{:S(2)}) collective-permute-start(bf16[32,1536]{1,0:T(8,128)(2,1)S(1)} %get-tuple-element.62), channel_id=1, source_target_pairs={{0,4},{2,6},{4,0},{6,2},{8,12},{10,14},{12,8},{14,10},{1,5},{3,7},... | collective-permute-start | bytes 294920 | tf_op jit(solution)/shard_map/ppermute | solution.py:394
  32.5 3.9 %copy-start.3 = (f32[1536]{0:T(1024)S(1)}, f32[1536]{0:T(1024)}, u32[]{:S(2)}) copy-start(f32[1536]{0:T(1024)} %param.17) | copy-start | bytes 18436
  32.9 5.6 %collective-permute-start.12 = (bf16[32,1536]{1,0:T(8,128)(2,1)S(1)}, bf16[32,1536]{1,0:T(8,128)(2,1)S(1)}, u32[]{:S(2)}, u32[]{:S(2)}) collective-permute-start(bf16[32,1536]{1,0:T(8,128)(2,1)S(1)} %get-tuple-element.68), channel_id=1, source_target_pairs={{0,6},{2,4},{4,2},{6,0},{8,14},{10,12},{12,10},{14,8},{1,7},{3,5},... | collective-permute-start | bytes 294920 | tf_op jit(solution)/shard_map/ppermute | solution.py:394
  33.3 5.7 %collective-permute-start.13 = (bf16[32,1536]{1,0:T(8,128)(2,1)S(1)}, bf16[32,1536]{1,0:T(8,128)(2,1)S(1)}, u32[]{:S(2)}, u32[]{:S(2)}) collective-permute-start(bf16[32,1536]{1,0:T(8,128)(2,1)S(1)} %get-tuple-element.69), channel_id=1, source_target_pairs={{0,4},{2,6},{4,0},{6,2},{8,12},{10,14},{12,8},{14,10},{1,5},{3,7},... | collective-permute-start | bytes 294920 | tf_op jit(solution)/shard_map/ppermute | solution.py:394
  35.3 4.6 %collective-permute-start.14 = (bf16[32,1536]{1,0:T(8,128)(2,1)S(1)}, bf16[32,1536]{1,0:T(8,128)(2,1)S(1)}, u32[]{:S(2)}, u32[]{:S(2)}) collective-permute-start(bf16[32,1536]{1,0:T(8,128)(2,1)S(1)} %get-tuple-element.70), channel_id=1, source_target_pairs={{0,2},{2,0},{4,6},{6,4},{8,10},{10,8},{12,14},{14,12},{1,3},{3,1},... | collective-permute-start | bytes 294920 | tf_op jit(solution)/shard_map/ppermute | solution.py:394

commit v22 on v21

--- a/solution.py
+++ b/solution.py
@@ -444,7 +444,23 @@
     )(params, x, raw, maps, before)
     col_entering = entering_states(col_made[0], col_made[1:], "row", row_count, 1, width)
     before = col_made[0]
-    known[0], before = own_rows(0, before)
+    y_col, silu, *col_known = call(
+        functools.partial(col_local_kernel, **sizes),
+        [
+            pltpu.VMEM((tokens, channels), F32),
+            pltpu.VMEM((tokens, channels), F32),
+            pltpu.VMEM((tokens, 2 * heads), BF16),
+            pltpu.VMEM((tokens, cols * state), BF16),
+        ],
+        2,
+        specs=[None] * 6 + [any_spec],
+    )(params, x, raw, maps, gate, skip.reshape(1, heads), before)
+    w = call(
+        functools.partial(col_out_kernel, heads=heads, width=width),
+        pltpu.VMEM((tokens, channels), F32),
+        0,
+    )(col_entering, y_col, *col_known)
+    before = y_col
     for i in range(1, len(pieces)):
         if len(pieces[i]) > 1 or col_count > 2 * group:
             known[i], before = own_rows(i, before)
@@ -465,6 +481,7 @@
         )(params, *got[i], before)
         known[i], before = [own], made
         entering[i] = [entering_states(made, [], "col", col_count, group, width, wrap=False)]
+    known[0], before = own_rows(0, before)
     parts_of = []
     for i, piece in enumerate(pieces):
         for j, rows in enumerate(piece):
@@ -481,25 +498,6 @@
         )(entering, *known, before, col_entering if back else before)
         back.append(exchange(y_row))
         before = y_row[0]
-        if len(back) > 1:
-            continue
-        y_col, silu, *col_known = call(
-            functools.partial(col_local_kernel, **sizes),
-            [
-                pltpu.VMEM((tokens, channels), F32),
-                pltpu.VMEM((tokens, channels), F32),
-                pltpu.VMEM((tokens, 2 * heads), BF16),
-                pltpu.VMEM((tokens, cols * state), BF16),
-            ],
-            2,
-            specs=[None] * 6 + [any_spec],
-        )(params, x, raw, maps, gate, skip.reshape(1, heads), before)
-        w = call(
-            functools.partial(col_out_kernel, heads=heads, width=width),
-            pltpu.VMEM((tokens, channels), F32),
-            0,
-        )(col_entering, y_col, *col_known)
-        before = y_col
 
     which = [0, *range(group - 1, 0, -1)]
     mixed = None

time: 41.1 us -> 40.1 us (0.976)
  the two profiles are of different devices: /device:TPU:26 before, /device:TPU:0 now
where the time goes in v22:
time: 40.1 us; the launch traced here: 40 us
  starting transfers between devices  22.5 us (56%)
  Pallas kernels  12.1 us (30%)
  waiting for transfers between devices  4.46 us (11%)
  between operations  0.85 us (2%)
    ppermute x12, starting transfers between devices, exchange(): lax.ppermute(blocks[i], 'col', [(at, partner(at, i, group)) for at in ran...  15.7 us
    ppermute x3, starting transfers between devices, entering_states(): entering = lax.ppermute(ends, axis, onward)  6.84 us
    ppermute x12, waiting for transfers between devices, exchange(): lax.ppermute(blocks[i], 'col', [(at, partner(at, i, group)) for at in ran...  4.39 us
    pallas_call x1, Pallas kernels, body(): call(functools.partial(col_local_kernel, **sizes), [pltpu.VMEM((tokens, c...  2.15 us
    pallas_call x2, Pallas kernels, body(): call(functools.partial(final_kernel, which=which, offset=first, share=sha...  1.89 us
    pallas_call x1, Pallas kernels, body(): pl.pallas_call(functools.partial(pack_kernel, heads=heads, state=state, *...  1.48 us
    pallas_call x1, Pallas kernels, body(): call(functools.partial(col_state_kernel, **sizes), state_shapes([cols * s...  1.47 us
    pallas_call x1, Pallas kernels, body(): call(functools.partial(row_both_kernel, **sizes, **shared), [pltpu.VMEM((...  1.39 us
  transfers between devices with their start and end apart: 15, of which 5 were waited for; matrix products, arithmetic and copies ran while one was open for 0% of the time, Pallas kernels for 24%

profile of v22, /device:TPU:0, one launch (start us, length us, event | category | flops | bytes accessed | tf_op | source)
XLA Modules:
  0.0 40.0 jit_solution(18097195736041243780)
XLA Ops:
  0.0 0.0 copy-start
  0.0 1.5 %shard_map.91 = (bf16[256,48]{1,0:T(8,128)(2,1)S(1)}, bf16[256,64]{1,0:T(8,128)(2,1)S(1)}, f32[48,1000]{1,0:T(8,128)S(1)}, f32[2,24]{1,0:T(2,128)S(1)}, bf16[32,...) custom-call(bf16[256,1536]{1,0:T(8,128)(2,1)} %bitcast.7, ...), custom_call_target="tpu_custom_call" | custom-call | flops 1000001024 | bytes 1024 | tf_op jit(solution)/shard_map/pallas_call | solution.py:366
  1.5 0.0 copy-start.1
  1.5 0.0 copy-start.2
  1.5 3.0 %collective-permute-start = (bf16[32,1664]{1,0:T(8,128)(2,1)S(1)}, bf16[32,1664]{1,0:T(8,128)(2,1)S(1)}, u32[]{:S(2)}, u32[]{:S(2)}) collective-permute-start(bf16[32,1664]{1,0:T(8,128)(2,1)S(1)} %get-tuple-element.45), channel_id=1, source_target_pairs={{0,2},{2,0},{4,6},{6,4},{8,10},{10,8},{12,14},{14,12},{1,3},{3,1},... | collective-permute-start | bytes 319496 | tf_op jit(solution)/shard_map/ppermute | solution.py:394
  4.5 1.6 %collective-permute-start.1 = (bf16[32,1664]{1,0:T(8,128)(2,1)S(1)}, bf16[32,1664]{1,0:T(8,128)(2,1)S(1)}, u32[]{:S(2)}, u32[]{:S(2)}) collective-permute-start(bf16[32,1664]{1,0:T(8,128)(2,1)S(1)} %get-tuple-element.46), channel_id=1, source_target_pairs={{0,4},{2,6},{4,0},{6,2},{8,12},{10,14},{12,8},{14,10},{1,5},{3,7},... | collective-permute-start | bytes 319496 | tf_op jit(solution)/shard_map/ppermute | solution.py:394
  6.1 0.0 collective-permute-start.2
  6.1 1.9 %collective-permute-start.5 = (bf16[32,1664]{1,0:T(8,128)(2,1)S(1)}, bf16[32,1664]{1,0:T(8,128)(2,1)S(1)}, u32[]{:S(2)}, u32[]{:S(2)}) collective-permute-start(bf16[32,1664]{1,0:T(8,128)(2,1)S(1)} %get-tuple-element.53), channel_id=1, source_target_pairs={{0,2},{2,0},{4,6},{6,4},{8,10},{10,8},{12,14},{14,12},{1,3},{3,1},... | collective-permute-start | bytes 319496 | tf_op jit(solution)/shard_map/ppermute | solution.py:394
  8.0 1.6 %collective-permute-start.6 = (bf16[32,1664]{1,0:T(8,128)(2,1)S(1)}, bf16[32,1664]{1,0:T(8,128)(2,1)S(1)}, u32[]{:S(2)}, u32[]{:S(2)}) collective-permute-start(bf16[32,1664]{1,0:T(8,128)(2,1)S(1)} %get-tuple-element.54), channel_id=1, source_target_pairs={{0,4},{2,6},{4,0},{6,2},{8,12},{10,14},{12,8},{14,10},{1,5},{3,7},... | collective-permute-start | bytes 319496 | tf_op jit(solution)/shard_map/ppermute | solution.py:394
  10.3 0.2 shard_map.92.params_ref.refs_4_
  10.4 0.0 collective-permute-done.refs_1_
  10.4 0.0 collective-permute-start.7
  10.5 0.0 collective-permute-done.1.refs_2_
  10.5 2.0 %collective-permute-done.2.refs_3_ = bf16[32,1664]{1,0:T(8,128)(2,1)S(1)} collective-permute-done((bf16[32,1664]{1,0:T(8,128)(2,1)S(1)}, bf16[32,1664]{1,0:T(8,128)(2,1)S(1)}, u32[]{:S(2)}, u32[]{:S(2)}) %collective-permute-start.2) | collective-permute-done | bytes 106528 | tf_op jit(solution)/shard_map/ppermute | solution.py:394
  12.5 1.1 %shard_map.93._ = bf16[64,1536]{1,0:T(8,128)(2,1)S(1)} custom-call(f32[8,48]{1,0:T(8,128)S(1)} %shard_map.92.params_ref.refs_4_, bf16[32,1664]{1,0:T(8,128)(2,1)S(1)} %get-tuple-element.44.refs_0_, bf16[32,1664]{1,0:T(8,128)(2,1)S(1)} %collective-permute-done.refs_1_, bf16[32,1664]{1,0:T(8,128)(2,1)S(1)} %collective-permute-done.1.refs_2_, ...), custom_call_target="tpu_custom_call" | custom-call | flops 1024 | bytes 1024 | tf_op jit(solution)/shard_map/pallas_call | solution.py:424
  13.6 3.0 %collective-permute-start.4 = (bf16[64,1536]{1,0:T(8,128)(2,1)S(1)}, bf16[64,1536]{1,0:T(8,128)(2,1)S(1)}, u32[]{:S(2)}, u32[]{:S(2)}) collective-permute-start(bf16[64,1536]{1,0:T(8,128)(2,1)S(1)} %shard_map.93._), channel_id=1, source_target_pairs={{0,8},{2,10},{4,12},{6,14},{8,0},{10,2},{12,4},{14,6},{1,9},{3,11}... | collective-permute-start | bytes 589832 | tf_op jit(solution)/shard_map/ppermute | solution.py:336
  16.6 0.0 copy-done
  16.6 1.5 %shard_map.94._ = bf16[128,1536]{1,0:T(8,128)(2,1)S(1)} custom-call(f32[8,48]{1,0:T(8,128)S(1)} %shard_map.92.params_ref.refs_4_, bf16[256,1536]{1,0:T(8,128)(2,1)S(1)} %bitcast.8, bf16[256,48]{1,0:T(8,128)(2,1)S(1)} %get-tuple-element.42.raw_ref, bf16[256,64]{1,0:T(8,128)(2,1)S(1)} %get-tuple-element.43.maps_ref, bf16[64,1536]{1,0:T(8,128)(2,1)S(1)} %shard_map.93._), custom_call_target="tpu_custom_call" | custom-call | flops 1024 | bytes 1024 | tf_op jit(solution)/shard_map/pallas_call | solution.py:439
  18.1 1.6 %collective-permute-start.3 = (bf16[128,1536]{1,0:T(8,128)(2,1)S(1)}, bf16[128,1536]{1,0:T(8,128)(2,1)S(1)}, u32[]{:S(2)}, u32[]{:S(2)}) collective-permute-start(bf16[128,1536]{1,0:T(8,128)(2,1)S(1)} %shard_map.94._), channel_id=1, source_target_pairs={{0,16},{16,0},{1,17},{17,1},{2,18},{18,2},{3,19},{19,3},{4,20},{20... | collective-permute-start | bytes 1179656 | tf_op jit(solution)/shard_map/ppermute | solution.py:336
  19.6 0.0 copy-done.1
  19.6 0.0 copy-done.2
  19.6 2.2 %shard_map.95 = (f32[256,1536]{1,0:T(8,128)S(1)}, f32[256,1536]{1,0:T(8,128)S(1)}, bf16[256,48]{1,0:T(8,128)(2,1)S(1)}, bf16[256,128]{1,0:T(8,128)(2,1)S(1)}) custom-call(f32[8,48]{1,0:T(8,128)S(1)} %shard_map.92.params_ref.refs_4_, bf16[256,1536]{1,0:T(8,128)(2,1)S(1)} %bitcast.9, bf16[256,48]{1,0:T(8,128)(2,1)S(1)} %get-tuple-element.42.raw_ref, ...), custom_call_target="tpu_custom_call" | custom-call | flops 2000001024 | bytes 1024 | tf_op jit(solution)/shard_map/pallas_call | solution.py:447
  21.8 0.0 collective-permute-done.5.refs_1_
  21.8 0.0 collective-permute-done.6.refs_2_
  21.8 0.0 collective-permute-done.7.refs_3_
  21.8 1.4 %shard_map.97 = (bf16[64,1536]{1,0:T(8,128)(2,1)S(1)}, f32[128,1536]{1,0:T(8,128)S(1)}, bf16[128,48]{1,0:T(8,128)(2,1)S(1)}, bf16[128,64]{1,0:T(8,128)(2,1)S(1)}) custom-call(f32[8,48]{1,0:T(8,128)S(1)} %shard_map.92.params_ref.refs_4_, bf16[32,1664]{1,0:T(8,128)(2,1)S(1)} %get-tuple-element.52.refs_0_, bf16[32,1664]{1,0:T(8,128)(2,1)S(1)} %collective-permute-done.5.refs_1_, ...), custom_call_target="tpu_custom_call" | custom-call | flops 2000001024 | bytes 1024 | tf_op jit(solution)/shard_map/pallas_call | solution.py:471
  23.2 2.3 %collective-permute-start.11 = (bf16[64,1536]{1,0:T(8,128)(2,1)S(1)}, bf16[64,1536]{1,0:T(8,128)(2,1)S(1)}, u32[]{:S(2)}, u32[]{:S(2)}) collective-permute-start(bf16[64,1536]{1,0:T(8,128)(2,1)S(1)} %get-tuple-element.56.refs_4_), channel_id=1, source_target_pairs={{0,8},{2,10},{4,12},{6,14},{1,9},{3,11},{5,13},{7,15},{16,24},{18,... | collective-permute-start | bytes 589832 | tf_op jit(solution)/shard_map/ppermute | solution.py:336
  25.5 1.2 %shard_map.98 = (f32[128,1536]{1,0:T(8,128)S(1)}, bf16[128,48]{1,0:T(8,128)(2,1)S(1)}, bf16[128,64]{1,0:T(8,128)(2,1)S(1)}) custom-call(f32[8,48]{1,0:T(8,128)S(1)} %shard_map.92.params_ref.refs_4_, bf16[32,1664]{1,0:T(8,128)(2,1)S(1)} %get-tuple-element.44.refs_0_, bf16[32,1664]{1,0:T(8,128)(2,1)S(1)} %collective-permute-done.refs_1_, ...), custom_call_target="tpu_custom_call" | custom-call | flops 2000001024 | bytes 1024 | tf_op jit(solution)/shard_map/pallas_call | solution.py:408
  26.7 0.0 copy-start.3
  26.7 0.0 collective-permute-done.4.s_ref
  26.7 0.3 shard_map.99
  27.1 1.4 %collective-permute-start.10 = (bf16[32,1536]{1,0:T(8,128)(2,1)S(1)}, bf16[32,1536]{1,0:T(8,128)(2,1)S(1)}, u32[]{:S(2)}, u32[]{:S(2)}) collective-permute-start(bf16[32,1536]{1,0:T(8,128)(2,1)S(1)} %get-tuple-element.63), channel_id=1, source_target_pairs={{0,2},{2,0},{4,6},{6,4},{8,10},{10,8},{12,14},{14,12},{1,3},{3,1},... | collective-permute-start | bytes 294920 | tf_op jit(solution)/shard_map/ppermute | solution.py:394
  28.5 1.6 %collective-permute-start.8 = (bf16[32,1536]{1,0:T(8,128)(2,1)S(1)}, bf16[32,1536]{1,0:T(8,128)(2,1)S(1)}, u32[]{:S(2)}, u32[]{:S(2)}) collective-permute-start(bf16[32,1536]{1,0:T(8,128)(2,1)S(1)} %get-tuple-element.61), channel_id=1, source_target_pairs={{0,6},{2,4},{4,2},{6,0},{8,14},{10,12},{12,10},{14,8},{1,7},{3,5},... | collective-permute-start | bytes 294920 | tf_op jit(solution)/shard_map/ppermute | solution.py:394
  30.0 0.6 %collective-permute-start.9 = (bf16[32,1536]{1,0:T(8,128)(2,1)S(1)}, bf16[32,1536]{1,0:T(8,128)(2,1)S(1)}, u32[]{:S(2)}, u32[]{:S(2)}) collective-permute-start(bf16[32,1536]{1,0:T(8,128)(2,1)S(1)} %get-tuple-element.62), channel_id=1, source_target_pairs={{0,4},{2,6},{4,0},{6,2},{8,12},{10,14},{12,8},{14,10},{1,5},{3,7},... | collective-permute-start | bytes 294920 | tf_op jit(solution)/shard_map/ppermute | solution.py:394
  30.6 0.1 collective-permute-done.11.s_ref
  30.7 0.0 collective-permute-done.3.s_ref.__
  30.7 0.3 shard_map.101
  31.1 2.4 %collective-permute-start.12 = (bf16[32,1536]{1,0:T(8,128)(2,1)S(1)}, bf16[32,1536]{1,0:T(8,128)(2,1)S(1)}, u32[]{:S(2)}, u32[]{:S(2)}) collective-permute-start(bf16[32,1536]{1,0:T(8,128)(2,1)S(1)} %get-tuple-element.68), channel_id=1, source_target_pairs={{0,6},{2,4},{4,2},{6,0},{8,14},{10,12},{12,10},{14,8},{1,7},{3,5},... | collective-permute-start | bytes 294920 | tf_op jit(solution)/shard_map/ppermute | solution.py:394
  33.5 0.4 %collective-permute-start.13 = (bf16[32,1536]{1,0:T(8,128)(2,1)S(1)}, bf16[32,1536]{1,0:T(8,128)(2,1)S(1)}, u32[]{:S(2)}, u32[]{:S(2)}) collective-permute-start(bf16[32,1536]{1,0:T(8,128)(2,1)S(1)} %get-tuple-element.69), channel_id=1, source_target_pairs={{0,4},{2,6},{4,0},{6,2},{8,12},{10,14},{12,8},{14,10},{1,5},{3,7},... | collective-permute-start | bytes 294920 | tf_op jit(solution)/shard_map/ppermute | solution.py:394
  33.9 0.5 %collective-permute-done.10.refs_3_ = bf16[32,1536]{1,0:T(8,128)(2,1)S(1)} collective-permute-done((bf16[32,1536]{1,0:T(8,128)(2,1)S(1)}, bf16[32,1536]{1,0:T(8,128)(2,1)S(1)}, u32[]{:S(2)}, u32[]{:S(2)}) %collective-permute-start.10) | collective-permute-done | bytes 98336 | tf_op jit(solution)/shard_map/ppermute | solution.py:394
  34.4 1.2 %collective-permute-start.14 = (bf16[32,1536]{1,0:T(8,128)(2,1)S(1)}, bf16[32,1536]{1,0:T(8,128)(2,1)S(1)}, u32[]{:S(2)}, u32[]{:S(2)}) collective-permute-start(bf16[32,1536]{1,0:T(8,128)(2,1)S(1)} %get-tuple-element.70), channel_id=1, source_target_pairs={{0,2},{2,0},{4,6},{6,4},{8,10},{10,8},{12,14},{14,12},{1,3},{3,1},... | collective-permute-start | bytes 294920 | tf_op jit(solution)/shard_map/ppermute | solution.py:394
  35.6 0.0 copy-done.3
  35.6 0.6 %shard_map.96.w_ref = f32[256,1536]{1,0:T(8,128)S(1)} custom-call(bf16[128,1536]{1,0:T(8,128)(2,1)S(1)} %collective-permute-done.3.s_ref.__, f32[256,1536]{1,0:T(8,128)S(1)} %get-tuple-element.48.y_ref.refs_4_, bf16[256,48]{1,0:T(8,128)(2,1)S(1)} %get-tuple-element.49.fade_ref, bf16[256,128]{1,0:T(8,128)(2,1)S(1)} %get-tuple-element.50.entry_ref), custom_call_target="tpu_custom_call" | custom-call | flops 1024 | bytes 1024 | tf_op jit(solution)/shard_map/pallas_call | solution.py:458
  36.2 0.0 collective-permute-done.8.refs_1_
  36.2 0.0 collective-permute-done.9.refs_2_
  36.2 0.9 %shard_map.100.refs_0_ = bf16[256,1536]{1,0:T(8,128)(2,1)} custom-call(f32[256,1536]{1,0:T(8,128)S(1)} %shard_map.96.w_ref, f32[256,1536]{1,0:T(8,128)S(1)} %get-tuple-element.51.g_ref, f32[1,1536]{1,0:T(1,128)S(1)} %reshape.27.gain_ref, bf16[32,1536]{1,0:T(8,128)(2,1)S(1)} %get-tuple-element.60.refs_0_._, ...), custom_call_target="tpu_custom_call" | custom-call | flops 1024 | bytes 1024 | tf_op jit(solution)/shard_map/pallas_call | solution.py:507
  37.2 0.0 collective-permute-done.12.refs_2_
  37.2 0.9 %collective-permute-done.13.refs_3_ = bf16[32,1536]{1,0:T(8,128)(2,1)S(1)} collective-permute-done((bf16[32,1536]{1,0:T(8,128)(2,1)S(1)}, bf16[32,1536]{1,0:T(8,128)(2,1)S(1)}, u32[]{:S(2)}, u32[]{:S(2)}) %collective-permute-start.13) | collective-permute-done | bytes 98336 | tf_op jit(solution)/shard_map/ppermute | solution.py:394
  38.1 1.0 %collective-permute-done.14.refs_4_ = bf16[32,1536]{1,0:T(8,128)(2,1)S(1)} collective-permute-done((bf16[32,1536]{1,0:T(8,128)(2,1)S(1)}, bf16[32,1536]{1,0:T(8,128)(2,1)S(1)}, u32[]{:S(2)}, u32[]{:S(2)}) %collective-permute-start.14) | collective-permute-done | bytes 98336 | tf_op jit(solution)/shard_map/ppermute | solution.py:394
  39.0 0.9 %shard_map.102 = bf16[256,1536]{1,0:T(8,128)(2,1)} custom-call(f32[256,1536]{1,0:T(8,128)S(1)} %shard_map.96.w_ref, f32[256,1536]{1,0:T(8,128)S(1)} %get-tuple-element.51.g_ref, f32[1,1536]{1,0:T(1,128)S(1)} %reshape.27.gain_ref, bf16[256,1536]{1,0:T(8,128)(2,1)} %shard_map.100.refs_0_, ...), custom_call_target="tpu_custom_call", output_to_operand_aliasing={{}: (3, {})} | custom-call | flops 1024 | bytes 1024 | tf_op jit(solution)/shard_map/pallas_call | solution.py:507
  (1 shorter events, 0.0 us)
Async XLA Ops:
  0.0 16.6 %copy-start = (bf16[1,32,8,1536]{3,2,1,0:T(8,128)(2,1)S(1)}, bf16[1,32,8,1536]{3,2,1,0:T(8,128)(2,1)}, u32[]{:S(2)}) copy-start(bf16[1,32,8,1536]{3,2,1,0:T(8,128)(2,1)} %param.9) | copy-start | bytes 2359300
  1.5 18.1 %copy-start.1 = (bf16[1,32,8,1536]{3,2,1,0:T(8,128)(2,1)S(1)}, bf16[1,32,8,1536]{3,2,1,0:T(8,128)(2,1)}, u32[]{:S(2)}) copy-start(bf16[1,32,8,1536]{3,2,1,0:T(8,128)(2,1)} %param.10) | copy-start | bytes 2359300
  1.5 18.1 %copy-start.2 = (f32[24]{0:T(128)S(1)}, f32[24]{0:T(128)}, u32[]{:S(2)}) copy-start(f32[24]{0:T(128)} %param.16) | copy-start | bytes 292
  1.5 8.9 %collective-permute-start = (bf16[32,1664]{1,0:T(8,128)(2,1)S(1)}, bf16[32,1664]{1,0:T(8,128)(2,1)S(1)}, u32[]{:S(2)}, u32[]{:S(2)}) collective-permute-start(bf16[32,1664]{1,0:T(8,128)(2,1)S(1)} %get-tuple-element.45), channel_id=1, source_target_pairs={{0,2},{2,0},{4,6},{6,4},{8,10},{10,8},{12,14},{14,12},{1,3},{3,1},... | collective-permute-start | bytes 319496 | tf_op jit(solution)/shard_map/ppermute | solution.py:394
  4.5 5.9 %collective-permute-start.1 = (bf16[32,1664]{1,0:T(8,128)(2,1)S(1)}, bf16[32,1664]{1,0:T(8,128)(2,1)S(1)}, u32[]{:S(2)}, u32[]{:S(2)}) collective-permute-start(bf16[32,1664]{1,0:T(8,128)(2,1)S(1)} %get-tuple-element.46), channel_id=1, source_target_pairs={{0,4},{2,6},{4,0},{6,2},{8,12},{10,14},{12,8},{14,10},{1,5},{3,7},... | collective-permute-start | bytes 319496 | tf_op jit(solution)/shard_map/ppermute | solution.py:394
  6.1 6.3 %collective-permute-start.2 = (bf16[32,1664]{1,0:T(8,128)(2,1)S(1)}, bf16[32,1664]{1,0:T(8,128)(2,1)S(1)}, u32[]{:S(2)}, u32[]{:S(2)}) collective-permute-start(bf16[32,1664]{1,0:T(8,128)(2,1)S(1)} %get-tuple-element.47), channel_id=1, source_target_pairs={{0,6},{2,4},{4,2},{6,0},{8,14},{10,12},{12,10},{14,8},{1,7},{3,5},... | collective-permute-start | bytes 319496 | tf_op jit(solution)/shard_map/ppermute | solution.py:394
  6.1 15.7 %collective-permute-start.5 = (bf16[32,1664]{1,0:T(8,128)(2,1)S(1)}, bf16[32,1664]{1,0:T(8,128)(2,1)S(1)}, u32[]{:S(2)}, u32[]{:S(2)}) collective-permute-start(bf16[32,1664]{1,0:T(8,128)(2,1)S(1)} %get-tuple-element.53), channel_id=1, source_target_pairs={{0,2},{2,0},{4,6},{6,4},{8,10},{10,8},{12,14},{14,12},{1,3},{3,1},... | collective-permute-start | bytes 319496 | tf_op jit(solution)/shard_map/ppermute | solution.py:394
  8.0 13.8 %collective-permute-start.6 = (bf16[32,1664]{1,0:T(8,128)(2,1)S(1)}, bf16[32,1664]{1,0:T(8,128)(2,1)S(1)}, u32[]{:S(2)}, u32[]{:S(2)}) collective-permute-start(bf16[32,1664]{1,0:T(8,128)(2,1)S(1)} %get-tuple-element.54), channel_id=1, source_target_pairs={{0,4},{2,6},{4,0},{6,2},{8,12},{10,14},{12,8},{14,10},{1,5},{3,7},... | collective-permute-start | bytes 319496 | tf_op jit(solution)/shard_map/ppermute | solution.py:394
  10.4 11.4 %collective-permute-start.7 = (bf16[32,1664]{1,0:T(8,128)(2,1)S(1)}, bf16[32,1664]{1,0:T(8,128)(2,1)S(1)}, u32[]{:S(2)}, u32[]{:S(2)}) collective-permute-start(bf16[32,1664]{1,0:T(8,128)(2,1)S(1)} %get-tuple-element.55), channel_id=1, source_target_pairs={{0,6},{2,4},{4,2},{6,0},{8,14},{10,12},{12,10},{14,8},{1,7},{3,5},... | collective-permute-start | bytes 319496 | tf_op jit(solution)/shard_map/ppermute | solution.py:394
  13.6 13.1 %collective-permute-start.4 = (bf16[64,1536]{1,0:T(8,128)(2,1)S(1)}, bf16[64,1536]{1,0:T(8,128)(2,1)S(1)}, u32[]{:S(2)}, u32[]{:S(2)}) collective-permute-start(bf16[64,1536]{1,0:T(8,128)(2,1)S(1)} %shard_map.93._), channel_id=1, source_target_pairs={{0,8},{2,10},{4,12},{6,14},{8,0},{10,2},{12,4},{14,6},{1,9},{3,11}... | collective-permute-start | bytes 589832 | tf_op jit(solution)/shard_map/ppermute | solution.py:336
  18.1 12.7 %collective-permute-start.3 = (bf16[128,1536]{1,0:T(8,128)(2,1)S(1)}, bf16[128,1536]{1,0:T(8,128)(2,1)S(1)}, u32[]{:S(2)}, u32[]{:S(2)}) collective-permute-start(bf16[128,1536]{1,0:T(8,128)(2,1)S(1)} %shard_map.94._), channel_id=1, source_target_pairs={{0,16},{16,0},{1,17},{17,1},{2,18},{18,2},{3,19},{19,3},{4,20},{20... | collective-permute-start | bytes 1179656 | tf_op jit(solution)/shard_map/ppermute | solution.py:336
  23.2 7.5 %collective-permute-start.11 = (bf16[64,1536]{1,0:T(8,128)(2,1)S(1)}, bf16[64,1536]{1,0:T(8,128)(2,1)S(1)}, u32[]{:S(2)}, u32[]{:S(2)}) collective-permute-start(bf16[64,1536]{1,0:T(8,128)(2,1)S(1)} %get-tuple-element.56.refs_4_), channel_id=1, source_target_pairs={{0,8},{2,10},{4,12},{6,14},{1,9},{3,11},{5,13},{7,15},{16,24},{18,... | collective-permute-start | bytes 589832 | tf_op jit(solution)/shard_map/ppermute | solution.py:336
  26.7 8.9 %copy-start.3 = (f32[1536]{0:T(1024)S(1)}, f32[1536]{0:T(1024)}, u32[]{:S(2)}) copy-start(f32[1536]{0:T(1024)} %param.17) | copy-start | bytes 18436
  27.1 7.3 %collective-permute-start.10 = (bf16[32,1536]{1,0:T(8,128)(2,1)S(1)}, bf16[32,1536]{1,0:T(8,128)(2,1)S(1)}, u32[]{:S(2)}, u32[]{:S(2)}) collective-permute-start(bf16[32,1536]{1,0:T(8,128)(2,1)S(1)} %get-tuple-element.63), channel_id=1, source_target_pairs={{0,2},{2,0},{4,6},{6,4},{8,10},{10,8},{12,14},{14,12},{1,3},{3,1},... | collective-permute-start | bytes 294920 | tf_op jit(solution)/shard_map/ppermute | solution.py:394
  28.5 7.7 %collective-permute-start.8 = (bf16[32,1536]{1,0:T(8,128)(2,1)S(1)}, bf16[32,1536]{1,0:T(8,128)(2,1)S(1)}, u32[]{:S(2)}, u32[]{:S(2)}) collective-permute-start(bf16[32,1536]{1,0:T(8,128)(2,1)S(1)} %get-tuple-element.61), channel_id=1, source_target_pairs={{0,6},{2,4},{4,2},{6,0},{8,14},{10,12},{12,10},{14,8},{1,7},{3,5},... | collective-permute-start | bytes 294920 | tf_op jit(solution)/shard_map/ppermute | solution.py:394
  30.0 6.2 %collective-permute-start.9 = (bf16[32,1536]{1,0:T(8,128)(2,1)S(1)}, bf16[32,1536]{1,0:T(8,128)(2,1)S(1)}, u32[]{:S(2)}, u32[]{:S(2)}) collective-permute-start(bf16[32,1536]{1,0:T(8,128)(2,1)S(1)} %get-tuple-element.62), channel_id=1, source_target_pairs={{0,4},{2,6},{4,0},{6,2},{8,12},{10,14},{12,8},{14,10},{1,5},{3,7},... | collective-permute-start | bytes 294920 | tf_op jit(solution)/shard_map/ppermute | solution.py:394
  31.1 6.1 %collective-permute-start.12 = (bf16[32,1536]{1,0:T(8,128)(2,1)S(1)}, bf16[32,1536]{1,0:T(8,128)(2,1)S(1)}, u32[]{:S(2)}, u32[]{:S(2)}) collective-permute-start(bf16[32,1536]{1,0:T(8,128)(2,1)S(1)} %get-tuple-element.68), channel_id=1, source_target_pairs={{0,6},{2,4},{4,2},{6,0},{8,14},{10,12},{12,10},{14,8},{1,7},{3,5},... | collective-permute-start | bytes 294920 | tf_op jit(solution)/shard_map/ppermute | solution.py:394
  33.5 4.6 %collective-permute-start.13 = (bf16[32,1536]{1,0:T(8,128)(2,1)S(1)}, bf16[32,1536]{1,0:T(8,128)(2,1)S(1)}, u32[]{:S(2)}, u32[]{:S(2)}) collective-permute-start(bf16[32,1536]{1,0:T(8,128)(2,1)S(1)} %get-tuple-element.69), channel_id=1, source_target_pairs={{0,4},{2,6},{4,0},{6,2},{8,12},{10,14},{12,8},{14,10},{1,5},{3,7},... | collective-permute-start | bytes 294920 | tf_op jit(solution)/shard_map/ppermute | solution.py:394
  34.4 4.6 %collective-permute-start.14 = (bf16[32,1536]{1,0:T(8,128)(2,1)S(1)}, bf16[32,1536]{1,0:T(8,128)(2,1)S(1)}, u32[]{:S(2)}, u32[]{:S(2)}) collective-permute-start(bf16[32,1536]{1,0:T(8,128)(2,1)S(1)} %get-tuple-element.70), channel_id=1, source_target_pairs={{0,2},{2,0},{4,6},{6,4},{8,10},{10,8},{12,14},{14,12},{1,3},{3,1},... | collective-permute-start | bytes 294920 | tf_op jit(solution)/shard_map/ppermute | solution.py:394

commit v23 on v22

--- a/solution.py
+++ b/solution.py
@@ -289,6 +289,28 @@
         g_ref[:, part] = gate / (1.0 + jnp.exp(-gate))
 
 
+def col_both_kernel(
+    params_ref, x_ref, raw_ref, maps_ref, gate_ref, skip_ref, _, s_ref, y_ref, g_ref, fade_ref, entry_ref,
+    *, cols, heads, state, width
+):
+    scan = col_scan(params_ref, raw_ref, maps_ref, cols, heads, state)
+    into = scan.into()
+    ends = parts(scan.ends(), 2)
+    mix = scan.within()
+    fade_ref[...] = scan.fade
+    entry_ref[...] = scan.entry(lax.axis_index("row") > 0)
+    skips = parts(jnp.broadcast_to(skip_ref[...], (8, heads)), 2)
+    for first, count in strips(x_ref.shape[1]):
+        pick = picks(heads, width, first, count)
+        part = slice(first, first + count)
+        x = x_ref[:, part].astype(F32)
+        values = (x * dot(scan.grow, pick)).astype(BF16)
+        s_ref[:, part] = (dot(into, values) * dot(ends, pick)).astype(BF16)
+        y_ref[:, part] = dot(mix, values) * dot(scan.fade, pick) + dot(skips, pick)[0:1, :] * x
+        gate = gate_ref[:, part].astype(F32)
+        g_ref[:, part] = gate / (1.0 + jnp.exp(-gate))
+
+
 def col_out_kernel(s_ref, y_ref, fade_ref, entry_ref, w_ref, *, heads, width):
     for first, count in strips(s_ref.shape[1]):
         pick = picks(heads, width, first, count)
@@ -436,31 +458,47 @@
 
     known, entering = [None] * len(pieces), [None] * len(pieces)
     entering[0], before = row_states(0, params)
-    col_made = call(
-        functools.partial(col_state_kernel, **sizes),
-        state_shapes([cols * state], row_count),
-        0,
-        specs=[None] * 4 + [any_spec],
-    )(params, x, raw, maps, before)
-    col_entering = entering_states(col_made[0], col_made[1:], "row", row_count, 1, width)
-    before = col_made[0]
-    y_col, silu, *col_known = call(
-        functools.partial(col_local_kernel, **sizes),
-        [
-            pltpu.VMEM((tokens, channels), F32),
-            pltpu.VMEM((tokens, channels), F32),
-            pltpu.VMEM((tokens, 2 * heads), BF16),
-            pltpu.VMEM((tokens, cols * state), BF16),
-        ],
-        2,
-        specs=[None] * 6 + [any_spec],
-    )(params, x, raw, maps, gate, skip.reshape(1, heads), before)
+    if row_count > 2:
+        col_made = call(
+            functools.partial(col_state_kernel, **sizes),
+            state_shapes([cols * state], row_count),
+            0,
+            specs=[None] * 4 + [any_spec],
+        )(params, x, raw, maps, before)
+        col_entering = entering_states(col_made[0], col_made[1:], "row", row_count, 1, width)
+        before = col_made[0]
+        y_col, silu, *col_known = call(
+            functools.partial(col_local_kernel, **sizes),
+            [
+                pltpu.VMEM((tokens, channels), F32),
+                pltpu.VMEM((tokens, channels), F32),
+                pltpu.VMEM((tokens, 2 * heads), BF16),
+                pltpu.VMEM((tokens, cols * state), BF16),
+            ],
+            2,
+            specs=[None] * 6 + [any_spec],
+        )(params, x, raw, maps, gate, skip.reshape(1, heads), before)
+    else:
+        ends, y_col, silu, *col_known = call(
+            functools.partial(col_both_kernel, **sizes),
+            [
+                pltpu.VMEM((cols * state, channels), BF16),
+                pltpu.VMEM((tokens, channels), F32),
+                pltpu.VMEM((tokens, channels), F32),
+                pltpu.VMEM((tokens, 2 * heads), BF16),
+                pltpu.VMEM((tokens, cols * state), BF16),
+            ],
+            0,
+            specs=[None] * 6 + [any_spec],
+        )(params, x, raw, maps, gate, skip.reshape(1, heads), before)
+        col_entering = entering_states(ends, [], "row", row_count, 1, width)
     w = call(
         functools.partial(col_out_kernel, heads=heads, width=width),
         pltpu.VMEM((tokens, channels), F32),
         0,
     )(col_entering, y_col, *col_known)
     before = y_col
+    known[0], before = own_rows(0, before)
     for i in range(1, len(pieces)):
         if len(pieces[i]) > 1 or col_count > 2 * group:
             known[i], before = own_rows(i, before)
@@ -481,7 +519,6 @@
         )(params, *got[i], before)
         known[i], before = [own], made
         entering[i] = [entering_states(made, [], "col", col_count, group, width, wrap=False)]
-    known[0], before = own_rows(0, before)
     parts_of = []
     for i, piece in enumerate(pieces):
         for j, rows in enumerate(piece):

time: 40.1 us -> 39.3 us (0.980)
  Pallas kernels: 12.1 us -> 10.9 us
    pallas_call x2 -> x1, Pallas kernels: 3.62 us -> 2.38 us  [body(): call(functools.partial(col_both_kernel, **sizes), [pltpu.VMEM((cols * sta...]
    ppermute x12, starting transfers between devices: 15.7 us -> 16.1 us  [exchange(): lax.ppermute(blocks[i], 'col', [(at, partner(at, i, group)) for at in ran...]
  transfers between devices with their start and end apart: 15 -> 15, of which waited for: 5 -> 3; matrix products, arithmetic and copies ran while one was open for 0% -> 0% of each run, Pallas kernels for 24% -> 22%
where the time goes in v23:
time: 39.3 us; the launch traced here: 39.1 us
  starting transfers between devices  22.9 us (58%)
  Pallas kernels  10.9 us (28%)
  waiting for transfers between devices  4.41 us (11%)
  between operations  0.81 us (2%)
    ppermute x12, starting transfers between devices, exchange(): lax.ppermute(blocks[i], 'col', [(at, partner(at, i, group)) for at in ran...  16.1 us
    ppermute x3, starting transfers between devices, entering_states(): entering = lax.ppermute(ends, axis, onward)  6.82 us
    ppermute x12, waiting for transfers between devices, exchange(): lax.ppermute(blocks[i], 'col', [(at, partner(at, i, group)) for at in ran...  4.41 us
    pallas_call x1, Pallas kernels, body(): call(functools.partial(col_both_kernel, **sizes), [pltpu.VMEM((cols * sta...  2.38 us
    pallas_call x2, Pallas kernels, body(): call(functools.partial(final_kernel, which=which, offset=first, share=sha...  1.89 us
    pallas_call x1, Pallas kernels, body(): pl.pallas_call(functools.partial(pack_kernel, heads=heads, state=state, *...  1.52 us
    pallas_call x1, Pallas kernels, body(): call(functools.partial(row_both_kernel, **sizes, **shared), [pltpu.VMEM((...  1.39 us
    pallas_call x1, Pallas kernels, own_rows(): call(functools.partial(row_local_kernel, offset=sum(pieces[i][:j]), **siz...  1.23 us
  transfers between devices with their start and end apart: 15, of which 3 were waited for; matrix products, arithmetic and copies ran while one was open for 0% of the time, Pallas kernels for 22%

profile of v23, /device:TPU:0, one launch (start us, length us, event | category | flops | bytes accessed | tf_op | source)
XLA Modules:
  0.0 39.1 jit_solution(3946394579295198345)
XLA Ops:
  0.0 0.0 copy-start
  0.0 0.0 copy-start.1
  0.0 0.0 copy-start.2
  0.0 1.5 %shard_map.91 = (bf16[256,48]{1,0:T(8,128)(2,1)S(1)}, bf16[256,64]{1,0:T(8,128)(2,1)S(1)}, f32[48,1000]{1,0:T(8,128)S(1)}, f32[2,24]{1,0:T(2,128)S(1)}, bf16[32,...) custom-call(bf16[256,1536]{1,0:T(8,128)(2,1)} %bitcast.7, ...), custom_call_target="tpu_custom_call" | custom-call | flops 1000001024 | bytes 1024 | tf_op jit(solution)/shard_map/pallas_call | solution.py:388
  1.5 3.0 %collective-permute-start = (bf16[32,1664]{1,0:T(8,128)(2,1)S(1)}, bf16[32,1664]{1,0:T(8,128)(2,1)S(1)}, u32[]{:S(2)}, u32[]{:S(2)}) collective-permute-start(bf16[32,1664]{1,0:T(8,128)(2,1)S(1)} %get-tuple-element.46), channel_id=1, source_target_pairs={{0,2},{2,0},{4,6},{6,4},{8,10},{10,8},{12,14},{14,12},{1,3},{3,1},... | collective-permute-start | bytes 319496 | tf_op jit(solution)/shard_map/ppermute | solution.py:416
  4.6 1.6 %collective-permute-start.1 = (bf16[32,1664]{1,0:T(8,128)(2,1)S(1)}, bf16[32,1664]{1,0:T(8,128)(2,1)S(1)}, u32[]{:S(2)}, u32[]{:S(2)}) collective-permute-start(bf16[32,1664]{1,0:T(8,128)(2,1)S(1)} %get-tuple-element.47), channel_id=1, source_target_pairs={{0,4},{2,6},{4,0},{6,2},{8,12},{10,14},{12,8},{14,10},{1,5},{3,7},... | collective-permute-start | bytes 319496 | tf_op jit(solution)/shard_map/ppermute | solution.py:416
  6.2 0.0 collective-permute-start.2
  6.2 1.9 %collective-permute-start.5 = (bf16[32,1664]{1,0:T(8,128)(2,1)S(1)}, bf16[32,1664]{1,0:T(8,128)(2,1)S(1)}, u32[]{:S(2)}, u32[]{:S(2)}) collective-permute-start(bf16[32,1664]{1,0:T(8,128)(2,1)S(1)} %get-tuple-element.58), channel_id=1, source_target_pairs={{0,2},{2,0},{4,6},{6,4},{8,10},{10,8},{12,14},{14,12},{1,3},{3,1},... | collective-permute-start | bytes 319496 | tf_op jit(solution)/shard_map/ppermute | solution.py:416
  8.1 1.6 %collective-permute-start.6 = (bf16[32,1664]{1,0:T(8,128)(2,1)S(1)}, bf16[32,1664]{1,0:T(8,128)(2,1)S(1)}, u32[]{:S(2)}, u32[]{:S(2)}) collective-permute-start(bf16[32,1664]{1,0:T(8,128)(2,1)S(1)} %get-tuple-element.59), channel_id=1, source_target_pairs={{0,4},{2,6},{4,0},{6,2},{8,12},{10,14},{12,8},{14,10},{1,5},{3,7},... | collective-permute-start | bytes 319496 | tf_op jit(solution)/shard_map/ppermute | solution.py:416
  10.3 0.2 shard_map.92.params_ref.refs_4_
  10.5 0.0 collective-permute-done.refs_1_
  10.5 0.0 collective-permute-start.7
  10.5 0.0 collective-permute-done.1.refs_2_
  10.5 2.0 %collective-permute-done.2.refs_3_ = bf16[32,1664]{1,0:T(8,128)(2,1)S(1)} collective-permute-done((bf16[32,1664]{1,0:T(8,128)(2,1)S(1)}, bf16[32,1664]{1,0:T(8,128)(2,1)S(1)}, u32[]{:S(2)}, u32[]{:S(2)}) %collective-permute-start.2) | collective-permute-done | bytes 106528 | tf_op jit(solution)/shard_map/ppermute | solution.py:416
  12.5 1.1 %shard_map.93._ = bf16[64,1536]{1,0:T(8,128)(2,1)S(1)} custom-call(f32[8,48]{1,0:T(8,128)S(1)} %shard_map.92.params_ref.refs_4_, bf16[32,1664]{1,0:T(8,128)(2,1)S(1)} %get-tuple-element.45.refs_0_, bf16[32,1664]{1,0:T(8,128)(2,1)S(1)} %collective-permute-done.refs_1_, bf16[32,1664]{1,0:T(8,128)(2,1)S(1)} %collective-permute-done.1.refs_2_, ...), custom_call_target="tpu_custom_call" | custom-call | flops 1024 | bytes 1024 | tf_op jit(solution)/shard_map/pallas_call | solution.py:446
  13.6 3.0 %collective-permute-start.4 = (bf16[64,1536]{1,0:T(8,128)(2,1)S(1)}, bf16[64,1536]{1,0:T(8,128)(2,1)S(1)}, u32[]{:S(2)}, u32[]{:S(2)}) collective-permute-start(bf16[64,1536]{1,0:T(8,128)(2,1)S(1)} %shard_map.93._), channel_id=1, source_target_pairs={{0,8},{2,10},{4,12},{6,14},{8,0},{10,2},{12,4},{14,6},{1,9},{3,11}... | collective-permute-start | bytes 589832 | tf_op jit(solution)/shard_map/ppermute | solution.py:358
  16.6 0.0 copy-done
  16.6 0.0 copy-done.1
  16.6 0.0 copy-done.2
  16.6 2.4 %shard_map.94 = (bf16[128,1536]{1,0:T(8,128)(2,1)S(1)}, f32[256,1536]{1,0:T(8,128)S(1)}, f32[256,1536]{1,0:T(8,128)S(1)}, bf16[256,48]{1,0:T(8,128)(2,1)S(1)}, bf16[256,128]{1,0:T(8,128)(2,1)S(1)}) custom-call(f32[8,48]{1,0:T(8,128)S(1)} %shard_map.92.params_ref.refs_4_, bf16[256,1536]{1,0:T(8,128)(2,1)S(1)} %bitcast.8, ...), custom_call_target="tpu_custom_call" | custom-call | flops 1024 | bytes 1024 | tf_op jit(solution)/shard_map/pallas_call | solution.py:482
  19.0 1.6 %collective-permute-start.3 = (bf16[128,1536]{1,0:T(8,128)(2,1)S(1)}, bf16[128,1536]{1,0:T(8,128)(2,1)S(1)}, u32[]{:S(2)}, u32[]{:S(2)}) collective-permute-start(bf16[128,1536]{1,0:T(8,128)(2,1)S(1)} %get-tuple-element.49), channel_id=1, source_target_pairs={{0,16},{16,0},{1,17},{17,1},{2,18},{18,2},{3,19},{19,3},{4,20},{20... | collective-permute-start | bytes 1179656 | tf_op jit(solution)/shard_map/ppermute | solution.py:358
  20.6 1.2 %shard_map.96 = (f32[128,1536]{1,0:T(8,128)S(1)}, bf16[128,48]{1,0:T(8,128)(2,1)S(1)}, bf16[128,64]{1,0:T(8,128)(2,1)S(1)}) custom-call(f32[8,48]{1,0:T(8,128)S(1)} %shard_map.92.params_ref.refs_4_, bf16[32,1664]{1,0:T(8,128)(2,1)S(1)} %get-tuple-element.45.refs_0_, bf16[32,1664]{1,0:T(8,128)(2,1)S(1)} %collective-permute-done.refs_1_, ...), custom_call_target="tpu_custom_call" | custom-call | flops 2000001024 | bytes 1024 | tf_op jit(solution)/shard_map/pallas_call | solution.py:430
  21.8 0.0 collective-permute-done.5.refs_1_
  21.8 0.0 collective-permute-done.6.refs_2_
  21.8 0.0 collective-permute-done.7.refs_3_
  21.8 1.4 %shard_map.97 = (bf16[64,1536]{1,0:T(8,128)(2,1)S(1)}, f32[128,1536]{1,0:T(8,128)S(1)}, bf16[128,48]{1,0:T(8,128)(2,1)S(1)}, bf16[128,64]{1,0:T(8,128)(2,1)S(1)}) custom-call(f32[8,48]{1,0:T(8,128)S(1)} %shard_map.92.params_ref.refs_4_, bf16[32,1664]{1,0:T(8,128)(2,1)S(1)} %get-tuple-element.57.refs_0_, bf16[32,1664]{1,0:T(8,128)(2,1)S(1)} %collective-permute-done.5.refs_1_, ...), custom_call_target="tpu_custom_call" | custom-call | flops 2000001024 | bytes 1024 | tf_op jit(solution)/shard_map/pallas_call | solution.py:509
  23.2 0.0 copy-start.3
  23.2 2.3 %collective-permute-start.11 = (bf16[64,1536]{1,0:T(8,128)(2,1)S(1)}, bf16[64,1536]{1,0:T(8,128)(2,1)S(1)}, u32[]{:S(2)}, u32[]{:S(2)}) collective-permute-start(bf16[64,1536]{1,0:T(8,128)(2,1)S(1)} %get-tuple-element.61._.__), channel_id=1, source_target_pairs={{0,8},{2,10},{4,12},{6,14},{1,9},{3,11},{5,13},{7,15},{16,24},{18,... | collective-permute-start | bytes 589832 | tf_op jit(solution)/shard_map/ppermute | solution.py:358
  25.5 0.0 collective-permute-done.4.s_ref
  25.5 0.3 shard_map.98
  25.9 1.4 %collective-permute-start.10 = (bf16[32,1536]{1,0:T(8,128)(2,1)S(1)}, bf16[32,1536]{1,0:T(8,128)(2,1)S(1)}, u32[]{:S(2)}, u32[]{:S(2)}) collective-permute-start(bf16[32,1536]{1,0:T(8,128)(2,1)S(1)} %get-tuple-element.65), channel_id=1, source_target_pairs={{0,2},{2,0},{4,6},{6,4},{8,10},{10,8},{12,14},{14,12},{1,3},{3,1},... | collective-permute-start | bytes 294920 | tf_op jit(solution)/shard_map/ppermute | solution.py:416
  27.3 1.6 %collective-permute-start.8 = (bf16[32,1536]{1,0:T(8,128)(2,1)S(1)}, bf16[32,1536]{1,0:T(8,128)(2,1)S(1)}, u32[]{:S(2)}, u32[]{:S(2)}) collective-permute-start(bf16[32,1536]{1,0:T(8,128)(2,1)S(1)} %get-tuple-element.63), channel_id=1, source_target_pairs={{0,6},{2,4},{4,2},{6,0},{8,14},{10,12},{12,10},{14,8},{1,7},{3,5},... | collective-permute-start | bytes 294920 | tf_op jit(solution)/shard_map/ppermute | solution.py:416
  28.8 0.6 %collective-permute-start.9 = (bf16[32,1536]{1,0:T(8,128)(2,1)S(1)}, bf16[32,1536]{1,0:T(8,128)(2,1)S(1)}, u32[]{:S(2)}, u32[]{:S(2)}) collective-permute-start(bf16[32,1536]{1,0:T(8,128)(2,1)S(1)} %get-tuple-element.64), channel_id=1, source_target_pairs={{0,4},{2,6},{4,0},{6,2},{8,12},{10,14},{12,8},{14,10},{1,5},{3,7},... | collective-permute-start | bytes 294920 | tf_op jit(solution)/shard_map/ppermute | solution.py:416
  29.4 0.0 collective-permute-done.11.s_ref
  29.4 0.0 collective-permute-done.3.s_ref.__
  29.4 0.3 shard_map.100
  29.8 3.8 %collective-permute-start.12 = (bf16[32,1536]{1,0:T(8,128)(2,1)S(1)}, bf16[32,1536]{1,0:T(8,128)(2,1)S(1)}, u32[]{:S(2)}, u32[]{:S(2)}) collective-permute-start(bf16[32,1536]{1,0:T(8,128)(2,1)S(1)} %get-tuple-element.70), channel_id=1, source_target_pairs={{0,6},{2,4},{4,2},{6,0},{8,14},{10,12},{12,10},{14,8},{1,7},{3,5},... | collective-permute-start | bytes 294920 | tf_op jit(solution)/shard_map/ppermute | solution.py:416
  33.6 0.0 collective-permute-start.13
  33.6 0.0 collective-permute-done.10.refs_3_
  33.6 0.6 %collective-permute-start.14 = (bf16[32,1536]{1,0:T(8,128)(2,1)S(1)}, bf16[32,1536]{1,0:T(8,128)(2,1)S(1)}, u32[]{:S(2)}, u32[]{:S(2)}) collective-permute-start(bf16[32,1536]{1,0:T(8,128)(2,1)S(1)} %get-tuple-element.72), channel_id=1, source_target_pairs={{0,2},{2,0},{4,6},{6,4},{8,10},{10,8},{12,14},{14,12},{1,3},{3,1},... | collective-permute-start | bytes 294920 | tf_op jit(solution)/shard_map/ppermute | solution.py:416
  34.2 0.0 copy-done.3
  34.2 0.6 %shard_map.95.w_ref = f32[256,1536]{1,0:T(8,128)S(1)} custom-call(bf16[128,1536]{1,0:T(8,128)(2,1)S(1)} %collective-permute-done.3.s_ref.__, f32[256,1536]{1,0:T(8,128)S(1)} %get-tuple-element.50.y_ref.refs_4_, bf16[256,48]{1,0:T(8,128)(2,1)S(1)} %get-tuple-element.51.fade_ref, bf16[256,128]{1,0:T(8,128)(2,1)S(1)} %get-tuple-element.52.entry_ref), custom_call_target="tpu_custom_call" | custom-call | flops 1024 | bytes 1024 | tf_op jit(solution)/shard_map/pallas_call | solution.py:495
  34.8 0.0 collective-permute-done.8.refs_1_
  34.8 0.0 collective-permute-done.9.refs_2_
  34.8 0.9 %shard_map.99.refs_0_ = bf16[256,1536]{1,0:T(8,128)(2,1)} custom-call(f32[256,1536]{1,0:T(8,128)S(1)} %shard_map.95.w_ref, f32[256,1536]{1,0:T(8,128)S(1)} %get-tuple-element.53.g_ref, f32[1,1536]{1,0:T(1,128)S(1)} %reshape.27.gain_ref, bf16[32,1536]{1,0:T(8,128)(2,1)S(1)} %get-tuple-element.62.refs_0_._, ...), custom_call_target="tpu_custom_call" | custom-call | flops 1024 | bytes 1024 | tf_op jit(solution)/shard_map/pallas_call | solution.py:544
  35.8 0.4 collective-permute-done.12.refs_2_
  36.2 2.0 %collective-permute-done.13.refs_3_ = bf16[32,1536]{1,0:T(8,128)(2,1)S(1)} collective-permute-done((bf16[32,1536]{1,0:T(8,128)(2,1)S(1)}, bf16[32,1536]{1,0:T(8,128)(2,1)S(1)}, u32[]{:S(2)}, u32[]{:S(2)}) %collective-permute-start.13) | collective-permute-done | bytes 98336 | tf_op jit(solution)/shard_map/ppermute | solution.py:416
  38.2 0.0 collective-permute-done.14.refs_4_
  38.2 0.9 %shard_map.101 = bf16[256,1536]{1,0:T(8,128)(2,1)} custom-call(f32[256,1536]{1,0:T(8,128)S(1)} %shard_map.95.w_ref, f32[256,1536]{1,0:T(8,128)S(1)} %get-tuple-element.53.g_ref, f32[1,1536]{1,0:T(1,128)S(1)} %reshape.27.gain_ref, bf16[256,1536]{1,0:T(8,128)(2,1)} %shard_map.99.refs_0_, ...), custom_call_target="tpu_custom_call", output_to_operand_aliasing={{}: (3, {})} | custom-call | flops 1024 | bytes 1024 | tf_op jit(solution)/shard_map/pallas_call | solution.py:544
  (1 shorter events, 0.0 us)
Async XLA Ops:
  0.0 16.6 %copy-start = (bf16[1,32,8,1536]{3,2,1,0:T(8,128)(2,1)S(1)}, bf16[1,32,8,1536]{3,2,1,0:T(8,128)(2,1)}, u32[]{:S(2)}) copy-start(bf16[1,32,8,1536]{3,2,1,0:T(8,128)(2,1)} %param.9) | copy-start | bytes 2359300
  0.0 16.6 %copy-start.1 = (bf16[1,32,8,1536]{3,2,1,0:T(8,128)(2,1)S(1)}, bf16[1,32,8,1536]{3,2,1,0:T(8,128)(2,1)}, u32[]{:S(2)}) copy-start(bf16[1,32,8,1536]{3,2,1,0:T(8,128)(2,1)} %param.10) | copy-start | bytes 2359300
  0.0 16.6 %copy-start.2 = (f32[24]{0:T(128)S(1)}, f32[24]{0:T(128)}, u32[]{:S(2)}) copy-start(f32[24]{0:T(128)} %param.16) | copy-start | bytes 292
  1.5 8.9 %collective-permute-start = (bf16[32,1664]{1,0:T(8,128)(2,1)S(1)}, bf16[32,1664]{1,0:T(8,128)(2,1)S(1)}, u32[]{:S(2)}, u32[]{:S(2)}) collective-permute-start(bf16[32,1664]{1,0:T(8,128)(2,1)S(1)} %get-tuple-element.46), channel_id=1, source_target_pairs={{0,2},{2,0},{4,6},{6,4},{8,10},{10,8},{12,14},{14,12},{1,3},{3,1},... | collective-permute-start | bytes 319496 | tf_op jit(solution)/shard_map/ppermute | solution.py:416
  4.6 5.9 %collective-permute-start.1 = (bf16[32,1664]{1,0:T(8,128)(2,1)S(1)}, bf16[32,1664]{1,0:T(8,128)(2,1)S(1)}, u32[]{:S(2)}, u32[]{:S(2)}) collective-permute-start(bf16[32,1664]{1,0:T(8,128)(2,1)S(1)} %get-tuple-element.47), channel_id=1, source_target_pairs={{0,4},{2,6},{4,0},{6,2},{8,12},{10,14},{12,8},{14,10},{1,5},{3,7},... | collective-permute-start | bytes 319496 | tf_op jit(solution)/shard_map/ppermute | solution.py:416
  6.2 6.3 %collective-permute-start.2 = (bf16[32,1664]{1,0:T(8,128)(2,1)S(1)}, bf16[32,1664]{1,0:T(8,128)(2,1)S(1)}, u32[]{:S(2)}, u32[]{:S(2)}) collective-permute-start(bf16[32,1664]{1,0:T(8,128)(2,1)S(1)} %get-tuple-element.48), channel_id=1, source_target_pairs={{0,6},{2,4},{4,2},{6,0},{8,14},{10,12},{12,10},{14,8},{1,7},{3,5},... | collective-permute-start | bytes 319496 | tf_op jit(solution)/shard_map/ppermute | solution.py:416
  6.2 15.6 %collective-permute-start.5 = (bf16[32,1664]{1,0:T(8,128)(2,1)S(1)}, bf16[32,1664]{1,0:T(8,128)(2,1)S(1)}, u32[]{:S(2)}, u32[]{:S(2)}) collective-permute-start(bf16[32,1664]{1,0:T(8,128)(2,1)S(1)} %get-tuple-element.58), channel_id=1, source_target_pairs={{0,2},{2,0},{4,6},{6,4},{8,10},{10,8},{12,14},{14,12},{1,3},{3,1},... | collective-permute-start | bytes 319496 | tf_op jit(solution)/shard_map/ppermute | solution.py:416
  8.1 13.7 %collective-permute-start.6 = (bf16[32,1664]{1,0:T(8,128)(2,1)S(1)}, bf16[32,1664]{1,0:T(8,128)(2,1)S(1)}, u32[]{:S(2)}, u32[]{:S(2)}) collective-permute-start(bf16[32,1664]{1,0:T(8,128)(2,1)S(1)} %get-tuple-element.59), channel_id=1, source_target_pairs={{0,4},{2,6},{4,0},{6,2},{8,12},{10,14},{12,8},{14,10},{1,5},{3,7},... | collective-permute-start | bytes 319496 | tf_op jit(solution)/shard_map/ppermute | solution.py:416
  10.5 11.3 %collective-permute-start.7 = (bf16[32,1664]{1,0:T(8,128)(2,1)S(1)}, bf16[32,1664]{1,0:T(8,128)(2,1)S(1)}, u32[]{:S(2)}, u32[]{:S(2)}) collective-permute-start(bf16[32,1664]{1,0:T(8,128)(2,1)S(1)} %get-tuple-element.60), channel_id=1, source_target_pairs={{0,6},{2,4},{4,2},{6,0},{8,14},{10,12},{12,10},{14,8},{1,7},{3,5},... | collective-permute-start | bytes 319496 | tf_op jit(solution)/shard_map/ppermute | solution.py:416
  13.6 11.9 %collective-permute-start.4 = (bf16[64,1536]{1,0:T(8,128)(2,1)S(1)}, bf16[64,1536]{1,0:T(8,128)(2,1)S(1)}, u32[]{:S(2)}, u32[]{:S(2)}) collective-permute-start(bf16[64,1536]{1,0:T(8,128)(2,1)S(1)} %shard_map.93._), channel_id=1, source_target_pairs={{0,8},{2,10},{4,12},{6,14},{8,0},{10,2},{12,4},{14,6},{1,9},{3,11}... | collective-permute-start | bytes 589832 | tf_op jit(solution)/shard_map/ppermute | solution.py:358
  19.0 10.4 %collective-permute-start.3 = (bf16[128,1536]{1,0:T(8,128)(2,1)S(1)}, bf16[128,1536]{1,0:T(8,128)(2,1)S(1)}, u32[]{:S(2)}, u32[]{:S(2)}) collective-permute-start(bf16[128,1536]{1,0:T(8,128)(2,1)S(1)} %get-tuple-element.49), channel_id=1, source_target_pairs={{0,16},{16,0},{1,17},{17,1},{2,18},{18,2},{3,19},{19,3},{4,20},{20... | collective-permute-start | bytes 1179656 | tf_op jit(solution)/shard_map/ppermute | solution.py:358
  23.2 11.0 %copy-start.3 = (f32[1536]{0:T(1024)S(1)}, f32[1536]{0:T(1024)}, u32[]{:S(2)}) copy-start(f32[1536]{0:T(1024)} %param.17) | copy-start | bytes 18436
  23.2 6.2 %collective-permute-start.11 = (bf16[64,1536]{1,0:T(8,128)(2,1)S(1)}, bf16[64,1536]{1,0:T(8,128)(2,1)S(1)}, u32[]{:S(2)}, u32[]{:S(2)}) collective-permute-start(bf16[64,1536]{1,0:T(8,128)(2,1)S(1)} %get-tuple-element.61._.__), channel_id=1, source_target_pairs={{0,8},{2,10},{4,12},{6,14},{1,9},{3,11},{5,13},{7,15},{16,24},{18,... | collective-permute-start | bytes 589832 | tf_op jit(solution)/shard_map/ppermute | solution.py:358
  25.9 7.7 %collective-permute-start.10 = (bf16[32,1536]{1,0:T(8,128)(2,1)S(1)}, bf16[32,1536]{1,0:T(8,128)(2,1)S(1)}, u32[]{:S(2)}, u32[]{:S(2)}) collective-permute-start(bf16[32,1536]{1,0:T(8,128)(2,1)S(1)} %get-tuple-element.65), channel_id=1, source_target_pairs={{0,2},{2,0},{4,6},{6,4},{8,10},{10,8},{12,14},{14,12},{1,3},{3,1},... | collective-permute-start | bytes 294920 | tf_op jit(solution)/shard_map/ppermute | solution.py:416
  27.3 7.6 %collective-permute-start.8 = (bf16[32,1536]{1,0:T(8,128)(2,1)S(1)}, bf16[32,1536]{1,0:T(8,128)(2,1)S(1)}, u32[]{:S(2)}, u32[]{:S(2)}) collective-permute-start(bf16[32,1536]{1,0:T(8,128)(2,1)S(1)} %get-tuple-element.63), channel_id=1, source_target_pairs={{0,6},{2,4},{4,2},{6,0},{8,14},{10,12},{12,10},{14,8},{1,7},{3,5},... | collective-permute-start | bytes 294920 | tf_op jit(solution)/shard_map/ppermute | solution.py:416
  28.8 6.0 %collective-permute-start.9 = (bf16[32,1536]{1,0:T(8,128)(2,1)S(1)}, bf16[32,1536]{1,0:T(8,128)(2,1)S(1)}, u32[]{:S(2)}, u32[]{:S(2)}) collective-permute-start(bf16[32,1536]{1,0:T(8,128)(2,1)S(1)} %get-tuple-element.64), channel_id=1, source_target_pairs={{0,4},{2,6},{4,0},{6,2},{8,12},{10,14},{12,8},{14,10},{1,5},{3,7},... | collective-permute-start | bytes 294920 | tf_op jit(solution)/shard_map/ppermute | solution.py:416
  29.8 6.4 %collective-permute-start.12 = (bf16[32,1536]{1,0:T(8,128)(2,1)S(1)}, bf16[32,1536]{1,0:T(8,128)(2,1)S(1)}, u32[]{:S(2)}, u32[]{:S(2)}) collective-permute-start(bf16[32,1536]{1,0:T(8,128)(2,1)S(1)} %get-tuple-element.70), channel_id=1, source_target_pairs={{0,6},{2,4},{4,2},{6,0},{8,14},{10,12},{12,10},{14,8},{1,7},{3,5},... | collective-permute-start | bytes 294920 | tf_op jit(solution)/shard_map/ppermute | solution.py:416
  33.6 4.6 %collective-permute-start.13 = (bf16[32,1536]{1,0:T(8,128)(2,1)S(1)}, bf16[32,1536]{1,0:T(8,128)(2,1)S(1)}, u32[]{:S(2)}, u32[]{:S(2)}) collective-permute-start(bf16[32,1536]{1,0:T(8,128)(2,1)S(1)} %get-tuple-element.71), channel_id=1, source_target_pairs={{0,4},{2,6},{4,0},{6,2},{8,12},{10,14},{12,8},{14,10},{1,5},{3,7},... | collective-permute-start | bytes 294920 | tf_op jit(solution)/shard_map/ppermute | solution.py:416
  33.6 4.6 %collective-permute-start.14 = (bf16[32,1536]{1,0:T(8,128)(2,1)S(1)}, bf16[32,1536]{1,0:T(8,128)(2,1)S(1)}, u32[]{:S(2)}, u32[]{:S(2)}) collective-permute-start(bf16[32,1536]{1,0:T(8,128)(2,1)S(1)} %get-tuple-element.72), channel_id=1, source_target_pairs={{0,2},{2,0},{4,6},{6,4},{8,10},{10,8},{12,14},{14,12},{1,3},{3,1},... | collective-permute-start | bytes 294920 | tf_op jit(solution)/shard_map/ppermute | solution.py:416
